TPU v7x, 32 devices: a whole 2x2x4 slice. The times are simulated.
32 devices in a mesh: dom: 8 (over z, y), feat: 4 (over x, core).
Axes of the slice: x: 2, y: 2, z: 4, core: 2. Of those that a mesh axis runs over, the one named last changes fastest.
Arguments:
- features: bfloat16 [2048, 512], P('dom', 'feat'), may hold values from -6 to 6
- w_self: bfloat16 [512, 512], P('feat'), may hold values from -0.25 to 0.25
- w_neigh: bfloat16 [512, 512], P('feat'), may hold values from -0.25 to 0.25
- bias: bfloat16 [512], P('feat'), may hold values from -3 to 3
- cotangent: bfloat16 [2048, 512], P('dom', 'feat'), may hold values from -6 to 6
- tile_vals: bfloat16 [8, 4, 128, 128], P('dom'), may hold values from -0.375 to 0.375
- tile_pos: int32 [8, 4], P('dom'), may hold values from 0 to 3, as said below
- tile_count: int32 [8], P('dom'), may hold values from 1 to 4, as said below
- send_rows: int32 [8, 8, 48], P('dom'), may hold values from 0 to 255
- recv_dest: int32 [8, 8, 48], P('dom'), may hold values from 0 to 255
- ghost_weight: float32 [8, 8, 48], P('dom'), may hold values from 0.2 to 1.8
- recv_count: int32 [8, 8], P('dom'), may hold values from 0 to 48, as said below
- hub_rows: int32 [8, 2], P('dom'), may hold values from 0 to 255, as said below
- hub_weight: bfloat16 [2048, 16], P('dom'), may hold values from -1.5 to 1.5
Outputs:
- output: bfloat16 [2048, 512], P('dom', 'feat')
- grad_features: bfloat16 [2048, 512], P('dom', 'feat')
- grad_self: float32 [512, 512], P('feat')
- grad_neigh: float32 [512, 512], P('feat')
- grad_bias: float32 [512], P('feat')
Inputs may be any that keep to these rules, and one draw needn't show every extreme that they name: `tile_pos`: within a partition the numbers are distinct. `tile_count`: some partition uses all 4 slots. `recv_count`: some partition receives 48 live slots from some peer. `hub_rows`: within a partition the rows are distinct.
All inputs are finite; a program needn't handle non-finite values.
Results may differ from a plain program's by a relative error of at most 0.017.
Values may be sent and summed in bfloat16 or wider, within the bound.
No kernel may reach another device: no remote copies, remote signals or barrier semaphores. Data moves between devices by JAX's collectives and lax.ppermute only.
A program may use at most 64 MiB of HBM per device.

v0:
```python
import math

import jax
import jax.numpy as jnp
from jax import lax
from jax.sharding import PartitionSpec as P


def tile_forward(tiles_here, places, count_here, blocks):
    block_count = blocks.shape[0]

    def add_tile(slot_index, totals):
        tile_place = places[slot_index]
        product = jnp.dot(
            tiles_here[slot_index],
            blocks[tile_place % block_count],
            preferred_element_type=jnp.float32,
        )
        return totals.at[tile_place // block_count].add(product)

    return lax.fori_loop(0, count_here, add_tile, jnp.zeros(blocks.shape, jnp.float32))


def tile_backward(tiles_here, places, count_here, blocks):
    block_count = blocks.shape[0]

    def add_tile(slot_index, totals):
        tile_place = places[slot_index]
        product = lax.dot_general(
            tiles_here[slot_index],
            blocks[tile_place // block_count],
            (((0,), (0,)), ((), ())),
            preferred_element_type=jnp.float32,
        )
        return totals.at[tile_place % block_count].add(product)

    return lax.fori_loop(0, count_here, add_tile, jnp.zeros(blocks.shape, jnp.float32))


def on_device(
    features,
    w_self,
    w_neigh,
    bias,
    cotangent,
    tile_vals,
    tile_pos,
    tile_count,
    send_rows,
    recv_dest,
    ghost_weight,
    recv_count,
    hub_rows,
    hub_weight,
):
    row_count, width_here = features.shape
    tile_size = tile_vals.shape[-1]
    block_count = row_count // tile_size
    slot_count = send_rows.shape[-1]
    hub_here = hub_rows.shape[-1]
    live = jnp.arange(slot_count, dtype=jnp.int32)[None, :] < recv_count[0][:, None]
    coef = jnp.where(live, ghost_weight[0], jnp.zeros_like(ghost_weight[0]))
    blocks = features.reshape(block_count, tile_size, width_here)
    local_part = tile_forward(tile_vals[0], tile_pos[0], tile_count[0], blocks).reshape(
        row_count, width_here
    )
    outgoing = features[send_rows[0]]
    incoming = lax.all_to_all(outgoing, "dom", split_axis=0, concat_axis=0, tiled=True)
    weighted = incoming.astype(jnp.float32) * coef[:, :, None]
    ghost_part = jax.ops.segment_sum(
        weighted.reshape(-1, width_here), recv_dest[0].reshape(-1), num_segments=row_count
    )
    owned_rows = features[hub_rows[0]]
    hub_part = jnp.dot(
        hub_weight,
        lax.all_gather(owned_rows, "dom", axis=0, tiled=True),
        preferred_element_type=jnp.float32,
    )
    neigh = (local_part + ghost_part + hub_part).astype(jnp.bfloat16)
    partial_sum = jnp.dot(features, w_self, preferred_element_type=jnp.float32) + jnp.dot(
        neigh, w_neigh, preferred_element_type=jnp.float32
    )
    preact = lax.psum_scatter(
        partial_sum.astype(jnp.bfloat16), "feat", scatter_dimension=1, tiled=True
    ).astype(jnp.float32)
    preact = preact + bias.astype(jnp.float32)
    output = jax.nn.silu(preact).astype(jnp.bfloat16)
    logistic = jax.nn.sigmoid(preact)
    grad_pre = (
        cotangent.astype(jnp.float32) * logistic * (1.0 + preact * (1.0 - logistic))
    ).astype(jnp.bfloat16)
    arrived_piece = lax.all_gather(grad_pre, "feat", axis=1, tiled=True)
    into_self = lax.dot_general(
        arrived_piece, w_self, (((1,), (1,)), ((), ())), preferred_element_type=jnp.float32
    )
    into_neigh = lax.dot_general(
        arrived_piece, w_neigh, (((1,), (1,)), ((), ())), preferred_element_type=jnp.float32
    )
    self_cols_grad = lax.dot_general(
        features, arrived_piece, (((0,), (0,)), ((), ())), preferred_element_type=jnp.float32
    )
    neigh_cols_grad = lax.dot_general(
        neigh, arrived_piece, (((0,), (0,)), ((), ())), preferred_element_type=jnp.float32
    )
    grad_self_part = self_cols_grad
    grad_neigh_part = neigh_cols_grad
    into_self, into_neigh, grad_self_part, grad_neigh_part = (
        into_self,
        into_neigh,
        grad_self_part,
        grad_neigh_part,
    )
    neigh_grad = into_neigh.astype(jnp.bfloat16)
    grad_blocks = neigh_grad.reshape(block_count, tile_size, width_here)
    local_back = tile_backward(tile_vals[0], tile_pos[0], tile_count[0], grad_blocks).reshape(
        row_count, width_here
    )
    returned = coef[:, :, None] * neigh_grad[recv_dest[0]].astype(jnp.float32)
    arrived_grads = lax.all_to_all(
        returned.astype(jnp.bfloat16), "dom", split_axis=0, concat_axis=0, tiled=True
    ).astype(returned.dtype)
    ghost_back = jax.ops.segment_sum(
        arrived_grads.reshape(-1, width_here), send_rows[0].reshape(-1), num_segments=row_count
    )
    hub_term = lax.dot_general(
        hub_weight, neigh_grad, (((0,), (0,)), ((), ())), preferred_element_type=jnp.float32
    )
    every_hub = lax.psum(hub_term, "dom")
    owned_grad = lax.dynamic_slice_in_dim(every_hub, lax.axis_index("dom") * hub_here, hub_here, 0)
    hub_back = jax.ops.segment_sum(owned_grad, hub_rows[0], num_segments=row_count)
    grad_features = (into_self + local_back + ghost_back + hub_back).astype(jnp.bfloat16)
    bias_part = jnp.sum(grad_pre.astype(jnp.float32), axis=0)
    total_self, total_neigh, total_bias = lax.psum(
        (grad_self_part, grad_neigh_part, bias_part), "dom"
    )
    scale = 1.0 / math.sqrt(lax.axis_size("dom") * row_count)
    return (output, grad_features, total_self * scale, total_neigh * scale, total_bias * scale)


def solution(mesh):
    placed = (
        P("dom", "feat"),
        P("feat", None),
        P("feat", None),
        P("feat"),
        P("dom", "feat"),
        P("dom", None, None, None),
        P("dom", None),
        P("dom"),
        P("dom", None, None),
        P("dom", None, None),
        P("dom", None, None),
        P("dom", None),
        P("dom", None),
        P("dom", None),
    )
    return jax.shard_map(
        on_device,
        mesh=mesh,
        in_specs=placed,
        out_specs=(P("dom", "feat"), P("dom", "feat"), P("feat", None), P("feat", None), P("feat")),
        check_vma=False,
    )
```

profile of v0, /device:TPU:0, one launch (start us, length us, event | category | flops | bytes accessed | tf_op | source)
XLA Modules:
  0.0 200.5 jit_solution(16713589266588235402)
XLA Ops:
  7.2 0.7 compare_select_fusion.1
  8.0 2.5 %gather_fusion.1 = bf16[384,128]{1,0:T(8,128)(2,1)} fusion(bf16[256,128]{1,0:T(8,128)(2,1)} %param.22, s32[1024]{0:T(1024)S(1)} %pad_clamp_fusion.1), kind=kCustom, calls=%fused_computation.1 | custom fusion | bytes 198144 | tf_op jit(solution)/shard_map/gather | solution.py:67
  10.5 7.4 %all-to-all-start = ((bf16[8,48,128]{2,1,0:T(8,128)(2,1)}), bf16[8,48,128]{2,1,0:T(8,128)(2,1)S(1)}, u32[]{:S(2)}, u32[]{:S(2)}) async-start(bf16[8,48,128]{2,1,0:T(8,128)(2,1)} %bitcast.21), calls=%async_computation | async-start | bytes 196608 | tf_op jit(solution)/shard_map/all_to_all | solution.py:68
  18.7 20.8 %all-gather.1 = bf16[8,2,128]{2,1,0:T(2,128)(2,1)S(1)} all-gather(bf16[1,2,128]{2,1,0:T(2,128)(2,1)S(1)} %bitcast.122), channel_id=2, replica_groups=mesh['dom'=8,'feat'=4] {'dom'}, dimensions={0}, use_global_device_ids=true | all-gather | bytes 4608 | tf_op jit(solution)/shard_map/all_gather | solution.py:76
  40.2 11.4 %while.26 = (s32[]{:T(128)}, f32[2,128,128]{2,1,0:T(8,128)S(1)}, s32[]{:T(128)}, s32[4]{0:T(128)S(1)}, bf16[4,128,128]{2,1,0:T(8,128)(2,1)S(1)}, /*index=5*/bf16...) while((s32[]{:T(128)}, f32[2,128,128]{2,1,0:T(8,128)S(1)}, ...), condition=%wide.region_2.3_spmd, body=%wide.region_0.2_spmd.sunk | while | flops 4227119 | bytes 197076 | solution.py:21
  44.0 0.7 and_reduce_fusion.4
  44.7 0.8 fusion.51
  49.4 0.7 and_reduce_fusion.4
  50.1 0.8 fusion.51
  52.6 0.8 copy-done.3
  54.4 2.7 %scatter_fusion = f32[256,128]{1,0:T(8,128)S(1)} fusion(f32[256,128]{1,0:T(8,128)S(1)} %copy.32, s32[384]{0:T(512)S(1)} %reshape.260, f32[384,128]{1,0:T(8,128)S(1)} %bitcast.117), kind=kCustom, calls=%fused_computation.3 | custom fusion | flops 49152 | bytes 591360 | tf_op jit(solution)/shard_map/scatter-add | solution.py:70
  57.4 0.8 copy.38
  59.7 23.2 %reduce-scatter.4.cloned.1.call-done = bf16[128,256]{1,0:T(8,128)(2,1)} async-done(((bf16[512,256]{1,0:T(8,128)(2,1)}), bf16[128,256]{1,0:T(8,128)(2,1)}) %reduce-scatter.4.cloned.1.call-update) | async-done | bytes 65552
  83.0 1.0 copy.39
  84.0 0.7 convert_reduce_fusion
  84.7 5.8 %all_gather.7 = bf16[256,512]{1,0:T(8,128)(2,1)S(1)} all-gather(bf16[256,128]{1,0:T(8,128)(2,1)S(1)} %get-tuple-element.241), channel_id=1, replica_groups=mesh['dom'=8,'feat'=4] {'feat'}, dimensions={1}, use_global_device_ids=true | all-gather | bytes 327680 | tf_op jit(solution)/shard_map/all_gather | solution.py:92
  90.7 1.0 fusion.23
  91.7 1.0 convolution_bitcast_fusion.2
  92.6 11.5 %while.27 = (s32[]{:T(128)}, f32[2,128,128]{2,1,0:T(8,128)S(1)}, s32[]{:T(128)}, s32[4]{0:T(128)S(1)}, bf16[4,128,128]{2,1,0:T(8,128)(2,1)S(1)}, /*index=5*/bf16...) while((s32[]{:T(128)}, f32[2,128,128]{2,1,0:T(8,128)S(1)}, ...), condition=%wide.region_7.8_spmd, body=%wide.region_5.7_spmd.sunk | while | flops 4227119 | bytes 197076 | solution.py:37
  96.5 0.7 and_reduce_fusion.5
  97.2 0.8 fusion.54
  101.9 0.7 and_reduce_fusion.5
  102.6 0.8 fusion.54
  104.3 1.4 gather_fusion.2
  105.8 0.8 fusion.20
  106.7 15.4 %all-to-all-start.1 = ((bf16[8,48,128]{2,1,0:T(8,128)(2,1)}), bf16[8,48,128]{2,1,0:T(8,128)(2,1)S(1)}, u32[]{:S(2)}, u32[]{:S(2)}) async-start(bf16[8,48,128]{2,1,0:T(8,128)(2,1)} %fusion.20), calls=%async_computation.1 | async-start | bytes 196608 | tf_op jit(solution)/shard_map/all_to_all | solution.py:119
  122.1 22.4 %all-reduce = (f32[16,128]{1,0:T(8,128)S(1)}, f32[128]{0:T(128)S(1)}) all-reduce(f32[16,128]{1,0:T(8,128)S(1)} %convolution_bitcast_fusion.4, f32[128]{0:T(128)S(1)} %get-tuple-element.240), channel_id=1, replica_groups=mesh['dom'=8,'feat'=4] {'dom'}, use_global_device_ids=true, to_apply=%region_9.10 | all-reduce | flops 2176 | bytes 17408 | tf_op jit(solution)/shard_map/psum | solution.py:128
  145.7 2.7 %scatter_custom_fusion.1 = f32[256,128]{1,0:T(8,128)S(1)} fusion(f32[256,128]{1,0:T(8,128)S(1)} %convolution_add_fusion.1, s32[384]{0:T(512)S(1)} %reshape.268, bf16[384,128]{1,0:T(8,128)(2,1)S(1)} %bitcast.118), kind=kCustom, calls=%fused_computation.34 | custom fusion | flops 98304 | bytes 229376 | tf_op jit(solution)/shard_map/scatter-add | solution.py:122
  149.0 41.9 %all-reduce.4.cloned.1.call-done = (f32[128,512]{0,1:T(8,128)}, f32[128,512]{0,1:T(8,128)}) async-done(((f32[128,512]{0,1:T(8,128)}, f32[128,512]{0,1:T(8,128)}), (f32[128,512]{0,1:T(8,128)}, f32[128,512]{0,1:T(8,128)})) %all-reduce.4.cloned.1.call-update) | async-done | bytes 524304 | tf_op jit(solution)/shard_map/psum | solution.py:133
  190.9 1.1 broadcast_multiply_fusion
  192.0 0.8 copy.35
  192.9 0.8 copy.34
  (63 shorter events, 10.0 us)
Async XLA Ops:
  7.2 50.0 %copy-start = (bf16[128,512]{1,0:T(8,128)(2,1)S(1)}, bf16[128,512]{1,0:T(8,128)(2,1)}, u32[]{:S(2)}) copy-start(bf16[128,512]{1,0:T(8,128)(2,1)} %param.24) | copy-start | bytes 393220
  10.5 7.5 %copy-start.13 = (s32[1,2]{1,0:T(1,128)S(1)}, s32[1,2]{1,0:T(1,128)}, u32[]{:S(2)}) copy-start(s32[1,2]{1,0:T(1,128)} %param.34) | copy-start | bytes 28
  10.5 7.5 %copy-start.8 = (s32[1,8,48]{2,1,0:T(8,128)S(1)}, s32[1,8,48]{2,1,0:T(8,128)}, u32[]{:S(2)}) copy-start(s32[1,8,48]{2,1,0:T(8,128)} %param.31) | copy-start | bytes 4612
  10.5 7.6 %copy-start.1 = (bf16[256,128]{1,0:T(8,128)(2,1)S(1)}, bf16[256,128]{1,0:T(8,128)(2,1)}, u32[]{:S(2)}) copy-start(bf16[256,128]{1,0:T(8,128)(2,1)} %param.22) | copy-start | bytes 196612
  10.5 43.8 %all-to-all-start = ((bf16[8,48,128]{2,1,0:T(8,128)(2,1)}), bf16[8,48,128]{2,1,0:T(8,128)(2,1)S(1)}, u32[]{:S(2)}, u32[]{:S(2)}) async-start(bf16[8,48,128]{2,1,0:T(8,128)(2,1)} %bitcast.21), calls=%async_computation | async-start | bytes 196608 | tf_op jit(solution)/shard_map/all_to_all | solution.py:68
  17.9 21.6 %copy-start.2 = (bf16[1,4,128,128]{3,2,1,0:T(8,128)(2,1)S(1)}, bf16[1,4,128,128]{3,2,1,0:T(8,128)(2,1)}, u32[]{:S(2)}) copy-start(bf16[1,4,128,128]{3,2,1,0:T(8,128)(2,1)} %param.27) | copy-start | bytes 393220
  17.9 65.0 %reduce-scatter.4.cloned.1.call-start = ((), (), s32[]{:S(2)}) async-start(), calls=%async_computation.3 | async-start | bytes 327680
  39.5 0.7 copy-start.5
  39.5 0.7 copy-start.12
  51.6 0.7 copy-start.6
  52.5 0.9 copy-start.3
  53.4 0.7 copy-start.9
  53.6 0.7 copy-start.10
  58.2 0.7 copy-start.7
  58.2 132.7 %all-reduce.4.cloned.1.call-start = ((), (), s32[]{:S(2)}) async-start(), calls=%async_computation.4 | async-start | bytes 1048576 | tf_op jit(solution)/shard_map/psum | solution.py:133
  59.0 0.7 copy-start.11
  83.0 1.0 copy-start.4
  106.7 39.0 %all-to-all-start.1 = ((bf16[8,48,128]{2,1,0:T(8,128)(2,1)}), bf16[8,48,128]{2,1,0:T(8,128)(2,1)S(1)}, u32[]{:S(2)}, u32[]{:S(2)}) async-start(bf16[8,48,128]{2,1,0:T(8,128)(2,1)} %fusion.20), calls=%async_computation.1 | async-start | bytes 196608 | tf_op jit(solution)/shard_map/all_to_all | solution.py:119
Sparse Core Ops, SparseCore 0:
  58.3 24.5 reduce-scatter.3
  106.7 84.1 all-reduce.3
where the time goes:
time: 202 us; the launch traced here: 201 us
  waiting for transfers between devices  65.2 us (32%)
  blocking collectives  49 us (24%)
  starting transfers between devices  22.9 us (11%)
  local copies, waits for them, and re-layouts  14.9 us (7%)
  loops' own time  14.5 us (7%)
  between operations  14.3 us (7%)
  other arithmetic  13.5 us (7%)
  matrix products  6.3 us (3%)
    psum x1, waiting for transfers between devices, on_device(): lax.psum((grad_self_part, grad_neigh_part, bias_part), 'dom')  41.9 us
    unnamed x3, waiting for transfers between devices  23.3 us
    psum x1, blocking collectives, on_device(): every_hub = lax.psum(hub_term, 'dom')  22.4 us
    all_gather x1, blocking collectives, on_device(): lax.all_gather(owned_rows, 'dom', axis=0, tiled=True)  20.8 us
    all_to_all x1, starting transfers between devices, on_device(): lax.all_to_all(returned.astype(jnp.bfloat16), 'dom', split_axis=0, concat...  15.4 us
    unnamed x32, local copies, waits for them, and re-layouts  7.48 us
    all_to_all x1, starting transfers between devices, on_device(): lax.all_to_all(outgoing, 'dom', split_axis=0, concat_axis=0, tiled=True)  7.42 us
    another operation x1, loops' own time, tile_forward(): lax.fori_loop(0, count_here, add_tile, jnp.zeros(blocks.shape, jnp.float32))  7.24 us
  transfers between devices with their start and end apart: 4, of which 2 were waited for; matrix products, arithmetic and copies ran while one was open for 5% of the time, Pallas kernels for 0%

commit v1 on v0

v1 whole, which is shorter than its diff:
```python
import functools
import math

import jax
import jax.numpy as jnp
from jax import lax
from jax.experimental import pallas as pl
from jax.experimental.pallas import tpu as pltpu
from jax.sharding import PartitionSpec as P

BF = jnp.bfloat16
F32 = jnp.float32


def spread_rows(table, width):
    peers, slots = table.shape
    lanes = peers * width
    lane = lax.broadcasted_iota(jnp.int32, (slots, lanes), 1)
    slot = lax.broadcasted_iota(jnp.int32, (slots, lanes), 0)
    place = jnp.where(lane % width == slot, 1.0, 0.0).astype(BF)
    wide = jnp.dot(table.astype(BF), place, preferred_element_type=F32)
    peer = lax.broadcasted_iota(jnp.int32, (peers, lanes), 0)
    at = lax.broadcasted_iota(jnp.int32, (peers, lanes), 1)
    return jnp.sum(jnp.where(at // width == peer, wide, 0.0), axis=0, keepdims=True)


def source_matrix(send, hubs, rows, width):
    peers, slots = send.shape
    hub_here = hubs.shape[1]
    lanes = peers * width
    lane = lax.broadcasted_iota(jnp.int32, (1, lanes), 1) % width
    index = spread_rows(send.astype(F32), width)
    for k in range(hub_here):
        index = jnp.where(lane == slots + k, hubs[0:1, k : k + 1].astype(F32), index)
    index = jnp.where(lane < slots + hub_here, index, -1.0)
    row = lax.broadcasted_iota(jnp.int32, (rows, lanes), 0).astype(F32)
    return jnp.where(row == index, 1.0, 0.0).astype(BF)


def send_kernel(width, x_ref, cot_ref, ws_ref, wn_ref, bias_ref, send_ref, hub_ref, out_ref, pack_ref):
    rows, cols = x_ref.shape
    depth, full = ws_ref.shape
    mark = source_matrix(send_ref[0], hub_ref[...], rows, width)
    taken = lax.dot_general(
        mark, x_ref[...], (((0,), (0,)), ((), ())), preferred_element_type=F32
    ).astype(BF)
    out_ref[...] = taken.reshape(out_ref.shape)
    blocks = full // cols
    for j in range(blocks):
        pack_ref[j * depth : (j + 1) * depth, :] = ws_ref[:, j * cols : (j + 1) * cols]
        pack_ref[(blocks + j) * depth : (blocks + j + 1) * depth, :] = wn_ref[:, j * cols : (j + 1) * cols]
    base = 2 * blocks * depth
    pack_ref[base : base + rows, :] = x_ref[...]
    pack_ref[base + rows : base + 2 * rows, :] = cot_ref[...]
    pack_ref[base + 2 * rows :, :] = jnp.broadcast_to(bias_ref[...], (16, cols))


def neigh_kernel(
    width, pos_ref, count_ref, live_ref, x_ref, got_ref, tile_ref, dest_ref, gw_ref, hw_ref, mix_ref, neigh_ref
):
    rows, cols = x_ref.shape
    tile = tile_ref.shape[-1]
    tiles = tile_ref.shape[1]
    peers, slots = dest_ref.shape[1:]
    side = rows // tile
    lanes = peers * width
    hubs = hw_ref.shape[1]
    hub_here = hubs // peers
    for r in range(side):
        for c in range(side):
            total = jnp.zeros((tile, tile), BF)
            for t in range(tiles):
                used = jnp.logical_and(pos_ref[0, t] == r * side + c, t < count_ref[0])
                total = jnp.where(used, tile_ref[0, t], total)
            mix_ref[r * tile : (r + 1) * tile, c * tile : (c + 1) * tile] = total
    dest = spread_rows(dest_ref[0].astype(F32), width)
    coef = spread_rows(gw_ref[0], width)
    lane = lax.broadcasted_iota(jnp.int32, (1, lanes), 1)
    limit = jnp.zeros((1, lanes), jnp.int32)
    for q in range(peers):
        limit = jnp.where(lane // width == q, live_ref[0, q], limit)
    coef = jnp.where(lane % width < jnp.minimum(limit, slots), coef, 0.0)
    row = lax.broadcasted_iota(jnp.int32, (rows, lanes), 0).astype(F32)
    ghost = jnp.where(row == dest, coef, 0.0)
    hub = lax.broadcasted_iota(jnp.int32, (hubs, lanes), 0)
    at = lax.broadcasted_iota(jnp.int32, (hubs, lanes), 1)
    place = jnp.where(
        jnp.logical_and(at // width == hub // hub_here, at % width == slots + hub % hub_here), 1.0, 0.0
    ).astype(BF)
    hub_mix = jnp.dot(hw_ref[...], place, preferred_element_type=F32)
    far = (ghost + hub_mix).astype(BF)
    mix_ref[:, rows:] = far
    total = jnp.dot(mix_ref[:, :rows], x_ref[...], preferred_element_type=F32)
    total = total + jnp.dot(far, got_ref[...].reshape(lanes, cols), preferred_element_type=F32)
    neigh_ref[...] = total.astype(BF)


def dense_kernel(
    slots, hub_here, me_ref, x_ref, ws_ref, wn_ref, p0_ref, p1_ref, p2_ref, p3_ref, n_ref, mix_ref,
    out_ref, back_ref, send_ref, pre_ref, cot_ref, bias_ref,
):
    rows, cols = x_ref.shape
    depth, full = ws_ref.shape
    blocks = full // cols
    peers, height = send_ref.shape[:2]
    lanes = mix_ref.shape[1] - rows
    width = lanes // peers
    me = me_ref[0]
    base = 2 * blocks * depth
    pre = jnp.zeros((rows, full), F32)
    for d, pack in enumerate((p0_ref, p1_ref, p2_ref, p3_ref)):
        owner = me ^ d
        cut = pl.ds(pl.multiple_of(owner * cols, cols), cols)
        cot_ref[:, cut] = pack[base + rows : base + 2 * rows, :]
        bias_ref[:, cut] = pack[base + 2 * rows : base + 2 * rows + 16, :]
        w_s = jnp.concatenate([pack[j * depth : (j + 1) * depth, :] for j in range(blocks)], axis=1)
        w_n = jnp.concatenate([pack[(blocks + j) * depth : (blocks + j + 1) * depth, :] for j in range(blocks)], axis=1)
        left = jnp.concatenate([pack[base : base + rows, :], n_ref[owner]], axis=1)
        right = jnp.concatenate([w_s, w_n], axis=0)
        pre = pre + jnp.dot(left, right, preferred_element_type=F32)
    pre = pre + bias_ref[0:1, :].astype(F32)
    pre_ref[...] = pre
    sig = jax.nn.sigmoid(pre)
    grad = (cot_ref[...].astype(F32) * sig * (1.0 + pre * (1.0 - sig))).astype(BF)
    cot_ref[...] = grad
    mine = pl.ds(pl.multiple_of(me * cols, cols), cols)
    own = pre_ref[:, mine]
    out_ref[...] = (own * jax.nn.sigmoid(own)).astype(BF)
    both = jnp.concatenate([ws_ref[...], wn_ref[...]], axis=0)
    into = lax.dot_general(grad, both, (((1,), (1,)), ((), ())), preferred_element_type=F32)
    neigh_grad = into[:, depth:].astype(BF)
    spread = lax.dot_general(
        mix_ref[...], neigh_grad, (((0,), (0,)), ((), ())), preferred_element_type=F32
    )
    back_ref[...] = into[:, :depth] + spread[:rows]
    sums = jnp.sum(cot_ref[:, mine].astype(F32), axis=0, keepdims=True)
    high = sums.astype(BF).astype(F32)
    line = lax.broadcasted_iota(jnp.int32, (lanes, cols), 0) % width
    away = jnp.where(line == slots + hub_here, high, spread[rows:])
    away = jnp.where(line == slots + hub_here + 1, sums - high, away)
    send_ref[:, :width, :] = away.astype(BF).reshape(peers, width, cols)
    pair = jnp.concatenate([x_ref[...], n_ref[me]], axis=1)
    weights = lax.dot_general(pair, grad, (((0,), (0,)), ((), ())), preferred_element_type=F32).astype(BF)
    share = height - width
    for j in range(blocks):
        for kind in range(2):
            block = weights[kind * depth : (kind + 1) * depth, j * cols : (j + 1) * cols]
            at = (j * 2 + kind) * depth
            for part in range(depth // share):
                send_ref[at // share + part, width:, :] = block[part * share : (part + 1) * share]


def gather_kernel(scale, slots, width, got_ref, back_ref, send_ref, hub_ref, grad_ref, bias_ref, part_ref):
    rows, cols = back_ref.shape
    peers = got_ref.shape[0]
    hub_here = hub_ref.shape[1]
    mark = source_matrix(send_ref[0], hub_ref[...], rows, width)
    near = got_ref[:, :width, :]
    total = back_ref[...] + jnp.dot(mark, near.reshape(peers * width, cols), preferred_element_type=F32)
    grad_ref[...] = total.astype(BF)
    first = slots + hub_here
    bias = jnp.zeros((2, cols), F32)
    share = jnp.zeros(part_ref.shape[1:], F32)
    for q in range(peers):
        bias = bias + got_ref[q, first : first + 2, :].astype(F32)
        share = share + got_ref[q, width:, :].astype(F32)
    bias_ref[...] = jnp.sum(bias, axis=0, keepdims=True) * scale
    part_ref[...] = jnp.broadcast_to(share.astype(BF), part_ref.shape)


def spread_kernel(scale, got_ref, self_ref, neigh_ref):
    depth, full = self_ref.shape
    peers, share, cols = got_ref.shape
    whole = got_ref[...].reshape(peers * share, cols).astype(F32) * scale
    for j in range(full // cols):
        at = 2 * j * depth
        self_ref[:, j * cols : (j + 1) * cols] = whole[at : at + depth]
        neigh_ref[:, j * cols : (j + 1) * cols] = whole[at + depth : at + 2 * depth]


VMEM = pl.BlockSpec(memory_space=pltpu.VMEM)
SMEM = pl.BlockSpec(memory_space=pltpu.SMEM)
PARAMS = pltpu.CompilerParams(vmem_limit_bytes=40 * 1024 * 1024)


def shape(dims, kind):
    return jax.ShapeDtypeStruct(dims, kind)


def on_device(
    features,
    w_self,
    w_neigh,
    bias,
    cotangent,
    tile_vals,
    tile_pos,
    tile_count,
    send_rows,
    recv_dest,
    ghost_weight,
    recv_count,
    hub_rows,
    hub_weight,
):
    rows, cols = features.shape
    depth, full = w_self.shape
    blocks = full // cols
    peers, slots = send_rows.shape[1:]
    hub_here = hub_rows.shape[-1]
    width = -(-(slots + hub_here + 2) // 16) * 16
    lanes = peers * width
    share = 2 * blocks * depth // peers
    scale = 1.0 / math.sqrt(peers * rows)
    feats = lax.axis_size("feat")
    me = lax.axis_index("feat").astype(jnp.int32).reshape(1)

    outgoing, pack = pl.pallas_call(
        functools.partial(send_kernel, width),
        out_shape=(
            shape((peers, width, cols), BF),
            shape((2 * blocks * depth + 2 * rows + 16, cols), BF),
        ),
        in_specs=[VMEM] * 7,
        out_specs=(VMEM, VMEM),
        compiler_params=PARAMS,
    )(features, cotangent, w_self, w_neigh, bias.reshape(1, cols), send_rows, hub_rows)

    far = lax.ppermute(pack, "feat", [(i, i ^ 2) for i in range(feats)])
    near = lax.ppermute(pack, "feat", [(i, i ^ 1) for i in range(feats)])
    last = lax.ppermute(far, "feat", [(i, i ^ 1) for i in range(feats)])

    incoming = lax.all_to_all(outgoing, "dom", split_axis=0, concat_axis=0, tiled=True)
    mix, neigh = pl.pallas_call(
        functools.partial(neigh_kernel, width),
        out_shape=(shape((rows, rows + lanes), BF), shape((rows, cols), BF)),
        in_specs=[SMEM] * 3 + [VMEM] * 6,
        out_specs=(VMEM, VMEM),
        compiler_params=PARAMS,
    )(tile_pos, tile_count, recv_count, features, incoming, tile_vals, recv_dest, ghost_weight, hub_weight)
    every = lax.all_gather(neigh, "feat", axis=0, tiled=False)

    output, back, returned = pl.pallas_call(
        functools.partial(dense_kernel, slots, hub_here),
        out_shape=(
            shape((rows, cols), BF),
            shape((rows, cols), F32),
            shape((peers, width + share, cols), BF),
        ),
        in_specs=[SMEM] + [VMEM] * 9,
        out_specs=(VMEM,) * 3,
        scratch_shapes=[
            pltpu.VMEM((rows, full), F32),
            pltpu.VMEM((rows, full), BF),
            pltpu.VMEM((16, full), BF),
        ],
        compiler_params=PARAMS,
    )(me, features, w_self, w_neigh, pack, near, far, last, every, mix)

    arrived = lax.all_to_all(returned, "dom", split_axis=0, concat_axis=0, tiled=True)
    grad_features, grad_bias, parts = pl.pallas_call(
        functools.partial(gather_kernel, scale, slots, width),
        out_shape=(
            shape((rows, cols), BF),
            shape((1, cols), F32),
            shape((peers, share, cols), BF),
        ),
        in_specs=[VMEM] * 4,
        out_specs=(VMEM,) * 3,
        compiler_params=PARAMS,
    )(arrived, back, send_rows, hub_rows)
    whole = lax.all_to_all(parts, "dom", split_axis=0, concat_axis=0, tiled=True)
    grad_self, grad_neigh = pl.pallas_call(
        functools.partial(spread_kernel, scale),
        out_shape=(shape((depth, full), F32), shape((depth, full), F32)),
        in_specs=[VMEM],
        out_specs=(VMEM, VMEM),
        compiler_params=PARAMS,
    )(whole)
    return output, grad_features, grad_self, grad_neigh, grad_bias.reshape(cols)


def solution(mesh):
    placed = (
        P("dom", "feat"),
        P("feat", None),
        P("feat", None),
        P("feat"),
        P("dom", "feat"),
        P("dom", None, None, None),
        P("dom", None),
        P("dom"),
        P("dom", None, None),
        P("dom", None, None),
        P("dom", None, None),
        P("dom", None),
        P("dom", None),
        P("dom", None),
    )
    return jax.shard_map(
        on_device,
        mesh=mesh,
        in_specs=placed,
        out_specs=(P("dom", "feat"), P("dom", "feat"), P("feat", None), P("feat", None), P("feat")),
        check_vma=False,
    )
```

time: 202 us -> 70.6 us (0.35)
  waiting for transfers between devices: 65.2 us -> 16 us
  blocking collectives: 49 us -> 33.4 us
  loops' own time: 14.5 us -> 0 us
  starting transfers between devices: 22.9 us -> 9.17 us
  other arithmetic: 13.5 us -> 0 us
  between operations: 14.3 us -> 1.45 us
  local copies, waits for them, and re-layouts: 14.9 us -> 5 us
  matrix products: 6.3 us -> 0 us
  Pallas kernels: 0 us -> 5.08 us
    psum x1 -> x0, waiting for transfers between devices: 41.9 us -> none  [on_device(): lax.psum((grad_self_part, grad_neigh_part, bias_part), 'dom')]
    all_to_all x0 -> x2, blocking collectives: none -> 27.5 us  [the longest x1 15.4 us: on_device(): lax.all_to_all(returned, 'dom', split_axis=0, concat_axis=0, tiled=True)]
    unnamed x3 -> x0, waiting for transfers between devices: 23.3 us -> none
    psum x1 -> x0, blocking collectives: 22.4 us -> none  [on_device(): every_hub = lax.psum(hub_term, 'dom')]
    all_gather x2 -> x1, blocking collectives: 26.6 us -> 5.92 us  [on_device(): every = lax.all_gather(neigh, 'feat', axis=0, tiled=False)]
    all_to_all x1 -> x0, starting transfers between devices: 15.4 us -> none  [on_device(): lax.all_to_all(returned.astype(jnp.bfloat16), 'dom', split_axis=0, concat...]
    another operation x2 -> x0, loops' own time: 14.5 us -> none  [the longest x1 7.24 us: tile_forward(): lax.fori_loop(0, count_here, add_tile, jnp.zeros(blocks.shape, jnp.float32))]
    ppermute x0 -> x3, waiting for transfers between devices: none -> 9.2 us  [the longest x1 9.19 us: on_device(): far = lax.ppermute(pack, 'feat', [(i, i ^ 2) for i in range(feats)])]
  transfers between devices with their start and end apart: 4 -> 4, of which waited for: 2 -> 2; matrix products, arithmetic and copies ran while one was open for 5% -> 0% of each run, Pallas kernels for 0% -> 1%
where the time goes in v1:
time: 70.6 us; the launch traced here: 70.1 us
  blocking collectives  33.4 us (47%)
  waiting for transfers between devices  16 us (23%)
  starting transfers between devices  9.17 us (13%)
  Pallas kernels  5.08 us (7%)
  local copies, waits for them, and re-layouts  5 us (7%)
  between operations  1.45 us (2%)
    all_to_all x1, blocking collectives, on_device(): lax.all_to_all(returned, 'dom', split_axis=0, concat_axis=0, tiled=True)  15.4 us
    all_to_all x1, blocking collectives, on_device(): lax.all_to_all(parts, 'dom', split_axis=0, concat_axis=0, tiled=True)  12.2 us
    ppermute x1, waiting for transfers between devices, on_device(): far = lax.ppermute(pack, 'feat', [(i, i ^ 2) for i in range(feats)])  9.19 us
    all_to_all x1, waiting for transfers between devices, on_device(): lax.all_to_all(outgoing, 'dom', split_axis=0, concat_axis=0, tiled=True)  6.78 us
    all_to_all x1, starting transfers between devices, on_device(): lax.all_to_all(outgoing, 'dom', split_axis=0, concat_axis=0, tiled=True)  6.23 us
    all_gather x1, blocking collectives, on_device(): every = lax.all_gather(neigh, 'feat', axis=0, tiled=False)  5.92 us
    unnamed x35, local copies, waits for them, and re-layouts  5 us
    ppermute x1, starting transfers between devices, on_device(): far = lax.ppermute(pack, 'feat', [(i, i ^ 2) for i in range(feats)])  2.94 us
  transfers between devices with their start and end apart: 4, of which 2 were waited for; matrix products, arithmetic and copies ran while one was open for 0% of the time, Pallas kernels for 1%

profile of v1, /device:TPU:0, one launch (start us, length us, event | category | flops | bytes accessed | tf_op | source)
XLA Modules:
  0.0 70.1 jit_solution(2130444727501059477)
XLA Ops:
  0.7 0.6 copy-done.12
  1.3 0.0 copy-done.13
  1.3 0.8 %copy-done = bf16[256,128]{1,0:T(8,128)(2,1)S(1)} copy-done((bf16[256,128]{1,0:T(8,128)(2,1)S(1)}, bf16[256,128]{1,0:T(8,128)(2,1)}, u32[]{:S(2)}) %copy-start) | copy-done | bytes 65560
  2.1 0.9 %copy-done.2 = bf16[128,512]{1,0:T(8,128)(2,1)S(1)} copy-done((bf16[128,512]{1,0:T(8,128)(2,1)S(1)}, bf16[128,512]{1,0:T(8,128)(2,1)}, u32[]{:S(2)}) %copy-start.2) | copy-done | bytes 131096
  3.1 0.9 %copy-done.4 = bf16[128,512]{1,0:T(8,128)(2,1)S(1)} copy-done((bf16[128,512]{1,0:T(8,128)(2,1)S(1)}, bf16[128,512]{1,0:T(8,128)(2,1)}, u32[]{:S(2)}) %copy-start.4) | copy-done | bytes 131096
  4.0 0.8 %copy-done.7 = bf16[256,128]{1,0:T(8,128)(2,1)S(1)} copy-done((bf16[256,128]{1,0:T(8,128)(2,1)S(1)}, bf16[256,128]{1,0:T(8,128)(2,1)}, u32[]{:S(2)}) %copy-start.7) | copy-done | bytes 65560
  4.8 0.7 copy-done.8
  5.5 1.1 %shard_map.173 = (bf16[8,64,128]{2,1,0:T(8,128)(2,1)}, bf16[1552,128]{1,0:T(8,128)(2,1)S(1)}) custom-call(bf16[256,128]{1,0:T(8,128)(2,1)S(1)} %copy-done, bf16[256,128]{1,0:T(8,128)(2,1)S(1)} %copy-done.7, bf16[128,512]{1,0:T(8,128)(2,1)S(1)} %copy-done.2, bf16[128,512]{1,0:T(8,128)(2,1)S(1)} %copy-done.4, bf16[1,128]{1,0:T(2,128)(2,1)S(1)} %bitcast.5, ...), custom_call_target="tpu_custom_call" | custom-call | tf_op jit(solution)/shard_map/pallas_call | solution.py:218
  6.5 2.9 %collective-permute-start.1 = (bf16[1552,128]{1,0:T(8,128)(2,1)S(1)}, bf16[1552,128]{1,0:T(8,128)(2,1)S(1)}, u32[]{:S(2)}, u32[]{:S(2)}) collective-permute-start(bf16[1552,128]{1,0:T(8,128)(2,1)S(1)} %get-tuple-element.17.p0_ref), channel_id=1, source_target_pairs={{0,2},{1,3},{2,0},{3,1},{4,6},{5,7},{6,4},{7,5},{8,10},{9,11},{10,... | collective-permute-start | bytes 1191944 | tf_op jit(solution)/shard_map/ppermute | solution.py:229
  9.5 0.0 collective-permute-start
  9.5 9.2 %collective-permute-done.1.p2_ref = bf16[1552,128]{1,0:T(8,128)(2,1)S(1)} collective-permute-done((bf16[1552,128]{1,0:T(8,128)(2,1)S(1)}, bf16[1552,128]{1,0:T(8,128)(2,1)S(1)}, u32[]{:S(2)}, u32[]{:S(2)}) %collective-permute-start.1) | collective-permute-done | bytes 397344 | tf_op jit(solution)/shard_map/ppermute | solution.py:229
  18.7 0.0 collective-permute-start.2
  18.7 6.2 %all-to-all-start = ((bf16[8,64,128]{2,1,0:T(8,128)(2,1)}), bf16[8,64,128]{2,1,0:T(8,128)(2,1)S(1)}, u32[]{:S(2)}, u32[]{:S(2)}) async-start(bf16[8,64,128]{2,1,0:T(8,128)(2,1)} %get-tuple-element.18), calls=%async_computation | async-start | bytes 262144 | tf_op jit(solution)/shard_map/all_to_all | solution.py:233
  25.6 0.0 copy-start.10
  25.6 0.0 copy-start.11
  25.6 0.0 copy-start.14
  25.7 0.0 copy-start.15
  25.7 0.1 copy.19.hw_ref
  25.8 6.8 %all-to-all-done.got_ref = bf16[8,64,128]{2,1,0:T(8,128)(2,1)S(1)} async-done(((bf16[8,64,128]{2,1,0:T(8,128)(2,1)}), bf16[8,64,128]{2,1,0:T(8,128)(2,1)S(1)}, u32[]{:S(2)}, u32[]{:S(2)}) %all-to-all-start) | async-done | bytes 131104 | tf_op jit(solution)/shard_map/all_to_all | solution.py:233
  32.6 0.0 copy-done.6
  32.6 0.0 copy-done.10
  32.6 1.0 %shard_map.174 = (bf16[256,768]{1,0:T(8,128)(2,1)S(1)}, bf16[256,128]{1,0:T(8,128)(2,1)S(1)}) custom-call(s32[1,4]{1,0:T(1,128)S(1)} %copy-done.14, s32[1]{0:T(128)S(6)} %copy.20.count_ref, s32[1,8]{1,0:T(1,128)S(1)} %copy-done.15, bf16[256,128]{1,0:T(8,128)(2,1)S(1)} %copy-done.1, bf16[8,64,128]{2,1,0:T(8,128)(2,1)S(1)} %all-to-all-done.got_ref, ...), custom_call_target="tpu_custom_call" | custom-call | tf_op jit(solution)/shard_map/pallas_call | solution.py:234
  33.6 0.0 copy-start.3
  33.6 0.0 copy-start.5
  33.6 5.9 %all-gather = bf16[1024,128]{1,0:T(8,128)(2,1)S(1)} all-gather(bf16[256,128]{1,0:T(8,128)(2,1)S(1)} %get-tuple-element.19), channel_id=2, replica_groups=mesh['dom'=8,'feat'=4] {'feat'}, dimensions={0}, use_global_device_ids=true | all-gather | bytes 327680 | tf_op jit(solution)/shard_map/all_gather | solution.py:241
  39.5 0.0 collective-permute-done.p1_ref
  39.5 0.0 collective-permute-done.2.p3_ref
  39.5 1.2 %shard_map.175 = (bf16[256,128]{1,0:T(8,128)(2,1)}, f32[256,128]{1,0:T(8,128)S(1)}, bf16[8,192,128]{2,1,0:T(8,128)(2,1)S(1)}) custom-call(s32[1]{0:T(128)} %bitcast.me_ref, bf16[256,128]{1,0:T(8,128)(2,1)S(1)} %copy-done.1, bf16[128,512]{1,0:T(8,128)(2,1)S(1)} %copy-done.3, bf16[128,512]{1,0:T(8,128)(2,1)S(1)} %copy-done.5, ...), custom_call_target="tpu_custom_call" | custom-call | tf_op jit(solution)/shard_map/pallas_call | solution.py:243
  40.8 15.4 %all_to_all.15.got_ref = bf16[8,192,128]{2,1,0:T(8,128)(2,1)S(1)} all-to-all(bf16[8,192,128]{2,1,0:T(8,128)(2,1)S(1)} %get-tuple-element.22), channel_id=1, replica_groups=mesh['dom'=8,'feat'=4] {'dom'}, dimensions={0} | all-to-all | bytes 786432 | tf_op jit(solution)/shard_map/all_to_all | solution.py:260
  56.1 1.0 %shard_map.176 = (bf16[256,128]{1,0:T(8,128)(2,1)}, f32[1,128]{1,0:T(1,128)}, bf16[8,128,128]{2,1,0:T(8,128)(2,1)S(1)}) custom-call(bf16[8,192,128]{2,1,0:T(8,128)(2,1)S(1)} %all_to_all.15.got_ref, f32[256,128]{1,0:T(8,128)S(1)} %get-tuple-element.23.back_ref, s32[1,8,48]{2,1,0:T(8,128)S(1)} %copy-done.9, s32[1,2]{1,0:T(1,128)S(1)} %copy-done.12), custom_call_target="tpu_custom_call" | custom-call | tf_op jit(solution)/shard_map/pallas_call | solution.py:261
  57.1 12.2 %all_to_all.16.got_ref = bf16[8,128,128]{2,1,0:T(8,128)(2,1)S(1)} all-to-all(bf16[8,128,128]{2,1,0:T(8,128)(2,1)S(1)} %get-tuple-element.25), channel_id=1, replica_groups=mesh['dom'=8,'feat'=4] {'dom'}, dimensions={0} | all-to-all | bytes 524288 | tf_op jit(solution)/shard_map/all_to_all | solution.py:272
  69.3 0.9 %shard_map.177 = (f32[128,512]{1,0:T(8,128)}, f32[128,512]{1,0:T(8,128)}) custom-call(bf16[8,128,128]{2,1,0:T(8,128)(2,1)S(1)} %all_to_all.16.got_ref), custom_call_target="tpu_custom_call" | custom-call | tf_op jit(solution)/shard_map/pallas_call | solution.py:273
  (19 shorter events, 0.0 us)
Async XLA Ops:
  0.6 0.7 copy-start.12
  0.6 0.7 copy-start.13
  1.3 0.8 %copy-start = (bf16[256,128]{1,0:T(8,128)(2,1)S(1)}, bf16[256,128]{1,0:T(8,128)(2,1)}, u32[]{:S(2)}) copy-start(bf16[256,128]{1,0:T(8,128)(2,1)} %x_ref.5) | copy-start | bytes 196612
  2.1 0.9 %copy-start.2 = (bf16[128,512]{1,0:T(8,128)(2,1)S(1)}, bf16[128,512]{1,0:T(8,128)(2,1)}, u32[]{:S(2)}) copy-start(bf16[128,512]{1,0:T(8,128)(2,1)} %ws_ref.3) | copy-start | bytes 393220
  3.0 0.9 %copy-start.4 = (bf16[128,512]{1,0:T(8,128)(2,1)S(1)}, bf16[128,512]{1,0:T(8,128)(2,1)}, u32[]{:S(2)}) copy-start(bf16[128,512]{1,0:T(8,128)(2,1)} %wn_ref.3) | copy-start | bytes 393220
  4.0 0.8 %copy-start.7 = (bf16[256,128]{1,0:T(8,128)(2,1)S(1)}, bf16[256,128]{1,0:T(8,128)(2,1)}, u32[]{:S(2)}) copy-start(bf16[256,128]{1,0:T(8,128)(2,1)} %cot_ref.1) | copy-start | bytes 196612
  4.8 0.7 copy-start.8
  6.5 12.1 %collective-permute-start.1 = (bf16[1552,128]{1,0:T(8,128)(2,1)S(1)}, bf16[1552,128]{1,0:T(8,128)(2,1)S(1)}, u32[]{:S(2)}, u32[]{:S(2)}) collective-permute-start(bf16[1552,128]{1,0:T(8,128)(2,1)S(1)} %get-tuple-element.17.p0_ref), channel_id=1, source_target_pairs={{0,2},{1,3},{2,0},{3,1},{4,6},{5,7},{6,4},{7,5},{8,10},{9,11},{10,... | collective-permute-start | bytes 1191944 | tf_op jit(solution)/shard_map/ppermute | solution.py:229
  9.5 30.0 %collective-permute-start = (bf16[1552,128]{1,0:T(8,128)(2,1)S(1)}, bf16[1552,128]{1,0:T(8,128)(2,1)S(1)}, u32[]{:S(2)}, u32[]{:S(2)}) collective-permute-start(bf16[1552,128]{1,0:T(8,128)(2,1)S(1)} %get-tuple-element.17.p0_ref), channel_id=1, source_target_pairs={{0,1},{1,0},{2,3},{3,2},{4,5},{5,4},{6,7},{7,6},{8,9},{9,8},{10,11... | collective-permute-start | bytes 1191944 | tf_op jit(solution)/shard_map/ppermute | solution.py:230
  18.7 20.8 %collective-permute-start.2 = (bf16[1552,128]{1,0:T(8,128)(2,1)S(1)}, bf16[1552,128]{1,0:T(8,128)(2,1)S(1)}, u32[]{:S(2)}, u32[]{:S(2)}) collective-permute-start(bf16[1552,128]{1,0:T(8,128)(2,1)S(1)} %collective-permute-done.1.p2_ref), channel_id=1, source_target_pairs={{0,1},{1,0},{2,3},{3,2},{4,5},{5,4},{6,7},{7,6},{8,9},{9,8},{10,11... | collective-permute-start | bytes 1191944 | tf_op jit(solution)/shard_map/ppermute | solution.py:231
  18.7 6.9 %copy-start.16 = (bf16[256,16]{0,1:T(8,128)(2,1)S(1)}, bf16[256,16]{0,1:T(8,128)(2,1)}, u32[]{:S(2)}) copy-start(bf16[256,16]{0,1:T(8,128)(2,1)} %param.27) | copy-start | bytes 24580
  18.7 13.9 %copy-start.6 = (bf16[1,4,128,128]{3,2,1,0:T(8,128)(2,1)S(1)}, bf16[1,4,128,128]{3,2,1,0:T(8,128)(2,1)}, u32[]{:S(2)}) copy-start(bf16[1,4,128,128]{3,2,1,0:T(8,128)(2,1)} %tile_ref.1) | copy-start | bytes 393220
  18.7 13.9 %all-to-all-start = ((bf16[8,64,128]{2,1,0:T(8,128)(2,1)}), bf16[8,64,128]{2,1,0:T(8,128)(2,1)S(1)}, u32[]{:S(2)}, u32[]{:S(2)}) async-start(bf16[8,64,128]{2,1,0:T(8,128)(2,1)} %get-tuple-element.18), calls=%async_computation | async-start | bytes 262144 | tf_op jit(solution)/shard_map/all_to_all | solution.py:233
  24.9 7.7 %copy-start.1 = (bf16[256,128]{1,0:T(8,128)(2,1)S(1)}, bf16[256,128]{1,0:T(8,128)(2,1)}, u32[]{:S(2)}) copy-start(bf16[256,128]{1,0:T(8,128)(2,1)} %x_ref.5) | copy-start | bytes 196612
  25.6 7.0 %copy-start.10 = (s32[1,8,48]{2,1,0:T(8,128)S(1)}, s32[1,8,48]{2,1,0:T(8,128)}, u32[]{:S(2)}) copy-start(s32[1,8,48]{2,1,0:T(8,128)} %dest_ref.1) | copy-start | bytes 4612
  25.6 7.0 %copy-start.11 = (f32[1,8,48]{2,1,0:T(8,128)S(1)}, f32[1,8,48]{2,1,0:T(8,128)}, u32[]{:S(2)}) copy-start(f32[1,8,48]{2,1,0:T(8,128)} %gw_ref.1) | copy-start | bytes 4612
  25.6 6.9 %copy-start.14 = (s32[1,4]{1,0:T(1,128)S(1)}, s32[1,4]{1,0:T(1,128)}, u32[]{:S(2)}) copy-start(s32[1,4]{1,0:T(1,128)} %pos_ref.1) | copy-start | bytes 52
  25.7 6.9 %copy-start.15 = (s32[1,8]{1,0:T(1,128)S(1)}, s32[1,8]{1,0:T(1,128)}, u32[]{:S(2)}) copy-start(s32[1,8]{1,0:T(1,128)} %live_ref.1) | copy-start | bytes 100
  33.6 6.0 %copy-start.3 = (bf16[128,512]{1,0:T(8,128)(2,1)S(1)}, bf16[128,512]{1,0:T(8,128)(2,1)}, u32[]{:S(2)}) copy-start(bf16[128,512]{1,0:T(8,128)(2,1)} %ws_ref.3) | copy-start | bytes 393220
  33.6 5.9 %copy-start.5 = (bf16[128,512]{1,0:T(8,128)(2,1)S(1)}, bf16[128,512]{1,0:T(8,128)(2,1)}, u32[]{:S(2)}) copy-start(bf16[128,512]{1,0:T(8,128)(2,1)} %wn_ref.3) | copy-start | bytes 393220
  40.8 15.4 %copy-start.9 = (s32[1,8,48]{2,1,0:T(8,128)S(1)}, s32[1,8,48]{2,1,0:T(8,128)}, u32[]{:S(2)}) copy-start(s32[1,8,48]{2,1,0:T(8,128)} %send_ref.3) | copy-start | bytes 4612

commit v2 on v1

--- a/solution.py
+++ b/solution.py
@@ -37,27 +37,58 @@
     return jnp.where(row == index, 1.0, 0.0).astype(BF)
 
 
-def send_kernel(width, x_ref, cot_ref, ws_ref, wn_ref, bias_ref, send_ref, hub_ref, out_ref, pack_ref):
+def ordered(refs, hold_ref, me):
+    if len(refs) == 1:
+        return refs[0]
+    for k, ref in enumerate(refs):
+        hold_ref[me ^ k] = ref[...]
+    return hold_ref
+
+
+def routed(refs, hold_ref, me):
+    if len(refs) > 1:
+        for k, ref in enumerate(refs):
+            ref[...] = hold_ref[me ^ k]
+
+
+def send_kernel(width, count, me_ref, *refs):
+    x_ref, cot_ref, ws_ref, wn_ref, bias_ref, send_ref, hub_ref = refs[:7]
+    out_refs, pack_ref = refs[7 : 7 + count], refs[7 + count]
+    hold_ref, send_v, hub_v, bias_v, sems = refs[8 + count :]
     rows, cols = x_ref.shape
     depth, full = ws_ref.shape
-    mark = source_matrix(send_ref[0], hub_ref[...], rows, width)
+    blocks = full // cols
+    base = 2 * blocks * depth
+    moves = [
+        (send_ref, send_v),
+        (hub_ref, hub_v),
+        (x_ref, pack_ref.at[base : base + rows, :]),
+        (bias_ref, bias_v),
+        (cot_ref, pack_ref.at[base + rows : base + 2 * rows, :]),
+    ]
+    for kind, w_ref in enumerate((ws_ref, wn_ref)):
+        for j in range(blocks):
+            at = (kind * blocks + j) * depth
+            moves.append((w_ref.at[:, j * cols : (j + 1) * cols], pack_ref.at[at : at + depth, :]))
+    copies = [pltpu.make_async_copy(src, dst, sems.at[i]) for i, (src, dst) in enumerate(moves)]
+    for copy in copies:
+        copy.start()
+    for copy in copies[:3]:
+        copy.wait()
+    mark = source_matrix(send_v[0], hub_v[...], rows, width)
     taken = lax.dot_general(
-        mark, x_ref[...], (((0,), (0,)), ((), ())), preferred_element_type=F32
+        mark, pack_ref[base : base + rows, :], (((0,), (0,)), ((), ())), preferred_element_type=F32
     ).astype(BF)
-    out_ref[...] = taken.reshape(out_ref.shape)
-    blocks = full // cols
-    for j in range(blocks):
-        pack_ref[j * depth : (j + 1) * depth, :] = ws_ref[:, j * cols : (j + 1) * cols]
-        pack_ref[(blocks + j) * depth : (blocks + j + 1) * depth, :] = wn_ref[:, j * cols : (j + 1) * cols]
-    base = 2 * blocks * depth
-    pack_ref[base : base + rows, :] = x_ref[...]
-    pack_ref[base + rows : base + 2 * rows, :] = cot_ref[...]
-    pack_ref[base + 2 * rows :, :] = jnp.broadcast_to(bias_ref[...], (16, cols))
-
-
-def neigh_kernel(
-    width, pos_ref, count_ref, live_ref, x_ref, got_ref, tile_ref, dest_ref, gw_ref, hw_ref, mix_ref, neigh_ref
-):
+    target = out_refs[0] if count == 1 else hold_ref
+    target[...] = taken.reshape(target.shape)
+    routed(out_refs, hold_ref, me_ref[0])
+    for copy in copies[3:]:
+        copy.wait()
+    pack_ref[base + 2 * rows :, :] = jnp.broadcast_to(bias_v[...], (16, cols))
+
+
+def neigh_kernel(width, me_ref, pos_ref, count_ref, live_ref, x_ref, tile_ref, dest_ref, gw_ref, hw_ref, far_ref, *refs):
+    got_refs, (mix_ref, neigh_ref, passed_ref, hold_ref) = refs[:-4], refs[-4:]
     rows, cols = x_ref.shape
     tile = tile_ref.shape[-1]
     tiles = tile_ref.shape[1]
@@ -90,15 +121,18 @@
     hub_mix = jnp.dot(hw_ref[...], place, preferred_element_type=F32)
     far = (ghost + hub_mix).astype(BF)
     mix_ref[:, rows:] = far
+    near = ordered(got_refs, hold_ref, me_ref[0])[...]
     total = jnp.dot(mix_ref[:, :rows], x_ref[...], preferred_element_type=F32)
-    total = total + jnp.dot(far, got_ref[...].reshape(lanes, cols), preferred_element_type=F32)
+    total = total + jnp.dot(far, near.reshape(lanes, cols), preferred_element_type=F32)
     neigh_ref[...] = total.astype(BF)
 
 
-def dense_kernel(
-    slots, hub_here, me_ref, x_ref, ws_ref, wn_ref, p0_ref, p1_ref, p2_ref, p3_ref, n_ref, mix_ref,
-    out_ref, back_ref, send_ref, pre_ref, cot_ref, bias_ref,
-):
+def dense_kernel(slots, hub_here, feats, count, dom_ref, me_ref, x_ref, ws_ref, wn_ref, mix_ref, *refs):
+    pack_refs, n_refs = refs[:feats], refs[feats : 2 * feats]
+    out_ref, back_ref = refs[2 * feats : 2 * feats + 2]
+    send_refs = refs[2 * feats + 2 : 2 * feats + 2 + count]
+    hold_ref, pre_ref, cot_ref, bias_ref = refs[2 * feats + 2 + count :]
+    send_ref = send_refs[0] if count == 1 else hold_ref
     rows, cols = x_ref.shape
     depth, full = ws_ref.shape
     blocks = full // cols
@@ -108,14 +142,14 @@
     me = me_ref[0]
     base = 2 * blocks * depth
     pre = jnp.zeros((rows, full), F32)
-    for d, pack in enumerate((p0_ref, p1_ref, p2_ref, p3_ref)):
+    for d, pack in enumerate(pack_refs):
         owner = me ^ d
         cut = pl.ds(pl.multiple_of(owner * cols, cols), cols)
         cot_ref[:, cut] = pack[base + rows : base + 2 * rows, :]
         bias_ref[:, cut] = pack[base + 2 * rows : base + 2 * rows + 16, :]
         w_s = jnp.concatenate([pack[j * depth : (j + 1) * depth, :] for j in range(blocks)], axis=1)
         w_n = jnp.concatenate([pack[(blocks + j) * depth : (blocks + j + 1) * depth, :] for j in range(blocks)], axis=1)
-        left = jnp.concatenate([pack[base : base + rows, :], n_ref[owner]], axis=1)
+        left = jnp.concatenate([pack[base : base + rows, :], n_refs[d][...]], axis=1)
         right = jnp.concatenate([w_s, w_n], axis=0)
         pre = pre + jnp.dot(left, right, preferred_element_type=F32)
     pre = pre + bias_ref[0:1, :].astype(F32)
@@ -139,7 +173,7 @@
     away = jnp.where(line == slots + hub_here, high, spread[rows:])
     away = jnp.where(line == slots + hub_here + 1, sums - high, away)
     send_ref[:, :width, :] = away.astype(BF).reshape(peers, width, cols)
-    pair = jnp.concatenate([x_ref[...], n_ref[me]], axis=1)
+    pair = jnp.concatenate([x_ref[...], n_refs[0][...]], axis=1)
     weights = lax.dot_general(pair, grad, (((0,), (0,)), ((), ())), preferred_element_type=F32).astype(BF)
     share = height - width
     for j in range(blocks):
@@ -148,19 +182,22 @@
             at = (j * 2 + kind) * depth
             for part in range(depth // share):
                 send_ref[at // share + part, width:, :] = block[part * share : (part + 1) * share]
-
-
-def gather_kernel(scale, slots, width, got_ref, back_ref, send_ref, hub_ref, grad_ref, bias_ref, part_ref):
+    routed(send_refs, hold_ref, dom_ref[0])
+
+
+def gather_kernel(scale, slots, width, me_ref, back_ref, send_ref, hub_ref, *refs):
+    got_refs, (grad_ref, bias_ref, part_ref, hold_ref) = refs[:-4], refs[-4:]
     rows, cols = back_ref.shape
-    peers = got_ref.shape[0]
+    peers = send_ref.shape[1]
     hub_here = hub_ref.shape[1]
     mark = source_matrix(send_ref[0], hub_ref[...], rows, width)
+    got_ref = ordered(got_refs, hold_ref, me_ref[0])
     near = got_ref[:, :width, :]
     total = back_ref[...] + jnp.dot(mark, near.reshape(peers * width, cols), preferred_element_type=F32)
     grad_ref[...] = total.astype(BF)
     first = slots + hub_here
     bias = jnp.zeros((2, cols), F32)
-    share = jnp.zeros(part_ref.shape[1:], F32)
+    share = jnp.zeros(part_ref.shape[-2:], F32)
     for q in range(peers):
         bias = bias + got_ref[q, first : first + 2, :].astype(F32)
         share = share + got_ref[q, width:, :].astype(F32)
@@ -168,8 +205,10 @@
     part_ref[...] = jnp.broadcast_to(share.astype(BF), part_ref.shape)
 
 
-def spread_kernel(scale, got_ref, self_ref, neigh_ref):
+def spread_kernel(scale, me_ref, *refs):
+    got_refs, (self_ref, neigh_ref, hold_ref) = refs[:-3], refs[-3:]
     depth, full = self_ref.shape
+    got_ref = ordered(got_refs, hold_ref, me_ref[0])
     peers, share, cols = got_ref.shape
     whole = got_ref[...].reshape(peers * share, cols).astype(F32) * scale
     for j in range(full // cols):
@@ -180,11 +219,23 @@
 
 VMEM = pl.BlockSpec(memory_space=pltpu.VMEM)
 SMEM = pl.BlockSpec(memory_space=pltpu.SMEM)
+ANY = pl.BlockSpec(memory_space=pl.ANY)
 PARAMS = pltpu.CompilerParams(vmem_limit_bytes=40 * 1024 * 1024)
+DIRECT = 8
 
 
 def shape(dims, kind):
     return jax.ShapeDtypeStruct(dims, kind)
+
+
+def partner(block, axis, k):
+    return lax.ppermute(block, axis, [(i, i ^ k) for i in range(lax.axis_size(axis))])
+
+
+def exchange(blocks, axis):
+    if len(blocks) == 1:
+        return [lax.all_to_all(blocks[0], axis, split_axis=0, concat_axis=0, tiled=True)]
+    return [blocks[0]] + [partner(block, axis, k) for k, block in enumerate(blocks) if k]
 
 
 def on_device(
@@ -214,69 +265,87 @@
     scale = 1.0 / math.sqrt(peers * rows)
     feats = lax.axis_size("feat")
     me = lax.axis_index("feat").astype(jnp.int32).reshape(1)
-
-    outgoing, pack = pl.pallas_call(
-        functools.partial(send_kernel, width),
-        out_shape=(
-            shape((peers, width, cols), BF),
-            shape((2 * blocks * depth + 2 * rows + 16, cols), BF),
-        ),
-        in_specs=[VMEM] * 7,
-        out_specs=(VMEM, VMEM),
-        compiler_params=PARAMS,
-    )(features, cotangent, w_self, w_neigh, bias.reshape(1, cols), send_rows, hub_rows)
-
-    far = lax.ppermute(pack, "feat", [(i, i ^ 2) for i in range(feats)])
-    near = lax.ppermute(pack, "feat", [(i, i ^ 1) for i in range(feats)])
-    last = lax.ppermute(far, "feat", [(i, i ^ 1) for i in range(feats)])
-
-    incoming = lax.all_to_all(outgoing, "dom", split_axis=0, concat_axis=0, tiled=True)
-    mix, neigh = pl.pallas_call(
+    dom = lax.axis_index("dom").astype(jnp.int32).reshape(1)
+    direct = peers <= DIRECT
+    count = peers if direct else 1
+
+    def stacked(height):
+        return [shape((height, cols), BF)] * peers if direct else [shape((peers, height, cols), BF)]
+
+    def hold(height):
+        return pltpu.VMEM((peers, height, cols) if direct else (1, 16, cols), BF)
+
+    pack_rows = 2 * blocks * depth + 2 * rows + 16
+    *outgoing, pack = pl.pallas_call(
+        functools.partial(send_kernel, width, count),
+        out_shape=(*stacked(width), shape((pack_rows, cols), BF)),
+        in_specs=[SMEM] + [ANY] * 7,
+        out_specs=(VMEM,) * (count + 1),
+        scratch_shapes=[
+            hold(width),
+            pltpu.VMEM(send_rows.shape, jnp.int32),
+            pltpu.VMEM(hub_rows.shape, jnp.int32),
+            pltpu.VMEM((1, cols), BF),
+            pltpu.SemaphoreType.DMA((5 + 2 * blocks,)),
+        ],
+        compiler_params=PARAMS,
+    )(dom, features, cotangent, w_self, w_neigh, bias.reshape(1, cols), send_rows, hub_rows)
+
+    incoming = exchange(outgoing, "dom")
+    far = partner(pack, "feat", 2)
+    near = partner(pack, "feat", 1)
+    mix, neigh, far = pl.pallas_call(
         functools.partial(neigh_kernel, width),
-        out_shape=(shape((rows, rows + lanes), BF), shape((rows, cols), BF)),
-        in_specs=[SMEM] * 3 + [VMEM] * 6,
-        out_specs=(VMEM, VMEM),
-        compiler_params=PARAMS,
-    )(tile_pos, tile_count, recv_count, features, incoming, tile_vals, recv_dest, ghost_weight, hub_weight)
-    every = lax.all_gather(neigh, "feat", axis=0, tiled=False)
-
-    output, back, returned = pl.pallas_call(
-        functools.partial(dense_kernel, slots, hub_here),
+        out_shape=(shape((rows, rows + lanes), BF), shape((rows, cols), BF), shape((pack_rows, cols), BF)),
+        in_specs=[SMEM] * 4 + [VMEM] * 5 + [ANY] + [VMEM] * count,
+        out_specs=(VMEM, VMEM, ANY),
+        scratch_shapes=[hold(width)],
+        input_output_aliases={9: 2},
+        compiler_params=PARAMS,
+    )(dom, tile_pos, tile_count, recv_count, features, tile_vals, recv_dest, ghost_weight, hub_weight, far, *incoming)
+    last = partner(far, "feat", 1)
+    every = [neigh] + [partner(neigh, "feat", k) for k in range(1, feats)]
+
+    output, back, *returned = pl.pallas_call(
+        functools.partial(dense_kernel, slots, hub_here, feats, count),
         out_shape=(
             shape((rows, cols), BF),
             shape((rows, cols), F32),
-            shape((peers, width + share, cols), BF),
+            *stacked(width + share),
         ),
-        in_specs=[SMEM] + [VMEM] * 9,
-        out_specs=(VMEM,) * 3,
+        in_specs=[SMEM] * 2 + [VMEM] * (4 + 2 * feats),
+        out_specs=(VMEM,) * (2 + count),
         scratch_shapes=[
+            hold(width + share),
             pltpu.VMEM((rows, full), F32),
             pltpu.VMEM((rows, full), BF),
             pltpu.VMEM((16, full), BF),
         ],
         compiler_params=PARAMS,
-    )(me, features, w_self, w_neigh, pack, near, far, last, every, mix)
-
-    arrived = lax.all_to_all(returned, "dom", split_axis=0, concat_axis=0, tiled=True)
-    grad_features, grad_bias, parts = pl.pallas_call(
+    )(dom, me, features, w_self, w_neigh, mix, pack, near, far, last, *every)
+
+    arrived = exchange(returned, "dom")
+    grad_features, grad_bias, part = pl.pallas_call(
         functools.partial(gather_kernel, scale, slots, width),
         out_shape=(
             shape((rows, cols), BF),
             shape((1, cols), F32),
-            shape((peers, share, cols), BF),
+            shape((share, cols) if direct else (peers, share, cols), BF),
         ),
-        in_specs=[VMEM] * 4,
+        in_specs=[SMEM] + [VMEM] * (3 + count),
         out_specs=(VMEM,) * 3,
-        compiler_params=PARAMS,
-    )(arrived, back, send_rows, hub_rows)
-    whole = lax.all_to_all(parts, "dom", split_axis=0, concat_axis=0, tiled=True)
+        scratch_shapes=[hold(width + share)],
+        compiler_params=PARAMS,
+    )(dom, back, send_rows, hub_rows, *arrived)
+    parts = exchange([part] * count, "dom")
     grad_self, grad_neigh = pl.pallas_call(
         functools.partial(spread_kernel, scale),
         out_shape=(shape((depth, full), F32), shape((depth, full), F32)),
-        in_specs=[VMEM],
+        in_specs=[SMEM] + [VMEM] * count,
         out_specs=(VMEM, VMEM),
-        compiler_params=PARAMS,
-    )(whole)
+        scratch_shapes=[hold(share)],
+        compiler_params=PARAMS,
+    )(dom, *parts)
     return output, grad_features, grad_self, grad_neigh, grad_bias.reshape(cols)
 
 

time: 70.6 us -> 64.8 us (0.918)
  blocking collectives: 33.4 us -> 0 us
  starting transfers between devices: 9.17 us -> 38.7 us
  waiting for transfers between devices: 16 us -> 14.8 us
    ppermute x3 -> x27, starting transfers between devices: 2.95 us -> 38.7 us  [partner(): lax.ppermute(block, axis, [(i, i ^ k) for i in range(lax.axis_size(axis))])]
    all_to_all x2 -> x0, blocking collectives: 27.5 us -> none  [the longest x1 15.4 us: on_device(): lax.all_to_all(returned, 'dom', split_axis=0, concat_axis=0, tiled=True)]
    all_to_all x1 -> x0, waiting for transfers between devices: 6.78 us -> none  [on_device(): lax.all_to_all(outgoing, 'dom', split_axis=0, concat_axis=0, tiled=True)]
    all_to_all x1 -> x0, starting transfers between devices: 6.23 us -> none  [on_device(): lax.all_to_all(outgoing, 'dom', split_axis=0, concat_axis=0, tiled=True)]
    all_gather x1 -> x0, blocking collectives: 5.92 us -> none  [on_device(): every = lax.all_gather(neigh, 'feat', axis=0, tiled=False)]
    ppermute x3 -> x27, waiting for transfers between devices: 9.2 us -> 14.8 us  [partner(): lax.ppermute(block, axis, [(i, i ^ k) for i in range(lax.axis_size(axis))])]
    unnamed x35 -> x33, local copies, waits for them, and re-layouts: 5 us -> 4.32 us
  transfers between devices with their start and end apart: 4 -> 27, of which waited for: 2 -> 10; matrix products, arithmetic and copies ran while one was open for 0% -> 0% of each run, Pallas kernels for 1% -> 2%
where the time goes in v2:
time: 64.8 us; the launch traced here: 64.5 us
  starting transfers between devices  38.7 us (60%)
  waiting for transfers between devices  14.8 us (23%)
  Pallas kernels  5.13 us (8%)
  local copies, waits for them, and re-layouts  4.32 us (7%)
  between operations  1.5 us (2%)
    ppermute x27, starting transfers between devices, partner(): lax.ppermute(block, axis, [(i, i ^ k) for i in range(lax.axis_size(axis))])  38.7 us
    ppermute x27, waiting for transfers between devices, partner(): lax.ppermute(block, axis, [(i, i ^ k) for i in range(lax.axis_size(axis))])  14.8 us
    unnamed x33, local copies, waits for them, and re-layouts  4.32 us
    pallas_call x1, Pallas kernels, on_device(): pl.pallas_call(functools.partial(dense_kernel, slots, hub_here, feats, co...  1.51 us
  transfers between devices with their start and end apart: 27, of which 10 were waited for; matrix products, arithmetic and copies ran while one was open for 0% of the time, Pallas kernels for 2%

profile of v2, /device:TPU:0, one launch (start us, length us, event | category | flops | bytes accessed | tf_op | source)
XLA Modules:
  0.0 64.5 jit_solution(14579563484451791065)
XLA Ops:
  1.3 0.8 %copy-done = bf16[256,128]{1,0:T(8,128)(2,1)S(1)} copy-done((bf16[256,128]{1,0:T(8,128)(2,1)S(1)}, bf16[256,128]{1,0:T(8,128)(2,1)}, u32[]{:S(2)}) %copy-start) | copy-done | bytes 65560
  2.2 0.9 %copy-done.2 = bf16[128,512]{1,0:T(8,128)(2,1)S(1)} copy-done((bf16[128,512]{1,0:T(8,128)(2,1)S(1)}, bf16[128,512]{1,0:T(8,128)(2,1)}, u32[]{:S(2)}) %copy-start.2) | copy-done | bytes 131096
  3.1 0.9 %copy-done.4 = bf16[128,512]{1,0:T(8,128)(2,1)S(1)} copy-done((bf16[128,512]{1,0:T(8,128)(2,1)S(1)}, bf16[128,512]{1,0:T(8,128)(2,1)}, u32[]{:S(2)}) %copy-start.4) | copy-done | bytes 131096
  4.0 0.8 %copy-done.7 = bf16[256,128]{1,0:T(8,128)(2,1)S(1)} copy-done((bf16[256,128]{1,0:T(8,128)(2,1)S(1)}, bf16[256,128]{1,0:T(8,128)(2,1)}, u32[]{:S(2)}) %copy-start.7) | copy-done | bytes 65560
  4.8 0.8 %shard_map.173 = (bf16[64,128]{1,0:T(8,128)(2,1)S(1)}, bf16[64,128]{1,0:T(8,128)(2,1)S(1)}, bf16[64,128]{1,0:T(8,128)(2,1)S(1)}, bf16[64,128]{1,0:T(8,128)(2,1)S...) custom-call(s32[1]{0:T(128)} %bitcast.me_ref.dom_ref, ...), custom_call_target="tpu_custom_call" | custom-call | tf_op jit(solution)/shard_map/pallas_call | solution.py:279
  5.6 3.0 %collective-permute-start = (bf16[1552,128]{1,0:T(8,128)(2,1)S(1)}, bf16[1552,128]{1,0:T(8,128)(2,1)S(1)}, u32[]{:S(2)}, u32[]{:S(2)}) collective-permute-start(bf16[1552,128]{1,0:T(8,128)(2,1)S(1)} %get-tuple-element.32.refs_0_), channel_id=1, source_target_pairs={{0,2},{1,3},{2,0},{3,1},{4,6},{5,7},{6,4},{7,5},{8,10},{9,11},{10,... | collective-permute-start | bytes 1191944 | tf_op jit(solution)/shard_map/ppermute | solution.py:232
  8.6 1.5 %collective-permute-start.1 = (bf16[64,128]{1,0:T(8,128)(2,1)S(1)}, bf16[64,128]{1,0:T(8,128)(2,1)S(1)}, u32[]{:S(2)}, u32[]{:S(2)}) collective-permute-start(bf16[64,128]{1,0:T(8,128)(2,1)S(1)} %get-tuple-element.34), channel_id=1, source_target_pairs={{0,4},{4,0},{8,12},{12,8},{16,20},{20,16},{24,28},{28,24},{1,5},{5... | collective-permute-start | bytes 49160 | tf_op jit(solution)/shard_map/ppermute | solution.py:232
  10.1 1.6 %collective-permute-start.2 = (bf16[64,128]{1,0:T(8,128)(2,1)S(1)}, bf16[64,128]{1,0:T(8,128)(2,1)S(1)}, u32[]{:S(2)}, u32[]{:S(2)}) collective-permute-start(bf16[64,128]{1,0:T(8,128)(2,1)S(1)} %get-tuple-element.35), channel_id=1, source_target_pairs={{0,8},{4,12},{8,0},{12,4},{16,24},{20,28},{24,16},{28,20},{1,9},{5... | collective-permute-start | bytes 49160 | tf_op jit(solution)/shard_map/ppermute | solution.py:232
  12.1 2.6 %collective-permute-start.4 = (bf16[64,128]{1,0:T(8,128)(2,1)S(1)}, bf16[64,128]{1,0:T(8,128)(2,1)S(1)}, u32[]{:S(2)}, u32[]{:S(2)}) collective-permute-start(bf16[64,128]{1,0:T(8,128)(2,1)S(1)} %get-tuple-element.37), channel_id=1, source_target_pairs={{0,16},{4,20},{8,24},{12,28},{16,0},{20,4},{24,8},{28,12},{1,17},{... | collective-permute-start | bytes 49160 | tf_op jit(solution)/shard_map/ppermute | solution.py:232
  14.7 1.3 %collective-permute-start.5 = (bf16[64,128]{1,0:T(8,128)(2,1)S(1)}, bf16[64,128]{1,0:T(8,128)(2,1)S(1)}, u32[]{:S(2)}, u32[]{:S(2)}) collective-permute-start(bf16[64,128]{1,0:T(8,128)(2,1)S(1)} %get-tuple-element.38), channel_id=1, source_target_pairs={{0,20},{4,16},{8,28},{12,24},{16,4},{20,0},{24,12},{28,8},{1,21},{... | collective-permute-start | bytes 49160 | tf_op jit(solution)/shard_map/ppermute | solution.py:232
  16.0 3.6 %collective-permute-start.6 = (bf16[64,128]{1,0:T(8,128)(2,1)S(1)}, bf16[64,128]{1,0:T(8,128)(2,1)S(1)}, u32[]{:S(2)}, u32[]{:S(2)}) collective-permute-start(bf16[64,128]{1,0:T(8,128)(2,1)S(1)} %get-tuple-element.39), channel_id=1, source_target_pairs={{0,24},{4,28},{8,16},{12,20},{16,8},{20,12},{24,0},{28,4},{1,25},{... | collective-permute-start | bytes 49160 | tf_op jit(solution)/shard_map/ppermute | solution.py:232
  20.7 0.8 %collective-permute-done.6.refs_6_ = bf16[64,128]{1,0:T(8,128)(2,1)S(1)} collective-permute-done((bf16[64,128]{1,0:T(8,128)(2,1)S(1)}, bf16[64,128]{1,0:T(8,128)(2,1)S(1)}, u32[]{:S(2)}, u32[]{:S(2)}) %collective-permute-start.6) | collective-permute-done | bytes 16416 | tf_op jit(solution)/shard_map/ppermute | solution.py:232
  21.5 4.5 %collective-permute-done.7.refs_7_ = bf16[64,128]{1,0:T(8,128)(2,1)S(1)} collective-permute-done((bf16[64,128]{1,0:T(8,128)(2,1)S(1)}, bf16[64,128]{1,0:T(8,128)(2,1)S(1)}, u32[]{:S(2)}, u32[]{:S(2)}) %collective-permute-start.7) | collective-permute-done | bytes 16416 | tf_op jit(solution)/shard_map/ppermute | solution.py:232
  26.1 1.0 %shard_map.174 = (bf16[256,768]{1,0:T(8,128)(2,1)S(1)}, bf16[256,128]{1,0:T(8,128)(2,1)S(1)}, bf16[1552,128]{1,0:T(8,128)(2,1)S(1)}) custom-call(s32[1]{0:T(128)} %bitcast.me_ref.dom_ref, s32[1,4]{1,0:T(1,128)S(1)} %copy-done.13, s32[1]{0:T(128)S(6)} %copy.22.count_ref, s32[1,8]{1,0:T(1,128)S(1)} %copy-done.14, ...), custom_call_target="tpu_custom_call", output_to_operand_aliasing={{2}: (9, {})} | custom-call | tf_op jit(solution)/shard_map/pallas_call | solution.py:297
  27.9 1.5 %collective-permute-start.11 = (bf16[256,128]{1,0:T(8,128)(2,1)S(1)}, bf16[256,128]{1,0:T(8,128)(2,1)S(1)}, u32[]{:S(2)}, u32[]{:S(2)}) collective-permute-start(bf16[256,128]{1,0:T(8,128)(2,1)S(1)} %get-tuple-element.43.refs_4_), channel_id=1, source_target_pairs={{0,2},{1,3},{2,0},{3,1},{4,6},{5,7},{6,4},{7,5},{8,10},{9,11},{10,... | collective-permute-start | bytes 196616 | tf_op jit(solution)/shard_map/ppermute | solution.py:232
  29.3 1.7 %collective-permute-done.12.refs_7_ = bf16[256,128]{1,0:T(8,128)(2,1)S(1)} collective-permute-done((bf16[256,128]{1,0:T(8,128)(2,1)S(1)}, bf16[256,128]{1,0:T(8,128)(2,1)S(1)}, u32[]{:S(2)}, u32[]{:S(2)}) %collective-permute-start.12) | collective-permute-done | bytes 65568 | tf_op jit(solution)/shard_map/ppermute | solution.py:232
  31.1 2.0 %collective-permute-done.11.refs_6_ = bf16[256,128]{1,0:T(8,128)(2,1)S(1)} collective-permute-done((bf16[256,128]{1,0:T(8,128)(2,1)S(1)}, bf16[256,128]{1,0:T(8,128)(2,1)S(1)}, u32[]{:S(2)}, u32[]{:S(2)}) %collective-permute-start.11) | collective-permute-done | bytes 65568 | tf_op jit(solution)/shard_map/ppermute | solution.py:232
  33.1 1.5 %shard_map.175 = (bf16[256,128]{1,0:T(8,128)(2,1)}, f32[256,128]{1,0:T(8,128)S(1)}, bf16[192,128]{1,0:T(8,128)(2,1)S(1)}, bf16[192,128]{1,0:T(8,128)(2,1)S(1)}, ...) custom-call(s32[1]{0:T(128)} %bitcast.me_ref.dom_ref, ...), custom_call_target="tpu_custom_call" | custom-call | tf_op jit(solution)/shard_map/pallas_call | solution.py:309
  35.1 3.0 %collective-permute-start.15 = (bf16[192,128]{1,0:T(8,128)(2,1)S(1)}, bf16[192,128]{1,0:T(8,128)(2,1)S(1)}, u32[]{:S(2)}, u32[]{:S(2)}) collective-permute-start(bf16[192,128]{1,0:T(8,128)(2,1)S(1)} %get-tuple-element.49), channel_id=1, source_target_pairs={{0,12},{4,8},{8,4},{12,0},{16,28},{20,24},{24,20},{28,16},{1,13},{... | collective-permute-start | bytes 147464 | tf_op jit(solution)/shard_map/ppermute | solution.py:232
  38.1 2.9 %collective-permute-start.17 = (bf16[192,128]{1,0:T(8,128)(2,1)S(1)}, bf16[192,128]{1,0:T(8,128)(2,1)S(1)}, u32[]{:S(2)}, u32[]{:S(2)}) collective-permute-start(bf16[192,128]{1,0:T(8,128)(2,1)S(1)} %get-tuple-element.51), channel_id=1, source_target_pairs={{0,20},{4,16},{8,28},{12,24},{16,4},{20,0},{24,12},{28,8},{1,21},{... | collective-permute-start | bytes 147464 | tf_op jit(solution)/shard_map/ppermute | solution.py:232
  41.2 4.5 %collective-permute-start.19 = (bf16[192,128]{1,0:T(8,128)(2,1)S(1)}, bf16[192,128]{1,0:T(8,128)(2,1)S(1)}, u32[]{:S(2)}, u32[]{:S(2)}) collective-permute-start(bf16[192,128]{1,0:T(8,128)(2,1)S(1)} %get-tuple-element.53), channel_id=1, source_target_pairs={{0,28},{4,24},{8,20},{12,16},{16,12},{20,8},{24,4},{28,0},{1,29},{... | collective-permute-start | bytes 147464 | tf_op jit(solution)/shard_map/ppermute | solution.py:232
  46.9 1.5 %collective-permute-done.19.refs_7_ = bf16[192,128]{1,0:T(8,128)(2,1)S(1)} collective-permute-done((bf16[192,128]{1,0:T(8,128)(2,1)S(1)}, bf16[192,128]{1,0:T(8,128)(2,1)S(1)}, u32[]{:S(2)}, u32[]{:S(2)}) %collective-permute-start.19) | collective-permute-done | bytes 49184 | tf_op jit(solution)/shard_map/ppermute | solution.py:232
  48.4 1.0 %shard_map.176 = (bf16[256,128]{1,0:T(8,128)(2,1)}, f32[1,128]{1,0:T(1,128)}, bf16[128,128]{1,0:T(8,128)(2,1)S(1)}) custom-call(s32[1]{0:T(128)} %bitcast.me_ref.dom_ref, f32[256,128]{1,0:T(8,128)S(1)} %get-tuple-element.45.back_ref, s32[1,8,48]{2,1,0:T(8,128)S(1)} %copy-done.8, s32[1,2]{1,0:T(1,128)S(1)} %copy-done.11, ...), custom_call_target="tpu_custom_call" | custom-call | tf_op jit(solution)/shard_map/pallas_call | solution.py:328
  49.4 4.1 %collective-permute-start.26 = (bf16[128,128]{1,0:T(8,128)(2,1)S(1)}, bf16[128,128]{1,0:T(8,128)(2,1)S(1)}, u32[]{:S(2)}, u32[]{:S(2)}) collective-permute-start(bf16[128,128]{1,0:T(8,128)(2,1)S(1)} %get-tuple-element.55.refs_0_), channel_id=1, source_target_pairs={{0,28},{4,24},{8,20},{12,16},{16,12},{20,8},{24,4},{28,0},{1,29},{... | collective-permute-start | bytes 98312 | tf_op jit(solution)/shard_map/ppermute | solution.py:232
  53.8 3.2 %collective-permute-start.23 = (bf16[128,128]{1,0:T(8,128)(2,1)S(1)}, bf16[128,128]{1,0:T(8,128)(2,1)S(1)}, u32[]{:S(2)}, u32[]{:S(2)}) collective-permute-start(bf16[128,128]{1,0:T(8,128)(2,1)S(1)} %get-tuple-element.55.refs_0_), channel_id=1, source_target_pairs={{0,16},{4,20},{8,24},{12,28},{16,0},{20,4},{24,8},{28,12},{1,17},{... | collective-permute-start | bytes 98312 | tf_op jit(solution)/shard_map/ppermute | solution.py:232
  57.0 1.7 %collective-permute-start.22 = (bf16[128,128]{1,0:T(8,128)(2,1)S(1)}, bf16[128,128]{1,0:T(8,128)(2,1)S(1)}, u32[]{:S(2)}, u32[]{:S(2)}) collective-permute-start(bf16[128,128]{1,0:T(8,128)(2,1)S(1)} %get-tuple-element.55.refs_0_), channel_id=1, source_target_pairs={{0,12},{4,8},{8,4},{12,0},{16,28},{20,24},{24,20},{28,16},{1,13},{... | collective-permute-start | bytes 98312 | tf_op jit(solution)/shard_map/ppermute | solution.py:232
  58.8 0.9 %collective-permute-start.21 = (bf16[128,128]{1,0:T(8,128)(2,1)S(1)}, bf16[128,128]{1,0:T(8,128)(2,1)S(1)}, u32[]{:S(2)}, u32[]{:S(2)}) collective-permute-start(bf16[128,128]{1,0:T(8,128)(2,1)S(1)} %get-tuple-element.55.refs_0_), channel_id=1, source_target_pairs={{0,8},{4,12},{8,0},{12,4},{16,24},{20,28},{24,16},{28,20},{1,9},{5... | collective-permute-start | bytes 98312 | tf_op jit(solution)/shard_map/ppermute | solution.py:232
  59.7 0.9 %collective-permute-start.20 = (bf16[128,128]{1,0:T(8,128)(2,1)S(1)}, bf16[128,128]{1,0:T(8,128)(2,1)S(1)}, u32[]{:S(2)}, u32[]{:S(2)}) collective-permute-start(bf16[128,128]{1,0:T(8,128)(2,1)S(1)} %get-tuple-element.55.refs_0_), channel_id=1, source_target_pairs={{0,4},{4,0},{8,12},{12,8},{16,20},{20,16},{24,28},{28,24},{1,5},{5... | collective-permute-start | bytes 98312 | tf_op jit(solution)/shard_map/ppermute | solution.py:232
  60.5 1.3 %collective-permute-done.22.refs_3_ = bf16[128,128]{1,0:T(8,128)(2,1)S(1)} collective-permute-done((bf16[128,128]{1,0:T(8,128)(2,1)S(1)}, bf16[128,128]{1,0:T(8,128)(2,1)S(1)}, u32[]{:S(2)}, u32[]{:S(2)}) %collective-permute-start.22) | collective-permute-done | bytes 32800 | tf_op jit(solution)/shard_map/ppermute | solution.py:232
  61.9 0.8 %collective-permute-done.21.refs_2_ = bf16[128,128]{1,0:T(8,128)(2,1)S(1)} collective-permute-done((bf16[128,128]{1,0:T(8,128)(2,1)S(1)}, bf16[128,128]{1,0:T(8,128)(2,1)S(1)}, u32[]{:S(2)}, u32[]{:S(2)}) %collective-permute-start.21) | collective-permute-done | bytes 32800 | tf_op jit(solution)/shard_map/ppermute | solution.py:232
  62.7 0.9 %collective-permute-done.20.refs_1_ = bf16[128,128]{1,0:T(8,128)(2,1)S(1)} collective-permute-done((bf16[128,128]{1,0:T(8,128)(2,1)S(1)}, bf16[128,128]{1,0:T(8,128)(2,1)S(1)}, u32[]{:S(2)}, u32[]{:S(2)}) %collective-permute-start.20) | collective-permute-done | bytes 32800 | tf_op jit(solution)/shard_map/ppermute | solution.py:232
  63.6 0.9 %shard_map.177 = (f32[128,512]{1,0:T(8,128)}, f32[128,512]{1,0:T(8,128)}) custom-call(s32[1]{0:T(128)} %bitcast.me_ref.dom_ref, bf16[128,128]{1,0:T(8,128)(2,1)S(1)} %get-tuple-element.55.refs_0_, bf16[128,128]{1,0:T(8,128)(2,1)S(1)} %collective-permute-done.20.refs_1_, bf16[128,128]{1,0:T(8,128)(2,1)S(1)} %collective-permute-done.21.refs_2_, ...), custom_call_target="tpu_custom_call" | custom-call | tf_op jit(solution)/shard_map/pallas_call | solution.py:341
  (60 shorter events, 4.5 us)
Async XLA Ops:
  4.8 15.6 %copy-start.15 = (bf16[256,16]{0,1:T(8,128)(2,1)S(1)}, bf16[256,16]{0,1:T(8,128)(2,1)}, u32[]{:S(2)}) copy-start(bf16[256,16]{0,1:T(8,128)(2,1)} %param.27) | copy-start | bytes 24580
  4.8 21.2 %copy-start.6 = (bf16[1,4,128,128]{3,2,1,0:T(8,128)(2,1)S(1)}, bf16[1,4,128,128]{3,2,1,0:T(8,128)(2,1)}, u32[]{:S(2)}) copy-start(bf16[1,4,128,128]{3,2,1,0:T(8,128)(2,1)} %tile_ref.1) | copy-start | bytes 393220
  5.6 20.4 %copy-start.1 = (bf16[256,128]{1,0:T(8,128)(2,1)S(1)}, bf16[256,128]{1,0:T(8,128)(2,1)}, u32[]{:S(2)}) copy-start(bf16[256,128]{1,0:T(8,128)(2,1)} %x_ref.3) | copy-start | bytes 196612
  5.6 20.4 %collective-permute-start = (bf16[1552,128]{1,0:T(8,128)(2,1)S(1)}, bf16[1552,128]{1,0:T(8,128)(2,1)S(1)}, u32[]{:S(2)}, u32[]{:S(2)}) collective-permute-start(bf16[1552,128]{1,0:T(8,128)(2,1)S(1)} %get-tuple-element.32.refs_0_), channel_id=1, source_target_pairs={{0,2},{1,3},{2,0},{3,1},{4,6},{5,7},{6,4},{7,5},{8,10},{9,11},{10,... | collective-permute-start | bytes 1191944 | tf_op jit(solution)/shard_map/ppermute | solution.py:232
  8.6 6.1 %collective-permute-start.1 = (bf16[64,128]{1,0:T(8,128)(2,1)S(1)}, bf16[64,128]{1,0:T(8,128)(2,1)S(1)}, u32[]{:S(2)}, u32[]{:S(2)}) collective-permute-start(bf16[64,128]{1,0:T(8,128)(2,1)S(1)} %get-tuple-element.34), channel_id=1, source_target_pairs={{0,4},{4,0},{8,12},{12,8},{16,20},{20,16},{24,28},{28,24},{1,5},{5... | collective-permute-start | bytes 49160 | tf_op jit(solution)/shard_map/ppermute | solution.py:232
  10.1 5.9 %collective-permute-start.2 = (bf16[64,128]{1,0:T(8,128)(2,1)S(1)}, bf16[64,128]{1,0:T(8,128)(2,1)S(1)}, u32[]{:S(2)}, u32[]{:S(2)}) collective-permute-start(bf16[64,128]{1,0:T(8,128)(2,1)S(1)} %get-tuple-element.35), channel_id=1, source_target_pairs={{0,8},{4,12},{8,0},{12,4},{16,24},{20,28},{24,16},{28,20},{1,9},{5... | collective-permute-start | bytes 49160 | tf_op jit(solution)/shard_map/ppermute | solution.py:232
  11.7 7.9 %collective-permute-start.3 = (bf16[64,128]{1,0:T(8,128)(2,1)S(1)}, bf16[64,128]{1,0:T(8,128)(2,1)S(1)}, u32[]{:S(2)}, u32[]{:S(2)}) collective-permute-start(bf16[64,128]{1,0:T(8,128)(2,1)S(1)} %get-tuple-element.36), channel_id=1, source_target_pairs={{0,12},{4,8},{8,4},{12,0},{16,28},{20,24},{24,20},{28,16},{1,13},{... | collective-permute-start | bytes 49160 | tf_op jit(solution)/shard_map/ppermute | solution.py:232
  12.1 8.5 %collective-permute-start.4 = (bf16[64,128]{1,0:T(8,128)(2,1)S(1)}, bf16[64,128]{1,0:T(8,128)(2,1)S(1)}, u32[]{:S(2)}, u32[]{:S(2)}) collective-permute-start(bf16[64,128]{1,0:T(8,128)(2,1)S(1)} %get-tuple-element.37), channel_id=1, source_target_pairs={{0,16},{4,20},{8,24},{12,28},{16,0},{20,4},{24,8},{28,12},{1,17},{... | collective-permute-start | bytes 49160 | tf_op jit(solution)/shard_map/ppermute | solution.py:232
  14.7 6.0 %collective-permute-start.5 = (bf16[64,128]{1,0:T(8,128)(2,1)S(1)}, bf16[64,128]{1,0:T(8,128)(2,1)S(1)}, u32[]{:S(2)}, u32[]{:S(2)}) collective-permute-start(bf16[64,128]{1,0:T(8,128)(2,1)S(1)} %get-tuple-element.38), channel_id=1, source_target_pairs={{0,20},{4,16},{8,28},{12,24},{16,4},{20,0},{24,12},{28,8},{1,21},{... | collective-permute-start | bytes 49160 | tf_op jit(solution)/shard_map/ppermute | solution.py:232
  16.0 5.5 %collective-permute-start.6 = (bf16[64,128]{1,0:T(8,128)(2,1)S(1)}, bf16[64,128]{1,0:T(8,128)(2,1)S(1)}, u32[]{:S(2)}, u32[]{:S(2)}) collective-permute-start(bf16[64,128]{1,0:T(8,128)(2,1)S(1)} %get-tuple-element.39), channel_id=1, source_target_pairs={{0,24},{4,28},{8,16},{12,20},{16,8},{20,12},{24,0},{28,4},{1,25},{... | collective-permute-start | bytes 49160 | tf_op jit(solution)/shard_map/ppermute | solution.py:232
  19.6 6.4 %collective-permute-start.7 = (bf16[64,128]{1,0:T(8,128)(2,1)S(1)}, bf16[64,128]{1,0:T(8,128)(2,1)S(1)}, u32[]{:S(2)}, u32[]{:S(2)}) collective-permute-start(bf16[64,128]{1,0:T(8,128)(2,1)S(1)} %get-tuple-element.40), channel_id=1, source_target_pairs={{0,28},{4,24},{8,20},{12,16},{16,12},{20,8},{24,4},{28,0},{1,29},{... | collective-permute-start | bytes 49160 | tf_op jit(solution)/shard_map/ppermute | solution.py:232
  20.6 8.7 %collective-permute-start.8 = (bf16[1552,128]{1,0:T(8,128)(2,1)S(1)}, bf16[1552,128]{1,0:T(8,128)(2,1)S(1)}, u32[]{:S(2)}, u32[]{:S(2)}) collective-permute-start(bf16[1552,128]{1,0:T(8,128)(2,1)S(1)} %get-tuple-element.32.refs_0_), channel_id=1, source_target_pairs={{0,1},{1,0},{2,3},{3,2},{4,5},{5,4},{6,7},{7,6},{8,9},{9,8},{10,11... | collective-permute-start | bytes 1191944 | tf_op jit(solution)/shard_map/ppermute | solution.py:232
  26.1 7.0 %copy-start.3 = (bf16[128,512]{1,0:T(8,128)(2,1)S(1)}, bf16[128,512]{1,0:T(8,128)(2,1)}, u32[]{:S(2)}) copy-start(bf16[128,512]{1,0:T(8,128)(2,1)} %ws_ref.1) | copy-start | bytes 393220
  26.1 7.0 %copy-start.5 = (bf16[128,512]{1,0:T(8,128)(2,1)S(1)}, bf16[128,512]{1,0:T(8,128)(2,1)}, u32[]{:S(2)}) copy-start(bf16[128,512]{1,0:T(8,128)(2,1)} %wn_ref.1) | copy-start | bytes 393220
  27.1 5.9 %collective-permute-start.9 = (bf16[1552,128]{1,0:T(8,128)(2,1)S(1)}, bf16[1552,128]{1,0:T(8,128)(2,1)S(1)}, u32[]{:S(2)}, u32[]{:S(2)}) collective-permute-start(bf16[1552,128]{1,0:T(8,128)(2,1)S(1)} %get-tuple-element.42.refs_2_), channel_id=1, source_target_pairs={{0,1},{1,0},{2,3},{3,2},{4,5},{5,4},{6,7},{7,6},{8,9},{9,8},{10,11... | collective-permute-start | bytes 1191944 | tf_op jit(solution)/shard_map/ppermute | solution.py:232
  27.2 3.9 %collective-permute-start.12 = (bf16[256,128]{1,0:T(8,128)(2,1)S(1)}, bf16[256,128]{1,0:T(8,128)(2,1)S(1)}, u32[]{:S(2)}, u32[]{:S(2)}) collective-permute-start(bf16[256,128]{1,0:T(8,128)(2,1)S(1)} %get-tuple-element.43.refs_4_), channel_id=1, source_target_pairs={{0,3},{1,2},{2,1},{3,0},{4,7},{5,6},{6,5},{7,4},{8,11},{9,10},{10,... | collective-permute-start | bytes 196616 | tf_op jit(solution)/shard_map/ppermute | solution.py:232
  27.9 5.2 %collective-permute-start.11 = (bf16[256,128]{1,0:T(8,128)(2,1)S(1)}, bf16[256,128]{1,0:T(8,128)(2,1)S(1)}, u32[]{:S(2)}, u32[]{:S(2)}) collective-permute-start(bf16[256,128]{1,0:T(8,128)(2,1)S(1)} %get-tuple-element.43.refs_4_), channel_id=1, source_target_pairs={{0,2},{1,3},{2,0},{3,1},{4,6},{5,7},{6,4},{7,5},{8,10},{9,11},{10,... | collective-permute-start | bytes 196616 | tf_op jit(solution)/shard_map/ppermute | solution.py:232
  29.3 3.7 %collective-permute-start.10 = (bf16[256,128]{1,0:T(8,128)(2,1)S(1)}, bf16[256,128]{1,0:T(8,128)(2,1)S(1)}, u32[]{:S(2)}, u32[]{:S(2)}) collective-permute-start(bf16[256,128]{1,0:T(8,128)(2,1)S(1)} %get-tuple-element.43.refs_4_), channel_id=1, source_target_pairs={{0,1},{1,0},{2,3},{3,2},{4,5},{5,4},{6,7},{7,6},{8,9},{9,8},{10,11... | collective-permute-start | bytes 196616 | tf_op jit(solution)/shard_map/ppermute | solution.py:232
  34.6 6.4 %collective-permute-start.13 = (bf16[192,128]{1,0:T(8,128)(2,1)S(1)}, bf16[192,128]{1,0:T(8,128)(2,1)S(1)}, u32[]{:S(2)}, u32[]{:S(2)}) collective-permute-start(bf16[192,128]{1,0:T(8,128)(2,1)S(1)} %get-tuple-element.47), channel_id=1, source_target_pairs={{0,4},{4,0},{8,12},{12,8},{16,20},{20,16},{24,28},{28,24},{1,5},{5... | collective-permute-start | bytes 147464 | tf_op jit(solution)/shard_map/ppermute | solution.py:232
  35.1 6.1 %collective-permute-start.14 = (bf16[192,128]{1,0:T(8,128)(2,1)S(1)}, bf16[192,128]{1,0:T(8,128)(2,1)S(1)}, u32[]{:S(2)}, u32[]{:S(2)}) collective-permute-start(bf16[192,128]{1,0:T(8,128)(2,1)S(1)} %get-tuple-element.48), channel_id=1, source_target_pairs={{0,8},{4,12},{8,0},{12,4},{16,24},{20,28},{24,16},{28,20},{1,9},{5... | collective-permute-start | bytes 147464 | tf_op jit(solution)/shard_map/ppermute | solution.py:232
  35.1 10.6 %collective-permute-start.15 = (bf16[192,128]{1,0:T(8,128)(2,1)S(1)}, bf16[192,128]{1,0:T(8,128)(2,1)S(1)}, u32[]{:S(2)}, u32[]{:S(2)}) collective-permute-start(bf16[192,128]{1,0:T(8,128)(2,1)S(1)} %get-tuple-element.49), channel_id=1, source_target_pairs={{0,12},{4,8},{8,4},{12,0},{16,28},{20,24},{24,20},{28,16},{1,13},{... | collective-permute-start | bytes 147464 | tf_op jit(solution)/shard_map/ppermute | solution.py:232
  38.1 7.7 %collective-permute-start.16 = (bf16[192,128]{1,0:T(8,128)(2,1)S(1)}, bf16[192,128]{1,0:T(8,128)(2,1)S(1)}, u32[]{:S(2)}, u32[]{:S(2)}) collective-permute-start(bf16[192,128]{1,0:T(8,128)(2,1)S(1)} %get-tuple-element.50), channel_id=1, source_target_pairs={{0,16},{4,20},{8,24},{12,28},{16,0},{20,4},{24,8},{28,12},{1,17},{... | collective-permute-start | bytes 147464 | tf_op jit(solution)/shard_map/ppermute | solution.py:232
  38.1 8.2 %collective-permute-start.17 = (bf16[192,128]{1,0:T(8,128)(2,1)S(1)}, bf16[192,128]{1,0:T(8,128)(2,1)S(1)}, u32[]{:S(2)}, u32[]{:S(2)}) collective-permute-start(bf16[192,128]{1,0:T(8,128)(2,1)S(1)} %get-tuple-element.51), channel_id=1, source_target_pairs={{0,20},{4,16},{8,28},{12,24},{16,4},{20,0},{24,12},{28,8},{1,21},{... | collective-permute-start | bytes 147464 | tf_op jit(solution)/shard_map/ppermute | solution.py:232
  41.0 6.0 %collective-permute-start.18 = (bf16[192,128]{1,0:T(8,128)(2,1)S(1)}, bf16[192,128]{1,0:T(8,128)(2,1)S(1)}, u32[]{:S(2)}, u32[]{:S(2)}) collective-permute-start(bf16[192,128]{1,0:T(8,128)(2,1)S(1)} %get-tuple-element.52), channel_id=1, source_target_pairs={{0,24},{4,28},{8,16},{12,20},{16,8},{20,12},{24,0},{28,4},{1,25},{... | collective-permute-start | bytes 147464 | tf_op jit(solution)/shard_map/ppermute | solution.py:232
  41.2 7.2 %collective-permute-start.19 = (bf16[192,128]{1,0:T(8,128)(2,1)S(1)}, bf16[192,128]{1,0:T(8,128)(2,1)S(1)}, u32[]{:S(2)}, u32[]{:S(2)}) collective-permute-start(bf16[192,128]{1,0:T(8,128)(2,1)S(1)} %get-tuple-element.53), channel_id=1, source_target_pairs={{0,28},{4,24},{8,20},{12,16},{16,12},{20,8},{24,4},{28,0},{1,29},{... | collective-permute-start | bytes 147464 | tf_op jit(solution)/shard_map/ppermute | solution.py:232
  49.4 9.4 %collective-permute-start.26 = (bf16[128,128]{1,0:T(8,128)(2,1)S(1)}, bf16[128,128]{1,0:T(8,128)(2,1)S(1)}, u32[]{:S(2)}, u32[]{:S(2)}) collective-permute-start(bf16[128,128]{1,0:T(8,128)(2,1)S(1)} %get-tuple-element.55.refs_0_), channel_id=1, source_target_pairs={{0,28},{4,24},{8,20},{12,16},{16,12},{20,8},{24,4},{28,0},{1,29},{... | collective-permute-start | bytes 98312 | tf_op jit(solution)/shard_map/ppermute | solution.py:232
  53.5 6.2 %collective-permute-start.25 = (bf16[128,128]{1,0:T(8,128)(2,1)S(1)}, bf16[128,128]{1,0:T(8,128)(2,1)S(1)}, u32[]{:S(2)}, u32[]{:S(2)}) collective-permute-start(bf16[128,128]{1,0:T(8,128)(2,1)S(1)} %get-tuple-element.55.refs_0_), channel_id=1, source_target_pairs={{0,24},{4,28},{8,16},{12,20},{16,8},{20,12},{24,0},{28,4},{1,25},{... | collective-permute-start | bytes 98312 | tf_op jit(solution)/shard_map/ppermute | solution.py:232
  53.8 6.7 %collective-permute-start.24 = (bf16[128,128]{1,0:T(8,128)(2,1)S(1)}, bf16[128,128]{1,0:T(8,128)(2,1)S(1)}, u32[]{:S(2)}, u32[]{:S(2)}) collective-permute-start(bf16[128,128]{1,0:T(8,128)(2,1)S(1)} %get-tuple-element.55.refs_0_), channel_id=1, source_target_pairs={{0,20},{4,16},{8,28},{12,24},{16,4},{20,0},{24,12},{28,8},{1,21},{... | collective-permute-start | bytes 98312 | tf_op jit(solution)/shard_map/ppermute | solution.py:232
  53.8 6.7 %collective-permute-start.23 = (bf16[128,128]{1,0:T(8,128)(2,1)S(1)}, bf16[128,128]{1,0:T(8,128)(2,1)S(1)}, u32[]{:S(2)}, u32[]{:S(2)}) collective-permute-start(bf16[128,128]{1,0:T(8,128)(2,1)S(1)} %get-tuple-element.55.refs_0_), channel_id=1, source_target_pairs={{0,16},{4,20},{8,24},{12,28},{16,0},{20,4},{24,8},{28,12},{1,17},{... | collective-permute-start | bytes 98312 | tf_op jit(solution)/shard_map/ppermute | solution.py:232
  57.0 4.8 %collective-permute-start.22 = (bf16[128,128]{1,0:T(8,128)(2,1)S(1)}, bf16[128,128]{1,0:T(8,128)(2,1)S(1)}, u32[]{:S(2)}, u32[]{:S(2)}) collective-permute-start(bf16[128,128]{1,0:T(8,128)(2,1)S(1)} %get-tuple-element.55.refs_0_), channel_id=1, source_target_pairs={{0,12},{4,8},{8,4},{12,0},{16,28},{20,24},{24,20},{28,16},{1,13},{... | collective-permute-start | bytes 98312 | tf_op jit(solution)/shard_map/ppermute | solution.py:232
  58.8 3.9 %collective-permute-start.21 = (bf16[128,128]{1,0:T(8,128)(2,1)S(1)}, bf16[128,128]{1,0:T(8,128)(2,1)S(1)}, u32[]{:S(2)}, u32[]{:S(2)}) collective-permute-start(bf16[128,128]{1,0:T(8,128)(2,1)S(1)} %get-tuple-element.55.refs_0_), channel_id=1, source_target_pairs={{0,8},{4,12},{8,0},{12,4},{16,24},{20,28},{24,16},{28,20},{1,9},{5... | collective-permute-start | bytes 98312 | tf_op jit(solution)/shard_map/ppermute | solution.py:232
  59.7 3.9 %collective-permute-start.20 = (bf16[128,128]{1,0:T(8,128)(2,1)S(1)}, bf16[128,128]{1,0:T(8,128)(2,1)S(1)}, u32[]{:S(2)}, u32[]{:S(2)}) collective-permute-start(bf16[128,128]{1,0:T(8,128)(2,1)S(1)} %get-tuple-element.55.refs_0_), channel_id=1, source_target_pairs={{0,4},{4,0},{8,12},{12,8},{16,20},{20,16},{24,28},{28,24},{1,5},{5... | collective-permute-start | bytes 98312 | tf_op jit(solution)/shard_map/ppermute | solution.py:232
  (11 other events, 27.8 us)

commit v3 on v2

--- a/solution.py
+++ b/solution.py
@@ -37,24 +37,9 @@
     return jnp.where(row == index, 1.0, 0.0).astype(BF)
 
 
-def ordered(refs, hold_ref, me):
-    if len(refs) == 1:
-        return refs[0]
-    for k, ref in enumerate(refs):
-        hold_ref[me ^ k] = ref[...]
-    return hold_ref
-
-
-def routed(refs, hold_ref, me):
-    if len(refs) > 1:
-        for k, ref in enumerate(refs):
-            ref[...] = hold_ref[me ^ k]
-
-
-def send_kernel(width, count, me_ref, *refs):
-    x_ref, cot_ref, ws_ref, wn_ref, bias_ref, send_ref, hub_ref = refs[:7]
-    out_refs, pack_ref = refs[7 : 7 + count], refs[7 + count]
-    hold_ref, send_v, hub_v, bias_v, sems = refs[8 + count :]
+def send_kernel(
+    width, x_ref, cot_ref, ws_ref, wn_ref, bias_ref, send_ref, hub_ref, out_ref, pack_ref, send_v, hub_v, bias_v, sems
+):
     rows, cols = x_ref.shape
     depth, full = ws_ref.shape
     blocks = full // cols
@@ -79,16 +64,16 @@
     taken = lax.dot_general(
         mark, pack_ref[base : base + rows, :], (((0,), (0,)), ((), ())), preferred_element_type=F32
     ).astype(BF)
-    target = out_refs[0] if count == 1 else hold_ref
-    target[...] = taken.reshape(target.shape)
-    routed(out_refs, hold_ref, me_ref[0])
+    out_ref[...] = taken.reshape(out_ref.shape)
     for copy in copies[3:]:
         copy.wait()
     pack_ref[base + 2 * rows :, :] = jnp.broadcast_to(bias_v[...], (16, cols))
 
 
-def neigh_kernel(width, me_ref, pos_ref, count_ref, live_ref, x_ref, tile_ref, dest_ref, gw_ref, hw_ref, far_ref, *refs):
-    got_refs, (mix_ref, neigh_ref, passed_ref, hold_ref) = refs[:-4], refs[-4:]
+def neigh_kernel(
+    width, pos_ref, count_ref, live_ref, x_ref, tile_ref, dest_ref, gw_ref, hw_ref, far_ref, got_ref,
+    mix_ref, neigh_ref, passed_ref,
+):
     rows, cols = x_ref.shape
     tile = tile_ref.shape[-1]
     tiles = tile_ref.shape[1]
@@ -121,18 +106,14 @@
     hub_mix = jnp.dot(hw_ref[...], place, preferred_element_type=F32)
     far = (ghost + hub_mix).astype(BF)
     mix_ref[:, rows:] = far
-    near = ordered(got_refs, hold_ref, me_ref[0])[...]
     total = jnp.dot(mix_ref[:, :rows], x_ref[...], preferred_element_type=F32)
-    total = total + jnp.dot(far, near.reshape(lanes, cols), preferred_element_type=F32)
+    total = total + jnp.dot(far, got_ref[...].reshape(lanes, cols), preferred_element_type=F32)
     neigh_ref[...] = total.astype(BF)
 
 
-def dense_kernel(slots, hub_here, feats, count, dom_ref, me_ref, x_ref, ws_ref, wn_ref, mix_ref, *refs):
+def dense_kernel(slots, hub_here, feats, me_ref, x_ref, ws_ref, wn_ref, mix_ref, *refs):
     pack_refs, n_refs = refs[:feats], refs[feats : 2 * feats]
-    out_ref, back_ref = refs[2 * feats : 2 * feats + 2]
-    send_refs = refs[2 * feats + 2 : 2 * feats + 2 + count]
-    hold_ref, pre_ref, cot_ref, bias_ref = refs[2 * feats + 2 + count :]
-    send_ref = send_refs[0] if count == 1 else hold_ref
+    out_ref, back_ref, send_ref, pre_ref, cot_ref, bias_ref = refs[2 * feats :]
     rows, cols = x_ref.shape
     depth, full = ws_ref.shape
     blocks = full // cols
@@ -182,16 +163,13 @@
             at = (j * 2 + kind) * depth
             for part in range(depth // share):
                 send_ref[at // share + part, width:, :] = block[part * share : (part + 1) * share]
-    routed(send_refs, hold_ref, dom_ref[0])
-
-
-def gather_kernel(scale, slots, width, me_ref, back_ref, send_ref, hub_ref, *refs):
-    got_refs, (grad_ref, bias_ref, part_ref, hold_ref) = refs[:-4], refs[-4:]
+
+
+def gather_kernel(scale, slots, width, back_ref, send_ref, hub_ref, got_ref, grad_ref, bias_ref, part_ref):
     rows, cols = back_ref.shape
     peers = send_ref.shape[1]
     hub_here = hub_ref.shape[1]
     mark = source_matrix(send_ref[0], hub_ref[...], rows, width)
-    got_ref = ordered(got_refs, hold_ref, me_ref[0])
     near = got_ref[:, :width, :]
     total = back_ref[...] + jnp.dot(mark, near.reshape(peers * width, cols), preferred_element_type=F32)
     grad_ref[...] = total.astype(BF)
@@ -205,10 +183,8 @@
     part_ref[...] = jnp.broadcast_to(share.astype(BF), part_ref.shape)
 
 
-def spread_kernel(scale, me_ref, *refs):
-    got_refs, (self_ref, neigh_ref, hold_ref) = refs[:-3], refs[-3:]
+def spread_kernel(scale, got_ref, self_ref, neigh_ref):
     depth, full = self_ref.shape
-    got_ref = ordered(got_refs, hold_ref, me_ref[0])
     peers, share, cols = got_ref.shape
     whole = got_ref[...].reshape(peers * share, cols).astype(F32) * scale
     for j in range(full // cols):
@@ -220,8 +196,8 @@
 VMEM = pl.BlockSpec(memory_space=pltpu.VMEM)
 SMEM = pl.BlockSpec(memory_space=pltpu.SMEM)
 ANY = pl.BlockSpec(memory_space=pl.ANY)
+HBM = pl.BlockSpec(memory_space=pltpu.HBM)
 PARAMS = pltpu.CompilerParams(vmem_limit_bytes=40 * 1024 * 1024)
-DIRECT = 8
 
 
 def shape(dims, kind):
@@ -232,10 +208,8 @@
     return lax.ppermute(block, axis, [(i, i ^ k) for i in range(lax.axis_size(axis))])
 
 
-def exchange(blocks, axis):
-    if len(blocks) == 1:
-        return [lax.all_to_all(blocks[0], axis, split_axis=0, concat_axis=0, tiled=True)]
-    return [blocks[0]] + [partner(block, axis, k) for k, block in enumerate(blocks) if k]
+def exchange(blocks):
+    return lax.all_to_all(blocks, "dom", split_axis=0, concat_axis=0, tiled=True)
 
 
 def on_device(
@@ -265,87 +239,75 @@
     scale = 1.0 / math.sqrt(peers * rows)
     feats = lax.axis_size("feat")
     me = lax.axis_index("feat").astype(jnp.int32).reshape(1)
-    dom = lax.axis_index("dom").astype(jnp.int32).reshape(1)
-    direct = peers <= DIRECT
-    count = peers if direct else 1
-
-    def stacked(height):
-        return [shape((height, cols), BF)] * peers if direct else [shape((peers, height, cols), BF)]
-
-    def hold(height):
-        return pltpu.VMEM((peers, height, cols) if direct else (1, 16, cols), BF)
-
     pack_rows = 2 * blocks * depth + 2 * rows + 16
-    *outgoing, pack = pl.pallas_call(
-        functools.partial(send_kernel, width, count),
-        out_shape=(*stacked(width), shape((pack_rows, cols), BF)),
-        in_specs=[SMEM] + [ANY] * 7,
-        out_specs=(VMEM,) * (count + 1),
+
+    raw = (features, cotangent, w_self, w_neigh, bias.reshape(1, cols), send_rows, hub_rows)
+    outgoing, pack = pl.pallas_call(
+        functools.partial(send_kernel, width),
+        out_shape=(shape((peers, width, cols), BF), shape((pack_rows, cols), BF)),
+        in_specs=[HBM] * 7,
+        out_specs=(VMEM, VMEM),
         scratch_shapes=[
-            hold(width),
             pltpu.VMEM(send_rows.shape, jnp.int32),
             pltpu.VMEM(hub_rows.shape, jnp.int32),
             pltpu.VMEM((1, cols), BF),
             pltpu.SemaphoreType.DMA((5 + 2 * blocks,)),
         ],
         compiler_params=PARAMS,
-    )(dom, features, cotangent, w_self, w_neigh, bias.reshape(1, cols), send_rows, hub_rows)
-
-    incoming = exchange(outgoing, "dom")
+    )(*(pltpu.with_memory_space_constraint(a, pltpu.HBM) for a in raw))
+
     far = partner(pack, "feat", 2)
     near = partner(pack, "feat", 1)
+    incoming = exchange(outgoing)
     mix, neigh, far = pl.pallas_call(
         functools.partial(neigh_kernel, width),
         out_shape=(shape((rows, rows + lanes), BF), shape((rows, cols), BF), shape((pack_rows, cols), BF)),
-        in_specs=[SMEM] * 4 + [VMEM] * 5 + [ANY] + [VMEM] * count,
+        in_specs=[SMEM] * 3 + [VMEM] * 5 + [ANY, VMEM],
         out_specs=(VMEM, VMEM, ANY),
-        scratch_shapes=[hold(width)],
-        input_output_aliases={9: 2},
-        compiler_params=PARAMS,
-    )(dom, tile_pos, tile_count, recv_count, features, tile_vals, recv_dest, ghost_weight, hub_weight, far, *incoming)
+        input_output_aliases={8: 2},
+        compiler_params=PARAMS,
+    )(tile_pos, tile_count, recv_count, features, tile_vals, recv_dest, ghost_weight, hub_weight, far, incoming)
     last = partner(far, "feat", 1)
-    every = [neigh] + [partner(neigh, "feat", k) for k in range(1, feats)]
-
-    output, back, *returned = pl.pallas_call(
-        functools.partial(dense_kernel, slots, hub_here, feats, count),
+    far_neigh = partner(neigh, "feat", 2)
+    every = [neigh, partner(neigh, "feat", 1), far_neigh, partner(far_neigh, "feat", 1)]
+
+    output, back, returned = pl.pallas_call(
+        functools.partial(dense_kernel, slots, hub_here, feats),
         out_shape=(
             shape((rows, cols), BF),
             shape((rows, cols), F32),
-            *stacked(width + share),
+            shape((peers, width + share, cols), BF),
         ),
-        in_specs=[SMEM] * 2 + [VMEM] * (4 + 2 * feats),
-        out_specs=(VMEM,) * (2 + count),
+        in_specs=[SMEM] + [VMEM] * (4 + 2 * feats),
+        out_specs=(VMEM,) * 3,
         scratch_shapes=[
-            hold(width + share),
             pltpu.VMEM((rows, full), F32),
             pltpu.VMEM((rows, full), BF),
             pltpu.VMEM((16, full), BF),
         ],
         compiler_params=PARAMS,
-    )(dom, me, features, w_self, w_neigh, mix, pack, near, far, last, *every)
-
-    arrived = exchange(returned, "dom")
+    )(me, features, w_self, w_neigh, mix, pack, near, far, last, *every)
+
+    arrived = exchange(returned)
     grad_features, grad_bias, part = pl.pallas_call(
         functools.partial(gather_kernel, scale, slots, width),
         out_shape=(
             shape((rows, cols), BF),
             shape((1, cols), F32),
-            shape((share, cols) if direct else (peers, share, cols), BF),
+            shape((peers, share, cols), BF),
         ),
-        in_specs=[SMEM] + [VMEM] * (3 + count),
+        in_specs=[VMEM] * 4,
         out_specs=(VMEM,) * 3,
-        scratch_shapes=[hold(width + share)],
-        compiler_params=PARAMS,
-    )(dom, back, send_rows, hub_rows, *arrived)
-    parts = exchange([part] * count, "dom")
+        compiler_params=PARAMS,
+    )(back, send_rows, hub_rows, arrived)
+    parts = exchange(part)
     grad_self, grad_neigh = pl.pallas_call(
         functools.partial(spread_kernel, scale),
         out_shape=(shape((depth, full), F32), shape((depth, full), F32)),
-        in_specs=[SMEM] + [VMEM] * count,
+        in_specs=[VMEM],
         out_specs=(VMEM, VMEM),
-        scratch_shapes=[hold(share)],
-        compiler_params=PARAMS,
-    )(dom, *parts)
+        compiler_params=PARAMS,
+    )(parts)
     return output, grad_features, grad_self, grad_neigh, grad_bias.reshape(cols)
 
 

time: 64.8 us -> 57.3 us (0.88)
  starting transfers between devices: 38.7 us -> 9.88 us
  blocking collectives: 0 us -> 27.3 us
  local copies, waits for them, and re-layouts: 4.32 us -> 0.82 us
  waiting for transfers between devices: 14.8 us -> 11.4 us
  Pallas kernels: 5.13 us -> 6.09 us
    ppermute x27 -> x6, starting transfers between devices: 38.7 us -> 3.91 us  [partner(): lax.ppermute(block, axis, [(i, i ^ k) for i in range(lax.axis_size(axis))])]
    all_to_all x0 -> x2, blocking collectives: none -> 27.3 us  [exchange(): lax.all_to_all(blocks, 'dom', split_axis=0, concat_axis=0, tiled=True)]
    ppermute x27 -> x6, waiting for transfers between devices: 14.8 us -> 5 us  [partner(): lax.ppermute(block, axis, [(i, i ^ k) for i in range(lax.axis_size(axis))])]
    all_to_all x0 -> x1, waiting for transfers between devices: none -> 6.41 us  [exchange(): lax.all_to_all(blocks, 'dom', split_axis=0, concat_axis=0, tiled=True)]
    all_to_all x0 -> x1, starting transfers between devices: none -> 5.97 us  [exchange(): lax.all_to_all(blocks, 'dom', split_axis=0, concat_axis=0, tiled=True)]
    unnamed x33 -> x23, local copies, waits for them, and re-layouts: 4.32 us -> 0.82 us
    pallas_call x2, Pallas kernels: 2.29 us -> 3.3 us  [the longest x1 2.07 us: on_device(): pl.pallas_call(functools.partial(send_kernel, width), out_shape=(shape((p...]
  transfers between devices with their start and end apart: 27 -> 7, of which waited for: 10 -> 3; matrix products, arithmetic and copies ran while one was open for 0% -> 0% of each run, Pallas kernels for 2% -> 2%
where the time goes in v3:
time: 57.3 us; the launch traced here: 56.9 us
  blocking collectives  27.3 us (48%)
  waiting for transfers between devices  11.4 us (20%)
  starting transfers between devices  9.88 us (17%)
  Pallas kernels  6.09 us (11%)
  between operations  1.42 us (2%)
  local copies, waits for them, and re-layouts  0.82 us (1%)
    all_to_all x2, blocking collectives, exchange(): lax.all_to_all(blocks, 'dom', split_axis=0, concat_axis=0, tiled=True)  27.3 us
    all_to_all x1, waiting for transfers between devices, exchange(): lax.all_to_all(blocks, 'dom', split_axis=0, concat_axis=0, tiled=True)  6.41 us
    all_to_all x1, starting transfers between devices, exchange(): lax.all_to_all(blocks, 'dom', split_axis=0, concat_axis=0, tiled=True)  5.97 us
    ppermute x6, waiting for transfers between devices, partner(): lax.ppermute(block, axis, [(i, i ^ k) for i in range(lax.axis_size(axis))])  5 us
    ppermute x6, starting transfers between devices, partner(): lax.ppermute(block, axis, [(i, i ^ k) for i in range(lax.axis_size(axis))])  3.91 us
    pallas_call x1, Pallas kernels, on_device(): pl.pallas_call(functools.partial(send_kernel, width), out_shape=(shape((p...  2.07 us
    pallas_call x1, Pallas kernels, on_device(): pl.pallas_call(functools.partial(dense_kernel, slots, hub_here, feats), o...  1.22 us
  transfers between devices with their start and end apart: 7, of which 3 were waited for; matrix products, arithmetic and copies ran while one was open for 0% of the time, Pallas kernels for 2%

profile of v3, /device:TPU:0, one launch (start us, length us, event | category | flops | bytes accessed | tf_op | source)
XLA Modules:
  0.0 56.9 jit_solution(2402648906492807093)
XLA Ops:
  0.6 2.1 %shard_map.173 = (bf16[8,64,128]{2,1,0:T(8,128)(2,1)}, bf16[1552,128]{1,0:T(8,128)(2,1)S(1)}) custom-call(bf16[256,128]{1,0:T(8,128)(2,1)} %x_ref.5, bf16[256,128]{1,0:T(8,128)(2,1)} %cot_ref.1, bf16[128,512]{1,0:T(8,128)(2,1)} %ws_ref.3, bf16[128,512]{1,0:T(8,128)(2,1)} %wn_ref.3, bf16[1,128]{1,0:T(2,128)(2,1)} %bitcast.3, s32[1,8,48]{2,1,0:T(8,128)} %send_ref.3, ...), custom_call_target="tpu_custom_call" | custom-call | tf_op jit(solution)/shard_map/pallas_call | solution.py:245
  2.7 3.0 %collective-permute-start = (bf16[1552,128]{1,0:T(8,128)(2,1)S(1)}, bf16[1552,128]{1,0:T(8,128)(2,1)S(1)}, u32[]{:S(2)}, u32[]{:S(2)}) collective-permute-start(bf16[1552,128]{1,0:T(8,128)(2,1)S(1)} %get-tuple-element.18.refs_0_), channel_id=1, source_target_pairs={{0,2},{1,3},{2,0},{3,1},{4,6},{5,7},{6,4},{7,5},{8,10},{9,11},{10,... | collective-permute-start | bytes 1191944 | tf_op jit(solution)/shard_map/ppermute | solution.py:208
  5.7 6.0 %all-to-all-start = ((bf16[8,64,128]{2,1,0:T(8,128)(2,1)}), bf16[8,64,128]{2,1,0:T(8,128)(2,1)S(1)}, u32[]{:S(2)}, u32[]{:S(2)}) async-start(bf16[8,64,128]{2,1,0:T(8,128)(2,1)} %get-tuple-element.19), calls=%async_computation | async-start | bytes 262144 | tf_op jit(solution)/shard_map/all_to_all | solution.py:212
  11.7 0.1 collective-permute-start.1
  12.4 0.0 copy-start.5
  12.4 0.0 copy-start.6
  12.5 0.0 copy-start.8
  12.5 0.0 copy-start.9
  12.5 0.1 copy.20.hw_ref
  12.6 0.0 copy-start.2
  12.6 6.4 %all-to-all-done.got_ref = bf16[8,64,128]{2,1,0:T(8,128)(2,1)S(1)} async-done(((bf16[8,64,128]{2,1,0:T(8,128)(2,1)}), bf16[8,64,128]{2,1,0:T(8,128)(2,1)S(1)}, u32[]{:S(2)}, u32[]{:S(2)}) %all-to-all-start) | async-done | bytes 131104 | tf_op jit(solution)/shard_map/all_to_all | solution.py:212
  19.0 0.0 collective-permute-done.far_ref
  19.0 0.0 copy-done
  19.0 0.0 copy-done.5
  19.1 0.0 copy-done.6
  19.1 0.0 copy-done.8
  19.1 1.0 %shard_map.174 = (bf16[256,768]{1,0:T(8,128)(2,1)S(1)}, bf16[256,128]{1,0:T(8,128)(2,1)S(1)}, bf16[1552,128]{1,0:T(8,128)(2,1)S(1)}) custom-call(s32[1,4]{1,0:T(1,128)S(1)} %copy-done.8, s32[1]{0:T(128)S(6)} %copy.22.count_ref, s32[1,8]{1,0:T(1,128)S(1)} %copy-done.9, bf16[256,128]{1,0:T(8,128)(2,1)S(1)} %copy-done, ...), custom_call_target="tpu_custom_call", output_to_operand_aliasing={{2}: (8, {})} | custom-call | tf_op jit(solution)/shard_map/pallas_call | solution.py:262
  20.1 0.1 collective-permute-start.2
  20.1 0.6 %collective-permute-start.4 = (bf16[256,128]{1,0:T(8,128)(2,1)S(1)}, bf16[256,128]{1,0:T(8,128)(2,1)S(1)}, u32[]{:S(2)}, u32[]{:S(2)}) collective-permute-start(bf16[256,128]{1,0:T(8,128)(2,1)S(1)} %get-tuple-element.22.refs_4_), channel_id=1, source_target_pairs={{0,2},{1,3},{2,0},{3,1},{4,6},{5,7},{6,4},{7,5},{8,10},{9,11},{10,... | collective-permute-start | bytes 196616 | tf_op jit(solution)/shard_map/ppermute | solution.py:208
  20.7 0.2 collective-permute-start.3
  20.9 3.7 %collective-permute-done.4.refs_6_ = bf16[256,128]{1,0:T(8,128)(2,1)S(1)} collective-permute-done((bf16[256,128]{1,0:T(8,128)(2,1)S(1)}, bf16[256,128]{1,0:T(8,128)(2,1)S(1)}, u32[]{:S(2)}, u32[]{:S(2)}) %collective-permute-start.4) | collective-permute-done | bytes 65568 | tf_op jit(solution)/shard_map/ppermute | solution.py:208
  24.6 0.0 collective-permute-start.5
  24.7 0.0 collective-permute-done.1.refs_1_
  24.7 0.0 collective-permute-done.3.refs_5_
  24.7 1.2 %collective-permute-done.5.refs_7_ = bf16[256,128]{1,0:T(8,128)(2,1)S(1)} collective-permute-done((bf16[256,128]{1,0:T(8,128)(2,1)S(1)}, bf16[256,128]{1,0:T(8,128)(2,1)S(1)}, u32[]{:S(2)}, u32[]{:S(2)}) %collective-permute-start.5) | collective-permute-done | bytes 65568 | tf_op jit(solution)/shard_map/ppermute | solution.py:208
  25.9 0.0 collective-permute-done.2.refs_3_
  25.9 1.2 %shard_map.175 = (bf16[256,128]{1,0:T(8,128)(2,1)}, f32[256,128]{1,0:T(8,128)S(1)}, bf16[8,192,128]{2,1,0:T(8,128)(2,1)S(1)}) custom-call(s32[1]{0:T(128)} %bitcast.me_ref, bf16[256,128]{1,0:T(8,128)(2,1)S(1)} %copy-done, bf16[128,512]{1,0:T(8,128)(2,1)S(1)} %copy-done.1, bf16[128,512]{1,0:T(8,128)(2,1)S(1)} %copy-done.2, ...), custom_call_target="tpu_custom_call" | custom-call | tf_op jit(solution)/shard_map/pallas_call | solution.py:274
  27.1 15.2 %all_to_all.15.got_ref = bf16[8,192,128]{2,1,0:T(8,128)(2,1)S(1)} all-to-all(bf16[8,192,128]{2,1,0:T(8,128)(2,1)S(1)} %get-tuple-element.25), channel_id=1, replica_groups=mesh['dom'=8,'feat'=4] {'dom'}, dimensions={0} | all-to-all | bytes 786432 | tf_op jit(solution)/shard_map/all_to_all | solution.py:212
  42.3 0.7 %copy-done.7 = s32[1,2]{1,0:T(1,128)S(1)} copy-done((s32[1,2]{1,0:T(1,128)S(1)}, s32[1,2]{1,0:T(1,128)}, u32[]{:S(2)}) %copy-start.7) | copy-done | bytes 32
  43.0 1.0 %shard_map.176 = (bf16[256,128]{1,0:T(8,128)(2,1)}, f32[1,128]{1,0:T(1,128)}, bf16[8,128,128]{2,1,0:T(8,128)(2,1)S(1)}) custom-call(f32[256,128]{1,0:T(8,128)S(1)} %get-tuple-element.24.back_ref, s32[1,8,48]{2,1,0:T(8,128)S(1)} %copy-done.4, s32[1,2]{1,0:T(1,128)S(1)} %copy-done.7, bf16[8,192,128]{2,1,0:T(8,128)(2,1)S(1)} %all_to_all.15.got_ref), custom_call_target="tpu_custom_call" | custom-call | tf_op jit(solution)/shard_map/pallas_call | solution.py:292
  43.9 12.1 %all_to_all.16.got_ref = bf16[8,128,128]{2,1,0:T(8,128)(2,1)S(1)} all-to-all(bf16[8,128,128]{2,1,0:T(8,128)(2,1)S(1)} %get-tuple-element.27), channel_id=1, replica_groups=mesh['dom'=8,'feat'=4] {'dom'}, dimensions={0} | all-to-all | bytes 524288 | tf_op jit(solution)/shard_map/all_to_all | solution.py:212
  56.0 0.9 %shard_map.177 = (f32[128,512]{1,0:T(8,128)}, f32[128,512]{1,0:T(8,128)}) custom-call(bf16[8,128,128]{2,1,0:T(8,128)(2,1)S(1)} %all_to_all.16.got_ref), custom_call_target="tpu_custom_call" | custom-call | tf_op jit(solution)/shard_map/pallas_call | solution.py:304
  (12 shorter events, 0.0 us)
Async XLA Ops:
  2.7 16.3 %collective-permute-start = (bf16[1552,128]{1,0:T(8,128)(2,1)S(1)}, bf16[1552,128]{1,0:T(8,128)(2,1)S(1)}, u32[]{:S(2)}, u32[]{:S(2)}) collective-permute-start(bf16[1552,128]{1,0:T(8,128)(2,1)S(1)} %get-tuple-element.18.refs_0_), channel_id=1, source_target_pairs={{0,2},{1,3},{2,0},{3,1},{4,6},{5,7},{6,4},{7,5},{8,10},{9,11},{10,... | collective-permute-start | bytes 1191944 | tf_op jit(solution)/shard_map/ppermute | solution.py:208
  5.7 6.7 %copy-start.10 = (bf16[256,16]{0,1:T(8,128)(2,1)S(1)}, bf16[256,16]{0,1:T(8,128)(2,1)}, u32[]{:S(2)}) copy-start(bf16[256,16]{0,1:T(8,128)(2,1)} %param.27) | copy-start | bytes 24580
  5.7 13.3 %copy-start.3 = (bf16[1,4,128,128]{3,2,1,0:T(8,128)(2,1)S(1)}, bf16[1,4,128,128]{3,2,1,0:T(8,128)(2,1)}, u32[]{:S(2)}) copy-start(bf16[1,4,128,128]{3,2,1,0:T(8,128)(2,1)} %tile_ref.1) | copy-start | bytes 393220
  5.7 13.3 %all-to-all-start = ((bf16[8,64,128]{2,1,0:T(8,128)(2,1)}), bf16[8,64,128]{2,1,0:T(8,128)(2,1)S(1)}, u32[]{:S(2)}, u32[]{:S(2)}) async-start(bf16[8,64,128]{2,1,0:T(8,128)(2,1)} %get-tuple-element.19), calls=%async_computation | async-start | bytes 262144 | tf_op jit(solution)/shard_map/all_to_all | solution.py:212
  11.7 7.4 %copy-start = (bf16[256,128]{1,0:T(8,128)(2,1)S(1)}, bf16[256,128]{1,0:T(8,128)(2,1)}, u32[]{:S(2)}) copy-start(bf16[256,128]{1,0:T(8,128)(2,1)} %x_ref.5) | copy-start | bytes 196612
  11.7 13.0 %collective-permute-start.1 = (bf16[1552,128]{1,0:T(8,128)(2,1)S(1)}, bf16[1552,128]{1,0:T(8,128)(2,1)S(1)}, u32[]{:S(2)}, u32[]{:S(2)}) collective-permute-start(bf16[1552,128]{1,0:T(8,128)(2,1)S(1)} %get-tuple-element.18.refs_0_), channel_id=1, source_target_pairs={{0,1},{1,0},{2,3},{3,2},{4,5},{5,4},{6,7},{7,6},{8,9},{9,8},{10,11... | collective-permute-start | bytes 1191944 | tf_op jit(solution)/shard_map/ppermute | solution.py:208
  12.4 6.6 %copy-start.5 = (s32[1,8,48]{2,1,0:T(8,128)S(1)}, s32[1,8,48]{2,1,0:T(8,128)}, u32[]{:S(2)}) copy-start(s32[1,8,48]{2,1,0:T(8,128)} %dest_ref.1) | copy-start | bytes 4612
  12.4 6.6 %copy-start.6 = (f32[1,8,48]{2,1,0:T(8,128)S(1)}, f32[1,8,48]{2,1,0:T(8,128)}, u32[]{:S(2)}) copy-start(f32[1,8,48]{2,1,0:T(8,128)} %gw_ref.1) | copy-start | bytes 4612
  12.5 6.6 %copy-start.8 = (s32[1,4]{1,0:T(1,128)S(1)}, s32[1,4]{1,0:T(1,128)}, u32[]{:S(2)}) copy-start(s32[1,4]{1,0:T(1,128)} %pos_ref.1) | copy-start | bytes 52
  12.5 6.6 %copy-start.9 = (s32[1,8]{1,0:T(1,128)S(1)}, s32[1,8]{1,0:T(1,128)}, u32[]{:S(2)}) copy-start(s32[1,8]{1,0:T(1,128)} %live_ref.1) | copy-start | bytes 100
  12.6 13.3 %copy-start.1 = (bf16[128,512]{1,0:T(8,128)(2,1)S(1)}, bf16[128,512]{1,0:T(8,128)(2,1)}, u32[]{:S(2)}) copy-start(bf16[128,512]{1,0:T(8,128)(2,1)} %ws_ref.3) | copy-start | bytes 393220
  12.6 13.3 %copy-start.2 = (bf16[128,512]{1,0:T(8,128)(2,1)S(1)}, bf16[128,512]{1,0:T(8,128)(2,1)}, u32[]{:S(2)}) copy-start(bf16[128,512]{1,0:T(8,128)(2,1)} %wn_ref.3) | copy-start | bytes 393220
  20.1 5.8 %collective-permute-start.2 = (bf16[1552,128]{1,0:T(8,128)(2,1)S(1)}, bf16[1552,128]{1,0:T(8,128)(2,1)S(1)}, u32[]{:S(2)}, u32[]{:S(2)}) collective-permute-start(bf16[1552,128]{1,0:T(8,128)(2,1)S(1)} %get-tuple-element.21.refs_2_), channel_id=1, source_target_pairs={{0,1},{1,0},{2,3},{3,2},{4,5},{5,4},{6,7},{7,6},{8,9},{9,8},{10,11... | collective-permute-start | bytes 1191944 | tf_op jit(solution)/shard_map/ppermute | solution.py:208
  20.1 4.5 %collective-permute-start.4 = (bf16[256,128]{1,0:T(8,128)(2,1)S(1)}, bf16[256,128]{1,0:T(8,128)(2,1)S(1)}, u32[]{:S(2)}, u32[]{:S(2)}) collective-permute-start(bf16[256,128]{1,0:T(8,128)(2,1)S(1)} %get-tuple-element.22.refs_4_), channel_id=1, source_target_pairs={{0,2},{1,3},{2,0},{3,1},{4,6},{5,7},{6,4},{7,5},{8,10},{9,11},{10,... | collective-permute-start | bytes 196616 | tf_op jit(solution)/shard_map/ppermute | solution.py:208
  20.7 3.9 %collective-permute-start.3 = (bf16[256,128]{1,0:T(8,128)(2,1)S(1)}, bf16[256,128]{1,0:T(8,128)(2,1)S(1)}, u32[]{:S(2)}, u32[]{:S(2)}) collective-permute-start(bf16[256,128]{1,0:T(8,128)(2,1)S(1)} %get-tuple-element.22.refs_4_), channel_id=1, source_target_pairs={{0,1},{1,0},{2,3},{3,2},{4,5},{5,4},{6,7},{7,6},{8,9},{9,8},{10,11... | collective-permute-start | bytes 196616 | tf_op jit(solution)/shard_map/ppermute | solution.py:208
  24.6 1.3 %collective-permute-start.5 = (bf16[256,128]{1,0:T(8,128)(2,1)S(1)}, bf16[256,128]{1,0:T(8,128)(2,1)S(1)}, u32[]{:S(2)}, u32[]{:S(2)}) collective-permute-start(bf16[256,128]{1,0:T(8,128)(2,1)S(1)} %collective-permute-done.4.refs_6_), channel_id=1, source_target_pairs={{0,1},{1,0},{2,3},{3,2},{4,5},{5,4},{6,7},{7,6},{8,9},{9,8},{10,11... | collective-permute-start | bytes 196616 | tf_op jit(solution)/shard_map/ppermute | solution.py:208
  27.1 15.2 %copy-start.4 = (s32[1,8,48]{2,1,0:T(8,128)S(1)}, s32[1,8,48]{2,1,0:T(8,128)}, u32[]{:S(2)}) copy-start(s32[1,8,48]{2,1,0:T(8,128)} %send_ref.3) | copy-start | bytes 4612
  42.3 0.7 %copy-start.7 = (s32[1,2]{1,0:T(1,128)S(1)}, s32[1,2]{1,0:T(1,128)}, u32[]{:S(2)}) copy-start(s32[1,2]{1,0:T(1,128)} %hub_ref.3) | copy-start | bytes 28

commit v4 on v3

--- a/solution.py
+++ b/solution.py
@@ -38,7 +38,8 @@
 
 
 def send_kernel(
-    width, x_ref, cot_ref, ws_ref, wn_ref, bias_ref, send_ref, hub_ref, out_ref, pack_ref, send_v, hub_v, bias_v, sems
+    width, x_ref, cot_ref, ws_ref, wn_ref, bias_ref, send_ref, hub_ref,
+    out_ref, pack_ref, mark_ref, send_v, hub_v, bias_v, sems
 ):
     rows, cols = x_ref.shape
     depth, full = ws_ref.shape
@@ -61,6 +62,7 @@
     for copy in copies[:3]:
         copy.wait()
     mark = source_matrix(send_v[0], hub_v[...], rows, width)
+    mark_ref[...] = mark
     taken = lax.dot_general(
         mark, pack_ref[base : base + rows, :], (((0,), (0,)), ((), ())), preferred_element_type=F32
     ).astype(BF)
@@ -71,8 +73,8 @@
 
 
 def neigh_kernel(
-    width, pos_ref, count_ref, live_ref, x_ref, tile_ref, dest_ref, gw_ref, hw_ref, far_ref, got_ref,
-    mix_ref, neigh_ref, passed_ref,
+    width, pos_ref, live_ref, count_ref, x_ref, tile_ref, dest_ref, gw_ref, hw_ref, far_ref, near_ref, got_ref,
+    mix_ref, neigh_ref, passed_far_ref, passed_near_ref,
 ):
     rows, cols = x_ref.shape
     tile = tile_ref.shape[-1]
@@ -80,13 +82,13 @@
     peers, slots = dest_ref.shape[1:]
     side = rows // tile
     lanes = peers * width
-    hubs = hw_ref.shape[1]
+    hubs = hw_ref.shape[0]
     hub_here = hubs // peers
     for r in range(side):
         for c in range(side):
             total = jnp.zeros((tile, tile), BF)
             for t in range(tiles):
-                used = jnp.logical_and(pos_ref[0, t] == r * side + c, t < count_ref[0])
+                used = jnp.logical_and(pos_ref[0, t] == r * side + c, t < count_ref[...])
                 total = jnp.where(used, tile_ref[0, t], total)
             mix_ref[r * tile : (r + 1) * tile, c * tile : (c + 1) * tile] = total
     dest = spread_rows(dest_ref[0].astype(F32), width)
@@ -103,7 +105,7 @@
     place = jnp.where(
         jnp.logical_and(at // width == hub // hub_here, at % width == slots + hub % hub_here), 1.0, 0.0
     ).astype(BF)
-    hub_mix = jnp.dot(hw_ref[...], place, preferred_element_type=F32)
+    hub_mix = lax.dot_general(hw_ref[...], place, (((0,), (0,)), ((), ())), preferred_element_type=F32)
     far = (ghost + hub_mix).astype(BF)
     mix_ref[:, rows:] = far
     total = jnp.dot(mix_ref[:, :rows], x_ref[...], preferred_element_type=F32)
@@ -165,13 +167,11 @@
                 send_ref[at // share + part, width:, :] = block[part * share : (part + 1) * share]
 
 
-def gather_kernel(scale, slots, width, back_ref, send_ref, hub_ref, got_ref, grad_ref, bias_ref, part_ref):
+def gather_kernel(scale, slots, hub_here, width, back_ref, mark_ref, got_ref, grad_ref, bias_ref, part_ref):
     rows, cols = back_ref.shape
-    peers = send_ref.shape[1]
-    hub_here = hub_ref.shape[1]
-    mark = source_matrix(send_ref[0], hub_ref[...], rows, width)
+    peers = got_ref.shape[0]
     near = got_ref[:, :width, :]
-    total = back_ref[...] + jnp.dot(mark, near.reshape(peers * width, cols), preferred_element_type=F32)
+    total = back_ref[...] + jnp.dot(mark_ref[...], near.reshape(peers * width, cols), preferred_element_type=F32)
     grad_ref[...] = total.astype(BF)
     first = slots + hub_here
     bias = jnp.zeros((2, cols), F32)
@@ -242,11 +242,11 @@
     pack_rows = 2 * blocks * depth + 2 * rows + 16
 
     raw = (features, cotangent, w_self, w_neigh, bias.reshape(1, cols), send_rows, hub_rows)
-    outgoing, pack = pl.pallas_call(
+    outgoing, pack, mark = pl.pallas_call(
         functools.partial(send_kernel, width),
-        out_shape=(shape((peers, width, cols), BF), shape((pack_rows, cols), BF)),
+        out_shape=(shape((peers, width, cols), BF), shape((pack_rows, cols), BF), shape((rows, lanes), BF)),
         in_specs=[HBM] * 7,
-        out_specs=(VMEM, VMEM),
+        out_specs=(VMEM,) * 3,
         scratch_shapes=[
             pltpu.VMEM(send_rows.shape, jnp.int32),
             pltpu.VMEM(hub_rows.shape, jnp.int32),
@@ -257,16 +257,24 @@
     )(*(pltpu.with_memory_space_constraint(a, pltpu.HBM) for a in raw))
 
     far = partner(pack, "feat", 2)
+    incoming = exchange(outgoing)
+    mix, neigh, far, pack = pl.pallas_call(
+        functools.partial(neigh_kernel, width),
+        out_shape=(
+            shape((rows, rows + lanes), BF),
+            shape((rows, cols), BF),
+            shape((pack_rows, cols), BF),
+            shape((pack_rows, cols), BF),
+        ),
+        in_specs=[SMEM] * 2 + [VMEM] * 6 + [ANY, ANY, VMEM],
+        out_specs=(VMEM, VMEM, ANY, ANY),
+        input_output_aliases={8: 2, 9: 3},
+        compiler_params=PARAMS,
+    )(
+        tile_pos, recv_count, tile_count.reshape(1, 1), features, tile_vals, recv_dest, ghost_weight, hub_weight.T,
+        far, pack, incoming,
+    )
     near = partner(pack, "feat", 1)
-    incoming = exchange(outgoing)
-    mix, neigh, far = pl.pallas_call(
-        functools.partial(neigh_kernel, width),
-        out_shape=(shape((rows, rows + lanes), BF), shape((rows, cols), BF), shape((pack_rows, cols), BF)),
-        in_specs=[SMEM] * 3 + [VMEM] * 5 + [ANY, VMEM],
-        out_specs=(VMEM, VMEM, ANY),
-        input_output_aliases={8: 2},
-        compiler_params=PARAMS,
-    )(tile_pos, tile_count, recv_count, features, tile_vals, recv_dest, ghost_weight, hub_weight, far, incoming)
     last = partner(far, "feat", 1)
     far_neigh = partner(neigh, "feat", 2)
     every = [neigh, partner(neigh, "feat", 1), far_neigh, partner(far_neigh, "feat", 1)]
@@ -290,16 +298,16 @@
 
     arrived = exchange(returned)
     grad_features, grad_bias, part = pl.pallas_call(
-        functools.partial(gather_kernel, scale, slots, width),
+        functools.partial(gather_kernel, scale, slots, hub_here, width),
         out_shape=(
             shape((rows, cols), BF),
             shape((1, cols), F32),
             shape((peers, share, cols), BF),
         ),
-        in_specs=[VMEM] * 4,
+        in_specs=[VMEM] * 3,
         out_specs=(VMEM,) * 3,
         compiler_params=PARAMS,
-    )(back, send_rows, hub_rows, arrived)
+    )(back, mark, arrived)
     parts = exchange(part)
     grad_self, grad_neigh = pl.pallas_call(
         functools.partial(spread_kernel, scale),

time: 57.3 us -> 57.4 us (level)
  transfers between devices with their start and end apart: 7 -> 7, of which waited for: 3 -> 3; matrix products, arithmetic and copies ran while one was open for 0% -> 0% of each run, Pallas kernels for 2% -> 0%
where the time goes in v4:
time: 57.4 us; the launch traced here: 56.9 us
  blocking collectives  27.2 us (47%)
  waiting for transfers between devices  11.7 us (20%)
  starting transfers between devices  10.1 us (18%)
  Pallas kernels  5.99 us (10%)
  between operations  1.38 us (2%)
  local copies, waits for them, and re-layouts  0.65 us (1%)
    all_to_all x2, blocking collectives, exchange(): lax.all_to_all(blocks, 'dom', split_axis=0, concat_axis=0, tiled=True)  27.2 us
    all_to_all x1, waiting for transfers between devices, exchange(): lax.all_to_all(blocks, 'dom', split_axis=0, concat_axis=0, tiled=True)  6.68 us
    all_to_all x1, starting transfers between devices, exchange(): lax.all_to_all(blocks, 'dom', split_axis=0, concat_axis=0, tiled=True)  5.98 us
    ppermute x6, waiting for transfers between devices, partner(): lax.ppermute(block, axis, [(i, i ^ k) for i in range(lax.axis_size(axis))])  4.99 us
    ppermute x6, starting transfers between devices, partner(): lax.ppermute(block, axis, [(i, i ^ k) for i in range(lax.axis_size(axis))])  4.11 us
    pallas_call x1, Pallas kernels, on_device(): pl.pallas_call(functools.partial(send_kernel, width), out_shape=(shape((p...  2.08 us
    pallas_call x1, Pallas kernels, on_device(): pl.pallas_call(functools.partial(dense_kernel, slots, hub_here, feats), o...  1.22 us
  transfers between devices with their start and end apart: 7, of which 3 were waited for; matrix products, arithmetic and copies ran while one was open for 0% of the time, Pallas kernels for 0%

profile of v4, /device:TPU:0, one launch (start us, length us, event | category | flops | bytes accessed | tf_op | source)
XLA Modules:
  0.0 56.9 jit_solution(18042920482017838281)
XLA Ops:
  0.6 2.1 %shard_map.173 = (bf16[8,64,128]{2,1,0:T(8,128)(2,1)}, bf16[1552,128]{1,0:T(8,128)(2,1)S(1)}, bf16[256,512]{1,0:T(8,128)(2,1)S(1)}) custom-call(bf16[256,128]{1,0:T(8,128)(2,1)} %x_ref.5, bf16[256,128]{1,0:T(8,128)(2,1)} %cot_ref.1, bf16[128,512]{1,0:T(8,128)(2,1)} %ws_ref.3, bf16[128,512]{1,0:T(8,128)(2,1)} %wn_ref.3, bf16[1,128]{1,0:T(2,128)(2,1)} %bitcast.7, ...), custom_call_target="tpu_custom_call" | custom-call | tf_op jit(solution)/shard_map/pallas_call | solution.py:245
  2.7 3.0 %collective-permute-start = (bf16[1552,128]{1,0:T(8,128)(2,1)S(1)}, bf16[1552,128]{1,0:T(8,128)(2,1)S(1)}, u32[]{:S(2)}, u32[]{:S(2)}) collective-permute-start(bf16[1552,128]{1,0:T(8,128)(2,1)S(1)} %get-tuple-element.20.near_ref), channel_id=1, source_target_pairs={{0,2},{1,3},{2,0},{3,1},{4,6},{5,7},{6,4},{7,5},{8,10},{9,11},{10,... | collective-permute-start | bytes 1191944 | tf_op jit(solution)/shard_map/ppermute | solution.py:208
  5.7 0.0 copy-start
  5.7 0.0 copy-start.3
  5.7 6.0 %all-to-all-start = ((bf16[8,64,128]{2,1,0:T(8,128)(2,1)}), bf16[8,64,128]{2,1,0:T(8,128)(2,1)S(1)}, u32[]{:S(2)}, u32[]{:S(2)}) async-start(bf16[8,64,128]{2,1,0:T(8,128)(2,1)} %get-tuple-element.21), calls=%async_computation | async-start | bytes 262144 | tf_op jit(solution)/shard_map/all_to_all | solution.py:212
  12.4 6.7 %all-to-all-done.got_ref = bf16[8,64,128]{2,1,0:T(8,128)(2,1)S(1)} async-done(((bf16[8,64,128]{2,1,0:T(8,128)(2,1)}), bf16[8,64,128]{2,1,0:T(8,128)(2,1)S(1)}, u32[]{:S(2)}, u32[]{:S(2)}) %all-to-all-start) | async-done | bytes 131104 | tf_op jit(solution)/shard_map/all_to_all | solution.py:212
  19.1 0.0 collective-permute-done.far_ref
  19.1 0.0 copy-done
  19.1 0.0 copy-done.3
  19.1 0.0 copy-done.4
  19.1 0.0 copy-done.6
  19.1 0.0 copy-done.5
  19.1 0.6 %copy-done.7 = s32[1,4]{1,0:T(1,128)S(1)} copy-done((s32[1,4]{1,0:T(1,128)S(1)}, s32[1,4]{1,0:T(1,128)}, u32[]{:S(2)}) %copy-start.7) | copy-done | bytes 40
  19.7 0.0 copy-done.8
  19.7 1.0 %shard_map.174 = (bf16[256,768]{1,0:T(8,128)(2,1)S(1)}, bf16[256,128]{1,0:T(8,128)(2,1)S(1)}, bf16[1552,128]{1,0:T(8,128)(2,1)S(1)}, bf16[1552,128]{1,0:T(8,128)(2,1)S(1)}) custom-call(s32[1,4]{1,0:T(1,128)S(1)} %copy-done.7, s32[1,8]{1,0:T(1,128)S(1)} %copy-done.8, s32[1,1]{1,0:T(1,128)} %bitcast.5.count_ref, ...), custom_call_target="tpu_custom_call", output_to_operand_aliasing={{2}: (8, {}), {3}: (9, {})} | custom-call | tf_op jit(solution)/shard_map/pallas_call | solution.py:261
  20.7 0.1 collective-permute-start.1
  20.8 0.5 collective-permute-start.2
  21.3 0.5 collective-permute-start.4
  21.9 0.0 collective-permute-start.3
  21.9 3.7 %collective-permute-done.4.refs_6_ = bf16[256,128]{1,0:T(8,128)(2,1)S(1)} collective-permute-done((bf16[256,128]{1,0:T(8,128)(2,1)S(1)}, bf16[256,128]{1,0:T(8,128)(2,1)S(1)}, u32[]{:S(2)}, u32[]{:S(2)}) %collective-permute-start.4) | collective-permute-done | bytes 65568 | tf_op jit(solution)/shard_map/ppermute | solution.py:208
  25.6 0.0 collective-permute-start.5
  25.6 0.0 collective-permute-done.3.refs_5_
  25.6 1.2 %collective-permute-done.5.refs_7_ = bf16[256,128]{1,0:T(8,128)(2,1)S(1)} collective-permute-done((bf16[256,128]{1,0:T(8,128)(2,1)S(1)}, bf16[256,128]{1,0:T(8,128)(2,1)S(1)}, u32[]{:S(2)}, u32[]{:S(2)}) %collective-permute-start.5) | collective-permute-done | bytes 65568 | tf_op jit(solution)/shard_map/ppermute | solution.py:208
  26.8 0.0 collective-permute-done.1.refs_1_
  26.8 0.0 collective-permute-done.2.refs_3_
  26.8 0.0 copy-done.1
  26.8 0.0 copy-done.2
  26.9 1.2 %shard_map.175 = (bf16[256,128]{1,0:T(8,128)(2,1)}, f32[256,128]{1,0:T(8,128)S(1)}, bf16[8,192,128]{2,1,0:T(8,128)(2,1)S(1)}) custom-call(s32[1]{0:T(128)} %bitcast.me_ref, bf16[256,128]{1,0:T(8,128)(2,1)S(1)} %copy-done, bf16[128,512]{1,0:T(8,128)(2,1)S(1)} %copy-done.1, bf16[128,512]{1,0:T(8,128)(2,1)S(1)} %copy-done.2, ...), custom_call_target="tpu_custom_call" | custom-call | tf_op jit(solution)/shard_map/pallas_call | solution.py:282
  28.1 15.0 %all_to_all.15.got_ref = bf16[8,192,128]{2,1,0:T(8,128)(2,1)S(1)} all-to-all(bf16[8,192,128]{2,1,0:T(8,128)(2,1)S(1)} %get-tuple-element.29), channel_id=1, replica_groups=mesh['dom'=8,'feat'=4] {'dom'}, dimensions={0} | all-to-all | bytes 786432 | tf_op jit(solution)/shard_map/all_to_all | solution.py:212
  43.1 0.8 %shard_map.176 = (bf16[256,128]{1,0:T(8,128)(2,1)}, f32[1,128]{1,0:T(1,128)}, bf16[8,128,128]{2,1,0:T(8,128)(2,1)S(1)}) custom-call(f32[256,128]{1,0:T(8,128)S(1)} %get-tuple-element.27.back_ref, bf16[256,512]{1,0:T(8,128)(2,1)S(1)} %get-tuple-element.28.mark_ref, bf16[8,192,128]{2,1,0:T(8,128)(2,1)S(1)} %all_to_all.15.got_ref), custom_call_target="tpu_custom_call" | custom-call | tf_op jit(solution)/shard_map/pallas_call | solution.py:300
  44.0 12.1 %all_to_all.16.got_ref = bf16[8,128,128]{2,1,0:T(8,128)(2,1)S(1)} all-to-all(bf16[8,128,128]{2,1,0:T(8,128)(2,1)S(1)} %get-tuple-element.31), channel_id=1, replica_groups=mesh['dom'=8,'feat'=4] {'dom'}, dimensions={0} | all-to-all | bytes 524288 | tf_op jit(solution)/shard_map/all_to_all | solution.py:212
  56.1 0.9 %shard_map.177 = (f32[128,512]{1,0:T(8,128)}, f32[128,512]{1,0:T(8,128)}) custom-call(bf16[8,128,128]{2,1,0:T(8,128)(2,1)S(1)} %all_to_all.16.got_ref), custom_call_target="tpu_custom_call" | custom-call | tf_op jit(solution)/shard_map/pallas_call | solution.py:312
  (7 shorter events, 0.0 us)
Async XLA Ops:
  2.7 16.3 %collective-permute-start = (bf16[1552,128]{1,0:T(8,128)(2,1)S(1)}, bf16[1552,128]{1,0:T(8,128)(2,1)S(1)}, u32[]{:S(2)}, u32[]{:S(2)}) collective-permute-start(bf16[1552,128]{1,0:T(8,128)(2,1)S(1)} %get-tuple-element.20.near_ref), channel_id=1, source_target_pairs={{0,2},{1,3},{2,0},{3,1},{4,6},{5,7},{6,4},{7,5},{8,10},{9,11},{10,... | collective-permute-start | bytes 1191944 | tf_op jit(solution)/shard_map/ppermute | solution.py:208
  5.7 13.3 %copy-start = (bf16[256,128]{1,0:T(8,128)(2,1)S(1)}, bf16[256,128]{1,0:T(8,128)(2,1)}, u32[]{:S(2)}) copy-start(bf16[256,128]{1,0:T(8,128)(2,1)} %x_ref.5) | copy-start | bytes 196612
  5.7 13.3 %copy-start.3 = (bf16[1,4,128,128]{3,2,1,0:T(8,128)(2,1)S(1)}, bf16[1,4,128,128]{3,2,1,0:T(8,128)(2,1)}, u32[]{:S(2)}) copy-start(bf16[1,4,128,128]{3,2,1,0:T(8,128)(2,1)} %tile_ref.1) | copy-start | bytes 393220
  5.7 13.4 %copy-start.4 = (bf16[256,16]{0,1:T(8,128)(2,1)S(1)}, bf16[256,16]{0,1:T(8,128)(2,1)}, u32[]{:S(2)}) copy-start(bf16[256,16]{0,1:T(8,128)(2,1)} %param.27) | copy-start | bytes 24580
  5.7 13.4 %copy-start.6 = (f32[1,8,48]{2,1,0:T(8,128)S(1)}, f32[1,8,48]{2,1,0:T(8,128)}, u32[]{:S(2)}) copy-start(f32[1,8,48]{2,1,0:T(8,128)} %gw_ref.1) | copy-start | bytes 4612
  5.7 13.3 %all-to-all-start = ((bf16[8,64,128]{2,1,0:T(8,128)(2,1)}), bf16[8,64,128]{2,1,0:T(8,128)(2,1)S(1)}, u32[]{:S(2)}, u32[]{:S(2)}) async-start(bf16[8,64,128]{2,1,0:T(8,128)(2,1)} %get-tuple-element.21), calls=%async_computation | async-start | bytes 262144 | tf_op jit(solution)/shard_map/all_to_all | solution.py:212
  11.7 7.4 %copy-start.5 = (s32[1,8,48]{2,1,0:T(8,128)S(1)}, s32[1,8,48]{2,1,0:T(8,128)}, u32[]{:S(2)}) copy-start(s32[1,8,48]{2,1,0:T(8,128)} %dest_ref.1) | copy-start | bytes 4612
  19.1 0.7 %copy-start.7 = (s32[1,4]{1,0:T(1,128)S(1)}, s32[1,4]{1,0:T(1,128)}, u32[]{:S(2)}) copy-start(s32[1,4]{1,0:T(1,128)} %pos_ref.1) | copy-start | bytes 52
  19.1 0.7 %copy-start.8 = (s32[1,8]{1,0:T(1,128)S(1)}, s32[1,8]{1,0:T(1,128)}, u32[]{:S(2)}) copy-start(s32[1,8]{1,0:T(1,128)} %live_ref.1) | copy-start | bytes 100
  19.7 7.1 %copy-start.1 = (bf16[128,512]{1,0:T(8,128)(2,1)S(1)}, bf16[128,512]{1,0:T(8,128)(2,1)}, u32[]{:S(2)}) copy-start(bf16[128,512]{1,0:T(8,128)(2,1)} %ws_ref.3) | copy-start | bytes 393220
  19.7 7.1 %copy-start.2 = (bf16[128,512]{1,0:T(8,128)(2,1)S(1)}, bf16[128,512]{1,0:T(8,128)(2,1)}, u32[]{:S(2)}) copy-start(bf16[128,512]{1,0:T(8,128)(2,1)} %wn_ref.3) | copy-start | bytes 393220
  20.7 6.1 %collective-permute-start.1 = (bf16[1552,128]{1,0:T(8,128)(2,1)S(1)}, bf16[1552,128]{1,0:T(8,128)(2,1)S(1)}, u32[]{:S(2)}, u32[]{:S(2)}) collective-permute-start(bf16[1552,128]{1,0:T(8,128)(2,1)S(1)} %get-tuple-element.23.refs_0_), channel_id=1, source_target_pairs={{0,1},{1,0},{2,3},{3,2},{4,5},{5,4},{6,7},{7,6},{8,9},{9,8},{10,11... | collective-permute-start | bytes 1191944 | tf_op jit(solution)/shard_map/ppermute | solution.py:208
  20.8 6.0 %collective-permute-start.2 = (bf16[1552,128]{1,0:T(8,128)(2,1)S(1)}, bf16[1552,128]{1,0:T(8,128)(2,1)S(1)}, u32[]{:S(2)}, u32[]{:S(2)}) collective-permute-start(bf16[1552,128]{1,0:T(8,128)(2,1)S(1)} %get-tuple-element.24.refs_2_), channel_id=1, source_target_pairs={{0,1},{1,0},{2,3},{3,2},{4,5},{5,4},{6,7},{7,6},{8,9},{9,8},{10,11... | collective-permute-start | bytes 1191944 | tf_op jit(solution)/shard_map/ppermute | solution.py:208
  21.3 4.3 %collective-permute-start.4 = (bf16[256,128]{1,0:T(8,128)(2,1)S(1)}, bf16[256,128]{1,0:T(8,128)(2,1)S(1)}, u32[]{:S(2)}, u32[]{:S(2)}) collective-permute-start(bf16[256,128]{1,0:T(8,128)(2,1)S(1)} %get-tuple-element.25.refs_4_), channel_id=1, source_target_pairs={{0,2},{1,3},{2,0},{3,1},{4,6},{5,7},{6,4},{7,5},{8,10},{9,11},{10,... | collective-permute-start | bytes 196616 | tf_op jit(solution)/shard_map/ppermute | solution.py:208
  21.9 3.7 %collective-permute-start.3 = (bf16[256,128]{1,0:T(8,128)(2,1)S(1)}, bf16[256,128]{1,0:T(8,128)(2,1)S(1)}, u32[]{:S(2)}, u32[]{:S(2)}) collective-permute-start(bf16[256,128]{1,0:T(8,128)(2,1)S(1)} %get-tuple-element.25.refs_4_), channel_id=1, source_target_pairs={{0,1},{1,0},{2,3},{3,2},{4,5},{5,4},{6,7},{7,6},{8,9},{9,8},{10,11... | collective-permute-start | bytes 196616 | tf_op jit(solution)/shard_map/ppermute | solution.py:208
  25.6 1.3 %collective-permute-start.5 = (bf16[256,128]{1,0:T(8,128)(2,1)S(1)}, bf16[256,128]{1,0:T(8,128)(2,1)S(1)}, u32[]{:S(2)}, u32[]{:S(2)}) collective-permute-start(bf16[256,128]{1,0:T(8,128)(2,1)S(1)} %collective-permute-done.4.refs_6_), channel_id=1, source_target_pairs={{0,1},{1,0},{2,3},{3,2},{4,5},{5,4},{6,7},{7,6},{8,9},{9,8},{10,11... | collective-permute-start | bytes 196616 | tf_op jit(solution)/shard_map/ppermute | solution.py:208

commit v5 on v4

--- a/solution.py
+++ b/solution.py
@@ -37,9 +37,27 @@
     return jnp.where(row == index, 1.0, 0.0).astype(BF)
 
 
+def source_rows(send, hubs, rows, width):
+    peers, slots = send.shape
+    hub_here = hubs.shape[1]
+    lanes = peers * width
+    slot = lax.broadcasted_iota(jnp.int32, (lanes, slots), 0) % width
+    place = jnp.where(slot == lax.broadcasted_iota(jnp.int32, (lanes, slots), 1), 1.0, 0.0).astype(BF)
+    wide = lax.dot_general(
+        place, send.astype(F32).astype(BF), (((1,), (1,)), ((), ())), preferred_element_type=F32
+    )
+    line = lax.broadcasted_iota(jnp.int32, (lanes, peers), 0)
+    for k in range(hub_here):
+        wide = jnp.where(line % width == slots + k, hubs[0:1, k : k + 1].astype(F32), wide)
+    wide = jnp.where(line % width < slots + hub_here, wide, -1.0)
+    wide = jnp.where(line // width == lax.broadcasted_iota(jnp.int32, (lanes, peers), 1), wide, 0.0)
+    index = jnp.dot(wide.astype(BF), jnp.ones((peers, rows), BF), preferred_element_type=F32)
+    row = lax.broadcasted_iota(jnp.int32, (lanes, rows), 1).astype(F32)
+    return jnp.where(row == index, 1.0, 0.0).astype(BF)
+
+
 def send_kernel(
-    width, x_ref, cot_ref, ws_ref, wn_ref, bias_ref, send_ref, hub_ref,
-    out_ref, pack_ref, mark_ref, send_v, hub_v, bias_v, sems
+    width, x_ref, cot_ref, ws_ref, wn_ref, bias_ref, send_ref, hub_ref, out_ref, pack_ref, send_v, hub_v, bias_v, sems
 ):
     rows, cols = x_ref.shape
     depth, full = ws_ref.shape
@@ -59,45 +77,52 @@
     copies = [pltpu.make_async_copy(src, dst, sems.at[i]) for i, (src, dst) in enumerate(moves)]
     for copy in copies:
         copy.start()
-    for copy in copies[:3]:
+    for copy in copies[:2]:
         copy.wait()
-    mark = source_matrix(send_v[0], hub_v[...], rows, width)
-    mark_ref[...] = mark
-    taken = lax.dot_general(
-        mark, pack_ref[base : base + rows, :], (((0,), (0,)), ((), ())), preferred_element_type=F32
-    ).astype(BF)
+    mark = source_rows(send_v[0], hub_v[...], rows, width)
+    copies[2].wait()
+    taken = jnp.dot(mark, pack_ref[base : base + rows, :], preferred_element_type=F32).astype(BF)
     out_ref[...] = taken.reshape(out_ref.shape)
     for copy in copies[3:]:
         copy.wait()
     pack_ref[base + 2 * rows :, :] = jnp.broadcast_to(bias_v[...], (16, cols))
 
 
-def neigh_kernel(
-    width, pos_ref, live_ref, count_ref, x_ref, tile_ref, dest_ref, gw_ref, hw_ref, far_ref, near_ref, got_ref,
-    mix_ref, neigh_ref, passed_far_ref, passed_near_ref,
+def mix_kernel(
+    width, count_ref, pos_ref, live_ref, tile_ref, dest_ref, gw_ref, hw_ref, send_ref, hub_ref,
+    mix_ref, turned_ref, mark_ref, pos_v, live_v, tile_v, dest_v, gw_v, hw_v, send_v, hub_v, sems,
 ):
-    rows, cols = x_ref.shape
-    tile = tile_ref.shape[-1]
-    tiles = tile_ref.shape[1]
-    peers, slots = dest_ref.shape[1:]
+    pairs = (
+        (pos_ref, pos_v), (live_ref, live_v), (tile_ref, tile_v), (dest_ref, dest_v),
+        (gw_ref, gw_v), (hw_ref, hw_v), (send_ref, send_v), (hub_ref, hub_v),
+    )
+    copies = [pltpu.make_async_copy(src, dst, sems.at[i]) for i, (src, dst) in enumerate(pairs)]
+    for copy in copies:
+        copy.start()
+    for copy in copies:
+        copy.wait()
+    rows = mix_ref.shape[0]
+    tiles, tile = tile_v.shape[1:3]
+    peers, slots = dest_v.shape[1:]
     side = rows // tile
     lanes = peers * width
-    hubs = hw_ref.shape[0]
+    hubs = hw_v.shape[0]
     hub_here = hubs // peers
     for r in range(side):
         for c in range(side):
             total = jnp.zeros((tile, tile), BF)
             for t in range(tiles):
-                used = jnp.logical_and(pos_ref[0, t] == r * side + c, t < count_ref[...])
-                total = jnp.where(used, tile_ref[0, t], total)
+                used = jnp.logical_and(pos_v[0:1, t : t + 1] == r * side + c, t < count_ref[...])
+                total = jnp.where(used, tile_v[0, t], total)
             mix_ref[r * tile : (r + 1) * tile, c * tile : (c + 1) * tile] = total
-    dest = spread_rows(dest_ref[0].astype(F32), width)
-    coef = spread_rows(gw_ref[0], width)
-    lane = lax.broadcasted_iota(jnp.int32, (1, lanes), 1)
-    limit = jnp.zeros((1, lanes), jnp.int32)
-    for q in range(peers):
-        limit = jnp.where(lane // width == q, live_ref[0, q], limit)
-    coef = jnp.where(lane % width < jnp.minimum(limit, slots), coef, 0.0)
+    dest = spread_rows(dest_v[0].astype(F32), width)
+    coef = spread_rows(gw_v[0], width)
+    peer = lax.broadcasted_iota(jnp.int32, (peers, lanes), 0)
+    at = lax.broadcasted_iota(jnp.int32, (peers, lanes), 1)
+    owner = jnp.where(at // width == peer, 1.0, 0.0).astype(BF)
+    limit = jnp.dot(live_v[...].astype(F32).astype(BF), owner, preferred_element_type=F32)
+    lane = lax.broadcasted_iota(jnp.int32, (1, lanes), 1) % width
+    coef = jnp.where(jnp.logical_and(lane.astype(F32) < limit, lane < slots), coef, 0.0)
     row = lax.broadcasted_iota(jnp.int32, (rows, lanes), 0).astype(F32)
     ghost = jnp.where(row == dest, coef, 0.0)
     hub = lax.broadcasted_iota(jnp.int32, (hubs, lanes), 0)
@@ -105,22 +130,28 @@
     place = jnp.where(
         jnp.logical_and(at // width == hub // hub_here, at % width == slots + hub % hub_here), 1.0, 0.0
     ).astype(BF)
-    hub_mix = lax.dot_general(hw_ref[...], place, (((0,), (0,)), ((), ())), preferred_element_type=F32)
-    far = (ghost + hub_mix).astype(BF)
-    mix_ref[:, rows:] = far
+    hub_mix = lax.dot_general(hw_v[...], place, (((0,), (0,)), ((), ())), preferred_element_type=F32)
+    mix_ref[:, rows:] = (ghost + hub_mix).astype(BF)
+    turned_ref[...] = mix_ref[...].T
+    mark_ref[...] = source_matrix(send_v[0], hub_v[...], rows, width)
+
+
+def neigh_kernel(x_ref, mix_ref, far_ref, got_ref, neigh_ref, passed_ref):
+    rows, cols = x_ref.shape
+    lanes = mix_ref.shape[1] - rows
     total = jnp.dot(mix_ref[:, :rows], x_ref[...], preferred_element_type=F32)
-    total = total + jnp.dot(far, got_ref[...].reshape(lanes, cols), preferred_element_type=F32)
+    total = total + jnp.dot(mix_ref[:, rows:], got_ref[...].reshape(lanes, cols), preferred_element_type=F32)
     neigh_ref[...] = total.astype(BF)
 
 
-def dense_kernel(slots, hub_here, feats, me_ref, x_ref, ws_ref, wn_ref, mix_ref, *refs):
+def dense_kernel(slots, hub_here, feats, me_ref, x_ref, ws_ref, wn_ref, turned_ref, *refs):
     pack_refs, n_refs = refs[:feats], refs[feats : 2 * feats]
     out_ref, back_ref, send_ref, pre_ref, cot_ref, bias_ref = refs[2 * feats :]
     rows, cols = x_ref.shape
     depth, full = ws_ref.shape
     blocks = full // cols
     peers, height = send_ref.shape[:2]
-    lanes = mix_ref.shape[1] - rows
+    lanes = turned_ref.shape[0] - rows
     width = lanes // peers
     me = me_ref[0]
     base = 2 * blocks * depth
@@ -146,9 +177,7 @@
     both = jnp.concatenate([ws_ref[...], wn_ref[...]], axis=0)
     into = lax.dot_general(grad, both, (((1,), (1,)), ((), ())), preferred_element_type=F32)
     neigh_grad = into[:, depth:].astype(BF)
-    spread = lax.dot_general(
-        mix_ref[...], neigh_grad, (((0,), (0,)), ((), ())), preferred_element_type=F32
-    )
+    spread = jnp.dot(turned_ref[...], neigh_grad, preferred_element_type=F32)
     back_ref[...] = into[:, :depth] + spread[:rows]
     sums = jnp.sum(cot_ref[:, mine].astype(F32), axis=0, keepdims=True)
     high = sums.astype(BF).astype(F32)
@@ -241,12 +270,15 @@
     me = lax.axis_index("feat").astype(jnp.int32).reshape(1)
     pack_rows = 2 * blocks * depth + 2 * rows + 16
 
-    raw = (features, cotangent, w_self, w_neigh, bias.reshape(1, cols), send_rows, hub_rows)
-    outgoing, pack, mark = pl.pallas_call(
+    def pinned(*arrays):
+        return [pltpu.with_memory_space_constraint(a, pltpu.HBM) for a in arrays]
+
+    first = pinned(features, cotangent, w_self, w_neigh, bias.reshape(1, cols), send_rows, hub_rows)
+    outgoing, pack = pl.pallas_call(
         functools.partial(send_kernel, width),
-        out_shape=(shape((peers, width, cols), BF), shape((pack_rows, cols), BF), shape((rows, lanes), BF)),
-        in_specs=[HBM] * 7,
-        out_specs=(VMEM,) * 3,
+        out_shape=(shape((peers, width, cols), BF), shape((pack_rows, cols), BF)),
+        in_specs=[HBM] * len(first),
+        out_specs=(VMEM,) * 2,
         scratch_shapes=[
             pltpu.VMEM(send_rows.shape, jnp.int32),
             pltpu.VMEM(hub_rows.shape, jnp.int32),
@@ -254,27 +286,35 @@
             pltpu.SemaphoreType.DMA((5 + 2 * blocks,)),
         ],
         compiler_params=PARAMS,
-    )(*(pltpu.with_memory_space_constraint(a, pltpu.HBM) for a in raw))
+    )(*first)
 
     far = partner(pack, "feat", 2)
+    near = partner(pack, "feat", 1)
     incoming = exchange(outgoing)
-    mix, neigh, far, pack = pl.pallas_call(
-        functools.partial(neigh_kernel, width),
+    edges = pinned(
+        tile_pos, recv_count, tile_vals, recv_dest, ghost_weight, hub_weight.T, send_rows, hub_rows
+    )
+    mix, turned, mark = pl.pallas_call(
+        functools.partial(mix_kernel, width),
         out_shape=(
             shape((rows, rows + lanes), BF),
-            shape((rows, cols), BF),
-            shape((pack_rows, cols), BF),
-            shape((pack_rows, cols), BF),
+            shape((rows + lanes, rows), BF),
+            shape((rows, lanes), BF),
         ),
-        in_specs=[SMEM] * 2 + [VMEM] * 6 + [ANY, ANY, VMEM],
-        out_specs=(VMEM, VMEM, ANY, ANY),
-        input_output_aliases={8: 2, 9: 3},
-        compiler_params=PARAMS,
-    )(
-        tile_pos, recv_count, tile_count.reshape(1, 1), features, tile_vals, recv_dest, ghost_weight, hub_weight.T,
-        far, pack, incoming,
-    )
-    near = partner(pack, "feat", 1)
+        in_specs=[VMEM] + [HBM] * len(edges),
+        out_specs=(VMEM,) * 3,
+        scratch_shapes=[pltpu.VMEM(a.shape, a.dtype) for a in edges] + [pltpu.SemaphoreType.DMA((len(edges),))],
+        compiler_params=PARAMS,
+        cost_estimate=pl.CostEstimate(flops=10**8, bytes_accessed=3 * 10**6, transcendentals=0),
+    )(tile_count.reshape(1, 1), *edges)
+    neigh, far = pl.pallas_call(
+        neigh_kernel,
+        out_shape=(shape((rows, cols), BF), shape((pack_rows, cols), BF)),
+        in_specs=[VMEM, VMEM, ANY, VMEM],
+        out_specs=(VMEM, ANY),
+        input_output_aliases={2: 1},
+        compiler_params=PARAMS,
+    )(features, mix, far, incoming)
     last = partner(far, "feat", 1)
     far_neigh = partner(neigh, "feat", 2)
     every = [neigh, partner(neigh, "feat", 1), far_neigh, partner(far_neigh, "feat", 1)]
@@ -294,7 +334,7 @@
             pltpu.VMEM((16, full), BF),
         ],
         compiler_params=PARAMS,
-    )(me, features, w_self, w_neigh, mix, pack, near, far, last, *every)
+    )(me, features, w_self, w_neigh, turned, pack, near, far, last, *every)
 
     arrived = exchange(returned)
     grad_features, grad_bias, part = pl.pallas_call(

time: 57.4 us -> 55.5 us (0.967)
  waiting for transfers between devices: 11.7 us -> 10.2 us
  Pallas kernels: 5.99 us -> 6.76 us
  local copies, waits for them, and re-layouts: 0.65 us -> 0.02 us
    all_to_all x1, waiting for transfers between devices: 6.68 us -> 5.22 us  [exchange(): lax.all_to_all(blocks, 'dom', split_axis=0, concat_axis=0, tiled=True)]
    pallas_call x1 -> x2, Pallas kernels: 1 us -> 1.7 us  [the longest x1 1.44 us: on_device(): pl.pallas_call(functools.partial(mix_kernel, width), out_shape=(shape((ro...]
    unnamed x18 -> x6, local copies, waits for them, and re-layouts: 0.65 us -> 0.02 us
  transfers between devices with their start and end apart: 7 -> 7, of which waited for: 3 -> 3; matrix products, arithmetic and copies ran while one was open for 0% -> 0% of each run, Pallas kernels for 0% -> 3%
where the time goes in v5:
time: 55.5 us; the launch traced here: 55.2 us
  blocking collectives  27.1 us (49%)
  waiting for transfers between devices  10.2 us (18%)
  starting transfers between devices  9.68 us (17%)
  Pallas kernels  6.76 us (12%)
  between operations  1.35 us (2%)
    all_to_all x2, blocking collectives, exchange(): lax.all_to_all(blocks, 'dom', split_axis=0, concat_axis=0, tiled=True)  27.1 us
    all_to_all x1, starting transfers between devices, exchange(): lax.all_to_all(blocks, 'dom', split_axis=0, concat_axis=0, tiled=True)  5.83 us
    all_to_all x1, waiting for transfers between devices, exchange(): lax.all_to_all(blocks, 'dom', split_axis=0, concat_axis=0, tiled=True)  5.22 us
    ppermute x6, waiting for transfers between devices, partner(): lax.ppermute(block, axis, [(i, i ^ k) for i in range(lax.axis_size(axis))])  5 us
    ppermute x6, starting transfers between devices, partner(): lax.ppermute(block, axis, [(i, i ^ k) for i in range(lax.axis_size(axis))])  3.84 us
    pallas_call x1, Pallas kernels, on_device(): pl.pallas_call(functools.partial(send_kernel, width), out_shape=(shape((p...  2.15 us
    pallas_call x1, Pallas kernels, on_device(): pl.pallas_call(functools.partial(mix_kernel, width), out_shape=(shape((ro...  1.44 us
    pallas_call x1, Pallas kernels, on_device(): pl.pallas_call(functools.partial(dense_kernel, slots, hub_here, feats), o...  1.22 us
  transfers between devices with their start and end apart: 7, of which 3 were waited for; matrix products, arithmetic and copies ran while one was open for 0% of the time, Pallas kernels for 3%

profile of v5, /device:TPU:0, one launch (start us, length us, event | category | flops | bytes accessed | tf_op | source)
XLA Modules:
  0.0 55.2 jit_solution(13494219130851980323)
XLA Ops:
  0.6 2.1 %shard_map.174 = (bf16[8,64,128]{2,1,0:T(8,128)(2,1)}, bf16[1552,128]{1,0:T(8,128)(2,1)S(1)}) custom-call(bf16[256,128]{1,0:T(8,128)(2,1)} %x_ref.5, bf16[256,128]{1,0:T(8,128)(2,1)} %cot_ref.1, bf16[128,512]{1,0:T(8,128)(2,1)} %ws_ref.3, bf16[128,512]{1,0:T(8,128)(2,1)} %wn_ref.3, bf16[1,128]{1,0:T(2,128)(2,1)} %bitcast.6, s32[1,8,48]{2,1,0:T(8,128)} %send_ref.3, ...), custom_call_target="tpu_custom_call" | custom-call | tf_op jit(solution)/shard_map/pallas_call | solution.py:277
  2.8 3.0 %collective-permute-start.1 = (bf16[1552,128]{1,0:T(8,128)(2,1)S(1)}, bf16[1552,128]{1,0:T(8,128)(2,1)S(1)}, u32[]{:S(2)}, u32[]{:S(2)}) collective-permute-start(bf16[1552,128]{1,0:T(8,128)(2,1)S(1)} %get-tuple-element.21.refs_0_), channel_id=1, source_target_pairs={{0,2},{1,3},{2,0},{3,1},{4,6},{5,7},{6,4},{7,5},{8,10},{9,11},{10,... | collective-permute-start | bytes 1191944 | tf_op jit(solution)/shard_map/ppermute | solution.py:237
  5.8 5.8 %all-to-all-start = ((bf16[8,64,128]{2,1,0:T(8,128)(2,1)}), bf16[8,64,128]{2,1,0:T(8,128)(2,1)S(1)}, u32[]{:S(2)}, u32[]{:S(2)}) async-start(bf16[8,64,128]{2,1,0:T(8,128)(2,1)} %get-tuple-element.23), calls=%async_computation | async-start | bytes 262144 | tf_op jit(solution)/shard_map/all_to_all | solution.py:241
  11.6 0.0 collective-permute-start
  12.3 0.0 copy-start
  12.3 1.4 %shard_map.173 = (bf16[256,768]{1,0:T(8,128)(2,1)S(1)}, bf16[768,256]{1,0:T(8,128)(2,1)S(1)}, bf16[256,512]{1,0:T(8,128)(2,1)S(1)}) custom-call(s32[1,1]{1,0:T(1,128)} %bitcast.5.count_ref, s32[1,4]{1,0:T(1,128)} %pos_ref.1, s32[1,8]{1,0:T(1,128)} %live_ref.1, bf16[1,4,128,128]{3,2,1,0:T(8,128)(2,1)} %tile_ref.1, s32[1,8,48]{2,1,0:T(8,128)} %dest_ref.1, ...), custom_call_target="tpu_custom_call" | custom-call | flops 100000000 | bytes 3000000 | tf_op jit(solution)/shard_map/pallas_call | solution.py:297
  13.7 5.2 %all-to-all-done.got_ref = bf16[8,64,128]{2,1,0:T(8,128)(2,1)S(1)} async-done(((bf16[8,64,128]{2,1,0:T(8,128)(2,1)}), bf16[8,64,128]{2,1,0:T(8,128)(2,1)S(1)}, u32[]{:S(2)}, u32[]{:S(2)}) %all-to-all-start) | async-done | bytes 131104 | tf_op jit(solution)/shard_map/all_to_all | solution.py:241
  19.0 0.0 collective-permute-done.1.far_ref
  19.0 0.0 copy-done
  19.0 0.0 copy-start.1
  19.0 0.0 copy-start.2
  19.0 0.3 shard_map.175
  19.2 0.1 collective-permute-start.2
  19.3 0.6 %collective-permute-start.4 = (bf16[256,128]{1,0:T(8,128)(2,1)S(1)}, bf16[256,128]{1,0:T(8,128)(2,1)S(1)}, u32[]{:S(2)}, u32[]{:S(2)}) collective-permute-start(bf16[256,128]{1,0:T(8,128)(2,1)S(1)} %get-tuple-element.25.refs_4_), channel_id=1, source_target_pairs={{0,2},{1,3},{2,0},{3,1},{4,6},{5,7},{6,4},{7,5},{8,10},{9,11},{10,... | collective-permute-start | bytes 196616 | tf_op jit(solution)/shard_map/ppermute | solution.py:237
  19.9 0.2 collective-permute-start.3
  20.1 3.7 %collective-permute-done.4.refs_6_ = bf16[256,128]{1,0:T(8,128)(2,1)S(1)} collective-permute-done((bf16[256,128]{1,0:T(8,128)(2,1)S(1)}, bf16[256,128]{1,0:T(8,128)(2,1)S(1)}, u32[]{:S(2)}, u32[]{:S(2)}) %collective-permute-start.4) | collective-permute-done | bytes 65568 | tf_op jit(solution)/shard_map/ppermute | solution.py:237
  23.8 0.0 collective-permute-start.5
  23.8 0.0 collective-permute-done.refs_1_
  23.8 0.0 collective-permute-done.3.refs_5_
  23.9 1.2 %collective-permute-done.5.refs_7_ = bf16[256,128]{1,0:T(8,128)(2,1)S(1)} collective-permute-done((bf16[256,128]{1,0:T(8,128)(2,1)S(1)}, bf16[256,128]{1,0:T(8,128)(2,1)S(1)}, u32[]{:S(2)}, u32[]{:S(2)}) %collective-permute-start.5) | collective-permute-done | bytes 65568 | tf_op jit(solution)/shard_map/ppermute | solution.py:237
  25.1 0.0 collective-permute-done.2.refs_3_
  25.1 0.0 copy-done.1
  25.1 0.0 copy-done.2
  25.1 1.2 %shard_map.176 = (bf16[256,128]{1,0:T(8,128)(2,1)}, f32[256,128]{1,0:T(8,128)S(1)}, bf16[8,192,128]{2,1,0:T(8,128)(2,1)S(1)}) custom-call(s32[1]{0:T(128)} %bitcast.me_ref, bf16[256,128]{1,0:T(8,128)(2,1)S(1)} %copy-done, bf16[128,512]{1,0:T(8,128)(2,1)S(1)} %copy-done.1, bf16[128,512]{1,0:T(8,128)(2,1)S(1)} %copy-done.2, ...), custom_call_target="tpu_custom_call" | custom-call | tf_op jit(solution)/shard_map/pallas_call | solution.py:322
  26.3 15.0 %all_to_all.15.got_ref = bf16[8,192,128]{2,1,0:T(8,128)(2,1)S(1)} all-to-all(bf16[8,192,128]{2,1,0:T(8,128)(2,1)S(1)} %get-tuple-element.29), channel_id=1, replica_groups=mesh['dom'=8,'feat'=4] {'dom'}, dimensions={0} | all-to-all | bytes 786432 | tf_op jit(solution)/shard_map/all_to_all | solution.py:241
  41.3 0.8 %shard_map.177 = (bf16[256,128]{1,0:T(8,128)(2,1)}, f32[1,128]{1,0:T(1,128)}, bf16[8,128,128]{2,1,0:T(8,128)(2,1)S(1)}) custom-call(f32[256,128]{1,0:T(8,128)S(1)} %get-tuple-element.27.back_ref, bf16[256,512]{1,0:T(8,128)(2,1)S(1)} %get-tuple-element.28.mark_ref, bf16[8,192,128]{2,1,0:T(8,128)(2,1)S(1)} %all_to_all.15.got_ref), custom_call_target="tpu_custom_call" | custom-call | tf_op jit(solution)/shard_map/pallas_call | solution.py:340
  42.2 12.1 %all_to_all.16.got_ref = bf16[8,128,128]{2,1,0:T(8,128)(2,1)S(1)} all-to-all(bf16[8,128,128]{2,1,0:T(8,128)(2,1)S(1)} %get-tuple-element.31), channel_id=1, replica_groups=mesh['dom'=8,'feat'=4] {'dom'}, dimensions={0} | all-to-all | bytes 524288 | tf_op jit(solution)/shard_map/all_to_all | solution.py:241
  54.3 0.9 %shard_map.178 = (f32[128,512]{1,0:T(8,128)}, f32[128,512]{1,0:T(8,128)}) custom-call(bf16[8,128,128]{2,1,0:T(8,128)(2,1)S(1)} %all_to_all.16.got_ref), custom_call_target="tpu_custom_call" | custom-call | tf_op jit(solution)/shard_map/pallas_call | solution.py:352
Async XLA Ops:
  2.8 16.2 %collective-permute-start.1 = (bf16[1552,128]{1,0:T(8,128)(2,1)S(1)}, bf16[1552,128]{1,0:T(8,128)(2,1)S(1)}, u32[]{:S(2)}, u32[]{:S(2)}) collective-permute-start(bf16[1552,128]{1,0:T(8,128)(2,1)S(1)} %get-tuple-element.21.refs_0_), channel_id=1, source_target_pairs={{0,2},{1,3},{2,0},{3,1},{4,6},{5,7},{6,4},{7,5},{8,10},{9,11},{10,... | collective-permute-start | bytes 1191944 | tf_op jit(solution)/shard_map/ppermute | solution.py:237
  5.8 13.2 %all-to-all-start = ((bf16[8,64,128]{2,1,0:T(8,128)(2,1)}), bf16[8,64,128]{2,1,0:T(8,128)(2,1)S(1)}, u32[]{:S(2)}, u32[]{:S(2)}) async-start(bf16[8,64,128]{2,1,0:T(8,128)(2,1)} %get-tuple-element.23), calls=%async_computation | async-start | bytes 262144 | tf_op jit(solution)/shard_map/all_to_all | solution.py:241
  11.6 12.2 %collective-permute-start = (bf16[1552,128]{1,0:T(8,128)(2,1)S(1)}, bf16[1552,128]{1,0:T(8,128)(2,1)S(1)}, u32[]{:S(2)}, u32[]{:S(2)}) collective-permute-start(bf16[1552,128]{1,0:T(8,128)(2,1)S(1)} %get-tuple-element.21.refs_0_), channel_id=1, source_target_pairs={{0,1},{1,0},{2,3},{3,2},{4,5},{5,4},{6,7},{7,6},{8,9},{9,8},{10,11... | collective-permute-start | bytes 1191944 | tf_op jit(solution)/shard_map/ppermute | solution.py:237
  12.3 6.7 %copy-start = (bf16[256,128]{1,0:T(8,128)(2,1)S(1)}, bf16[256,128]{1,0:T(8,128)(2,1)}, u32[]{:S(2)}) copy-start(bf16[256,128]{1,0:T(8,128)(2,1)} %x_ref.5) | copy-start | bytes 196612
  19.0 6.1 %copy-start.1 = (bf16[128,512]{1,0:T(8,128)(2,1)S(1)}, bf16[128,512]{1,0:T(8,128)(2,1)}, u32[]{:S(2)}) copy-start(bf16[128,512]{1,0:T(8,128)(2,1)} %ws_ref.3) | copy-start | bytes 393220
  19.0 6.1 %copy-start.2 = (bf16[128,512]{1,0:T(8,128)(2,1)S(1)}, bf16[128,512]{1,0:T(8,128)(2,1)}, u32[]{:S(2)}) copy-start(bf16[128,512]{1,0:T(8,128)(2,1)} %wn_ref.3) | copy-start | bytes 393220
  19.2 5.8 %collective-permute-start.2 = (bf16[1552,128]{1,0:T(8,128)(2,1)S(1)}, bf16[1552,128]{1,0:T(8,128)(2,1)S(1)}, u32[]{:S(2)}, u32[]{:S(2)}) collective-permute-start(bf16[1552,128]{1,0:T(8,128)(2,1)S(1)} %get-tuple-element.24.refs_2_), channel_id=1, source_target_pairs={{0,1},{1,0},{2,3},{3,2},{4,5},{5,4},{6,7},{7,6},{8,9},{9,8},{10,11... | collective-permute-start | bytes 1191944 | tf_op jit(solution)/shard_map/ppermute | solution.py:237
  19.3 4.5 %collective-permute-start.4 = (bf16[256,128]{1,0:T(8,128)(2,1)S(1)}, bf16[256,128]{1,0:T(8,128)(2,1)S(1)}, u32[]{:S(2)}, u32[]{:S(2)}) collective-permute-start(bf16[256,128]{1,0:T(8,128)(2,1)S(1)} %get-tuple-element.25.refs_4_), channel_id=1, source_target_pairs={{0,2},{1,3},{2,0},{3,1},{4,6},{5,7},{6,4},{7,5},{8,10},{9,11},{10,... | collective-permute-start | bytes 196616 | tf_op jit(solution)/shard_map/ppermute | solution.py:237
  19.9 3.9 %collective-permute-start.3 = (bf16[256,128]{1,0:T(8,128)(2,1)S(1)}, bf16[256,128]{1,0:T(8,128)(2,1)S(1)}, u32[]{:S(2)}, u32[]{:S(2)}) collective-permute-start(bf16[256,128]{1,0:T(8,128)(2,1)S(1)} %get-tuple-element.25.refs_4_), channel_id=1, source_target_pairs={{0,1},{1,0},{2,3},{3,2},{4,5},{5,4},{6,7},{7,6},{8,9},{9,8},{10,11... | collective-permute-start | bytes 196616 | tf_op jit(solution)/shard_map/ppermute | solution.py:237
  23.8 1.3 %collective-permute-start.5 = (bf16[256,128]{1,0:T(8,128)(2,1)S(1)}, bf16[256,128]{1,0:T(8,128)(2,1)S(1)}, u32[]{:S(2)}, u32[]{:S(2)}) collective-permute-start(bf16[256,128]{1,0:T(8,128)(2,1)S(1)} %collective-permute-done.4.refs_6_), channel_id=1, source_target_pairs={{0,1},{1,0},{2,3},{3,2},{4,5},{5,4},{6,7},{7,6},{8,9},{9,8},{10,11... | collective-permute-start | bytes 196616 | tf_op jit(solution)/shard_map/ppermute | solution.py:237

commit v6 on v5

--- a/solution.py
+++ b/solution.py
@@ -144,15 +144,14 @@
     neigh_ref[...] = total.astype(BF)
 
 
-def dense_kernel(slots, hub_here, feats, me_ref, x_ref, ws_ref, wn_ref, turned_ref, *refs):
+def dense_kernel(slots, hub_here, feats, width, me_ref, side_ref, x_ref, ws_ref, wn_ref, turned_ref, *refs):
     pack_refs, n_refs = refs[:feats], refs[feats : 2 * feats]
-    out_ref, back_ref, send_ref, pre_ref, cot_ref, bias_ref = refs[2 * feats :]
+    out_ref, back_ref, send_ref, pre_ref, cot_ref, bias_ref, hold_ref = refs[2 * feats :]
     rows, cols = x_ref.shape
     depth, full = ws_ref.shape
     blocks = full // cols
-    peers, height = send_ref.shape[:2]
+    half, height = send_ref.shape[:2]
     lanes = turned_ref.shape[0] - rows
-    width = lanes // peers
     me = me_ref[0]
     base = 2 * blocks * depth
     pre = jnp.zeros((rows, full), F32)
@@ -184,42 +183,71 @@
     line = lax.broadcasted_iota(jnp.int32, (lanes, cols), 0) % width
     away = jnp.where(line == slots + hub_here, high, spread[rows:])
     away = jnp.where(line == slots + hub_here + 1, sums - high, away)
-    send_ref[:, :width, :] = away.astype(BF).reshape(peers, width, cols)
+    hold_ref[...] = away.astype(BF).reshape(hold_ref.shape)
+    here = side_ref[0] * half
+    send_ref[:, :width, :] = hold_ref[pl.ds(here, half)]
+    send_ref[:, width : 2 * width, :] = hold_ref[pl.ds(half - here, half)]
     pair = jnp.concatenate([x_ref[...], n_refs[0][...]], axis=1)
     weights = lax.dot_general(pair, grad, (((0,), (0,)), ((), ())), preferred_element_type=F32).astype(BF)
-    share = height - width
+    share = height - 2 * width
+    step = min(share, depth)
     for j in range(blocks):
         for kind in range(2):
             block = weights[kind * depth : (kind + 1) * depth, j * cols : (j + 1) * cols]
-            at = (j * 2 + kind) * depth
-            for part in range(depth // share):
-                send_ref[at // share + part, width:, :] = block[part * share : (part + 1) * share]
-
-
-def gather_kernel(scale, slots, hub_here, width, back_ref, mark_ref, got_ref, grad_ref, bias_ref, part_ref):
-    rows, cols = back_ref.shape
-    peers = got_ref.shape[0]
-    near = got_ref[:, :width, :]
-    total = back_ref[...] + jnp.dot(mark_ref[...], near.reshape(peers * width, cols), preferred_element_type=F32)
-    grad_ref[...] = total.astype(BF)
+            for part in range(depth // step):
+                at = (j * 2 + kind) * depth + part * step
+                low = 2 * width + at % share
+                send_ref[at // share, low : low + step, :] = block[part * step : (part + 1) * step]
+
+
+def sum_kernel(width, got_ref, sum_ref, relay_ref):
+    half = got_ref.shape[0]
+    total = jnp.zeros(sum_ref.shape, F32)
+    for j in range(half):
+        total = total + got_ref[j, 2 * width :, :].astype(F32)
+    sum_ref[...] = total.astype(BF)
+    relay_ref[...] = got_ref[:, width : 2 * width, :]
+
+
+def total_kernel(own_ref, other_ref, relay_ref, part_ref, passed_ref):
+    total = (own_ref[...].astype(F32) + other_ref[...].astype(F32)).astype(BF)
+    part_ref[...] = jnp.broadcast_to(total, part_ref.shape)
+
+
+def near_rows(slots, hub_here, width, start, mark_ref, got_ref):
+    half = got_ref.shape[0]
+    cols = got_ref.shape[-1]
+    cut = pl.ds(pl.multiple_of(start * width, 128), half * width)
+    rows = got_ref[:, :width, :]
+    added = jnp.dot(mark_ref[:, cut], rows.reshape(half * width, cols), preferred_element_type=F32)
     first = slots + hub_here
     bias = jnp.zeros((2, cols), F32)
-    share = jnp.zeros(part_ref.shape[-2:], F32)
-    for q in range(peers):
-        bias = bias + got_ref[q, first : first + 2, :].astype(F32)
-        share = share + got_ref[q, width:, :].astype(F32)
-    bias_ref[...] = jnp.sum(bias, axis=0, keepdims=True) * scale
-    part_ref[...] = jnp.broadcast_to(share.astype(BF), part_ref.shape)
-
-
-def spread_kernel(scale, got_ref, self_ref, neigh_ref):
+    for j in range(half):
+        bias = bias + got_ref[j, first : first + 2, :].astype(F32)
+    return added, jnp.sum(bias, axis=0, keepdims=True)
+
+
+def near_kernel(slots, hub_here, width, side_ref, back_ref, mark_ref, got_ref, sum_ref, bias_ref):
+    half = got_ref.shape[0]
+    added, bias = near_rows(slots, hub_here, width, side_ref[0] * half, mark_ref, got_ref)
+    sum_ref[...] = back_ref[...] + added
+    bias_ref[...] = bias
+
+
+def last_kernel(
+    scale, slots, hub_here, width, side_ref, back_ref, near_ref, mark_ref, got_ref, part_ref,
+    grad_ref, bias_ref, self_ref, neigh_ref,
+):
     depth, full = self_ref.shape
-    peers, share, cols = got_ref.shape
-    whole = got_ref[...].reshape(peers * share, cols).astype(F32) * scale
+    half, share, cols = part_ref.shape
+    whole = part_ref[...].reshape(half * share, cols).astype(F32) * scale
     for j in range(full // cols):
         at = 2 * j * depth
         self_ref[:, j * cols : (j + 1) * cols] = whole[at : at + depth]
         neigh_ref[:, j * cols : (j + 1) * cols] = whole[at + depth : at + 2 * depth]
+    added, bias = near_rows(slots, hub_here, width, half - side_ref[0] * half, mark_ref, got_ref)
+    grad_ref[...] = (back_ref[...] + added).astype(BF)
+    bias_ref[...] = (near_ref[...] + bias) * scale
 
 
 VMEM = pl.BlockSpec(memory_space=pltpu.VMEM)
@@ -237,8 +265,8 @@
     return lax.ppermute(block, axis, [(i, i ^ k) for i in range(lax.axis_size(axis))])
 
 
-def exchange(blocks):
-    return lax.all_to_all(blocks, "dom", split_axis=0, concat_axis=0, tiled=True)
+def exchange(blocks, groups=None):
+    return lax.all_to_all(blocks, "dom", split_axis=0, concat_axis=0, axis_index_groups=groups, tiled=True)
 
 
 def on_device(
@@ -264,10 +292,13 @@
     hub_here = hub_rows.shape[-1]
     width = -(-(slots + hub_here + 2) // 16) * 16
     lanes = peers * width
-    share = 2 * blocks * depth // peers
+    half = peers // 2
+    share = 2 * blocks * depth // half
+    halves = [list(range(half)), list(range(half, peers))]
     scale = 1.0 / math.sqrt(peers * rows)
     feats = lax.axis_size("feat")
     me = lax.axis_index("feat").astype(jnp.int32).reshape(1)
+    side = (lax.axis_index("dom") >= half).astype(jnp.int32).reshape(1)
     pack_rows = 2 * blocks * depth + 2 * rows + 16
 
     def pinned(*arrays):
@@ -320,42 +351,62 @@
     every = [neigh, partner(neigh, "feat", 1), far_neigh, partner(far_neigh, "feat", 1)]
 
     output, back, returned = pl.pallas_call(
-        functools.partial(dense_kernel, slots, hub_here, feats),
+        functools.partial(dense_kernel, slots, hub_here, feats, width),
         out_shape=(
             shape((rows, cols), BF),
             shape((rows, cols), F32),
-            shape((peers, width + share, cols), BF),
+            shape((half, 2 * width + share, cols), BF),
         ),
-        in_specs=[SMEM] + [VMEM] * (4 + 2 * feats),
+        in_specs=[SMEM] * 2 + [VMEM] * (4 + 2 * feats),
         out_specs=(VMEM,) * 3,
         scratch_shapes=[
             pltpu.VMEM((rows, full), F32),
             pltpu.VMEM((rows, full), BF),
             pltpu.VMEM((16, full), BF),
+            pltpu.VMEM((peers, width, cols), BF),
         ],
         compiler_params=PARAMS,
-    )(me, features, w_self, w_neigh, turned, pack, near, far, last, *every)
-
-    arrived = exchange(returned)
-    grad_features, grad_bias, part = pl.pallas_call(
-        functools.partial(gather_kernel, scale, slots, hub_here, width),
+    )(me, side, features, w_self, w_neigh, turned, pack, near, far, last, *every)
+
+    arrived = exchange(returned, halves)
+    half_sum, relay = pl.pallas_call(
+        functools.partial(sum_kernel, width),
+        out_shape=(shape((share, cols), BF), shape((half, width, cols), BF)),
+        in_specs=[VMEM],
+        out_specs=(VMEM,) * 2,
+        compiler_params=PARAMS,
+    )(arrived)
+    other_sum = partner(half_sum, "dom", half)
+    back, near_bias = pl.pallas_call(
+        functools.partial(near_kernel, slots, hub_here, width),
+        out_shape=(shape((rows, cols), F32), shape((1, cols), F32)),
+        in_specs=[SMEM] + [VMEM] * 3,
+        out_specs=(VMEM,) * 2,
+        compiler_params=PARAMS,
+        cost_estimate=pl.CostEstimate(flops=10**8, bytes_accessed=10**6, transcendentals=0),
+    )(side, back, mark, arrived)
+    part, relay = pl.pallas_call(
+        total_kernel,
+        out_shape=(shape((half, share, cols), BF), shape((half, width, cols), BF)),
+        in_specs=[VMEM, VMEM, ANY],
+        out_specs=(VMEM, ANY),
+        input_output_aliases={2: 1},
+        compiler_params=PARAMS,
+    )(half_sum, other_sum, relay)
+    crossed = partner(relay, "dom", half)
+    parts = exchange(part, halves)
+    grad_features, grad_bias, grad_self, grad_neigh = pl.pallas_call(
+        functools.partial(last_kernel, scale, slots, hub_here, width),
         out_shape=(
             shape((rows, cols), BF),
             shape((1, cols), F32),
-            shape((peers, share, cols), BF),
+            shape((depth, full), F32),
+            shape((depth, full), F32),
         ),
-        in_specs=[VMEM] * 3,
-        out_specs=(VMEM,) * 3,
-        compiler_params=PARAMS,
-    )(back, mark, arrived)
-    parts = exchange(part)
-    grad_self, grad_neigh = pl.pallas_call(
-        functools.partial(spread_kernel, scale),
-        out_shape=(shape((depth, full), F32), shape((depth, full), F32)),
-        in_specs=[VMEM],
-        out_specs=(VMEM, VMEM),
-        compiler_params=PARAMS,
-    )(parts)
+        in_specs=[SMEM] + [VMEM] * 5,
+        out_specs=(VMEM,) * 4,
+        compiler_params=PARAMS,
+    )(side, back, near_bias, mark, crossed, parts)
     return output, grad_features, grad_self, grad_neigh, grad_bias.reshape(cols)
 
 

time: 55.5 us -> 53.9 us (0.971)
  blocking collectives: 27.1 us -> 10.1 us
  waiting for transfers between devices: 10.2 us -> 21.3 us
  starting transfers between devices: 9.68 us -> 13.6 us
    all_to_all x2 -> x1, blocking collectives: 27.1 us -> 10.1 us  [exchange(): lax.all_to_all(blocks, 'dom', split_axis=0, concat_axis=0, axis_index_gro...]
    ppermute x6 -> x8, waiting for transfers between devices: 5 us -> 15.5 us  [partner(): lax.ppermute(block, axis, [(i, i ^ k) for i in range(lax.axis_size(axis))])]
    all_to_all x1 -> x2, starting transfers between devices: 5.83 us -> 9.24 us  [exchange(): lax.all_to_all(blocks, 'dom', split_axis=0, concat_axis=0, axis_index_gro...]
    ppermute x6 -> x8, starting transfers between devices: 3.84 us -> 4.38 us  [partner(): lax.ppermute(block, axis, [(i, i ^ k) for i in range(lax.axis_size(axis))])]
    all_to_all x1 -> x2, waiting for transfers between devices: 5.22 us -> 5.73 us  [exchange(): lax.all_to_all(blocks, 'dom', split_axis=0, concat_axis=0, axis_index_gro...]
    pallas_call x3 -> x5, Pallas kernels: 2.91 us -> 3.32 us  [the longest x1 1.5 us: on_device(): pl.pallas_call(functools.partial(dense_kernel, slots, hub_here, feats, wi...]
  transfers between devices with their start and end apart: 7 -> 10, of which waited for: 3 -> 6; matrix products, arithmetic and copies ran while one was open for 0% -> 0% of each run, Pallas kernels for 3% -> 3%
where the time goes in v6:
time: 53.9 us; the launch traced here: 53.5 us
  waiting for transfers between devices  21.3 us (40%)
  starting transfers between devices  13.6 us (25%)
  blocking collectives  10.1 us (19%)
  Pallas kernels  7.17 us (13%)
  between operations  1.38 us (3%)
    ppermute x8, waiting for transfers between devices, partner(): lax.ppermute(block, axis, [(i, i ^ k) for i in range(lax.axis_size(axis))])  15.5 us
    all_to_all x1, blocking collectives, exchange(): lax.all_to_all(blocks, 'dom', split_axis=0, concat_axis=0, axis_index_gro...  10.1 us
    all_to_all x2, starting transfers between devices, exchange(): lax.all_to_all(blocks, 'dom', split_axis=0, concat_axis=0, axis_index_gro...  9.24 us
    all_to_all x2, waiting for transfers between devices, exchange(): lax.all_to_all(blocks, 'dom', split_axis=0, concat_axis=0, axis_index_gro...  5.73 us
    ppermute x8, starting transfers between devices, partner(): lax.ppermute(block, axis, [(i, i ^ k) for i in range(lax.axis_size(axis))])  4.38 us
    pallas_call x1, Pallas kernels, on_device(): pl.pallas_call(functools.partial(send_kernel, width), out_shape=(shape((p...  2.15 us
    pallas_call x1, Pallas kernels, on_device(): pl.pallas_call(functools.partial(dense_kernel, slots, hub_here, feats, wi...  1.5 us
    pallas_call x1, Pallas kernels, on_device(): pl.pallas_call(functools.partial(mix_kernel, width), out_shape=(shape((ro...  1.45 us
  transfers between devices with their start and end apart: 10, of which 6 were waited for; matrix products, arithmetic and copies ran while one was open for 0% of the time, Pallas kernels for 3%

profile of v6, /device:TPU:0, one launch (start us, length us, event | category | flops | bytes accessed | tf_op | source)
XLA Modules:
  0.0 53.5 jit_solution(6119555399852689747)
XLA Ops:
  0.6 2.1 %shard_map.174 = (bf16[8,64,128]{2,1,0:T(8,128)(2,1)}, bf16[1552,128]{1,0:T(8,128)(2,1)S(1)}) custom-call(bf16[256,128]{1,0:T(8,128)(2,1)} %x_ref.5, bf16[256,128]{1,0:T(8,128)(2,1)} %cot_ref.1, bf16[128,512]{1,0:T(8,128)(2,1)} %ws_ref.3, bf16[128,512]{1,0:T(8,128)(2,1)} %wn_ref.3, bf16[1,128]{1,0:T(2,128)(2,1)} %bitcast.7, s32[1,8,48]{2,1,0:T(8,128)} %send_ref.3, ...), custom_call_target="tpu_custom_call" | custom-call | tf_op jit(solution)/shard_map/pallas_call | solution.py:308
  2.8 3.0 %collective-permute-start.1 = (bf16[1552,128]{1,0:T(8,128)(2,1)S(1)}, bf16[1552,128]{1,0:T(8,128)(2,1)S(1)}, u32[]{:S(2)}, u32[]{:S(2)}) collective-permute-start(bf16[1552,128]{1,0:T(8,128)(2,1)S(1)} %get-tuple-element.26.refs_0_), channel_id=1, source_target_pairs={{0,2},{1,3},{2,0},{3,1},{4,6},{5,7},{6,4},{7,5},{8,10},{9,11},{10,... | collective-permute-start | bytes 1191944 | tf_op jit(solution)/shard_map/ppermute | solution.py:265
  5.8 5.8 %all-to-all-start = ((bf16[8,64,128]{2,1,0:T(8,128)(2,1)}), bf16[8,64,128]{2,1,0:T(8,128)(2,1)S(1)}, u32[]{:S(2)}, u32[]{:S(2)}) async-start(bf16[8,64,128]{2,1,0:T(8,128)(2,1)} %get-tuple-element.28), calls=%async_computation | async-start | bytes 262144 | tf_op jit(solution)/shard_map/all_to_all | solution.py:269
  11.6 0.0 collective-permute-start
  12.3 0.0 copy-start
  12.3 1.4 %shard_map.173 = (bf16[256,768]{1,0:T(8,128)(2,1)S(1)}, bf16[768,256]{1,0:T(8,128)(2,1)S(1)}, bf16[256,512]{1,0:T(8,128)(2,1)S(1)}) custom-call(s32[1,1]{1,0:T(1,128)} %bitcast.6.count_ref, s32[1,4]{1,0:T(1,128)} %pos_ref.1, s32[1,8]{1,0:T(1,128)} %live_ref.1, bf16[1,4,128,128]{3,2,1,0:T(8,128)(2,1)} %tile_ref.1, s32[1,8,48]{2,1,0:T(8,128)} %dest_ref.1, ...), custom_call_target="tpu_custom_call" | custom-call | flops 100000000 | bytes 3000000 | tf_op jit(solution)/shard_map/pallas_call | solution.py:328
  13.7 5.2 %all-to-all-done.got_ref = bf16[8,64,128]{2,1,0:T(8,128)(2,1)S(1)} async-done(((bf16[8,64,128]{2,1,0:T(8,128)(2,1)}), bf16[8,64,128]{2,1,0:T(8,128)(2,1)S(1)}, u32[]{:S(2)}, u32[]{:S(2)}) %all-to-all-start) | async-done | bytes 131104 | tf_op jit(solution)/shard_map/all_to_all | solution.py:269
  19.0 0.0 collective-permute-done.1.far_ref
  19.0 0.0 copy-done
  19.0 0.0 copy-start.2
  19.0 0.3 shard_map.175
  19.2 0.1 collective-permute-start.2
  19.3 0.6 %collective-permute-start.4 = (bf16[256,128]{1,0:T(8,128)(2,1)S(1)}, bf16[256,128]{1,0:T(8,128)(2,1)S(1)}, u32[]{:S(2)}, u32[]{:S(2)}) collective-permute-start(bf16[256,128]{1,0:T(8,128)(2,1)S(1)} %get-tuple-element.30.refs_4_), channel_id=1, source_target_pairs={{0,2},{1,3},{2,0},{3,1},{4,6},{5,7},{6,4},{7,5},{8,10},{9,11},{10,... | collective-permute-start | bytes 196616 | tf_op jit(solution)/shard_map/ppermute | solution.py:265
  19.9 0.2 collective-permute-start.3
  20.1 3.7 %collective-permute-done.4.refs_6_ = bf16[256,128]{1,0:T(8,128)(2,1)S(1)} collective-permute-done((bf16[256,128]{1,0:T(8,128)(2,1)S(1)}, bf16[256,128]{1,0:T(8,128)(2,1)S(1)}, u32[]{:S(2)}, u32[]{:S(2)}) %collective-permute-start.4) | collective-permute-done | bytes 65568 | tf_op jit(solution)/shard_map/ppermute | solution.py:265
  23.8 0.0 collective-permute-start.5
  23.8 0.0 collective-permute-done.refs_1_
  23.8 0.0 collective-permute-done.3.refs_5_
  23.9 1.2 %collective-permute-done.5.refs_7_ = bf16[256,128]{1,0:T(8,128)(2,1)S(1)} collective-permute-done((bf16[256,128]{1,0:T(8,128)(2,1)S(1)}, bf16[256,128]{1,0:T(8,128)(2,1)S(1)}, u32[]{:S(2)}, u32[]{:S(2)}) %collective-permute-start.5) | collective-permute-done | bytes 65568 | tf_op jit(solution)/shard_map/ppermute | solution.py:265
  25.1 0.0 collective-permute-done.2.refs_3_
  25.1 0.0 copy-done.1
  25.1 1.5 %shard_map.176 = (bf16[256,128]{1,0:T(8,128)(2,1)}, f32[256,128]{1,0:T(8,128)S(1)}, bf16[4,384,128]{2,1,0:T(8,128)(2,1)S(1)}) custom-call(s32[1]{0:T(128)} %bitcast.me_ref, s32[1]{0:T(128)} %bitcast.1.side_ref, bf16[256,128]{1,0:T(8,128)(2,1)S(1)} %copy-done, bf16[128,512]{1,0:T(8,128)(2,1)S(1)} %copy-done.1, bf16[128,512]{1,0:T(8,128)(2,1)S(1)} %copy-done.2, ...), custom_call_target="tpu_custom_call" | custom-call | tf_op jit(solution)/shard_map/pallas_call | solution.py:353
  26.6 10.1 %all_to_all.15.got_ref = bf16[4,384,128]{2,1,0:T(8,128)(2,1)S(1)} all-to-all(bf16[4,384,128]{2,1,0:T(8,128)(2,1)S(1)} %get-tuple-element.34), channel_id=1, replica_groups={{0,4,8,12},{16,20,24,28},{1,5,9,13},{17,21,25,29},{2,6,10,14},{18,22,26..., dimensions={0} | all-to-all | bytes 786432 | tf_op jit(solution)/shard_map/all_to_all | solution.py:269
  36.7 0.5 collective-permute-start.6
  37.2 5.5 %collective-permute-done.6.other_ref = bf16[256,128]{1,0:T(8,128)(2,1)S(1)} collective-permute-done((bf16[256,128]{1,0:T(8,128)(2,1)S(1)}, bf16[256,128]{1,0:T(8,128)(2,1)S(1)}, u32[]{:S(2)}, u32[]{:S(2)}) %collective-permute-start.6) | collective-permute-done | bytes 65568 | tf_op jit(solution)/shard_map/ppermute | solution.py:265
  42.7 0.7 %shard_map.179 = (bf16[4,256,128]{2,1,0:T(8,128)(2,1)}, bf16[4,64,128]{2,1,0:T(8,128)(2,1)S(1)}) custom-call(bf16[256,128]{1,0:T(8,128)(2,1)S(1)} %get-tuple-element.37.own_ref, bf16[256,128]{1,0:T(8,128)(2,1)S(1)} %collective-permute-done.6.other_ref, bf16[4,64,128]{2,1,0:T(8,128)(2,1)S(1)} %get-tuple-element.38.relay_ref), custom_call_target="tpu_custom_call", output_to_operand_aliasing={{1}: (2, {})} | custom-call | tf_op jit(solution)/shard_map/pallas_call | solution.py:388
  43.4 3.4 %all-to-all-start.2 = ((bf16[4,256,128]{2,1,0:T(8,128)(2,1)}), bf16[4,256,128]{2,1,0:T(8,128)(2,1)S(1)}, u32[]{:S(2)}, u32[]{:S(2)}) async-start(bf16[4,256,128]{2,1,0:T(8,128)(2,1)} %get-tuple-element.40), calls=%async_computation.2 | async-start | bytes 524288 | tf_op jit(solution)/shard_map/all_to_all | solution.py:269
  46.8 0.1 collective-permute-start.7
  46.9 0.2 shard_map.177
  47.1 5.1 %collective-permute-done.7.got_ref = bf16[4,64,128]{2,1,0:T(8,128)(2,1)S(1)} collective-permute-done((bf16[4,64,128]{2,1,0:T(8,128)(2,1)S(1)}, bf16[4,64,128]{2,1,0:T(8,128)(2,1)S(1)}, u32[]{:S(2)}, u32[]{:S(2)}) %collective-permute-start.7) | collective-permute-done | bytes 65568 | tf_op jit(solution)/shard_map/ppermute | solution.py:265
  52.2 0.5 all-to-all-done.2.part_ref
  52.7 0.9 %shard_map.180 = (bf16[256,128]{1,0:T(8,128)(2,1)}, f32[1,128]{1,0:T(1,128)}, f32[128,512]{1,0:T(8,128)}, f32[128,512]{1,0:T(8,128)}) custom-call(s32[1]{0:T(128)} %bitcast.1.side_ref, f32[256,128]{1,0:T(8,128)S(1)} %get-tuple-element.35.back_ref, f32[1,128]{1,0:T(1,128)S(1)} %get-tuple-element.36.near_ref, bf16[256,512]{1,0:T(8,128)(2,1)S(1)} %get-tuple-element.33.mark_ref, ...), custom_call_target="tpu_custom_call" | custom-call | tf_op jit(solution)/shard_map/pallas_call | solution.py:398
  (3 shorter events, 0.0 us)
Async XLA Ops:
  2.8 16.2 %collective-permute-start.1 = (bf16[1552,128]{1,0:T(8,128)(2,1)S(1)}, bf16[1552,128]{1,0:T(8,128)(2,1)S(1)}, u32[]{:S(2)}, u32[]{:S(2)}) collective-permute-start(bf16[1552,128]{1,0:T(8,128)(2,1)S(1)} %get-tuple-element.26.refs_0_), channel_id=1, source_target_pairs={{0,2},{1,3},{2,0},{3,1},{4,6},{5,7},{6,4},{7,5},{8,10},{9,11},{10,... | collective-permute-start | bytes 1191944 | tf_op jit(solution)/shard_map/ppermute | solution.py:265
  5.8 13.2 %all-to-all-start = ((bf16[8,64,128]{2,1,0:T(8,128)(2,1)}), bf16[8,64,128]{2,1,0:T(8,128)(2,1)S(1)}, u32[]{:S(2)}, u32[]{:S(2)}) async-start(bf16[8,64,128]{2,1,0:T(8,128)(2,1)} %get-tuple-element.28), calls=%async_computation | async-start | bytes 262144 | tf_op jit(solution)/shard_map/all_to_all | solution.py:269
  11.6 12.2 %collective-permute-start = (bf16[1552,128]{1,0:T(8,128)(2,1)S(1)}, bf16[1552,128]{1,0:T(8,128)(2,1)S(1)}, u32[]{:S(2)}, u32[]{:S(2)}) collective-permute-start(bf16[1552,128]{1,0:T(8,128)(2,1)S(1)} %get-tuple-element.26.refs_0_), channel_id=1, source_target_pairs={{0,1},{1,0},{2,3},{3,2},{4,5},{5,4},{6,7},{7,6},{8,9},{9,8},{10,11... | collective-permute-start | bytes 1191944 | tf_op jit(solution)/shard_map/ppermute | solution.py:265
  12.3 6.7 %copy-start = (bf16[256,128]{1,0:T(8,128)(2,1)S(1)}, bf16[256,128]{1,0:T(8,128)(2,1)}, u32[]{:S(2)}) copy-start(bf16[256,128]{1,0:T(8,128)(2,1)} %x_ref.5) | copy-start | bytes 196612
  19.0 6.1 %copy-start.1 = (bf16[128,512]{1,0:T(8,128)(2,1)S(1)}, bf16[128,512]{1,0:T(8,128)(2,1)}, u32[]{:S(2)}) copy-start(bf16[128,512]{1,0:T(8,128)(2,1)} %ws_ref.3) | copy-start | bytes 393220
  19.0 6.1 %copy-start.2 = (bf16[128,512]{1,0:T(8,128)(2,1)S(1)}, bf16[128,512]{1,0:T(8,128)(2,1)}, u32[]{:S(2)}) copy-start(bf16[128,512]{1,0:T(8,128)(2,1)} %wn_ref.3) | copy-start | bytes 393220
  19.2 5.8 %collective-permute-start.2 = (bf16[1552,128]{1,0:T(8,128)(2,1)S(1)}, bf16[1552,128]{1,0:T(8,128)(2,1)S(1)}, u32[]{:S(2)}, u32[]{:S(2)}) collective-permute-start(bf16[1552,128]{1,0:T(8,128)(2,1)S(1)} %get-tuple-element.29.refs_2_), channel_id=1, source_target_pairs={{0,1},{1,0},{2,3},{3,2},{4,5},{5,4},{6,7},{7,6},{8,9},{9,8},{10,11... | collective-permute-start | bytes 1191944 | tf_op jit(solution)/shard_map/ppermute | solution.py:265
  19.3 4.5 %collective-permute-start.4 = (bf16[256,128]{1,0:T(8,128)(2,1)S(1)}, bf16[256,128]{1,0:T(8,128)(2,1)S(1)}, u32[]{:S(2)}, u32[]{:S(2)}) collective-permute-start(bf16[256,128]{1,0:T(8,128)(2,1)S(1)} %get-tuple-element.30.refs_4_), channel_id=1, source_target_pairs={{0,2},{1,3},{2,0},{3,1},{4,6},{5,7},{6,4},{7,5},{8,10},{9,11},{10,... | collective-permute-start | bytes 196616 | tf_op jit(solution)/shard_map/ppermute | solution.py:265
  19.9 3.9 %collective-permute-start.3 = (bf16[256,128]{1,0:T(8,128)(2,1)S(1)}, bf16[256,128]{1,0:T(8,128)(2,1)S(1)}, u32[]{:S(2)}, u32[]{:S(2)}) collective-permute-start(bf16[256,128]{1,0:T(8,128)(2,1)S(1)} %get-tuple-element.30.refs_4_), channel_id=1, source_target_pairs={{0,1},{1,0},{2,3},{3,2},{4,5},{5,4},{6,7},{7,6},{8,9},{9,8},{10,11... | collective-permute-start | bytes 196616 | tf_op jit(solution)/shard_map/ppermute | solution.py:265
  23.8 1.3 %collective-permute-start.5 = (bf16[256,128]{1,0:T(8,128)(2,1)S(1)}, bf16[256,128]{1,0:T(8,128)(2,1)S(1)}, u32[]{:S(2)}, u32[]{:S(2)}) collective-permute-start(bf16[256,128]{1,0:T(8,128)(2,1)S(1)} %collective-permute-done.4.refs_6_), channel_id=1, source_target_pairs={{0,1},{1,0},{2,3},{3,2},{4,5},{5,4},{6,7},{7,6},{8,9},{9,8},{10,11... | collective-permute-start | bytes 196616 | tf_op jit(solution)/shard_map/ppermute | solution.py:265
  36.7 5.9 %collective-permute-start.6 = (bf16[256,128]{1,0:T(8,128)(2,1)S(1)}, bf16[256,128]{1,0:T(8,128)(2,1)S(1)}, u32[]{:S(2)}, u32[]{:S(2)}) collective-permute-start(bf16[256,128]{1,0:T(8,128)(2,1)S(1)} %get-tuple-element.37.own_ref), channel_id=1, source_target_pairs={{0,16},{4,20},{8,24},{12,28},{16,0},{20,4},{24,8},{28,12},{1,17},{... | collective-permute-start | bytes 196616 | tf_op jit(solution)/shard_map/ppermute | solution.py:265
  43.4 9.3 %all-to-all-start.2 = ((bf16[4,256,128]{2,1,0:T(8,128)(2,1)}), bf16[4,256,128]{2,1,0:T(8,128)(2,1)S(1)}, u32[]{:S(2)}, u32[]{:S(2)}) async-start(bf16[4,256,128]{2,1,0:T(8,128)(2,1)} %get-tuple-element.40), calls=%async_computation.2 | async-start | bytes 524288 | tf_op jit(solution)/shard_map/all_to_all | solution.py:269
  46.8 5.3 %collective-permute-start.7 = (bf16[4,64,128]{2,1,0:T(8,128)(2,1)S(1)}, bf16[4,64,128]{2,1,0:T(8,128)(2,1)S(1)}, u32[]{:S(2)}, u32[]{:S(2)}) collective-permute-start(bf16[4,64,128]{2,1,0:T(8,128)(2,1)S(1)} %get-tuple-element.39), channel_id=1, source_target_pairs={{0,16},{4,20},{8,24},{12,28},{16,0},{20,4},{24,8},{28,12},{1,17},{... | collective-permute-start | bytes 196616 | tf_op jit(solution)/shard_map/ppermute | solution.py:265

commit v7 on v6

--- a/solution.py
+++ b/solution.py
@@ -57,7 +57,8 @@
 
 
 def send_kernel(
-    width, x_ref, cot_ref, ws_ref, wn_ref, bias_ref, send_ref, hub_ref, out_ref, pack_ref, send_v, hub_v, bias_v, sems
+    width, x_ref, cot_ref, ws_ref, wn_ref, bias_ref, send_ref, hub_ref, pos_ref, live_ref, tile_ref, dest_ref, gw_ref, hw_ref,
+    out_ref, pack_ref, send_v, hub_v, pos_v, live_v, tile_v, dest_v, gw_v, hw_v, bias_v, sems,
 ):
     rows, cols = x_ref.shape
     depth, full = ws_ref.shape
@@ -74,6 +75,10 @@
         for j in range(blocks):
             at = (kind * blocks + j) * depth
             moves.append((w_ref.at[:, j * cols : (j + 1) * cols], pack_ref.at[at : at + depth, :]))
+    moves += [
+        (pos_ref, pos_v), (live_ref, live_v), (tile_ref, tile_v), (dest_ref, dest_v),
+        (gw_ref, gw_v), (hw_ref, hw_v),
+    ]
     copies = [pltpu.make_async_copy(src, dst, sems.at[i]) for i, (src, dst) in enumerate(moves)]
     for copy in copies:
         copy.start()
@@ -88,19 +93,7 @@
     pack_ref[base + 2 * rows :, :] = jnp.broadcast_to(bias_v[...], (16, cols))
 
 
-def mix_kernel(
-    width, count_ref, pos_ref, live_ref, tile_ref, dest_ref, gw_ref, hw_ref, send_ref, hub_ref,
-    mix_ref, turned_ref, mark_ref, pos_v, live_v, tile_v, dest_v, gw_v, hw_v, send_v, hub_v, sems,
-):
-    pairs = (
-        (pos_ref, pos_v), (live_ref, live_v), (tile_ref, tile_v), (dest_ref, dest_v),
-        (gw_ref, gw_v), (hw_ref, hw_v), (send_ref, send_v), (hub_ref, hub_v),
-    )
-    copies = [pltpu.make_async_copy(src, dst, sems.at[i]) for i, (src, dst) in enumerate(pairs)]
-    for copy in copies:
-        copy.start()
-    for copy in copies:
-        copy.wait()
+def mix_kernel(width, count_ref, send_v, hub_v, pos_v, live_v, tile_v, dest_v, gw_v, hw_v, mix_ref, turned_ref, mark_ref):
     rows = mix_ref.shape[0]
     tiles, tile = tile_v.shape[1:3]
     peers, slots = dest_v.shape[1:]
@@ -136,7 +129,11 @@
     mark_ref[...] = source_matrix(send_v[0], hub_v[...], rows, width)
 
 
-def neigh_kernel(x_ref, mix_ref, far_ref, got_ref, neigh_ref, passed_ref):
+def pass_kernel(after_ref, far_ref, passed_ref):
+    pass
+
+
+def neigh_kernel(x_ref, mix_ref, got_ref, neigh_ref):
     rows, cols = x_ref.shape
     lanes = mix_ref.shape[1] - rows
     total = jnp.dot(mix_ref[:, :rows], x_ref[...], preferred_element_type=F32)
@@ -146,12 +143,11 @@
 
 def dense_kernel(slots, hub_here, feats, width, me_ref, side_ref, x_ref, ws_ref, wn_ref, turned_ref, *refs):
     pack_refs, n_refs = refs[:feats], refs[feats : 2 * feats]
-    out_ref, back_ref, send_ref, pre_ref, cot_ref, bias_ref, hold_ref = refs[2 * feats :]
+    out_ref, back_ref, send_ref, pre_ref, cot_ref, bias_ref = refs[2 * feats :]
     rows, cols = x_ref.shape
     depth, full = ws_ref.shape
     blocks = full // cols
     half, height = send_ref.shape[:2]
-    lanes = turned_ref.shape[0] - rows
     me = me_ref[0]
     base = 2 * blocks * depth
     pre = jnp.zeros((rows, full), F32)
@@ -176,17 +172,17 @@
     both = jnp.concatenate([ws_ref[...], wn_ref[...]], axis=0)
     into = lax.dot_general(grad, both, (((1,), (1,)), ((), ())), preferred_element_type=F32)
     neigh_grad = into[:, depth:].astype(BF)
-    spread = jnp.dot(turned_ref[...], neigh_grad, preferred_element_type=F32)
-    back_ref[...] = into[:, :depth] + spread[:rows]
+    back_ref[...] = into[:, :depth] + jnp.dot(turned_ref[:rows, :], neigh_grad, preferred_element_type=F32)
     sums = jnp.sum(cot_ref[:, mine].astype(F32), axis=0, keepdims=True)
     high = sums.astype(BF).astype(F32)
-    line = lax.broadcasted_iota(jnp.int32, (lanes, cols), 0) % width
-    away = jnp.where(line == slots + hub_here, high, spread[rows:])
-    away = jnp.where(line == slots + hub_here + 1, sums - high, away)
-    hold_ref[...] = away.astype(BF).reshape(hold_ref.shape)
+    line = lax.broadcasted_iota(jnp.int32, (half * width, cols), 0) % width
     here = side_ref[0] * half
-    send_ref[:, :width, :] = hold_ref[pl.ds(here, half)]
-    send_ref[:, width : 2 * width, :] = hold_ref[pl.ds(half - here, half)]
+    for at, start in ((0, here), (width, half - here)):
+        cut = pl.ds(pl.multiple_of(rows + start * width, 128), half * width)
+        away = jnp.dot(turned_ref[cut, :], neigh_grad, preferred_element_type=F32)
+        away = jnp.where(line == slots + hub_here, high, away)
+        away = jnp.where(line == slots + hub_here + 1, sums - high, away)
+        send_ref[:, at : at + width, :] = away.astype(BF).reshape(half, width, cols)
     pair = jnp.concatenate([x_ref[...], n_refs[0][...]], axis=1)
     weights = lax.dot_general(pair, grad, (((0,), (0,)), ((), ())), preferred_element_type=F32).astype(BF)
     share = height - 2 * width
@@ -209,7 +205,7 @@
     relay_ref[...] = got_ref[:, width : 2 * width, :]
 
 
-def total_kernel(own_ref, other_ref, relay_ref, part_ref, passed_ref):
+def total_kernel(own_ref, other_ref, part_ref):
     total = (own_ref[...].astype(F32) + other_ref[...].astype(F32)).astype(BF)
     part_ref[...] = jnp.broadcast_to(total, part_ref.shape)
 
@@ -305,26 +301,27 @@
         return [pltpu.with_memory_space_constraint(a, pltpu.HBM) for a in arrays]
 
     first = pinned(features, cotangent, w_self, w_neigh, bias.reshape(1, cols), send_rows, hub_rows)
-    outgoing, pack = pl.pallas_call(
+    edges = pinned(tile_pos, recv_count, tile_vals, recv_dest, ghost_weight, hub_weight.T)
+    moved = (send_rows, hub_rows, *edges)
+    outgoing, pack, *moved = pl.pallas_call(
         functools.partial(send_kernel, width),
-        out_shape=(shape((peers, width, cols), BF), shape((pack_rows, cols), BF)),
-        in_specs=[HBM] * len(first),
-        out_specs=(VMEM,) * 2,
+        out_shape=(
+            shape((peers, width, cols), BF),
+            shape((pack_rows, cols), BF),
+            *(shape(a.shape, a.dtype) for a in moved),
+        ),
+        in_specs=[HBM] * (len(first) + len(edges)),
+        out_specs=(VMEM,) * (2 + len(moved)),
         scratch_shapes=[
-            pltpu.VMEM(send_rows.shape, jnp.int32),
-            pltpu.VMEM(hub_rows.shape, jnp.int32),
             pltpu.VMEM((1, cols), BF),
-            pltpu.SemaphoreType.DMA((5 + 2 * blocks,)),
+            pltpu.SemaphoreType.DMA((11 + 2 * blocks,)),
         ],
         compiler_params=PARAMS,
-    )(*first)
+    )(*first, *edges)
 
     far = partner(pack, "feat", 2)
     near = partner(pack, "feat", 1)
     incoming = exchange(outgoing)
-    edges = pinned(
-        tile_pos, recv_count, tile_vals, recv_dest, ghost_weight, hub_weight.T, send_rows, hub_rows
-    )
     mix, turned, mark = pl.pallas_call(
         functools.partial(mix_kernel, width),
         out_shape=(
@@ -332,23 +329,30 @@
             shape((rows + lanes, rows), BF),
             shape((rows, lanes), BF),
         ),
-        in_specs=[VMEM] + [HBM] * len(edges),
+        in_specs=[VMEM] * (1 + len(moved)),
         out_specs=(VMEM,) * 3,
-        scratch_shapes=[pltpu.VMEM(a.shape, a.dtype) for a in edges] + [pltpu.SemaphoreType.DMA((len(edges),))],
         compiler_params=PARAMS,
         cost_estimate=pl.CostEstimate(flops=10**8, bytes_accessed=3 * 10**6, transcendentals=0),
-    )(tile_count.reshape(1, 1), *edges)
-    neigh, far = pl.pallas_call(
+    )(tile_count.reshape(1, 1), *moved)
+    neigh = pl.pallas_call(
         neigh_kernel,
-        out_shape=(shape((rows, cols), BF), shape((pack_rows, cols), BF)),
-        in_specs=[VMEM, VMEM, ANY, VMEM],
-        out_specs=(VMEM, ANY),
-        input_output_aliases={2: 1},
-        compiler_params=PARAMS,
-    )(features, mix, far, incoming)
+        out_shape=shape((rows, cols), BF),
+        in_specs=[VMEM] * 3,
+        out_specs=VMEM,
+        compiler_params=PARAMS,
+    )(features, mix, incoming)
+    far_neigh = partner(neigh, "feat", 2)
+    near_neigh = partner(neigh, "feat", 1)
+    far = pl.pallas_call(
+        pass_kernel,
+        out_shape=shape((pack_rows, cols), BF),
+        in_specs=[ANY, ANY],
+        out_specs=ANY,
+        input_output_aliases={1: 0},
+        compiler_params=PARAMS,
+    )(near_neigh, far)
     last = partner(far, "feat", 1)
-    far_neigh = partner(neigh, "feat", 2)
-    every = [neigh, partner(neigh, "feat", 1), far_neigh, partner(far_neigh, "feat", 1)]
+    every = [neigh, near_neigh, far_neigh, partner(far_neigh, "feat", 1)]
 
     output, back, returned = pl.pallas_call(
         functools.partial(dense_kernel, slots, hub_here, feats, width),
@@ -363,7 +367,6 @@
             pltpu.VMEM((rows, full), F32),
             pltpu.VMEM((rows, full), BF),
             pltpu.VMEM((16, full), BF),
-            pltpu.VMEM((peers, width, cols), BF),
         ],
         compiler_params=PARAMS,
     )(me, side, features, w_self, w_neigh, turned, pack, near, far, last, *every)
@@ -385,15 +388,14 @@
         compiler_params=PARAMS,
         cost_estimate=pl.CostEstimate(flops=10**8, bytes_accessed=10**6, transcendentals=0),
     )(side, back, mark, arrived)
-    part, relay = pl.pallas_call(
+    crossed = partner(relay, "dom", half)
+    part = pl.pallas_call(
         total_kernel,
-        out_shape=(shape((half, share, cols), BF), shape((half, width, cols), BF)),
-        in_specs=[VMEM, VMEM, ANY],
-        out_specs=(VMEM, ANY),
-        input_output_aliases={2: 1},
-        compiler_params=PARAMS,
-    )(half_sum, other_sum, relay)
-    crossed = partner(relay, "dom", half)
+        out_shape=shape((half, share, cols), BF),
+        in_specs=[VMEM, VMEM],
+        out_specs=VMEM,
+        compiler_params=PARAMS,
+    )(half_sum, other_sum)
     parts = exchange(part, halves)
     grad_features, grad_bias, grad_self, grad_neigh = pl.pallas_call(
         functools.partial(last_kernel, scale, slots, hub_here, width),

time: 53.9 us -> 55.1 us (1.022)
  waiting for transfers between devices: 21.3 us -> 23.2 us
  Pallas kernels: 7.17 us -> 6.04 us
    all_to_all x2, waiting for transfers between devices: 5.73 us -> 6.79 us  [exchange(): lax.all_to_all(blocks, 'dom', split_axis=0, concat_axis=0, axis_index_gro...]
    pallas_call x1, Pallas kernels: 1.45 us -> 0.39 us  [on_device(): pl.pallas_call(functools.partial(mix_kernel, width), out_shape=(shape((ro...]
    ppermute x8, waiting for transfers between devices: 15.5 us -> 16.4 us  [partner(): lax.ppermute(block, axis, [(i, i ^ k) for i in range(lax.axis_size(axis))])]
  transfers between devices with their start and end apart: 10 -> 10, of which waited for: 6 -> 7; matrix products, arithmetic and copies ran while one was open for 0% -> 0% of each run, Pallas kernels for 3% -> 1%
where the time goes in v7:
time: 55.1 us; the launch traced here: 54.8 us
  waiting for transfers between devices  23.2 us (42%)
  starting transfers between devices  14 us (25%)
  blocking collectives  10.1 us (18%)
  Pallas kernels  6.04 us (11%)
  between operations  1.39 us (3%)
    ppermute x8, waiting for transfers between devices, partner(): lax.ppermute(block, axis, [(i, i ^ k) for i in range(lax.axis_size(axis))])  16.4 us
    all_to_all x1, blocking collectives, exchange(): lax.all_to_all(blocks, 'dom', split_axis=0, concat_axis=0, axis_index_gro...  10.1 us
    all_to_all x2, starting transfers between devices, exchange(): lax.all_to_all(blocks, 'dom', split_axis=0, concat_axis=0, axis_index_gro...  9.24 us
    all_to_all x2, waiting for transfers between devices, exchange(): lax.all_to_all(blocks, 'dom', split_axis=0, concat_axis=0, axis_index_gro...  6.79 us
    ppermute x8, starting transfers between devices, partner(): lax.ppermute(block, axis, [(i, i ^ k) for i in range(lax.axis_size(axis))])  4.79 us
    pallas_call x1, Pallas kernels, on_device(): pl.pallas_call(functools.partial(send_kernel, width), out_shape=(shape((p...  2.23 us
    pallas_call x1, Pallas kernels, on_device(): pl.pallas_call(functools.partial(dense_kernel, slots, hub_here, feats, wi...  1.36 us
  transfers between devices with their start and end apart: 10, of which 7 were waited for; matrix products, arithmetic and copies ran while one was open for 0% of the time, Pallas kernels for 1%

profile of v7, /device:TPU:0, one launch (start us, length us, event | category | flops | bytes accessed | tf_op | source)
XLA Modules:
  0.0 54.8 jit_solution(164920041931498387)
XLA Ops:
  0.6 2.2 %shard_map.173 = (bf16[8,64,128]{2,1,0:T(8,128)(2,1)}, bf16[1552,128]{1,0:T(8,128)(2,1)S(1)}, s32[1,8,48]{2,1,0:T(8,128)S(1)}, s32[1,2]{1,0:T(1,128)S(1)}, s32[1...) custom-call(bf16[256,128]{1,0:T(8,128)(2,1)} %x_ref.5, ...), custom_call_target="tpu_custom_call" | custom-call | tf_op jit(solution)/shard_map/pallas_call | solution.py:306
  2.9 3.0 %collective-permute-start.2 = (bf16[1552,128]{1,0:T(8,128)(2,1)S(1)}, bf16[1552,128]{1,0:T(8,128)(2,1)S(1)}, u32[]{:S(2)}, u32[]{:S(2)}) collective-permute-start(bf16[1552,128]{1,0:T(8,128)(2,1)S(1)} %get-tuple-element.38.refs_0_), channel_id=1, source_target_pairs={{0,2},{1,3},{2,0},{3,1},{4,6},{5,7},{6,4},{7,5},{8,10},{9,11},{10,... | collective-permute-start | bytes 1191944 | tf_op jit(solution)/shard_map/ppermute | solution.py:261
  5.9 5.8 %all-to-all-start = ((bf16[8,64,128]{2,1,0:T(8,128)(2,1)}), bf16[8,64,128]{2,1,0:T(8,128)(2,1)S(1)}, u32[]{:S(2)}, u32[]{:S(2)}) async-start(bf16[8,64,128]{2,1,0:T(8,128)(2,1)} %get-tuple-element.40), calls=%async_computation | async-start | bytes 262144 | tf_op jit(solution)/shard_map/all_to_all | solution.py:265
  12.4 0.0 copy-start
  12.4 0.4 shard_map.174
  12.8 6.3 %all-to-all-done.got_ref = bf16[8,64,128]{2,1,0:T(8,128)(2,1)S(1)} async-done(((bf16[8,64,128]{2,1,0:T(8,128)(2,1)}), bf16[8,64,128]{2,1,0:T(8,128)(2,1)S(1)}, u32[]{:S(2)}, u32[]{:S(2)}) %all-to-all-start) | async-done | bytes 131104 | tf_op jit(solution)/shard_map/all_to_all | solution.py:265
  19.1 0.0 copy-done
  19.1 0.2 shard_map.175.refs_4_
  19.3 0.0 copy-start.1
  19.3 0.0 copy-start.2
  19.3 0.1 collective-permute-start.1
  19.4 0.5 collective-permute-start
  19.9 0.7 %collective-permute-done.1.after_ref.refs_5_ = bf16[256,128]{1,0:T(8,128)(2,1)S(1)} collective-permute-done((bf16[256,128]{1,0:T(8,128)(2,1)S(1)}, bf16[256,128]{1,0:T(8,128)(2,1)S(1)}, u32[]{:S(2)}, u32[]{:S(2)}) %collective-permute-start.1) | collective-permute-done | bytes 65568 | tf_op jit(solution)/shard_map/ppermute | solution.py:261
  20.6 0.0 collective-permute-done.2.far_ref
  20.7 0.2 collective-permute-start.3
  20.8 0.5 collective-permute-start.4
  21.3 3.8 %collective-permute-done.4.refs_6_ = bf16[256,128]{1,0:T(8,128)(2,1)S(1)} collective-permute-done((bf16[256,128]{1,0:T(8,128)(2,1)S(1)}, bf16[256,128]{1,0:T(8,128)(2,1)S(1)}, u32[]{:S(2)}, u32[]{:S(2)}) %collective-permute-start.4) | collective-permute-done | bytes 65568 | tf_op jit(solution)/shard_map/ppermute | solution.py:261
  25.2 0.0 collective-permute-start.5
  25.2 1.3 %collective-permute-done.5.refs_7_ = bf16[256,128]{1,0:T(8,128)(2,1)S(1)} collective-permute-done((bf16[256,128]{1,0:T(8,128)(2,1)S(1)}, bf16[256,128]{1,0:T(8,128)(2,1)S(1)}, u32[]{:S(2)}, u32[]{:S(2)}) %collective-permute-start.5) | collective-permute-done | bytes 65568 | tf_op jit(solution)/shard_map/ppermute | solution.py:261
  26.4 0.0 collective-permute-done.refs_1_
  26.4 0.0 collective-permute-done.3.refs_3_
  26.4 1.4 %shard_map.177 = (bf16[256,128]{1,0:T(8,128)(2,1)}, f32[256,128]{1,0:T(8,128)S(1)}, bf16[4,384,128]{2,1,0:T(8,128)(2,1)S(1)}) custom-call(s32[1]{0:T(128)} %bitcast.me_ref, s32[1]{0:T(128)} %bitcast.1.side_ref, bf16[256,128]{1,0:T(8,128)(2,1)S(1)} %copy-done, bf16[128,512]{1,0:T(8,128)(2,1)S(1)} %copy-done.1, bf16[128,512]{1,0:T(8,128)(2,1)S(1)} %copy-done.2, ...), custom_call_target="tpu_custom_call" | custom-call | tf_op jit(solution)/shard_map/pallas_call | solution.py:357
  27.8 10.1 %all_to_all.15.got_ref = bf16[4,384,128]{2,1,0:T(8,128)(2,1)S(1)} all-to-all(bf16[4,384,128]{2,1,0:T(8,128)(2,1)S(1)} %get-tuple-element.44), channel_id=1, replica_groups={{0,4,8,12},{16,20,24,28},{1,5,9,13},{17,21,25,29},{2,6,10,14},{18,22,26..., dimensions={0} | all-to-all | bytes 786432 | tf_op jit(solution)/shard_map/all_to_all | solution.py:265
  38.0 0.5 collective-permute-start.7
  38.4 5.5 %collective-permute-done.7.other_ref = bf16[256,128]{1,0:T(8,128)(2,1)S(1)} collective-permute-done((bf16[256,128]{1,0:T(8,128)(2,1)S(1)}, bf16[256,128]{1,0:T(8,128)(2,1)S(1)}, u32[]{:S(2)}, u32[]{:S(2)}) %collective-permute-start.7) | collective-permute-done | bytes 65568 | tf_op jit(solution)/shard_map/ppermute | solution.py:261
  43.9 0.7 %shard_map.180 = bf16[4,256,128]{2,1,0:T(8,128)(2,1)} custom-call(bf16[256,128]{1,0:T(8,128)(2,1)S(1)} %get-tuple-element.48.own_ref, bf16[256,128]{1,0:T(8,128)(2,1)S(1)} %collective-permute-done.7.other_ref), custom_call_target="tpu_custom_call" | custom-call | tf_op jit(solution)/shard_map/pallas_call | solution.py:392
  44.6 3.4 %all-to-all-start.2 = ((bf16[4,256,128]{2,1,0:T(8,128)(2,1)}), bf16[4,256,128]{2,1,0:T(8,128)(2,1)S(1)}, u32[]{:S(2)}, u32[]{:S(2)}) async-start(bf16[4,256,128]{2,1,0:T(8,128)(2,1)} %shard_map.180), calls=%async_computation.2 | async-start | bytes 524288 | tf_op jit(solution)/shard_map/all_to_all | solution.py:265
  48.0 0.1 collective-permute-start.6
  48.1 0.2 shard_map.178
  48.3 5.1 %collective-permute-done.6.got_ref = bf16[4,64,128]{2,1,0:T(8,128)(2,1)S(1)} collective-permute-done((bf16[4,64,128]{2,1,0:T(8,128)(2,1)S(1)}, bf16[4,64,128]{2,1,0:T(8,128)(2,1)S(1)}, u32[]{:S(2)}, u32[]{:S(2)}) %collective-permute-start.6) | collective-permute-done | bytes 65568 | tf_op jit(solution)/shard_map/ppermute | solution.py:261
  53.4 0.5 all-to-all-done.2.part_ref
  53.9 0.9 %shard_map.181 = (bf16[256,128]{1,0:T(8,128)(2,1)}, f32[1,128]{1,0:T(1,128)}, f32[128,512]{1,0:T(8,128)}, f32[128,512]{1,0:T(8,128)}) custom-call(s32[1]{0:T(128)} %bitcast.1.side_ref, f32[256,128]{1,0:T(8,128)S(1)} %get-tuple-element.45.back_ref, f32[1,128]{1,0:T(1,128)S(1)} %get-tuple-element.46.near_ref, bf16[256,512]{1,0:T(8,128)(2,1)S(1)} %get-tuple-element.43.mark_ref, ...), custom_call_target="tpu_custom_call" | custom-call | tf_op jit(solution)/shard_map/pallas_call | solution.py:400
  (4 shorter events, 0.0 us)
Async XLA Ops:
  2.9 17.8 %collective-permute-start.2 = (bf16[1552,128]{1,0:T(8,128)(2,1)S(1)}, bf16[1552,128]{1,0:T(8,128)(2,1)S(1)}, u32[]{:S(2)}, u32[]{:S(2)}) collective-permute-start(bf16[1552,128]{1,0:T(8,128)(2,1)S(1)} %get-tuple-element.38.refs_0_), channel_id=1, source_target_pairs={{0,2},{1,3},{2,0},{3,1},{4,6},{5,7},{6,4},{7,5},{8,10},{9,11},{10,... | collective-permute-start | bytes 1191944 | tf_op jit(solution)/shard_map/ppermute | solution.py:261
  5.9 13.2 %all-to-all-start = ((bf16[8,64,128]{2,1,0:T(8,128)(2,1)}), bf16[8,64,128]{2,1,0:T(8,128)(2,1)S(1)}, u32[]{:S(2)}, u32[]{:S(2)}) async-start(bf16[8,64,128]{2,1,0:T(8,128)(2,1)} %get-tuple-element.40), calls=%async_computation | async-start | bytes 262144 | tf_op jit(solution)/shard_map/all_to_all | solution.py:265
  12.4 6.7 %copy-start = (bf16[256,128]{1,0:T(8,128)(2,1)S(1)}, bf16[256,128]{1,0:T(8,128)(2,1)}, u32[]{:S(2)}) copy-start(bf16[256,128]{1,0:T(8,128)(2,1)} %x_ref.5) | copy-start | bytes 196612
  19.3 7.1 %copy-start.1 = (bf16[128,512]{1,0:T(8,128)(2,1)S(1)}, bf16[128,512]{1,0:T(8,128)(2,1)}, u32[]{:S(2)}) copy-start(bf16[128,512]{1,0:T(8,128)(2,1)} %ws_ref.3) | copy-start | bytes 393220
  19.3 7.1 %copy-start.2 = (bf16[128,512]{1,0:T(8,128)(2,1)S(1)}, bf16[128,512]{1,0:T(8,128)(2,1)}, u32[]{:S(2)}) copy-start(bf16[128,512]{1,0:T(8,128)(2,1)} %wn_ref.3) | copy-start | bytes 393220
  19.3 1.3 %collective-permute-start.1 = (bf16[256,128]{1,0:T(8,128)(2,1)S(1)}, bf16[256,128]{1,0:T(8,128)(2,1)S(1)}, u32[]{:S(2)}, u32[]{:S(2)}) collective-permute-start(bf16[256,128]{1,0:T(8,128)(2,1)S(1)} %shard_map.175.refs_4_), channel_id=1, source_target_pairs={{0,1},{1,0},{2,3},{3,2},{4,5},{5,4},{6,7},{7,6},{8,9},{9,8},{10,11... | collective-permute-start | bytes 196616 | tf_op jit(solution)/shard_map/ppermute | solution.py:261
  19.4 7.0 %collective-permute-start = (bf16[1552,128]{1,0:T(8,128)(2,1)S(1)}, bf16[1552,128]{1,0:T(8,128)(2,1)S(1)}, u32[]{:S(2)}, u32[]{:S(2)}) collective-permute-start(bf16[1552,128]{1,0:T(8,128)(2,1)S(1)} %get-tuple-element.38.refs_0_), channel_id=1, source_target_pairs={{0,1},{1,0},{2,3},{3,2},{4,5},{5,4},{6,7},{7,6},{8,9},{9,8},{10,11... | collective-permute-start | bytes 1191944 | tf_op jit(solution)/shard_map/ppermute | solution.py:261
  20.7 5.8 %collective-permute-start.3 = (bf16[1552,128]{1,0:T(8,128)(2,1)S(1)}, bf16[1552,128]{1,0:T(8,128)(2,1)S(1)}, u32[]{:S(2)}, u32[]{:S(2)}) collective-permute-start(bf16[1552,128]{1,0:T(8,128)(2,1)S(1)} %shard_map.176.refs_2_), channel_id=1, source_target_pairs={{0,1},{1,0},{2,3},{3,2},{4,5},{5,4},{6,7},{7,6},{8,9},{9,8},{10,11... | collective-permute-start | bytes 1191944 | tf_op jit(solution)/shard_map/ppermute | solution.py:261
  20.8 4.4 %collective-permute-start.4 = (bf16[256,128]{1,0:T(8,128)(2,1)S(1)}, bf16[256,128]{1,0:T(8,128)(2,1)S(1)}, u32[]{:S(2)}, u32[]{:S(2)}) collective-permute-start(bf16[256,128]{1,0:T(8,128)(2,1)S(1)} %shard_map.175.refs_4_), channel_id=1, source_target_pairs={{0,2},{1,3},{2,0},{3,1},{4,6},{5,7},{6,4},{7,5},{8,10},{9,11},{10,... | collective-permute-start | bytes 196616 | tf_op jit(solution)/shard_map/ppermute | solution.py:261
  25.2 1.3 %collective-permute-start.5 = (bf16[256,128]{1,0:T(8,128)(2,1)S(1)}, bf16[256,128]{1,0:T(8,128)(2,1)S(1)}, u32[]{:S(2)}, u32[]{:S(2)}) collective-permute-start(bf16[256,128]{1,0:T(8,128)(2,1)S(1)} %collective-permute-done.4.refs_6_), channel_id=1, source_target_pairs={{0,1},{1,0},{2,3},{3,2},{4,5},{5,4},{6,7},{7,6},{8,9},{9,8},{10,11... | collective-permute-start | bytes 196616 | tf_op jit(solution)/shard_map/ppermute | solution.py:261
  38.0 5.9 %collective-permute-start.7 = (bf16[256,128]{1,0:T(8,128)(2,1)S(1)}, bf16[256,128]{1,0:T(8,128)(2,1)S(1)}, u32[]{:S(2)}, u32[]{:S(2)}) collective-permute-start(bf16[256,128]{1,0:T(8,128)(2,1)S(1)} %get-tuple-element.48.own_ref), channel_id=1, source_target_pairs={{0,16},{4,20},{8,24},{12,28},{16,0},{20,4},{24,8},{28,12},{1,17},{... | collective-permute-start | bytes 196616 | tf_op jit(solution)/shard_map/ppermute | solution.py:261
  44.6 9.3 %all-to-all-start.2 = ((bf16[4,256,128]{2,1,0:T(8,128)(2,1)}), bf16[4,256,128]{2,1,0:T(8,128)(2,1)S(1)}, u32[]{:S(2)}, u32[]{:S(2)}) async-start(bf16[4,256,128]{2,1,0:T(8,128)(2,1)} %shard_map.180), calls=%async_computation.2 | async-start | bytes 524288 | tf_op jit(solution)/shard_map/all_to_all | solution.py:265
  48.0 5.3 %collective-permute-start.6 = (bf16[4,64,128]{2,1,0:T(8,128)(2,1)S(1)}, bf16[4,64,128]{2,1,0:T(8,128)(2,1)S(1)}, u32[]{:S(2)}, u32[]{:S(2)}) collective-permute-start(bf16[4,64,128]{2,1,0:T(8,128)(2,1)S(1)} %get-tuple-element.47), channel_id=1, source_target_pairs={{0,16},{4,20},{8,24},{12,28},{16,0},{20,4},{24,8},{28,12},{1,17},{... | collective-permute-start | bytes 196616 | tf_op jit(solution)/shard_map/ppermute | solution.py:261

commit v8 on v7

--- a/solution.py
+++ b/solution.py
@@ -129,11 +129,7 @@
     mark_ref[...] = source_matrix(send_v[0], hub_v[...], rows, width)
 
 
-def pass_kernel(after_ref, far_ref, passed_ref):
-    pass
-
-
-def neigh_kernel(x_ref, mix_ref, got_ref, neigh_ref):
+def neigh_kernel(x_ref, mix_ref, far_ref, got_ref, neigh_ref, passed_ref):
     rows, cols = x_ref.shape
     lanes = mix_ref.shape[1] - rows
     total = jnp.dot(mix_ref[:, :rows], x_ref[...], preferred_element_type=F32)
@@ -141,9 +137,12 @@
     neigh_ref[...] = total.astype(BF)
 
 
-def dense_kernel(slots, hub_here, feats, width, me_ref, side_ref, x_ref, ws_ref, wn_ref, turned_ref, *refs):
+def dense_kernel(slots, hub_here, feats, width, count, me_ref, side_ref, seat_ref, x_ref, ws_ref, wn_ref, turned_ref, *refs):
     pack_refs, n_refs = refs[:feats], refs[feats : 2 * feats]
-    out_ref, back_ref, send_ref, pre_ref, cot_ref, bias_ref = refs[2 * feats :]
+    out_ref, back_ref = refs[2 * feats : 2 * feats + 2]
+    send_refs = refs[2 * feats + 2 : 2 * feats + 2 + count]
+    pre_ref, cot_ref, bias_ref, hold_ref = refs[2 * feats + 2 + count :]
+    send_ref = send_refs[0] if count == 1 else hold_ref
     rows, cols = x_ref.shape
     depth, full = ws_ref.shape
     blocks = full // cols
@@ -194,15 +193,25 @@
                 at = (j * 2 + kind) * depth + part * step
                 low = 2 * width + at % share
                 send_ref[at // share, low : low + step, :] = block[part * step : (part + 1) * step]
-
-
-def sum_kernel(width, got_ref, sum_ref, relay_ref):
-    half = got_ref.shape[0]
+    if count > 1:
+        for k, ref in enumerate(send_refs):
+            ref[...] = hold_ref[seat_ref[0] ^ k]
+
+
+def seated(refs, seat):
+    if len(refs) == 1:
+        return [(j, refs[0].at[j]) for j in range(refs[0].shape[0])]
+    return [(seat ^ k, ref) for k, ref in enumerate(refs)]
+
+
+def sum_kernel(width, seat_ref, *refs):
+    got_refs, (sum_ref, near_ref, relay_ref) = refs[:-3], refs[-3:]
     total = jnp.zeros(sum_ref.shape, F32)
-    for j in range(half):
-        total = total + got_ref[j, 2 * width :, :].astype(F32)
+    for j, got_ref in seated(got_refs, seat_ref[0]):
+        total = total + got_ref[2 * width :, :].astype(F32)
+        near_ref[j] = got_ref[:width, :]
+        relay_ref[j] = got_ref[width : 2 * width, :]
     sum_ref[...] = total.astype(BF)
-    relay_ref[...] = got_ref[:, width : 2 * width, :]
 
 
 def total_kernel(own_ref, other_ref, part_ref):
@@ -210,12 +219,10 @@
     part_ref[...] = jnp.broadcast_to(total, part_ref.shape)
 
 
-def near_rows(slots, hub_here, width, start, mark_ref, got_ref):
-    half = got_ref.shape[0]
-    cols = got_ref.shape[-1]
+def near_rows(slots, hub_here, start, mark_ref, got_ref):
+    half, width, cols = got_ref.shape
     cut = pl.ds(pl.multiple_of(start * width, 128), half * width)
-    rows = got_ref[:, :width, :]
-    added = jnp.dot(mark_ref[:, cut], rows.reshape(half * width, cols), preferred_element_type=F32)
+    added = jnp.dot(mark_ref[:, cut], got_ref[...].reshape(half * width, cols), preferred_element_type=F32)
     first = slots + hub_here
     bias = jnp.zeros((2, cols), F32)
     for j in range(half):
@@ -223,27 +230,35 @@
     return added, jnp.sum(bias, axis=0, keepdims=True)
 
 
-def near_kernel(slots, hub_here, width, side_ref, back_ref, mark_ref, got_ref, sum_ref, bias_ref):
+def near_kernel(slots, hub_here, side_ref, back_ref, mark_ref, got_ref, sum_ref, bias_ref):
     half = got_ref.shape[0]
-    added, bias = near_rows(slots, hub_here, width, side_ref[0] * half, mark_ref, got_ref)
+    added, bias = near_rows(slots, hub_here, side_ref[0] * half, mark_ref, got_ref)
     sum_ref[...] = back_ref[...] + added
     bias_ref[...] = bias
 
 
-def last_kernel(
-    scale, slots, hub_here, width, side_ref, back_ref, near_ref, mark_ref, got_ref, part_ref,
-    grad_ref, bias_ref, self_ref, neigh_ref,
-):
+def grad_kernel(scale, slots, hub_here, side_ref, back_ref, near_ref, mark_ref, got_ref, grad_ref, bias_ref):
+    half = got_ref.shape[0]
+    added, bias = near_rows(slots, hub_here, half - side_ref[0] * half, mark_ref, got_ref)
+    grad_ref[...] = (back_ref[...] + added).astype(BF)
+    bias_ref[...] = (near_ref[...] + bias) * scale
+
+
+def spread_kernel(scale, seat_ref, *refs):
+    got_refs, (self_ref, neigh_ref) = refs[:-2], refs[-2:]
     depth, full = self_ref.shape
-    half, share, cols = part_ref.shape
-    whole = part_ref[...].reshape(half * share, cols).astype(F32) * scale
+    cols = got_refs[0].shape[-1]
+    if len(got_refs) > 1:
+        for j, ref in seated(got_refs, seat_ref[0]):
+            cut = pl.ds(pl.multiple_of(j * cols, cols), cols)
+            self_ref[:, cut] = ref[:depth, :].astype(F32) * scale
+            neigh_ref[:, cut] = ref[depth:, :].astype(F32) * scale
+        return
+    whole = got_refs[0][...].reshape(2 * (full // cols) * depth, cols).astype(F32) * scale
     for j in range(full // cols):
         at = 2 * j * depth
         self_ref[:, j * cols : (j + 1) * cols] = whole[at : at + depth]
         neigh_ref[:, j * cols : (j + 1) * cols] = whole[at + depth : at + 2 * depth]
-    added, bias = near_rows(slots, hub_here, width, half - side_ref[0] * half, mark_ref, got_ref)
-    grad_ref[...] = (back_ref[...] + added).astype(BF)
-    bias_ref[...] = (near_ref[...] + bias) * scale
 
 
 VMEM = pl.BlockSpec(memory_space=pltpu.VMEM)
@@ -263,6 +278,10 @@
 
 def exchange(blocks, groups=None):
     return lax.all_to_all(blocks, "dom", split_axis=0, concat_axis=0, axis_index_groups=groups, tiled=True)
+
+
+def swap(blocks):
+    return [blocks[0]] + [partner(block, "dom", k) for k, block in enumerate(blocks) if k]
 
 
 def on_device(
@@ -290,11 +309,14 @@
     lanes = peers * width
     half = peers // 2
     share = 2 * blocks * depth // half
+    direct = half == blocks
+    count = half if direct else 1
     halves = [list(range(half)), list(range(half, peers))]
     scale = 1.0 / math.sqrt(peers * rows)
     feats = lax.axis_size("feat")
     me = lax.axis_index("feat").astype(jnp.int32).reshape(1)
     side = (lax.axis_index("dom") >= half).astype(jnp.int32).reshape(1)
+    seat = lax.rem(lax.axis_index("dom"), half).astype(jnp.int32).reshape(1)
     pack_rows = 2 * blocks * depth + 2 * rows + 16
 
     def pinned(*arrays):
@@ -334,81 +356,78 @@
         compiler_params=PARAMS,
         cost_estimate=pl.CostEstimate(flops=10**8, bytes_accessed=3 * 10**6, transcendentals=0),
     )(tile_count.reshape(1, 1), *moved)
-    neigh = pl.pallas_call(
+    neigh, far = pl.pallas_call(
         neigh_kernel,
-        out_shape=shape((rows, cols), BF),
-        in_specs=[VMEM] * 3,
-        out_specs=VMEM,
-        compiler_params=PARAMS,
-    )(features, mix, incoming)
+        out_shape=(shape((rows, cols), BF), shape((pack_rows, cols), BF)),
+        in_specs=[VMEM, VMEM, ANY, VMEM],
+        out_specs=(VMEM, ANY),
+        input_output_aliases={2: 1},
+        compiler_params=PARAMS,
+    )(features, mix, far, incoming)
+    last = partner(far, "feat", 1)
     far_neigh = partner(neigh, "feat", 2)
-    near_neigh = partner(neigh, "feat", 1)
-    far = pl.pallas_call(
-        pass_kernel,
-        out_shape=shape((pack_rows, cols), BF),
-        in_specs=[ANY, ANY],
-        out_specs=ANY,
-        input_output_aliases={1: 0},
-        compiler_params=PARAMS,
-    )(near_neigh, far)
-    last = partner(far, "feat", 1)
-    every = [neigh, near_neigh, far_neigh, partner(far_neigh, "feat", 1)]
-
-    output, back, returned = pl.pallas_call(
-        functools.partial(dense_kernel, slots, hub_here, feats, width),
+    every = [neigh, partner(neigh, "feat", 1), far_neigh, partner(far_neigh, "feat", 1)]
+
+    height = 2 * width + share
+    output, back, *returned = pl.pallas_call(
+        functools.partial(dense_kernel, slots, hub_here, feats, width, count),
         out_shape=(
             shape((rows, cols), BF),
             shape((rows, cols), F32),
-            shape((half, 2 * width + share, cols), BF),
+            *([shape((height, cols), BF)] * half if direct else [shape((half, height, cols), BF)]),
         ),
-        in_specs=[SMEM] * 2 + [VMEM] * (4 + 2 * feats),
-        out_specs=(VMEM,) * 3,
+        in_specs=[SMEM] * 3 + [VMEM] * (4 + 2 * feats),
+        out_specs=(VMEM,) * (2 + count),
         scratch_shapes=[
             pltpu.VMEM((rows, full), F32),
             pltpu.VMEM((rows, full), BF),
             pltpu.VMEM((16, full), BF),
+            pltpu.VMEM((half, height, cols) if direct else (1, 16, cols), BF),
         ],
         compiler_params=PARAMS,
-    )(me, side, features, w_self, w_neigh, turned, pack, near, far, last, *every)
-
-    arrived = exchange(returned, halves)
-    half_sum, relay = pl.pallas_call(
+    )(me, side, seat, features, w_self, w_neigh, turned, pack, near, far, last, *every)
+
+    arrived = swap(returned) if direct else [exchange(returned[0], halves)]
+    half_sum, near_ghosts, relay = pl.pallas_call(
         functools.partial(sum_kernel, width),
-        out_shape=(shape((share, cols), BF), shape((half, width, cols), BF)),
-        in_specs=[VMEM],
-        out_specs=(VMEM,) * 2,
-        compiler_params=PARAMS,
-    )(arrived)
+        out_shape=(shape((share, cols), BF), shape((half, width, cols), BF), shape((half, width, cols), BF)),
+        in_specs=[SMEM] + [VMEM] * count,
+        out_specs=(VMEM,) * 3,
+        compiler_params=PARAMS,
+    )(seat, *arrived)
     other_sum = partner(half_sum, "dom", half)
+    crossed = partner(relay, "dom", half)
     back, near_bias = pl.pallas_call(
-        functools.partial(near_kernel, slots, hub_here, width),
+        functools.partial(near_kernel, slots, hub_here),
         out_shape=(shape((rows, cols), F32), shape((1, cols), F32)),
         in_specs=[SMEM] + [VMEM] * 3,
         out_specs=(VMEM,) * 2,
         compiler_params=PARAMS,
         cost_estimate=pl.CostEstimate(flops=10**8, bytes_accessed=10**6, transcendentals=0),
-    )(side, back, mark, arrived)
-    crossed = partner(relay, "dom", half)
+    )(side, back, mark, near_ghosts)
     part = pl.pallas_call(
         total_kernel,
-        out_shape=shape((half, share, cols), BF),
+        out_shape=shape((share, cols) if direct else (half, share, cols), BF),
         in_specs=[VMEM, VMEM],
         out_specs=VMEM,
         compiler_params=PARAMS,
     )(half_sum, other_sum)
-    parts = exchange(part, halves)
-    grad_features, grad_bias, grad_self, grad_neigh = pl.pallas_call(
-        functools.partial(last_kernel, scale, slots, hub_here, width),
-        out_shape=(
-            shape((rows, cols), BF),
-            shape((1, cols), F32),
-            shape((depth, full), F32),
-            shape((depth, full), F32),
-        ),
-        in_specs=[SMEM] + [VMEM] * 5,
-        out_specs=(VMEM,) * 4,
-        compiler_params=PARAMS,
-    )(side, back, near_bias, mark, crossed, parts)
+    parts = swap([part] * half) if direct else [exchange(part, halves)]
+    grad_features, grad_bias = pl.pallas_call(
+        functools.partial(grad_kernel, scale, slots, hub_here),
+        out_shape=(shape((rows, cols), BF), shape((1, cols), F32)),
+        in_specs=[SMEM] + [VMEM] * 4,
+        out_specs=(VMEM,) * 2,
+        compiler_params=PARAMS,
+        cost_estimate=pl.CostEstimate(flops=2 * 10**9, bytes_accessed=10**6, transcendentals=0),
+    )(side, back, near_bias, mark, crossed)
+    grad_self, grad_neigh = pl.pallas_call(
+        functools.partial(spread_kernel, scale),
+        out_shape=(shape((depth, full), F32), shape((depth, full), F32)),
+        in_specs=[SMEM] + [VMEM] * count,
+        out_specs=(VMEM,) * 2,
+        compiler_params=PARAMS,
+    )(seat, *parts)
     return output, grad_features, grad_self, grad_neigh, grad_bias.reshape(cols)
 
 

time: 55.1 us -> 49.8 us (0.904)
  blocking collectives: 10.1 us -> 0 us
  starting transfers between devices: 14 us -> 19.7 us
  waiting for transfers between devices: 23.2 us -> 22.1 us
    all_to_all x1 -> x0, blocking collectives: 10.1 us -> none  [exchange(): lax.all_to_all(blocks, 'dom', split_axis=0, concat_axis=0, axis_index_gro...]
    ppermute x8 -> x14, starting transfers between devices: 4.79 us -> 13.9 us  [partner(): lax.ppermute(block, axis, [(i, i ^ k) for i in range(lax.axis_size(axis))])]
    all_to_all x2 -> x1, starting transfers between devices: 9.24 us -> 5.83 us  [exchange(): lax.all_to_all(blocks, 'dom', split_axis=0, concat_axis=0, axis_index_gro...]
    ppermute x8 -> x14, waiting for transfers between devices: 16.4 us -> 15.8 us  [partner(): lax.ppermute(block, axis, [(i, i ^ k) for i in range(lax.axis_size(axis))])]
    all_to_all x2 -> x1, waiting for transfers between devices: 6.79 us -> 6.27 us  [exchange(): lax.all_to_all(blocks, 'dom', split_axis=0, concat_axis=0, axis_index_gro...]
  transfers between devices with their start and end apart: 10 -> 15, of which waited for: 7 -> 9; matrix products, arithmetic and copies ran while one was open for 0% -> 0% of each run, Pallas kernels for 1% -> 3%
where the time goes in v8:
time: 49.8 us; the launch traced here: 49.5 us
  waiting for transfers between devices  22.1 us (44%)
  starting transfers between devices  19.7 us (40%)
  Pallas kernels  6.3 us (13%)
  between operations  1.38 us (3%)
    ppermute x14, waiting for transfers between devices, partner(): lax.ppermute(block, axis, [(i, i ^ k) for i in range(lax.axis_size(axis))])  15.8 us
    ppermute x14, starting transfers between devices, partner(): lax.ppermute(block, axis, [(i, i ^ k) for i in range(lax.axis_size(axis))])  13.9 us
    all_to_all x1, waiting for transfers between devices, exchange(): lax.all_to_all(blocks, 'dom', split_axis=0, concat_axis=0, axis_index_gro...  6.27 us
    all_to_all x1, starting transfers between devices, exchange(): lax.all_to_all(blocks, 'dom', split_axis=0, concat_axis=0, axis_index_gro...  5.83 us
    pallas_call x1, Pallas kernels, on_device(): pl.pallas_call(functools.partial(send_kernel, width), out_shape=(shape((p...  2.23 us
    pallas_call x1, Pallas kernels, on_device(): pl.pallas_call(functools.partial(dense_kernel, slots, hub_here, feats, wi...  1.53 us
  transfers between devices with their start and end apart: 15, of which 9 were waited for; matrix products, arithmetic and copies ran while one was open for 0% of the time, Pallas kernels for 3%

profile of v8, /device:TPU:0, one launch (start us, length us, event | category | flops | bytes accessed | tf_op | source)
XLA Modules:
  0.0 49.5 jit_solution(15924462296697071168)
XLA Ops:
  0.6 2.2 %shard_map.173 = (bf16[8,64,128]{2,1,0:T(8,128)(2,1)}, bf16[1552,128]{1,0:T(8,128)(2,1)S(1)}, s32[1,8,48]{2,1,0:T(8,128)S(1)}, s32[1,2]{1,0:T(1,128)S(1)}, s32[1...) custom-call(bf16[256,128]{1,0:T(8,128)(2,1)} %x_ref.5, ...), custom_call_target="tpu_custom_call" | custom-call | tf_op jit(solution)/shard_map/pallas_call | solution.py:328
  2.9 3.0 %collective-permute-start.1 = (bf16[1552,128]{1,0:T(8,128)(2,1)S(1)}, bf16[1552,128]{1,0:T(8,128)(2,1)S(1)}, u32[]{:S(2)}, u32[]{:S(2)}) collective-permute-start(bf16[1552,128]{1,0:T(8,128)(2,1)S(1)} %get-tuple-element.44.refs_0_), channel_id=1, source_target_pairs={{0,2},{1,3},{2,0},{3,1},{4,6},{5,7},{6,4},{7,5},{8,10},{9,11},{10,... | collective-permute-start | bytes 1191944 | tf_op jit(solution)/shard_map/ppermute | solution.py:276
  5.9 5.8 %all-to-all-start = ((bf16[8,64,128]{2,1,0:T(8,128)(2,1)}), bf16[8,64,128]{2,1,0:T(8,128)(2,1)S(1)}, u32[]{:S(2)}, u32[]{:S(2)}) async-start(bf16[8,64,128]{2,1,0:T(8,128)(2,1)} %get-tuple-element.46), calls=%async_computation | async-start | bytes 262144 | tf_op jit(solution)/shard_map/all_to_all | solution.py:280
  12.4 0.0 copy-start
  12.4 0.4 shard_map.174
  12.8 6.3 %all-to-all-done.got_ref = bf16[8,64,128]{2,1,0:T(8,128)(2,1)S(1)} async-done(((bf16[8,64,128]{2,1,0:T(8,128)(2,1)}), bf16[8,64,128]{2,1,0:T(8,128)(2,1)S(1)}, u32[]{:S(2)}, u32[]{:S(2)}) %all-to-all-start) | async-done | bytes 131104 | tf_op jit(solution)/shard_map/all_to_all | solution.py:280
  19.1 0.0 copy-start.2
  19.1 0.3 shard_map.175
  19.3 0.1 collective-permute-start.2
  19.4 0.6 %collective-permute-start.4 = (bf16[256,128]{1,0:T(8,128)(2,1)S(1)}, bf16[256,128]{1,0:T(8,128)(2,1)S(1)}, u32[]{:S(2)}, u32[]{:S(2)}) collective-permute-start(bf16[256,128]{1,0:T(8,128)(2,1)S(1)} %get-tuple-element.48.refs_4_), channel_id=1, source_target_pairs={{0,2},{1,3},{2,0},{3,1},{4,6},{5,7},{6,4},{7,5},{8,10},{9,11},{10,... | collective-permute-start | bytes 196616 | tf_op jit(solution)/shard_map/ppermute | solution.py:276
  20.0 0.2 collective-permute-start.3
  20.2 3.7 %collective-permute-done.4.refs_6_ = bf16[256,128]{1,0:T(8,128)(2,1)S(1)} collective-permute-done((bf16[256,128]{1,0:T(8,128)(2,1)S(1)}, bf16[256,128]{1,0:T(8,128)(2,1)S(1)}, u32[]{:S(2)}, u32[]{:S(2)}) %collective-permute-start.4) | collective-permute-done | bytes 65568 | tf_op jit(solution)/shard_map/ppermute | solution.py:276
  23.9 1.2 %collective-permute-done.5.refs_7_ = bf16[256,128]{1,0:T(8,128)(2,1)S(1)} collective-permute-done((bf16[256,128]{1,0:T(8,128)(2,1)S(1)}, bf16[256,128]{1,0:T(8,128)(2,1)S(1)}, u32[]{:S(2)}, u32[]{:S(2)}) %collective-permute-start.5) | collective-permute-done | bytes 65568 | tf_op jit(solution)/shard_map/ppermute | solution.py:276
  25.2 1.5 %shard_map.176 = (bf16[256,128]{1,0:T(8,128)(2,1)}, f32[256,128]{1,0:T(8,128)S(1)}, bf16[384,128]{1,0:T(8,128)(2,1)S(1)}, bf16[384,128]{1,0:T(8,128)(2,1)S(1)}, ...) custom-call(s32[1]{0:T(128)} %bitcast.me_ref, s32[1]{0:T(128)} %bitcast.1.side_ref, s32[1]{0:T(128)} %bitcast.2.seat_ref, ...), custom_call_target="tpu_custom_call" | custom-call | tf_op jit(solution)/shard_map/pallas_call | solution.py:372
  26.7 0.2 collective-permute-start.6
  26.9 1.1 %collective-permute-start.7 = (bf16[384,128]{1,0:T(8,128)(2,1)S(1)}, bf16[384,128]{1,0:T(8,128)(2,1)S(1)}, u32[]{:S(2)}, u32[]{:S(2)}) collective-permute-start(bf16[384,128]{1,0:T(8,128)(2,1)S(1)} %get-tuple-element.54), channel_id=1, source_target_pairs={{0,8},{4,12},{8,0},{12,4},{16,24},{20,28},{24,16},{28,20},{1,9},{5... | collective-permute-start | bytes 294920 | tf_op jit(solution)/shard_map/ppermute | solution.py:276
  28.0 2.2 %collective-permute-start.8 = (bf16[384,128]{1,0:T(8,128)(2,1)S(1)}, bf16[384,128]{1,0:T(8,128)(2,1)S(1)}, u32[]{:S(2)}, u32[]{:S(2)}) collective-permute-start(bf16[384,128]{1,0:T(8,128)(2,1)S(1)} %get-tuple-element.55), channel_id=1, source_target_pairs={{0,12},{4,8},{8,4},{12,0},{16,28},{20,24},{24,20},{28,16},{1,13},{... | collective-permute-start | bytes 294920 | tf_op jit(solution)/shard_map/ppermute | solution.py:276
  30.2 1.4 %collective-permute-done.6.refs_1_ = bf16[384,128]{1,0:T(8,128)(2,1)S(1)} collective-permute-done((bf16[384,128]{1,0:T(8,128)(2,1)S(1)}, bf16[384,128]{1,0:T(8,128)(2,1)S(1)}, u32[]{:S(2)}, u32[]{:S(2)}) %collective-permute-start.6) | collective-permute-done | bytes 98336 | tf_op jit(solution)/shard_map/ppermute | solution.py:276
  31.6 0.9 %collective-permute-done.7.refs_2_ = bf16[384,128]{1,0:T(8,128)(2,1)S(1)} collective-permute-done((bf16[384,128]{1,0:T(8,128)(2,1)S(1)}, bf16[384,128]{1,0:T(8,128)(2,1)S(1)}, u32[]{:S(2)}, u32[]{:S(2)}) %collective-permute-start.7) | collective-permute-done | bytes 98336 | tf_op jit(solution)/shard_map/ppermute | solution.py:276
  32.5 2.4 %collective-permute-done.8.refs_3_ = bf16[384,128]{1,0:T(8,128)(2,1)S(1)} collective-permute-done((bf16[384,128]{1,0:T(8,128)(2,1)S(1)}, bf16[384,128]{1,0:T(8,128)(2,1)S(1)}, u32[]{:S(2)}, u32[]{:S(2)}) %collective-permute-start.8) | collective-permute-done | bytes 98336 | tf_op jit(solution)/shard_map/ppermute | solution.py:276
  34.9 0.4 collective-permute-start.10
  35.4 2.5 %collective-permute-start.9 = (bf16[4,64,128]{2,1,0:T(8,128)(2,1)S(1)}, bf16[4,64,128]{2,1,0:T(8,128)(2,1)S(1)}, u32[]{:S(2)}, u32[]{:S(2)}) collective-permute-start(bf16[4,64,128]{2,1,0:T(8,128)(2,1)S(1)} %get-tuple-element.59), channel_id=1, source_target_pairs={{0,16},{4,20},{8,24},{12,28},{16,0},{20,4},{24,8},{28,12},{1,17},{... | collective-permute-start | bytes 196616 | tf_op jit(solution)/shard_map/ppermute | solution.py:276
  37.9 0.2 shard_map.178
  38.1 3.9 %collective-permute-done.10.other_ref = bf16[256,128]{1,0:T(8,128)(2,1)S(1)} collective-permute-done((bf16[256,128]{1,0:T(8,128)(2,1)S(1)}, bf16[256,128]{1,0:T(8,128)(2,1)S(1)}, u32[]{:S(2)}, u32[]{:S(2)}) %collective-permute-start.10) | collective-permute-done | bytes 65568 | tf_op jit(solution)/shard_map/ppermute | solution.py:276
  42.0 0.1 collective-permute-start.13
  42.1 2.2 %collective-permute-start.12 = (bf16[256,128]{1,0:T(8,128)(2,1)S(1)}, bf16[256,128]{1,0:T(8,128)(2,1)S(1)}, u32[]{:S(2)}, u32[]{:S(2)}) collective-permute-start(bf16[256,128]{1,0:T(8,128)(2,1)S(1)} %shard_map.180.refs_0_), channel_id=1, source_target_pairs={{0,8},{4,12},{8,0},{12,4},{16,24},{20,28},{24,16},{28,20},{1,9},{5... | collective-permute-start | bytes 196616 | tf_op jit(solution)/shard_map/ppermute | solution.py:276
  44.3 1.3 %collective-permute-start.11 = (bf16[256,128]{1,0:T(8,128)(2,1)S(1)}, bf16[256,128]{1,0:T(8,128)(2,1)S(1)}, u32[]{:S(2)}, u32[]{:S(2)}) collective-permute-start(bf16[256,128]{1,0:T(8,128)(2,1)S(1)} %shard_map.180.refs_0_), channel_id=1, source_target_pairs={{0,4},{4,0},{8,12},{12,8},{16,20},{20,16},{24,28},{28,24},{1,5},{5... | collective-permute-start | bytes 196616 | tf_op jit(solution)/shard_map/ppermute | solution.py:276
  45.6 0.8 %shard_map.179 = (bf16[256,128]{1,0:T(8,128)(2,1)}, f32[1,128]{1,0:T(1,128)}) custom-call(s32[1]{0:T(128)} %bitcast.1.side_ref, f32[256,128]{1,0:T(8,128)S(1)} %get-tuple-element.57.back_ref, f32[1,128]{1,0:T(1,128)S(1)} %get-tuple-element.58.near_ref, bf16[256,512]{1,0:T(8,128)(2,1)S(1)} %get-tuple-element.51.mark_ref, ...), custom_call_target="tpu_custom_call" | custom-call | flops 2000000000 | bytes 1000000 | tf_op jit(solution)/shard_map/pallas_call | solution.py:416
  46.4 0.9 %collective-permute-done.13.refs_3_ = bf16[256,128]{1,0:T(8,128)(2,1)S(1)} collective-permute-done((bf16[256,128]{1,0:T(8,128)(2,1)S(1)}, bf16[256,128]{1,0:T(8,128)(2,1)S(1)}, u32[]{:S(2)}, u32[]{:S(2)}) %collective-permute-start.13) | collective-permute-done | bytes 65568 | tf_op jit(solution)/shard_map/ppermute | solution.py:276
  47.3 0.0 collective-permute-done.12.refs_2_
  47.3 1.3 %collective-permute-done.11.refs_1_ = bf16[256,128]{1,0:T(8,128)(2,1)S(1)} collective-permute-done((bf16[256,128]{1,0:T(8,128)(2,1)S(1)}, bf16[256,128]{1,0:T(8,128)(2,1)S(1)}, u32[]{:S(2)}, u32[]{:S(2)}) %collective-permute-start.11) | collective-permute-done | bytes 65568 | tf_op jit(solution)/shard_map/ppermute | solution.py:276
  48.6 0.9 %shard_map.181 = (f32[128,512]{1,0:T(8,128)}, f32[128,512]{1,0:T(8,128)}) custom-call(s32[1]{0:T(128)} %bitcast.2.seat_ref, bf16[256,128]{1,0:T(8,128)(2,1)S(1)} %shard_map.180.refs_0_, bf16[256,128]{1,0:T(8,128)(2,1)S(1)} %collective-permute-done.11.refs_1_, bf16[256,128]{1,0:T(8,128)(2,1)S(1)} %collective-permute-done.12.refs_2_, ...), custom_call_target="tpu_custom_call" | custom-call | tf_op jit(solution)/shard_map/pallas_call | solution.py:424
  (13 shorter events, 0.1 us)
Async XLA Ops:
  2.9 16.2 %collective-permute-start.1 = (bf16[1552,128]{1,0:T(8,128)(2,1)S(1)}, bf16[1552,128]{1,0:T(8,128)(2,1)S(1)}, u32[]{:S(2)}, u32[]{:S(2)}) collective-permute-start(bf16[1552,128]{1,0:T(8,128)(2,1)S(1)} %get-tuple-element.44.refs_0_), channel_id=1, source_target_pairs={{0,2},{1,3},{2,0},{3,1},{4,6},{5,7},{6,4},{7,5},{8,10},{9,11},{10,... | collective-permute-start | bytes 1191944 | tf_op jit(solution)/shard_map/ppermute | solution.py:276
  5.9 13.2 %all-to-all-start = ((bf16[8,64,128]{2,1,0:T(8,128)(2,1)}), bf16[8,64,128]{2,1,0:T(8,128)(2,1)S(1)}, u32[]{:S(2)}, u32[]{:S(2)}) async-start(bf16[8,64,128]{2,1,0:T(8,128)(2,1)} %get-tuple-element.46), calls=%async_computation | async-start | bytes 262144 | tf_op jit(solution)/shard_map/all_to_all | solution.py:280
  11.7 12.2 %collective-permute-start = (bf16[1552,128]{1,0:T(8,128)(2,1)S(1)}, bf16[1552,128]{1,0:T(8,128)(2,1)S(1)}, u32[]{:S(2)}, u32[]{:S(2)}) collective-permute-start(bf16[1552,128]{1,0:T(8,128)(2,1)S(1)} %get-tuple-element.44.refs_0_), channel_id=1, source_target_pairs={{0,1},{1,0},{2,3},{3,2},{4,5},{5,4},{6,7},{7,6},{8,9},{9,8},{10,11... | collective-permute-start | bytes 1191944 | tf_op jit(solution)/shard_map/ppermute | solution.py:276
  12.4 6.7 %copy-start = (bf16[256,128]{1,0:T(8,128)(2,1)S(1)}, bf16[256,128]{1,0:T(8,128)(2,1)}, u32[]{:S(2)}) copy-start(bf16[256,128]{1,0:T(8,128)(2,1)} %x_ref.5) | copy-start | bytes 196612
  19.1 6.1 %copy-start.1 = (bf16[128,512]{1,0:T(8,128)(2,1)S(1)}, bf16[128,512]{1,0:T(8,128)(2,1)}, u32[]{:S(2)}) copy-start(bf16[128,512]{1,0:T(8,128)(2,1)} %ws_ref.3) | copy-start | bytes 393220
  19.1 6.1 %copy-start.2 = (bf16[128,512]{1,0:T(8,128)(2,1)S(1)}, bf16[128,512]{1,0:T(8,128)(2,1)}, u32[]{:S(2)}) copy-start(bf16[128,512]{1,0:T(8,128)(2,1)} %wn_ref.3) | copy-start | bytes 393220
  19.3 5.8 %collective-permute-start.2 = (bf16[1552,128]{1,0:T(8,128)(2,1)S(1)}, bf16[1552,128]{1,0:T(8,128)(2,1)S(1)}, u32[]{:S(2)}, u32[]{:S(2)}) collective-permute-start(bf16[1552,128]{1,0:T(8,128)(2,1)S(1)} %get-tuple-element.47.refs_2_), channel_id=1, source_target_pairs={{0,1},{1,0},{2,3},{3,2},{4,5},{5,4},{6,7},{7,6},{8,9},{9,8},{10,11... | collective-permute-start | bytes 1191944 | tf_op jit(solution)/shard_map/ppermute | solution.py:276
  19.4 4.5 %collective-permute-start.4 = (bf16[256,128]{1,0:T(8,128)(2,1)S(1)}, bf16[256,128]{1,0:T(8,128)(2,1)S(1)}, u32[]{:S(2)}, u32[]{:S(2)}) collective-permute-start(bf16[256,128]{1,0:T(8,128)(2,1)S(1)} %get-tuple-element.48.refs_4_), channel_id=1, source_target_pairs={{0,2},{1,3},{2,0},{3,1},{4,6},{5,7},{6,4},{7,5},{8,10},{9,11},{10,... | collective-permute-start | bytes 196616 | tf_op jit(solution)/shard_map/ppermute | solution.py:276
  20.0 3.9 %collective-permute-start.3 = (bf16[256,128]{1,0:T(8,128)(2,1)S(1)}, bf16[256,128]{1,0:T(8,128)(2,1)S(1)}, u32[]{:S(2)}, u32[]{:S(2)}) collective-permute-start(bf16[256,128]{1,0:T(8,128)(2,1)S(1)} %get-tuple-element.48.refs_4_), channel_id=1, source_target_pairs={{0,1},{1,0},{2,3},{3,2},{4,5},{5,4},{6,7},{7,6},{8,9},{9,8},{10,11... | collective-permute-start | bytes 196616 | tf_op jit(solution)/shard_map/ppermute | solution.py:276
  23.9 1.3 %collective-permute-start.5 = (bf16[256,128]{1,0:T(8,128)(2,1)S(1)}, bf16[256,128]{1,0:T(8,128)(2,1)S(1)}, u32[]{:S(2)}, u32[]{:S(2)}) collective-permute-start(bf16[256,128]{1,0:T(8,128)(2,1)S(1)} %collective-permute-done.4.refs_6_), channel_id=1, source_target_pairs={{0,1},{1,0},{2,3},{3,2},{4,5},{5,4},{6,7},{7,6},{8,9},{9,8},{10,11... | collective-permute-start | bytes 196616 | tf_op jit(solution)/shard_map/ppermute | solution.py:276
  26.7 4.9 %collective-permute-start.6 = (bf16[384,128]{1,0:T(8,128)(2,1)S(1)}, bf16[384,128]{1,0:T(8,128)(2,1)S(1)}, u32[]{:S(2)}, u32[]{:S(2)}) collective-permute-start(bf16[384,128]{1,0:T(8,128)(2,1)S(1)} %get-tuple-element.53), channel_id=1, source_target_pairs={{0,4},{4,0},{8,12},{12,8},{16,20},{20,16},{24,28},{28,24},{1,5},{5... | collective-permute-start | bytes 294920 | tf_op jit(solution)/shard_map/ppermute | solution.py:276
  26.9 5.6 %collective-permute-start.7 = (bf16[384,128]{1,0:T(8,128)(2,1)S(1)}, bf16[384,128]{1,0:T(8,128)(2,1)S(1)}, u32[]{:S(2)}, u32[]{:S(2)}) collective-permute-start(bf16[384,128]{1,0:T(8,128)(2,1)S(1)} %get-tuple-element.54), channel_id=1, source_target_pairs={{0,8},{4,12},{8,0},{12,4},{16,24},{20,28},{24,16},{28,20},{1,9},{5... | collective-permute-start | bytes 294920 | tf_op jit(solution)/shard_map/ppermute | solution.py:276
  28.0 6.8 %collective-permute-start.8 = (bf16[384,128]{1,0:T(8,128)(2,1)S(1)}, bf16[384,128]{1,0:T(8,128)(2,1)S(1)}, u32[]{:S(2)}, u32[]{:S(2)}) collective-permute-start(bf16[384,128]{1,0:T(8,128)(2,1)S(1)} %get-tuple-element.55), channel_id=1, source_target_pairs={{0,12},{4,8},{8,4},{12,0},{16,28},{20,24},{24,20},{28,16},{1,13},{... | collective-permute-start | bytes 294920 | tf_op jit(solution)/shard_map/ppermute | solution.py:276
  34.9 7.1 %collective-permute-start.10 = (bf16[256,128]{1,0:T(8,128)(2,1)S(1)}, bf16[256,128]{1,0:T(8,128)(2,1)S(1)}, u32[]{:S(2)}, u32[]{:S(2)}) collective-permute-start(bf16[256,128]{1,0:T(8,128)(2,1)S(1)} %get-tuple-element.61.own_ref), channel_id=1, source_target_pairs={{0,16},{4,20},{8,24},{12,28},{16,0},{20,4},{24,8},{28,12},{1,17},{... | collective-permute-start | bytes 196616 | tf_op jit(solution)/shard_map/ppermute | solution.py:276
  35.4 10.2 %collective-permute-start.9 = (bf16[4,64,128]{2,1,0:T(8,128)(2,1)S(1)}, bf16[4,64,128]{2,1,0:T(8,128)(2,1)S(1)}, u32[]{:S(2)}, u32[]{:S(2)}) collective-permute-start(bf16[4,64,128]{2,1,0:T(8,128)(2,1)S(1)} %get-tuple-element.59), channel_id=1, source_target_pairs={{0,16},{4,20},{8,24},{12,28},{16,0},{20,4},{24,8},{28,12},{1,17},{... | collective-permute-start | bytes 196616 | tf_op jit(solution)/shard_map/ppermute | solution.py:276
  42.0 5.2 %collective-permute-start.13 = (bf16[256,128]{1,0:T(8,128)(2,1)S(1)}, bf16[256,128]{1,0:T(8,128)(2,1)S(1)}, u32[]{:S(2)}, u32[]{:S(2)}) collective-permute-start(bf16[256,128]{1,0:T(8,128)(2,1)S(1)} %shard_map.180.refs_0_), channel_id=1, source_target_pairs={{0,12},{4,8},{8,4},{12,0},{16,28},{20,24},{24,20},{28,16},{1,13},{... | collective-permute-start | bytes 196616 | tf_op jit(solution)/shard_map/ppermute | solution.py:276
  42.1 5.2 %collective-permute-start.12 = (bf16[256,128]{1,0:T(8,128)(2,1)S(1)}, bf16[256,128]{1,0:T(8,128)(2,1)S(1)}, u32[]{:S(2)}, u32[]{:S(2)}) collective-permute-start(bf16[256,128]{1,0:T(8,128)(2,1)S(1)} %shard_map.180.refs_0_), channel_id=1, source_target_pairs={{0,8},{4,12},{8,0},{12,4},{16,24},{20,28},{24,16},{28,20},{1,9},{5... | collective-permute-start | bytes 196616 | tf_op jit(solution)/shard_map/ppermute | solution.py:276
  44.3 4.3 %collective-permute-start.11 = (bf16[256,128]{1,0:T(8,128)(2,1)S(1)}, bf16[256,128]{1,0:T(8,128)(2,1)S(1)}, u32[]{:S(2)}, u32[]{:S(2)}) collective-permute-start(bf16[256,128]{1,0:T(8,128)(2,1)S(1)} %shard_map.180.refs_0_), channel_id=1, source_target_pairs={{0,4},{4,0},{8,12},{12,8},{16,20},{20,16},{24,28},{28,24},{1,5},{5... | collective-permute-start | bytes 196616 | tf_op jit(solution)/shard_map/ppermute | solution.py:276

commit v9 on v8

--- a/solution.py
+++ b/solution.py
@@ -139,9 +139,9 @@
 
 def dense_kernel(slots, hub_here, feats, width, count, me_ref, side_ref, seat_ref, x_ref, ws_ref, wn_ref, turned_ref, *refs):
     pack_refs, n_refs = refs[:feats], refs[feats : 2 * feats]
-    out_ref, back_ref = refs[2 * feats : 2 * feats + 2]
-    send_refs = refs[2 * feats + 2 : 2 * feats + 2 + count]
-    pre_ref, cot_ref, bias_ref, hold_ref = refs[2 * feats + 2 + count :]
+    out_ref, back_ref, mirror_ref = refs[2 * feats : 2 * feats + 3]
+    send_refs = refs[2 * feats + 3 : 2 * feats + 3 + count]
+    pre_ref, cot_ref, bias_ref, hold_ref, turn_ref = refs[2 * feats + 3 + count :]
     send_ref = send_refs[0] if count == 1 else hold_ref
     rows, cols = x_ref.shape
     depth, full = ws_ref.shape
@@ -149,7 +149,7 @@
     half, height = send_ref.shape[:2]
     me = me_ref[0]
     base = 2 * blocks * depth
-    pre = jnp.zeros((rows, full), F32)
+    left, right = [], []
     for d, pack in enumerate(pack_refs):
         owner = me ^ d
         cut = pl.ds(pl.multiple_of(owner * cols, cols), cols)
@@ -157,9 +157,9 @@
         bias_ref[:, cut] = pack[base + 2 * rows : base + 2 * rows + 16, :]
         w_s = jnp.concatenate([pack[j * depth : (j + 1) * depth, :] for j in range(blocks)], axis=1)
         w_n = jnp.concatenate([pack[(blocks + j) * depth : (blocks + j + 1) * depth, :] for j in range(blocks)], axis=1)
-        left = jnp.concatenate([pack[base : base + rows, :], n_refs[d][...]], axis=1)
-        right = jnp.concatenate([w_s, w_n], axis=0)
-        pre = pre + jnp.dot(left, right, preferred_element_type=F32)
+        left += [pack[base : base + rows, :], n_refs[d][...]]
+        right += [w_s, w_n]
+    pre = jnp.dot(jnp.concatenate(left, axis=1), jnp.concatenate(right, axis=0), preferred_element_type=F32)
     pre = pre + bias_ref[0:1, :].astype(F32)
     pre_ref[...] = pre
     sig = jax.nn.sigmoid(pre)
@@ -176,22 +176,24 @@
     high = sums.astype(BF).astype(F32)
     line = lax.broadcasted_iota(jnp.int32, (half * width, cols), 0) % width
     here = side_ref[0] * half
-    for at, start in ((0, here), (width, half - here)):
+    for target, start in ((send_ref, here), (turn_ref, half - here)):
         cut = pl.ds(pl.multiple_of(rows + start * width, 128), half * width)
         away = jnp.dot(turned_ref[cut, :], neigh_grad, preferred_element_type=F32)
         away = jnp.where(line == slots + hub_here, high, away)
         away = jnp.where(line == slots + hub_here + 1, sums - high, away)
-        send_ref[:, at : at + width, :] = away.astype(BF).reshape(half, width, cols)
+        target[:, :width, :] = away.astype(BF).reshape(half, width, cols)
+    for k in range(half):
+        mirror_ref[k] = turn_ref[seat_ref[0] ^ k if count > 1 else k]
     pair = jnp.concatenate([x_ref[...], n_refs[0][...]], axis=1)
     weights = lax.dot_general(pair, grad, (((0,), (0,)), ((), ())), preferred_element_type=F32).astype(BF)
-    share = height - 2 * width
+    share = height - width
     step = min(share, depth)
     for j in range(blocks):
         for kind in range(2):
             block = weights[kind * depth : (kind + 1) * depth, j * cols : (j + 1) * cols]
             for part in range(depth // step):
                 at = (j * 2 + kind) * depth + part * step
-                low = 2 * width + at % share
+                low = width + at % share
                 send_ref[at // share, low : low + step, :] = block[part * step : (part + 1) * step]
     if count > 1:
         for k, ref in enumerate(send_refs):
@@ -205,13 +207,17 @@
 
 
 def sum_kernel(width, seat_ref, *refs):
-    got_refs, (sum_ref, near_ref, relay_ref) = refs[:-3], refs[-3:]
+    got_refs, (sum_ref, near_ref) = refs[:-2], refs[-2:]
     total = jnp.zeros(sum_ref.shape, F32)
     for j, got_ref in seated(got_refs, seat_ref[0]):
-        total = total + got_ref[2 * width :, :].astype(F32)
+        total = total + got_ref[width:, :].astype(F32)
         near_ref[j] = got_ref[:width, :]
-        relay_ref[j] = got_ref[width : 2 * width, :]
     sum_ref[...] = total.astype(BF)
+
+
+def deal_kernel(got_ref, *out_refs):
+    for k, ref in enumerate(out_refs):
+        ref[...] = got_ref[k]
 
 
 def total_kernel(own_ref, other_ref, part_ref):
@@ -237,9 +243,12 @@
     bias_ref[...] = bias
 
 
-def grad_kernel(scale, slots, hub_here, side_ref, back_ref, near_ref, mark_ref, got_ref, grad_ref, bias_ref):
-    half = got_ref.shape[0]
-    added, bias = near_rows(slots, hub_here, half - side_ref[0] * half, mark_ref, got_ref)
+def grad_kernel(scale, slots, hub_here, side_ref, seat_ref, back_ref, near_ref, mark_ref, *refs):
+    got_refs, (grad_ref, bias_ref, hold_ref) = refs[:-3], refs[-3:]
+    half = hold_ref.shape[0]
+    for j, got_ref in seated(got_refs, seat_ref[0]):
+        hold_ref[j] = got_ref[...]
+    added, bias = near_rows(slots, hub_here, half - side_ref[0] * half, mark_ref, hold_ref)
     grad_ref[...] = (back_ref[...] + added).astype(BF)
     bias_ref[...] = (near_ref[...] + bias) * scale
 
@@ -368,35 +377,49 @@
     far_neigh = partner(neigh, "feat", 2)
     every = [neigh, partner(neigh, "feat", 1), far_neigh, partner(far_neigh, "feat", 1)]
 
-    height = 2 * width + share
-    output, back, *returned = pl.pallas_call(
+    height = width + share
+    output, back, mirror, *returned = pl.pallas_call(
         functools.partial(dense_kernel, slots, hub_here, feats, width, count),
         out_shape=(
             shape((rows, cols), BF),
             shape((rows, cols), F32),
+            shape((half, width, cols), BF),
             *([shape((height, cols), BF)] * half if direct else [shape((half, height, cols), BF)]),
         ),
         in_specs=[SMEM] * 3 + [VMEM] * (4 + 2 * feats),
-        out_specs=(VMEM,) * (2 + count),
+        out_specs=(VMEM,) * (3 + count),
         scratch_shapes=[
             pltpu.VMEM((rows, full), F32),
             pltpu.VMEM((rows, full), BF),
             pltpu.VMEM((16, full), BF),
             pltpu.VMEM((half, height, cols) if direct else (1, 16, cols), BF),
+            pltpu.VMEM((half, width, cols), BF),
         ],
         compiler_params=PARAMS,
     )(me, side, seat, features, w_self, w_neigh, turned, pack, near, far, last, *every)
 
     arrived = swap(returned) if direct else [exchange(returned[0], halves)]
-    half_sum, near_ghosts, relay = pl.pallas_call(
+    mirror = partner(mirror, "dom", half)
+    half_sum, near_ghosts = pl.pallas_call(
         functools.partial(sum_kernel, width),
-        out_shape=(shape((share, cols), BF), shape((half, width, cols), BF), shape((half, width, cols), BF)),
+        out_shape=(shape((share, cols), BF), shape((half, width, cols), BF)),
         in_specs=[SMEM] + [VMEM] * count,
-        out_specs=(VMEM,) * 3,
+        out_specs=(VMEM,) * 2,
         compiler_params=PARAMS,
     )(seat, *arrived)
     other_sum = partner(half_sum, "dom", half)
-    crossed = partner(relay, "dom", half)
+    if direct:
+        crossed = swap(
+            pl.pallas_call(
+                deal_kernel,
+                out_shape=(shape((width, cols), BF),) * half,
+                in_specs=[VMEM],
+                out_specs=(VMEM,) * half,
+                compiler_params=PARAMS,
+            )(mirror)
+        )
+    else:
+        crossed = [exchange(mirror, halves)]
     back, near_bias = pl.pallas_call(
         functools.partial(near_kernel, slots, hub_here),
         out_shape=(shape((rows, cols), F32), shape((1, cols), F32)),
@@ -416,11 +439,12 @@
     grad_features, grad_bias = pl.pallas_call(
         functools.partial(grad_kernel, scale, slots, hub_here),
         out_shape=(shape((rows, cols), BF), shape((1, cols), F32)),
-        in_specs=[SMEM] + [VMEM] * 4,
+        in_specs=[SMEM] * 2 + [VMEM] * (3 + count),
         out_specs=(VMEM,) * 2,
+        scratch_shapes=[pltpu.VMEM((half, width, cols), BF)],
         compiler_params=PARAMS,
         cost_estimate=pl.CostEstimate(flops=2 * 10**9, bytes_accessed=10**6, transcendentals=0),
-    )(side, back, near_bias, mark, crossed)
+    )(side, seat, back, near_bias, mark, *crossed)
     grad_self, grad_neigh = pl.pallas_call(
         functools.partial(spread_kernel, scale),
         out_shape=(shape((depth, full), F32), shape((depth, full), F32)),

time: 49.8 us -> 47.9 us (0.962)
  waiting for transfers between devices: 22.1 us -> 19.2 us
  starting transfers between devices: 19.7 us -> 20.7 us
    ppermute x14 -> x17, waiting for transfers between devices: 15.8 us -> 12.9 us  [partner(): lax.ppermute(block, axis, [(i, i ^ k) for i in range(lax.axis_size(axis))])]
    ppermute x14 -> x17, starting transfers between devices: 13.9 us -> 14.9 us  [partner(): lax.ppermute(block, axis, [(i, i ^ k) for i in range(lax.axis_size(axis))])]
  transfers between devices with their start and end apart: 15 -> 18, of which waited for: 9 -> 10; matrix products, arithmetic and copies ran while one was open for 0% -> 0% of each run, Pallas kernels for 3% -> 4%
where the time goes in v9:
time: 47.9 us; the launch traced here: 47.6 us
  starting transfers between devices  20.7 us (43%)
  waiting for transfers between devices  19.2 us (40%)
  Pallas kernels  6.31 us (13%)
  between operations  1.38 us (3%)
    ppermute x17, starting transfers between devices, partner(): lax.ppermute(block, axis, [(i, i ^ k) for i in range(lax.axis_size(axis))])  14.9 us
    ppermute x17, waiting for transfers between devices, partner(): lax.ppermute(block, axis, [(i, i ^ k) for i in range(lax.axis_size(axis))])  12.9 us
    all_to_all x1, waiting for transfers between devices, exchange(): lax.all_to_all(blocks, 'dom', split_axis=0, concat_axis=0, axis_index_gro...  6.27 us
    all_to_all x1, starting transfers between devices, exchange(): lax.all_to_all(blocks, 'dom', split_axis=0, concat_axis=0, axis_index_gro...  5.83 us
    pallas_call x1, Pallas kernels, on_device(): pl.pallas_call(functools.partial(send_kernel, width), out_shape=(shape((p...  2.23 us
    pallas_call x1, Pallas kernels, on_device(): pl.pallas_call(functools.partial(dense_kernel, slots, hub_here, feats, wi...  1.53 us
  transfers between devices with their start and end apart: 18, of which 10 were waited for; matrix products, arithmetic and copies ran while one was open for 0% of the time, Pallas kernels for 4%

profile of v9, /device:TPU:0, one launch (start us, length us, event | category | flops | bytes accessed | tf_op | source)
XLA Modules:
  0.0 47.6 jit_solution(6629490335178329912)
XLA Ops:
  0.6 2.2 %shard_map.173 = (bf16[8,64,128]{2,1,0:T(8,128)(2,1)}, bf16[1552,128]{1,0:T(8,128)(2,1)S(1)}, s32[1,8,48]{2,1,0:T(8,128)S(1)}, s32[1,2]{1,0:T(1,128)S(1)}, s32[1...) custom-call(bf16[256,128]{1,0:T(8,128)(2,1)} %x_ref.5, ...), custom_call_target="tpu_custom_call" | custom-call | tf_op jit(solution)/shard_map/pallas_call | solution.py:337
  2.9 3.0 %collective-permute-start.1 = (bf16[1552,128]{1,0:T(8,128)(2,1)S(1)}, bf16[1552,128]{1,0:T(8,128)(2,1)S(1)}, u32[]{:S(2)}, u32[]{:S(2)}) collective-permute-start(bf16[1552,128]{1,0:T(8,128)(2,1)S(1)} %get-tuple-element.48.refs_0_), channel_id=1, source_target_pairs={{0,2},{1,3},{2,0},{3,1},{4,6},{5,7},{6,4},{7,5},{8,10},{9,11},{10,... | collective-permute-start | bytes 1191944 | tf_op jit(solution)/shard_map/ppermute | solution.py:285
  5.9 5.8 %all-to-all-start = ((bf16[8,64,128]{2,1,0:T(8,128)(2,1)}), bf16[8,64,128]{2,1,0:T(8,128)(2,1)S(1)}, u32[]{:S(2)}, u32[]{:S(2)}) async-start(bf16[8,64,128]{2,1,0:T(8,128)(2,1)} %get-tuple-element.50), calls=%async_computation | async-start | bytes 262144 | tf_op jit(solution)/shard_map/all_to_all | solution.py:289
  12.4 0.4 shard_map.174
  12.8 6.3 %all-to-all-done.got_ref = bf16[8,64,128]{2,1,0:T(8,128)(2,1)S(1)} async-done(((bf16[8,64,128]{2,1,0:T(8,128)(2,1)}), bf16[8,64,128]{2,1,0:T(8,128)(2,1)S(1)}, u32[]{:S(2)}, u32[]{:S(2)}) %all-to-all-start) | async-done | bytes 131104 | tf_op jit(solution)/shard_map/all_to_all | solution.py:289
  19.1 0.3 shard_map.175
  19.4 0.6 %collective-permute-start.4 = (bf16[256,128]{1,0:T(8,128)(2,1)S(1)}, bf16[256,128]{1,0:T(8,128)(2,1)S(1)}, u32[]{:S(2)}, u32[]{:S(2)}) collective-permute-start(bf16[256,128]{1,0:T(8,128)(2,1)S(1)} %get-tuple-element.52.refs_4_), channel_id=1, source_target_pairs={{0,2},{1,3},{2,0},{3,1},{4,6},{5,7},{6,4},{7,5},{8,10},{9,11},{10,... | collective-permute-start | bytes 196616 | tf_op jit(solution)/shard_map/ppermute | solution.py:285
  20.0 0.2 collective-permute-start.3
  20.2 3.7 %collective-permute-done.4.refs_6_ = bf16[256,128]{1,0:T(8,128)(2,1)S(1)} collective-permute-done((bf16[256,128]{1,0:T(8,128)(2,1)S(1)}, bf16[256,128]{1,0:T(8,128)(2,1)S(1)}, u32[]{:S(2)}, u32[]{:S(2)}) %collective-permute-start.4) | collective-permute-done | bytes 65568 | tf_op jit(solution)/shard_map/ppermute | solution.py:285
  23.9 1.2 %collective-permute-done.5.refs_7_ = bf16[256,128]{1,0:T(8,128)(2,1)S(1)} collective-permute-done((bf16[256,128]{1,0:T(8,128)(2,1)S(1)}, bf16[256,128]{1,0:T(8,128)(2,1)S(1)}, u32[]{:S(2)}, u32[]{:S(2)}) %collective-permute-start.5) | collective-permute-done | bytes 65568 | tf_op jit(solution)/shard_map/ppermute | solution.py:285
  25.2 1.5 %shard_map.176 = (bf16[256,128]{1,0:T(8,128)(2,1)}, f32[256,128]{1,0:T(8,128)S(1)}, bf16[4,64,128]{2,1,0:T(8,128)(2,1)S(1)}, bf16[320,128]{1,0:T(8,128)(2,1)S(1)...) custom-call(s32[1]{0:T(128)} %bitcast.me_ref, s32[1]{0:T(128)} %bitcast.1.side_ref, ...), custom_call_target="tpu_custom_call" | custom-call | tf_op jit(solution)/shard_map/pallas_call | solution.py:381
  26.7 0.2 collective-permute-start.6
  26.9 1.1 %collective-permute-start.7 = (bf16[320,128]{1,0:T(8,128)(2,1)S(1)}, bf16[320,128]{1,0:T(8,128)(2,1)S(1)}, u32[]{:S(2)}, u32[]{:S(2)}) collective-permute-start(bf16[320,128]{1,0:T(8,128)(2,1)S(1)} %get-tuple-element.58), channel_id=1, source_target_pairs={{0,8},{4,12},{8,0},{12,4},{16,24},{20,28},{24,16},{28,20},{1,9},{5... | collective-permute-start | bytes 245768 | tf_op jit(solution)/shard_map/ppermute | solution.py:285
  28.0 2.2 %collective-permute-start.8 = (bf16[320,128]{1,0:T(8,128)(2,1)S(1)}, bf16[320,128]{1,0:T(8,128)(2,1)S(1)}, u32[]{:S(2)}, u32[]{:S(2)}) collective-permute-start(bf16[320,128]{1,0:T(8,128)(2,1)S(1)} %get-tuple-element.59), channel_id=1, source_target_pairs={{0,12},{4,8},{8,4},{12,0},{16,28},{20,24},{24,20},{28,16},{1,13},{... | collective-permute-start | bytes 245768 | tf_op jit(solution)/shard_map/ppermute | solution.py:285
  30.2 0.4 collective-permute-start.9
  30.6 0.6 %collective-permute-done.6.refs_1_ = bf16[320,128]{1,0:T(8,128)(2,1)S(1)} collective-permute-done((bf16[320,128]{1,0:T(8,128)(2,1)S(1)}, bf16[320,128]{1,0:T(8,128)(2,1)S(1)}, u32[]{:S(2)}, u32[]{:S(2)}) %collective-permute-start.6) | collective-permute-done | bytes 81952 | tf_op jit(solution)/shard_map/ppermute | solution.py:285
  31.2 0.9 %collective-permute-done.7.refs_2_ = bf16[320,128]{1,0:T(8,128)(2,1)S(1)} collective-permute-done((bf16[320,128]{1,0:T(8,128)(2,1)S(1)}, bf16[320,128]{1,0:T(8,128)(2,1)S(1)}, u32[]{:S(2)}, u32[]{:S(2)}) %collective-permute-start.7) | collective-permute-done | bytes 81952 | tf_op jit(solution)/shard_map/ppermute | solution.py:285
  32.1 3.2 %collective-permute-done.8.refs_3_ = bf16[320,128]{1,0:T(8,128)(2,1)S(1)} collective-permute-done((bf16[320,128]{1,0:T(8,128)(2,1)S(1)}, bf16[320,128]{1,0:T(8,128)(2,1)S(1)}, u32[]{:S(2)}, u32[]{:S(2)}) %collective-permute-start.8) | collective-permute-done | bytes 81952 | tf_op jit(solution)/shard_map/ppermute | solution.py:285
  35.4 0.1 collective-permute-start.13
  35.5 0.2 collective-permute-done.9.got_ref
  35.7 0.8 %collective-permute-start.10 = (bf16[64,128]{1,0:T(8,128)(2,1)S(1)}, bf16[64,128]{1,0:T(8,128)(2,1)S(1)}, u32[]{:S(2)}, u32[]{:S(2)}) collective-permute-start(bf16[64,128]{1,0:T(8,128)(2,1)S(1)} %get-tuple-element.65), channel_id=1, source_target_pairs={{0,4},{4,0},{8,12},{12,8},{16,20},{20,16},{24,28},{28,24},{1,5},{5... | collective-permute-start | bytes 49160 | tf_op jit(solution)/shard_map/ppermute | solution.py:285
  36.5 1.0 %collective-permute-start.11 = (bf16[64,128]{1,0:T(8,128)(2,1)S(1)}, bf16[64,128]{1,0:T(8,128)(2,1)S(1)}, u32[]{:S(2)}, u32[]{:S(2)}) collective-permute-start(bf16[64,128]{1,0:T(8,128)(2,1)S(1)} %get-tuple-element.66), channel_id=1, source_target_pairs={{0,8},{4,12},{8,0},{12,4},{16,24},{20,28},{24,16},{28,20},{1,9},{5... | collective-permute-start | bytes 49160 | tf_op jit(solution)/shard_map/ppermute | solution.py:285
  37.5 1.7 %collective-permute-start.12 = (bf16[64,128]{1,0:T(8,128)(2,1)S(1)}, bf16[64,128]{1,0:T(8,128)(2,1)S(1)}, u32[]{:S(2)}, u32[]{:S(2)}) collective-permute-start(bf16[64,128]{1,0:T(8,128)(2,1)S(1)} %get-tuple-element.67), channel_id=1, source_target_pairs={{0,12},{4,8},{8,4},{12,0},{16,28},{20,24},{24,20},{28,16},{1,13},{... | collective-permute-start | bytes 49160 | tf_op jit(solution)/shard_map/ppermute | solution.py:285
  39.1 0.2 shard_map.178
  39.3 1.5 %collective-permute-done.13.other_ref = bf16[256,128]{1,0:T(8,128)(2,1)S(1)} collective-permute-done((bf16[256,128]{1,0:T(8,128)(2,1)S(1)}, bf16[256,128]{1,0:T(8,128)(2,1)S(1)}, u32[]{:S(2)}, u32[]{:S(2)}) %collective-permute-start.13) | collective-permute-done | bytes 65568 | tf_op jit(solution)/shard_map/ppermute | solution.py:285
  40.8 0.5 %collective-permute-start.16 = (bf16[256,128]{1,0:T(8,128)(2,1)S(1)}, bf16[256,128]{1,0:T(8,128)(2,1)S(1)}, u32[]{:S(2)}, u32[]{:S(2)}) collective-permute-start(bf16[256,128]{1,0:T(8,128)(2,1)S(1)} %shard_map.181.refs_0_), channel_id=1, source_target_pairs={{0,12},{4,8},{8,4},{12,0},{16,28},{20,24},{24,20},{28,16},{1,13},{... | collective-permute-start | bytes 196616 | tf_op jit(solution)/shard_map/ppermute | solution.py:285
  41.4 0.3 collective-permute-start.15
  41.7 2.7 %collective-permute-start.14 = (bf16[256,128]{1,0:T(8,128)(2,1)S(1)}, bf16[256,128]{1,0:T(8,128)(2,1)S(1)}, u32[]{:S(2)}, u32[]{:S(2)}) collective-permute-start(bf16[256,128]{1,0:T(8,128)(2,1)S(1)} %shard_map.181.refs_0_), channel_id=1, source_target_pairs={{0,4},{4,0},{8,12},{12,8},{16,20},{20,16},{24,28},{28,24},{1,5},{5... | collective-permute-start | bytes 196616 | tf_op jit(solution)/shard_map/ppermute | solution.py:285
  44.4 0.8 %shard_map.180 = (bf16[256,128]{1,0:T(8,128)(2,1)}, f32[1,128]{1,0:T(1,128)}) custom-call(s32[1]{0:T(128)} %bitcast.1.side_ref, s32[1]{0:T(128)} %bitcast.2.seat_ref, f32[256,128]{1,0:T(8,128)S(1)} %get-tuple-element.61.back_ref, f32[1,128]{1,0:T(1,128)S(1)} %get-tuple-element.62.near_ref, bf16[256,512]{1,0:T(8,128)(2,1)S(1)} %get-tuple-element.55.mark_ref, ...), custom_call_target="tpu_custom_call" | custom-call | flops 2000000000 | bytes 1000000 | tf_op jit(solution)/shard_map/pallas_call | solution.py:439
  45.2 0.9 %collective-permute-done.16.refs_3_ = bf16[256,128]{1,0:T(8,128)(2,1)S(1)} collective-permute-done((bf16[256,128]{1,0:T(8,128)(2,1)S(1)}, bf16[256,128]{1,0:T(8,128)(2,1)S(1)}, u32[]{:S(2)}, u32[]{:S(2)}) %collective-permute-start.16) | collective-permute-done | bytes 65568 | tf_op jit(solution)/shard_map/ppermute | solution.py:285
  46.1 0.7 %collective-permute-done.14.refs_1_ = bf16[256,128]{1,0:T(8,128)(2,1)S(1)} collective-permute-done((bf16[256,128]{1,0:T(8,128)(2,1)S(1)}, bf16[256,128]{1,0:T(8,128)(2,1)S(1)}, u32[]{:S(2)}, u32[]{:S(2)}) %collective-permute-start.14) | collective-permute-done | bytes 65568 | tf_op jit(solution)/shard_map/ppermute | solution.py:285
  46.8 0.9 %shard_map.182 = (f32[128,512]{1,0:T(8,128)}, f32[128,512]{1,0:T(8,128)}) custom-call(s32[1]{0:T(128)} %bitcast.2.seat_ref, bf16[256,128]{1,0:T(8,128)(2,1)S(1)} %shard_map.181.refs_0_, bf16[256,128]{1,0:T(8,128)(2,1)S(1)} %collective-permute-done.14.refs_1_, bf16[256,128]{1,0:T(8,128)(2,1)S(1)} %collective-permute-done.15.refs_2_, ...), custom_call_target="tpu_custom_call" | custom-call | tf_op jit(solution)/shard_map/pallas_call | solution.py:448
  (20 shorter events, 0.2 us)
Async XLA Ops:
  2.9 16.2 %collective-permute-start.1 = (bf16[1552,128]{1,0:T(8,128)(2,1)S(1)}, bf16[1552,128]{1,0:T(8,128)(2,1)S(1)}, u32[]{:S(2)}, u32[]{:S(2)}) collective-permute-start(bf16[1552,128]{1,0:T(8,128)(2,1)S(1)} %get-tuple-element.48.refs_0_), channel_id=1, source_target_pairs={{0,2},{1,3},{2,0},{3,1},{4,6},{5,7},{6,4},{7,5},{8,10},{9,11},{10,... | collective-permute-start | bytes 1191944 | tf_op jit(solution)/shard_map/ppermute | solution.py:285
  5.9 13.2 %all-to-all-start = ((bf16[8,64,128]{2,1,0:T(8,128)(2,1)}), bf16[8,64,128]{2,1,0:T(8,128)(2,1)S(1)}, u32[]{:S(2)}, u32[]{:S(2)}) async-start(bf16[8,64,128]{2,1,0:T(8,128)(2,1)} %get-tuple-element.50), calls=%async_computation | async-start | bytes 262144 | tf_op jit(solution)/shard_map/all_to_all | solution.py:289
  11.7 12.2 %collective-permute-start = (bf16[1552,128]{1,0:T(8,128)(2,1)S(1)}, bf16[1552,128]{1,0:T(8,128)(2,1)S(1)}, u32[]{:S(2)}, u32[]{:S(2)}) collective-permute-start(bf16[1552,128]{1,0:T(8,128)(2,1)S(1)} %get-tuple-element.48.refs_0_), channel_id=1, source_target_pairs={{0,1},{1,0},{2,3},{3,2},{4,5},{5,4},{6,7},{7,6},{8,9},{9,8},{10,11... | collective-permute-start | bytes 1191944 | tf_op jit(solution)/shard_map/ppermute | solution.py:285
  12.4 6.7 %copy-start = (bf16[256,128]{1,0:T(8,128)(2,1)S(1)}, bf16[256,128]{1,0:T(8,128)(2,1)}, u32[]{:S(2)}) copy-start(bf16[256,128]{1,0:T(8,128)(2,1)} %x_ref.5) | copy-start | bytes 196612
  19.1 6.1 %copy-start.1 = (bf16[128,512]{1,0:T(8,128)(2,1)S(1)}, bf16[128,512]{1,0:T(8,128)(2,1)}, u32[]{:S(2)}) copy-start(bf16[128,512]{1,0:T(8,128)(2,1)} %ws_ref.3) | copy-start | bytes 393220
  19.1 6.1 %copy-start.2 = (bf16[128,512]{1,0:T(8,128)(2,1)S(1)}, bf16[128,512]{1,0:T(8,128)(2,1)}, u32[]{:S(2)}) copy-start(bf16[128,512]{1,0:T(8,128)(2,1)} %wn_ref.3) | copy-start | bytes 393220
  19.3 5.8 %collective-permute-start.2 = (bf16[1552,128]{1,0:T(8,128)(2,1)S(1)}, bf16[1552,128]{1,0:T(8,128)(2,1)S(1)}, u32[]{:S(2)}, u32[]{:S(2)}) collective-permute-start(bf16[1552,128]{1,0:T(8,128)(2,1)S(1)} %get-tuple-element.51.refs_2_), channel_id=1, source_target_pairs={{0,1},{1,0},{2,3},{3,2},{4,5},{5,4},{6,7},{7,6},{8,9},{9,8},{10,11... | collective-permute-start | bytes 1191944 | tf_op jit(solution)/shard_map/ppermute | solution.py:285
  19.4 4.5 %collective-permute-start.4 = (bf16[256,128]{1,0:T(8,128)(2,1)S(1)}, bf16[256,128]{1,0:T(8,128)(2,1)S(1)}, u32[]{:S(2)}, u32[]{:S(2)}) collective-permute-start(bf16[256,128]{1,0:T(8,128)(2,1)S(1)} %get-tuple-element.52.refs_4_), channel_id=1, source_target_pairs={{0,2},{1,3},{2,0},{3,1},{4,6},{5,7},{6,4},{7,5},{8,10},{9,11},{10,... | collective-permute-start | bytes 196616 | tf_op jit(solution)/shard_map/ppermute | solution.py:285
  20.0 3.9 %collective-permute-start.3 = (bf16[256,128]{1,0:T(8,128)(2,1)S(1)}, bf16[256,128]{1,0:T(8,128)(2,1)S(1)}, u32[]{:S(2)}, u32[]{:S(2)}) collective-permute-start(bf16[256,128]{1,0:T(8,128)(2,1)S(1)} %get-tuple-element.52.refs_4_), channel_id=1, source_target_pairs={{0,1},{1,0},{2,3},{3,2},{4,5},{5,4},{6,7},{7,6},{8,9},{9,8},{10,11... | collective-permute-start | bytes 196616 | tf_op jit(solution)/shard_map/ppermute | solution.py:285
  23.9 1.3 %collective-permute-start.5 = (bf16[256,128]{1,0:T(8,128)(2,1)S(1)}, bf16[256,128]{1,0:T(8,128)(2,1)S(1)}, u32[]{:S(2)}, u32[]{:S(2)}) collective-permute-start(bf16[256,128]{1,0:T(8,128)(2,1)S(1)} %collective-permute-done.4.refs_6_), channel_id=1, source_target_pairs={{0,1},{1,0},{2,3},{3,2},{4,5},{5,4},{6,7},{7,6},{8,9},{9,8},{10,11... | collective-permute-start | bytes 196616 | tf_op jit(solution)/shard_map/ppermute | solution.py:285
  26.7 4.5 %collective-permute-start.6 = (bf16[320,128]{1,0:T(8,128)(2,1)S(1)}, bf16[320,128]{1,0:T(8,128)(2,1)S(1)}, u32[]{:S(2)}, u32[]{:S(2)}) collective-permute-start(bf16[320,128]{1,0:T(8,128)(2,1)S(1)} %get-tuple-element.57), channel_id=1, source_target_pairs={{0,4},{4,0},{8,12},{12,8},{16,20},{20,16},{24,28},{28,24},{1,5},{5... | collective-permute-start | bytes 245768 | tf_op jit(solution)/shard_map/ppermute | solution.py:285
  26.9 5.2 %collective-permute-start.7 = (bf16[320,128]{1,0:T(8,128)(2,1)S(1)}, bf16[320,128]{1,0:T(8,128)(2,1)S(1)}, u32[]{:S(2)}, u32[]{:S(2)}) collective-permute-start(bf16[320,128]{1,0:T(8,128)(2,1)S(1)} %get-tuple-element.58), channel_id=1, source_target_pairs={{0,8},{4,12},{8,0},{12,4},{16,24},{20,28},{24,16},{28,20},{1,9},{5... | collective-permute-start | bytes 245768 | tf_op jit(solution)/shard_map/ppermute | solution.py:285
  28.0 7.3 %collective-permute-start.8 = (bf16[320,128]{1,0:T(8,128)(2,1)S(1)}, bf16[320,128]{1,0:T(8,128)(2,1)S(1)}, u32[]{:S(2)}, u32[]{:S(2)}) collective-permute-start(bf16[320,128]{1,0:T(8,128)(2,1)S(1)} %get-tuple-element.59), channel_id=1, source_target_pairs={{0,12},{4,8},{8,4},{12,0},{16,28},{20,24},{24,20},{28,16},{1,13},{... | collective-permute-start | bytes 245768 | tf_op jit(solution)/shard_map/ppermute | solution.py:285
  30.2 5.4 %collective-permute-start.9 = (bf16[4,64,128]{2,1,0:T(8,128)(2,1)S(1)}, bf16[4,64,128]{2,1,0:T(8,128)(2,1)S(1)}, u32[]{:S(2)}, u32[]{:S(2)}) collective-permute-start(bf16[4,64,128]{2,1,0:T(8,128)(2,1)S(1)} %get-tuple-element.63), channel_id=1, source_target_pairs={{0,16},{4,20},{8,24},{12,28},{16,0},{20,4},{24,8},{28,12},{1,17},{... | collective-permute-start | bytes 196616 | tf_op jit(solution)/shard_map/ppermute | solution.py:285
  35.4 5.4 %collective-permute-start.13 = (bf16[256,128]{1,0:T(8,128)(2,1)S(1)}, bf16[256,128]{1,0:T(8,128)(2,1)S(1)}, u32[]{:S(2)}, u32[]{:S(2)}) collective-permute-start(bf16[256,128]{1,0:T(8,128)(2,1)S(1)} %get-tuple-element.69.own_ref), channel_id=1, source_target_pairs={{0,16},{4,20},{8,24},{12,28},{16,0},{20,4},{24,8},{28,12},{1,17},{... | collective-permute-start | bytes 196616 | tf_op jit(solution)/shard_map/ppermute | solution.py:285
  35.7 6.1 %collective-permute-start.10 = (bf16[64,128]{1,0:T(8,128)(2,1)S(1)}, bf16[64,128]{1,0:T(8,128)(2,1)S(1)}, u32[]{:S(2)}, u32[]{:S(2)}) collective-permute-start(bf16[64,128]{1,0:T(8,128)(2,1)S(1)} %get-tuple-element.65), channel_id=1, source_target_pairs={{0,4},{4,0},{8,12},{12,8},{16,20},{20,16},{24,28},{28,24},{1,5},{5... | collective-permute-start | bytes 49160 | tf_op jit(solution)/shard_map/ppermute | solution.py:285
  36.5 7.9 %collective-permute-start.11 = (bf16[64,128]{1,0:T(8,128)(2,1)S(1)}, bf16[64,128]{1,0:T(8,128)(2,1)S(1)}, u32[]{:S(2)}, u32[]{:S(2)}) collective-permute-start(bf16[64,128]{1,0:T(8,128)(2,1)S(1)} %get-tuple-element.66), channel_id=1, source_target_pairs={{0,8},{4,12},{8,0},{12,4},{16,24},{20,28},{24,16},{28,20},{1,9},{5... | collective-permute-start | bytes 49160 | tf_op jit(solution)/shard_map/ppermute | solution.py:285
  37.5 6.9 %collective-permute-start.12 = (bf16[64,128]{1,0:T(8,128)(2,1)S(1)}, bf16[64,128]{1,0:T(8,128)(2,1)S(1)}, u32[]{:S(2)}, u32[]{:S(2)}) collective-permute-start(bf16[64,128]{1,0:T(8,128)(2,1)S(1)} %get-tuple-element.67), channel_id=1, source_target_pairs={{0,12},{4,8},{8,4},{12,0},{16,28},{20,24},{24,20},{28,16},{1,13},{... | collective-permute-start | bytes 49160 | tf_op jit(solution)/shard_map/ppermute | solution.py:285
  40.8 5.2 %collective-permute-start.16 = (bf16[256,128]{1,0:T(8,128)(2,1)S(1)}, bf16[256,128]{1,0:T(8,128)(2,1)S(1)}, u32[]{:S(2)}, u32[]{:S(2)}) collective-permute-start(bf16[256,128]{1,0:T(8,128)(2,1)S(1)} %shard_map.181.refs_0_), channel_id=1, source_target_pairs={{0,12},{4,8},{8,4},{12,0},{16,28},{20,24},{24,20},{28,16},{1,13},{... | collective-permute-start | bytes 196616 | tf_op jit(solution)/shard_map/ppermute | solution.py:285
  41.4 4.7 %collective-permute-start.15 = (bf16[256,128]{1,0:T(8,128)(2,1)S(1)}, bf16[256,128]{1,0:T(8,128)(2,1)S(1)}, u32[]{:S(2)}, u32[]{:S(2)}) collective-permute-start(bf16[256,128]{1,0:T(8,128)(2,1)S(1)} %shard_map.181.refs_0_), channel_id=1, source_target_pairs={{0,8},{4,12},{8,0},{12,4},{16,24},{20,28},{24,16},{28,20},{1,9},{5... | collective-permute-start | bytes 196616 | tf_op jit(solution)/shard_map/ppermute | solution.py:285
  41.7 5.1 %collective-permute-start.14 = (bf16[256,128]{1,0:T(8,128)(2,1)S(1)}, bf16[256,128]{1,0:T(8,128)(2,1)S(1)}, u32[]{:S(2)}, u32[]{:S(2)}) collective-permute-start(bf16[256,128]{1,0:T(8,128)(2,1)S(1)} %shard_map.181.refs_0_), channel_id=1, source_target_pairs={{0,4},{4,0},{8,12},{12,8},{16,20},{20,16},{24,28},{28,24},{1,5},{5... | collective-permute-start | bytes 196616 | tf_op jit(solution)/shard_map/ppermute | solution.py:285

commit v10 on v9

--- a/solution.py
+++ b/solution.py
@@ -141,12 +141,12 @@
     pack_refs, n_refs = refs[:feats], refs[feats : 2 * feats]
     out_ref, back_ref, mirror_ref = refs[2 * feats : 2 * feats + 3]
     send_refs = refs[2 * feats + 3 : 2 * feats + 3 + count]
-    pre_ref, cot_ref, bias_ref, hold_ref, turn_ref = refs[2 * feats + 3 + count :]
-    send_ref = send_refs[0] if count == 1 else hold_ref
+    pre_ref, cot_ref, bias_ref = refs[2 * feats + 3 + count :]
     rows, cols = x_ref.shape
     depth, full = ws_ref.shape
     blocks = full // cols
-    half, height = send_ref.shape[:2]
+    half = mirror_ref.shape[0]
+    height = send_refs[0].shape[-2]
     me = me_ref[0]
     base = 2 * blocks * depth
     left, right = [], []
@@ -174,19 +174,30 @@
     back_ref[...] = into[:, :depth] + jnp.dot(turned_ref[:rows, :], neigh_grad, preferred_element_type=F32)
     sums = jnp.sum(cot_ref[:, mine].astype(F32), axis=0, keepdims=True)
     high = sums.astype(BF).astype(F32)
-    line = lax.broadcasted_iota(jnp.int32, (half * width, cols), 0) % width
     here = side_ref[0] * half
-    for target, start in ((send_ref, here), (turn_ref, half - here)):
-        cut = pl.ds(pl.multiple_of(rows + start * width, 128), half * width)
+    share = height - width
+
+    def ghosts(start, peers):
+        line = lax.broadcasted_iota(jnp.int32, (peers * width, cols), 0) % width
+        cut = pl.ds(pl.multiple_of(rows + start * width, 16), peers * width)
         away = jnp.dot(turned_ref[cut, :], neigh_grad, preferred_element_type=F32)
         away = jnp.where(line == slots + hub_here, high, away)
         away = jnp.where(line == slots + hub_here + 1, sums - high, away)
-        target[:, :width, :] = away.astype(BF).reshape(half, width, cols)
-    for k in range(half):
-        mirror_ref[k] = turn_ref[seat_ref[0] ^ k if count > 1 else k]
-    pair = jnp.concatenate([x_ref[...], n_refs[0][...]], axis=1)
-    weights = lax.dot_general(pair, grad, (((0,), (0,)), ((), ())), preferred_element_type=F32).astype(BF)
-    share = height - width
+        return away.astype(BF)
+
+    pair = jnp.concatenate([x_ref[...], n_refs[0][...]], axis=1).T
+    if count > 1:
+        for k, ref in enumerate(send_refs):
+            peer = seat_ref[0] ^ k
+            ref[:width, :] = ghosts(here + peer, 1)
+            mirror_ref[k] = ghosts(half - here + peer, 1)
+            block = cot_ref[:, pl.ds(pl.multiple_of(peer * cols, cols), cols)]
+            ref[width:, :] = jnp.dot(pair, block, preferred_element_type=F32).astype(BF)
+        return
+    send_ref = send_refs[0]
+    send_ref[:, :width, :] = ghosts(here, half).reshape(half, width, cols)
+    mirror_ref[...] = ghosts(half - here, half).reshape(half, width, cols)
+    weights = jnp.dot(pair, grad, preferred_element_type=F32).astype(BF)
     step = min(share, depth)
     for j in range(blocks):
         for kind in range(2):
@@ -195,9 +206,6 @@
                 at = (j * 2 + kind) * depth + part * step
                 low = width + at % share
                 send_ref[at // share, low : low + step, :] = block[part * step : (part + 1) * step]
-    if count > 1:
-        for k, ref in enumerate(send_refs):
-            ref[...] = hold_ref[seat_ref[0] ^ k]
 
 
 def seated(refs, seat):
@@ -209,7 +217,7 @@
 def sum_kernel(width, seat_ref, *refs):
     got_refs, (sum_ref, near_ref) = refs[:-2], refs[-2:]
     total = jnp.zeros(sum_ref.shape, F32)
-    for j, got_ref in seated(got_refs, seat_ref[0]):
+    for j, got_ref in seated(got_refs[::-1], seat_ref[0]):
         total = total + got_ref[width:, :].astype(F32)
         near_ref[j] = got_ref[:width, :]
     sum_ref[...] = total.astype(BF)
@@ -392,13 +400,11 @@
             pltpu.VMEM((rows, full), F32),
             pltpu.VMEM((rows, full), BF),
             pltpu.VMEM((16, full), BF),
-            pltpu.VMEM((half, height, cols) if direct else (1, 16, cols), BF),
-            pltpu.VMEM((half, width, cols), BF),
         ],
         compiler_params=PARAMS,
     )(me, side, seat, features, w_self, w_neigh, turned, pack, near, far, last, *every)
 
-    arrived = swap(returned) if direct else [exchange(returned[0], halves)]
+    arrived = swap(returned)[::-1] if direct else [exchange(returned[0], halves)]
     mirror = partner(mirror, "dom", half)
     half_sum, near_ghosts = pl.pallas_call(
         functools.partial(sum_kernel, width),

time: 47.9 us -> 47.9 us (level)
  no operation moved by 1% of the time
where the time goes in v10:
time: 47.9 us; the launch traced here: 47.6 us
  starting transfers between devices  21 us (44%)
  waiting for transfers between devices  18.9 us (39%)
  Pallas kernels  6.3 us (13%)
  between operations  1.38 us (3%)
    ppermute x17, starting transfers between devices, partner(): lax.ppermute(block, axis, [(i, i ^ k) for i in range(lax.axis_size(axis))])  15.2 us
    ppermute x17, waiting for transfers between devices, partner(): lax.ppermute(block, axis, [(i, i ^ k) for i in range(lax.axis_size(axis))])  12.6 us
    all_to_all x1, waiting for transfers between devices, exchange(): lax.all_to_all(blocks, 'dom', split_axis=0, concat_axis=0, axis_index_gro...  6.27 us
    all_to_all x1, starting transfers between devices, exchange(): lax.all_to_all(blocks, 'dom', split_axis=0, concat_axis=0, axis_index_gro...  5.83 us
    pallas_call x1, Pallas kernels, on_device(): pl.pallas_call(functools.partial(send_kernel, width), out_shape=(shape((p...  2.23 us
    pallas_call x1, Pallas kernels, on_device(): pl.pallas_call(functools.partial(dense_kernel, slots, hub_here, feats, wi...  1.53 us
  transfers between devices with their start and end apart: 18, of which 10 were waited for; matrix products, arithmetic and copies ran while one was open for 0% of the time, Pallas kernels for 4%

profile of v10, /device:TPU:0, one launch (start us, length us, event | category | flops | bytes accessed | tf_op | source)
XLA Modules:
  0.0 47.6 jit_solution(12228644095603397141)
XLA Ops:
  0.6 2.2 %shard_map.173 = (bf16[8,64,128]{2,1,0:T(8,128)(2,1)}, bf16[1552,128]{1,0:T(8,128)(2,1)S(1)}, s32[1,8,48]{2,1,0:T(8,128)S(1)}, s32[1,2]{1,0:T(1,128)S(1)}, s32[1...) custom-call(bf16[256,128]{1,0:T(8,128)(2,1)} %x_ref.5, ...), custom_call_target="tpu_custom_call" | custom-call | tf_op jit(solution)/shard_map/pallas_call | solution.py:345
  2.9 3.0 %collective-permute-start.1 = (bf16[1552,128]{1,0:T(8,128)(2,1)S(1)}, bf16[1552,128]{1,0:T(8,128)(2,1)S(1)}, u32[]{:S(2)}, u32[]{:S(2)}) collective-permute-start(bf16[1552,128]{1,0:T(8,128)(2,1)S(1)} %get-tuple-element.48.refs_0_), channel_id=1, source_target_pairs={{0,2},{1,3},{2,0},{3,1},{4,6},{5,7},{6,4},{7,5},{8,10},{9,11},{10,... | collective-permute-start | bytes 1191944 | tf_op jit(solution)/shard_map/ppermute | solution.py:293
  5.9 5.8 %all-to-all-start = ((bf16[8,64,128]{2,1,0:T(8,128)(2,1)}), bf16[8,64,128]{2,1,0:T(8,128)(2,1)S(1)}, u32[]{:S(2)}, u32[]{:S(2)}) async-start(bf16[8,64,128]{2,1,0:T(8,128)(2,1)} %get-tuple-element.50), calls=%async_computation | async-start | bytes 262144 | tf_op jit(solution)/shard_map/all_to_all | solution.py:297
  12.4 0.4 shard_map.174
  12.8 6.3 %all-to-all-done.got_ref = bf16[8,64,128]{2,1,0:T(8,128)(2,1)S(1)} async-done(((bf16[8,64,128]{2,1,0:T(8,128)(2,1)}), bf16[8,64,128]{2,1,0:T(8,128)(2,1)S(1)}, u32[]{:S(2)}, u32[]{:S(2)}) %all-to-all-start) | async-done | bytes 131104 | tf_op jit(solution)/shard_map/all_to_all | solution.py:297
  19.1 0.3 shard_map.175
  19.4 0.6 %collective-permute-start.4 = (bf16[256,128]{1,0:T(8,128)(2,1)S(1)}, bf16[256,128]{1,0:T(8,128)(2,1)S(1)}, u32[]{:S(2)}, u32[]{:S(2)}) collective-permute-start(bf16[256,128]{1,0:T(8,128)(2,1)S(1)} %get-tuple-element.52.refs_4_), channel_id=1, source_target_pairs={{0,2},{1,3},{2,0},{3,1},{4,6},{5,7},{6,4},{7,5},{8,10},{9,11},{10,... | collective-permute-start | bytes 196616 | tf_op jit(solution)/shard_map/ppermute | solution.py:293
  20.0 0.2 collective-permute-start.3
  20.2 3.7 %collective-permute-done.4.refs_6_ = bf16[256,128]{1,0:T(8,128)(2,1)S(1)} collective-permute-done((bf16[256,128]{1,0:T(8,128)(2,1)S(1)}, bf16[256,128]{1,0:T(8,128)(2,1)S(1)}, u32[]{:S(2)}, u32[]{:S(2)}) %collective-permute-start.4) | collective-permute-done | bytes 65568 | tf_op jit(solution)/shard_map/ppermute | solution.py:293
  23.9 1.2 %collective-permute-done.5.refs_7_ = bf16[256,128]{1,0:T(8,128)(2,1)S(1)} collective-permute-done((bf16[256,128]{1,0:T(8,128)(2,1)S(1)}, bf16[256,128]{1,0:T(8,128)(2,1)S(1)}, u32[]{:S(2)}, u32[]{:S(2)}) %collective-permute-start.5) | collective-permute-done | bytes 65568 | tf_op jit(solution)/shard_map/ppermute | solution.py:293
  25.2 1.5 %shard_map.176 = (bf16[256,128]{1,0:T(8,128)(2,1)}, f32[256,128]{1,0:T(8,128)S(1)}, bf16[4,64,128]{2,1,0:T(8,128)(2,1)S(1)}, bf16[320,128]{1,0:T(8,128)(2,1)S(1)...) custom-call(s32[1]{0:T(128)} %bitcast.me_ref, s32[1]{0:T(128)} %bitcast.1.side_ref, ...), custom_call_target="tpu_custom_call" | custom-call | tf_op jit(solution)/shard_map/pallas_call | solution.py:389
  26.7 0.7 %collective-permute-start.6 = (bf16[320,128]{1,0:T(8,128)(2,1)S(1)}, bf16[320,128]{1,0:T(8,128)(2,1)S(1)}, u32[]{:S(2)}, u32[]{:S(2)}) collective-permute-start(bf16[320,128]{1,0:T(8,128)(2,1)S(1)} %get-tuple-element.56), channel_id=1, source_target_pairs={{0,12},{4,8},{8,4},{12,0},{16,28},{20,24},{24,20},{28,16},{1,13},{... | collective-permute-start | bytes 245768 | tf_op jit(solution)/shard_map/ppermute | solution.py:293
  27.5 0.9 %collective-permute-start.7 = (bf16[320,128]{1,0:T(8,128)(2,1)S(1)}, bf16[320,128]{1,0:T(8,128)(2,1)S(1)}, u32[]{:S(2)}, u32[]{:S(2)}) collective-permute-start(bf16[320,128]{1,0:T(8,128)(2,1)S(1)} %get-tuple-element.57), channel_id=1, source_target_pairs={{0,8},{4,12},{8,0},{12,4},{16,24},{20,28},{24,16},{28,20},{1,9},{5... | collective-permute-start | bytes 245768 | tf_op jit(solution)/shard_map/ppermute | solution.py:293
  28.4 1.8 %collective-permute-start.8 = (bf16[320,128]{1,0:T(8,128)(2,1)S(1)}, bf16[320,128]{1,0:T(8,128)(2,1)S(1)}, u32[]{:S(2)}, u32[]{:S(2)}) collective-permute-start(bf16[320,128]{1,0:T(8,128)(2,1)S(1)} %get-tuple-element.58), channel_id=1, source_target_pairs={{0,4},{4,0},{8,12},{12,8},{16,20},{20,16},{24,28},{28,24},{1,5},{5... | collective-permute-start | bytes 245768 | tf_op jit(solution)/shard_map/ppermute | solution.py:293
  30.2 0.4 collective-permute-start.9
  30.6 3.0 %collective-permute-done.6.refs_0_ = bf16[320,128]{1,0:T(8,128)(2,1)S(1)} collective-permute-done((bf16[320,128]{1,0:T(8,128)(2,1)S(1)}, bf16[320,128]{1,0:T(8,128)(2,1)S(1)}, u32[]{:S(2)}, u32[]{:S(2)}) %collective-permute-start.6) | collective-permute-done | bytes 81952 | tf_op jit(solution)/shard_map/ppermute | solution.py:293
  33.6 0.3 collective-permute-done.8.refs_2_
  33.9 0.4 collective-permute-start.13
  34.4 1.2 %collective-permute-done.9.got_ref = bf16[4,64,128]{2,1,0:T(8,128)(2,1)S(1)} collective-permute-done((bf16[4,64,128]{2,1,0:T(8,128)(2,1)S(1)}, bf16[4,64,128]{2,1,0:T(8,128)(2,1)S(1)}, u32[]{:S(2)}, u32[]{:S(2)}) %collective-permute-start.9) | collective-permute-done | bytes 65568 | tf_op jit(solution)/shard_map/ppermute | solution.py:293
  35.5 0.8 %collective-permute-start.10 = (bf16[64,128]{1,0:T(8,128)(2,1)S(1)}, bf16[64,128]{1,0:T(8,128)(2,1)S(1)}, u32[]{:S(2)}, u32[]{:S(2)}) collective-permute-start(bf16[64,128]{1,0:T(8,128)(2,1)S(1)} %get-tuple-element.65), channel_id=1, source_target_pairs={{0,4},{4,0},{8,12},{12,8},{16,20},{20,16},{24,28},{28,24},{1,5},{5... | collective-permute-start | bytes 49160 | tf_op jit(solution)/shard_map/ppermute | solution.py:293
  36.4 0.4 collective-permute-start.11
  36.8 2.2 %collective-permute-start.12 = (bf16[64,128]{1,0:T(8,128)(2,1)S(1)}, bf16[64,128]{1,0:T(8,128)(2,1)S(1)}, u32[]{:S(2)}, u32[]{:S(2)}) collective-permute-start(bf16[64,128]{1,0:T(8,128)(2,1)S(1)} %get-tuple-element.67), channel_id=1, source_target_pairs={{0,12},{4,8},{8,4},{12,0},{16,28},{20,24},{24,20},{28,16},{1,13},{... | collective-permute-start | bytes 49160 | tf_op jit(solution)/shard_map/ppermute | solution.py:293
  39.0 0.2 shard_map.178
  39.2 0.6 %collective-permute-done.13.other_ref = bf16[256,128]{1,0:T(8,128)(2,1)S(1)} collective-permute-done((bf16[256,128]{1,0:T(8,128)(2,1)S(1)}, bf16[256,128]{1,0:T(8,128)(2,1)S(1)}, u32[]{:S(2)}, u32[]{:S(2)}) %collective-permute-start.13) | collective-permute-done | bytes 65568 | tf_op jit(solution)/shard_map/ppermute | solution.py:293
  39.8 0.1 collective-permute-start.16
  40.0 2.5 %collective-permute-start.15 = (bf16[256,128]{1,0:T(8,128)(2,1)S(1)}, bf16[256,128]{1,0:T(8,128)(2,1)S(1)}, u32[]{:S(2)}, u32[]{:S(2)}) collective-permute-start(bf16[256,128]{1,0:T(8,128)(2,1)S(1)} %shard_map.181.refs_0_), channel_id=1, source_target_pairs={{0,8},{4,12},{8,0},{12,4},{16,24},{20,28},{24,16},{28,20},{1,9},{5... | collective-permute-start | bytes 196616 | tf_op jit(solution)/shard_map/ppermute | solution.py:293
  42.5 0.9 %collective-permute-start.14 = (bf16[256,128]{1,0:T(8,128)(2,1)S(1)}, bf16[256,128]{1,0:T(8,128)(2,1)S(1)}, u32[]{:S(2)}, u32[]{:S(2)}) collective-permute-start(bf16[256,128]{1,0:T(8,128)(2,1)S(1)} %shard_map.181.refs_0_), channel_id=1, source_target_pairs={{0,4},{4,0},{8,12},{12,8},{16,20},{20,16},{24,28},{28,24},{1,5},{5... | collective-permute-start | bytes 196616 | tf_op jit(solution)/shard_map/ppermute | solution.py:293
  43.4 0.8 %shard_map.180 = (bf16[256,128]{1,0:T(8,128)(2,1)}, f32[1,128]{1,0:T(1,128)}) custom-call(s32[1]{0:T(128)} %bitcast.1.side_ref, s32[1]{0:T(128)} %bitcast.2.seat_ref, f32[256,128]{1,0:T(8,128)S(1)} %get-tuple-element.61.back_ref, f32[1,128]{1,0:T(1,128)S(1)} %get-tuple-element.62.near_ref, bf16[256,512]{1,0:T(8,128)(2,1)S(1)} %get-tuple-element.55.mark_ref, ...), custom_call_target="tpu_custom_call" | custom-call | flops 2000000000 | bytes 1000000 | tf_op jit(solution)/shard_map/pallas_call | solution.py:445
  44.2 0.8 %collective-permute-done.16.refs_3_ = bf16[256,128]{1,0:T(8,128)(2,1)S(1)} collective-permute-done((bf16[256,128]{1,0:T(8,128)(2,1)S(1)}, bf16[256,128]{1,0:T(8,128)(2,1)S(1)}, u32[]{:S(2)}, u32[]{:S(2)}) %collective-permute-start.16) | collective-permute-done | bytes 65568 | tf_op jit(solution)/shard_map/ppermute | solution.py:293
  45.1 0.4 collective-permute-done.15.refs_2_
  45.5 1.3 %collective-permute-done.14.refs_1_ = bf16[256,128]{1,0:T(8,128)(2,1)S(1)} collective-permute-done((bf16[256,128]{1,0:T(8,128)(2,1)S(1)}, bf16[256,128]{1,0:T(8,128)(2,1)S(1)}, u32[]{:S(2)}, u32[]{:S(2)}) %collective-permute-start.14) | collective-permute-done | bytes 65568 | tf_op jit(solution)/shard_map/ppermute | solution.py:293
  46.8 0.9 %shard_map.182 = (f32[128,512]{1,0:T(8,128)}, f32[128,512]{1,0:T(8,128)}) custom-call(s32[1]{0:T(128)} %bitcast.2.seat_ref, bf16[256,128]{1,0:T(8,128)(2,1)S(1)} %shard_map.181.refs_0_, bf16[256,128]{1,0:T(8,128)(2,1)S(1)} %collective-permute-done.14.refs_1_, bf16[256,128]{1,0:T(8,128)(2,1)S(1)} %collective-permute-done.15.refs_2_, ...), custom_call_target="tpu_custom_call" | custom-call | tf_op jit(solution)/shard_map/pallas_call | solution.py:454
  (20 shorter events, 0.2 us)
Async XLA Ops:
  2.9 16.2 %collective-permute-start.1 = (bf16[1552,128]{1,0:T(8,128)(2,1)S(1)}, bf16[1552,128]{1,0:T(8,128)(2,1)S(1)}, u32[]{:S(2)}, u32[]{:S(2)}) collective-permute-start(bf16[1552,128]{1,0:T(8,128)(2,1)S(1)} %get-tuple-element.48.refs_0_), channel_id=1, source_target_pairs={{0,2},{1,3},{2,0},{3,1},{4,6},{5,7},{6,4},{7,5},{8,10},{9,11},{10,... | collective-permute-start | bytes 1191944 | tf_op jit(solution)/shard_map/ppermute | solution.py:293
  5.9 13.2 %all-to-all-start = ((bf16[8,64,128]{2,1,0:T(8,128)(2,1)}), bf16[8,64,128]{2,1,0:T(8,128)(2,1)S(1)}, u32[]{:S(2)}, u32[]{:S(2)}) async-start(bf16[8,64,128]{2,1,0:T(8,128)(2,1)} %get-tuple-element.50), calls=%async_computation | async-start | bytes 262144 | tf_op jit(solution)/shard_map/all_to_all | solution.py:297
  11.7 12.2 %collective-permute-start = (bf16[1552,128]{1,0:T(8,128)(2,1)S(1)}, bf16[1552,128]{1,0:T(8,128)(2,1)S(1)}, u32[]{:S(2)}, u32[]{:S(2)}) collective-permute-start(bf16[1552,128]{1,0:T(8,128)(2,1)S(1)} %get-tuple-element.48.refs_0_), channel_id=1, source_target_pairs={{0,1},{1,0},{2,3},{3,2},{4,5},{5,4},{6,7},{7,6},{8,9},{9,8},{10,11... | collective-permute-start | bytes 1191944 | tf_op jit(solution)/shard_map/ppermute | solution.py:293
  12.4 6.7 %copy-start = (bf16[256,128]{1,0:T(8,128)(2,1)S(1)}, bf16[256,128]{1,0:T(8,128)(2,1)}, u32[]{:S(2)}) copy-start(bf16[256,128]{1,0:T(8,128)(2,1)} %x_ref.5) | copy-start | bytes 196612
  19.1 6.1 %copy-start.1 = (bf16[128,512]{1,0:T(8,128)(2,1)S(1)}, bf16[128,512]{1,0:T(8,128)(2,1)}, u32[]{:S(2)}) copy-start(bf16[128,512]{1,0:T(8,128)(2,1)} %ws_ref.3) | copy-start | bytes 393220
  19.1 6.1 %copy-start.2 = (bf16[128,512]{1,0:T(8,128)(2,1)S(1)}, bf16[128,512]{1,0:T(8,128)(2,1)}, u32[]{:S(2)}) copy-start(bf16[128,512]{1,0:T(8,128)(2,1)} %wn_ref.3) | copy-start | bytes 393220
  19.3 5.8 %collective-permute-start.2 = (bf16[1552,128]{1,0:T(8,128)(2,1)S(1)}, bf16[1552,128]{1,0:T(8,128)(2,1)S(1)}, u32[]{:S(2)}, u32[]{:S(2)}) collective-permute-start(bf16[1552,128]{1,0:T(8,128)(2,1)S(1)} %get-tuple-element.51.refs_2_), channel_id=1, source_target_pairs={{0,1},{1,0},{2,3},{3,2},{4,5},{5,4},{6,7},{7,6},{8,9},{9,8},{10,11... | collective-permute-start | bytes 1191944 | tf_op jit(solution)/shard_map/ppermute | solution.py:293
  19.4 4.5 %collective-permute-start.4 = (bf16[256,128]{1,0:T(8,128)(2,1)S(1)}, bf16[256,128]{1,0:T(8,128)(2,1)S(1)}, u32[]{:S(2)}, u32[]{:S(2)}) collective-permute-start(bf16[256,128]{1,0:T(8,128)(2,1)S(1)} %get-tuple-element.52.refs_4_), channel_id=1, source_target_pairs={{0,2},{1,3},{2,0},{3,1},{4,6},{5,7},{6,4},{7,5},{8,10},{9,11},{10,... | collective-permute-start | bytes 196616 | tf_op jit(solution)/shard_map/ppermute | solution.py:293
  20.0 3.9 %collective-permute-start.3 = (bf16[256,128]{1,0:T(8,128)(2,1)S(1)}, bf16[256,128]{1,0:T(8,128)(2,1)S(1)}, u32[]{:S(2)}, u32[]{:S(2)}) collective-permute-start(bf16[256,128]{1,0:T(8,128)(2,1)S(1)} %get-tuple-element.52.refs_4_), channel_id=1, source_target_pairs={{0,1},{1,0},{2,3},{3,2},{4,5},{5,4},{6,7},{7,6},{8,9},{9,8},{10,11... | collective-permute-start | bytes 196616 | tf_op jit(solution)/shard_map/ppermute | solution.py:293
  23.9 1.3 %collective-permute-start.5 = (bf16[256,128]{1,0:T(8,128)(2,1)S(1)}, bf16[256,128]{1,0:T(8,128)(2,1)S(1)}, u32[]{:S(2)}, u32[]{:S(2)}) collective-permute-start(bf16[256,128]{1,0:T(8,128)(2,1)S(1)} %collective-permute-done.4.refs_6_), channel_id=1, source_target_pairs={{0,1},{1,0},{2,3},{3,2},{4,5},{5,4},{6,7},{7,6},{8,9},{9,8},{10,11... | collective-permute-start | bytes 196616 | tf_op jit(solution)/shard_map/ppermute | solution.py:293
  26.7 6.9 %collective-permute-start.6 = (bf16[320,128]{1,0:T(8,128)(2,1)S(1)}, bf16[320,128]{1,0:T(8,128)(2,1)S(1)}, u32[]{:S(2)}, u32[]{:S(2)}) collective-permute-start(bf16[320,128]{1,0:T(8,128)(2,1)S(1)} %get-tuple-element.56), channel_id=1, source_target_pairs={{0,12},{4,8},{8,4},{12,0},{16,28},{20,24},{24,20},{28,16},{1,13},{... | collective-permute-start | bytes 245768 | tf_op jit(solution)/shard_map/ppermute | solution.py:293
  27.5 6.1 %collective-permute-start.7 = (bf16[320,128]{1,0:T(8,128)(2,1)S(1)}, bf16[320,128]{1,0:T(8,128)(2,1)S(1)}, u32[]{:S(2)}, u32[]{:S(2)}) collective-permute-start(bf16[320,128]{1,0:T(8,128)(2,1)S(1)} %get-tuple-element.57), channel_id=1, source_target_pairs={{0,8},{4,12},{8,0},{12,4},{16,24},{20,28},{24,16},{28,20},{1,9},{5... | collective-permute-start | bytes 245768 | tf_op jit(solution)/shard_map/ppermute | solution.py:293
  28.4 5.5 %collective-permute-start.8 = (bf16[320,128]{1,0:T(8,128)(2,1)S(1)}, bf16[320,128]{1,0:T(8,128)(2,1)S(1)}, u32[]{:S(2)}, u32[]{:S(2)}) collective-permute-start(bf16[320,128]{1,0:T(8,128)(2,1)S(1)} %get-tuple-element.58), channel_id=1, source_target_pairs={{0,4},{4,0},{8,12},{12,8},{16,20},{20,16},{24,28},{28,24},{1,5},{5... | collective-permute-start | bytes 245768 | tf_op jit(solution)/shard_map/ppermute | solution.py:293
  30.2 5.3 %collective-permute-start.9 = (bf16[4,64,128]{2,1,0:T(8,128)(2,1)S(1)}, bf16[4,64,128]{2,1,0:T(8,128)(2,1)S(1)}, u32[]{:S(2)}, u32[]{:S(2)}) collective-permute-start(bf16[4,64,128]{2,1,0:T(8,128)(2,1)S(1)} %get-tuple-element.63), channel_id=1, source_target_pairs={{0,16},{4,20},{8,24},{12,28},{16,0},{20,4},{24,8},{28,12},{1,17},{... | collective-permute-start | bytes 196616 | tf_op jit(solution)/shard_map/ppermute | solution.py:293
  33.9 5.9 %collective-permute-start.13 = (bf16[256,128]{1,0:T(8,128)(2,1)S(1)}, bf16[256,128]{1,0:T(8,128)(2,1)S(1)}, u32[]{:S(2)}, u32[]{:S(2)}) collective-permute-start(bf16[256,128]{1,0:T(8,128)(2,1)S(1)} %get-tuple-element.69.own_ref), channel_id=1, source_target_pairs={{0,16},{4,20},{8,24},{12,28},{16,0},{20,4},{24,8},{28,12},{1,17},{... | collective-permute-start | bytes 196616 | tf_op jit(solution)/shard_map/ppermute | solution.py:293
  35.5 7.0 %collective-permute-start.10 = (bf16[64,128]{1,0:T(8,128)(2,1)S(1)}, bf16[64,128]{1,0:T(8,128)(2,1)S(1)}, u32[]{:S(2)}, u32[]{:S(2)}) collective-permute-start(bf16[64,128]{1,0:T(8,128)(2,1)S(1)} %get-tuple-element.65), channel_id=1, source_target_pairs={{0,4},{4,0},{8,12},{12,8},{16,20},{20,16},{24,28},{28,24},{1,5},{5... | collective-permute-start | bytes 49160 | tf_op jit(solution)/shard_map/ppermute | solution.py:293
  36.4 7.0 %collective-permute-start.11 = (bf16[64,128]{1,0:T(8,128)(2,1)S(1)}, bf16[64,128]{1,0:T(8,128)(2,1)S(1)}, u32[]{:S(2)}, u32[]{:S(2)}) collective-permute-start(bf16[64,128]{1,0:T(8,128)(2,1)S(1)} %get-tuple-element.66), channel_id=1, source_target_pairs={{0,8},{4,12},{8,0},{12,4},{16,24},{20,28},{24,16},{28,20},{1,9},{5... | collective-permute-start | bytes 49160 | tf_op jit(solution)/shard_map/ppermute | solution.py:293
  36.8 6.6 %collective-permute-start.12 = (bf16[64,128]{1,0:T(8,128)(2,1)S(1)}, bf16[64,128]{1,0:T(8,128)(2,1)S(1)}, u32[]{:S(2)}, u32[]{:S(2)}) collective-permute-start(bf16[64,128]{1,0:T(8,128)(2,1)S(1)} %get-tuple-element.67), channel_id=1, source_target_pairs={{0,12},{4,8},{8,4},{12,0},{16,28},{20,24},{24,20},{28,16},{1,13},{... | collective-permute-start | bytes 49160 | tf_op jit(solution)/shard_map/ppermute | solution.py:293
  39.8 5.2 %collective-permute-start.16 = (bf16[256,128]{1,0:T(8,128)(2,1)S(1)}, bf16[256,128]{1,0:T(8,128)(2,1)S(1)}, u32[]{:S(2)}, u32[]{:S(2)}) collective-permute-start(bf16[256,128]{1,0:T(8,128)(2,1)S(1)} %shard_map.181.refs_0_), channel_id=1, source_target_pairs={{0,12},{4,8},{8,4},{12,0},{16,28},{20,24},{24,20},{28,16},{1,13},{... | collective-permute-start | bytes 196616 | tf_op jit(solution)/shard_map/ppermute | solution.py:293
  40.0 5.5 %collective-permute-start.15 = (bf16[256,128]{1,0:T(8,128)(2,1)S(1)}, bf16[256,128]{1,0:T(8,128)(2,1)S(1)}, u32[]{:S(2)}, u32[]{:S(2)}) collective-permute-start(bf16[256,128]{1,0:T(8,128)(2,1)S(1)} %shard_map.181.refs_0_), channel_id=1, source_target_pairs={{0,8},{4,12},{8,0},{12,4},{16,24},{20,28},{24,16},{28,20},{1,9},{5... | collective-permute-start | bytes 196616 | tf_op jit(solution)/shard_map/ppermute | solution.py:293
  42.5 4.3 %collective-permute-start.14 = (bf16[256,128]{1,0:T(8,128)(2,1)S(1)}, bf16[256,128]{1,0:T(8,128)(2,1)S(1)}, u32[]{:S(2)}, u32[]{:S(2)}) collective-permute-start(bf16[256,128]{1,0:T(8,128)(2,1)S(1)} %shard_map.181.refs_0_), channel_id=1, source_target_pairs={{0,4},{4,0},{8,12},{12,8},{16,20},{20,16},{24,28},{28,24},{1,5},{5... | collective-permute-start | bytes 196616 | tf_op jit(solution)/shard_map/ppermute | solution.py:293

commit v11 on v10

--- a/solution.py
+++ b/solution.py
@@ -37,12 +37,16 @@
     return jnp.where(row == index, 1.0, 0.0).astype(BF)
 
 
-def source_rows(send, hubs, rows, width):
+def source_places(peers, slots, width):
+    lanes = peers * width
+    slot = lax.broadcasted_iota(jnp.int32, (lanes, slots), 0) % width
+    return jnp.where(slot == lax.broadcasted_iota(jnp.int32, (lanes, slots), 1), 1.0, 0.0).astype(BF)
+
+
+def source_rows(place, send, hubs, rows, width):
     peers, slots = send.shape
     hub_here = hubs.shape[1]
     lanes = peers * width
-    slot = lax.broadcasted_iota(jnp.int32, (lanes, slots), 0) % width
-    place = jnp.where(slot == lax.broadcasted_iota(jnp.int32, (lanes, slots), 1), 1.0, 0.0).astype(BF)
     wide = lax.dot_general(
         place, send.astype(F32).astype(BF), (((1,), (1,)), ((), ())), preferred_element_type=F32
     )
@@ -58,7 +62,7 @@
 
 def send_kernel(
     width, x_ref, cot_ref, ws_ref, wn_ref, bias_ref, send_ref, hub_ref, pos_ref, live_ref, tile_ref, dest_ref, gw_ref, hw_ref,
-    out_ref, pack_ref, send_v, hub_v, pos_v, live_v, tile_v, dest_v, gw_v, hw_v, bias_v, sems,
+    out_ref, pack_ref, send_v, hub_v, pos_v, live_v, tile_v, dest_v, gw_v, hw_v, bias_v, place_ref, sems,
 ):
     rows, cols = x_ref.shape
     depth, full = ws_ref.shape
@@ -82,9 +86,11 @@
     copies = [pltpu.make_async_copy(src, dst, sems.at[i]) for i, (src, dst) in enumerate(moves)]
     for copy in copies:
         copy.start()
+    peers, slots = send_v.shape[1:]
+    place_ref[...] = source_places(peers, slots, width)
     for copy in copies[:2]:
         copy.wait()
-    mark = source_rows(send_v[0], hub_v[...], rows, width)
+    mark = source_rows(place_ref[...], send_v[0], hub_v[...], rows, width)
     copies[2].wait()
     taken = jnp.dot(mark, pack_ref[base : base + rows, :], preferred_element_type=F32).astype(BF)
     out_ref[...] = taken.reshape(out_ref.shape)
@@ -149,27 +155,36 @@
     height = send_refs[0].shape[-2]
     me = me_ref[0]
     base = 2 * blocks * depth
-    left, right = [], []
+    left = []
     for d, pack in enumerate(pack_refs):
         owner = me ^ d
         cut = pl.ds(pl.multiple_of(owner * cols, cols), cols)
         cot_ref[:, cut] = pack[base + rows : base + 2 * rows, :]
         bias_ref[:, cut] = pack[base + 2 * rows : base + 2 * rows + 16, :]
-        w_s = jnp.concatenate([pack[j * depth : (j + 1) * depth, :] for j in range(blocks)], axis=1)
-        w_n = jnp.concatenate([pack[(blocks + j) * depth : (blocks + j + 1) * depth, :] for j in range(blocks)], axis=1)
         left += [pack[base : base + rows, :], n_refs[d][...]]
-        right += [w_s, w_n]
-    pre = jnp.dot(jnp.concatenate(left, axis=1), jnp.concatenate(right, axis=0), preferred_element_type=F32)
-    pre = pre + bias_ref[0:1, :].astype(F32)
-    pre_ref[...] = pre
-    sig = jax.nn.sigmoid(pre)
-    grad = (cot_ref[...].astype(F32) * sig * (1.0 + pre * (1.0 - sig))).astype(BF)
-    cot_ref[...] = grad
+    left = jnp.concatenate(left, axis=1)
+    both = jnp.concatenate([ws_ref[...], wn_ref[...]], axis=0)
+    into = jnp.zeros((rows, 2 * depth), F32)
+    span = 2
+    for j in range(0, blocks, span):
+        right = [
+            jnp.concatenate([pack[(kind * blocks + i) * depth : (kind * blocks + i + 1) * depth, :] for i in range(j, j + span)], axis=1)
+            for pack in pack_refs
+            for kind in range(2)
+        ]
+        cut = slice(j * cols, (j + span) * cols)
+        pre = jnp.dot(left, jnp.concatenate(right, axis=0), preferred_element_type=F32)
+        pre = pre + bias_ref[0:1, cut].astype(F32)
+        pre_ref[:, cut] = pre
+        sig = jax.nn.sigmoid(pre)
+        grad = (cot_ref[:, cut].astype(F32) * sig * (1.0 + pre * (1.0 - sig))).astype(BF)
+        cot_ref[:, cut] = grad
+        into = into + lax.dot_general(
+            grad, both[:, cut], (((1,), (1,)), ((), ())), preferred_element_type=F32
+        )
     mine = pl.ds(pl.multiple_of(me * cols, cols), cols)
     own = pre_ref[:, mine]
     out_ref[...] = (own * jax.nn.sigmoid(own)).astype(BF)
-    both = jnp.concatenate([ws_ref[...], wn_ref[...]], axis=0)
-    into = lax.dot_general(grad, both, (((1,), (1,)), ((), ())), preferred_element_type=F32)
     neigh_grad = into[:, depth:].astype(BF)
     back_ref[...] = into[:, :depth] + jnp.dot(turned_ref[:rows, :], neigh_grad, preferred_element_type=F32)
     sums = jnp.sum(cot_ref[:, mine].astype(F32), axis=0, keepdims=True)
@@ -197,7 +212,7 @@
     send_ref = send_refs[0]
     send_ref[:, :width, :] = ghosts(here, half).reshape(half, width, cols)
     mirror_ref[...] = ghosts(half - here, half).reshape(half, width, cols)
-    weights = jnp.dot(pair, grad, preferred_element_type=F32).astype(BF)
+    weights = jnp.dot(pair, cot_ref[...], preferred_element_type=F32).astype(BF)
     step = min(share, depth)
     for j in range(blocks):
         for kind in range(2):
@@ -262,20 +277,27 @@
 
 
 def spread_kernel(scale, seat_ref, *refs):
-    got_refs, (self_ref, neigh_ref) = refs[:-2], refs[-2:]
+    got_refs, (self_ref, neigh_ref, wide_ref, sems) = refs[:-4], refs[-4:]
     depth, full = self_ref.shape
     cols = got_refs[0].shape[-1]
+    blocks = full // cols
     if len(got_refs) > 1:
-        for j, ref in seated(got_refs, seat_ref[0]):
-            cut = pl.ds(pl.multiple_of(j * cols, cols), cols)
-            self_ref[:, cut] = ref[:depth, :].astype(F32) * scale
-            neigh_ref[:, cut] = ref[depth:, :].astype(F32) * scale
-        return
-    whole = got_refs[0][...].reshape(2 * (full // cols) * depth, cols).astype(F32) * scale
-    for j in range(full // cols):
-        at = 2 * j * depth
-        self_ref[:, j * cols : (j + 1) * cols] = whole[at : at + depth]
-        neigh_ref[:, j * cols : (j + 1) * cols] = whole[at + depth : at + 2 * depth]
+        parts = [(j, ref[...]) for j, ref in seated(got_refs, seat_ref[0])]
+    else:
+        whole = got_refs[0][...].reshape(2 * blocks * depth, cols)
+        parts = [(j, whole[2 * j * depth : 2 * (j + 1) * depth]) for j in range(blocks)]
+    copies = []
+    for at, (j, part) in enumerate(parts):
+        wide_ref[at] = part.astype(F32) * scale
+        cut = pl.ds(pl.multiple_of(j * cols, cols), cols)
+        for kind, out_ref in enumerate((self_ref, neigh_ref)):
+            copy = pltpu.make_async_copy(
+                wide_ref.at[at, kind * depth : (kind + 1) * depth, :], out_ref.at[:, cut], sems.at[2 * at + kind]
+            )
+            copy.start()
+            copies.append(copy)
+    for copy in copies:
+        copy.wait()
 
 
 VMEM = pl.BlockSpec(memory_space=pltpu.VMEM)
@@ -353,6 +375,7 @@
         out_specs=(VMEM,) * (2 + len(moved)),
         scratch_shapes=[
             pltpu.VMEM((1, cols), BF),
+            pltpu.VMEM((lanes, slots), BF),
             pltpu.SemaphoreType.DMA((11 + 2 * blocks,)),
         ],
         compiler_params=PARAMS,
@@ -455,7 +478,8 @@
         functools.partial(spread_kernel, scale),
         out_shape=(shape((depth, full), F32), shape((depth, full), F32)),
         in_specs=[SMEM] + [VMEM] * count,
-        out_specs=(VMEM,) * 2,
+        out_specs=(HBM,) * 2,
+        scratch_shapes=[pltpu.VMEM((blocks, 2 * depth, cols), F32), pltpu.SemaphoreType.DMA((2 * blocks,))],
         compiler_params=PARAMS,
     )(seat, *parts)
     return output, grad_features, grad_self, grad_neigh, grad_bias.reshape(cols)

time: 47.9 us -> 47.8 us (level)
  no operation moved by 1% of the time
where the time goes in v11:
time: 47.8 us; the launch traced here: 47.5 us
  starting transfers between devices  21 us (44%)
  waiting for transfers between devices  18.8 us (39%)
  Pallas kernels  6.3 us (13%)
  between operations  1.38 us (3%)
    ppermute x17, starting transfers between devices, partner(): lax.ppermute(block, axis, [(i, i ^ k) for i in range(lax.axis_size(axis))])  15.2 us
    ppermute x17, waiting for transfers between devices, partner(): lax.ppermute(block, axis, [(i, i ^ k) for i in range(lax.axis_size(axis))])  12.5 us
    all_to_all x1, waiting for transfers between devices, exchange(): lax.all_to_all(blocks, 'dom', split_axis=0, concat_axis=0, axis_index_gro...  6.27 us
    all_to_all x1, starting transfers between devices, exchange(): lax.all_to_all(blocks, 'dom', split_axis=0, concat_axis=0, axis_index_gro...  5.83 us
    pallas_call x1, Pallas kernels, on_device(): pl.pallas_call(functools.partial(send_kernel, width), out_shape=(shape((p...  2.22 us
    pallas_call x1, Pallas kernels, on_device(): pl.pallas_call(functools.partial(dense_kernel, slots, hub_here, feats, wi...  1.52 us
  transfers between devices with their start and end apart: 18, of which 10 were waited for; matrix products, arithmetic and copies ran while one was open for 0% of the time, Pallas kernels for 4%

profile of v11, /device:TPU:0, one launch (start us, length us, event | category | flops | bytes accessed | tf_op | source)
XLA Modules:
  0.0 47.5 jit_solution(15168276953127255288)
XLA Ops:
  0.6 2.2 %shard_map.173 = (bf16[8,64,128]{2,1,0:T(8,128)(2,1)}, bf16[1552,128]{1,0:T(8,128)(2,1)S(1)}, s32[1,8,48]{2,1,0:T(8,128)S(1)}, s32[1,2]{1,0:T(1,128)S(1)}, s32[1...) custom-call(bf16[256,128]{1,0:T(8,128)(2,1)} %x_ref.5, ...), custom_call_target="tpu_custom_call" | custom-call | tf_op jit(solution)/shard_map/pallas_call | solution.py:367
  2.9 3.0 %collective-permute-start.1 = (bf16[1552,128]{1,0:T(8,128)(2,1)S(1)}, bf16[1552,128]{1,0:T(8,128)(2,1)S(1)}, u32[]{:S(2)}, u32[]{:S(2)}) collective-permute-start(bf16[1552,128]{1,0:T(8,128)(2,1)S(1)} %get-tuple-element.48.refs_0_), channel_id=1, source_target_pairs={{0,2},{1,3},{2,0},{3,1},{4,6},{5,7},{6,4},{7,5},{8,10},{9,11},{10,... | collective-permute-start | bytes 1191944 | tf_op jit(solution)/shard_map/ppermute | solution.py:315
  5.9 5.8 %all-to-all-start = ((bf16[8,64,128]{2,1,0:T(8,128)(2,1)}), bf16[8,64,128]{2,1,0:T(8,128)(2,1)S(1)}, u32[]{:S(2)}, u32[]{:S(2)}) async-start(bf16[8,64,128]{2,1,0:T(8,128)(2,1)} %get-tuple-element.50), calls=%async_computation | async-start | bytes 262144 | tf_op jit(solution)/shard_map/all_to_all | solution.py:319
  12.4 0.4 shard_map.174
  12.8 6.3 %all-to-all-done.got_ref = bf16[8,64,128]{2,1,0:T(8,128)(2,1)S(1)} async-done(((bf16[8,64,128]{2,1,0:T(8,128)(2,1)}), bf16[8,64,128]{2,1,0:T(8,128)(2,1)S(1)}, u32[]{:S(2)}, u32[]{:S(2)}) %all-to-all-start) | async-done | bytes 131104 | tf_op jit(solution)/shard_map/all_to_all | solution.py:319
  19.1 0.3 shard_map.175
  19.4 0.6 %collective-permute-start.4 = (bf16[256,128]{1,0:T(8,128)(2,1)S(1)}, bf16[256,128]{1,0:T(8,128)(2,1)S(1)}, u32[]{:S(2)}, u32[]{:S(2)}) collective-permute-start(bf16[256,128]{1,0:T(8,128)(2,1)S(1)} %get-tuple-element.52.refs_4_), channel_id=1, source_target_pairs={{0,2},{1,3},{2,0},{3,1},{4,6},{5,7},{6,4},{7,5},{8,10},{9,11},{10,... | collective-permute-start | bytes 196616 | tf_op jit(solution)/shard_map/ppermute | solution.py:315
  20.0 0.2 collective-permute-start.3
  20.2 3.8 %collective-permute-done.4.refs_6_ = bf16[256,128]{1,0:T(8,128)(2,1)S(1)} collective-permute-done((bf16[256,128]{1,0:T(8,128)(2,1)S(1)}, bf16[256,128]{1,0:T(8,128)(2,1)S(1)}, u32[]{:S(2)}, u32[]{:S(2)}) %collective-permute-start.4) | collective-permute-done | bytes 65568 | tf_op jit(solution)/shard_map/ppermute | solution.py:315
  23.9 1.2 %collective-permute-done.5.refs_7_ = bf16[256,128]{1,0:T(8,128)(2,1)S(1)} collective-permute-done((bf16[256,128]{1,0:T(8,128)(2,1)S(1)}, bf16[256,128]{1,0:T(8,128)(2,1)S(1)}, u32[]{:S(2)}, u32[]{:S(2)}) %collective-permute-start.5) | collective-permute-done | bytes 65568 | tf_op jit(solution)/shard_map/ppermute | solution.py:315
  25.2 1.5 %shard_map.176 = (bf16[256,128]{1,0:T(8,128)(2,1)}, f32[256,128]{1,0:T(8,128)S(1)}, bf16[4,64,128]{2,1,0:T(8,128)(2,1)S(1)}, bf16[320,128]{1,0:T(8,128)(2,1)S(1)...) custom-call(s32[1]{0:T(128)} %bitcast.me_ref, s32[1]{0:T(128)} %bitcast.1.side_ref, ...), custom_call_target="tpu_custom_call" | custom-call | tf_op jit(solution)/shard_map/pallas_call | solution.py:412
  26.7 0.7 %collective-permute-start.6 = (bf16[320,128]{1,0:T(8,128)(2,1)S(1)}, bf16[320,128]{1,0:T(8,128)(2,1)S(1)}, u32[]{:S(2)}, u32[]{:S(2)}) collective-permute-start(bf16[320,128]{1,0:T(8,128)(2,1)S(1)} %get-tuple-element.56), channel_id=1, source_target_pairs={{0,12},{4,8},{8,4},{12,0},{16,28},{20,24},{24,20},{28,16},{1,13},{... | collective-permute-start | bytes 245768 | tf_op jit(solution)/shard_map/ppermute | solution.py:315
  27.4 0.9 %collective-permute-start.7 = (bf16[320,128]{1,0:T(8,128)(2,1)S(1)}, bf16[320,128]{1,0:T(8,128)(2,1)S(1)}, u32[]{:S(2)}, u32[]{:S(2)}) collective-permute-start(bf16[320,128]{1,0:T(8,128)(2,1)S(1)} %get-tuple-element.57), channel_id=1, source_target_pairs={{0,8},{4,12},{8,0},{12,4},{16,24},{20,28},{24,16},{28,20},{1,9},{5... | collective-permute-start | bytes 245768 | tf_op jit(solution)/shard_map/ppermute | solution.py:315
  28.4 1.8 %collective-permute-start.8 = (bf16[320,128]{1,0:T(8,128)(2,1)S(1)}, bf16[320,128]{1,0:T(8,128)(2,1)S(1)}, u32[]{:S(2)}, u32[]{:S(2)}) collective-permute-start(bf16[320,128]{1,0:T(8,128)(2,1)S(1)} %get-tuple-element.58), channel_id=1, source_target_pairs={{0,4},{4,0},{8,12},{12,8},{16,20},{20,16},{24,28},{28,24},{1,5},{5... | collective-permute-start | bytes 245768 | tf_op jit(solution)/shard_map/ppermute | solution.py:315
  30.2 0.4 collective-permute-start.9
  30.6 3.0 %collective-permute-done.6.refs_0_ = bf16[320,128]{1,0:T(8,128)(2,1)S(1)} collective-permute-done((bf16[320,128]{1,0:T(8,128)(2,1)S(1)}, bf16[320,128]{1,0:T(8,128)(2,1)S(1)}, u32[]{:S(2)}, u32[]{:S(2)}) %collective-permute-start.6) | collective-permute-done | bytes 81952 | tf_op jit(solution)/shard_map/ppermute | solution.py:315
  33.6 0.3 collective-permute-done.8.refs_2_
  33.9 0.5 collective-permute-start.13
  34.3 1.2 %collective-permute-done.9.got_ref = bf16[4,64,128]{2,1,0:T(8,128)(2,1)S(1)} collective-permute-done((bf16[4,64,128]{2,1,0:T(8,128)(2,1)S(1)}, bf16[4,64,128]{2,1,0:T(8,128)(2,1)S(1)}, u32[]{:S(2)}, u32[]{:S(2)}) %collective-permute-start.9) | collective-permute-done | bytes 65568 | tf_op jit(solution)/shard_map/ppermute | solution.py:315
  35.5 0.8 %collective-permute-start.10 = (bf16[64,128]{1,0:T(8,128)(2,1)S(1)}, bf16[64,128]{1,0:T(8,128)(2,1)S(1)}, u32[]{:S(2)}, u32[]{:S(2)}) collective-permute-start(bf16[64,128]{1,0:T(8,128)(2,1)S(1)} %get-tuple-element.65), channel_id=1, source_target_pairs={{0,4},{4,0},{8,12},{12,8},{16,20},{20,16},{24,28},{28,24},{1,5},{5... | collective-permute-start | bytes 49160 | tf_op jit(solution)/shard_map/ppermute | solution.py:315
  36.4 0.3 collective-permute-start.11
  36.7 2.4 %collective-permute-start.12 = (bf16[64,128]{1,0:T(8,128)(2,1)S(1)}, bf16[64,128]{1,0:T(8,128)(2,1)S(1)}, u32[]{:S(2)}, u32[]{:S(2)}) collective-permute-start(bf16[64,128]{1,0:T(8,128)(2,1)S(1)} %get-tuple-element.67), channel_id=1, source_target_pairs={{0,12},{4,8},{8,4},{12,0},{16,28},{20,24},{24,20},{28,16},{1,13},{... | collective-permute-start | bytes 49160 | tf_op jit(solution)/shard_map/ppermute | solution.py:315
  39.0 0.2 shard_map.178
  39.2 0.6 %collective-permute-done.13.other_ref = bf16[256,128]{1,0:T(8,128)(2,1)S(1)} collective-permute-done((bf16[256,128]{1,0:T(8,128)(2,1)S(1)}, bf16[256,128]{1,0:T(8,128)(2,1)S(1)}, u32[]{:S(2)}, u32[]{:S(2)}) %collective-permute-start.13) | collective-permute-done | bytes 65568 | tf_op jit(solution)/shard_map/ppermute | solution.py:315
  39.8 0.1 collective-permute-start.16
  40.0 2.4 %collective-permute-start.15 = (bf16[256,128]{1,0:T(8,128)(2,1)S(1)}, bf16[256,128]{1,0:T(8,128)(2,1)S(1)}, u32[]{:S(2)}, u32[]{:S(2)}) collective-permute-start(bf16[256,128]{1,0:T(8,128)(2,1)S(1)} %shard_map.181.refs_0_), channel_id=1, source_target_pairs={{0,8},{4,12},{8,0},{12,4},{16,24},{20,28},{24,16},{28,20},{1,9},{5... | collective-permute-start | bytes 196616 | tf_op jit(solution)/shard_map/ppermute | solution.py:315
  42.4 1.0 %collective-permute-start.14 = (bf16[256,128]{1,0:T(8,128)(2,1)S(1)}, bf16[256,128]{1,0:T(8,128)(2,1)S(1)}, u32[]{:S(2)}, u32[]{:S(2)}) collective-permute-start(bf16[256,128]{1,0:T(8,128)(2,1)S(1)} %shard_map.181.refs_0_), channel_id=1, source_target_pairs={{0,4},{4,0},{8,12},{12,8},{16,20},{20,16},{24,28},{28,24},{1,5},{5... | collective-permute-start | bytes 196616 | tf_op jit(solution)/shard_map/ppermute | solution.py:315
  43.4 0.8 %shard_map.180 = (bf16[256,128]{1,0:T(8,128)(2,1)}, f32[1,128]{1,0:T(1,128)}) custom-call(s32[1]{0:T(128)} %bitcast.1.side_ref, s32[1]{0:T(128)} %bitcast.2.seat_ref, f32[256,128]{1,0:T(8,128)S(1)} %get-tuple-element.61.back_ref, f32[1,128]{1,0:T(1,128)S(1)} %get-tuple-element.62.near_ref, bf16[256,512]{1,0:T(8,128)(2,1)S(1)} %get-tuple-element.55.mark_ref, ...), custom_call_target="tpu_custom_call" | custom-call | flops 2000000000 | bytes 1000000 | tf_op jit(solution)/shard_map/pallas_call | solution.py:468
  44.2 0.8 %collective-permute-done.16.refs_3_ = bf16[256,128]{1,0:T(8,128)(2,1)S(1)} collective-permute-done((bf16[256,128]{1,0:T(8,128)(2,1)S(1)}, bf16[256,128]{1,0:T(8,128)(2,1)S(1)}, u32[]{:S(2)}, u32[]{:S(2)}) %collective-permute-start.16) | collective-permute-done | bytes 65568 | tf_op jit(solution)/shard_map/ppermute | solution.py:315
  45.1 0.3 collective-permute-done.15.refs_2_
  45.3 1.3 %collective-permute-done.14.refs_1_ = bf16[256,128]{1,0:T(8,128)(2,1)S(1)} collective-permute-done((bf16[256,128]{1,0:T(8,128)(2,1)S(1)}, bf16[256,128]{1,0:T(8,128)(2,1)S(1)}, u32[]{:S(2)}, u32[]{:S(2)}) %collective-permute-start.14) | collective-permute-done | bytes 65568 | tf_op jit(solution)/shard_map/ppermute | solution.py:315
  46.7 0.9 %shard_map.182 = (f32[128,512]{1,0:T(8,128)}, f32[128,512]{1,0:T(8,128)}) custom-call(s32[1]{0:T(128)} %bitcast.2.seat_ref, bf16[256,128]{1,0:T(8,128)(2,1)S(1)} %shard_map.181.refs_0_, bf16[256,128]{1,0:T(8,128)(2,1)S(1)} %collective-permute-done.14.refs_1_, bf16[256,128]{1,0:T(8,128)(2,1)S(1)} %collective-permute-done.15.refs_2_, ...), custom_call_target="tpu_custom_call" | custom-call | tf_op jit(solution)/shard_map/pallas_call | solution.py:477
  (20 shorter events, 0.2 us)
Async XLA Ops:
  2.9 16.2 %collective-permute-start.1 = (bf16[1552,128]{1,0:T(8,128)(2,1)S(1)}, bf16[1552,128]{1,0:T(8,128)(2,1)S(1)}, u32[]{:S(2)}, u32[]{:S(2)}) collective-permute-start(bf16[1552,128]{1,0:T(8,128)(2,1)S(1)} %get-tuple-element.48.refs_0_), channel_id=1, source_target_pairs={{0,2},{1,3},{2,0},{3,1},{4,6},{5,7},{6,4},{7,5},{8,10},{9,11},{10,... | collective-permute-start | bytes 1191944 | tf_op jit(solution)/shard_map/ppermute | solution.py:315
  5.9 13.2 %all-to-all-start = ((bf16[8,64,128]{2,1,0:T(8,128)(2,1)}), bf16[8,64,128]{2,1,0:T(8,128)(2,1)S(1)}, u32[]{:S(2)}, u32[]{:S(2)}) async-start(bf16[8,64,128]{2,1,0:T(8,128)(2,1)} %get-tuple-element.50), calls=%async_computation | async-start | bytes 262144 | tf_op jit(solution)/shard_map/all_to_all | solution.py:319
  11.7 12.2 %collective-permute-start = (bf16[1552,128]{1,0:T(8,128)(2,1)S(1)}, bf16[1552,128]{1,0:T(8,128)(2,1)S(1)}, u32[]{:S(2)}, u32[]{:S(2)}) collective-permute-start(bf16[1552,128]{1,0:T(8,128)(2,1)S(1)} %get-tuple-element.48.refs_0_), channel_id=1, source_target_pairs={{0,1},{1,0},{2,3},{3,2},{4,5},{5,4},{6,7},{7,6},{8,9},{9,8},{10,11... | collective-permute-start | bytes 1191944 | tf_op jit(solution)/shard_map/ppermute | solution.py:315
  12.4 6.7 %copy-start = (bf16[256,128]{1,0:T(8,128)(2,1)S(1)}, bf16[256,128]{1,0:T(8,128)(2,1)}, u32[]{:S(2)}) copy-start(bf16[256,128]{1,0:T(8,128)(2,1)} %x_ref.5) | copy-start | bytes 196612
  19.0 6.1 %copy-start.1 = (bf16[128,512]{1,0:T(8,128)(2,1)S(1)}, bf16[128,512]{1,0:T(8,128)(2,1)}, u32[]{:S(2)}) copy-start(bf16[128,512]{1,0:T(8,128)(2,1)} %ws_ref.3) | copy-start | bytes 393220
  19.1 6.1 %copy-start.2 = (bf16[128,512]{1,0:T(8,128)(2,1)S(1)}, bf16[128,512]{1,0:T(8,128)(2,1)}, u32[]{:S(2)}) copy-start(bf16[128,512]{1,0:T(8,128)(2,1)} %wn_ref.3) | copy-start | bytes 393220
  19.3 5.8 %collective-permute-start.2 = (bf16[1552,128]{1,0:T(8,128)(2,1)S(1)}, bf16[1552,128]{1,0:T(8,128)(2,1)S(1)}, u32[]{:S(2)}, u32[]{:S(2)}) collective-permute-start(bf16[1552,128]{1,0:T(8,128)(2,1)S(1)} %get-tuple-element.51.refs_2_), channel_id=1, source_target_pairs={{0,1},{1,0},{2,3},{3,2},{4,5},{5,4},{6,7},{7,6},{8,9},{9,8},{10,11... | collective-permute-start | bytes 1191944 | tf_op jit(solution)/shard_map/ppermute | solution.py:315
  19.4 4.5 %collective-permute-start.4 = (bf16[256,128]{1,0:T(8,128)(2,1)S(1)}, bf16[256,128]{1,0:T(8,128)(2,1)S(1)}, u32[]{:S(2)}, u32[]{:S(2)}) collective-permute-start(bf16[256,128]{1,0:T(8,128)(2,1)S(1)} %get-tuple-element.52.refs_4_), channel_id=1, source_target_pairs={{0,2},{1,3},{2,0},{3,1},{4,6},{5,7},{6,4},{7,5},{8,10},{9,11},{10,... | collective-permute-start | bytes 196616 | tf_op jit(solution)/shard_map/ppermute | solution.py:315
  20.0 3.9 %collective-permute-start.3 = (bf16[256,128]{1,0:T(8,128)(2,1)S(1)}, bf16[256,128]{1,0:T(8,128)(2,1)S(1)}, u32[]{:S(2)}, u32[]{:S(2)}) collective-permute-start(bf16[256,128]{1,0:T(8,128)(2,1)S(1)} %get-tuple-element.52.refs_4_), channel_id=1, source_target_pairs={{0,1},{1,0},{2,3},{3,2},{4,5},{5,4},{6,7},{7,6},{8,9},{9,8},{10,11... | collective-permute-start | bytes 196616 | tf_op jit(solution)/shard_map/ppermute | solution.py:315
  23.9 1.3 %collective-permute-start.5 = (bf16[256,128]{1,0:T(8,128)(2,1)S(1)}, bf16[256,128]{1,0:T(8,128)(2,1)S(1)}, u32[]{:S(2)}, u32[]{:S(2)}) collective-permute-start(bf16[256,128]{1,0:T(8,128)(2,1)S(1)} %collective-permute-done.4.refs_6_), channel_id=1, source_target_pairs={{0,1},{1,0},{2,3},{3,2},{4,5},{5,4},{6,7},{7,6},{8,9},{9,8},{10,11... | collective-permute-start | bytes 196616 | tf_op jit(solution)/shard_map/ppermute | solution.py:315
  26.7 6.9 %collective-permute-start.6 = (bf16[320,128]{1,0:T(8,128)(2,1)S(1)}, bf16[320,128]{1,0:T(8,128)(2,1)S(1)}, u32[]{:S(2)}, u32[]{:S(2)}) collective-permute-start(bf16[320,128]{1,0:T(8,128)(2,1)S(1)} %get-tuple-element.56), channel_id=1, source_target_pairs={{0,12},{4,8},{8,4},{12,0},{16,28},{20,24},{24,20},{28,16},{1,13},{... | collective-permute-start | bytes 245768 | tf_op jit(solution)/shard_map/ppermute | solution.py:315
  27.4 6.2 %collective-permute-start.7 = (bf16[320,128]{1,0:T(8,128)(2,1)S(1)}, bf16[320,128]{1,0:T(8,128)(2,1)S(1)}, u32[]{:S(2)}, u32[]{:S(2)}) collective-permute-start(bf16[320,128]{1,0:T(8,128)(2,1)S(1)} %get-tuple-element.57), channel_id=1, source_target_pairs={{0,8},{4,12},{8,0},{12,4},{16,24},{20,28},{24,16},{28,20},{1,9},{5... | collective-permute-start | bytes 245768 | tf_op jit(solution)/shard_map/ppermute | solution.py:315
  28.4 5.5 %collective-permute-start.8 = (bf16[320,128]{1,0:T(8,128)(2,1)S(1)}, bf16[320,128]{1,0:T(8,128)(2,1)S(1)}, u32[]{:S(2)}, u32[]{:S(2)}) collective-permute-start(bf16[320,128]{1,0:T(8,128)(2,1)S(1)} %get-tuple-element.58), channel_id=1, source_target_pairs={{0,4},{4,0},{8,12},{12,8},{16,20},{20,16},{24,28},{28,24},{1,5},{5... | collective-permute-start | bytes 245768 | tf_op jit(solution)/shard_map/ppermute | solution.py:315
  30.2 5.3 %collective-permute-start.9 = (bf16[4,64,128]{2,1,0:T(8,128)(2,1)S(1)}, bf16[4,64,128]{2,1,0:T(8,128)(2,1)S(1)}, u32[]{:S(2)}, u32[]{:S(2)}) collective-permute-start(bf16[4,64,128]{2,1,0:T(8,128)(2,1)S(1)} %get-tuple-element.63), channel_id=1, source_target_pairs={{0,16},{4,20},{8,24},{12,28},{16,0},{20,4},{24,8},{28,12},{1,17},{... | collective-permute-start | bytes 196616 | tf_op jit(solution)/shard_map/ppermute | solution.py:315
  33.9 5.9 %collective-permute-start.13 = (bf16[256,128]{1,0:T(8,128)(2,1)S(1)}, bf16[256,128]{1,0:T(8,128)(2,1)S(1)}, u32[]{:S(2)}, u32[]{:S(2)}) collective-permute-start(bf16[256,128]{1,0:T(8,128)(2,1)S(1)} %get-tuple-element.69.own_ref), channel_id=1, source_target_pairs={{0,16},{4,20},{8,24},{12,28},{16,0},{20,4},{24,8},{28,12},{1,17},{... | collective-permute-start | bytes 196616 | tf_op jit(solution)/shard_map/ppermute | solution.py:315
  35.5 6.9 %collective-permute-start.10 = (bf16[64,128]{1,0:T(8,128)(2,1)S(1)}, bf16[64,128]{1,0:T(8,128)(2,1)S(1)}, u32[]{:S(2)}, u32[]{:S(2)}) collective-permute-start(bf16[64,128]{1,0:T(8,128)(2,1)S(1)} %get-tuple-element.65), channel_id=1, source_target_pairs={{0,4},{4,0},{8,12},{12,8},{16,20},{20,16},{24,28},{28,24},{1,5},{5... | collective-permute-start | bytes 49160 | tf_op jit(solution)/shard_map/ppermute | solution.py:315
  36.4 7.0 %collective-permute-start.11 = (bf16[64,128]{1,0:T(8,128)(2,1)S(1)}, bf16[64,128]{1,0:T(8,128)(2,1)S(1)}, u32[]{:S(2)}, u32[]{:S(2)}) collective-permute-start(bf16[64,128]{1,0:T(8,128)(2,1)S(1)} %get-tuple-element.66), channel_id=1, source_target_pairs={{0,8},{4,12},{8,0},{12,4},{16,24},{20,28},{24,16},{28,20},{1,9},{5... | collective-permute-start | bytes 49160 | tf_op jit(solution)/shard_map/ppermute | solution.py:315
  36.7 6.7 %collective-permute-start.12 = (bf16[64,128]{1,0:T(8,128)(2,1)S(1)}, bf16[64,128]{1,0:T(8,128)(2,1)S(1)}, u32[]{:S(2)}, u32[]{:S(2)}) collective-permute-start(bf16[64,128]{1,0:T(8,128)(2,1)S(1)} %get-tuple-element.67), channel_id=1, source_target_pairs={{0,12},{4,8},{8,4},{12,0},{16,28},{20,24},{24,20},{28,16},{1,13},{... | collective-permute-start | bytes 49160 | tf_op jit(solution)/shard_map/ppermute | solution.py:315
  39.8 5.2 %collective-permute-start.16 = (bf16[256,128]{1,0:T(8,128)(2,1)S(1)}, bf16[256,128]{1,0:T(8,128)(2,1)S(1)}, u32[]{:S(2)}, u32[]{:S(2)}) collective-permute-start(bf16[256,128]{1,0:T(8,128)(2,1)S(1)} %shard_map.181.refs_0_), channel_id=1, source_target_pairs={{0,12},{4,8},{8,4},{12,0},{16,28},{20,24},{24,20},{28,16},{1,13},{... | collective-permute-start | bytes 196616 | tf_op jit(solution)/shard_map/ppermute | solution.py:315
  40.0 5.4 %collective-permute-start.15 = (bf16[256,128]{1,0:T(8,128)(2,1)S(1)}, bf16[256,128]{1,0:T(8,128)(2,1)S(1)}, u32[]{:S(2)}, u32[]{:S(2)}) collective-permute-start(bf16[256,128]{1,0:T(8,128)(2,1)S(1)} %shard_map.181.refs_0_), channel_id=1, source_target_pairs={{0,8},{4,12},{8,0},{12,4},{16,24},{20,28},{24,16},{28,20},{1,9},{5... | collective-permute-start | bytes 196616 | tf_op jit(solution)/shard_map/ppermute | solution.py:315
  42.4 4.3 %collective-permute-start.14 = (bf16[256,128]{1,0:T(8,128)(2,1)S(1)}, bf16[256,128]{1,0:T(8,128)(2,1)S(1)}, u32[]{:S(2)}, u32[]{:S(2)}) collective-permute-start(bf16[256,128]{1,0:T(8,128)(2,1)S(1)} %shard_map.181.refs_0_), channel_id=1, source_target_pairs={{0,4},{4,0},{8,12},{12,8},{16,20},{20,16},{24,28},{28,24},{1,5},{5... | collective-permute-start | bytes 196616 | tf_op jit(solution)/shard_map/ppermute | solution.py:315

commit v12 on v11

--- a/solution.py
+++ b/solution.py
@@ -229,7 +229,11 @@
     return [(seat ^ k, ref) for k, ref in enumerate(refs)]
 
 
-def sum_kernel(width, seat_ref, *refs):
+def store_kernel(held_ref, out_ref):
+    out_ref[...] = held_ref[...]
+
+
+def sum_kernel(width, seat_ref, stored_ref, *refs):
     got_refs, (sum_ref, near_ref) = refs[:-2], refs[-2:]
     total = jnp.zeros(sum_ref.shape, F32)
     for j, got_ref in seated(got_refs[::-1], seat_ref[0]):
@@ -309,6 +313,10 @@
 
 def shape(dims, kind):
     return jax.ShapeDtypeStruct(dims, kind)
+
+
+def kept(dims, kind):
+    return pltpu.VMEM(dims, kind)
 
 
 def partner(block, axis, k):
@@ -367,7 +375,7 @@
     outgoing, pack, *moved = pl.pallas_call(
         functools.partial(send_kernel, width),
         out_shape=(
-            shape((peers, width, cols), BF),
+            kept((peers, width, cols), BF),
             shape((pack_rows, cols), BF),
             *(shape(a.shape, a.dtype) for a in moved),
         ),
@@ -412,7 +420,7 @@
     output, back, mirror, *returned = pl.pallas_call(
         functools.partial(dense_kernel, slots, hub_here, feats, width, count),
         out_shape=(
-            shape((rows, cols), BF),
+            kept((rows, cols), BF),
             shape((rows, cols), F32),
             shape((half, width, cols), BF),
             *([shape((height, cols), BF)] * half if direct else [shape((half, height, cols), BF)]),
@@ -429,13 +437,21 @@
 
     arrived = swap(returned)[::-1] if direct else [exchange(returned[0], halves)]
     mirror = partner(mirror, "dom", half)
+    output = pl.pallas_call(
+        store_kernel,
+        out_shape=shape((rows, cols), BF),
+        in_specs=[VMEM],
+        out_specs=VMEM,
+        compiler_params=PARAMS,
+        cost_estimate=pl.CostEstimate(flops=10**8, bytes_accessed=10**6, transcendentals=0),
+    )(output)
     half_sum, near_ghosts = pl.pallas_call(
         functools.partial(sum_kernel, width),
         out_shape=(shape((share, cols), BF), shape((half, width, cols), BF)),
-        in_specs=[SMEM] + [VMEM] * count,
+        in_specs=[SMEM, HBM] + [VMEM] * count,
         out_specs=(VMEM,) * 2,
         compiler_params=PARAMS,
-    )(seat, *arrived)
+    )(seat, *pinned(output), *arrived)
     other_sum = partner(half_sum, "dom", half)
     if direct:
         crossed = swap(

time: 47.8 us -> 47.6 us (level)
  waiting for transfers between devices: 18.8 us -> 18.3 us
    pallas_call x1 -> x2, Pallas kernels: 2.22 us -> 2.85 us  [the longest x1 2.22 us: on_device(): pl.pallas_call(functools.partial(send_kernel, width), out_shape=(kept((pe...]
    ppermute x17, waiting for transfers between devices: 12.5 us -> 12 us  [partner(): lax.ppermute(block, axis, [(i, i ^ k) for i in range(lax.axis_size(axis))])]
  transfers between devices with their start and end apart: 18 -> 18, of which waited for: 10 -> 10; matrix products, arithmetic and copies ran while one was open for 0% -> 0% of each run, Pallas kernels for 4% -> 5%
where the time goes in v12:
time: 47.6 us; the launch traced here: 47.3 us
  starting transfers between devices  21.1 us (44%)
  waiting for transfers between devices  18.3 us (38%)
  Pallas kernels  6.56 us (14%)
  between operations  1.38 us (3%)
    ppermute x17, starting transfers between devices, partner(): lax.ppermute(block, axis, [(i, i ^ k) for i in range(lax.axis_size(axis))])  15.3 us
    ppermute x17, waiting for transfers between devices, partner(): lax.ppermute(block, axis, [(i, i ^ k) for i in range(lax.axis_size(axis))])  12 us
    all_to_all x1, waiting for transfers between devices, exchange(): lax.all_to_all(blocks, 'dom', split_axis=0, concat_axis=0, axis_index_gro...  6.27 us
    all_to_all x1, starting transfers between devices, exchange(): lax.all_to_all(blocks, 'dom', split_axis=0, concat_axis=0, axis_index_gro...  5.83 us
    pallas_call x1, Pallas kernels, on_device(): pl.pallas_call(functools.partial(send_kernel, width), out_shape=(kept((pe...  2.22 us
    pallas_call x1, Pallas kernels, on_device(): pl.pallas_call(functools.partial(dense_kernel, slots, hub_here, feats, wi...  1.15 us
  transfers between devices with their start and end apart: 18, of which 10 were waited for; matrix products, arithmetic and copies ran while one was open for 0% of the time, Pallas kernels for 5%

profile of v12, /device:TPU:0, one launch (start us, length us, event | category | flops | bytes accessed | tf_op | source)
XLA Modules:
  0.0 47.3 jit_solution(14523740879133194228)
XLA Ops:
  0.6 2.2 %shard_map.173 = (bf16[8,64,128]{2,1,0:T(8,128)(2,1)}, bf16[1552,128]{1,0:T(8,128)(2,1)S(1)}, s32[1,8,48]{2,1,0:T(8,128)S(1)}, s32[1,2]{1,0:T(1,128)S(1)}, s32[1...) custom-call(bf16[256,128]{1,0:T(8,128)(2,1)} %x_ref.5, ...), custom_call_target="tpu_custom_call" | custom-call | tf_op jit(solution)/shard_map/pallas_call | solution.py:375
  2.9 3.0 %collective-permute-start.1 = (bf16[1552,128]{1,0:T(8,128)(2,1)S(1)}, bf16[1552,128]{1,0:T(8,128)(2,1)S(1)}, u32[]{:S(2)}, u32[]{:S(2)}) collective-permute-start(bf16[1552,128]{1,0:T(8,128)(2,1)S(1)} %get-tuple-element.48.refs_0_), channel_id=1, source_target_pairs={{0,2},{1,3},{2,0},{3,1},{4,6},{5,7},{6,4},{7,5},{8,10},{9,11},{10,... | collective-permute-start | bytes 1191944 | tf_op jit(solution)/shard_map/ppermute | solution.py:323
  5.9 5.8 %all-to-all-start = ((bf16[8,64,128]{2,1,0:T(8,128)(2,1)}), bf16[8,64,128]{2,1,0:T(8,128)(2,1)S(1)}, u32[]{:S(2)}, u32[]{:S(2)}) async-start(bf16[8,64,128]{2,1,0:T(8,128)(2,1)} %get-tuple-element.50), calls=%async_computation | async-start | bytes 262144 | tf_op jit(solution)/shard_map/all_to_all | solution.py:327
  12.4 0.4 shard_map.174
  12.8 6.3 %all-to-all-done.got_ref = bf16[8,64,128]{2,1,0:T(8,128)(2,1)S(1)} async-done(((bf16[8,64,128]{2,1,0:T(8,128)(2,1)}), bf16[8,64,128]{2,1,0:T(8,128)(2,1)S(1)}, u32[]{:S(2)}, u32[]{:S(2)}) %all-to-all-start) | async-done | bytes 131104 | tf_op jit(solution)/shard_map/all_to_all | solution.py:327
  19.1 0.3 shard_map.175
  19.4 0.6 %collective-permute-start.4 = (bf16[256,128]{1,0:T(8,128)(2,1)S(1)}, bf16[256,128]{1,0:T(8,128)(2,1)S(1)}, u32[]{:S(2)}, u32[]{:S(2)}) collective-permute-start(bf16[256,128]{1,0:T(8,128)(2,1)S(1)} %get-tuple-element.52.refs_4_), channel_id=1, source_target_pairs={{0,2},{1,3},{2,0},{3,1},{4,6},{5,7},{6,4},{7,5},{8,10},{9,11},{10,... | collective-permute-start | bytes 196616 | tf_op jit(solution)/shard_map/ppermute | solution.py:323
  20.0 0.2 collective-permute-start.3
  20.2 3.8 %collective-permute-done.4.refs_6_ = bf16[256,128]{1,0:T(8,128)(2,1)S(1)} collective-permute-done((bf16[256,128]{1,0:T(8,128)(2,1)S(1)}, bf16[256,128]{1,0:T(8,128)(2,1)S(1)}, u32[]{:S(2)}, u32[]{:S(2)}) %collective-permute-start.4) | collective-permute-done | bytes 65568 | tf_op jit(solution)/shard_map/ppermute | solution.py:323
  23.9 1.2 %collective-permute-done.5.refs_7_ = bf16[256,128]{1,0:T(8,128)(2,1)S(1)} collective-permute-done((bf16[256,128]{1,0:T(8,128)(2,1)S(1)}, bf16[256,128]{1,0:T(8,128)(2,1)S(1)}, u32[]{:S(2)}, u32[]{:S(2)}) %collective-permute-start.5) | collective-permute-done | bytes 65568 | tf_op jit(solution)/shard_map/ppermute | solution.py:323
  25.2 1.1 %shard_map.176 = (bf16[256,128]{1,0:T(8,128)(2,1)S(1)}, f32[256,128]{1,0:T(8,128)S(1)}, bf16[4,64,128]{2,1,0:T(8,128)(2,1)S(1)}, bf16[320,128]{1,0:T(8,128)(2,1)...) custom-call(s32[1]{0:T(128)} %bitcast.me_ref, s32[1]{0:T(128)} %bitcast.1.side_ref, ...), custom_call_target="tpu_custom_call" | custom-call | tf_op jit(solution)/shard_map/pallas_call | solution.py:420
  26.3 0.8 %collective-permute-start.6 = (bf16[320,128]{1,0:T(8,128)(2,1)S(1)}, bf16[320,128]{1,0:T(8,128)(2,1)S(1)}, u32[]{:S(2)}, u32[]{:S(2)}) collective-permute-start(bf16[320,128]{1,0:T(8,128)(2,1)S(1)} %get-tuple-element.56), channel_id=1, source_target_pairs={{0,12},{4,8},{8,4},{12,0},{16,28},{20,24},{24,20},{28,16},{1,13},{... | collective-permute-start | bytes 245768 | tf_op jit(solution)/shard_map/ppermute | solution.py:323
  27.1 0.9 %collective-permute-start.7 = (bf16[320,128]{1,0:T(8,128)(2,1)S(1)}, bf16[320,128]{1,0:T(8,128)(2,1)S(1)}, u32[]{:S(2)}, u32[]{:S(2)}) collective-permute-start(bf16[320,128]{1,0:T(8,128)(2,1)S(1)} %get-tuple-element.57), channel_id=1, source_target_pairs={{0,8},{4,12},{8,0},{12,4},{16,24},{20,28},{24,16},{28,20},{1,9},{5... | collective-permute-start | bytes 245768 | tf_op jit(solution)/shard_map/ppermute | solution.py:323
  28.1 1.8 %collective-permute-start.8 = (bf16[320,128]{1,0:T(8,128)(2,1)S(1)}, bf16[320,128]{1,0:T(8,128)(2,1)S(1)}, u32[]{:S(2)}, u32[]{:S(2)}) collective-permute-start(bf16[320,128]{1,0:T(8,128)(2,1)S(1)} %get-tuple-element.58), channel_id=1, source_target_pairs={{0,4},{4,0},{8,12},{12,8},{16,20},{20,16},{24,28},{28,24},{1,5},{5... | collective-permute-start | bytes 245768 | tf_op jit(solution)/shard_map/ppermute | solution.py:323
  29.9 0.4 collective-permute-start.9
  30.3 0.6 %shard_map.177.stored_ref = bf16[256,128]{1,0:T(8,128)(2,1)} custom-call(bf16[256,128]{1,0:T(8,128)(2,1)S(1)} %get-tuple-element.53.held_ref), custom_call_target="tpu_custom_call" | custom-call | flops 100000000 | bytes 1000000 | tf_op jit(solution)/shard_map/pallas_call | solution.py:440
  30.9 2.4 %collective-permute-done.6.refs_0_ = bf16[320,128]{1,0:T(8,128)(2,1)S(1)} collective-permute-done((bf16[320,128]{1,0:T(8,128)(2,1)S(1)}, bf16[320,128]{1,0:T(8,128)(2,1)S(1)}, u32[]{:S(2)}, u32[]{:S(2)}) %collective-permute-start.6) | collective-permute-done | bytes 81952 | tf_op jit(solution)/shard_map/ppermute | solution.py:323
  33.3 0.3 collective-permute-done.8.refs_2_
  33.6 0.4 collective-permute-start.13
  34.0 1.2 %collective-permute-done.9.got_ref = bf16[4,64,128]{2,1,0:T(8,128)(2,1)S(1)} collective-permute-done((bf16[4,64,128]{2,1,0:T(8,128)(2,1)S(1)}, bf16[4,64,128]{2,1,0:T(8,128)(2,1)S(1)}, u32[]{:S(2)}, u32[]{:S(2)}) %collective-permute-start.9) | collective-permute-done | bytes 65568 | tf_op jit(solution)/shard_map/ppermute | solution.py:323
  35.2 0.8 %collective-permute-start.10 = (bf16[64,128]{1,0:T(8,128)(2,1)S(1)}, bf16[64,128]{1,0:T(8,128)(2,1)S(1)}, u32[]{:S(2)}, u32[]{:S(2)}) collective-permute-start(bf16[64,128]{1,0:T(8,128)(2,1)S(1)} %get-tuple-element.65), channel_id=1, source_target_pairs={{0,4},{4,0},{8,12},{12,8},{16,20},{20,16},{24,28},{28,24},{1,5},{5... | collective-permute-start | bytes 49160 | tf_op jit(solution)/shard_map/ppermute | solution.py:323
  36.0 0.4 collective-permute-start.11
  36.5 2.3 %collective-permute-start.12 = (bf16[64,128]{1,0:T(8,128)(2,1)S(1)}, bf16[64,128]{1,0:T(8,128)(2,1)S(1)}, u32[]{:S(2)}, u32[]{:S(2)}) collective-permute-start(bf16[64,128]{1,0:T(8,128)(2,1)S(1)} %get-tuple-element.67), channel_id=1, source_target_pairs={{0,12},{4,8},{8,4},{12,0},{16,28},{20,24},{24,20},{28,16},{1,13},{... | collective-permute-start | bytes 49160 | tf_op jit(solution)/shard_map/ppermute | solution.py:323
  38.7 0.2 shard_map.179
  38.9 0.6 %collective-permute-done.13.other_ref = bf16[256,128]{1,0:T(8,128)(2,1)S(1)} collective-permute-done((bf16[256,128]{1,0:T(8,128)(2,1)S(1)}, bf16[256,128]{1,0:T(8,128)(2,1)S(1)}, u32[]{:S(2)}, u32[]{:S(2)}) %collective-permute-start.13) | collective-permute-done | bytes 65568 | tf_op jit(solution)/shard_map/ppermute | solution.py:323
  39.7 2.5 %collective-permute-start.15 = (bf16[256,128]{1,0:T(8,128)(2,1)S(1)}, bf16[256,128]{1,0:T(8,128)(2,1)S(1)}, u32[]{:S(2)}, u32[]{:S(2)}) collective-permute-start(bf16[256,128]{1,0:T(8,128)(2,1)S(1)} %shard_map.182.refs_0_), channel_id=1, source_target_pairs={{0,8},{4,12},{8,0},{12,4},{16,24},{20,28},{24,16},{28,20},{1,9},{5... | collective-permute-start | bytes 196616 | tf_op jit(solution)/shard_map/ppermute | solution.py:323
  42.2 0.9 %collective-permute-start.14 = (bf16[256,128]{1,0:T(8,128)(2,1)S(1)}, bf16[256,128]{1,0:T(8,128)(2,1)S(1)}, u32[]{:S(2)}, u32[]{:S(2)}) collective-permute-start(bf16[256,128]{1,0:T(8,128)(2,1)S(1)} %shard_map.182.refs_0_), channel_id=1, source_target_pairs={{0,4},{4,0},{8,12},{12,8},{16,20},{20,16},{24,28},{28,24},{1,5},{5... | collective-permute-start | bytes 196616 | tf_op jit(solution)/shard_map/ppermute | solution.py:323
  43.1 0.8 %shard_map.181 = (bf16[256,128]{1,0:T(8,128)(2,1)}, f32[1,128]{1,0:T(1,128)}) custom-call(s32[1]{0:T(128)} %bitcast.1.side_ref, s32[1]{0:T(128)} %bitcast.2.seat_ref, f32[256,128]{1,0:T(8,128)S(1)} %get-tuple-element.61.back_ref, f32[1,128]{1,0:T(1,128)S(1)} %get-tuple-element.62.near_ref, bf16[256,512]{1,0:T(8,128)(2,1)S(1)} %get-tuple-element.55.mark_ref, ...), custom_call_target="tpu_custom_call" | custom-call | flops 2000000000 | bytes 1000000 | tf_op jit(solution)/shard_map/pallas_call | solution.py:484
  43.9 0.8 %collective-permute-done.16.refs_3_ = bf16[256,128]{1,0:T(8,128)(2,1)S(1)} collective-permute-done((bf16[256,128]{1,0:T(8,128)(2,1)S(1)}, bf16[256,128]{1,0:T(8,128)(2,1)S(1)}, u32[]{:S(2)}, u32[]{:S(2)}) %collective-permute-start.16) | collective-permute-done | bytes 65568 | tf_op jit(solution)/shard_map/ppermute | solution.py:323
  44.8 0.4 collective-permute-done.15.refs_2_
  45.1 1.3 %collective-permute-done.14.refs_1_ = bf16[256,128]{1,0:T(8,128)(2,1)S(1)} collective-permute-done((bf16[256,128]{1,0:T(8,128)(2,1)S(1)}, bf16[256,128]{1,0:T(8,128)(2,1)S(1)}, u32[]{:S(2)}, u32[]{:S(2)}) %collective-permute-start.14) | collective-permute-done | bytes 65568 | tf_op jit(solution)/shard_map/ppermute | solution.py:323
  46.5 0.9 %shard_map.183 = (f32[128,512]{1,0:T(8,128)}, f32[128,512]{1,0:T(8,128)}) custom-call(s32[1]{0:T(128)} %bitcast.2.seat_ref, bf16[256,128]{1,0:T(8,128)(2,1)S(1)} %shard_map.182.refs_0_, bf16[256,128]{1,0:T(8,128)(2,1)S(1)} %collective-permute-done.14.refs_1_, bf16[256,128]{1,0:T(8,128)(2,1)S(1)} %collective-permute-done.15.refs_2_, ...), custom_call_target="tpu_custom_call" | custom-call | tf_op jit(solution)/shard_map/pallas_call | solution.py:493
  (21 shorter events, 0.3 us)
Async XLA Ops:
  2.9 16.2 %collective-permute-start.1 = (bf16[1552,128]{1,0:T(8,128)(2,1)S(1)}, bf16[1552,128]{1,0:T(8,128)(2,1)S(1)}, u32[]{:S(2)}, u32[]{:S(2)}) collective-permute-start(bf16[1552,128]{1,0:T(8,128)(2,1)S(1)} %get-tuple-element.48.refs_0_), channel_id=1, source_target_pairs={{0,2},{1,3},{2,0},{3,1},{4,6},{5,7},{6,4},{7,5},{8,10},{9,11},{10,... | collective-permute-start | bytes 1191944 | tf_op jit(solution)/shard_map/ppermute | solution.py:323
  5.9 13.2 %all-to-all-start = ((bf16[8,64,128]{2,1,0:T(8,128)(2,1)}), bf16[8,64,128]{2,1,0:T(8,128)(2,1)S(1)}, u32[]{:S(2)}, u32[]{:S(2)}) async-start(bf16[8,64,128]{2,1,0:T(8,128)(2,1)} %get-tuple-element.50), calls=%async_computation | async-start | bytes 262144 | tf_op jit(solution)/shard_map/all_to_all | solution.py:327
  11.7 12.2 %collective-permute-start = (bf16[1552,128]{1,0:T(8,128)(2,1)S(1)}, bf16[1552,128]{1,0:T(8,128)(2,1)S(1)}, u32[]{:S(2)}, u32[]{:S(2)}) collective-permute-start(bf16[1552,128]{1,0:T(8,128)(2,1)S(1)} %get-tuple-element.48.refs_0_), channel_id=1, source_target_pairs={{0,1},{1,0},{2,3},{3,2},{4,5},{5,4},{6,7},{7,6},{8,9},{9,8},{10,11... | collective-permute-start | bytes 1191944 | tf_op jit(solution)/shard_map/ppermute | solution.py:323
  12.4 6.7 %copy-start = (bf16[256,128]{1,0:T(8,128)(2,1)S(1)}, bf16[256,128]{1,0:T(8,128)(2,1)}, u32[]{:S(2)}) copy-start(bf16[256,128]{1,0:T(8,128)(2,1)} %x_ref.5) | copy-start | bytes 196612
  19.0 6.1 %copy-start.1 = (bf16[128,512]{1,0:T(8,128)(2,1)S(1)}, bf16[128,512]{1,0:T(8,128)(2,1)}, u32[]{:S(2)}) copy-start(bf16[128,512]{1,0:T(8,128)(2,1)} %ws_ref.3) | copy-start | bytes 393220
  19.1 6.1 %copy-start.2 = (bf16[128,512]{1,0:T(8,128)(2,1)S(1)}, bf16[128,512]{1,0:T(8,128)(2,1)}, u32[]{:S(2)}) copy-start(bf16[128,512]{1,0:T(8,128)(2,1)} %wn_ref.3) | copy-start | bytes 393220
  19.3 5.8 %collective-permute-start.2 = (bf16[1552,128]{1,0:T(8,128)(2,1)S(1)}, bf16[1552,128]{1,0:T(8,128)(2,1)S(1)}, u32[]{:S(2)}, u32[]{:S(2)}) collective-permute-start(bf16[1552,128]{1,0:T(8,128)(2,1)S(1)} %get-tuple-element.51.refs_2_), channel_id=1, source_target_pairs={{0,1},{1,0},{2,3},{3,2},{4,5},{5,4},{6,7},{7,6},{8,9},{9,8},{10,11... | collective-permute-start | bytes 1191944 | tf_op jit(solution)/shard_map/ppermute | solution.py:323
  19.4 4.5 %collective-permute-start.4 = (bf16[256,128]{1,0:T(8,128)(2,1)S(1)}, bf16[256,128]{1,0:T(8,128)(2,1)S(1)}, u32[]{:S(2)}, u32[]{:S(2)}) collective-permute-start(bf16[256,128]{1,0:T(8,128)(2,1)S(1)} %get-tuple-element.52.refs_4_), channel_id=1, source_target_pairs={{0,2},{1,3},{2,0},{3,1},{4,6},{5,7},{6,4},{7,5},{8,10},{9,11},{10,... | collective-permute-start | bytes 196616 | tf_op jit(solution)/shard_map/ppermute | solution.py:323
  20.0 3.9 %collective-permute-start.3 = (bf16[256,128]{1,0:T(8,128)(2,1)S(1)}, bf16[256,128]{1,0:T(8,128)(2,1)S(1)}, u32[]{:S(2)}, u32[]{:S(2)}) collective-permute-start(bf16[256,128]{1,0:T(8,128)(2,1)S(1)} %get-tuple-element.52.refs_4_), channel_id=1, source_target_pairs={{0,1},{1,0},{2,3},{3,2},{4,5},{5,4},{6,7},{7,6},{8,9},{9,8},{10,11... | collective-permute-start | bytes 196616 | tf_op jit(solution)/shard_map/ppermute | solution.py:323
  23.9 1.3 %collective-permute-start.5 = (bf16[256,128]{1,0:T(8,128)(2,1)S(1)}, bf16[256,128]{1,0:T(8,128)(2,1)S(1)}, u32[]{:S(2)}, u32[]{:S(2)}) collective-permute-start(bf16[256,128]{1,0:T(8,128)(2,1)S(1)} %collective-permute-done.4.refs_6_), channel_id=1, source_target_pairs={{0,1},{1,0},{2,3},{3,2},{4,5},{5,4},{6,7},{7,6},{8,9},{9,8},{10,11... | collective-permute-start | bytes 196616 | tf_op jit(solution)/shard_map/ppermute | solution.py:323
  26.3 6.9 %collective-permute-start.6 = (bf16[320,128]{1,0:T(8,128)(2,1)S(1)}, bf16[320,128]{1,0:T(8,128)(2,1)S(1)}, u32[]{:S(2)}, u32[]{:S(2)}) collective-permute-start(bf16[320,128]{1,0:T(8,128)(2,1)S(1)} %get-tuple-element.56), channel_id=1, source_target_pairs={{0,12},{4,8},{8,4},{12,0},{16,28},{20,24},{24,20},{28,16},{1,13},{... | collective-permute-start | bytes 245768 | tf_op jit(solution)/shard_map/ppermute | solution.py:323
  27.1 6.1 %collective-permute-start.7 = (bf16[320,128]{1,0:T(8,128)(2,1)S(1)}, bf16[320,128]{1,0:T(8,128)(2,1)S(1)}, u32[]{:S(2)}, u32[]{:S(2)}) collective-permute-start(bf16[320,128]{1,0:T(8,128)(2,1)S(1)} %get-tuple-element.57), channel_id=1, source_target_pairs={{0,8},{4,12},{8,0},{12,4},{16,24},{20,28},{24,16},{28,20},{1,9},{5... | collective-permute-start | bytes 245768 | tf_op jit(solution)/shard_map/ppermute | solution.py:323
  28.1 5.5 %collective-permute-start.8 = (bf16[320,128]{1,0:T(8,128)(2,1)S(1)}, bf16[320,128]{1,0:T(8,128)(2,1)S(1)}, u32[]{:S(2)}, u32[]{:S(2)}) collective-permute-start(bf16[320,128]{1,0:T(8,128)(2,1)S(1)} %get-tuple-element.58), channel_id=1, source_target_pairs={{0,4},{4,0},{8,12},{12,8},{16,20},{20,16},{24,28},{28,24},{1,5},{5... | collective-permute-start | bytes 245768 | tf_op jit(solution)/shard_map/ppermute | solution.py:323
  29.9 5.3 %collective-permute-start.9 = (bf16[4,64,128]{2,1,0:T(8,128)(2,1)S(1)}, bf16[4,64,128]{2,1,0:T(8,128)(2,1)S(1)}, u32[]{:S(2)}, u32[]{:S(2)}) collective-permute-start(bf16[4,64,128]{2,1,0:T(8,128)(2,1)S(1)} %get-tuple-element.63), channel_id=1, source_target_pairs={{0,16},{4,20},{8,24},{12,28},{16,0},{20,4},{24,8},{28,12},{1,17},{... | collective-permute-start | bytes 196616 | tf_op jit(solution)/shard_map/ppermute | solution.py:323
  33.6 5.9 %collective-permute-start.13 = (bf16[256,128]{1,0:T(8,128)(2,1)S(1)}, bf16[256,128]{1,0:T(8,128)(2,1)S(1)}, u32[]{:S(2)}, u32[]{:S(2)}) collective-permute-start(bf16[256,128]{1,0:T(8,128)(2,1)S(1)} %get-tuple-element.69.own_ref), channel_id=1, source_target_pairs={{0,16},{4,20},{8,24},{12,28},{16,0},{20,4},{24,8},{28,12},{1,17},{... | collective-permute-start | bytes 196616 | tf_op jit(solution)/shard_map/ppermute | solution.py:323
  35.2 7.0 %collective-permute-start.10 = (bf16[64,128]{1,0:T(8,128)(2,1)S(1)}, bf16[64,128]{1,0:T(8,128)(2,1)S(1)}, u32[]{:S(2)}, u32[]{:S(2)}) collective-permute-start(bf16[64,128]{1,0:T(8,128)(2,1)S(1)} %get-tuple-element.65), channel_id=1, source_target_pairs={{0,4},{4,0},{8,12},{12,8},{16,20},{20,16},{24,28},{28,24},{1,5},{5... | collective-permute-start | bytes 49160 | tf_op jit(solution)/shard_map/ppermute | solution.py:323
  36.0 7.0 %collective-permute-start.11 = (bf16[64,128]{1,0:T(8,128)(2,1)S(1)}, bf16[64,128]{1,0:T(8,128)(2,1)S(1)}, u32[]{:S(2)}, u32[]{:S(2)}) collective-permute-start(bf16[64,128]{1,0:T(8,128)(2,1)S(1)} %get-tuple-element.66), channel_id=1, source_target_pairs={{0,8},{4,12},{8,0},{12,4},{16,24},{20,28},{24,16},{28,20},{1,9},{5... | collective-permute-start | bytes 49160 | tf_op jit(solution)/shard_map/ppermute | solution.py:323
  36.5 6.6 %collective-permute-start.12 = (bf16[64,128]{1,0:T(8,128)(2,1)S(1)}, bf16[64,128]{1,0:T(8,128)(2,1)S(1)}, u32[]{:S(2)}, u32[]{:S(2)}) collective-permute-start(bf16[64,128]{1,0:T(8,128)(2,1)S(1)} %get-tuple-element.67), channel_id=1, source_target_pairs={{0,12},{4,8},{8,4},{12,0},{16,28},{20,24},{24,20},{28,16},{1,13},{... | collective-permute-start | bytes 49160 | tf_op jit(solution)/shard_map/ppermute | solution.py:323
  39.5 5.2 %collective-permute-start.16 = (bf16[256,128]{1,0:T(8,128)(2,1)S(1)}, bf16[256,128]{1,0:T(8,128)(2,1)S(1)}, u32[]{:S(2)}, u32[]{:S(2)}) collective-permute-start(bf16[256,128]{1,0:T(8,128)(2,1)S(1)} %shard_map.182.refs_0_), channel_id=1, source_target_pairs={{0,12},{4,8},{8,4},{12,0},{16,28},{20,24},{24,20},{28,16},{1,13},{... | collective-permute-start | bytes 196616 | tf_op jit(solution)/shard_map/ppermute | solution.py:323
  39.7 5.5 %collective-permute-start.15 = (bf16[256,128]{1,0:T(8,128)(2,1)S(1)}, bf16[256,128]{1,0:T(8,128)(2,1)S(1)}, u32[]{:S(2)}, u32[]{:S(2)}) collective-permute-start(bf16[256,128]{1,0:T(8,128)(2,1)S(1)} %shard_map.182.refs_0_), channel_id=1, source_target_pairs={{0,8},{4,12},{8,0},{12,4},{16,24},{20,28},{24,16},{28,20},{1,9},{5... | collective-permute-start | bytes 196616 | tf_op jit(solution)/shard_map/ppermute | solution.py:323
  42.2 4.3 %collective-permute-start.14 = (bf16[256,128]{1,0:T(8,128)(2,1)S(1)}, bf16[256,128]{1,0:T(8,128)(2,1)S(1)}, u32[]{:S(2)}, u32[]{:S(2)}) collective-permute-start(bf16[256,128]{1,0:T(8,128)(2,1)S(1)} %shard_map.182.refs_0_), channel_id=1, source_target_pairs={{0,4},{4,0},{8,12},{12,8},{16,20},{20,16},{24,28},{28,24},{1,5},{5... | collective-permute-start | bytes 196616 | tf_op jit(solution)/shard_map/ppermute | solution.py:323

commit v13 on v12

--- a/solution.py
+++ b/solution.py
@@ -242,14 +242,13 @@
     sum_ref[...] = total.astype(BF)
 
 
-def deal_kernel(got_ref, *out_refs):
-    for k, ref in enumerate(out_refs):
-        ref[...] = got_ref[k]
-
-
-def total_kernel(own_ref, other_ref, part_ref):
+def total_kernel(own_ref, other_ref, mirror_ref, *out_refs):
+    share = own_ref.shape[0]
     total = (own_ref[...].astype(F32) + other_ref[...].astype(F32)).astype(BF)
-    part_ref[...] = jnp.broadcast_to(total, part_ref.shape)
+    for k in range(mirror_ref.shape[0]):
+        out_ref = out_refs[k] if len(out_refs) > 1 else out_refs[0].at[k]
+        out_ref[:share, :] = total
+        out_ref[share:, :] = mirror_ref[k]
 
 
 def near_rows(slots, hub_here, start, mark_ref, got_ref):
@@ -270,25 +269,19 @@
     bias_ref[...] = bias
 
 
-def grad_kernel(scale, slots, hub_here, side_ref, seat_ref, back_ref, near_ref, mark_ref, *refs):
-    got_refs, (grad_ref, bias_ref, hold_ref) = refs[:-3], refs[-3:]
-    half = hold_ref.shape[0]
-    for j, got_ref in seated(got_refs, seat_ref[0]):
-        hold_ref[j] = got_ref[...]
-    added, bias = near_rows(slots, hub_here, half - side_ref[0] * half, mark_ref, hold_ref)
-    grad_ref[...] = (back_ref[...] + added).astype(BF)
-    bias_ref[...] = (near_ref[...] + bias) * scale
-
-
-def spread_kernel(scale, seat_ref, *refs):
-    got_refs, (self_ref, neigh_ref, wide_ref, sems) = refs[:-4], refs[-4:]
+def last_kernel(scale, slots, hub_here, side_ref, seat_ref, back_ref, near_ref, mark_ref, *refs):
+    got_refs, (grad_ref, bias_ref, self_ref, neigh_ref, hold_ref, wide_ref, sems) = refs[:-7], refs[-7:]
     depth, full = self_ref.shape
-    cols = got_refs[0].shape[-1]
+    half, width, cols = hold_ref.shape
     blocks = full // cols
+    share = got_refs[0].shape[-2] - width
+    parts = seated(got_refs, seat_ref[0])
+    for j, ref in parts:
+        hold_ref[j] = ref[share:, :]
     if len(got_refs) > 1:
-        parts = [(j, ref[...]) for j, ref in seated(got_refs, seat_ref[0])]
+        parts = [(j, ref[:share, :]) for j, ref in parts]
     else:
-        whole = got_refs[0][...].reshape(2 * blocks * depth, cols)
+        whole = got_refs[0][:, :share, :].reshape(half * share, cols)
         parts = [(j, whole[2 * j * depth : 2 * (j + 1) * depth]) for j in range(blocks)]
     copies = []
     for at, (j, part) in enumerate(parts):
@@ -300,6 +293,9 @@
             )
             copy.start()
             copies.append(copy)
+    added, bias = near_rows(slots, hub_here, half - side_ref[0] * half, mark_ref, hold_ref)
+    grad_ref[...] = (back_ref[...] + added).astype(BF)
+    bias_ref[...] = (near_ref[...] + bias) * scale
     for copy in copies:
         copy.wait()
 
@@ -453,18 +449,6 @@
         compiler_params=PARAMS,
     )(seat, *pinned(output), *arrived)
     other_sum = partner(half_sum, "dom", half)
-    if direct:
-        crossed = swap(
-            pl.pallas_call(
-                deal_kernel,
-                out_shape=(shape((width, cols), BF),) * half,
-                in_specs=[VMEM],
-                out_specs=(VMEM,) * half,
-                compiler_params=PARAMS,
-            )(mirror)
-        )
-    else:
-        crossed = [exchange(mirror, halves)]
     back, near_bias = pl.pallas_call(
         functools.partial(near_kernel, slots, hub_here),
         out_shape=(shape((rows, cols), F32), shape((1, cols), F32)),
@@ -473,31 +457,31 @@
         compiler_params=PARAMS,
         cost_estimate=pl.CostEstimate(flops=10**8, bytes_accessed=10**6, transcendentals=0),
     )(side, back, mark, near_ghosts)
-    part = pl.pallas_call(
+    parts = pl.pallas_call(
         total_kernel,
-        out_shape=shape((share, cols) if direct else (half, share, cols), BF),
-        in_specs=[VMEM, VMEM],
-        out_specs=VMEM,
-        compiler_params=PARAMS,
-    )(half_sum, other_sum)
-    parts = swap([part] * half) if direct else [exchange(part, halves)]
-    grad_features, grad_bias = pl.pallas_call(
-        functools.partial(grad_kernel, scale, slots, hub_here),
-        out_shape=(shape((rows, cols), BF), shape((1, cols), F32)),
+        out_shape=[shape((height, cols), BF)] * half if direct else [shape((half, height, cols), BF)],
+        in_specs=[VMEM] * 3,
+        out_specs=[VMEM] * count,
+        compiler_params=PARAMS,
+    )(half_sum, other_sum, mirror)
+    parts = swap(parts) if direct else [exchange(parts[0], halves)]
+    grad_features, grad_bias, grad_self, grad_neigh = pl.pallas_call(
+        functools.partial(last_kernel, scale, slots, hub_here),
+        out_shape=(
+            shape((rows, cols), BF),
+            shape((1, cols), F32),
+            shape((depth, full), F32),
+            shape((depth, full), F32),
+        ),
         in_specs=[SMEM] * 2 + [VMEM] * (3 + count),
-        out_specs=(VMEM,) * 2,
-        scratch_shapes=[pltpu.VMEM((half, width, cols), BF)],
-        compiler_params=PARAMS,
-        cost_estimate=pl.CostEstimate(flops=2 * 10**9, bytes_accessed=10**6, transcendentals=0),
-    )(side, seat, back, near_bias, mark, *crossed)
-    grad_self, grad_neigh = pl.pallas_call(
-        functools.partial(spread_kernel, scale),
-        out_shape=(shape((depth, full), F32), shape((depth, full), F32)),
-        in_specs=[SMEM] + [VMEM] * count,
-        out_specs=(HBM,) * 2,
-        scratch_shapes=[pltpu.VMEM((blocks, 2 * depth, cols), F32), pltpu.SemaphoreType.DMA((2 * blocks,))],
-        compiler_params=PARAMS,
-    )(seat, *parts)
+        out_specs=(VMEM,) * 2 + (HBM,) * 2,
+        scratch_shapes=[
+            pltpu.VMEM((half, width, cols), BF),
+            pltpu.VMEM((blocks, 2 * depth, cols), F32),
+            pltpu.SemaphoreType.DMA((2 * blocks,)),
+        ],
+        compiler_params=PARAMS,
+    )(side, seat, back, near_bias, mark, *parts)
     return output, grad_features, grad_self, grad_neigh, grad_bias.reshape(cols)
 
 

time: 47.6 us -> 48.2 us (1.013)
  waiting for transfers between devices: 18.3 us -> 22.5 us
  starting transfers between devices: 21.1 us -> 17.6 us
    ppermute x17 -> x14, waiting for transfers between devices: 12 us -> 16.2 us  [partner(): lax.ppermute(block, axis, [(i, i ^ k) for i in range(lax.axis_size(axis))])]
    ppermute x17 -> x14, starting transfers between devices: 15.3 us -> 11.8 us  [partner(): lax.ppermute(block, axis, [(i, i ^ k) for i in range(lax.axis_size(axis))])]
    pallas_call x4 -> x2, Pallas kernels: 1.7 us -> 1.57 us  [the longest x1 1.55 us: on_device(): pl.pallas_call(functools.partial(last_kernel, scale, slots, hub_here), ou...]
  transfers between devices with their start and end apart: 18 -> 15, of which waited for: 10 -> 10; matrix products, arithmetic and copies ran while one was open for 0% -> 0% of each run, Pallas kernels for 5% -> 3%
where the time goes in v13:
time: 48.2 us; the launch traced here: 47.9 us
  waiting for transfers between devices  22.5 us (47%)
  starting transfers between devices  17.6 us (37%)
  Pallas kernels  6.44 us (13%)
  between operations  1.38 us (3%)
    ppermute x14, waiting for transfers between devices, partner(): lax.ppermute(block, axis, [(i, i ^ k) for i in range(lax.axis_size(axis))])  16.2 us
    ppermute x14, starting transfers between devices, partner(): lax.ppermute(block, axis, [(i, i ^ k) for i in range(lax.axis_size(axis))])  11.8 us
    all_to_all x1, waiting for transfers between devices, exchange(): lax.all_to_all(blocks, 'dom', split_axis=0, concat_axis=0, axis_index_gro...  6.27 us
    all_to_all x1, starting transfers between devices, exchange(): lax.all_to_all(blocks, 'dom', split_axis=0, concat_axis=0, axis_index_gro...  5.83 us
    pallas_call x1, Pallas kernels, on_device(): pl.pallas_call(functools.partial(send_kernel, width), out_shape=(kept((pe...  2.22 us
    pallas_call x1, Pallas kernels, on_device(): pl.pallas_call(functools.partial(last_kernel, scale, slots, hub_here), ou...  1.55 us
    pallas_call x1, Pallas kernels, on_device(): pl.pallas_call(functools.partial(dense_kernel, slots, hub_here, feats, wi...  1.15 us
  transfers between devices with their start and end apart: 15, of which 10 were waited for; matrix products, arithmetic and copies ran while one was open for 0% of the time, Pallas kernels for 3%

profile of v13, /device:TPU:0, one launch (start us, length us, event | category | flops | bytes accessed | tf_op | source)
XLA Modules:
  0.0 47.9 jit_solution(8730092097901629290)
XLA Ops:
  0.6 2.2 %shard_map.173 = (bf16[8,64,128]{2,1,0:T(8,128)(2,1)}, bf16[1552,128]{1,0:T(8,128)(2,1)S(1)}, s32[1,8,48]{2,1,0:T(8,128)S(1)}, s32[1,2]{1,0:T(1,128)S(1)}, s32[1...) custom-call(bf16[256,128]{1,0:T(8,128)(2,1)} %x_ref.5, ...), custom_call_target="tpu_custom_call" | custom-call | tf_op jit(solution)/shard_map/pallas_call | solution.py:371
  2.9 3.0 %collective-permute-start.1 = (bf16[1552,128]{1,0:T(8,128)(2,1)S(1)}, bf16[1552,128]{1,0:T(8,128)(2,1)S(1)}, u32[]{:S(2)}, u32[]{:S(2)}) collective-permute-start(bf16[1552,128]{1,0:T(8,128)(2,1)S(1)} %get-tuple-element.48.refs_0_), channel_id=1, source_target_pairs={{0,2},{1,3},{2,0},{3,1},{4,6},{5,7},{6,4},{7,5},{8,10},{9,11},{10,... | collective-permute-start | bytes 1191944 | tf_op jit(solution)/shard_map/ppermute | solution.py:319
  5.9 5.8 %all-to-all-start = ((bf16[8,64,128]{2,1,0:T(8,128)(2,1)}), bf16[8,64,128]{2,1,0:T(8,128)(2,1)S(1)}, u32[]{:S(2)}, u32[]{:S(2)}) async-start(bf16[8,64,128]{2,1,0:T(8,128)(2,1)} %get-tuple-element.50), calls=%async_computation | async-start | bytes 262144 | tf_op jit(solution)/shard_map/all_to_all | solution.py:323
  12.4 0.0 copy-start
  12.4 0.4 shard_map.174
  12.8 6.3 %all-to-all-done.got_ref = bf16[8,64,128]{2,1,0:T(8,128)(2,1)S(1)} async-done(((bf16[8,64,128]{2,1,0:T(8,128)(2,1)}), bf16[8,64,128]{2,1,0:T(8,128)(2,1)S(1)}, u32[]{:S(2)}, u32[]{:S(2)}) %all-to-all-start) | async-done | bytes 131104 | tf_op jit(solution)/shard_map/all_to_all | solution.py:323
  19.0 0.0 collective-permute-done.1.far_ref
  19.1 0.0 copy-start.2
  19.1 0.3 shard_map.175
  19.3 0.1 collective-permute-start.2
  19.4 0.6 %collective-permute-start.4 = (bf16[256,128]{1,0:T(8,128)(2,1)S(1)}, bf16[256,128]{1,0:T(8,128)(2,1)S(1)}, u32[]{:S(2)}, u32[]{:S(2)}) collective-permute-start(bf16[256,128]{1,0:T(8,128)(2,1)S(1)} %get-tuple-element.52.refs_4_), channel_id=1, source_target_pairs={{0,2},{1,3},{2,0},{3,1},{4,6},{5,7},{6,4},{7,5},{8,10},{9,11},{10,... | collective-permute-start | bytes 196616 | tf_op jit(solution)/shard_map/ppermute | solution.py:319
  20.0 0.2 collective-permute-start.3
  20.2 3.8 %collective-permute-done.4.refs_6_ = bf16[256,128]{1,0:T(8,128)(2,1)S(1)} collective-permute-done((bf16[256,128]{1,0:T(8,128)(2,1)S(1)}, bf16[256,128]{1,0:T(8,128)(2,1)S(1)}, u32[]{:S(2)}, u32[]{:S(2)}) %collective-permute-start.4) | collective-permute-done | bytes 65568 | tf_op jit(solution)/shard_map/ppermute | solution.py:319
  23.9 1.2 %collective-permute-done.5.refs_7_ = bf16[256,128]{1,0:T(8,128)(2,1)S(1)} collective-permute-done((bf16[256,128]{1,0:T(8,128)(2,1)S(1)}, bf16[256,128]{1,0:T(8,128)(2,1)S(1)}, u32[]{:S(2)}, u32[]{:S(2)}) %collective-permute-start.5) | collective-permute-done | bytes 65568 | tf_op jit(solution)/shard_map/ppermute | solution.py:319
  25.2 1.1 %shard_map.176 = (bf16[256,128]{1,0:T(8,128)(2,1)S(1)}, f32[256,128]{1,0:T(8,128)S(1)}, bf16[4,64,128]{2,1,0:T(8,128)(2,1)S(1)}, bf16[320,128]{1,0:T(8,128)(2,1)...) custom-call(s32[1]{0:T(128)} %bitcast.me_ref, s32[1]{0:T(128)} %bitcast.1.side_ref, ...), custom_call_target="tpu_custom_call" | custom-call | tf_op jit(solution)/shard_map/pallas_call | solution.py:416
  26.3 0.8 %collective-permute-start.6 = (bf16[320,128]{1,0:T(8,128)(2,1)S(1)}, bf16[320,128]{1,0:T(8,128)(2,1)S(1)}, u32[]{:S(2)}, u32[]{:S(2)}) collective-permute-start(bf16[320,128]{1,0:T(8,128)(2,1)S(1)} %get-tuple-element.56), channel_id=1, source_target_pairs={{0,12},{4,8},{8,4},{12,0},{16,28},{20,24},{24,20},{28,16},{1,13},{... | collective-permute-start | bytes 245768 | tf_op jit(solution)/shard_map/ppermute | solution.py:319
  27.1 0.9 %collective-permute-start.7 = (bf16[320,128]{1,0:T(8,128)(2,1)S(1)}, bf16[320,128]{1,0:T(8,128)(2,1)S(1)}, u32[]{:S(2)}, u32[]{:S(2)}) collective-permute-start(bf16[320,128]{1,0:T(8,128)(2,1)S(1)} %get-tuple-element.57), channel_id=1, source_target_pairs={{0,8},{4,12},{8,0},{12,4},{16,24},{20,28},{24,16},{28,20},{1,9},{5... | collective-permute-start | bytes 245768 | tf_op jit(solution)/shard_map/ppermute | solution.py:319
  28.1 1.8 %collective-permute-start.8 = (bf16[320,128]{1,0:T(8,128)(2,1)S(1)}, bf16[320,128]{1,0:T(8,128)(2,1)S(1)}, u32[]{:S(2)}, u32[]{:S(2)}) collective-permute-start(bf16[320,128]{1,0:T(8,128)(2,1)S(1)} %get-tuple-element.58), channel_id=1, source_target_pairs={{0,4},{4,0},{8,12},{12,8},{16,20},{20,16},{24,28},{28,24},{1,5},{5... | collective-permute-start | bytes 245768 | tf_op jit(solution)/shard_map/ppermute | solution.py:319
  29.9 0.4 collective-permute-start.10
  30.3 0.6 %shard_map.177.stored_ref = bf16[256,128]{1,0:T(8,128)(2,1)} custom-call(bf16[256,128]{1,0:T(8,128)(2,1)S(1)} %get-tuple-element.53.held_ref), custom_call_target="tpu_custom_call" | custom-call | flops 100000000 | bytes 1000000 | tf_op jit(solution)/shard_map/pallas_call | solution.py:436
  30.9 2.4 %collective-permute-done.6.refs_0_ = bf16[320,128]{1,0:T(8,128)(2,1)S(1)} collective-permute-done((bf16[320,128]{1,0:T(8,128)(2,1)S(1)}, bf16[320,128]{1,0:T(8,128)(2,1)S(1)}, u32[]{:S(2)}, u32[]{:S(2)}) %collective-permute-start.6) | collective-permute-done | bytes 81952 | tf_op jit(solution)/shard_map/ppermute | solution.py:319
  33.3 0.3 collective-permute-done.8.refs_2_
  33.6 0.4 collective-permute-start.9
  34.0 1.2 %collective-permute-done.10.mirror_ref = bf16[4,64,128]{2,1,0:T(8,128)(2,1)S(1)} collective-permute-done((bf16[4,64,128]{2,1,0:T(8,128)(2,1)S(1)}, bf16[4,64,128]{2,1,0:T(8,128)(2,1)S(1)}, u32[]{:S(2)}, u32[]{:S(2)}) %collective-permute-start.10) | collective-permute-done | bytes 65568 | tf_op jit(solution)/shard_map/ppermute | solution.py:319
  35.2 4.3 %collective-permute-done.9.other_ref = bf16[256,128]{1,0:T(8,128)(2,1)S(1)} collective-permute-done((bf16[256,128]{1,0:T(8,128)(2,1)S(1)}, bf16[256,128]{1,0:T(8,128)(2,1)S(1)}, u32[]{:S(2)}, u32[]{:S(2)}) %collective-permute-start.9) | collective-permute-done | bytes 65568 | tf_op jit(solution)/shard_map/ppermute | solution.py:319
  39.5 1.2 %collective-permute-start.11 = (bf16[320,128]{1,0:T(8,128)(2,1)S(1)}, bf16[320,128]{1,0:T(8,128)(2,1)S(1)}, u32[]{:S(2)}, u32[]{:S(2)}) collective-permute-start(bf16[320,128]{1,0:T(8,128)(2,1)S(1)} %get-tuple-element.66), channel_id=1, source_target_pairs={{0,4},{4,0},{8,12},{12,8},{16,20},{20,16},{24,28},{28,24},{1,5},{5... | collective-permute-start | bytes 245768 | tf_op jit(solution)/shard_map/ppermute | solution.py:319
  40.8 2.3 %collective-permute-start.13 = (bf16[320,128]{1,0:T(8,128)(2,1)S(1)}, bf16[320,128]{1,0:T(8,128)(2,1)S(1)}, u32[]{:S(2)}, u32[]{:S(2)}) collective-permute-start(bf16[320,128]{1,0:T(8,128)(2,1)S(1)} %get-tuple-element.68), channel_id=1, source_target_pairs={{0,12},{4,8},{8,4},{12,0},{16,28},{20,24},{24,20},{28,16},{1,13},{... | collective-permute-start | bytes 245768 | tf_op jit(solution)/shard_map/ppermute | solution.py:319
  43.1 0.2 shard_map.179
  43.3 0.8 %collective-permute-done.11.refs_1_ = bf16[320,128]{1,0:T(8,128)(2,1)S(1)} collective-permute-done((bf16[320,128]{1,0:T(8,128)(2,1)S(1)}, bf16[320,128]{1,0:T(8,128)(2,1)S(1)}, u32[]{:S(2)}, u32[]{:S(2)}) %collective-permute-start.11) | collective-permute-done | bytes 81952 | tf_op jit(solution)/shard_map/ppermute | solution.py:319
  44.1 1.1 %collective-permute-done.12.refs_2_ = bf16[320,128]{1,0:T(8,128)(2,1)S(1)} collective-permute-done((bf16[320,128]{1,0:T(8,128)(2,1)S(1)}, bf16[320,128]{1,0:T(8,128)(2,1)S(1)}, u32[]{:S(2)}, u32[]{:S(2)}) %collective-permute-start.12) | collective-permute-done | bytes 81952 | tf_op jit(solution)/shard_map/ppermute | solution.py:319
  45.2 1.2 %collective-permute-done.13.refs_3_ = bf16[320,128]{1,0:T(8,128)(2,1)S(1)} collective-permute-done((bf16[320,128]{1,0:T(8,128)(2,1)S(1)}, bf16[320,128]{1,0:T(8,128)(2,1)S(1)}, u32[]{:S(2)}, u32[]{:S(2)}) %collective-permute-start.13) | collective-permute-done | bytes 81952 | tf_op jit(solution)/shard_map/ppermute | solution.py:319
  46.4 1.5 %shard_map.181 = (bf16[256,128]{1,0:T(8,128)(2,1)}, f32[1,128]{1,0:T(1,128)}, f32[128,512]{1,0:T(8,128)}, f32[128,512]{1,0:T(8,128)}) custom-call(s32[1]{0:T(128)} %bitcast.1.side_ref, s32[1]{0:T(128)} %bitcast.2.seat_ref, f32[256,128]{1,0:T(8,128)S(1)} %get-tuple-element.61.back_ref, f32[1,128]{1,0:T(1,128)S(1)} %get-tuple-element.62.near_ref, ...), custom_call_target="tpu_custom_call" | custom-call | tf_op jit(solution)/shard_map/pallas_call | solution.py:468
  (13 shorter events, 0.1 us)
Async XLA Ops:
  2.9 16.2 %collective-permute-start.1 = (bf16[1552,128]{1,0:T(8,128)(2,1)S(1)}, bf16[1552,128]{1,0:T(8,128)(2,1)S(1)}, u32[]{:S(2)}, u32[]{:S(2)}) collective-permute-start(bf16[1552,128]{1,0:T(8,128)(2,1)S(1)} %get-tuple-element.48.refs_0_), channel_id=1, source_target_pairs={{0,2},{1,3},{2,0},{3,1},{4,6},{5,7},{6,4},{7,5},{8,10},{9,11},{10,... | collective-permute-start | bytes 1191944 | tf_op jit(solution)/shard_map/ppermute | solution.py:319
  5.9 13.2 %all-to-all-start = ((bf16[8,64,128]{2,1,0:T(8,128)(2,1)}), bf16[8,64,128]{2,1,0:T(8,128)(2,1)S(1)}, u32[]{:S(2)}, u32[]{:S(2)}) async-start(bf16[8,64,128]{2,1,0:T(8,128)(2,1)} %get-tuple-element.50), calls=%async_computation | async-start | bytes 262144 | tf_op jit(solution)/shard_map/all_to_all | solution.py:323
  11.7 12.2 %collective-permute-start = (bf16[1552,128]{1,0:T(8,128)(2,1)S(1)}, bf16[1552,128]{1,0:T(8,128)(2,1)S(1)}, u32[]{:S(2)}, u32[]{:S(2)}) collective-permute-start(bf16[1552,128]{1,0:T(8,128)(2,1)S(1)} %get-tuple-element.48.refs_0_), channel_id=1, source_target_pairs={{0,1},{1,0},{2,3},{3,2},{4,5},{5,4},{6,7},{7,6},{8,9},{9,8},{10,11... | collective-permute-start | bytes 1191944 | tf_op jit(solution)/shard_map/ppermute | solution.py:319
  12.4 6.7 %copy-start = (bf16[256,128]{1,0:T(8,128)(2,1)S(1)}, bf16[256,128]{1,0:T(8,128)(2,1)}, u32[]{:S(2)}) copy-start(bf16[256,128]{1,0:T(8,128)(2,1)} %x_ref.5) | copy-start | bytes 196612
  19.0 6.1 %copy-start.1 = (bf16[128,512]{1,0:T(8,128)(2,1)S(1)}, bf16[128,512]{1,0:T(8,128)(2,1)}, u32[]{:S(2)}) copy-start(bf16[128,512]{1,0:T(8,128)(2,1)} %ws_ref.3) | copy-start | bytes 393220
  19.1 6.1 %copy-start.2 = (bf16[128,512]{1,0:T(8,128)(2,1)S(1)}, bf16[128,512]{1,0:T(8,128)(2,1)}, u32[]{:S(2)}) copy-start(bf16[128,512]{1,0:T(8,128)(2,1)} %wn_ref.3) | copy-start | bytes 393220
  19.3 5.8 %collective-permute-start.2 = (bf16[1552,128]{1,0:T(8,128)(2,1)S(1)}, bf16[1552,128]{1,0:T(8,128)(2,1)S(1)}, u32[]{:S(2)}, u32[]{:S(2)}) collective-permute-start(bf16[1552,128]{1,0:T(8,128)(2,1)S(1)} %get-tuple-element.51.refs_2_), channel_id=1, source_target_pairs={{0,1},{1,0},{2,3},{3,2},{4,5},{5,4},{6,7},{7,6},{8,9},{9,8},{10,11... | collective-permute-start | bytes 1191944 | tf_op jit(solution)/shard_map/ppermute | solution.py:319
  19.4 4.5 %collective-permute-start.4 = (bf16[256,128]{1,0:T(8,128)(2,1)S(1)}, bf16[256,128]{1,0:T(8,128)(2,1)S(1)}, u32[]{:S(2)}, u32[]{:S(2)}) collective-permute-start(bf16[256,128]{1,0:T(8,128)(2,1)S(1)} %get-tuple-element.52.refs_4_), channel_id=1, source_target_pairs={{0,2},{1,3},{2,0},{3,1},{4,6},{5,7},{6,4},{7,5},{8,10},{9,11},{10,... | collective-permute-start | bytes 196616 | tf_op jit(solution)/shard_map/ppermute | solution.py:319
  20.0 3.9 %collective-permute-start.3 = (bf16[256,128]{1,0:T(8,128)(2,1)S(1)}, bf16[256,128]{1,0:T(8,128)(2,1)S(1)}, u32[]{:S(2)}, u32[]{:S(2)}) collective-permute-start(bf16[256,128]{1,0:T(8,128)(2,1)S(1)} %get-tuple-element.52.refs_4_), channel_id=1, source_target_pairs={{0,1},{1,0},{2,3},{3,2},{4,5},{5,4},{6,7},{7,6},{8,9},{9,8},{10,11... | collective-permute-start | bytes 196616 | tf_op jit(solution)/shard_map/ppermute | solution.py:319
  23.9 1.3 %collective-permute-start.5 = (bf16[256,128]{1,0:T(8,128)(2,1)S(1)}, bf16[256,128]{1,0:T(8,128)(2,1)S(1)}, u32[]{:S(2)}, u32[]{:S(2)}) collective-permute-start(bf16[256,128]{1,0:T(8,128)(2,1)S(1)} %collective-permute-done.4.refs_6_), channel_id=1, source_target_pairs={{0,1},{1,0},{2,3},{3,2},{4,5},{5,4},{6,7},{7,6},{8,9},{9,8},{10,11... | collective-permute-start | bytes 196616 | tf_op jit(solution)/shard_map/ppermute | solution.py:319
  26.3 6.9 %collective-permute-start.6 = (bf16[320,128]{1,0:T(8,128)(2,1)S(1)}, bf16[320,128]{1,0:T(8,128)(2,1)S(1)}, u32[]{:S(2)}, u32[]{:S(2)}) collective-permute-start(bf16[320,128]{1,0:T(8,128)(2,1)S(1)} %get-tuple-element.56), channel_id=1, source_target_pairs={{0,12},{4,8},{8,4},{12,0},{16,28},{20,24},{24,20},{28,16},{1,13},{... | collective-permute-start | bytes 245768 | tf_op jit(solution)/shard_map/ppermute | solution.py:319
  27.1 6.1 %collective-permute-start.7 = (bf16[320,128]{1,0:T(8,128)(2,1)S(1)}, bf16[320,128]{1,0:T(8,128)(2,1)S(1)}, u32[]{:S(2)}, u32[]{:S(2)}) collective-permute-start(bf16[320,128]{1,0:T(8,128)(2,1)S(1)} %get-tuple-element.57), channel_id=1, source_target_pairs={{0,8},{4,12},{8,0},{12,4},{16,24},{20,28},{24,16},{28,20},{1,9},{5... | collective-permute-start | bytes 245768 | tf_op jit(solution)/shard_map/ppermute | solution.py:319
  28.1 5.5 %collective-permute-start.8 = (bf16[320,128]{1,0:T(8,128)(2,1)S(1)}, bf16[320,128]{1,0:T(8,128)(2,1)S(1)}, u32[]{:S(2)}, u32[]{:S(2)}) collective-permute-start(bf16[320,128]{1,0:T(8,128)(2,1)S(1)} %get-tuple-element.58), channel_id=1, source_target_pairs={{0,4},{4,0},{8,12},{12,8},{16,20},{20,16},{24,28},{28,24},{1,5},{5... | collective-permute-start | bytes 245768 | tf_op jit(solution)/shard_map/ppermute | solution.py:319
  29.9 5.3 %collective-permute-start.10 = (bf16[4,64,128]{2,1,0:T(8,128)(2,1)S(1)}, bf16[4,64,128]{2,1,0:T(8,128)(2,1)S(1)}, u32[]{:S(2)}, u32[]{:S(2)}) collective-permute-start(bf16[4,64,128]{2,1,0:T(8,128)(2,1)S(1)} %get-tuple-element.64), channel_id=1, source_target_pairs={{0,16},{4,20},{8,24},{12,28},{16,0},{20,4},{24,8},{28,12},{1,17},{... | collective-permute-start | bytes 196616 | tf_op jit(solution)/shard_map/ppermute | solution.py:319
  33.6 5.9 %collective-permute-start.9 = (bf16[256,128]{1,0:T(8,128)(2,1)S(1)}, bf16[256,128]{1,0:T(8,128)(2,1)S(1)}, u32[]{:S(2)}, u32[]{:S(2)}) collective-permute-start(bf16[256,128]{1,0:T(8,128)(2,1)S(1)} %get-tuple-element.63.own_ref), channel_id=1, source_target_pairs={{0,16},{4,20},{8,24},{12,28},{16,0},{20,4},{24,8},{28,12},{1,17},{... | collective-permute-start | bytes 196616 | tf_op jit(solution)/shard_map/ppermute | solution.py:319
  39.5 4.5 %collective-permute-start.11 = (bf16[320,128]{1,0:T(8,128)(2,1)S(1)}, bf16[320,128]{1,0:T(8,128)(2,1)S(1)}, u32[]{:S(2)}, u32[]{:S(2)}) collective-permute-start(bf16[320,128]{1,0:T(8,128)(2,1)S(1)} %get-tuple-element.66), channel_id=1, source_target_pairs={{0,4},{4,0},{8,12},{12,8},{16,20},{20,16},{24,28},{28,24},{1,5},{5... | collective-permute-start | bytes 245768 | tf_op jit(solution)/shard_map/ppermute | solution.py:319
  40.8 4.4 %collective-permute-start.12 = (bf16[320,128]{1,0:T(8,128)(2,1)S(1)}, bf16[320,128]{1,0:T(8,128)(2,1)S(1)}, u32[]{:S(2)}, u32[]{:S(2)}) collective-permute-start(bf16[320,128]{1,0:T(8,128)(2,1)S(1)} %get-tuple-element.67), channel_id=1, source_target_pairs={{0,8},{4,12},{8,0},{12,4},{16,24},{20,28},{24,16},{28,20},{1,9},{5... | collective-permute-start | bytes 245768 | tf_op jit(solution)/shard_map/ppermute | solution.py:319
  40.8 5.6 %collective-permute-start.13 = (bf16[320,128]{1,0:T(8,128)(2,1)S(1)}, bf16[320,128]{1,0:T(8,128)(2,1)S(1)}, u32[]{:S(2)}, u32[]{:S(2)}) collective-permute-start(bf16[320,128]{1,0:T(8,128)(2,1)S(1)} %get-tuple-element.68), channel_id=1, source_target_pairs={{0,12},{4,8},{8,4},{12,0},{16,28},{20,24},{24,20},{28,16},{1,13},{... | collective-permute-start | bytes 245768 | tf_op jit(solution)/shard_map/ppermute | solution.py:319

commit v14 on v12

--- a/solution.py
+++ b/solution.py
@@ -145,14 +145,14 @@
 
 def dense_kernel(slots, hub_here, feats, width, count, me_ref, side_ref, seat_ref, x_ref, ws_ref, wn_ref, turned_ref, *refs):
     pack_refs, n_refs = refs[:feats], refs[feats : 2 * feats]
-    out_ref, back_ref, mirror_ref = refs[2 * feats : 2 * feats + 3]
-    send_refs = refs[2 * feats + 3 : 2 * feats + 3 + count]
-    pre_ref, cot_ref, bias_ref = refs[2 * feats + 3 + count :]
+    out_ref, back_ref, ghost_ref, mirror_ref = refs[2 * feats : 2 * feats + 4]
+    send_refs = refs[2 * feats + 4 : 2 * feats + 4 + count]
+    pre_ref, cot_ref, bias_ref = refs[2 * feats + 4 + count :]
     rows, cols = x_ref.shape
     depth, full = ws_ref.shape
     blocks = full // cols
     half = mirror_ref.shape[0]
-    height = send_refs[0].shape[-2]
+    share = send_refs[0].shape[-2]
     me = me_ref[0]
     base = 2 * blocks * depth
     left = []
@@ -190,7 +190,6 @@
     sums = jnp.sum(cot_ref[:, mine].astype(F32), axis=0, keepdims=True)
     high = sums.astype(BF).astype(F32)
     here = side_ref[0] * half
-    share = height - width
 
     def ghosts(start, peers):
         line = lax.broadcasted_iota(jnp.int32, (peers * width, cols), 0) % width
@@ -204,13 +203,13 @@
     if count > 1:
         for k, ref in enumerate(send_refs):
             peer = seat_ref[0] ^ k
-            ref[:width, :] = ghosts(here + peer, 1)
+            ghost_ref[k] = ghosts(here + peer, 1)
             mirror_ref[k] = ghosts(half - here + peer, 1)
             block = cot_ref[:, pl.ds(pl.multiple_of(peer * cols, cols), cols)]
-            ref[width:, :] = jnp.dot(pair, block, preferred_element_type=F32).astype(BF)
+            ref[...] = jnp.dot(pair, block, preferred_element_type=F32).astype(BF)
         return
     send_ref = send_refs[0]
-    send_ref[:, :width, :] = ghosts(here, half).reshape(half, width, cols)
+    ghost_ref[...] = ghosts(here, half).reshape(half, width, cols)
     mirror_ref[...] = ghosts(half - here, half).reshape(half, width, cols)
     weights = jnp.dot(pair, cot_ref[...], preferred_element_type=F32).astype(BF)
     step = min(share, depth)
@@ -219,7 +218,7 @@
             block = weights[kind * depth : (kind + 1) * depth, j * cols : (j + 1) * cols]
             for part in range(depth // step):
                 at = (j * 2 + kind) * depth + part * step
-                low = width + at % share
+                low = at % share
                 send_ref[at // share, low : low + step, :] = block[part * step : (part + 1) * step]
 
 
@@ -233,18 +232,20 @@
     out_ref[...] = held_ref[...]
 
 
-def sum_kernel(width, seat_ref, stored_ref, *refs):
-    got_refs, (sum_ref, near_ref) = refs[:-2], refs[-2:]
+def sum_kernel(stored_ref, *refs):
+    got_refs, sum_ref = refs[:-1], refs[-1]
     total = jnp.zeros(sum_ref.shape, F32)
-    for j, got_ref in seated(got_refs[::-1], seat_ref[0]):
-        total = total + got_ref[width:, :].astype(F32)
-        near_ref[j] = got_ref[:width, :]
+    for got_ref in got_refs if len(got_refs) > 1 else [got_refs[0].at[j] for j in range(got_refs[0].shape[0])]:
+        total = total + got_ref[...].astype(F32)
     sum_ref[...] = total.astype(BF)
 
 
-def deal_kernel(got_ref, *out_refs):
-    for k, ref in enumerate(out_refs):
-        ref[...] = got_ref[k]
+def deal_kernel(ghost_ref, mirror_ref, *out_refs):
+    width = ghost_ref.shape[1]
+    for k in range(ghost_ref.shape[0]):
+        out_ref = out_refs[k] if len(out_refs) > 1 else out_refs[0].at[k]
+        out_ref[:width, :] = ghost_ref[k]
+        out_ref[width:, :] = mirror_ref[k]
 
 
 def total_kernel(own_ref, other_ref, part_ref):
@@ -263,21 +264,17 @@
     return added, jnp.sum(bias, axis=0, keepdims=True)
 
 
-def near_kernel(slots, hub_here, side_ref, back_ref, mark_ref, got_ref, sum_ref, bias_ref):
-    half = got_ref.shape[0]
-    added, bias = near_rows(slots, hub_here, side_ref[0] * half, mark_ref, got_ref)
-    sum_ref[...] = back_ref[...] + added
-    bias_ref[...] = bias
-
-
-def grad_kernel(scale, slots, hub_here, side_ref, seat_ref, back_ref, near_ref, mark_ref, *refs):
-    got_refs, (grad_ref, bias_ref, hold_ref) = refs[:-3], refs[-3:]
-    half = hold_ref.shape[0]
+def grad_kernel(scale, slots, hub_here, side_ref, seat_ref, back_ref, mark_ref, *refs):
+    got_refs, (grad_ref, bias_ref, near_ref, far_ref) = refs[:-4], refs[-4:]
+    half, width = near_ref.shape[:2]
     for j, got_ref in seated(got_refs, seat_ref[0]):
-        hold_ref[j] = got_ref[...]
-    added, bias = near_rows(slots, hub_here, half - side_ref[0] * half, mark_ref, hold_ref)
-    grad_ref[...] = (back_ref[...] + added).astype(BF)
-    bias_ref[...] = (near_ref[...] + bias) * scale
+        near_ref[j] = got_ref[:width, :]
+        far_ref[j] = got_ref[width:, :]
+    here = side_ref[0] * half
+    near, near_bias = near_rows(slots, hub_here, here, mark_ref, near_ref)
+    far, far_bias = near_rows(slots, hub_here, half - here, mark_ref, far_ref)
+    grad_ref[...] = (back_ref[...] + near + far).astype(BF)
+    bias_ref[...] = (near_bias + far_bias) * scale
 
 
 def spread_kernel(scale, seat_ref, *refs):
@@ -416,17 +413,17 @@
     far_neigh = partner(neigh, "feat", 2)
     every = [neigh, partner(neigh, "feat", 1), far_neigh, partner(far_neigh, "feat", 1)]
 
-    height = width + share
-    output, back, mirror, *returned = pl.pallas_call(
+    output, back, ghosts, mirror, *returned = pl.pallas_call(
         functools.partial(dense_kernel, slots, hub_here, feats, width, count),
         out_shape=(
             kept((rows, cols), BF),
             shape((rows, cols), F32),
             shape((half, width, cols), BF),
-            *([shape((height, cols), BF)] * half if direct else [shape((half, height, cols), BF)]),
+            shape((half, width, cols), BF),
+            *([shape((share, cols), BF)] * half if direct else [shape((half, share, cols), BF)]),
         ),
         in_specs=[SMEM] * 3 + [VMEM] * (4 + 2 * feats),
-        out_specs=(VMEM,) * (3 + count),
+        out_specs=(VMEM,) * (4 + count),
         scratch_shapes=[
             pltpu.VMEM((rows, full), F32),
             pltpu.VMEM((rows, full), BF),
@@ -445,34 +442,22 @@
         compiler_params=PARAMS,
         cost_estimate=pl.CostEstimate(flops=10**8, bytes_accessed=10**6, transcendentals=0),
     )(output)
-    half_sum, near_ghosts = pl.pallas_call(
-        functools.partial(sum_kernel, width),
-        out_shape=(shape((share, cols), BF), shape((half, width, cols), BF)),
-        in_specs=[SMEM, HBM] + [VMEM] * count,
-        out_specs=(VMEM,) * 2,
-        compiler_params=PARAMS,
-    )(seat, *pinned(output), *arrived)
+    half_sum = pl.pallas_call(
+        sum_kernel,
+        out_shape=shape((share, cols), BF),
+        in_specs=[HBM] + [VMEM] * count,
+        out_specs=VMEM,
+        compiler_params=PARAMS,
+    )(*pinned(output), *arrived)
     other_sum = partner(half_sum, "dom", half)
-    if direct:
-        crossed = swap(
-            pl.pallas_call(
-                deal_kernel,
-                out_shape=(shape((width, cols), BF),) * half,
-                in_specs=[VMEM],
-                out_specs=(VMEM,) * half,
-                compiler_params=PARAMS,
-            )(mirror)
-        )
-    else:
-        crossed = [exchange(mirror, halves)]
-    back, near_bias = pl.pallas_call(
-        functools.partial(near_kernel, slots, hub_here),
-        out_shape=(shape((rows, cols), F32), shape((1, cols), F32)),
-        in_specs=[SMEM] + [VMEM] * 3,
-        out_specs=(VMEM,) * 2,
-        compiler_params=PARAMS,
-        cost_estimate=pl.CostEstimate(flops=10**8, bytes_accessed=10**6, transcendentals=0),
-    )(side, back, mark, near_ghosts)
+    dealt = pl.pallas_call(
+        deal_kernel,
+        out_shape=[shape((2 * width, cols), BF)] * half if direct else [shape((half, 2 * width, cols), BF)],
+        in_specs=[VMEM] * 2,
+        out_specs=[VMEM] * count,
+        compiler_params=PARAMS,
+    )(ghosts, mirror)
+    dealt = swap(dealt) if direct else [exchange(dealt[0], halves)]
     part = pl.pallas_call(
         total_kernel,
         out_shape=shape((share, cols) if direct else (half, share, cols), BF),
@@ -484,12 +469,12 @@
     grad_features, grad_bias = pl.pallas_call(
         functools.partial(grad_kernel, scale, slots, hub_here),
         out_shape=(shape((rows, cols), BF), shape((1, cols), F32)),
-        in_specs=[SMEM] * 2 + [VMEM] * (3 + count),
+        in_specs=[SMEM] * 2 + [VMEM] * (2 + count),
         out_specs=(VMEM,) * 2,
-        scratch_shapes=[pltpu.VMEM((half, width, cols), BF)],
+        scratch_shapes=[pltpu.VMEM((half, width, cols), BF)] * 2,
         compiler_params=PARAMS,
         cost_estimate=pl.CostEstimate(flops=2 * 10**9, bytes_accessed=10**6, transcendentals=0),
-    )(side, seat, back, near_bias, mark, *crossed)
+    )(side, seat, back, mark, *dealt)
     grad_self, grad_neigh = pl.pallas_call(
         functools.partial(spread_kernel, scale),
         out_shape=(shape((depth, full), F32), shape((depth, full), F32)),

time: 47.6 us -> 46.9 us (0.985)
  waiting for transfers between devices: 18.3 us -> 17.3 us
    ppermute x17, waiting for transfers between devices: 12 us -> 11.1 us  [partner(): lax.ppermute(block, axis, [(i, i ^ k) for i in range(lax.axis_size(axis))])]
  transfers between devices with their start and end apart: 18 -> 18, of which waited for: 10 -> 9; matrix products, arithmetic and copies ran while one was open for 0% -> 0% of each run, Pallas kernels for 5% -> 5%
where the time goes in v14:
time: 46.9 us; the launch traced here: 46.6 us
  starting transfers between devices  21.4 us (46%)
  waiting for transfers between devices  17.3 us (37%)
  Pallas kernels  6.43 us (14%)
  between operations  1.38 us (3%)
    ppermute x17, starting transfers between devices, partner(): lax.ppermute(block, axis, [(i, i ^ k) for i in range(lax.axis_size(axis))])  15.6 us
    ppermute x17, waiting for transfers between devices, partner(): lax.ppermute(block, axis, [(i, i ^ k) for i in range(lax.axis_size(axis))])  11.1 us
    all_to_all x1, waiting for transfers between devices, exchange(): lax.all_to_all(blocks, 'dom', split_axis=0, concat_axis=0, axis_index_gro...  6.27 us
    all_to_all x1, starting transfers between devices, exchange(): lax.all_to_all(blocks, 'dom', split_axis=0, concat_axis=0, axis_index_gro...  5.83 us
    pallas_call x1, Pallas kernels, on_device(): pl.pallas_call(functools.partial(send_kernel, width), out_shape=(kept((pe...  2.22 us
    pallas_call x1, Pallas kernels, on_device(): pl.pallas_call(functools.partial(dense_kernel, slots, hub_here, feats, wi...  1.15 us
  transfers between devices with their start and end apart: 18, of which 9 were waited for; matrix products, arithmetic and copies ran while one was open for 0% of the time, Pallas kernels for 5%

profile of v14, /device:TPU:0, one launch (start us, length us, event | category | flops | bytes accessed | tf_op | source)
XLA Modules:
  0.0 46.6 jit_solution(6437234827113447175)
XLA Ops:
  0.6 2.2 %shard_map.173 = (bf16[8,64,128]{2,1,0:T(8,128)(2,1)}, bf16[1552,128]{1,0:T(8,128)(2,1)S(1)}, s32[1,8,48]{2,1,0:T(8,128)S(1)}, s32[1,2]{1,0:T(1,128)S(1)}, s32[1...) custom-call(bf16[256,128]{1,0:T(8,128)(2,1)} %x_ref.5, ...), custom_call_target="tpu_custom_call" | custom-call | tf_op jit(solution)/shard_map/pallas_call | solution.py:372
  2.9 3.0 %collective-permute-start.1 = (bf16[1552,128]{1,0:T(8,128)(2,1)S(1)}, bf16[1552,128]{1,0:T(8,128)(2,1)S(1)}, u32[]{:S(2)}, u32[]{:S(2)}) collective-permute-start(bf16[1552,128]{1,0:T(8,128)(2,1)S(1)} %get-tuple-element.45.refs_0_), channel_id=1, source_target_pairs={{0,2},{1,3},{2,0},{3,1},{4,6},{5,7},{6,4},{7,5},{8,10},{9,11},{10,... | collective-permute-start | bytes 1191944 | tf_op jit(solution)/shard_map/ppermute | solution.py:320
  5.9 5.8 %all-to-all-start = ((bf16[8,64,128]{2,1,0:T(8,128)(2,1)}), bf16[8,64,128]{2,1,0:T(8,128)(2,1)S(1)}, u32[]{:S(2)}, u32[]{:S(2)}) async-start(bf16[8,64,128]{2,1,0:T(8,128)(2,1)} %get-tuple-element.47), calls=%async_computation | async-start | bytes 262144 | tf_op jit(solution)/shard_map/all_to_all | solution.py:324
  12.4 0.4 shard_map.174
  12.8 6.3 %all-to-all-done.got_ref = bf16[8,64,128]{2,1,0:T(8,128)(2,1)S(1)} async-done(((bf16[8,64,128]{2,1,0:T(8,128)(2,1)}), bf16[8,64,128]{2,1,0:T(8,128)(2,1)S(1)}, u32[]{:S(2)}, u32[]{:S(2)}) %all-to-all-start) | async-done | bytes 131104 | tf_op jit(solution)/shard_map/all_to_all | solution.py:324
  19.1 0.3 shard_map.175
  19.3 0.1 collective-permute-start.2
  19.4 0.6 %collective-permute-start.4 = (bf16[256,128]{1,0:T(8,128)(2,1)S(1)}, bf16[256,128]{1,0:T(8,128)(2,1)S(1)}, u32[]{:S(2)}, u32[]{:S(2)}) collective-permute-start(bf16[256,128]{1,0:T(8,128)(2,1)S(1)} %get-tuple-element.49.refs_4_), channel_id=1, source_target_pairs={{0,2},{1,3},{2,0},{3,1},{4,6},{5,7},{6,4},{7,5},{8,10},{9,11},{10,... | collective-permute-start | bytes 196616 | tf_op jit(solution)/shard_map/ppermute | solution.py:320
  20.0 0.2 collective-permute-start.3
  20.2 3.8 %collective-permute-done.4.refs_6_ = bf16[256,128]{1,0:T(8,128)(2,1)S(1)} collective-permute-done((bf16[256,128]{1,0:T(8,128)(2,1)S(1)}, bf16[256,128]{1,0:T(8,128)(2,1)S(1)}, u32[]{:S(2)}, u32[]{:S(2)}) %collective-permute-start.4) | collective-permute-done | bytes 65568 | tf_op jit(solution)/shard_map/ppermute | solution.py:320
  23.9 1.2 %collective-permute-done.5.refs_7_ = bf16[256,128]{1,0:T(8,128)(2,1)S(1)} collective-permute-done((bf16[256,128]{1,0:T(8,128)(2,1)S(1)}, bf16[256,128]{1,0:T(8,128)(2,1)S(1)}, u32[]{:S(2)}, u32[]{:S(2)}) %collective-permute-start.5) | collective-permute-done | bytes 65568 | tf_op jit(solution)/shard_map/ppermute | solution.py:320
  25.2 1.1 %shard_map.176 = (bf16[256,128]{1,0:T(8,128)(2,1)S(1)}, f32[256,128]{1,0:T(8,128)S(1)}, bf16[4,64,128]{2,1,0:T(8,128)(2,1)S(1)}, bf16[4,64,128]{2,1,0:T(8,128)(2...) custom-call(s32[1]{0:T(128)} %bitcast.me_ref, ...), custom_call_target="tpu_custom_call" | custom-call | tf_op jit(solution)/shard_map/pallas_call | solution.py:416
  26.3 0.8 %collective-permute-start.10 = (bf16[256,128]{1,0:T(8,128)(2,1)S(1)}, bf16[256,128]{1,0:T(8,128)(2,1)S(1)}, u32[]{:S(2)}, u32[]{:S(2)}) collective-permute-start(bf16[256,128]{1,0:T(8,128)(2,1)S(1)} %get-tuple-element.60), channel_id=1, source_target_pairs={{0,12},{4,8},{8,4},{12,0},{16,28},{20,24},{24,20},{28,16},{1,13},{... | collective-permute-start | bytes 196616 | tf_op jit(solution)/shard_map/ppermute | solution.py:320
  27.1 0.9 %collective-permute-start.11 = (bf16[256,128]{1,0:T(8,128)(2,1)S(1)}, bf16[256,128]{1,0:T(8,128)(2,1)S(1)}, u32[]{:S(2)}, u32[]{:S(2)}) collective-permute-start(bf16[256,128]{1,0:T(8,128)(2,1)S(1)} %get-tuple-element.61), channel_id=1, source_target_pairs={{0,8},{4,12},{8,0},{12,4},{16,24},{20,28},{24,16},{28,20},{1,9},{5... | collective-permute-start | bytes 196616 | tf_op jit(solution)/shard_map/ppermute | solution.py:320
  28.1 1.8 %collective-permute-start.12 = (bf16[256,128]{1,0:T(8,128)(2,1)S(1)}, bf16[256,128]{1,0:T(8,128)(2,1)S(1)}, u32[]{:S(2)}, u32[]{:S(2)}) collective-permute-start(bf16[256,128]{1,0:T(8,128)(2,1)S(1)} %get-tuple-element.62), channel_id=1, source_target_pairs={{0,4},{4,0},{8,12},{12,8},{16,20},{20,16},{24,28},{28,24},{1,5},{5... | collective-permute-start | bytes 196616 | tf_op jit(solution)/shard_map/ppermute | solution.py:320
  29.9 0.4 collective-permute-start.6
  30.3 0.6 %shard_map.177.stored_ref = bf16[256,128]{1,0:T(8,128)(2,1)} custom-call(bf16[256,128]{1,0:T(8,128)(2,1)S(1)} %get-tuple-element.50.held_ref), custom_call_target="tpu_custom_call" | custom-call | flops 100000000 | bytes 1000000 | tf_op jit(solution)/shard_map/pallas_call | solution.py:437
  30.9 1.2 %collective-permute-done.10.refs_0_ = bf16[256,128]{1,0:T(8,128)(2,1)S(1)} collective-permute-done((bf16[256,128]{1,0:T(8,128)(2,1)S(1)}, bf16[256,128]{1,0:T(8,128)(2,1)S(1)}, u32[]{:S(2)}, u32[]{:S(2)}) %collective-permute-start.10) | collective-permute-done | bytes 65568 | tf_op jit(solution)/shard_map/ppermute | solution.py:320
  32.2 0.7 %collective-permute-done.12.refs_2_ = bf16[256,128]{1,0:T(8,128)(2,1)S(1)} collective-permute-done((bf16[256,128]{1,0:T(8,128)(2,1)S(1)}, bf16[256,128]{1,0:T(8,128)(2,1)S(1)}, u32[]{:S(2)}, u32[]{:S(2)}) %collective-permute-start.12) | collective-permute-done | bytes 65568 | tf_op jit(solution)/shard_map/ppermute | solution.py:320
  32.9 0.7 %collective-permute-start.13 = (bf16[256,128]{1,0:T(8,128)(2,1)S(1)}, bf16[256,128]{1,0:T(8,128)(2,1)S(1)}, u32[]{:S(2)}, u32[]{:S(2)}) collective-permute-start(bf16[256,128]{1,0:T(8,128)(2,1)S(1)} %shard_map.180.own_ref), channel_id=1, source_target_pairs={{0,16},{4,20},{8,24},{12,28},{16,0},{20,4},{24,8},{28,12},{1,17},{... | collective-permute-start | bytes 196616 | tf_op jit(solution)/shard_map/ppermute | solution.py:320
  33.6 1.6 %collective-permute-done.6.mirror_ref = bf16[4,64,128]{2,1,0:T(8,128)(2,1)S(1)} collective-permute-done((bf16[4,64,128]{2,1,0:T(8,128)(2,1)S(1)}, bf16[4,64,128]{2,1,0:T(8,128)(2,1)S(1)}, u32[]{:S(2)}, u32[]{:S(2)}) %collective-permute-start.6) | collective-permute-done | bytes 65568 | tf_op jit(solution)/shard_map/ppermute | solution.py:320
  35.2 0.8 %collective-permute-start.7 = (bf16[128,128]{1,0:T(8,128)(2,1)S(1)}, bf16[128,128]{1,0:T(8,128)(2,1)S(1)}, u32[]{:S(2)}, u32[]{:S(2)}) collective-permute-start(bf16[128,128]{1,0:T(8,128)(2,1)S(1)} %get-tuple-element.56), channel_id=1, source_target_pairs={{0,4},{4,0},{8,12},{12,8},{16,20},{20,16},{24,28},{28,24},{1,5},{5... | collective-permute-start | bytes 98312 | tf_op jit(solution)/shard_map/ppermute | solution.py:320
  36.0 0.5 %collective-permute-start.8 = (bf16[128,128]{1,0:T(8,128)(2,1)S(1)}, bf16[128,128]{1,0:T(8,128)(2,1)S(1)}, u32[]{:S(2)}, u32[]{:S(2)}) collective-permute-start(bf16[128,128]{1,0:T(8,128)(2,1)S(1)} %get-tuple-element.57), channel_id=1, source_target_pairs={{0,8},{4,12},{8,0},{12,4},{16,24},{20,28},{24,16},{28,20},{1,9},{5... | collective-permute-start | bytes 98312 | tf_op jit(solution)/shard_map/ppermute | solution.py:320
  36.5 2.3 %collective-permute-start.9 = (bf16[128,128]{1,0:T(8,128)(2,1)S(1)}, bf16[128,128]{1,0:T(8,128)(2,1)S(1)}, u32[]{:S(2)}, u32[]{:S(2)}) collective-permute-start(bf16[128,128]{1,0:T(8,128)(2,1)S(1)} %get-tuple-element.58), channel_id=1, source_target_pairs={{0,12},{4,8},{8,4},{12,0},{16,28},{20,24},{24,20},{28,16},{1,13},{... | collective-permute-start | bytes 98312 | tf_op jit(solution)/shard_map/ppermute | solution.py:320
  38.8 0.7 %collective-permute-start.16 = (bf16[256,128]{1,0:T(8,128)(2,1)S(1)}, bf16[256,128]{1,0:T(8,128)(2,1)S(1)}, u32[]{:S(2)}, u32[]{:S(2)}) collective-permute-start(bf16[256,128]{1,0:T(8,128)(2,1)S(1)} %shard_map.181.refs_0_), channel_id=1, source_target_pairs={{0,12},{4,8},{8,4},{12,0},{16,28},{20,24},{24,20},{28,16},{1,13},{... | collective-permute-start | bytes 196616 | tf_op jit(solution)/shard_map/ppermute | solution.py:320
  39.6 1.9 %collective-permute-start.15 = (bf16[256,128]{1,0:T(8,128)(2,1)S(1)}, bf16[256,128]{1,0:T(8,128)(2,1)S(1)}, u32[]{:S(2)}, u32[]{:S(2)}) collective-permute-start(bf16[256,128]{1,0:T(8,128)(2,1)S(1)} %shard_map.181.refs_0_), channel_id=1, source_target_pairs={{0,8},{4,12},{8,0},{12,4},{16,24},{20,28},{24,16},{28,20},{1,9},{5... | collective-permute-start | bytes 196616 | tf_op jit(solution)/shard_map/ppermute | solution.py:320
  41.4 1.0 %collective-permute-start.14 = (bf16[256,128]{1,0:T(8,128)(2,1)S(1)}, bf16[256,128]{1,0:T(8,128)(2,1)S(1)}, u32[]{:S(2)}, u32[]{:S(2)}) collective-permute-start(bf16[256,128]{1,0:T(8,128)(2,1)S(1)} %shard_map.181.refs_0_), channel_id=1, source_target_pairs={{0,4},{4,0},{8,12},{12,8},{16,20},{20,16},{24,28},{28,24},{1,5},{5... | collective-permute-start | bytes 196616 | tf_op jit(solution)/shard_map/ppermute | solution.py:320
  42.4 0.9 %shard_map.179 = (bf16[256,128]{1,0:T(8,128)(2,1)}, f32[1,128]{1,0:T(1,128)}) custom-call(s32[1]{0:T(128)} %bitcast.1.side_ref, s32[1]{0:T(128)} %bitcast.2.seat_ref, f32[256,128]{1,0:T(8,128)S(1)} %get-tuple-element.51.back_ref, bf16[256,512]{1,0:T(8,128)(2,1)S(1)} %get-tuple-element.52.mark_ref, bf16[128,128]{1,0:T(8,128)(2,1)S(1)} %get-tuple-element.55.refs_0_, ...), custom_call_target="tpu_custom_call" | custom-call | flops 2000000000 | bytes 1000000 | tf_op jit(solution)/shard_map/pallas_call | solution.py:469
  43.3 0.8 %collective-permute-done.16.refs_3_ = bf16[256,128]{1,0:T(8,128)(2,1)S(1)} collective-permute-done((bf16[256,128]{1,0:T(8,128)(2,1)S(1)}, bf16[256,128]{1,0:T(8,128)(2,1)S(1)}, u32[]{:S(2)}, u32[]{:S(2)}) %collective-permute-start.16) | collective-permute-done | bytes 65568 | tf_op jit(solution)/shard_map/ppermute | solution.py:320
  44.1 0.3 collective-permute-done.15.refs_2_
  44.4 1.3 %collective-permute-done.14.refs_1_ = bf16[256,128]{1,0:T(8,128)(2,1)S(1)} collective-permute-done((bf16[256,128]{1,0:T(8,128)(2,1)S(1)}, bf16[256,128]{1,0:T(8,128)(2,1)S(1)}, u32[]{:S(2)}, u32[]{:S(2)}) %collective-permute-start.14) | collective-permute-done | bytes 65568 | tf_op jit(solution)/shard_map/ppermute | solution.py:320
  45.7 0.9 %shard_map.182 = (f32[128,512]{1,0:T(8,128)}, f32[128,512]{1,0:T(8,128)}) custom-call(s32[1]{0:T(128)} %bitcast.2.seat_ref, bf16[256,128]{1,0:T(8,128)(2,1)S(1)} %shard_map.181.refs_0_, bf16[256,128]{1,0:T(8,128)(2,1)S(1)} %collective-permute-done.14.refs_1_, bf16[256,128]{1,0:T(8,128)(2,1)S(1)} %collective-permute-done.15.refs_2_, ...), custom_call_target="tpu_custom_call" | custom-call | tf_op jit(solution)/shard_map/pallas_call | solution.py:478
  (20 shorter events, 0.1 us)
Async XLA Ops:
  2.9 16.2 %collective-permute-start.1 = (bf16[1552,128]{1,0:T(8,128)(2,1)S(1)}, bf16[1552,128]{1,0:T(8,128)(2,1)S(1)}, u32[]{:S(2)}, u32[]{:S(2)}) collective-permute-start(bf16[1552,128]{1,0:T(8,128)(2,1)S(1)} %get-tuple-element.45.refs_0_), channel_id=1, source_target_pairs={{0,2},{1,3},{2,0},{3,1},{4,6},{5,7},{6,4},{7,5},{8,10},{9,11},{10,... | collective-permute-start | bytes 1191944 | tf_op jit(solution)/shard_map/ppermute | solution.py:320
  5.9 13.2 %all-to-all-start = ((bf16[8,64,128]{2,1,0:T(8,128)(2,1)}), bf16[8,64,128]{2,1,0:T(8,128)(2,1)S(1)}, u32[]{:S(2)}, u32[]{:S(2)}) async-start(bf16[8,64,128]{2,1,0:T(8,128)(2,1)} %get-tuple-element.47), calls=%async_computation | async-start | bytes 262144 | tf_op jit(solution)/shard_map/all_to_all | solution.py:324
  11.7 12.2 %collective-permute-start = (bf16[1552,128]{1,0:T(8,128)(2,1)S(1)}, bf16[1552,128]{1,0:T(8,128)(2,1)S(1)}, u32[]{:S(2)}, u32[]{:S(2)}) collective-permute-start(bf16[1552,128]{1,0:T(8,128)(2,1)S(1)} %get-tuple-element.45.refs_0_), channel_id=1, source_target_pairs={{0,1},{1,0},{2,3},{3,2},{4,5},{5,4},{6,7},{7,6},{8,9},{9,8},{10,11... | collective-permute-start | bytes 1191944 | tf_op jit(solution)/shard_map/ppermute | solution.py:320
  12.4 6.7 %copy-start = (bf16[256,128]{1,0:T(8,128)(2,1)S(1)}, bf16[256,128]{1,0:T(8,128)(2,1)}, u32[]{:S(2)}) copy-start(bf16[256,128]{1,0:T(8,128)(2,1)} %x_ref.5) | copy-start | bytes 196612
  19.0 6.1 %copy-start.1 = (bf16[128,512]{1,0:T(8,128)(2,1)S(1)}, bf16[128,512]{1,0:T(8,128)(2,1)}, u32[]{:S(2)}) copy-start(bf16[128,512]{1,0:T(8,128)(2,1)} %ws_ref.3) | copy-start | bytes 393220
  19.1 6.1 %copy-start.2 = (bf16[128,512]{1,0:T(8,128)(2,1)S(1)}, bf16[128,512]{1,0:T(8,128)(2,1)}, u32[]{:S(2)}) copy-start(bf16[128,512]{1,0:T(8,128)(2,1)} %wn_ref.3) | copy-start | bytes 393220
  19.3 5.8 %collective-permute-start.2 = (bf16[1552,128]{1,0:T(8,128)(2,1)S(1)}, bf16[1552,128]{1,0:T(8,128)(2,1)S(1)}, u32[]{:S(2)}, u32[]{:S(2)}) collective-permute-start(bf16[1552,128]{1,0:T(8,128)(2,1)S(1)} %get-tuple-element.48.refs_2_), channel_id=1, source_target_pairs={{0,1},{1,0},{2,3},{3,2},{4,5},{5,4},{6,7},{7,6},{8,9},{9,8},{10,11... | collective-permute-start | bytes 1191944 | tf_op jit(solution)/shard_map/ppermute | solution.py:320
  19.4 4.5 %collective-permute-start.4 = (bf16[256,128]{1,0:T(8,128)(2,1)S(1)}, bf16[256,128]{1,0:T(8,128)(2,1)S(1)}, u32[]{:S(2)}, u32[]{:S(2)}) collective-permute-start(bf16[256,128]{1,0:T(8,128)(2,1)S(1)} %get-tuple-element.49.refs_4_), channel_id=1, source_target_pairs={{0,2},{1,3},{2,0},{3,1},{4,6},{5,7},{6,4},{7,5},{8,10},{9,11},{10,... | collective-permute-start | bytes 196616 | tf_op jit(solution)/shard_map/ppermute | solution.py:320
  20.0 3.9 %collective-permute-start.3 = (bf16[256,128]{1,0:T(8,128)(2,1)S(1)}, bf16[256,128]{1,0:T(8,128)(2,1)S(1)}, u32[]{:S(2)}, u32[]{:S(2)}) collective-permute-start(bf16[256,128]{1,0:T(8,128)(2,1)S(1)} %get-tuple-element.49.refs_4_), channel_id=1, source_target_pairs={{0,1},{1,0},{2,3},{3,2},{4,5},{5,4},{6,7},{7,6},{8,9},{9,8},{10,11... | collective-permute-start | bytes 196616 | tf_op jit(solution)/shard_map/ppermute | solution.py:320
  23.9 1.3 %collective-permute-start.5 = (bf16[256,128]{1,0:T(8,128)(2,1)S(1)}, bf16[256,128]{1,0:T(8,128)(2,1)S(1)}, u32[]{:S(2)}, u32[]{:S(2)}) collective-permute-start(bf16[256,128]{1,0:T(8,128)(2,1)S(1)} %collective-permute-done.4.refs_6_), channel_id=1, source_target_pairs={{0,1},{1,0},{2,3},{3,2},{4,5},{5,4},{6,7},{7,6},{8,9},{9,8},{10,11... | collective-permute-start | bytes 196616 | tf_op jit(solution)/shard_map/ppermute | solution.py:320
  26.3 5.8 %collective-permute-start.10 = (bf16[256,128]{1,0:T(8,128)(2,1)S(1)}, bf16[256,128]{1,0:T(8,128)(2,1)S(1)}, u32[]{:S(2)}, u32[]{:S(2)}) collective-permute-start(bf16[256,128]{1,0:T(8,128)(2,1)S(1)} %get-tuple-element.60), channel_id=1, source_target_pairs={{0,12},{4,8},{8,4},{12,0},{16,28},{20,24},{24,20},{28,16},{1,13},{... | collective-permute-start | bytes 196616 | tf_op jit(solution)/shard_map/ppermute | solution.py:320
  27.1 5.0 %collective-permute-start.11 = (bf16[256,128]{1,0:T(8,128)(2,1)S(1)}, bf16[256,128]{1,0:T(8,128)(2,1)S(1)}, u32[]{:S(2)}, u32[]{:S(2)}) collective-permute-start(bf16[256,128]{1,0:T(8,128)(2,1)S(1)} %get-tuple-element.61), channel_id=1, source_target_pairs={{0,8},{4,12},{8,0},{12,4},{16,24},{20,28},{24,16},{28,20},{1,9},{5... | collective-permute-start | bytes 196616 | tf_op jit(solution)/shard_map/ppermute | solution.py:320
  28.1 4.8 %collective-permute-start.12 = (bf16[256,128]{1,0:T(8,128)(2,1)S(1)}, bf16[256,128]{1,0:T(8,128)(2,1)S(1)}, u32[]{:S(2)}, u32[]{:S(2)}) collective-permute-start(bf16[256,128]{1,0:T(8,128)(2,1)S(1)} %get-tuple-element.62), channel_id=1, source_target_pairs={{0,4},{4,0},{8,12},{12,8},{16,20},{20,16},{24,28},{28,24},{1,5},{5... | collective-permute-start | bytes 196616 | tf_op jit(solution)/shard_map/ppermute | solution.py:320
  29.9 5.3 %collective-permute-start.6 = (bf16[4,64,128]{2,1,0:T(8,128)(2,1)S(1)}, bf16[4,64,128]{2,1,0:T(8,128)(2,1)S(1)}, u32[]{:S(2)}, u32[]{:S(2)}) collective-permute-start(bf16[4,64,128]{2,1,0:T(8,128)(2,1)S(1)} %get-tuple-element.54), channel_id=1, source_target_pairs={{0,16},{4,20},{8,24},{12,28},{16,0},{20,4},{24,8},{28,12},{1,17},{... | collective-permute-start | bytes 196616 | tf_op jit(solution)/shard_map/ppermute | solution.py:320
  32.9 5.9 %collective-permute-start.13 = (bf16[256,128]{1,0:T(8,128)(2,1)S(1)}, bf16[256,128]{1,0:T(8,128)(2,1)S(1)}, u32[]{:S(2)}, u32[]{:S(2)}) collective-permute-start(bf16[256,128]{1,0:T(8,128)(2,1)S(1)} %shard_map.180.own_ref), channel_id=1, source_target_pairs={{0,16},{4,20},{8,24},{12,28},{16,0},{20,4},{24,8},{28,12},{1,17},{... | collective-permute-start | bytes 196616 | tf_op jit(solution)/shard_map/ppermute | solution.py:320
  35.2 6.2 %collective-permute-start.7 = (bf16[128,128]{1,0:T(8,128)(2,1)S(1)}, bf16[128,128]{1,0:T(8,128)(2,1)S(1)}, u32[]{:S(2)}, u32[]{:S(2)}) collective-permute-start(bf16[128,128]{1,0:T(8,128)(2,1)S(1)} %get-tuple-element.56), channel_id=1, source_target_pairs={{0,4},{4,0},{8,12},{12,8},{16,20},{20,16},{24,28},{28,24},{1,5},{5... | collective-permute-start | bytes 98312 | tf_op jit(solution)/shard_map/ppermute | solution.py:320
  36.0 6.4 %collective-permute-start.8 = (bf16[128,128]{1,0:T(8,128)(2,1)S(1)}, bf16[128,128]{1,0:T(8,128)(2,1)S(1)}, u32[]{:S(2)}, u32[]{:S(2)}) collective-permute-start(bf16[128,128]{1,0:T(8,128)(2,1)S(1)} %get-tuple-element.57), channel_id=1, source_target_pairs={{0,8},{4,12},{8,0},{12,4},{16,24},{20,28},{24,16},{28,20},{1,9},{5... | collective-permute-start | bytes 98312 | tf_op jit(solution)/shard_map/ppermute | solution.py:320
  36.5 5.9 %collective-permute-start.9 = (bf16[128,128]{1,0:T(8,128)(2,1)S(1)}, bf16[128,128]{1,0:T(8,128)(2,1)S(1)}, u32[]{:S(2)}, u32[]{:S(2)}) collective-permute-start(bf16[128,128]{1,0:T(8,128)(2,1)S(1)} %get-tuple-element.58), channel_id=1, source_target_pairs={{0,12},{4,8},{8,4},{12,0},{16,28},{20,24},{24,20},{28,16},{1,13},{... | collective-permute-start | bytes 98312 | tf_op jit(solution)/shard_map/ppermute | solution.py:320
  38.8 5.2 %collective-permute-start.16 = (bf16[256,128]{1,0:T(8,128)(2,1)S(1)}, bf16[256,128]{1,0:T(8,128)(2,1)S(1)}, u32[]{:S(2)}, u32[]{:S(2)}) collective-permute-start(bf16[256,128]{1,0:T(8,128)(2,1)S(1)} %shard_map.181.refs_0_), channel_id=1, source_target_pairs={{0,12},{4,8},{8,4},{12,0},{16,28},{20,24},{24,20},{28,16},{1,13},{... | collective-permute-start | bytes 196616 | tf_op jit(solution)/shard_map/ppermute | solution.py:320
  39.6 4.8 %collective-permute-start.15 = (bf16[256,128]{1,0:T(8,128)(2,1)S(1)}, bf16[256,128]{1,0:T(8,128)(2,1)S(1)}, u32[]{:S(2)}, u32[]{:S(2)}) collective-permute-start(bf16[256,128]{1,0:T(8,128)(2,1)S(1)} %shard_map.181.refs_0_), channel_id=1, source_target_pairs={{0,8},{4,12},{8,0},{12,4},{16,24},{20,28},{24,16},{28,20},{1,9},{5... | collective-permute-start | bytes 196616 | tf_op jit(solution)/shard_map/ppermute | solution.py:320
  41.4 4.3 %collective-permute-start.14 = (bf16[256,128]{1,0:T(8,128)(2,1)S(1)}, bf16[256,128]{1,0:T(8,128)(2,1)S(1)}, u32[]{:S(2)}, u32[]{:S(2)}) collective-permute-start(bf16[256,128]{1,0:T(8,128)(2,1)S(1)} %shard_map.181.refs_0_), channel_id=1, source_target_pairs={{0,4},{4,0},{8,12},{12,8},{16,20},{20,16},{24,28},{28,24},{1,5},{5... | collective-permute-start | bytes 196616 | tf_op jit(solution)/shard_map/ppermute | solution.py:320

commit v15 on v14

--- a/solution.py
+++ b/solution.py
@@ -232,7 +232,7 @@
     out_ref[...] = held_ref[...]
 
 
-def sum_kernel(stored_ref, *refs):
+def sum_kernel(stored_ref, mirror_ref, *refs):
     got_refs, sum_ref = refs[:-1], refs[-1]
     total = jnp.zeros(sum_ref.shape, F32)
     for got_ref in got_refs if len(got_refs) > 1 else [got_refs[0].at[j] for j in range(got_refs[0].shape[0])]:
@@ -445,10 +445,10 @@
     half_sum = pl.pallas_call(
         sum_kernel,
         out_shape=shape((share, cols), BF),
-        in_specs=[HBM] + [VMEM] * count,
+        in_specs=[HBM, VMEM] + [VMEM] * count,
         out_specs=VMEM,
         compiler_params=PARAMS,
-    )(*pinned(output), *arrived)
+    )(*pinned(output), mirror, *arrived)
     other_sum = partner(half_sum, "dom", half)
     dealt = pl.pallas_call(
         deal_kernel,

time: 46.9 us -> 47.7 us (1.017)
  starting transfers between devices: 21.4 us -> 22.8 us
  waiting for transfers between devices: 17.3 us -> 16.8 us
    ppermute x17, starting transfers between devices: 15.6 us -> 16.9 us  [partner(): lax.ppermute(block, axis, [(i, i ^ k) for i in range(lax.axis_size(axis))])]
    ppermute x17, waiting for transfers between devices: 11.1 us -> 10.6 us  [partner(): lax.ppermute(block, axis, [(i, i ^ k) for i in range(lax.axis_size(axis))])]
  transfers between devices with their start and end apart: 18 -> 18, of which waited for: 9 -> 10; matrix products, arithmetic and copies ran while one was open for 0% -> 0% of each run, Pallas kernels for 5% -> 5%
where the time goes in v15:
time: 47.7 us; the launch traced here: 47.4 us
  starting transfers between devices  22.8 us (48%)
  waiting for transfers between devices  16.8 us (35%)
  Pallas kernels  6.43 us (13%)
  between operations  1.38 us (3%)
    ppermute x17, starting transfers between devices, partner(): lax.ppermute(block, axis, [(i, i ^ k) for i in range(lax.axis_size(axis))])  16.9 us
    ppermute x17, waiting for transfers between devices, partner(): lax.ppermute(block, axis, [(i, i ^ k) for i in range(lax.axis_size(axis))])  10.6 us
    all_to_all x1, waiting for transfers between devices, exchange(): lax.all_to_all(blocks, 'dom', split_axis=0, concat_axis=0, axis_index_gro...  6.27 us
    all_to_all x1, starting transfers between devices, exchange(): lax.all_to_all(blocks, 'dom', split_axis=0, concat_axis=0, axis_index_gro...  5.83 us
    pallas_call x1, Pallas kernels, on_device(): pl.pallas_call(functools.partial(send_kernel, width), out_shape=(kept((pe...  2.22 us
    pallas_call x1, Pallas kernels, on_device(): pl.pallas_call(functools.partial(dense_kernel, slots, hub_here, feats, wi...  1.15 us
  transfers between devices with their start and end apart: 18, of which 10 were waited for; matrix products, arithmetic and copies ran while one was open for 0% of the time, Pallas kernels for 5%

profile of v15, /device:TPU:0, one launch (start us, length us, event | category | flops | bytes accessed | tf_op | source)
XLA Modules:
  0.0 47.4 jit_solution(4575055466937986993)
XLA Ops:
  0.6 2.2 %shard_map.173 = (bf16[8,64,128]{2,1,0:T(8,128)(2,1)}, bf16[1552,128]{1,0:T(8,128)(2,1)S(1)}, s32[1,8,48]{2,1,0:T(8,128)S(1)}, s32[1,2]{1,0:T(1,128)S(1)}, s32[1...) custom-call(bf16[256,128]{1,0:T(8,128)(2,1)} %x_ref.5, ...), custom_call_target="tpu_custom_call" | custom-call | tf_op jit(solution)/shard_map/pallas_call | solution.py:372
  2.9 3.0 %collective-permute-start.1 = (bf16[1552,128]{1,0:T(8,128)(2,1)S(1)}, bf16[1552,128]{1,0:T(8,128)(2,1)S(1)}, u32[]{:S(2)}, u32[]{:S(2)}) collective-permute-start(bf16[1552,128]{1,0:T(8,128)(2,1)S(1)} %get-tuple-element.45.refs_0_), channel_id=1, source_target_pairs={{0,2},{1,3},{2,0},{3,1},{4,6},{5,7},{6,4},{7,5},{8,10},{9,11},{10,... | collective-permute-start | bytes 1191944 | tf_op jit(solution)/shard_map/ppermute | solution.py:320
  5.9 5.8 %all-to-all-start = ((bf16[8,64,128]{2,1,0:T(8,128)(2,1)}), bf16[8,64,128]{2,1,0:T(8,128)(2,1)S(1)}, u32[]{:S(2)}, u32[]{:S(2)}) async-start(bf16[8,64,128]{2,1,0:T(8,128)(2,1)} %get-tuple-element.47), calls=%async_computation | async-start | bytes 262144 | tf_op jit(solution)/shard_map/all_to_all | solution.py:324
  12.4 0.4 shard_map.174
  12.8 6.3 %all-to-all-done.got_ref = bf16[8,64,128]{2,1,0:T(8,128)(2,1)S(1)} async-done(((bf16[8,64,128]{2,1,0:T(8,128)(2,1)}), bf16[8,64,128]{2,1,0:T(8,128)(2,1)S(1)}, u32[]{:S(2)}, u32[]{:S(2)}) %all-to-all-start) | async-done | bytes 131104 | tf_op jit(solution)/shard_map/all_to_all | solution.py:324
  19.1 0.3 shard_map.175
  19.4 0.6 %collective-permute-start.4 = (bf16[256,128]{1,0:T(8,128)(2,1)S(1)}, bf16[256,128]{1,0:T(8,128)(2,1)S(1)}, u32[]{:S(2)}, u32[]{:S(2)}) collective-permute-start(bf16[256,128]{1,0:T(8,128)(2,1)S(1)} %get-tuple-element.49.refs_4_), channel_id=1, source_target_pairs={{0,2},{1,3},{2,0},{3,1},{4,6},{5,7},{6,4},{7,5},{8,10},{9,11},{10,... | collective-permute-start | bytes 196616 | tf_op jit(solution)/shard_map/ppermute | solution.py:320
  20.0 0.2 collective-permute-start.3
  20.2 3.8 %collective-permute-done.4.refs_6_ = bf16[256,128]{1,0:T(8,128)(2,1)S(1)} collective-permute-done((bf16[256,128]{1,0:T(8,128)(2,1)S(1)}, bf16[256,128]{1,0:T(8,128)(2,1)S(1)}, u32[]{:S(2)}, u32[]{:S(2)}) %collective-permute-start.4) | collective-permute-done | bytes 65568 | tf_op jit(solution)/shard_map/ppermute | solution.py:320
  23.9 1.2 %collective-permute-done.5.refs_7_ = bf16[256,128]{1,0:T(8,128)(2,1)S(1)} collective-permute-done((bf16[256,128]{1,0:T(8,128)(2,1)S(1)}, bf16[256,128]{1,0:T(8,128)(2,1)S(1)}, u32[]{:S(2)}, u32[]{:S(2)}) %collective-permute-start.5) | collective-permute-done | bytes 65568 | tf_op jit(solution)/shard_map/ppermute | solution.py:320
  25.2 1.1 %shard_map.176 = (bf16[256,128]{1,0:T(8,128)(2,1)S(1)}, f32[256,128]{1,0:T(8,128)S(1)}, bf16[4,64,128]{2,1,0:T(8,128)(2,1)S(1)}, bf16[4,64,128]{2,1,0:T(8,128)(2...) custom-call(s32[1]{0:T(128)} %bitcast.me_ref, ...), custom_call_target="tpu_custom_call" | custom-call | tf_op jit(solution)/shard_map/pallas_call | solution.py:416
  26.3 0.5 collective-permute-start.6
  26.8 1.3 %collective-permute-start.10 = (bf16[256,128]{1,0:T(8,128)(2,1)S(1)}, bf16[256,128]{1,0:T(8,128)(2,1)S(1)}, u32[]{:S(2)}, u32[]{:S(2)}) collective-permute-start(bf16[256,128]{1,0:T(8,128)(2,1)S(1)} %get-tuple-element.60), channel_id=1, source_target_pairs={{0,12},{4,8},{8,4},{12,0},{16,28},{20,24},{24,20},{28,16},{1,13},{... | collective-permute-start | bytes 196616 | tf_op jit(solution)/shard_map/ppermute | solution.py:320
  28.0 0.4 collective-permute-start.11
  28.5 1.8 %collective-permute-start.12 = (bf16[256,128]{1,0:T(8,128)(2,1)S(1)}, bf16[256,128]{1,0:T(8,128)(2,1)S(1)}, u32[]{:S(2)}, u32[]{:S(2)}) collective-permute-start(bf16[256,128]{1,0:T(8,128)(2,1)S(1)} %get-tuple-element.62), channel_id=1, source_target_pairs={{0,4},{4,0},{8,12},{12,8},{16,20},{20,16},{24,28},{28,24},{1,5},{5... | collective-permute-start | bytes 196616 | tf_op jit(solution)/shard_map/ppermute | solution.py:320
  30.3 0.6 %shard_map.177.stored_ref = bf16[256,128]{1,0:T(8,128)(2,1)} custom-call(bf16[256,128]{1,0:T(8,128)(2,1)S(1)} %get-tuple-element.50.held_ref), custom_call_target="tpu_custom_call" | custom-call | flops 100000000 | bytes 1000000 | tf_op jit(solution)/shard_map/pallas_call | solution.py:437
  30.9 1.4 %collective-permute-done.6.mirror_ref = bf16[4,64,128]{2,1,0:T(8,128)(2,1)S(1)} collective-permute-done((bf16[4,64,128]{2,1,0:T(8,128)(2,1)S(1)}, bf16[4,64,128]{2,1,0:T(8,128)(2,1)S(1)}, u32[]{:S(2)}, u32[]{:S(2)}) %collective-permute-start.6) | collective-permute-done | bytes 65568 | tf_op jit(solution)/shard_map/ppermute | solution.py:320
  32.3 0.9 %collective-permute-done.10.refs_0_ = bf16[256,128]{1,0:T(8,128)(2,1)S(1)} collective-permute-done((bf16[256,128]{1,0:T(8,128)(2,1)S(1)}, bf16[256,128]{1,0:T(8,128)(2,1)S(1)}, u32[]{:S(2)}, u32[]{:S(2)}) %collective-permute-start.10) | collective-permute-done | bytes 65568 | tf_op jit(solution)/shard_map/ppermute | solution.py:320
  33.2 0.3 collective-permute-done.11.refs_1_
  33.6 2.1 %collective-permute-start.13 = (bf16[256,128]{1,0:T(8,128)(2,1)S(1)}, bf16[256,128]{1,0:T(8,128)(2,1)S(1)}, u32[]{:S(2)}, u32[]{:S(2)}) collective-permute-start(bf16[256,128]{1,0:T(8,128)(2,1)S(1)} %shard_map.180.own_ref), channel_id=1, source_target_pairs={{0,16},{4,20},{8,24},{12,28},{16,0},{20,4},{24,8},{28,12},{1,17},{... | collective-permute-start | bytes 196616 | tf_op jit(solution)/shard_map/ppermute | solution.py:320
  35.6 1.6 %collective-permute-start.7 = (bf16[128,128]{1,0:T(8,128)(2,1)S(1)}, bf16[128,128]{1,0:T(8,128)(2,1)S(1)}, u32[]{:S(2)}, u32[]{:S(2)}) collective-permute-start(bf16[128,128]{1,0:T(8,128)(2,1)S(1)} %get-tuple-element.56), channel_id=1, source_target_pairs={{0,4},{4,0},{8,12},{12,8},{16,20},{20,16},{24,28},{28,24},{1,5},{5... | collective-permute-start | bytes 98312 | tf_op jit(solution)/shard_map/ppermute | solution.py:320
  37.3 0.2 collective-permute-start.8
  37.5 1.7 %collective-permute-start.9 = (bf16[128,128]{1,0:T(8,128)(2,1)S(1)}, bf16[128,128]{1,0:T(8,128)(2,1)S(1)}, u32[]{:S(2)}, u32[]{:S(2)}) collective-permute-start(bf16[128,128]{1,0:T(8,128)(2,1)S(1)} %get-tuple-element.58), channel_id=1, source_target_pairs={{0,12},{4,8},{8,4},{12,0},{16,28},{20,24},{24,20},{28,16},{1,13},{... | collective-permute-start | bytes 98312 | tf_op jit(solution)/shard_map/ppermute | solution.py:320
  39.2 0.3 collective-permute-done.13.other_ref
  39.5 1.0 %collective-permute-start.16 = (bf16[256,128]{1,0:T(8,128)(2,1)S(1)}, bf16[256,128]{1,0:T(8,128)(2,1)S(1)}, u32[]{:S(2)}, u32[]{:S(2)}) collective-permute-start(bf16[256,128]{1,0:T(8,128)(2,1)S(1)} %shard_map.181.refs_0_), channel_id=1, source_target_pairs={{0,12},{4,8},{8,4},{12,0},{16,28},{20,24},{24,20},{28,16},{1,13},{... | collective-permute-start | bytes 196616 | tf_op jit(solution)/shard_map/ppermute | solution.py:320
  40.5 1.8 %collective-permute-start.15 = (bf16[256,128]{1,0:T(8,128)(2,1)S(1)}, bf16[256,128]{1,0:T(8,128)(2,1)S(1)}, u32[]{:S(2)}, u32[]{:S(2)}) collective-permute-start(bf16[256,128]{1,0:T(8,128)(2,1)S(1)} %shard_map.181.refs_0_), channel_id=1, source_target_pairs={{0,8},{4,12},{8,0},{12,4},{16,24},{20,28},{24,16},{28,20},{1,9},{5... | collective-permute-start | bytes 196616 | tf_op jit(solution)/shard_map/ppermute | solution.py:320
  42.3 0.8 %collective-permute-start.14 = (bf16[256,128]{1,0:T(8,128)(2,1)S(1)}, bf16[256,128]{1,0:T(8,128)(2,1)S(1)}, u32[]{:S(2)}, u32[]{:S(2)}) collective-permute-start(bf16[256,128]{1,0:T(8,128)(2,1)S(1)} %shard_map.181.refs_0_), channel_id=1, source_target_pairs={{0,4},{4,0},{8,12},{12,8},{16,20},{20,16},{24,28},{28,24},{1,5},{5... | collective-permute-start | bytes 196616 | tf_op jit(solution)/shard_map/ppermute | solution.py:320
  43.1 0.9 %shard_map.179 = (bf16[256,128]{1,0:T(8,128)(2,1)}, f32[1,128]{1,0:T(1,128)}) custom-call(s32[1]{0:T(128)} %bitcast.1.side_ref, s32[1]{0:T(128)} %bitcast.2.seat_ref, f32[256,128]{1,0:T(8,128)S(1)} %get-tuple-element.51.back_ref, bf16[256,512]{1,0:T(8,128)(2,1)S(1)} %get-tuple-element.52.mark_ref, bf16[128,128]{1,0:T(8,128)(2,1)S(1)} %get-tuple-element.55.refs_0_, ...), custom_call_target="tpu_custom_call" | custom-call | flops 2000000000 | bytes 1000000 | tf_op jit(solution)/shard_map/pallas_call | solution.py:469
  43.9 0.8 %collective-permute-done.16.refs_3_ = bf16[256,128]{1,0:T(8,128)(2,1)S(1)} collective-permute-done((bf16[256,128]{1,0:T(8,128)(2,1)S(1)}, bf16[256,128]{1,0:T(8,128)(2,1)S(1)}, u32[]{:S(2)}, u32[]{:S(2)}) %collective-permute-start.16) | collective-permute-done | bytes 65568 | tf_op jit(solution)/shard_map/ppermute | solution.py:320
  44.7 0.5 %collective-permute-done.15.refs_2_ = bf16[256,128]{1,0:T(8,128)(2,1)S(1)} collective-permute-done((bf16[256,128]{1,0:T(8,128)(2,1)S(1)}, bf16[256,128]{1,0:T(8,128)(2,1)S(1)}, u32[]{:S(2)}, u32[]{:S(2)}) %collective-permute-start.15) | collective-permute-done | bytes 65568 | tf_op jit(solution)/shard_map/ppermute | solution.py:320
  45.2 1.3 %collective-permute-done.14.refs_1_ = bf16[256,128]{1,0:T(8,128)(2,1)S(1)} collective-permute-done((bf16[256,128]{1,0:T(8,128)(2,1)S(1)}, bf16[256,128]{1,0:T(8,128)(2,1)S(1)}, u32[]{:S(2)}, u32[]{:S(2)}) %collective-permute-start.14) | collective-permute-done | bytes 65568 | tf_op jit(solution)/shard_map/ppermute | solution.py:320
  46.6 0.9 %shard_map.182 = (f32[128,512]{1,0:T(8,128)}, f32[128,512]{1,0:T(8,128)}) custom-call(s32[1]{0:T(128)} %bitcast.2.seat_ref, bf16[256,128]{1,0:T(8,128)(2,1)S(1)} %shard_map.181.refs_0_, bf16[256,128]{1,0:T(8,128)(2,1)S(1)} %collective-permute-done.14.refs_1_, bf16[256,128]{1,0:T(8,128)(2,1)S(1)} %collective-permute-done.15.refs_2_, ...), custom_call_target="tpu_custom_call" | custom-call | tf_op jit(solution)/shard_map/pallas_call | solution.py:478
  (20 shorter events, 0.2 us)
Async XLA Ops:
  2.9 16.2 %collective-permute-start.1 = (bf16[1552,128]{1,0:T(8,128)(2,1)S(1)}, bf16[1552,128]{1,0:T(8,128)(2,1)S(1)}, u32[]{:S(2)}, u32[]{:S(2)}) collective-permute-start(bf16[1552,128]{1,0:T(8,128)(2,1)S(1)} %get-tuple-element.45.refs_0_), channel_id=1, source_target_pairs={{0,2},{1,3},{2,0},{3,1},{4,6},{5,7},{6,4},{7,5},{8,10},{9,11},{10,... | collective-permute-start | bytes 1191944 | tf_op jit(solution)/shard_map/ppermute | solution.py:320
  5.9 13.2 %all-to-all-start = ((bf16[8,64,128]{2,1,0:T(8,128)(2,1)}), bf16[8,64,128]{2,1,0:T(8,128)(2,1)S(1)}, u32[]{:S(2)}, u32[]{:S(2)}) async-start(bf16[8,64,128]{2,1,0:T(8,128)(2,1)} %get-tuple-element.47), calls=%async_computation | async-start | bytes 262144 | tf_op jit(solution)/shard_map/all_to_all | solution.py:324
  11.7 12.2 %collective-permute-start = (bf16[1552,128]{1,0:T(8,128)(2,1)S(1)}, bf16[1552,128]{1,0:T(8,128)(2,1)S(1)}, u32[]{:S(2)}, u32[]{:S(2)}) collective-permute-start(bf16[1552,128]{1,0:T(8,128)(2,1)S(1)} %get-tuple-element.45.refs_0_), channel_id=1, source_target_pairs={{0,1},{1,0},{2,3},{3,2},{4,5},{5,4},{6,7},{7,6},{8,9},{9,8},{10,11... | collective-permute-start | bytes 1191944 | tf_op jit(solution)/shard_map/ppermute | solution.py:320
  12.4 6.7 %copy-start = (bf16[256,128]{1,0:T(8,128)(2,1)S(1)}, bf16[256,128]{1,0:T(8,128)(2,1)}, u32[]{:S(2)}) copy-start(bf16[256,128]{1,0:T(8,128)(2,1)} %x_ref.5) | copy-start | bytes 196612
  19.0 6.1 %copy-start.1 = (bf16[128,512]{1,0:T(8,128)(2,1)S(1)}, bf16[128,512]{1,0:T(8,128)(2,1)}, u32[]{:S(2)}) copy-start(bf16[128,512]{1,0:T(8,128)(2,1)} %ws_ref.3) | copy-start | bytes 393220
  19.1 6.1 %copy-start.2 = (bf16[128,512]{1,0:T(8,128)(2,1)S(1)}, bf16[128,512]{1,0:T(8,128)(2,1)}, u32[]{:S(2)}) copy-start(bf16[128,512]{1,0:T(8,128)(2,1)} %wn_ref.3) | copy-start | bytes 393220
  19.3 5.8 %collective-permute-start.2 = (bf16[1552,128]{1,0:T(8,128)(2,1)S(1)}, bf16[1552,128]{1,0:T(8,128)(2,1)S(1)}, u32[]{:S(2)}, u32[]{:S(2)}) collective-permute-start(bf16[1552,128]{1,0:T(8,128)(2,1)S(1)} %get-tuple-element.48.refs_2_), channel_id=1, source_target_pairs={{0,1},{1,0},{2,3},{3,2},{4,5},{5,4},{6,7},{7,6},{8,9},{9,8},{10,11... | collective-permute-start | bytes 1191944 | tf_op jit(solution)/shard_map/ppermute | solution.py:320
  19.4 4.5 %collective-permute-start.4 = (bf16[256,128]{1,0:T(8,128)(2,1)S(1)}, bf16[256,128]{1,0:T(8,128)(2,1)S(1)}, u32[]{:S(2)}, u32[]{:S(2)}) collective-permute-start(bf16[256,128]{1,0:T(8,128)(2,1)S(1)} %get-tuple-element.49.refs_4_), channel_id=1, source_target_pairs={{0,2},{1,3},{2,0},{3,1},{4,6},{5,7},{6,4},{7,5},{8,10},{9,11},{10,... | collective-permute-start | bytes 196616 | tf_op jit(solution)/shard_map/ppermute | solution.py:320
  20.0 3.9 %collective-permute-start.3 = (bf16[256,128]{1,0:T(8,128)(2,1)S(1)}, bf16[256,128]{1,0:T(8,128)(2,1)S(1)}, u32[]{:S(2)}, u32[]{:S(2)}) collective-permute-start(bf16[256,128]{1,0:T(8,128)(2,1)S(1)} %get-tuple-element.49.refs_4_), channel_id=1, source_target_pairs={{0,1},{1,0},{2,3},{3,2},{4,5},{5,4},{6,7},{7,6},{8,9},{9,8},{10,11... | collective-permute-start | bytes 196616 | tf_op jit(solution)/shard_map/ppermute | solution.py:320
  23.9 1.3 %collective-permute-start.5 = (bf16[256,128]{1,0:T(8,128)(2,1)S(1)}, bf16[256,128]{1,0:T(8,128)(2,1)S(1)}, u32[]{:S(2)}, u32[]{:S(2)}) collective-permute-start(bf16[256,128]{1,0:T(8,128)(2,1)S(1)} %collective-permute-done.4.refs_6_), channel_id=1, source_target_pairs={{0,1},{1,0},{2,3},{3,2},{4,5},{5,4},{6,7},{7,6},{8,9},{9,8},{10,11... | collective-permute-start | bytes 196616 | tf_op jit(solution)/shard_map/ppermute | solution.py:320
  26.3 5.9 %collective-permute-start.6 = (bf16[4,64,128]{2,1,0:T(8,128)(2,1)S(1)}, bf16[4,64,128]{2,1,0:T(8,128)(2,1)S(1)}, u32[]{:S(2)}, u32[]{:S(2)}) collective-permute-start(bf16[4,64,128]{2,1,0:T(8,128)(2,1)S(1)} %get-tuple-element.54), channel_id=1, source_target_pairs={{0,16},{4,20},{8,24},{12,28},{16,0},{20,4},{24,8},{28,12},{1,17},{... | collective-permute-start | bytes 196616 | tf_op jit(solution)/shard_map/ppermute | solution.py:320
  26.8 6.4 %collective-permute-start.10 = (bf16[256,128]{1,0:T(8,128)(2,1)S(1)}, bf16[256,128]{1,0:T(8,128)(2,1)S(1)}, u32[]{:S(2)}, u32[]{:S(2)}) collective-permute-start(bf16[256,128]{1,0:T(8,128)(2,1)S(1)} %get-tuple-element.60), channel_id=1, source_target_pairs={{0,12},{4,8},{8,4},{12,0},{16,28},{20,24},{24,20},{28,16},{1,13},{... | collective-permute-start | bytes 196616 | tf_op jit(solution)/shard_map/ppermute | solution.py:320
  28.0 5.5 %collective-permute-start.11 = (bf16[256,128]{1,0:T(8,128)(2,1)S(1)}, bf16[256,128]{1,0:T(8,128)(2,1)S(1)}, u32[]{:S(2)}, u32[]{:S(2)}) collective-permute-start(bf16[256,128]{1,0:T(8,128)(2,1)S(1)} %get-tuple-element.61), channel_id=1, source_target_pairs={{0,8},{4,12},{8,0},{12,4},{16,24},{20,28},{24,16},{28,20},{1,9},{5... | collective-permute-start | bytes 196616 | tf_op jit(solution)/shard_map/ppermute | solution.py:320
  28.5 5.1 %collective-permute-start.12 = (bf16[256,128]{1,0:T(8,128)(2,1)S(1)}, bf16[256,128]{1,0:T(8,128)(2,1)S(1)}, u32[]{:S(2)}, u32[]{:S(2)}) collective-permute-start(bf16[256,128]{1,0:T(8,128)(2,1)S(1)} %get-tuple-element.62), channel_id=1, source_target_pairs={{0,4},{4,0},{8,12},{12,8},{16,20},{20,16},{24,28},{28,24},{1,5},{5... | collective-permute-start | bytes 196616 | tf_op jit(solution)/shard_map/ppermute | solution.py:320
  33.6 5.9 %collective-permute-start.13 = (bf16[256,128]{1,0:T(8,128)(2,1)S(1)}, bf16[256,128]{1,0:T(8,128)(2,1)S(1)}, u32[]{:S(2)}, u32[]{:S(2)}) collective-permute-start(bf16[256,128]{1,0:T(8,128)(2,1)S(1)} %shard_map.180.own_ref), channel_id=1, source_target_pairs={{0,16},{4,20},{8,24},{12,28},{16,0},{20,4},{24,8},{28,12},{1,17},{... | collective-permute-start | bytes 196616 | tf_op jit(solution)/shard_map/ppermute | solution.py:320
  35.6 6.7 %collective-permute-start.7 = (bf16[128,128]{1,0:T(8,128)(2,1)S(1)}, bf16[128,128]{1,0:T(8,128)(2,1)S(1)}, u32[]{:S(2)}, u32[]{:S(2)}) collective-permute-start(bf16[128,128]{1,0:T(8,128)(2,1)S(1)} %get-tuple-element.56), channel_id=1, source_target_pairs={{0,4},{4,0},{8,12},{12,8},{16,20},{20,16},{24,28},{28,24},{1,5},{5... | collective-permute-start | bytes 98312 | tf_op jit(solution)/shard_map/ppermute | solution.py:320
  37.3 5.8 %collective-permute-start.8 = (bf16[128,128]{1,0:T(8,128)(2,1)S(1)}, bf16[128,128]{1,0:T(8,128)(2,1)S(1)}, u32[]{:S(2)}, u32[]{:S(2)}) collective-permute-start(bf16[128,128]{1,0:T(8,128)(2,1)S(1)} %get-tuple-element.57), channel_id=1, source_target_pairs={{0,8},{4,12},{8,0},{12,4},{16,24},{20,28},{24,16},{28,20},{1,9},{5... | collective-permute-start | bytes 98312 | tf_op jit(solution)/shard_map/ppermute | solution.py:320
  37.5 5.6 %collective-permute-start.9 = (bf16[128,128]{1,0:T(8,128)(2,1)S(1)}, bf16[128,128]{1,0:T(8,128)(2,1)S(1)}, u32[]{:S(2)}, u32[]{:S(2)}) collective-permute-start(bf16[128,128]{1,0:T(8,128)(2,1)S(1)} %get-tuple-element.58), channel_id=1, source_target_pairs={{0,12},{4,8},{8,4},{12,0},{16,28},{20,24},{24,20},{28,16},{1,13},{... | collective-permute-start | bytes 98312 | tf_op jit(solution)/shard_map/ppermute | solution.py:320
  39.5 5.2 %collective-permute-start.16 = (bf16[256,128]{1,0:T(8,128)(2,1)S(1)}, bf16[256,128]{1,0:T(8,128)(2,1)S(1)}, u32[]{:S(2)}, u32[]{:S(2)}) collective-permute-start(bf16[256,128]{1,0:T(8,128)(2,1)S(1)} %shard_map.181.refs_0_), channel_id=1, source_target_pairs={{0,12},{4,8},{8,4},{12,0},{16,28},{20,24},{24,20},{28,16},{1,13},{... | collective-permute-start | bytes 196616 | tf_op jit(solution)/shard_map/ppermute | solution.py:320
  40.5 4.8 %collective-permute-start.15 = (bf16[256,128]{1,0:T(8,128)(2,1)S(1)}, bf16[256,128]{1,0:T(8,128)(2,1)S(1)}, u32[]{:S(2)}, u32[]{:S(2)}) collective-permute-start(bf16[256,128]{1,0:T(8,128)(2,1)S(1)} %shard_map.181.refs_0_), channel_id=1, source_target_pairs={{0,8},{4,12},{8,0},{12,4},{16,24},{20,28},{24,16},{28,20},{1,9},{5... | collective-permute-start | bytes 196616 | tf_op jit(solution)/shard_map/ppermute | solution.py:320
  42.3 4.3 %collective-permute-start.14 = (bf16[256,128]{1,0:T(8,128)(2,1)S(1)}, bf16[256,128]{1,0:T(8,128)(2,1)S(1)}, u32[]{:S(2)}, u32[]{:S(2)}) collective-permute-start(bf16[256,128]{1,0:T(8,128)(2,1)S(1)} %shard_map.181.refs_0_), channel_id=1, source_target_pairs={{0,4},{4,0},{8,12},{12,8},{16,20},{20,16},{24,28},{28,24},{1,5},{5... | collective-permute-start | bytes 196616 | tf_op jit(solution)/shard_map/ppermute | solution.py:320

commit v16 on v14

--- a/solution.py
+++ b/solution.py
@@ -277,16 +277,9 @@
     bias_ref[...] = (near_bias + far_bias) * scale
 
 
-def spread_kernel(scale, seat_ref, *refs):
-    got_refs, (self_ref, neigh_ref, wide_ref, sems) = refs[:-4], refs[-4:]
+def write_blocks(scale, parts, self_ref, neigh_ref, wide_ref, sems):
     depth, full = self_ref.shape
-    cols = got_refs[0].shape[-1]
-    blocks = full // cols
-    if len(got_refs) > 1:
-        parts = [(j, ref[...]) for j, ref in seated(got_refs, seat_ref[0])]
-    else:
-        whole = got_refs[0][...].reshape(2 * blocks * depth, cols)
-        parts = [(j, whole[2 * j * depth : 2 * (j + 1) * depth]) for j in range(blocks)]
+    cols = wide_ref.shape[-1]
     copies = []
     for at, (j, part) in enumerate(parts):
         wide_ref[at] = part.astype(F32) * scale
@@ -299,6 +292,22 @@
             copies.append(copy)
     for copy in copies:
         copy.wait()
+
+
+def spread_kernel(scale, seat_ref, *refs):
+    got_refs, (self_ref, neigh_ref, wide_ref, sems) = refs[:-4], refs[-4:]
+    depth, full = self_ref.shape
+    cols = wide_ref.shape[-1]
+    if len(got_refs) > 1:
+        parts = [(j, ref[...]) for j, ref in seated(got_refs, seat_ref[0])]
+    else:
+        whole = got_refs[0][...].reshape(2 * full // cols * depth, cols)
+        parts = [(j, whole[2 * j * depth : 2 * (j + 1) * depth]) for j in range(full // cols)]
+    write_blocks(scale, parts, self_ref, neigh_ref, wide_ref, sems)
+
+
+def finish_kernel(scale, k, seat_ref, got_ref, begun_self_ref, begun_neigh_ref, self_ref, neigh_ref, wide_ref, sems):
+    write_blocks(scale, [(seat_ref[0] ^ k, got_ref[...])], self_ref, neigh_ref, wide_ref, sems)
 
 
 VMEM = pl.BlockSpec(memory_space=pltpu.VMEM)
@@ -475,14 +484,25 @@
         compiler_params=PARAMS,
         cost_estimate=pl.CostEstimate(flops=2 * 10**9, bytes_accessed=10**6, transcendentals=0),
     )(side, seat, back, mark, *dealt)
+    early = half - 1 if direct else 1
     grad_self, grad_neigh = pl.pallas_call(
         functools.partial(spread_kernel, scale),
         out_shape=(shape((depth, full), F32), shape((depth, full), F32)),
-        in_specs=[SMEM] + [VMEM] * count,
+        in_specs=[SMEM] + [VMEM] * early,
         out_specs=(HBM,) * 2,
         scratch_shapes=[pltpu.VMEM((blocks, 2 * depth, cols), F32), pltpu.SemaphoreType.DMA((2 * blocks,))],
         compiler_params=PARAMS,
-    )(seat, *parts)
+    )(seat, *parts[:early])
+    if direct:
+        grad_self, grad_neigh = pl.pallas_call(
+            functools.partial(finish_kernel, scale, early),
+            out_shape=(shape((depth, full), F32), shape((depth, full), F32)),
+            in_specs=[SMEM, VMEM, HBM, HBM],
+            out_specs=(HBM,) * 2,
+            scratch_shapes=[pltpu.VMEM((1, 2 * depth, cols), F32), pltpu.SemaphoreType.DMA((2,))],
+            input_output_aliases={2: 0, 3: 1},
+            compiler_params=PARAMS,
+        )(seat, parts[early], *pinned(grad_self, grad_neigh))
     return output, grad_features, grad_self, grad_neigh, grad_bias.reshape(cols)
 
 

time: 46.9 us -> 46.3 us (0.987)
  waiting for transfers between devices: 17.3 us -> 16.1 us
  Pallas kernels: 6.43 us -> 7.07 us
    ppermute x17, waiting for transfers between devices: 11.1 us -> 9.83 us  [partner(): lax.ppermute(block, axis, [(i, i ^ k) for i in range(lax.axis_size(axis))])]
    pallas_call x0 -> x1, Pallas kernels: none -> 0.68 us  [on_device(): pl.pallas_call(functools.partial(finish_kernel, scale, early), out_shape=...]
  transfers between devices with their start and end apart: 18 -> 18, of which waited for: 9 -> 8; matrix products, arithmetic and copies ran while one was open for 0% -> 0% of each run, Pallas kernels for 5% -> 7%
where the time goes in v16:
time: 46.3 us; the launch traced here: 46 us
  starting transfers between devices  21.4 us (46%)
  waiting for transfers between devices  16.1 us (35%)
  Pallas kernels  7.07 us (15%)
  between operations  1.39 us (3%)
    ppermute x17, starting transfers between devices, partner(): lax.ppermute(block, axis, [(i, i ^ k) for i in range(lax.axis_size(axis))])  15.6 us
    ppermute x17, waiting for transfers between devices, partner(): lax.ppermute(block, axis, [(i, i ^ k) for i in range(lax.axis_size(axis))])  9.83 us
    all_to_all x1, waiting for transfers between devices, exchange(): lax.all_to_all(blocks, 'dom', split_axis=0, concat_axis=0, axis_index_gro...  6.27 us
    all_to_all x1, starting transfers between devices, exchange(): lax.all_to_all(blocks, 'dom', split_axis=0, concat_axis=0, axis_index_gro...  5.83 us
    pallas_call x1, Pallas kernels, on_device(): pl.pallas_call(functools.partial(send_kernel, width), out_shape=(kept((pe...  2.22 us
    pallas_call x1, Pallas kernels, on_device(): pl.pallas_call(functools.partial(dense_kernel, slots, hub_here, feats, wi...  1.15 us
  transfers between devices with their start and end apart: 18, of which 8 were waited for; matrix products, arithmetic and copies ran while one was open for 0% of the time, Pallas kernels for 7%

profile of v16, /device:TPU:0, one launch (start us, length us, event | category | flops | bytes accessed | tf_op | source)
XLA Modules:
  0.0 46.0 jit_solution(4539234591489084173)
XLA Ops:
  0.6 2.2 %shard_map.173 = (bf16[8,64,128]{2,1,0:T(8,128)(2,1)}, bf16[1552,128]{1,0:T(8,128)(2,1)S(1)}, s32[1,8,48]{2,1,0:T(8,128)S(1)}, s32[1,2]{1,0:T(1,128)S(1)}, s32[1...) custom-call(bf16[256,128]{1,0:T(8,128)(2,1)} %x_ref.5, ...), custom_call_target="tpu_custom_call" | custom-call | tf_op jit(solution)/shard_map/pallas_call | solution.py:381
  2.9 3.0 %collective-permute-start.1 = (bf16[1552,128]{1,0:T(8,128)(2,1)S(1)}, bf16[1552,128]{1,0:T(8,128)(2,1)S(1)}, u32[]{:S(2)}, u32[]{:S(2)}) collective-permute-start(bf16[1552,128]{1,0:T(8,128)(2,1)S(1)} %get-tuple-element.47.refs_0_), channel_id=1, source_target_pairs={{0,2},{1,3},{2,0},{3,1},{4,6},{5,7},{6,4},{7,5},{8,10},{9,11},{10,... | collective-permute-start | bytes 1191944 | tf_op jit(solution)/shard_map/ppermute | solution.py:329
  5.9 5.8 %all-to-all-start = ((bf16[8,64,128]{2,1,0:T(8,128)(2,1)}), bf16[8,64,128]{2,1,0:T(8,128)(2,1)S(1)}, u32[]{:S(2)}, u32[]{:S(2)}) async-start(bf16[8,64,128]{2,1,0:T(8,128)(2,1)} %get-tuple-element.49), calls=%async_computation | async-start | bytes 262144 | tf_op jit(solution)/shard_map/all_to_all | solution.py:333
  12.4 0.4 shard_map.174
  12.8 6.3 %all-to-all-done.got_ref = bf16[8,64,128]{2,1,0:T(8,128)(2,1)S(1)} async-done(((bf16[8,64,128]{2,1,0:T(8,128)(2,1)}), bf16[8,64,128]{2,1,0:T(8,128)(2,1)S(1)}, u32[]{:S(2)}, u32[]{:S(2)}) %all-to-all-start) | async-done | bytes 131104 | tf_op jit(solution)/shard_map/all_to_all | solution.py:333
  19.1 0.3 shard_map.175
  19.3 0.1 collective-permute-start.2
  19.4 0.6 %collective-permute-start.4 = (bf16[256,128]{1,0:T(8,128)(2,1)S(1)}, bf16[256,128]{1,0:T(8,128)(2,1)S(1)}, u32[]{:S(2)}, u32[]{:S(2)}) collective-permute-start(bf16[256,128]{1,0:T(8,128)(2,1)S(1)} %get-tuple-element.51.refs_4_), channel_id=1, source_target_pairs={{0,2},{1,3},{2,0},{3,1},{4,6},{5,7},{6,4},{7,5},{8,10},{9,11},{10,... | collective-permute-start | bytes 196616 | tf_op jit(solution)/shard_map/ppermute | solution.py:329
  20.0 0.2 collective-permute-start.3
  20.2 3.8 %collective-permute-done.4.refs_6_ = bf16[256,128]{1,0:T(8,128)(2,1)S(1)} collective-permute-done((bf16[256,128]{1,0:T(8,128)(2,1)S(1)}, bf16[256,128]{1,0:T(8,128)(2,1)S(1)}, u32[]{:S(2)}, u32[]{:S(2)}) %collective-permute-start.4) | collective-permute-done | bytes 65568 | tf_op jit(solution)/shard_map/ppermute | solution.py:329
  23.9 1.2 %collective-permute-done.5.refs_7_ = bf16[256,128]{1,0:T(8,128)(2,1)S(1)} collective-permute-done((bf16[256,128]{1,0:T(8,128)(2,1)S(1)}, bf16[256,128]{1,0:T(8,128)(2,1)S(1)}, u32[]{:S(2)}, u32[]{:S(2)}) %collective-permute-start.5) | collective-permute-done | bytes 65568 | tf_op jit(solution)/shard_map/ppermute | solution.py:329
  25.2 1.1 %shard_map.176 = (bf16[256,128]{1,0:T(8,128)(2,1)S(1)}, f32[256,128]{1,0:T(8,128)S(1)}, bf16[4,64,128]{2,1,0:T(8,128)(2,1)S(1)}, bf16[4,64,128]{2,1,0:T(8,128)(2...) custom-call(s32[1]{0:T(128)} %bitcast.me_ref, ...), custom_call_target="tpu_custom_call" | custom-call | tf_op jit(solution)/shard_map/pallas_call | solution.py:425
  26.3 0.8 %collective-permute-start.10 = (bf16[256,128]{1,0:T(8,128)(2,1)S(1)}, bf16[256,128]{1,0:T(8,128)(2,1)S(1)}, u32[]{:S(2)}, u32[]{:S(2)}) collective-permute-start(bf16[256,128]{1,0:T(8,128)(2,1)S(1)} %get-tuple-element.62), channel_id=1, source_target_pairs={{0,12},{4,8},{8,4},{12,0},{16,28},{20,24},{24,20},{28,16},{1,13},{... | collective-permute-start | bytes 196616 | tf_op jit(solution)/shard_map/ppermute | solution.py:329
  27.1 0.9 %collective-permute-start.11 = (bf16[256,128]{1,0:T(8,128)(2,1)S(1)}, bf16[256,128]{1,0:T(8,128)(2,1)S(1)}, u32[]{:S(2)}, u32[]{:S(2)}) collective-permute-start(bf16[256,128]{1,0:T(8,128)(2,1)S(1)} %get-tuple-element.63), channel_id=1, source_target_pairs={{0,8},{4,12},{8,0},{12,4},{16,24},{20,28},{24,16},{28,20},{1,9},{5... | collective-permute-start | bytes 196616 | tf_op jit(solution)/shard_map/ppermute | solution.py:329
  28.1 1.8 %collective-permute-start.12 = (bf16[256,128]{1,0:T(8,128)(2,1)S(1)}, bf16[256,128]{1,0:T(8,128)(2,1)S(1)}, u32[]{:S(2)}, u32[]{:S(2)}) collective-permute-start(bf16[256,128]{1,0:T(8,128)(2,1)S(1)} %get-tuple-element.64), channel_id=1, source_target_pairs={{0,4},{4,0},{8,12},{12,8},{16,20},{20,16},{24,28},{28,24},{1,5},{5... | collective-permute-start | bytes 196616 | tf_op jit(solution)/shard_map/ppermute | solution.py:329
  29.9 0.4 collective-permute-start.6
  30.3 0.6 %shard_map.177.stored_ref = bf16[256,128]{1,0:T(8,128)(2,1)} custom-call(bf16[256,128]{1,0:T(8,128)(2,1)S(1)} %get-tuple-element.52.held_ref), custom_call_target="tpu_custom_call" | custom-call | flops 100000000 | bytes 1000000 | tf_op jit(solution)/shard_map/pallas_call | solution.py:446
  30.9 1.2 %collective-permute-done.10.refs_0_ = bf16[256,128]{1,0:T(8,128)(2,1)S(1)} collective-permute-done((bf16[256,128]{1,0:T(8,128)(2,1)S(1)}, bf16[256,128]{1,0:T(8,128)(2,1)S(1)}, u32[]{:S(2)}, u32[]{:S(2)}) %collective-permute-start.10) | collective-permute-done | bytes 65568 | tf_op jit(solution)/shard_map/ppermute | solution.py:329
  32.2 0.7 %collective-permute-done.12.refs_2_ = bf16[256,128]{1,0:T(8,128)(2,1)S(1)} collective-permute-done((bf16[256,128]{1,0:T(8,128)(2,1)S(1)}, bf16[256,128]{1,0:T(8,128)(2,1)S(1)}, u32[]{:S(2)}, u32[]{:S(2)}) %collective-permute-start.12) | collective-permute-done | bytes 65568 | tf_op jit(solution)/shard_map/ppermute | solution.py:329
  32.9 0.7 %collective-permute-start.13 = (bf16[256,128]{1,0:T(8,128)(2,1)S(1)}, bf16[256,128]{1,0:T(8,128)(2,1)S(1)}, u32[]{:S(2)}, u32[]{:S(2)}) collective-permute-start(bf16[256,128]{1,0:T(8,128)(2,1)S(1)} %shard_map.180.own_ref), channel_id=1, source_target_pairs={{0,16},{4,20},{8,24},{12,28},{16,0},{20,4},{24,8},{28,12},{1,17},{... | collective-permute-start | bytes 196616 | tf_op jit(solution)/shard_map/ppermute | solution.py:329
  33.6 1.6 %collective-permute-done.6.mirror_ref = bf16[4,64,128]{2,1,0:T(8,128)(2,1)S(1)} collective-permute-done((bf16[4,64,128]{2,1,0:T(8,128)(2,1)S(1)}, bf16[4,64,128]{2,1,0:T(8,128)(2,1)S(1)}, u32[]{:S(2)}, u32[]{:S(2)}) %collective-permute-start.6) | collective-permute-done | bytes 65568 | tf_op jit(solution)/shard_map/ppermute | solution.py:329
  35.2 0.8 %collective-permute-start.7 = (bf16[128,128]{1,0:T(8,128)(2,1)S(1)}, bf16[128,128]{1,0:T(8,128)(2,1)S(1)}, u32[]{:S(2)}, u32[]{:S(2)}) collective-permute-start(bf16[128,128]{1,0:T(8,128)(2,1)S(1)} %get-tuple-element.58), channel_id=1, source_target_pairs={{0,4},{4,0},{8,12},{12,8},{16,20},{20,16},{24,28},{28,24},{1,5},{5... | collective-permute-start | bytes 98312 | tf_op jit(solution)/shard_map/ppermute | solution.py:329
  36.0 0.5 %collective-permute-start.8 = (bf16[128,128]{1,0:T(8,128)(2,1)S(1)}, bf16[128,128]{1,0:T(8,128)(2,1)S(1)}, u32[]{:S(2)}, u32[]{:S(2)}) collective-permute-start(bf16[128,128]{1,0:T(8,128)(2,1)S(1)} %get-tuple-element.59), channel_id=1, source_target_pairs={{0,8},{4,12},{8,0},{12,4},{16,24},{20,28},{24,16},{28,20},{1,9},{5... | collective-permute-start | bytes 98312 | tf_op jit(solution)/shard_map/ppermute | solution.py:329
  36.5 2.3 %collective-permute-start.9 = (bf16[128,128]{1,0:T(8,128)(2,1)S(1)}, bf16[128,128]{1,0:T(8,128)(2,1)S(1)}, u32[]{:S(2)}, u32[]{:S(2)}) collective-permute-start(bf16[128,128]{1,0:T(8,128)(2,1)S(1)} %get-tuple-element.60), channel_id=1, source_target_pairs={{0,12},{4,8},{8,4},{12,0},{16,28},{20,24},{24,20},{28,16},{1,13},{... | collective-permute-start | bytes 98312 | tf_op jit(solution)/shard_map/ppermute | solution.py:329
  38.8 0.3 collective-permute-start.16
  39.1 1.0 %collective-permute-start.15 = (bf16[256,128]{1,0:T(8,128)(2,1)S(1)}, bf16[256,128]{1,0:T(8,128)(2,1)S(1)}, u32[]{:S(2)}, u32[]{:S(2)}) collective-permute-start(bf16[256,128]{1,0:T(8,128)(2,1)S(1)} %shard_map.181.refs_0_), channel_id=1, source_target_pairs={{0,4},{4,0},{8,12},{12,8},{16,20},{20,16},{24,28},{28,24},{1,5},{5... | collective-permute-start | bytes 196616 | tf_op jit(solution)/shard_map/ppermute | solution.py:329
  40.1 2.3 %collective-permute-start.14 = (bf16[256,128]{1,0:T(8,128)(2,1)S(1)}, bf16[256,128]{1,0:T(8,128)(2,1)S(1)}, u32[]{:S(2)}, u32[]{:S(2)}) collective-permute-start(bf16[256,128]{1,0:T(8,128)(2,1)S(1)} %shard_map.181.refs_0_), channel_id=1, source_target_pairs={{0,12},{4,8},{8,4},{12,0},{16,28},{20,24},{24,20},{28,16},{1,13},{... | collective-permute-start | bytes 196616 | tf_op jit(solution)/shard_map/ppermute | solution.py:329
  42.4 0.9 %shard_map.179 = (bf16[256,128]{1,0:T(8,128)(2,1)}, f32[1,128]{1,0:T(1,128)}) custom-call(s32[1]{0:T(128)} %bitcast.1.side_ref, s32[1]{0:T(128)} %bitcast.2.seat_ref, f32[256,128]{1,0:T(8,128)S(1)} %get-tuple-element.53.back_ref, bf16[256,512]{1,0:T(8,128)(2,1)S(1)} %get-tuple-element.54.mark_ref, bf16[128,128]{1,0:T(8,128)(2,1)S(1)} %get-tuple-element.57.refs_0_, ...), custom_call_target="tpu_custom_call" | custom-call | flops 2000000000 | bytes 1000000 | tf_op jit(solution)/shard_map/pallas_call | solution.py:478
  43.3 0.1 collective-permute-done.15.refs_1_
  43.4 0.8 %shard_map.182 = (f32[128,512]{1,0:T(8,128)}, f32[128,512]{1,0:T(8,128)}) custom-call(s32[1]{0:T(128)} %bitcast.2.seat_ref, bf16[256,128]{1,0:T(8,128)(2,1)S(1)} %shard_map.181.refs_0_, bf16[256,128]{1,0:T(8,128)(2,1)S(1)} %collective-permute-done.15.refs_1_, bf16[256,128]{1,0:T(8,128)(2,1)S(1)} %collective-permute-done.16.refs_2_), custom_call_target="tpu_custom_call" | custom-call | tf_op jit(solution)/shard_map/pallas_call | solution.py:488
  44.2 1.1 %collective-permute-done.14.got_ref = bf16[256,128]{1,0:T(8,128)(2,1)S(1)} collective-permute-done((bf16[256,128]{1,0:T(8,128)(2,1)S(1)}, bf16[256,128]{1,0:T(8,128)(2,1)S(1)}, u32[]{:S(2)}, u32[]{:S(2)}) %collective-permute-start.14) | collective-permute-done | bytes 65568 | tf_op jit(solution)/shard_map/ppermute | solution.py:329
  45.3 0.7 %shard_map.183 = (f32[128,512]{1,0:T(8,128)}, f32[128,512]{1,0:T(8,128)}) custom-call(s32[1]{0:T(128)} %bitcast.2.seat_ref, bf16[256,128]{1,0:T(8,128)(2,1)S(1)} %collective-permute-done.14.got_ref, f32[128,512]{1,0:T(8,128)} %get-tuple-element.66.begun_self_ref, ...), custom_call_target="tpu_custom_call", output_to_operand_aliasing={{0}: (2, {}), {1}: (3, {})} | custom-call | tf_op jit(solution)/shard_map/pallas_call | solution.py:497
  (21 shorter events, 0.1 us)
Async XLA Ops:
  2.9 16.2 %collective-permute-start.1 = (bf16[1552,128]{1,0:T(8,128)(2,1)S(1)}, bf16[1552,128]{1,0:T(8,128)(2,1)S(1)}, u32[]{:S(2)}, u32[]{:S(2)}) collective-permute-start(bf16[1552,128]{1,0:T(8,128)(2,1)S(1)} %get-tuple-element.47.refs_0_), channel_id=1, source_target_pairs={{0,2},{1,3},{2,0},{3,1},{4,6},{5,7},{6,4},{7,5},{8,10},{9,11},{10,... | collective-permute-start | bytes 1191944 | tf_op jit(solution)/shard_map/ppermute | solution.py:329
  5.9 13.2 %all-to-all-start = ((bf16[8,64,128]{2,1,0:T(8,128)(2,1)}), bf16[8,64,128]{2,1,0:T(8,128)(2,1)S(1)}, u32[]{:S(2)}, u32[]{:S(2)}) async-start(bf16[8,64,128]{2,1,0:T(8,128)(2,1)} %get-tuple-element.49), calls=%async_computation | async-start | bytes 262144 | tf_op jit(solution)/shard_map/all_to_all | solution.py:333
  11.7 12.2 %collective-permute-start = (bf16[1552,128]{1,0:T(8,128)(2,1)S(1)}, bf16[1552,128]{1,0:T(8,128)(2,1)S(1)}, u32[]{:S(2)}, u32[]{:S(2)}) collective-permute-start(bf16[1552,128]{1,0:T(8,128)(2,1)S(1)} %get-tuple-element.47.refs_0_), channel_id=1, source_target_pairs={{0,1},{1,0},{2,3},{3,2},{4,5},{5,4},{6,7},{7,6},{8,9},{9,8},{10,11... | collective-permute-start | bytes 1191944 | tf_op jit(solution)/shard_map/ppermute | solution.py:329
  12.4 6.7 %copy-start = (bf16[256,128]{1,0:T(8,128)(2,1)S(1)}, bf16[256,128]{1,0:T(8,128)(2,1)}, u32[]{:S(2)}) copy-start(bf16[256,128]{1,0:T(8,128)(2,1)} %x_ref.5) | copy-start | bytes 196612
  19.0 6.1 %copy-start.1 = (bf16[128,512]{1,0:T(8,128)(2,1)S(1)}, bf16[128,512]{1,0:T(8,128)(2,1)}, u32[]{:S(2)}) copy-start(bf16[128,512]{1,0:T(8,128)(2,1)} %ws_ref.3) | copy-start | bytes 393220
  19.1 6.1 %copy-start.2 = (bf16[128,512]{1,0:T(8,128)(2,1)S(1)}, bf16[128,512]{1,0:T(8,128)(2,1)}, u32[]{:S(2)}) copy-start(bf16[128,512]{1,0:T(8,128)(2,1)} %wn_ref.3) | copy-start | bytes 393220
  19.3 5.8 %collective-permute-start.2 = (bf16[1552,128]{1,0:T(8,128)(2,1)S(1)}, bf16[1552,128]{1,0:T(8,128)(2,1)S(1)}, u32[]{:S(2)}, u32[]{:S(2)}) collective-permute-start(bf16[1552,128]{1,0:T(8,128)(2,1)S(1)} %get-tuple-element.50.refs_2_), channel_id=1, source_target_pairs={{0,1},{1,0},{2,3},{3,2},{4,5},{5,4},{6,7},{7,6},{8,9},{9,8},{10,11... | collective-permute-start | bytes 1191944 | tf_op jit(solution)/shard_map/ppermute | solution.py:329
  19.4 4.5 %collective-permute-start.4 = (bf16[256,128]{1,0:T(8,128)(2,1)S(1)}, bf16[256,128]{1,0:T(8,128)(2,1)S(1)}, u32[]{:S(2)}, u32[]{:S(2)}) collective-permute-start(bf16[256,128]{1,0:T(8,128)(2,1)S(1)} %get-tuple-element.51.refs_4_), channel_id=1, source_target_pairs={{0,2},{1,3},{2,0},{3,1},{4,6},{5,7},{6,4},{7,5},{8,10},{9,11},{10,... | collective-permute-start | bytes 196616 | tf_op jit(solution)/shard_map/ppermute | solution.py:329
  20.0 3.9 %collective-permute-start.3 = (bf16[256,128]{1,0:T(8,128)(2,1)S(1)}, bf16[256,128]{1,0:T(8,128)(2,1)S(1)}, u32[]{:S(2)}, u32[]{:S(2)}) collective-permute-start(bf16[256,128]{1,0:T(8,128)(2,1)S(1)} %get-tuple-element.51.refs_4_), channel_id=1, source_target_pairs={{0,1},{1,0},{2,3},{3,2},{4,5},{5,4},{6,7},{7,6},{8,9},{9,8},{10,11... | collective-permute-start | bytes 196616 | tf_op jit(solution)/shard_map/ppermute | solution.py:329
  23.9 1.3 %collective-permute-start.5 = (bf16[256,128]{1,0:T(8,128)(2,1)S(1)}, bf16[256,128]{1,0:T(8,128)(2,1)S(1)}, u32[]{:S(2)}, u32[]{:S(2)}) collective-permute-start(bf16[256,128]{1,0:T(8,128)(2,1)S(1)} %collective-permute-done.4.refs_6_), channel_id=1, source_target_pairs={{0,1},{1,0},{2,3},{3,2},{4,5},{5,4},{6,7},{7,6},{8,9},{9,8},{10,11... | collective-permute-start | bytes 196616 | tf_op jit(solution)/shard_map/ppermute | solution.py:329
  26.3 5.8 %collective-permute-start.10 = (bf16[256,128]{1,0:T(8,128)(2,1)S(1)}, bf16[256,128]{1,0:T(8,128)(2,1)S(1)}, u32[]{:S(2)}, u32[]{:S(2)}) collective-permute-start(bf16[256,128]{1,0:T(8,128)(2,1)S(1)} %get-tuple-element.62), channel_id=1, source_target_pairs={{0,12},{4,8},{8,4},{12,0},{16,28},{20,24},{24,20},{28,16},{1,13},{... | collective-permute-start | bytes 196616 | tf_op jit(solution)/shard_map/ppermute | solution.py:329
  27.1 5.0 %collective-permute-start.11 = (bf16[256,128]{1,0:T(8,128)(2,1)S(1)}, bf16[256,128]{1,0:T(8,128)(2,1)S(1)}, u32[]{:S(2)}, u32[]{:S(2)}) collective-permute-start(bf16[256,128]{1,0:T(8,128)(2,1)S(1)} %get-tuple-element.63), channel_id=1, source_target_pairs={{0,8},{4,12},{8,0},{12,4},{16,24},{20,28},{24,16},{28,20},{1,9},{5... | collective-permute-start | bytes 196616 | tf_op jit(solution)/shard_map/ppermute | solution.py:329
  28.1 4.8 %collective-permute-start.12 = (bf16[256,128]{1,0:T(8,128)(2,1)S(1)}, bf16[256,128]{1,0:T(8,128)(2,1)S(1)}, u32[]{:S(2)}, u32[]{:S(2)}) collective-permute-start(bf16[256,128]{1,0:T(8,128)(2,1)S(1)} %get-tuple-element.64), channel_id=1, source_target_pairs={{0,4},{4,0},{8,12},{12,8},{16,20},{20,16},{24,28},{28,24},{1,5},{5... | collective-permute-start | bytes 196616 | tf_op jit(solution)/shard_map/ppermute | solution.py:329
  29.9 5.3 %collective-permute-start.6 = (bf16[4,64,128]{2,1,0:T(8,128)(2,1)S(1)}, bf16[4,64,128]{2,1,0:T(8,128)(2,1)S(1)}, u32[]{:S(2)}, u32[]{:S(2)}) collective-permute-start(bf16[4,64,128]{2,1,0:T(8,128)(2,1)S(1)} %get-tuple-element.56), channel_id=1, source_target_pairs={{0,16},{4,20},{8,24},{12,28},{16,0},{20,4},{24,8},{28,12},{1,17},{... | collective-permute-start | bytes 196616 | tf_op jit(solution)/shard_map/ppermute | solution.py:329
  32.9 5.9 %collective-permute-start.13 = (bf16[256,128]{1,0:T(8,128)(2,1)S(1)}, bf16[256,128]{1,0:T(8,128)(2,1)S(1)}, u32[]{:S(2)}, u32[]{:S(2)}) collective-permute-start(bf16[256,128]{1,0:T(8,128)(2,1)S(1)} %shard_map.180.own_ref), channel_id=1, source_target_pairs={{0,16},{4,20},{8,24},{12,28},{16,0},{20,4},{24,8},{28,12},{1,17},{... | collective-permute-start | bytes 196616 | tf_op jit(solution)/shard_map/ppermute | solution.py:329
  35.2 4.9 %collective-permute-start.7 = (bf16[128,128]{1,0:T(8,128)(2,1)S(1)}, bf16[128,128]{1,0:T(8,128)(2,1)S(1)}, u32[]{:S(2)}, u32[]{:S(2)}) collective-permute-start(bf16[128,128]{1,0:T(8,128)(2,1)S(1)} %get-tuple-element.58), channel_id=1, source_target_pairs={{0,4},{4,0},{8,12},{12,8},{16,20},{20,16},{24,28},{28,24},{1,5},{5... | collective-permute-start | bytes 98312 | tf_op jit(solution)/shard_map/ppermute | solution.py:329
  36.0 6.4 %collective-permute-start.8 = (bf16[128,128]{1,0:T(8,128)(2,1)S(1)}, bf16[128,128]{1,0:T(8,128)(2,1)S(1)}, u32[]{:S(2)}, u32[]{:S(2)}) collective-permute-start(bf16[128,128]{1,0:T(8,128)(2,1)S(1)} %get-tuple-element.59), channel_id=1, source_target_pairs={{0,8},{4,12},{8,0},{12,4},{16,24},{20,28},{24,16},{28,20},{1,9},{5... | collective-permute-start | bytes 98312 | tf_op jit(solution)/shard_map/ppermute | solution.py:329
  36.5 5.9 %collective-permute-start.9 = (bf16[128,128]{1,0:T(8,128)(2,1)S(1)}, bf16[128,128]{1,0:T(8,128)(2,1)S(1)}, u32[]{:S(2)}, u32[]{:S(2)}) collective-permute-start(bf16[128,128]{1,0:T(8,128)(2,1)S(1)} %get-tuple-element.60), channel_id=1, source_target_pairs={{0,12},{4,8},{8,4},{12,0},{16,28},{20,24},{24,20},{28,16},{1,13},{... | collective-permute-start | bytes 98312 | tf_op jit(solution)/shard_map/ppermute | solution.py:329
  38.8 4.4 %collective-permute-start.16 = (bf16[256,128]{1,0:T(8,128)(2,1)S(1)}, bf16[256,128]{1,0:T(8,128)(2,1)S(1)}, u32[]{:S(2)}, u32[]{:S(2)}) collective-permute-start(bf16[256,128]{1,0:T(8,128)(2,1)S(1)} %shard_map.181.refs_0_), channel_id=1, source_target_pairs={{0,8},{4,12},{8,0},{12,4},{16,24},{20,28},{24,16},{28,20},{1,9},{5... | collective-permute-start | bytes 196616 | tf_op jit(solution)/shard_map/ppermute | solution.py:329
  39.1 4.3 %collective-permute-start.15 = (bf16[256,128]{1,0:T(8,128)(2,1)S(1)}, bf16[256,128]{1,0:T(8,128)(2,1)S(1)}, u32[]{:S(2)}, u32[]{:S(2)}) collective-permute-start(bf16[256,128]{1,0:T(8,128)(2,1)S(1)} %shard_map.181.refs_0_), channel_id=1, source_target_pairs={{0,4},{4,0},{8,12},{12,8},{16,20},{20,16},{24,28},{28,24},{1,5},{5... | collective-permute-start | bytes 196616 | tf_op jit(solution)/shard_map/ppermute | solution.py:329
  40.1 5.2 %collective-permute-start.14 = (bf16[256,128]{1,0:T(8,128)(2,1)S(1)}, bf16[256,128]{1,0:T(8,128)(2,1)S(1)}, u32[]{:S(2)}, u32[]{:S(2)}) collective-permute-start(bf16[256,128]{1,0:T(8,128)(2,1)S(1)} %shard_map.181.refs_0_), channel_id=1, source_target_pairs={{0,12},{4,8},{8,4},{12,0},{16,28},{20,24},{24,20},{28,16},{1,13},{... | collective-permute-start | bytes 196616 | tf_op jit(solution)/shard_map/ppermute | solution.py:329

commit v17 on v16

--- a/solution.py
+++ b/solution.py
@@ -12,51 +12,34 @@
 F32 = jnp.float32
 
 
-def spread_rows(table, width):
-    peers, slots = table.shape
+def slot_places(peers, slots, width):
     lanes = peers * width
     lane = lax.broadcasted_iota(jnp.int32, (slots, lanes), 1)
     slot = lax.broadcasted_iota(jnp.int32, (slots, lanes), 0)
-    place = jnp.where(lane % width == slot, 1.0, 0.0).astype(BF)
+    return jnp.where(lane % width == slot, 1.0, 0.0).astype(BF)
+
+
+def spread_rows(table, width, place=None):
+    peers, slots = table.shape
+    lanes = peers * width
+    if place is None:
+        place = slot_places(peers, slots, width)
     wide = jnp.dot(table.astype(BF), place, preferred_element_type=F32)
     peer = lax.broadcasted_iota(jnp.int32, (peers, lanes), 0)
     at = lax.broadcasted_iota(jnp.int32, (peers, lanes), 1)
     return jnp.sum(jnp.where(at // width == peer, wide, 0.0), axis=0, keepdims=True)
 
 
-def source_matrix(send, hubs, rows, width):
+def source_matrix(send, hubs, rows, width, place=None):
     peers, slots = send.shape
     hub_here = hubs.shape[1]
     lanes = peers * width
     lane = lax.broadcasted_iota(jnp.int32, (1, lanes), 1) % width
-    index = spread_rows(send.astype(F32), width)
+    index = spread_rows(send.astype(F32), width, place)
     for k in range(hub_here):
         index = jnp.where(lane == slots + k, hubs[0:1, k : k + 1].astype(F32), index)
     index = jnp.where(lane < slots + hub_here, index, -1.0)
     row = lax.broadcasted_iota(jnp.int32, (rows, lanes), 0).astype(F32)
-    return jnp.where(row == index, 1.0, 0.0).astype(BF)
-
-
-def source_places(peers, slots, width):
-    lanes = peers * width
-    slot = lax.broadcasted_iota(jnp.int32, (lanes, slots), 0) % width
-    return jnp.where(slot == lax.broadcasted_iota(jnp.int32, (lanes, slots), 1), 1.0, 0.0).astype(BF)
-
-
-def source_rows(place, send, hubs, rows, width):
-    peers, slots = send.shape
-    hub_here = hubs.shape[1]
-    lanes = peers * width
-    wide = lax.dot_general(
-        place, send.astype(F32).astype(BF), (((1,), (1,)), ((), ())), preferred_element_type=F32
-    )
-    line = lax.broadcasted_iota(jnp.int32, (lanes, peers), 0)
-    for k in range(hub_here):
-        wide = jnp.where(line % width == slots + k, hubs[0:1, k : k + 1].astype(F32), wide)
-    wide = jnp.where(line % width < slots + hub_here, wide, -1.0)
-    wide = jnp.where(line // width == lax.broadcasted_iota(jnp.int32, (lanes, peers), 1), wide, 0.0)
-    index = jnp.dot(wide.astype(BF), jnp.ones((peers, rows), BF), preferred_element_type=F32)
-    row = lax.broadcasted_iota(jnp.int32, (lanes, rows), 1).astype(F32)
     return jnp.where(row == index, 1.0, 0.0).astype(BF)
 
 
@@ -87,12 +70,14 @@
     for copy in copies:
         copy.start()
     peers, slots = send_v.shape[1:]
-    place_ref[...] = source_places(peers, slots, width)
+    place_ref[...] = slot_places(peers, slots, width)
     for copy in copies[:2]:
         copy.wait()
-    mark = source_rows(place_ref[...], send_v[0], hub_v[...], rows, width)
+    mark = source_matrix(send_v[0], hub_v[...], rows, width, place_ref[...])
     copies[2].wait()
-    taken = jnp.dot(mark, pack_ref[base : base + rows, :], preferred_element_type=F32).astype(BF)
+    taken = lax.dot_general(
+        mark, pack_ref[base : base + rows, :], (((0,), (0,)), ((), ())), preferred_element_type=F32
+    ).astype(BF)
     out_ref[...] = taken.reshape(out_ref.shape)
     for copy in copies[3:]:
         copy.wait()
@@ -143,11 +128,22 @@
     neigh_ref[...] = total.astype(BF)
 
 
+def ghost_rows(slots, hub_here, width, start, peers, turned_ref, neigh_grad, sums):
+    rows, cols = neigh_grad.shape
+    high = sums.astype(BF).astype(F32)
+    line = lax.broadcasted_iota(jnp.int32, (peers * width, cols), 0) % width
+    cut = pl.ds(pl.multiple_of(rows + start * width, 16), peers * width)
+    away = jnp.dot(turned_ref[cut, :], neigh_grad, preferred_element_type=F32)
+    away = jnp.where(line == slots + hub_here, high, away)
+    away = jnp.where(line == slots + hub_here + 1, sums - high, away)
+    return away.astype(BF)
+
+
 def dense_kernel(slots, hub_here, feats, width, count, me_ref, side_ref, seat_ref, x_ref, ws_ref, wn_ref, turned_ref, *refs):
     pack_refs, n_refs = refs[:feats], refs[feats : 2 * feats]
-    out_ref, back_ref, ghost_ref, mirror_ref = refs[2 * feats : 2 * feats + 4]
-    send_refs = refs[2 * feats + 4 : 2 * feats + 4 + count]
-    pre_ref, cot_ref, bias_ref = refs[2 * feats + 4 + count :]
+    own_ref, cot_ref, slope_ref, sums_ref, mirror_ref = refs[2 * feats : 2 * feats + 5]
+    send_refs = refs[2 * feats + 5 : 2 * feats + 5 + count]
+    pre_ref, bias_ref = refs[2 * feats + 5 + count :]
     rows, cols = x_ref.shape
     depth, full = ws_ref.shape
     blocks = full // cols
@@ -163,8 +159,7 @@
         bias_ref[:, cut] = pack[base + 2 * rows : base + 2 * rows + 16, :]
         left += [pack[base : base + rows, :], n_refs[d][...]]
     left = jnp.concatenate(left, axis=1)
-    both = jnp.concatenate([ws_ref[...], wn_ref[...]], axis=0)
-    into = jnp.zeros((rows, 2 * depth), F32)
+    into = jnp.zeros((rows, depth), F32)
     span = 2
     for j in range(0, blocks, span):
         right = [
@@ -180,37 +175,27 @@
         grad = (cot_ref[:, cut].astype(F32) * sig * (1.0 + pre * (1.0 - sig))).astype(BF)
         cot_ref[:, cut] = grad
         into = into + lax.dot_general(
-            grad, both[:, cut], (((1,), (1,)), ((), ())), preferred_element_type=F32
+            grad, wn_ref[:, cut], (((1,), (1,)), ((), ())), preferred_element_type=F32
         )
     mine = pl.ds(pl.multiple_of(me * cols, cols), cols)
-    own = pre_ref[:, mine]
-    out_ref[...] = (own * jax.nn.sigmoid(own)).astype(BF)
-    neigh_grad = into[:, depth:].astype(BF)
-    back_ref[...] = into[:, :depth] + jnp.dot(turned_ref[:rows, :], neigh_grad, preferred_element_type=F32)
+    own_ref[...] = pre_ref[:, mine]
+    neigh_grad = into.astype(BF)
+    slope_ref[...] = neigh_grad
     sums = jnp.sum(cot_ref[:, mine].astype(F32), axis=0, keepdims=True)
-    high = sums.astype(BF).astype(F32)
-    here = side_ref[0] * half
-
-    def ghosts(start, peers):
-        line = lax.broadcasted_iota(jnp.int32, (peers * width, cols), 0) % width
-        cut = pl.ds(pl.multiple_of(rows + start * width, 16), peers * width)
-        away = jnp.dot(turned_ref[cut, :], neigh_grad, preferred_element_type=F32)
-        away = jnp.where(line == slots + hub_here, high, away)
-        away = jnp.where(line == slots + hub_here + 1, sums - high, away)
-        return away.astype(BF)
-
+    sums_ref[...] = sums
+    there = half - side_ref[0] * half
     pair = jnp.concatenate([x_ref[...], n_refs[0][...]], axis=1).T
     if count > 1:
         for k, ref in enumerate(send_refs):
             peer = seat_ref[0] ^ k
-            ghost_ref[k] = ghosts(here + peer, 1)
-            mirror_ref[k] = ghosts(half - here + peer, 1)
+            mirror_ref[k] = ghost_rows(slots, hub_here, width, there + peer, 1, turned_ref, neigh_grad, sums)
             block = cot_ref[:, pl.ds(pl.multiple_of(peer * cols, cols), cols)]
             ref[...] = jnp.dot(pair, block, preferred_element_type=F32).astype(BF)
         return
     send_ref = send_refs[0]
-    ghost_ref[...] = ghosts(here, half).reshape(half, width, cols)
-    mirror_ref[...] = ghosts(half - here, half).reshape(half, width, cols)
+    mirror_ref[...] = ghost_rows(
+        slots, hub_here, width, there, half, turned_ref, neigh_grad, sums
+    ).reshape(half, width, cols)
     weights = jnp.dot(pair, cot_ref[...], preferred_element_type=F32).astype(BF)
     step = min(share, depth)
     for j in range(blocks):
@@ -228,8 +213,24 @@
     return [(seat ^ k, ref) for k, ref in enumerate(refs)]
 
 
-def store_kernel(held_ref, out_ref):
-    out_ref[...] = held_ref[...]
+def side_kernel(
+    slots, hub_here, count, side_ref, seat_ref, own_ref, grad_ref, slope_ref, sums_ref, turned_ref, ws_ref,
+    out_ref, back_ref, ghost_ref,
+):
+    own = own_ref[...]
+    out_ref[...] = (own * jax.nn.sigmoid(own)).astype(BF)
+    rows, cols = own.shape
+    half, width = ghost_ref.shape[:2]
+    slope, sums = slope_ref[...], sums_ref[...]
+    back = lax.dot_general(grad_ref[...], ws_ref[...], (((1,), (1,)), ((), ())), preferred_element_type=F32)
+    back_ref[...] = back + jnp.dot(turned_ref[:rows, :], slope, preferred_element_type=F32)
+    here = side_ref[0] * half
+    if count > 1:
+        for k in range(half):
+            peer = here + (seat_ref[0] ^ k)
+            ghost_ref[k] = ghost_rows(slots, hub_here, width, peer, 1, turned_ref, slope, sums)
+        return
+    ghost_ref[...] = ghost_rows(slots, hub_here, width, here, half, turned_ref, slope, sums).reshape(half, width, cols)
 
 
 def sum_kernel(stored_ref, *refs):
@@ -319,10 +320,6 @@
 
 def shape(dims, kind):
     return jax.ShapeDtypeStruct(dims, kind)
-
-
-def kept(dims, kind):
-    return pltpu.VMEM(dims, kind)
 
 
 def partner(block, axis, k):
@@ -381,7 +378,7 @@
     outgoing, pack, *moved = pl.pallas_call(
         functools.partial(send_kernel, width),
         out_shape=(
-            kept((peers, width, cols), BF),
+            shape((peers, width, cols), BF),
             shape((pack_rows, cols), BF),
             *(shape(a.shape, a.dtype) for a in moved),
         ),
@@ -389,7 +386,7 @@
         out_specs=(VMEM,) * (2 + len(moved)),
         scratch_shapes=[
             pltpu.VMEM((1, cols), BF),
-            pltpu.VMEM((lanes, slots), BF),
+            pltpu.VMEM((slots, lanes), BF),
             pltpu.SemaphoreType.DMA((11 + 2 * blocks,)),
         ],
         compiler_params=PARAMS,
@@ -422,20 +419,20 @@
     far_neigh = partner(neigh, "feat", 2)
     every = [neigh, partner(neigh, "feat", 1), far_neigh, partner(far_neigh, "feat", 1)]
 
-    output, back, ghosts, mirror, *returned = pl.pallas_call(
+    own, grad, slope, sums, mirror, *returned = pl.pallas_call(
         functools.partial(dense_kernel, slots, hub_here, feats, width, count),
         out_shape=(
-            kept((rows, cols), BF),
             shape((rows, cols), F32),
-            shape((half, width, cols), BF),
+            shape((rows, full), BF),
+            shape((rows, cols), BF),
+            shape((1, cols), F32),
             shape((half, width, cols), BF),
             *([shape((share, cols), BF)] * half if direct else [shape((half, share, cols), BF)]),
         ),
         in_specs=[SMEM] * 3 + [VMEM] * (4 + 2 * feats),
-        out_specs=(VMEM,) * (4 + count),
+        out_specs=(VMEM,) * (5 + count),
         scratch_shapes=[
             pltpu.VMEM((rows, full), F32),
-            pltpu.VMEM((rows, full), BF),
             pltpu.VMEM((16, full), BF),
         ],
         compiler_params=PARAMS,
@@ -443,14 +440,14 @@
 
     arrived = swap(returned)[::-1] if direct else [exchange(returned[0], halves)]
     mirror = partner(mirror, "dom", half)
-    output = pl.pallas_call(
-        store_kernel,
-        out_shape=shape((rows, cols), BF),
-        in_specs=[VMEM],
-        out_specs=VMEM,
+    output, back, ghosts = pl.pallas_call(
+        functools.partial(side_kernel, slots, hub_here, count),
+        out_shape=(shape((rows, cols), BF), shape((rows, cols), F32), shape((half, width, cols), BF)),
+        in_specs=[SMEM] * 2 + [VMEM] * 6,
+        out_specs=(VMEM,) * 3,
         compiler_params=PARAMS,
         cost_estimate=pl.CostEstimate(flops=10**8, bytes_accessed=10**6, transcendentals=0),
-    )(output)
+    )(side, seat, own, grad, slope, sums, turned, w_self)
     half_sum = pl.pallas_call(
         sum_kernel,
         out_shape=shape((share, cols), BF),

time: 46.3 us -> 46 us (level)
  waiting for transfers between devices: 16.1 us -> 15.6 us
    ppermute x17, waiting for transfers between devices: 9.83 us -> 9.36 us  [partner(): lax.ppermute(block, axis, [(i, i ^ k) for i in range(lax.axis_size(axis))])]
where the time goes in v17:
time: 46 us; the launch traced here: 45.7 us
  starting transfers between devices  21.6 us (47%)
  waiting for transfers between devices  15.6 us (34%)
  Pallas kernels  7.02 us (15%)
  between operations  1.39 us (3%)
    ppermute x17, starting transfers between devices, partner(): lax.ppermute(block, axis, [(i, i ^ k) for i in range(lax.axis_size(axis))])  15.8 us
    ppermute x17, waiting for transfers between devices, partner(): lax.ppermute(block, axis, [(i, i ^ k) for i in range(lax.axis_size(axis))])  9.36 us
    all_to_all x1, waiting for transfers between devices, exchange(): lax.all_to_all(blocks, 'dom', split_axis=0, concat_axis=0, axis_index_gro...  6.27 us
    all_to_all x1, starting transfers between devices, exchange(): lax.all_to_all(blocks, 'dom', split_axis=0, concat_axis=0, axis_index_gro...  5.83 us
    pallas_call x1, Pallas kernels, on_device(): pl.pallas_call(functools.partial(send_kernel, width), out_shape=(shape((p...  2.01 us
    pallas_call x1, Pallas kernels, on_device(): pl.pallas_call(functools.partial(dense_kernel, slots, hub_here, feats, wi...  1.07 us
  transfers between devices with their start and end apart: 18, of which 8 were waited for; matrix products, arithmetic and copies ran while one was open for 0% of the time, Pallas kernels for 7%

profile of v17, /device:TPU:0, one launch (start us, length us, event | category | flops | bytes accessed | tf_op | source)
XLA Modules:
  0.0 45.7 jit_solution(14101217636888641863)
XLA Ops:
  0.6 2.0 %shard_map.173 = (bf16[8,64,128]{2,1,0:T(8,128)(2,1)}, bf16[1552,128]{1,0:T(8,128)(2,1)S(1)}, s32[1,8,48]{2,1,0:T(8,128)S(1)}, s32[1,2]{1,0:T(1,128)S(1)}, s32[1...) custom-call(bf16[256,128]{1,0:T(8,128)(2,1)} %x_ref.5, ...), custom_call_target="tpu_custom_call" | custom-call | tf_op jit(solution)/shard_map/pallas_call | solution.py:378
  2.6 3.0 %collective-permute-start.1 = (bf16[1552,128]{1,0:T(8,128)(2,1)S(1)}, bf16[1552,128]{1,0:T(8,128)(2,1)S(1)}, u32[]{:S(2)}, u32[]{:S(2)}) collective-permute-start(bf16[1552,128]{1,0:T(8,128)(2,1)S(1)} %get-tuple-element.51.refs_0_), channel_id=1, source_target_pairs={{0,2},{1,3},{2,0},{3,1},{4,6},{5,7},{6,4},{7,5},{8,10},{9,11},{10,... | collective-permute-start | bytes 1191944 | tf_op jit(solution)/shard_map/ppermute | solution.py:326
  5.7 5.8 %all-to-all-start = ((bf16[8,64,128]{2,1,0:T(8,128)(2,1)}), bf16[8,64,128]{2,1,0:T(8,128)(2,1)S(1)}, u32[]{:S(2)}, u32[]{:S(2)}) async-start(bf16[8,64,128]{2,1,0:T(8,128)(2,1)} %get-tuple-element.53), calls=%async_computation | async-start | bytes 262144 | tf_op jit(solution)/shard_map/all_to_all | solution.py:330
  12.2 0.4 shard_map.174
  12.6 6.3 %all-to-all-done.got_ref = bf16[8,64,128]{2,1,0:T(8,128)(2,1)S(1)} async-done(((bf16[8,64,128]{2,1,0:T(8,128)(2,1)}), bf16[8,64,128]{2,1,0:T(8,128)(2,1)S(1)}, u32[]{:S(2)}, u32[]{:S(2)}) %all-to-all-start) | async-done | bytes 131104 | tf_op jit(solution)/shard_map/all_to_all | solution.py:330
  18.9 0.3 shard_map.175
  19.1 0.1 collective-permute-start.2
  19.2 0.6 %collective-permute-start.4 = (bf16[256,128]{1,0:T(8,128)(2,1)S(1)}, bf16[256,128]{1,0:T(8,128)(2,1)S(1)}, u32[]{:S(2)}, u32[]{:S(2)}) collective-permute-start(bf16[256,128]{1,0:T(8,128)(2,1)S(1)} %get-tuple-element.55.refs_4_), channel_id=1, source_target_pairs={{0,2},{1,3},{2,0},{3,1},{4,6},{5,7},{6,4},{7,5},{8,10},{9,11},{10,... | collective-permute-start | bytes 196616 | tf_op jit(solution)/shard_map/ppermute | solution.py:326
  19.8 0.2 collective-permute-start.3
  20.0 3.7 %collective-permute-done.4.refs_6_ = bf16[256,128]{1,0:T(8,128)(2,1)S(1)} collective-permute-done((bf16[256,128]{1,0:T(8,128)(2,1)S(1)}, bf16[256,128]{1,0:T(8,128)(2,1)S(1)}, u32[]{:S(2)}, u32[]{:S(2)}) %collective-permute-start.4) | collective-permute-done | bytes 65568 | tf_op jit(solution)/shard_map/ppermute | solution.py:326
  23.7 1.2 %collective-permute-done.5.refs_7_ = bf16[256,128]{1,0:T(8,128)(2,1)S(1)} collective-permute-done((bf16[256,128]{1,0:T(8,128)(2,1)S(1)}, bf16[256,128]{1,0:T(8,128)(2,1)S(1)}, u32[]{:S(2)}, u32[]{:S(2)}) %collective-permute-start.5) | collective-permute-done | bytes 65568 | tf_op jit(solution)/shard_map/ppermute | solution.py:326
  25.0 1.1 %shard_map.176 = (f32[256,128]{1,0:T(8,128)S(1)}, bf16[256,512]{1,0:T(8,128)(2,1)S(1)}, bf16[256,128]{1,0:T(8,128)(2,1)S(1)}, f32[1,128]{1,0:T(1,128)S(1)}, bf16...) custom-call(s32[1]{0:T(128)} %bitcast.2.me_ref, ...), custom_call_target="tpu_custom_call" | custom-call | tf_op jit(solution)/shard_map/pallas_call | solution.py:422
  26.0 0.8 %collective-permute-start.10 = (bf16[256,128]{1,0:T(8,128)(2,1)S(1)}, bf16[256,128]{1,0:T(8,128)(2,1)S(1)}, u32[]{:S(2)}, u32[]{:S(2)}) collective-permute-start(bf16[256,128]{1,0:T(8,128)(2,1)S(1)} %get-tuple-element.70), channel_id=1, source_target_pairs={{0,12},{4,8},{8,4},{12,0},{16,28},{20,24},{24,20},{28,16},{1,13},{... | collective-permute-start | bytes 196616 | tf_op jit(solution)/shard_map/ppermute | solution.py:326
  26.9 0.9 %collective-permute-start.11 = (bf16[256,128]{1,0:T(8,128)(2,1)S(1)}, bf16[256,128]{1,0:T(8,128)(2,1)S(1)}, u32[]{:S(2)}, u32[]{:S(2)}) collective-permute-start(bf16[256,128]{1,0:T(8,128)(2,1)S(1)} %get-tuple-element.71), channel_id=1, source_target_pairs={{0,8},{4,12},{8,0},{12,4},{16,24},{20,28},{24,16},{28,20},{1,9},{5... | collective-permute-start | bytes 196616 | tf_op jit(solution)/shard_map/ppermute | solution.py:326
  27.8 1.8 %collective-permute-start.12 = (bf16[256,128]{1,0:T(8,128)(2,1)S(1)}, bf16[256,128]{1,0:T(8,128)(2,1)S(1)}, u32[]{:S(2)}, u32[]{:S(2)}) collective-permute-start(bf16[256,128]{1,0:T(8,128)(2,1)S(1)} %get-tuple-element.72), channel_id=1, source_target_pairs={{0,4},{4,0},{8,12},{12,8},{16,20},{20,16},{24,28},{28,24},{1,5},{5... | collective-permute-start | bytes 196616 | tf_op jit(solution)/shard_map/ppermute | solution.py:326
  29.6 0.4 collective-permute-start.6
  30.0 0.9 %shard_map.177 = (bf16[256,128]{1,0:T(8,128)(2,1)}, f32[256,128]{1,0:T(8,128)S(1)}, bf16[4,64,128]{2,1,0:T(8,128)(2,1)S(1)}) custom-call(s32[1]{0:T(128)} %bitcast.side_ref, s32[1]{0:T(128)} %bitcast.1.seat_ref, f32[256,128]{1,0:T(8,128)S(1)} %get-tuple-element.56.own_ref, bf16[256,512]{1,0:T(8,128)(2,1)S(1)} %get-tuple-element.57.grad_ref, ...), custom_call_target="tpu_custom_call" | custom-call | flops 100000000 | bytes 1000000 | tf_op jit(solution)/shard_map/pallas_call | solution.py:443
  30.9 1.0 %collective-permute-done.10.refs_0_ = bf16[256,128]{1,0:T(8,128)(2,1)S(1)} collective-permute-done((bf16[256,128]{1,0:T(8,128)(2,1)S(1)}, bf16[256,128]{1,0:T(8,128)(2,1)S(1)}, u32[]{:S(2)}, u32[]{:S(2)}) %collective-permute-start.10) | collective-permute-done | bytes 65568 | tf_op jit(solution)/shard_map/ppermute | solution.py:326
  31.9 0.7 %collective-permute-done.12.refs_2_ = bf16[256,128]{1,0:T(8,128)(2,1)S(1)} collective-permute-done((bf16[256,128]{1,0:T(8,128)(2,1)S(1)}, bf16[256,128]{1,0:T(8,128)(2,1)S(1)}, u32[]{:S(2)}, u32[]{:S(2)}) %collective-permute-start.12) | collective-permute-done | bytes 65568 | tf_op jit(solution)/shard_map/ppermute | solution.py:326
  32.6 0.9 %collective-permute-start.13 = (bf16[256,128]{1,0:T(8,128)(2,1)S(1)}, bf16[256,128]{1,0:T(8,128)(2,1)S(1)}, u32[]{:S(2)}, u32[]{:S(2)}) collective-permute-start(bf16[256,128]{1,0:T(8,128)(2,1)S(1)} %shard_map.180.own_ref), channel_id=1, source_target_pairs={{0,16},{4,20},{8,24},{12,28},{16,0},{20,4},{24,8},{28,12},{1,17},{... | collective-permute-start | bytes 196616 | tf_op jit(solution)/shard_map/ppermute | solution.py:326
  33.5 1.4 %collective-permute-done.6.mirror_ref = bf16[4,64,128]{2,1,0:T(8,128)(2,1)S(1)} collective-permute-done((bf16[4,64,128]{2,1,0:T(8,128)(2,1)S(1)}, bf16[4,64,128]{2,1,0:T(8,128)(2,1)S(1)}, u32[]{:S(2)}, u32[]{:S(2)}) %collective-permute-start.6) | collective-permute-done | bytes 65568 | tf_op jit(solution)/shard_map/ppermute | solution.py:326
  34.9 0.8 %collective-permute-start.7 = (bf16[128,128]{1,0:T(8,128)(2,1)S(1)}, bf16[128,128]{1,0:T(8,128)(2,1)S(1)}, u32[]{:S(2)}, u32[]{:S(2)}) collective-permute-start(bf16[128,128]{1,0:T(8,128)(2,1)S(1)} %get-tuple-element.66), channel_id=1, source_target_pairs={{0,4},{4,0},{8,12},{12,8},{16,20},{20,16},{24,28},{28,24},{1,5},{5... | collective-permute-start | bytes 98312 | tf_op jit(solution)/shard_map/ppermute | solution.py:326
  35.8 0.5 %collective-permute-start.8 = (bf16[128,128]{1,0:T(8,128)(2,1)S(1)}, bf16[128,128]{1,0:T(8,128)(2,1)S(1)}, u32[]{:S(2)}, u32[]{:S(2)}) collective-permute-start(bf16[128,128]{1,0:T(8,128)(2,1)S(1)} %get-tuple-element.67), channel_id=1, source_target_pairs={{0,8},{4,12},{8,0},{12,4},{16,24},{20,28},{24,16},{28,20},{1,9},{5... | collective-permute-start | bytes 98312 | tf_op jit(solution)/shard_map/ppermute | solution.py:326
  36.3 2.2 %collective-permute-start.9 = (bf16[128,128]{1,0:T(8,128)(2,1)S(1)}, bf16[128,128]{1,0:T(8,128)(2,1)S(1)}, u32[]{:S(2)}, u32[]{:S(2)}) collective-permute-start(bf16[128,128]{1,0:T(8,128)(2,1)S(1)} %get-tuple-element.68), channel_id=1, source_target_pairs={{0,12},{4,8},{8,4},{12,0},{16,28},{20,24},{24,20},{28,16},{1,13},{... | collective-permute-start | bytes 98312 | tf_op jit(solution)/shard_map/ppermute | solution.py:326
  38.6 0.3 collective-permute-start.16
  38.9 1.0 %collective-permute-start.15 = (bf16[256,128]{1,0:T(8,128)(2,1)S(1)}, bf16[256,128]{1,0:T(8,128)(2,1)S(1)}, u32[]{:S(2)}, u32[]{:S(2)}) collective-permute-start(bf16[256,128]{1,0:T(8,128)(2,1)S(1)} %shard_map.181.refs_0_), channel_id=1, source_target_pairs={{0,4},{4,0},{8,12},{12,8},{16,20},{20,16},{24,28},{28,24},{1,5},{5... | collective-permute-start | bytes 196616 | tf_op jit(solution)/shard_map/ppermute | solution.py:326
  39.8 2.3 %collective-permute-start.14 = (bf16[256,128]{1,0:T(8,128)(2,1)S(1)}, bf16[256,128]{1,0:T(8,128)(2,1)S(1)}, u32[]{:S(2)}, u32[]{:S(2)}) collective-permute-start(bf16[256,128]{1,0:T(8,128)(2,1)S(1)} %shard_map.181.refs_0_), channel_id=1, source_target_pairs={{0,12},{4,8},{8,4},{12,0},{16,28},{20,24},{24,20},{28,16},{1,13},{... | collective-permute-start | bytes 196616 | tf_op jit(solution)/shard_map/ppermute | solution.py:326
  42.1 0.9 %shard_map.179 = (bf16[256,128]{1,0:T(8,128)(2,1)}, f32[1,128]{1,0:T(1,128)}) custom-call(s32[1]{0:T(128)} %bitcast.side_ref, s32[1]{0:T(128)} %bitcast.1.seat_ref, f32[256,128]{1,0:T(8,128)S(1)} %get-tuple-element.61.back_ref, bf16[256,512]{1,0:T(8,128)(2,1)S(1)} %get-tuple-element.62.mark_ref, bf16[128,128]{1,0:T(8,128)(2,1)S(1)} %get-tuple-element.65.refs_0_, ...), custom_call_target="tpu_custom_call" | custom-call | flops 2000000000 | bytes 1000000 | tf_op jit(solution)/shard_map/pallas_call | solution.py:475
  43.0 0.2 collective-permute-done.15.refs_1_
  43.1 0.8 %shard_map.182 = (f32[128,512]{1,0:T(8,128)}, f32[128,512]{1,0:T(8,128)}) custom-call(s32[1]{0:T(128)} %bitcast.1.seat_ref, bf16[256,128]{1,0:T(8,128)(2,1)S(1)} %shard_map.181.refs_0_, bf16[256,128]{1,0:T(8,128)(2,1)S(1)} %collective-permute-done.15.refs_1_, bf16[256,128]{1,0:T(8,128)(2,1)S(1)} %collective-permute-done.16.refs_2_), custom_call_target="tpu_custom_call" | custom-call | tf_op jit(solution)/shard_map/pallas_call | solution.py:485
  44.0 1.0 %collective-permute-done.14.got_ref = bf16[256,128]{1,0:T(8,128)(2,1)S(1)} collective-permute-done((bf16[256,128]{1,0:T(8,128)(2,1)S(1)}, bf16[256,128]{1,0:T(8,128)(2,1)S(1)}, u32[]{:S(2)}, u32[]{:S(2)}) %collective-permute-start.14) | collective-permute-done | bytes 65568 | tf_op jit(solution)/shard_map/ppermute | solution.py:326
  45.0 0.7 %shard_map.183 = (f32[128,512]{1,0:T(8,128)}, f32[128,512]{1,0:T(8,128)}) custom-call(s32[1]{0:T(128)} %bitcast.1.seat_ref, bf16[256,128]{1,0:T(8,128)(2,1)S(1)} %collective-permute-done.14.got_ref, f32[128,512]{1,0:T(8,128)} %get-tuple-element.74.begun_self_ref, ...), custom_call_target="tpu_custom_call", output_to_operand_aliasing={{0}: (2, {}), {1}: (3, {})} | custom-call | tf_op jit(solution)/shard_map/pallas_call | solution.py:494
  (21 shorter events, 0.1 us)
Async XLA Ops:
  2.6 16.2 %collective-permute-start.1 = (bf16[1552,128]{1,0:T(8,128)(2,1)S(1)}, bf16[1552,128]{1,0:T(8,128)(2,1)S(1)}, u32[]{:S(2)}, u32[]{:S(2)}) collective-permute-start(bf16[1552,128]{1,0:T(8,128)(2,1)S(1)} %get-tuple-element.51.refs_0_), channel_id=1, source_target_pairs={{0,2},{1,3},{2,0},{3,1},{4,6},{5,7},{6,4},{7,5},{8,10},{9,11},{10,... | collective-permute-start | bytes 1191944 | tf_op jit(solution)/shard_map/ppermute | solution.py:326
  5.7 13.2 %all-to-all-start = ((bf16[8,64,128]{2,1,0:T(8,128)(2,1)}), bf16[8,64,128]{2,1,0:T(8,128)(2,1)S(1)}, u32[]{:S(2)}, u32[]{:S(2)}) async-start(bf16[8,64,128]{2,1,0:T(8,128)(2,1)} %get-tuple-element.53), calls=%async_computation | async-start | bytes 262144 | tf_op jit(solution)/shard_map/all_to_all | solution.py:330
  11.5 12.2 %collective-permute-start = (bf16[1552,128]{1,0:T(8,128)(2,1)S(1)}, bf16[1552,128]{1,0:T(8,128)(2,1)S(1)}, u32[]{:S(2)}, u32[]{:S(2)}) collective-permute-start(bf16[1552,128]{1,0:T(8,128)(2,1)S(1)} %get-tuple-element.51.refs_0_), channel_id=1, source_target_pairs={{0,1},{1,0},{2,3},{3,2},{4,5},{5,4},{6,7},{7,6},{8,9},{9,8},{10,11... | collective-permute-start | bytes 1191944 | tf_op jit(solution)/shard_map/ppermute | solution.py:326
  12.1 6.7 %copy-start.1 = (bf16[256,128]{1,0:T(8,128)(2,1)S(1)}, bf16[256,128]{1,0:T(8,128)(2,1)}, u32[]{:S(2)}) copy-start(bf16[256,128]{1,0:T(8,128)(2,1)} %x_ref.5) | copy-start | bytes 196612
  18.8 6.1 %copy-start = (bf16[128,512]{1,0:T(8,128)(2,1)S(1)}, bf16[128,512]{1,0:T(8,128)(2,1)}, u32[]{:S(2)}) copy-start(bf16[128,512]{1,0:T(8,128)(2,1)} %ws_ref.5) | copy-start | bytes 393220
  18.8 6.1 %copy-start.2 = (bf16[128,512]{1,0:T(8,128)(2,1)S(1)}, bf16[128,512]{1,0:T(8,128)(2,1)}, u32[]{:S(2)}) copy-start(bf16[128,512]{1,0:T(8,128)(2,1)} %wn_ref.3) | copy-start | bytes 393220
  19.1 5.8 %collective-permute-start.2 = (bf16[1552,128]{1,0:T(8,128)(2,1)S(1)}, bf16[1552,128]{1,0:T(8,128)(2,1)S(1)}, u32[]{:S(2)}, u32[]{:S(2)}) collective-permute-start(bf16[1552,128]{1,0:T(8,128)(2,1)S(1)} %get-tuple-element.54.refs_2_), channel_id=1, source_target_pairs={{0,1},{1,0},{2,3},{3,2},{4,5},{5,4},{6,7},{7,6},{8,9},{9,8},{10,11... | collective-permute-start | bytes 1191944 | tf_op jit(solution)/shard_map/ppermute | solution.py:326
  19.2 4.5 %collective-permute-start.4 = (bf16[256,128]{1,0:T(8,128)(2,1)S(1)}, bf16[256,128]{1,0:T(8,128)(2,1)S(1)}, u32[]{:S(2)}, u32[]{:S(2)}) collective-permute-start(bf16[256,128]{1,0:T(8,128)(2,1)S(1)} %get-tuple-element.55.refs_4_), channel_id=1, source_target_pairs={{0,2},{1,3},{2,0},{3,1},{4,6},{5,7},{6,4},{7,5},{8,10},{9,11},{10,... | collective-permute-start | bytes 196616 | tf_op jit(solution)/shard_map/ppermute | solution.py:326
  19.8 3.9 %collective-permute-start.3 = (bf16[256,128]{1,0:T(8,128)(2,1)S(1)}, bf16[256,128]{1,0:T(8,128)(2,1)S(1)}, u32[]{:S(2)}, u32[]{:S(2)}) collective-permute-start(bf16[256,128]{1,0:T(8,128)(2,1)S(1)} %get-tuple-element.55.refs_4_), channel_id=1, source_target_pairs={{0,1},{1,0},{2,3},{3,2},{4,5},{5,4},{6,7},{7,6},{8,9},{9,8},{10,11... | collective-permute-start | bytes 196616 | tf_op jit(solution)/shard_map/ppermute | solution.py:326
  23.7 1.3 %collective-permute-start.5 = (bf16[256,128]{1,0:T(8,128)(2,1)S(1)}, bf16[256,128]{1,0:T(8,128)(2,1)S(1)}, u32[]{:S(2)}, u32[]{:S(2)}) collective-permute-start(bf16[256,128]{1,0:T(8,128)(2,1)S(1)} %collective-permute-done.4.refs_6_), channel_id=1, source_target_pairs={{0,1},{1,0},{2,3},{3,2},{4,5},{5,4},{6,7},{7,6},{8,9},{9,8},{10,11... | collective-permute-start | bytes 196616 | tf_op jit(solution)/shard_map/ppermute | solution.py:326
  26.0 5.8 %collective-permute-start.10 = (bf16[256,128]{1,0:T(8,128)(2,1)S(1)}, bf16[256,128]{1,0:T(8,128)(2,1)S(1)}, u32[]{:S(2)}, u32[]{:S(2)}) collective-permute-start(bf16[256,128]{1,0:T(8,128)(2,1)S(1)} %get-tuple-element.70), channel_id=1, source_target_pairs={{0,12},{4,8},{8,4},{12,0},{16,28},{20,24},{24,20},{28,16},{1,13},{... | collective-permute-start | bytes 196616 | tf_op jit(solution)/shard_map/ppermute | solution.py:326
  26.9 5.0 %collective-permute-start.11 = (bf16[256,128]{1,0:T(8,128)(2,1)S(1)}, bf16[256,128]{1,0:T(8,128)(2,1)S(1)}, u32[]{:S(2)}, u32[]{:S(2)}) collective-permute-start(bf16[256,128]{1,0:T(8,128)(2,1)S(1)} %get-tuple-element.71), channel_id=1, source_target_pairs={{0,8},{4,12},{8,0},{12,4},{16,24},{20,28},{24,16},{28,20},{1,9},{5... | collective-permute-start | bytes 196616 | tf_op jit(solution)/shard_map/ppermute | solution.py:326
  27.8 4.8 %collective-permute-start.12 = (bf16[256,128]{1,0:T(8,128)(2,1)S(1)}, bf16[256,128]{1,0:T(8,128)(2,1)S(1)}, u32[]{:S(2)}, u32[]{:S(2)}) collective-permute-start(bf16[256,128]{1,0:T(8,128)(2,1)S(1)} %get-tuple-element.72), channel_id=1, source_target_pairs={{0,4},{4,0},{8,12},{12,8},{16,20},{20,16},{24,28},{28,24},{1,5},{5... | collective-permute-start | bytes 196616 | tf_op jit(solution)/shard_map/ppermute | solution.py:326
  29.6 5.3 %collective-permute-start.6 = (bf16[4,64,128]{2,1,0:T(8,128)(2,1)S(1)}, bf16[4,64,128]{2,1,0:T(8,128)(2,1)S(1)}, u32[]{:S(2)}, u32[]{:S(2)}) collective-permute-start(bf16[4,64,128]{2,1,0:T(8,128)(2,1)S(1)} %get-tuple-element.64), channel_id=1, source_target_pairs={{0,16},{4,20},{8,24},{12,28},{16,0},{20,4},{24,8},{28,12},{1,17},{... | collective-permute-start | bytes 196616 | tf_op jit(solution)/shard_map/ppermute | solution.py:326
  32.6 5.9 %collective-permute-start.13 = (bf16[256,128]{1,0:T(8,128)(2,1)S(1)}, bf16[256,128]{1,0:T(8,128)(2,1)S(1)}, u32[]{:S(2)}, u32[]{:S(2)}) collective-permute-start(bf16[256,128]{1,0:T(8,128)(2,1)S(1)} %shard_map.180.own_ref), channel_id=1, source_target_pairs={{0,16},{4,20},{8,24},{12,28},{16,0},{20,4},{24,8},{28,12},{1,17},{... | collective-permute-start | bytes 196616 | tf_op jit(solution)/shard_map/ppermute | solution.py:326
  34.9 4.9 %collective-permute-start.7 = (bf16[128,128]{1,0:T(8,128)(2,1)S(1)}, bf16[128,128]{1,0:T(8,128)(2,1)S(1)}, u32[]{:S(2)}, u32[]{:S(2)}) collective-permute-start(bf16[128,128]{1,0:T(8,128)(2,1)S(1)} %get-tuple-element.66), channel_id=1, source_target_pairs={{0,4},{4,0},{8,12},{12,8},{16,20},{20,16},{24,28},{28,24},{1,5},{5... | collective-permute-start | bytes 98312 | tf_op jit(solution)/shard_map/ppermute | solution.py:326
  35.8 6.4 %collective-permute-start.8 = (bf16[128,128]{1,0:T(8,128)(2,1)S(1)}, bf16[128,128]{1,0:T(8,128)(2,1)S(1)}, u32[]{:S(2)}, u32[]{:S(2)}) collective-permute-start(bf16[128,128]{1,0:T(8,128)(2,1)S(1)} %get-tuple-element.67), channel_id=1, source_target_pairs={{0,8},{4,12},{8,0},{12,4},{16,24},{20,28},{24,16},{28,20},{1,9},{5... | collective-permute-start | bytes 98312 | tf_op jit(solution)/shard_map/ppermute | solution.py:326
  36.3 5.9 %collective-permute-start.9 = (bf16[128,128]{1,0:T(8,128)(2,1)S(1)}, bf16[128,128]{1,0:T(8,128)(2,1)S(1)}, u32[]{:S(2)}, u32[]{:S(2)}) collective-permute-start(bf16[128,128]{1,0:T(8,128)(2,1)S(1)} %get-tuple-element.68), channel_id=1, source_target_pairs={{0,12},{4,8},{8,4},{12,0},{16,28},{20,24},{24,20},{28,16},{1,13},{... | collective-permute-start | bytes 98312 | tf_op jit(solution)/shard_map/ppermute | solution.py:326
  38.6 4.4 %collective-permute-start.16 = (bf16[256,128]{1,0:T(8,128)(2,1)S(1)}, bf16[256,128]{1,0:T(8,128)(2,1)S(1)}, u32[]{:S(2)}, u32[]{:S(2)}) collective-permute-start(bf16[256,128]{1,0:T(8,128)(2,1)S(1)} %shard_map.181.refs_0_), channel_id=1, source_target_pairs={{0,8},{4,12},{8,0},{12,4},{16,24},{20,28},{24,16},{28,20},{1,9},{5... | collective-permute-start | bytes 196616 | tf_op jit(solution)/shard_map/ppermute | solution.py:326
  38.9 4.3 %collective-permute-start.15 = (bf16[256,128]{1,0:T(8,128)(2,1)S(1)}, bf16[256,128]{1,0:T(8,128)(2,1)S(1)}, u32[]{:S(2)}, u32[]{:S(2)}) collective-permute-start(bf16[256,128]{1,0:T(8,128)(2,1)S(1)} %shard_map.181.refs_0_), channel_id=1, source_target_pairs={{0,4},{4,0},{8,12},{12,8},{16,20},{20,16},{24,28},{28,24},{1,5},{5... | collective-permute-start | bytes 196616 | tf_op jit(solution)/shard_map/ppermute | solution.py:326
  39.8 5.2 %collective-permute-start.14 = (bf16[256,128]{1,0:T(8,128)(2,1)S(1)}, bf16[256,128]{1,0:T(8,128)(2,1)S(1)}, u32[]{:S(2)}, u32[]{:S(2)}) collective-permute-start(bf16[256,128]{1,0:T(8,128)(2,1)S(1)} %shard_map.181.refs_0_), channel_id=1, source_target_pairs={{0,12},{4,8},{8,4},{12,0},{16,28},{20,24},{24,20},{28,16},{1,13},{... | collective-permute-start | bytes 196616 | tf_op jit(solution)/shard_map/ppermute | solution.py:326

commit v18 on v17

--- a/solution.py
+++ b/solution.py
@@ -78,7 +78,9 @@
     taken = lax.dot_general(
         mark, pack_ref[base : base + rows, :], (((0,), (0,)), ((), ())), preferred_element_type=F32
     ).astype(BF)
-    out_ref[...] = taken.reshape(out_ref.shape)
+    kept = out_ref.shape[1]
+    for q in range(peers):
+        out_ref[q] = taken[q * width : q * width + kept]
     for copy in copies[3:]:
         copy.wait()
     pack_ref[base + 2 * rows :, :] = jnp.broadcast_to(bias_v[...], (16, cols))
@@ -120,11 +122,13 @@
     mark_ref[...] = source_matrix(send_v[0], hub_v[...], rows, width)
 
 
-def neigh_kernel(x_ref, mix_ref, far_ref, got_ref, neigh_ref, passed_ref):
+def neigh_kernel(x_ref, mix_ref, far_ref, got_ref, neigh_ref, passed_ref, wide_ref):
     rows, cols = x_ref.shape
     lanes = mix_ref.shape[1] - rows
+    wide_ref[...] = jnp.zeros_like(wide_ref)
+    wide_ref[:, : got_ref.shape[1], :] = got_ref[...]
     total = jnp.dot(mix_ref[:, :rows], x_ref[...], preferred_element_type=F32)
-    total = total + jnp.dot(mix_ref[:, rows:], got_ref[...].reshape(lanes, cols), preferred_element_type=F32)
+    total = total + jnp.dot(mix_ref[:, rows:], wide_ref[...].reshape(lanes, cols), preferred_element_type=F32)
     neigh_ref[...] = total.astype(BF)
 
 
@@ -188,14 +192,14 @@
     if count > 1:
         for k, ref in enumerate(send_refs):
             peer = seat_ref[0] ^ k
-            mirror_ref[k] = ghost_rows(slots, hub_here, width, there + peer, 1, turned_ref, neigh_grad, sums)
+            away = ghost_rows(slots, hub_here, width, there + peer, 1, turned_ref, neigh_grad, sums)
+            mirror_ref[k] = away[: mirror_ref.shape[1]]
             block = cot_ref[:, pl.ds(pl.multiple_of(peer * cols, cols), cols)]
             ref[...] = jnp.dot(pair, block, preferred_element_type=F32).astype(BF)
         return
     send_ref = send_refs[0]
-    mirror_ref[...] = ghost_rows(
-        slots, hub_here, width, there, half, turned_ref, neigh_grad, sums
-    ).reshape(half, width, cols)
+    away = ghost_rows(slots, hub_here, width, there, half, turned_ref, neigh_grad, sums).reshape(half, width, cols)
+    mirror_ref[...] = away[:, : mirror_ref.shape[1]]
     weights = jnp.dot(pair, cot_ref[...], preferred_element_type=F32).astype(BF)
     step = min(share, depth)
     for j in range(blocks):
@@ -246,7 +250,8 @@
     for k in range(ghost_ref.shape[0]):
         out_ref = out_refs[k] if len(out_refs) > 1 else out_refs[0].at[k]
         out_ref[:width, :] = ghost_ref[k]
-        out_ref[width:, :] = mirror_ref[k]
+        out_ref[width:, :] = jnp.zeros(ghost_ref.shape[1:], BF)
+        out_ref[width : width + mirror_ref.shape[1], :] = mirror_ref[k]
 
 
 def total_kernel(own_ref, other_ref, part_ref):
@@ -356,6 +361,7 @@
     peers, slots = send_rows.shape[1:]
     hub_here = hub_rows.shape[-1]
     width = -(-(slots + hub_here + 2) // 16) * 16
+    sent = -(-(slots + hub_here + 2) // 8) * 8
     lanes = peers * width
     half = peers // 2
     share = 2 * blocks * depth // half
@@ -378,7 +384,7 @@
     outgoing, pack, *moved = pl.pallas_call(
         functools.partial(send_kernel, width),
         out_shape=(
-            shape((peers, width, cols), BF),
+            shape((peers, sent, cols), BF),
             shape((pack_rows, cols), BF),
             *(shape(a.shape, a.dtype) for a in moved),
         ),
@@ -413,6 +419,7 @@
         in_specs=[VMEM, VMEM, ANY, VMEM],
         out_specs=(VMEM, ANY),
         input_output_aliases={2: 1},
+        scratch_shapes=[pltpu.VMEM((peers, width, cols), BF)],
         compiler_params=PARAMS,
     )(features, mix, far, incoming)
     last = partner(far, "feat", 1)
@@ -426,7 +433,7 @@
             shape((rows, full), BF),
             shape((rows, cols), BF),
             shape((1, cols), F32),
-            shape((half, width, cols), BF),
+            shape((half, sent, cols), BF),
             *([shape((share, cols), BF)] * half if direct else [shape((half, share, cols), BF)]),
         ),
         in_specs=[SMEM] * 3 + [VMEM] * (4 + 2 * feats),

time: 46 us -> 45.8 us (level)
  transfers between devices with their start and end apart: 18 -> 18, of which waited for: 8 -> 9; matrix products, arithmetic and copies ran while one was open for 0% -> 0% of each run, Pallas kernels for 7% -> 7%
where the time goes in v18:
time: 45.8 us; the launch traced here: 45.5 us
  starting transfers between devices  21.7 us (47%)
  waiting for transfers between devices  15.4 us (34%)
  Pallas kernels  7.04 us (15%)
  between operations  1.39 us (3%)
    ppermute x17, starting transfers between devices, partner(): lax.ppermute(block, axis, [(i, i ^ k) for i in range(lax.axis_size(axis))])  15.8 us
    ppermute x17, waiting for transfers between devices, partner(): lax.ppermute(block, axis, [(i, i ^ k) for i in range(lax.axis_size(axis))])  9.22 us
    all_to_all x1, waiting for transfers between devices, exchange(): lax.all_to_all(blocks, 'dom', split_axis=0, concat_axis=0, axis_index_gro...  6.16 us
    all_to_all x1, starting transfers between devices, exchange(): lax.all_to_all(blocks, 'dom', split_axis=0, concat_axis=0, axis_index_gro...  5.83 us
    pallas_call x1, Pallas kernels, on_device(): pl.pallas_call(functools.partial(send_kernel, width), out_shape=(shape((p...  2 us
    pallas_call x1, Pallas kernels, on_device(): pl.pallas_call(functools.partial(dense_kernel, slots, hub_here, feats, wi...  1.07 us
  transfers between devices with their start and end apart: 18, of which 9 were waited for; matrix products, arithmetic and copies ran while one was open for 0% of the time, Pallas kernels for 7%

profile of v18, /device:TPU:0, one launch (start us, length us, event | category | flops | bytes accessed | tf_op | source)
XLA Modules:
  0.0 45.5 jit_solution(5538610013080542197)
XLA Ops:
  0.6 2.0 %shard_map.173 = (bf16[8,56,128]{2,1,0:T(8,128)(2,1)}, bf16[1552,128]{1,0:T(8,128)(2,1)S(1)}, s32[1,8,48]{2,1,0:T(8,128)S(1)}, s32[1,2]{1,0:T(1,128)S(1)}, s32[1...) custom-call(bf16[256,128]{1,0:T(8,128)(2,1)} %x_ref.5, ...), custom_call_target="tpu_custom_call" | custom-call | tf_op jit(solution)/shard_map/pallas_call | solution.py:384
  2.6 3.0 %collective-permute-start.1 = (bf16[1552,128]{1,0:T(8,128)(2,1)S(1)}, bf16[1552,128]{1,0:T(8,128)(2,1)S(1)}, u32[]{:S(2)}, u32[]{:S(2)}) collective-permute-start(bf16[1552,128]{1,0:T(8,128)(2,1)S(1)} %get-tuple-element.51.refs_0_), channel_id=1, source_target_pairs={{0,2},{1,3},{2,0},{3,1},{4,6},{5,7},{6,4},{7,5},{8,10},{9,11},{10,... | collective-permute-start | bytes 1191944 | tf_op jit(solution)/shard_map/ppermute | solution.py:331
  5.6 5.8 %all-to-all-start = ((bf16[8,56,128]{2,1,0:T(8,128)(2,1)}), bf16[8,56,128]{2,1,0:T(8,128)(2,1)S(1)}, u32[]{:S(2)}, u32[]{:S(2)}) async-start(bf16[8,56,128]{2,1,0:T(8,128)(2,1)} %get-tuple-element.53), calls=%async_computation | async-start | bytes 229376 | tf_op jit(solution)/shard_map/all_to_all | solution.py:335
  12.1 0.4 shard_map.174
  12.5 6.2 %all-to-all-done.got_ref = bf16[8,56,128]{2,1,0:T(8,128)(2,1)S(1)} async-done(((bf16[8,56,128]{2,1,0:T(8,128)(2,1)}), bf16[8,56,128]{2,1,0:T(8,128)(2,1)S(1)}, u32[]{:S(2)}, u32[]{:S(2)}) %all-to-all-start) | async-done | bytes 114720 | tf_op jit(solution)/shard_map/all_to_all | solution.py:335
  18.7 0.3 shard_map.175
  19.1 0.6 %collective-permute-start.4 = (bf16[256,128]{1,0:T(8,128)(2,1)S(1)}, bf16[256,128]{1,0:T(8,128)(2,1)S(1)}, u32[]{:S(2)}, u32[]{:S(2)}) collective-permute-start(bf16[256,128]{1,0:T(8,128)(2,1)S(1)} %get-tuple-element.55.refs_4_), channel_id=1, source_target_pairs={{0,2},{1,3},{2,0},{3,1},{4,6},{5,7},{6,4},{7,5},{8,10},{9,11},{10,... | collective-permute-start | bytes 196616 | tf_op jit(solution)/shard_map/ppermute | solution.py:331
  19.7 0.2 collective-permute-start.3
  19.9 3.7 %collective-permute-done.4.refs_6_ = bf16[256,128]{1,0:T(8,128)(2,1)S(1)} collective-permute-done((bf16[256,128]{1,0:T(8,128)(2,1)S(1)}, bf16[256,128]{1,0:T(8,128)(2,1)S(1)}, u32[]{:S(2)}, u32[]{:S(2)}) %collective-permute-start.4) | collective-permute-done | bytes 65568 | tf_op jit(solution)/shard_map/ppermute | solution.py:331
  23.6 1.2 %collective-permute-done.5.refs_7_ = bf16[256,128]{1,0:T(8,128)(2,1)S(1)} collective-permute-done((bf16[256,128]{1,0:T(8,128)(2,1)S(1)}, bf16[256,128]{1,0:T(8,128)(2,1)S(1)}, u32[]{:S(2)}, u32[]{:S(2)}) %collective-permute-start.5) | collective-permute-done | bytes 65568 | tf_op jit(solution)/shard_map/ppermute | solution.py:331
  24.9 1.1 %shard_map.176 = (f32[256,128]{1,0:T(8,128)S(1)}, bf16[256,512]{1,0:T(8,128)(2,1)S(1)}, bf16[256,128]{1,0:T(8,128)(2,1)S(1)}, f32[1,128]{1,0:T(1,128)S(1)}, bf16...) custom-call(s32[1]{0:T(128)} %bitcast.2.me_ref, ...), custom_call_target="tpu_custom_call" | custom-call | tf_op jit(solution)/shard_map/pallas_call | solution.py:429
  25.9 0.8 %collective-permute-start.10 = (bf16[256,128]{1,0:T(8,128)(2,1)S(1)}, bf16[256,128]{1,0:T(8,128)(2,1)S(1)}, u32[]{:S(2)}, u32[]{:S(2)}) collective-permute-start(bf16[256,128]{1,0:T(8,128)(2,1)S(1)} %get-tuple-element.70), channel_id=1, source_target_pairs={{0,12},{4,8},{8,4},{12,0},{16,28},{20,24},{24,20},{28,16},{1,13},{... | collective-permute-start | bytes 196616 | tf_op jit(solution)/shard_map/ppermute | solution.py:331
  26.7 1.0 %collective-permute-start.11 = (bf16[256,128]{1,0:T(8,128)(2,1)S(1)}, bf16[256,128]{1,0:T(8,128)(2,1)S(1)}, u32[]{:S(2)}, u32[]{:S(2)}) collective-permute-start(bf16[256,128]{1,0:T(8,128)(2,1)S(1)} %get-tuple-element.71), channel_id=1, source_target_pairs={{0,8},{4,12},{8,0},{12,4},{16,24},{20,28},{24,16},{28,20},{1,9},{5... | collective-permute-start | bytes 196616 | tf_op jit(solution)/shard_map/ppermute | solution.py:331
  27.7 1.8 %collective-permute-start.12 = (bf16[256,128]{1,0:T(8,128)(2,1)S(1)}, bf16[256,128]{1,0:T(8,128)(2,1)S(1)}, u32[]{:S(2)}, u32[]{:S(2)}) collective-permute-start(bf16[256,128]{1,0:T(8,128)(2,1)S(1)} %get-tuple-element.72), channel_id=1, source_target_pairs={{0,4},{4,0},{8,12},{12,8},{16,20},{20,16},{24,28},{28,24},{1,5},{5... | collective-permute-start | bytes 196616 | tf_op jit(solution)/shard_map/ppermute | solution.py:331
  29.5 0.4 collective-permute-start.6
  29.9 0.9 %shard_map.177 = (bf16[256,128]{1,0:T(8,128)(2,1)}, f32[256,128]{1,0:T(8,128)S(1)}, bf16[4,64,128]{2,1,0:T(8,128)(2,1)S(1)}) custom-call(s32[1]{0:T(128)} %bitcast.side_ref, s32[1]{0:T(128)} %bitcast.1.seat_ref, f32[256,128]{1,0:T(8,128)S(1)} %get-tuple-element.56.own_ref, bf16[256,512]{1,0:T(8,128)(2,1)S(1)} %get-tuple-element.57.grad_ref, ...), custom_call_target="tpu_custom_call" | custom-call | flops 100000000 | bytes 1000000 | tf_op jit(solution)/shard_map/pallas_call | solution.py:450
  30.8 1.0 %collective-permute-done.10.refs_0_ = bf16[256,128]{1,0:T(8,128)(2,1)S(1)} collective-permute-done((bf16[256,128]{1,0:T(8,128)(2,1)S(1)}, bf16[256,128]{1,0:T(8,128)(2,1)S(1)}, u32[]{:S(2)}, u32[]{:S(2)}) %collective-permute-start.10) | collective-permute-done | bytes 65568 | tf_op jit(solution)/shard_map/ppermute | solution.py:331
  31.8 0.7 %collective-permute-done.12.refs_2_ = bf16[256,128]{1,0:T(8,128)(2,1)S(1)} collective-permute-done((bf16[256,128]{1,0:T(8,128)(2,1)S(1)}, bf16[256,128]{1,0:T(8,128)(2,1)S(1)}, u32[]{:S(2)}, u32[]{:S(2)}) %collective-permute-start.12) | collective-permute-done | bytes 65568 | tf_op jit(solution)/shard_map/ppermute | solution.py:331
  32.5 0.9 %collective-permute-start.13 = (bf16[256,128]{1,0:T(8,128)(2,1)S(1)}, bf16[256,128]{1,0:T(8,128)(2,1)S(1)}, u32[]{:S(2)}, u32[]{:S(2)}) collective-permute-start(bf16[256,128]{1,0:T(8,128)(2,1)S(1)} %shard_map.180.own_ref), channel_id=1, source_target_pairs={{0,16},{4,20},{8,24},{12,28},{16,0},{20,4},{24,8},{28,12},{1,17},{... | collective-permute-start | bytes 196616 | tf_op jit(solution)/shard_map/ppermute | solution.py:331
  33.4 1.2 %collective-permute-done.6.mirror_ref = bf16[4,56,128]{2,1,0:T(8,128)(2,1)S(1)} collective-permute-done((bf16[4,56,128]{2,1,0:T(8,128)(2,1)S(1)}, bf16[4,56,128]{2,1,0:T(8,128)(2,1)S(1)}, u32[]{:S(2)}, u32[]{:S(2)}) %collective-permute-start.6) | collective-permute-done | bytes 57376 | tf_op jit(solution)/shard_map/ppermute | solution.py:331
  34.7 0.9 %collective-permute-start.7 = (bf16[128,128]{1,0:T(8,128)(2,1)S(1)}, bf16[128,128]{1,0:T(8,128)(2,1)S(1)}, u32[]{:S(2)}, u32[]{:S(2)}) collective-permute-start(bf16[128,128]{1,0:T(8,128)(2,1)S(1)} %get-tuple-element.66), channel_id=1, source_target_pairs={{0,4},{4,0},{8,12},{12,8},{16,20},{20,16},{24,28},{28,24},{1,5},{5... | collective-permute-start | bytes 98312 | tf_op jit(solution)/shard_map/ppermute | solution.py:331
  35.5 0.5 %collective-permute-start.8 = (bf16[128,128]{1,0:T(8,128)(2,1)S(1)}, bf16[128,128]{1,0:T(8,128)(2,1)S(1)}, u32[]{:S(2)}, u32[]{:S(2)}) collective-permute-start(bf16[128,128]{1,0:T(8,128)(2,1)S(1)} %get-tuple-element.67), channel_id=1, source_target_pairs={{0,8},{4,12},{8,0},{12,4},{16,24},{20,28},{24,16},{28,20},{1,9},{5... | collective-permute-start | bytes 98312 | tf_op jit(solution)/shard_map/ppermute | solution.py:331
  36.1 2.1 %collective-permute-start.9 = (bf16[128,128]{1,0:T(8,128)(2,1)S(1)}, bf16[128,128]{1,0:T(8,128)(2,1)S(1)}, u32[]{:S(2)}, u32[]{:S(2)}) collective-permute-start(bf16[128,128]{1,0:T(8,128)(2,1)S(1)} %get-tuple-element.68), channel_id=1, source_target_pairs={{0,12},{4,8},{8,4},{12,0},{16,28},{20,24},{24,20},{28,16},{1,13},{... | collective-permute-start | bytes 98312 | tf_op jit(solution)/shard_map/ppermute | solution.py:331
  38.2 0.2 collective-permute-done.13.other_ref
  38.5 0.3 collective-permute-start.16
  38.8 0.9 %collective-permute-start.15 = (bf16[256,128]{1,0:T(8,128)(2,1)S(1)}, bf16[256,128]{1,0:T(8,128)(2,1)S(1)}, u32[]{:S(2)}, u32[]{:S(2)}) collective-permute-start(bf16[256,128]{1,0:T(8,128)(2,1)S(1)} %shard_map.181.refs_0_), channel_id=1, source_target_pairs={{0,4},{4,0},{8,12},{12,8},{16,20},{20,16},{24,28},{28,24},{1,5},{5... | collective-permute-start | bytes 196616 | tf_op jit(solution)/shard_map/ppermute | solution.py:331
  39.6 2.4 %collective-permute-start.14 = (bf16[256,128]{1,0:T(8,128)(2,1)S(1)}, bf16[256,128]{1,0:T(8,128)(2,1)S(1)}, u32[]{:S(2)}, u32[]{:S(2)}) collective-permute-start(bf16[256,128]{1,0:T(8,128)(2,1)S(1)} %shard_map.181.refs_0_), channel_id=1, source_target_pairs={{0,12},{4,8},{8,4},{12,0},{16,28},{20,24},{24,20},{28,16},{1,13},{... | collective-permute-start | bytes 196616 | tf_op jit(solution)/shard_map/ppermute | solution.py:331
  42.0 0.9 %shard_map.179 = (bf16[256,128]{1,0:T(8,128)(2,1)}, f32[1,128]{1,0:T(1,128)}) custom-call(s32[1]{0:T(128)} %bitcast.side_ref, s32[1]{0:T(128)} %bitcast.1.seat_ref, f32[256,128]{1,0:T(8,128)S(1)} %get-tuple-element.61.back_ref, bf16[256,512]{1,0:T(8,128)(2,1)S(1)} %get-tuple-element.62.mark_ref, bf16[128,128]{1,0:T(8,128)(2,1)S(1)} %get-tuple-element.65.refs_0_, ...), custom_call_target="tpu_custom_call" | custom-call | flops 2000000000 | bytes 1000000 | tf_op jit(solution)/shard_map/pallas_call | solution.py:482
  42.9 0.2 collective-permute-done.15.refs_1_
  43.0 0.8 %shard_map.182 = (f32[128,512]{1,0:T(8,128)}, f32[128,512]{1,0:T(8,128)}) custom-call(s32[1]{0:T(128)} %bitcast.1.seat_ref, bf16[256,128]{1,0:T(8,128)(2,1)S(1)} %shard_map.181.refs_0_, bf16[256,128]{1,0:T(8,128)(2,1)S(1)} %collective-permute-done.15.refs_1_, bf16[256,128]{1,0:T(8,128)(2,1)S(1)} %collective-permute-done.16.refs_2_), custom_call_target="tpu_custom_call" | custom-call | tf_op jit(solution)/shard_map/pallas_call | solution.py:492
  43.9 1.0 %collective-permute-done.14.got_ref = bf16[256,128]{1,0:T(8,128)(2,1)S(1)} collective-permute-done((bf16[256,128]{1,0:T(8,128)(2,1)S(1)}, bf16[256,128]{1,0:T(8,128)(2,1)S(1)}, u32[]{:S(2)}, u32[]{:S(2)}) %collective-permute-start.14) | collective-permute-done | bytes 65568 | tf_op jit(solution)/shard_map/ppermute | solution.py:331
  44.8 0.7 %shard_map.183 = (f32[128,512]{1,0:T(8,128)}, f32[128,512]{1,0:T(8,128)}) custom-call(s32[1]{0:T(128)} %bitcast.1.seat_ref, bf16[256,128]{1,0:T(8,128)(2,1)S(1)} %collective-permute-done.14.got_ref, f32[128,512]{1,0:T(8,128)} %get-tuple-element.74.begun_self_ref, ...), custom_call_target="tpu_custom_call", output_to_operand_aliasing={{0}: (2, {}), {1}: (3, {})} | custom-call | tf_op jit(solution)/shard_map/pallas_call | solution.py:501
  (21 shorter events, 0.2 us)
Async XLA Ops:
  2.6 16.1 %collective-permute-start.1 = (bf16[1552,128]{1,0:T(8,128)(2,1)S(1)}, bf16[1552,128]{1,0:T(8,128)(2,1)S(1)}, u32[]{:S(2)}, u32[]{:S(2)}) collective-permute-start(bf16[1552,128]{1,0:T(8,128)(2,1)S(1)} %get-tuple-element.51.refs_0_), channel_id=1, source_target_pairs={{0,2},{1,3},{2,0},{3,1},{4,6},{5,7},{6,4},{7,5},{8,10},{9,11},{10,... | collective-permute-start | bytes 1191944 | tf_op jit(solution)/shard_map/ppermute | solution.py:331
  5.6 13.1 %all-to-all-start = ((bf16[8,56,128]{2,1,0:T(8,128)(2,1)}), bf16[8,56,128]{2,1,0:T(8,128)(2,1)S(1)}, u32[]{:S(2)}, u32[]{:S(2)}) async-start(bf16[8,56,128]{2,1,0:T(8,128)(2,1)} %get-tuple-element.53), calls=%async_computation | async-start | bytes 229376 | tf_op jit(solution)/shard_map/all_to_all | solution.py:335
  11.5 12.1 %collective-permute-start = (bf16[1552,128]{1,0:T(8,128)(2,1)S(1)}, bf16[1552,128]{1,0:T(8,128)(2,1)S(1)}, u32[]{:S(2)}, u32[]{:S(2)}) collective-permute-start(bf16[1552,128]{1,0:T(8,128)(2,1)S(1)} %get-tuple-element.51.refs_0_), channel_id=1, source_target_pairs={{0,1},{1,0},{2,3},{3,2},{4,5},{5,4},{6,7},{7,6},{8,9},{9,8},{10,11... | collective-permute-start | bytes 1191944 | tf_op jit(solution)/shard_map/ppermute | solution.py:331
  12.1 6.6 %copy-start.1 = (bf16[256,128]{1,0:T(8,128)(2,1)S(1)}, bf16[256,128]{1,0:T(8,128)(2,1)}, u32[]{:S(2)}) copy-start(bf16[256,128]{1,0:T(8,128)(2,1)} %x_ref.5) | copy-start | bytes 196612
  18.7 6.1 %copy-start = (bf16[128,512]{1,0:T(8,128)(2,1)S(1)}, bf16[128,512]{1,0:T(8,128)(2,1)}, u32[]{:S(2)}) copy-start(bf16[128,512]{1,0:T(8,128)(2,1)} %ws_ref.5) | copy-start | bytes 393220
  18.7 6.1 %copy-start.2 = (bf16[128,512]{1,0:T(8,128)(2,1)S(1)}, bf16[128,512]{1,0:T(8,128)(2,1)}, u32[]{:S(2)}) copy-start(bf16[128,512]{1,0:T(8,128)(2,1)} %wn_ref.3) | copy-start | bytes 393220
  19.0 5.8 %collective-permute-start.2 = (bf16[1552,128]{1,0:T(8,128)(2,1)S(1)}, bf16[1552,128]{1,0:T(8,128)(2,1)S(1)}, u32[]{:S(2)}, u32[]{:S(2)}) collective-permute-start(bf16[1552,128]{1,0:T(8,128)(2,1)S(1)} %get-tuple-element.54.refs_2_), channel_id=1, source_target_pairs={{0,1},{1,0},{2,3},{3,2},{4,5},{5,4},{6,7},{7,6},{8,9},{9,8},{10,11... | collective-permute-start | bytes 1191944 | tf_op jit(solution)/shard_map/ppermute | solution.py:331
  19.1 4.5 %collective-permute-start.4 = (bf16[256,128]{1,0:T(8,128)(2,1)S(1)}, bf16[256,128]{1,0:T(8,128)(2,1)S(1)}, u32[]{:S(2)}, u32[]{:S(2)}) collective-permute-start(bf16[256,128]{1,0:T(8,128)(2,1)S(1)} %get-tuple-element.55.refs_4_), channel_id=1, source_target_pairs={{0,2},{1,3},{2,0},{3,1},{4,6},{5,7},{6,4},{7,5},{8,10},{9,11},{10,... | collective-permute-start | bytes 196616 | tf_op jit(solution)/shard_map/ppermute | solution.py:331
  19.7 3.9 %collective-permute-start.3 = (bf16[256,128]{1,0:T(8,128)(2,1)S(1)}, bf16[256,128]{1,0:T(8,128)(2,1)S(1)}, u32[]{:S(2)}, u32[]{:S(2)}) collective-permute-start(bf16[256,128]{1,0:T(8,128)(2,1)S(1)} %get-tuple-element.55.refs_4_), channel_id=1, source_target_pairs={{0,1},{1,0},{2,3},{3,2},{4,5},{5,4},{6,7},{7,6},{8,9},{9,8},{10,11... | collective-permute-start | bytes 196616 | tf_op jit(solution)/shard_map/ppermute | solution.py:331
  23.6 1.3 %collective-permute-start.5 = (bf16[256,128]{1,0:T(8,128)(2,1)S(1)}, bf16[256,128]{1,0:T(8,128)(2,1)S(1)}, u32[]{:S(2)}, u32[]{:S(2)}) collective-permute-start(bf16[256,128]{1,0:T(8,128)(2,1)S(1)} %collective-permute-done.4.refs_6_), channel_id=1, source_target_pairs={{0,1},{1,0},{2,3},{3,2},{4,5},{5,4},{6,7},{7,6},{8,9},{9,8},{10,11... | collective-permute-start | bytes 196616 | tf_op jit(solution)/shard_map/ppermute | solution.py:331
  25.9 5.8 %collective-permute-start.10 = (bf16[256,128]{1,0:T(8,128)(2,1)S(1)}, bf16[256,128]{1,0:T(8,128)(2,1)S(1)}, u32[]{:S(2)}, u32[]{:S(2)}) collective-permute-start(bf16[256,128]{1,0:T(8,128)(2,1)S(1)} %get-tuple-element.70), channel_id=1, source_target_pairs={{0,12},{4,8},{8,4},{12,0},{16,28},{20,24},{24,20},{28,16},{1,13},{... | collective-permute-start | bytes 196616 | tf_op jit(solution)/shard_map/ppermute | solution.py:331
  26.7 5.0 %collective-permute-start.11 = (bf16[256,128]{1,0:T(8,128)(2,1)S(1)}, bf16[256,128]{1,0:T(8,128)(2,1)S(1)}, u32[]{:S(2)}, u32[]{:S(2)}) collective-permute-start(bf16[256,128]{1,0:T(8,128)(2,1)S(1)} %get-tuple-element.71), channel_id=1, source_target_pairs={{0,8},{4,12},{8,0},{12,4},{16,24},{20,28},{24,16},{28,20},{1,9},{5... | collective-permute-start | bytes 196616 | tf_op jit(solution)/shard_map/ppermute | solution.py:331
  27.7 4.7 %collective-permute-start.12 = (bf16[256,128]{1,0:T(8,128)(2,1)S(1)}, bf16[256,128]{1,0:T(8,128)(2,1)S(1)}, u32[]{:S(2)}, u32[]{:S(2)}) collective-permute-start(bf16[256,128]{1,0:T(8,128)(2,1)S(1)} %get-tuple-element.72), channel_id=1, source_target_pairs={{0,4},{4,0},{8,12},{12,8},{16,20},{20,16},{24,28},{28,24},{1,5},{5... | collective-permute-start | bytes 196616 | tf_op jit(solution)/shard_map/ppermute | solution.py:331
  29.5 5.1 %collective-permute-start.6 = (bf16[4,56,128]{2,1,0:T(8,128)(2,1)S(1)}, bf16[4,56,128]{2,1,0:T(8,128)(2,1)S(1)}, u32[]{:S(2)}, u32[]{:S(2)}) collective-permute-start(bf16[4,56,128]{2,1,0:T(8,128)(2,1)S(1)} %get-tuple-element.64), channel_id=1, source_target_pairs={{0,16},{4,20},{8,24},{12,28},{16,0},{20,4},{24,8},{28,12},{1,17},{... | collective-permute-start | bytes 172040 | tf_op jit(solution)/shard_map/ppermute | solution.py:331
  32.5 5.9 %collective-permute-start.13 = (bf16[256,128]{1,0:T(8,128)(2,1)S(1)}, bf16[256,128]{1,0:T(8,128)(2,1)S(1)}, u32[]{:S(2)}, u32[]{:S(2)}) collective-permute-start(bf16[256,128]{1,0:T(8,128)(2,1)S(1)} %shard_map.180.own_ref), channel_id=1, source_target_pairs={{0,16},{4,20},{8,24},{12,28},{16,0},{20,4},{24,8},{28,12},{1,17},{... | collective-permute-start | bytes 196616 | tf_op jit(solution)/shard_map/ppermute | solution.py:331
  34.7 5.0 %collective-permute-start.7 = (bf16[128,128]{1,0:T(8,128)(2,1)S(1)}, bf16[128,128]{1,0:T(8,128)(2,1)S(1)}, u32[]{:S(2)}, u32[]{:S(2)}) collective-permute-start(bf16[128,128]{1,0:T(8,128)(2,1)S(1)} %get-tuple-element.66), channel_id=1, source_target_pairs={{0,4},{4,0},{8,12},{12,8},{16,20},{20,16},{24,28},{28,24},{1,5},{5... | collective-permute-start | bytes 98312 | tf_op jit(solution)/shard_map/ppermute | solution.py:331
  35.5 6.5 %collective-permute-start.8 = (bf16[128,128]{1,0:T(8,128)(2,1)S(1)}, bf16[128,128]{1,0:T(8,128)(2,1)S(1)}, u32[]{:S(2)}, u32[]{:S(2)}) collective-permute-start(bf16[128,128]{1,0:T(8,128)(2,1)S(1)} %get-tuple-element.67), channel_id=1, source_target_pairs={{0,8},{4,12},{8,0},{12,4},{16,24},{20,28},{24,16},{28,20},{1,9},{5... | collective-permute-start | bytes 98312 | tf_op jit(solution)/shard_map/ppermute | solution.py:331
  36.1 6.0 %collective-permute-start.9 = (bf16[128,128]{1,0:T(8,128)(2,1)S(1)}, bf16[128,128]{1,0:T(8,128)(2,1)S(1)}, u32[]{:S(2)}, u32[]{:S(2)}) collective-permute-start(bf16[128,128]{1,0:T(8,128)(2,1)S(1)} %get-tuple-element.68), channel_id=1, source_target_pairs={{0,12},{4,8},{8,4},{12,0},{16,28},{20,24},{24,20},{28,16},{1,13},{... | collective-permute-start | bytes 98312 | tf_op jit(solution)/shard_map/ppermute | solution.py:331
  38.5 4.4 %collective-permute-start.16 = (bf16[256,128]{1,0:T(8,128)(2,1)S(1)}, bf16[256,128]{1,0:T(8,128)(2,1)S(1)}, u32[]{:S(2)}, u32[]{:S(2)}) collective-permute-start(bf16[256,128]{1,0:T(8,128)(2,1)S(1)} %shard_map.181.refs_0_), channel_id=1, source_target_pairs={{0,8},{4,12},{8,0},{12,4},{16,24},{20,28},{24,16},{28,20},{1,9},{5... | collective-permute-start | bytes 196616 | tf_op jit(solution)/shard_map/ppermute | solution.py:331
  38.8 4.3 %collective-permute-start.15 = (bf16[256,128]{1,0:T(8,128)(2,1)S(1)}, bf16[256,128]{1,0:T(8,128)(2,1)S(1)}, u32[]{:S(2)}, u32[]{:S(2)}) collective-permute-start(bf16[256,128]{1,0:T(8,128)(2,1)S(1)} %shard_map.181.refs_0_), channel_id=1, source_target_pairs={{0,4},{4,0},{8,12},{12,8},{16,20},{20,16},{24,28},{28,24},{1,5},{5... | collective-permute-start | bytes 196616 | tf_op jit(solution)/shard_map/ppermute | solution.py:331
  39.6 5.2 %collective-permute-start.14 = (bf16[256,128]{1,0:T(8,128)(2,1)S(1)}, bf16[256,128]{1,0:T(8,128)(2,1)S(1)}, u32[]{:S(2)}, u32[]{:S(2)}) collective-permute-start(bf16[256,128]{1,0:T(8,128)(2,1)S(1)} %shard_map.181.refs_0_), channel_id=1, source_target_pairs={{0,12},{4,8},{8,4},{12,0},{16,28},{20,24},{24,20},{28,16},{1,13},{... | collective-permute-start | bytes 196616 | tf_op jit(solution)/shard_map/ppermute | solution.py:331

commit v19 on v18

--- a/solution.py
+++ b/solution.py
@@ -445,7 +445,9 @@
         compiler_params=PARAMS,
     )(me, side, seat, features, w_self, w_neigh, turned, pack, near, far, last, *every)
 
-    arrived = swap(returned)[::-1] if direct else [exchange(returned[0], halves)]
+    arrived = swap(returned) if direct else [exchange(returned[0], halves)]
+    if direct:
+        arrived = arrived[-2:0:-1] + arrived[-1:] + arrived[:1]
     mirror = partner(mirror, "dom", half)
     output, back, ghosts = pl.pallas_call(
         functools.partial(side_kernel, slots, hub_here, count),

time: 45.8 us -> 47.2 us (1.031)
  waiting for transfers between devices: 15.4 us -> 17 us
    ppermute x17, waiting for transfers between devices: 9.22 us -> 10.9 us  [partner(): lax.ppermute(block, axis, [(i, i ^ k) for i in range(lax.axis_size(axis))])]
  transfers between devices with their start and end apart: 18 -> 18, of which waited for: 9 -> 8; matrix products, arithmetic and copies ran while one was open for 0% -> 0% of each run, Pallas kernels for 7% -> 7%
where the time goes in v19:
time: 47.2 us; the launch traced here: 46.9 us
  starting transfers between devices  21.4 us (45%)
  waiting for transfers between devices  17 us (36%)
  Pallas kernels  7.04 us (15%)
  between operations  1.39 us (3%)
    ppermute x17, starting transfers between devices, partner(): lax.ppermute(block, axis, [(i, i ^ k) for i in range(lax.axis_size(axis))])  15.6 us
    ppermute x17, waiting for transfers between devices, partner(): lax.ppermute(block, axis, [(i, i ^ k) for i in range(lax.axis_size(axis))])  10.9 us
    all_to_all x1, waiting for transfers between devices, exchange(): lax.all_to_all(blocks, 'dom', split_axis=0, concat_axis=0, axis_index_gro...  6.16 us
    all_to_all x1, starting transfers between devices, exchange(): lax.all_to_all(blocks, 'dom', split_axis=0, concat_axis=0, axis_index_gro...  5.83 us
    pallas_call x1, Pallas kernels, on_device(): pl.pallas_call(functools.partial(send_kernel, width), out_shape=(shape((p...  2 us
    pallas_call x1, Pallas kernels, on_device(): pl.pallas_call(functools.partial(dense_kernel, slots, hub_here, feats, wi...  1.07 us
  transfers between devices with their start and end apart: 18, of which 8 were waited for; matrix products, arithmetic and copies ran while one was open for 0% of the time, Pallas kernels for 7%

profile of v19, /device:TPU:0, one launch (start us, length us, event | category | flops | bytes accessed | tf_op | source)
XLA Modules:
  0.0 46.9 jit_solution(15379293377880642846)
XLA Ops:
  0.6 2.0 %shard_map.173 = (bf16[8,56,128]{2,1,0:T(8,128)(2,1)}, bf16[1552,128]{1,0:T(8,128)(2,1)S(1)}, s32[1,8,48]{2,1,0:T(8,128)S(1)}, s32[1,2]{1,0:T(1,128)S(1)}, s32[1...) custom-call(bf16[256,128]{1,0:T(8,128)(2,1)} %x_ref.5, ...), custom_call_target="tpu_custom_call" | custom-call | tf_op jit(solution)/shard_map/pallas_call | solution.py:384
  2.6 3.0 %collective-permute-start.1 = (bf16[1552,128]{1,0:T(8,128)(2,1)S(1)}, bf16[1552,128]{1,0:T(8,128)(2,1)S(1)}, u32[]{:S(2)}, u32[]{:S(2)}) collective-permute-start(bf16[1552,128]{1,0:T(8,128)(2,1)S(1)} %get-tuple-element.51.refs_0_), channel_id=1, source_target_pairs={{0,2},{1,3},{2,0},{3,1},{4,6},{5,7},{6,4},{7,5},{8,10},{9,11},{10,... | collective-permute-start | bytes 1191944 | tf_op jit(solution)/shard_map/ppermute | solution.py:331
  5.6 5.8 %all-to-all-start = ((bf16[8,56,128]{2,1,0:T(8,128)(2,1)}), bf16[8,56,128]{2,1,0:T(8,128)(2,1)S(1)}, u32[]{:S(2)}, u32[]{:S(2)}) async-start(bf16[8,56,128]{2,1,0:T(8,128)(2,1)} %get-tuple-element.53), calls=%async_computation | async-start | bytes 229376 | tf_op jit(solution)/shard_map/all_to_all | solution.py:335
  12.1 0.4 shard_map.174
  12.5 6.2 %all-to-all-done.got_ref = bf16[8,56,128]{2,1,0:T(8,128)(2,1)S(1)} async-done(((bf16[8,56,128]{2,1,0:T(8,128)(2,1)}), bf16[8,56,128]{2,1,0:T(8,128)(2,1)S(1)}, u32[]{:S(2)}, u32[]{:S(2)}) %all-to-all-start) | async-done | bytes 114720 | tf_op jit(solution)/shard_map/all_to_all | solution.py:335
  18.7 0.3 shard_map.175
  19.0 0.1 collective-permute-start.2
  19.1 0.6 %collective-permute-start.4 = (bf16[256,128]{1,0:T(8,128)(2,1)S(1)}, bf16[256,128]{1,0:T(8,128)(2,1)S(1)}, u32[]{:S(2)}, u32[]{:S(2)}) collective-permute-start(bf16[256,128]{1,0:T(8,128)(2,1)S(1)} %get-tuple-element.55.refs_4_), channel_id=1, source_target_pairs={{0,2},{1,3},{2,0},{3,1},{4,6},{5,7},{6,4},{7,5},{8,10},{9,11},{10,... | collective-permute-start | bytes 196616 | tf_op jit(solution)/shard_map/ppermute | solution.py:331
  19.7 0.2 collective-permute-start.3
  19.9 3.7 %collective-permute-done.4.refs_6_ = bf16[256,128]{1,0:T(8,128)(2,1)S(1)} collective-permute-done((bf16[256,128]{1,0:T(8,128)(2,1)S(1)}, bf16[256,128]{1,0:T(8,128)(2,1)S(1)}, u32[]{:S(2)}, u32[]{:S(2)}) %collective-permute-start.4) | collective-permute-done | bytes 65568 | tf_op jit(solution)/shard_map/ppermute | solution.py:331
  23.6 1.2 %collective-permute-done.5.refs_7_ = bf16[256,128]{1,0:T(8,128)(2,1)S(1)} collective-permute-done((bf16[256,128]{1,0:T(8,128)(2,1)S(1)}, bf16[256,128]{1,0:T(8,128)(2,1)S(1)}, u32[]{:S(2)}, u32[]{:S(2)}) %collective-permute-start.5) | collective-permute-done | bytes 65568 | tf_op jit(solution)/shard_map/ppermute | solution.py:331
  24.9 1.1 %shard_map.176 = (f32[256,128]{1,0:T(8,128)S(1)}, bf16[256,512]{1,0:T(8,128)(2,1)S(1)}, bf16[256,128]{1,0:T(8,128)(2,1)S(1)}, f32[1,128]{1,0:T(1,128)S(1)}, bf16...) custom-call(s32[1]{0:T(128)} %bitcast.2.me_ref, ...), custom_call_target="tpu_custom_call" | custom-call | tf_op jit(solution)/shard_map/pallas_call | solution.py:429
  25.9 0.1 collective-permute-start.10
  26.0 1.3 %collective-permute-start.11 = (bf16[256,128]{1,0:T(8,128)(2,1)S(1)}, bf16[256,128]{1,0:T(8,128)(2,1)S(1)}, u32[]{:S(2)}, u32[]{:S(2)}) collective-permute-start(bf16[256,128]{1,0:T(8,128)(2,1)S(1)} %get-tuple-element.71), channel_id=1, source_target_pairs={{0,4},{4,0},{8,12},{12,8},{16,20},{20,16},{24,28},{28,24},{1,5},{5... | collective-permute-start | bytes 196616 | tf_op jit(solution)/shard_map/ppermute | solution.py:331
  27.3 2.2 %collective-permute-start.12 = (bf16[256,128]{1,0:T(8,128)(2,1)S(1)}, bf16[256,128]{1,0:T(8,128)(2,1)S(1)}, u32[]{:S(2)}, u32[]{:S(2)}) collective-permute-start(bf16[256,128]{1,0:T(8,128)(2,1)S(1)} %get-tuple-element.72), channel_id=1, source_target_pairs={{0,12},{4,8},{8,4},{12,0},{16,28},{20,24},{24,20},{28,16},{1,13},{... | collective-permute-start | bytes 196616 | tf_op jit(solution)/shard_map/ppermute | solution.py:331
  29.5 0.4 collective-permute-start.6
  29.9 0.9 %shard_map.177 = (bf16[256,128]{1,0:T(8,128)(2,1)}, f32[256,128]{1,0:T(8,128)S(1)}, bf16[4,64,128]{2,1,0:T(8,128)(2,1)S(1)}) custom-call(s32[1]{0:T(128)} %bitcast.side_ref, s32[1]{0:T(128)} %bitcast.1.seat_ref, f32[256,128]{1,0:T(8,128)S(1)} %get-tuple-element.56.own_ref, bf16[256,512]{1,0:T(8,128)(2,1)S(1)} %get-tuple-element.57.grad_ref, ...), custom_call_target="tpu_custom_call" | custom-call | flops 100000000 | bytes 1000000 | tf_op jit(solution)/shard_map/pallas_call | solution.py:452
  30.8 2.3 %collective-permute-done.12.refs_2_ = bf16[256,128]{1,0:T(8,128)(2,1)S(1)} collective-permute-done((bf16[256,128]{1,0:T(8,128)(2,1)S(1)}, bf16[256,128]{1,0:T(8,128)(2,1)S(1)}, u32[]{:S(2)}, u32[]{:S(2)}) %collective-permute-start.12) | collective-permute-done | bytes 65568 | tf_op jit(solution)/shard_map/ppermute | solution.py:331
  33.1 0.7 %collective-permute-start.13 = (bf16[256,128]{1,0:T(8,128)(2,1)S(1)}, bf16[256,128]{1,0:T(8,128)(2,1)S(1)}, u32[]{:S(2)}, u32[]{:S(2)}) collective-permute-start(bf16[256,128]{1,0:T(8,128)(2,1)S(1)} %shard_map.180.own_ref), channel_id=1, source_target_pairs={{0,16},{4,20},{8,24},{12,28},{16,0},{20,4},{24,8},{28,12},{1,17},{... | collective-permute-start | bytes 196616 | tf_op jit(solution)/shard_map/ppermute | solution.py:331
  33.8 1.1 %collective-permute-done.6.mirror_ref = bf16[4,56,128]{2,1,0:T(8,128)(2,1)S(1)} collective-permute-done((bf16[4,56,128]{2,1,0:T(8,128)(2,1)S(1)}, bf16[4,56,128]{2,1,0:T(8,128)(2,1)S(1)}, u32[]{:S(2)}, u32[]{:S(2)}) %collective-permute-start.6) | collective-permute-done | bytes 57376 | tf_op jit(solution)/shard_map/ppermute | solution.py:331
  35.0 0.5 %collective-permute-start.7 = (bf16[128,128]{1,0:T(8,128)(2,1)S(1)}, bf16[128,128]{1,0:T(8,128)(2,1)S(1)}, u32[]{:S(2)}, u32[]{:S(2)}) collective-permute-start(bf16[128,128]{1,0:T(8,128)(2,1)S(1)} %get-tuple-element.66), channel_id=1, source_target_pairs={{0,4},{4,0},{8,12},{12,8},{16,20},{20,16},{24,28},{28,24},{1,5},{5... | collective-permute-start | bytes 98312 | tf_op jit(solution)/shard_map/ppermute | solution.py:331
  35.5 0.9 %collective-permute-start.8 = (bf16[128,128]{1,0:T(8,128)(2,1)S(1)}, bf16[128,128]{1,0:T(8,128)(2,1)S(1)}, u32[]{:S(2)}, u32[]{:S(2)}) collective-permute-start(bf16[128,128]{1,0:T(8,128)(2,1)S(1)} %get-tuple-element.67), channel_id=1, source_target_pairs={{0,8},{4,12},{8,0},{12,4},{16,24},{20,28},{24,16},{28,20},{1,9},{5... | collective-permute-start | bytes 98312 | tf_op jit(solution)/shard_map/ppermute | solution.py:331
  36.4 2.1 %collective-permute-start.9 = (bf16[128,128]{1,0:T(8,128)(2,1)S(1)}, bf16[128,128]{1,0:T(8,128)(2,1)S(1)}, u32[]{:S(2)}, u32[]{:S(2)}) collective-permute-start(bf16[128,128]{1,0:T(8,128)(2,1)S(1)} %get-tuple-element.68), channel_id=1, source_target_pairs={{0,12},{4,8},{8,4},{12,0},{16,28},{20,24},{24,20},{28,16},{1,13},{... | collective-permute-start | bytes 98312 | tf_op jit(solution)/shard_map/ppermute | solution.py:331
  38.5 0.4 collective-permute-done.13.other_ref
  39.0 0.3 collective-permute-start.16
  39.2 1.9 %collective-permute-start.15 = (bf16[256,128]{1,0:T(8,128)(2,1)S(1)}, bf16[256,128]{1,0:T(8,128)(2,1)S(1)}, u32[]{:S(2)}, u32[]{:S(2)}) collective-permute-start(bf16[256,128]{1,0:T(8,128)(2,1)S(1)} %shard_map.181.refs_0_), channel_id=1, source_target_pairs={{0,4},{4,0},{8,12},{12,8},{16,20},{20,16},{24,28},{28,24},{1,5},{5... | collective-permute-start | bytes 196616 | tf_op jit(solution)/shard_map/ppermute | solution.py:331
  41.1 1.4 %collective-permute-start.14 = (bf16[256,128]{1,0:T(8,128)(2,1)S(1)}, bf16[256,128]{1,0:T(8,128)(2,1)S(1)}, u32[]{:S(2)}, u32[]{:S(2)}) collective-permute-start(bf16[256,128]{1,0:T(8,128)(2,1)S(1)} %shard_map.181.refs_0_), channel_id=1, source_target_pairs={{0,12},{4,8},{8,4},{12,0},{16,28},{20,24},{24,20},{28,16},{1,13},{... | collective-permute-start | bytes 196616 | tf_op jit(solution)/shard_map/ppermute | solution.py:331
  42.5 0.9 %shard_map.179 = (bf16[256,128]{1,0:T(8,128)(2,1)}, f32[1,128]{1,0:T(1,128)}) custom-call(s32[1]{0:T(128)} %bitcast.side_ref, s32[1]{0:T(128)} %bitcast.1.seat_ref, f32[256,128]{1,0:T(8,128)S(1)} %get-tuple-element.61.back_ref, bf16[256,512]{1,0:T(8,128)(2,1)S(1)} %get-tuple-element.62.mark_ref, bf16[128,128]{1,0:T(8,128)(2,1)S(1)} %get-tuple-element.65.refs_0_, ...), custom_call_target="tpu_custom_call" | custom-call | flops 2000000000 | bytes 1000000 | tf_op jit(solution)/shard_map/pallas_call | solution.py:484
  43.4 0.1 collective-permute-done.15.refs_1_
  43.5 0.8 %shard_map.182 = (f32[128,512]{1,0:T(8,128)}, f32[128,512]{1,0:T(8,128)}) custom-call(s32[1]{0:T(128)} %bitcast.1.seat_ref, bf16[256,128]{1,0:T(8,128)(2,1)S(1)} %shard_map.181.refs_0_, bf16[256,128]{1,0:T(8,128)(2,1)S(1)} %collective-permute-done.15.refs_1_, bf16[256,128]{1,0:T(8,128)(2,1)S(1)} %collective-permute-done.16.refs_2_), custom_call_target="tpu_custom_call" | custom-call | tf_op jit(solution)/shard_map/pallas_call | solution.py:494
  44.3 1.9 %collective-permute-done.14.got_ref = bf16[256,128]{1,0:T(8,128)(2,1)S(1)} collective-permute-done((bf16[256,128]{1,0:T(8,128)(2,1)S(1)}, bf16[256,128]{1,0:T(8,128)(2,1)S(1)}, u32[]{:S(2)}, u32[]{:S(2)}) %collective-permute-start.14) | collective-permute-done | bytes 65568 | tf_op jit(solution)/shard_map/ppermute | solution.py:331
  46.2 0.7 %shard_map.183 = (f32[128,512]{1,0:T(8,128)}, f32[128,512]{1,0:T(8,128)}) custom-call(s32[1]{0:T(128)} %bitcast.1.seat_ref, bf16[256,128]{1,0:T(8,128)(2,1)S(1)} %collective-permute-done.14.got_ref, f32[128,512]{1,0:T(8,128)} %get-tuple-element.74.begun_self_ref, ...), custom_call_target="tpu_custom_call", output_to_operand_aliasing={{0}: (2, {}), {1}: (3, {})} | custom-call | tf_op jit(solution)/shard_map/pallas_call | solution.py:503
  (21 shorter events, 0.1 us)
Async XLA Ops:
  2.6 16.1 %collective-permute-start.1 = (bf16[1552,128]{1,0:T(8,128)(2,1)S(1)}, bf16[1552,128]{1,0:T(8,128)(2,1)S(1)}, u32[]{:S(2)}, u32[]{:S(2)}) collective-permute-start(bf16[1552,128]{1,0:T(8,128)(2,1)S(1)} %get-tuple-element.51.refs_0_), channel_id=1, source_target_pairs={{0,2},{1,3},{2,0},{3,1},{4,6},{5,7},{6,4},{7,5},{8,10},{9,11},{10,... | collective-permute-start | bytes 1191944 | tf_op jit(solution)/shard_map/ppermute | solution.py:331
  5.6 13.1 %all-to-all-start = ((bf16[8,56,128]{2,1,0:T(8,128)(2,1)}), bf16[8,56,128]{2,1,0:T(8,128)(2,1)S(1)}, u32[]{:S(2)}, u32[]{:S(2)}) async-start(bf16[8,56,128]{2,1,0:T(8,128)(2,1)} %get-tuple-element.53), calls=%async_computation | async-start | bytes 229376 | tf_op jit(solution)/shard_map/all_to_all | solution.py:335
  11.5 12.1 %collective-permute-start = (bf16[1552,128]{1,0:T(8,128)(2,1)S(1)}, bf16[1552,128]{1,0:T(8,128)(2,1)S(1)}, u32[]{:S(2)}, u32[]{:S(2)}) collective-permute-start(bf16[1552,128]{1,0:T(8,128)(2,1)S(1)} %get-tuple-element.51.refs_0_), channel_id=1, source_target_pairs={{0,1},{1,0},{2,3},{3,2},{4,5},{5,4},{6,7},{7,6},{8,9},{9,8},{10,11... | collective-permute-start | bytes 1191944 | tf_op jit(solution)/shard_map/ppermute | solution.py:331
  12.1 6.6 %copy-start.1 = (bf16[256,128]{1,0:T(8,128)(2,1)S(1)}, bf16[256,128]{1,0:T(8,128)(2,1)}, u32[]{:S(2)}) copy-start(bf16[256,128]{1,0:T(8,128)(2,1)} %x_ref.5) | copy-start | bytes 196612
  18.7 6.1 %copy-start = (bf16[128,512]{1,0:T(8,128)(2,1)S(1)}, bf16[128,512]{1,0:T(8,128)(2,1)}, u32[]{:S(2)}) copy-start(bf16[128,512]{1,0:T(8,128)(2,1)} %ws_ref.5) | copy-start | bytes 393220
  18.7 6.1 %copy-start.2 = (bf16[128,512]{1,0:T(8,128)(2,1)S(1)}, bf16[128,512]{1,0:T(8,128)(2,1)}, u32[]{:S(2)}) copy-start(bf16[128,512]{1,0:T(8,128)(2,1)} %wn_ref.3) | copy-start | bytes 393220
  19.0 5.8 %collective-permute-start.2 = (bf16[1552,128]{1,0:T(8,128)(2,1)S(1)}, bf16[1552,128]{1,0:T(8,128)(2,1)S(1)}, u32[]{:S(2)}, u32[]{:S(2)}) collective-permute-start(bf16[1552,128]{1,0:T(8,128)(2,1)S(1)} %get-tuple-element.54.refs_2_), channel_id=1, source_target_pairs={{0,1},{1,0},{2,3},{3,2},{4,5},{5,4},{6,7},{7,6},{8,9},{9,8},{10,11... | collective-permute-start | bytes 1191944 | tf_op jit(solution)/shard_map/ppermute | solution.py:331
  19.1 4.5 %collective-permute-start.4 = (bf16[256,128]{1,0:T(8,128)(2,1)S(1)}, bf16[256,128]{1,0:T(8,128)(2,1)S(1)}, u32[]{:S(2)}, u32[]{:S(2)}) collective-permute-start(bf16[256,128]{1,0:T(8,128)(2,1)S(1)} %get-tuple-element.55.refs_4_), channel_id=1, source_target_pairs={{0,2},{1,3},{2,0},{3,1},{4,6},{5,7},{6,4},{7,5},{8,10},{9,11},{10,... | collective-permute-start | bytes 196616 | tf_op jit(solution)/shard_map/ppermute | solution.py:331
  19.7 3.9 %collective-permute-start.3 = (bf16[256,128]{1,0:T(8,128)(2,1)S(1)}, bf16[256,128]{1,0:T(8,128)(2,1)S(1)}, u32[]{:S(2)}, u32[]{:S(2)}) collective-permute-start(bf16[256,128]{1,0:T(8,128)(2,1)S(1)} %get-tuple-element.55.refs_4_), channel_id=1, source_target_pairs={{0,1},{1,0},{2,3},{3,2},{4,5},{5,4},{6,7},{7,6},{8,9},{9,8},{10,11... | collective-permute-start | bytes 196616 | tf_op jit(solution)/shard_map/ppermute | solution.py:331
  23.6 1.3 %collective-permute-start.5 = (bf16[256,128]{1,0:T(8,128)(2,1)S(1)}, bf16[256,128]{1,0:T(8,128)(2,1)S(1)}, u32[]{:S(2)}, u32[]{:S(2)}) collective-permute-start(bf16[256,128]{1,0:T(8,128)(2,1)S(1)} %collective-permute-done.4.refs_6_), channel_id=1, source_target_pairs={{0,1},{1,0},{2,3},{3,2},{4,5},{5,4},{6,7},{7,6},{8,9},{9,8},{10,11... | collective-permute-start | bytes 196616 | tf_op jit(solution)/shard_map/ppermute | solution.py:331
  25.9 4.8 %collective-permute-start.10 = (bf16[256,128]{1,0:T(8,128)(2,1)S(1)}, bf16[256,128]{1,0:T(8,128)(2,1)S(1)}, u32[]{:S(2)}, u32[]{:S(2)}) collective-permute-start(bf16[256,128]{1,0:T(8,128)(2,1)S(1)} %get-tuple-element.70), channel_id=1, source_target_pairs={{0,8},{4,12},{8,0},{12,4},{16,24},{20,28},{24,16},{28,20},{1,9},{5... | collective-permute-start | bytes 196616 | tf_op jit(solution)/shard_map/ppermute | solution.py:331
  26.0 4.8 %collective-permute-start.11 = (bf16[256,128]{1,0:T(8,128)(2,1)S(1)}, bf16[256,128]{1,0:T(8,128)(2,1)S(1)}, u32[]{:S(2)}, u32[]{:S(2)}) collective-permute-start(bf16[256,128]{1,0:T(8,128)(2,1)S(1)} %get-tuple-element.71), channel_id=1, source_target_pairs={{0,4},{4,0},{8,12},{12,8},{16,20},{20,16},{24,28},{28,24},{1,5},{5... | collective-permute-start | bytes 196616 | tf_op jit(solution)/shard_map/ppermute | solution.py:331
  27.3 5.8 %collective-permute-start.12 = (bf16[256,128]{1,0:T(8,128)(2,1)S(1)}, bf16[256,128]{1,0:T(8,128)(2,1)S(1)}, u32[]{:S(2)}, u32[]{:S(2)}) collective-permute-start(bf16[256,128]{1,0:T(8,128)(2,1)S(1)} %get-tuple-element.72), channel_id=1, source_target_pairs={{0,12},{4,8},{8,4},{12,0},{16,28},{20,24},{24,20},{28,16},{1,13},{... | collective-permute-start | bytes 196616 | tf_op jit(solution)/shard_map/ppermute | solution.py:331
  29.5 5.5 %collective-permute-start.6 = (bf16[4,56,128]{2,1,0:T(8,128)(2,1)S(1)}, bf16[4,56,128]{2,1,0:T(8,128)(2,1)S(1)}, u32[]{:S(2)}, u32[]{:S(2)}) collective-permute-start(bf16[4,56,128]{2,1,0:T(8,128)(2,1)S(1)} %get-tuple-element.64), channel_id=1, source_target_pairs={{0,16},{4,20},{8,24},{12,28},{16,0},{20,4},{24,8},{28,12},{1,17},{... | collective-permute-start | bytes 172040 | tf_op jit(solution)/shard_map/ppermute | solution.py:331
  33.1 5.8 %collective-permute-start.13 = (bf16[256,128]{1,0:T(8,128)(2,1)S(1)}, bf16[256,128]{1,0:T(8,128)(2,1)S(1)}, u32[]{:S(2)}, u32[]{:S(2)}) collective-permute-start(bf16[256,128]{1,0:T(8,128)(2,1)S(1)} %shard_map.180.own_ref), channel_id=1, source_target_pairs={{0,16},{4,20},{8,24},{12,28},{16,0},{20,4},{24,8},{28,12},{1,17},{... | collective-permute-start | bytes 196616 | tf_op jit(solution)/shard_map/ppermute | solution.py:331
  35.0 6.1 %collective-permute-start.7 = (bf16[128,128]{1,0:T(8,128)(2,1)S(1)}, bf16[128,128]{1,0:T(8,128)(2,1)S(1)}, u32[]{:S(2)}, u32[]{:S(2)}) collective-permute-start(bf16[128,128]{1,0:T(8,128)(2,1)S(1)} %get-tuple-element.66), channel_id=1, source_target_pairs={{0,4},{4,0},{8,12},{12,8},{16,20},{20,16},{24,28},{28,24},{1,5},{5... | collective-permute-start | bytes 98312 | tf_op jit(solution)/shard_map/ppermute | solution.py:331
  35.5 7.0 %collective-permute-start.8 = (bf16[128,128]{1,0:T(8,128)(2,1)S(1)}, bf16[128,128]{1,0:T(8,128)(2,1)S(1)}, u32[]{:S(2)}, u32[]{:S(2)}) collective-permute-start(bf16[128,128]{1,0:T(8,128)(2,1)S(1)} %get-tuple-element.67), channel_id=1, source_target_pairs={{0,8},{4,12},{8,0},{12,4},{16,24},{20,28},{24,16},{28,20},{1,9},{5... | collective-permute-start | bytes 98312 | tf_op jit(solution)/shard_map/ppermute | solution.py:331
  36.4 6.1 %collective-permute-start.9 = (bf16[128,128]{1,0:T(8,128)(2,1)S(1)}, bf16[128,128]{1,0:T(8,128)(2,1)S(1)}, u32[]{:S(2)}, u32[]{:S(2)}) collective-permute-start(bf16[128,128]{1,0:T(8,128)(2,1)S(1)} %get-tuple-element.68), channel_id=1, source_target_pairs={{0,12},{4,8},{8,4},{12,0},{16,28},{20,24},{24,20},{28,16},{1,13},{... | collective-permute-start | bytes 98312 | tf_op jit(solution)/shard_map/ppermute | solution.py:331
  39.0 4.4 %collective-permute-start.16 = (bf16[256,128]{1,0:T(8,128)(2,1)S(1)}, bf16[256,128]{1,0:T(8,128)(2,1)S(1)}, u32[]{:S(2)}, u32[]{:S(2)}) collective-permute-start(bf16[256,128]{1,0:T(8,128)(2,1)S(1)} %shard_map.181.refs_0_), channel_id=1, source_target_pairs={{0,8},{4,12},{8,0},{12,4},{16,24},{20,28},{24,16},{28,20},{1,9},{5... | collective-permute-start | bytes 196616 | tf_op jit(solution)/shard_map/ppermute | solution.py:331
  39.2 4.3 %collective-permute-start.15 = (bf16[256,128]{1,0:T(8,128)(2,1)S(1)}, bf16[256,128]{1,0:T(8,128)(2,1)S(1)}, u32[]{:S(2)}, u32[]{:S(2)}) collective-permute-start(bf16[256,128]{1,0:T(8,128)(2,1)S(1)} %shard_map.181.refs_0_), channel_id=1, source_target_pairs={{0,4},{4,0},{8,12},{12,8},{16,20},{20,16},{24,28},{28,24},{1,5},{5... | collective-permute-start | bytes 196616 | tf_op jit(solution)/shard_map/ppermute | solution.py:331
  41.1 5.2 %collective-permute-start.14 = (bf16[256,128]{1,0:T(8,128)(2,1)S(1)}, bf16[256,128]{1,0:T(8,128)(2,1)S(1)}, u32[]{:S(2)}, u32[]{:S(2)}) collective-permute-start(bf16[256,128]{1,0:T(8,128)(2,1)S(1)} %shard_map.181.refs_0_), channel_id=1, source_target_pairs={{0,12},{4,8},{8,4},{12,0},{16,28},{20,24},{24,20},{28,16},{1,13},{... | collective-permute-start | bytes 196616 | tf_op jit(solution)/shard_map/ppermute | solution.py:331

commit v20 on v18

--- a/solution.py
+++ b/solution.py
@@ -45,7 +45,7 @@
 
 def send_kernel(
     width, x_ref, cot_ref, ws_ref, wn_ref, bias_ref, send_ref, hub_ref, pos_ref, live_ref, tile_ref, dest_ref, gw_ref, hw_ref,
-    out_ref, pack_ref, send_v, hub_v, pos_v, live_v, tile_v, dest_v, gw_v, hw_v, bias_v, place_ref, sems,
+    out_ref, pack_ref, send_v, hub_v, pos_v, live_v, tile_v, dest_v, gw_v, hw_v, bias_v, place_ref, taken_ref, sems,
 ):
     rows, cols = x_ref.shape
     depth, full = ws_ref.shape
@@ -75,15 +75,24 @@
         copy.wait()
     mark = source_matrix(send_v[0], hub_v[...], rows, width, place_ref[...])
     copies[2].wait()
-    taken = lax.dot_general(
-        mark, pack_ref[base : base + rows, :], (((0,), (0,)), ((), ())), preferred_element_type=F32
-    ).astype(BF)
     kept = out_ref.shape[1]
-    for q in range(peers):
-        out_ref[q] = taken[q * width : q * width + kept]
-    for copy in copies[3:]:
+    half = peers // 2
+    for part in range(2):
+        taken = lax.dot_general(
+            mark[:, part * half * width : (part + 1) * half * width],
+            pack_ref[base : base + rows, :],
+            (((0,), (0,)), ((), ())),
+            preferred_element_type=F32,
+        ).astype(BF)
+        for q in range(half):
+            taken_ref[part * half + q] = taken[q * width : q * width + kept]
+        mine = pl.ds(part * half, half)
+        copies.append(pltpu.make_async_copy(taken_ref.at[mine], out_ref.at[mine], sems.at[len(copies)]))
+        copies[-1].start()
+    copies[3].wait()
+    pack_ref[base + 2 * rows :, :] = jnp.broadcast_to(bias_v[...], (16, cols))
+    for copy in copies[4:]:
         copy.wait()
-    pack_ref[base + 2 * rows :, :] = jnp.broadcast_to(bias_v[...], (16, cols))
 
 
 def mix_kernel(width, count_ref, send_v, hub_v, pos_v, live_v, tile_v, dest_v, gw_v, hw_v, mix_ref, turned_ref, mark_ref):
@@ -389,11 +398,12 @@
             *(shape(a.shape, a.dtype) for a in moved),
         ),
         in_specs=[HBM] * (len(first) + len(edges)),
-        out_specs=(VMEM,) * (2 + len(moved)),
+        out_specs=(HBM,) + (VMEM,) * (1 + len(moved)),
         scratch_shapes=[
             pltpu.VMEM((1, cols), BF),
             pltpu.VMEM((slots, lanes), BF),
-            pltpu.SemaphoreType.DMA((11 + 2 * blocks,)),
+            pltpu.VMEM((peers, sent, cols), BF),
+            pltpu.SemaphoreType.DMA((13 + 2 * blocks,)),
         ],
         compiler_params=PARAMS,
     )(*first, *edges)

time: 45.8 us -> 45.8 us (level)
  no operation moved by 1% of the time
where the time goes in v20:
time: 45.8 us; the launch traced here: 45.5 us
  starting transfers between devices  21.7 us (47%)
  waiting for transfers between devices  15.4 us (34%)
  Pallas kernels  6.99 us (15%)
  between operations  1.39 us (3%)
    ppermute x17, starting transfers between devices, partner(): lax.ppermute(block, axis, [(i, i ^ k) for i in range(lax.axis_size(axis))])  15.8 us
    ppermute x17, waiting for transfers between devices, partner(): lax.ppermute(block, axis, [(i, i ^ k) for i in range(lax.axis_size(axis))])  9.22 us
    all_to_all x1, waiting for transfers between devices, exchange(): lax.all_to_all(blocks, 'dom', split_axis=0, concat_axis=0, axis_index_gro...  6.16 us
    all_to_all x1, starting transfers between devices, exchange(): lax.all_to_all(blocks, 'dom', split_axis=0, concat_axis=0, axis_index_gro...  5.83 us
    pallas_call x1, Pallas kernels, on_device(): pl.pallas_call(functools.partial(send_kernel, width), out_shape=(shape((p...  1.96 us
    pallas_call x1, Pallas kernels, on_device(): pl.pallas_call(functools.partial(dense_kernel, slots, hub_here, feats, wi...  1.07 us
  transfers between devices with their start and end apart: 18, of which 9 were waited for; matrix products, arithmetic and copies ran while one was open for 0% of the time, Pallas kernels for 7%

profile of v20, /device:TPU:0, one launch (start us, length us, event | category | flops | bytes accessed | tf_op | source)
XLA Modules:
  0.0 45.5 jit_solution(12497999125454739192)
XLA Ops:
  0.6 2.0 %shard_map.173 = (bf16[8,56,128]{2,1,0:T(8,128)(2,1)}, bf16[1552,128]{1,0:T(8,128)(2,1)S(1)}, s32[1,8,48]{2,1,0:T(8,128)S(1)}, s32[1,2]{1,0:T(1,128)S(1)}, s32[1...) custom-call(bf16[256,128]{1,0:T(8,128)(2,1)} %x_ref.5, ...), custom_call_target="tpu_custom_call" | custom-call | tf_op jit(solution)/shard_map/pallas_call | solution.py:393
  2.6 3.0 %collective-permute-start.1 = (bf16[1552,128]{1,0:T(8,128)(2,1)S(1)}, bf16[1552,128]{1,0:T(8,128)(2,1)S(1)}, u32[]{:S(2)}, u32[]{:S(2)}) collective-permute-start(bf16[1552,128]{1,0:T(8,128)(2,1)S(1)} %get-tuple-element.51.refs_0_), channel_id=1, source_target_pairs={{0,2},{1,3},{2,0},{3,1},{4,6},{5,7},{6,4},{7,5},{8,10},{9,11},{10,... | collective-permute-start | bytes 1191944 | tf_op jit(solution)/shard_map/ppermute | solution.py:340
  5.6 5.8 %all-to-all-start = ((bf16[8,56,128]{2,1,0:T(8,128)(2,1)}), bf16[8,56,128]{2,1,0:T(8,128)(2,1)S(1)}, u32[]{:S(2)}, u32[]{:S(2)}) async-start(bf16[8,56,128]{2,1,0:T(8,128)(2,1)} %get-tuple-element.53), calls=%async_computation | async-start | bytes 229376 | tf_op jit(solution)/shard_map/all_to_all | solution.py:344
  12.1 0.4 shard_map.174
  12.5 6.2 %all-to-all-done.got_ref = bf16[8,56,128]{2,1,0:T(8,128)(2,1)S(1)} async-done(((bf16[8,56,128]{2,1,0:T(8,128)(2,1)}), bf16[8,56,128]{2,1,0:T(8,128)(2,1)S(1)}, u32[]{:S(2)}, u32[]{:S(2)}) %all-to-all-start) | async-done | bytes 114720 | tf_op jit(solution)/shard_map/all_to_all | solution.py:344
  18.7 0.3 shard_map.175
  19.1 0.6 %collective-permute-start.4 = (bf16[256,128]{1,0:T(8,128)(2,1)S(1)}, bf16[256,128]{1,0:T(8,128)(2,1)S(1)}, u32[]{:S(2)}, u32[]{:S(2)}) collective-permute-start(bf16[256,128]{1,0:T(8,128)(2,1)S(1)} %get-tuple-element.55.refs_4_), channel_id=1, source_target_pairs={{0,2},{1,3},{2,0},{3,1},{4,6},{5,7},{6,4},{7,5},{8,10},{9,11},{10,... | collective-permute-start | bytes 196616 | tf_op jit(solution)/shard_map/ppermute | solution.py:340
  19.7 0.2 collective-permute-start.3
  19.8 3.7 %collective-permute-done.4.refs_6_ = bf16[256,128]{1,0:T(8,128)(2,1)S(1)} collective-permute-done((bf16[256,128]{1,0:T(8,128)(2,1)S(1)}, bf16[256,128]{1,0:T(8,128)(2,1)S(1)}, u32[]{:S(2)}, u32[]{:S(2)}) %collective-permute-start.4) | collective-permute-done | bytes 65568 | tf_op jit(solution)/shard_map/ppermute | solution.py:340
  23.6 1.2 %collective-permute-done.5.refs_7_ = bf16[256,128]{1,0:T(8,128)(2,1)S(1)} collective-permute-done((bf16[256,128]{1,0:T(8,128)(2,1)S(1)}, bf16[256,128]{1,0:T(8,128)(2,1)S(1)}, u32[]{:S(2)}, u32[]{:S(2)}) %collective-permute-start.5) | collective-permute-done | bytes 65568 | tf_op jit(solution)/shard_map/ppermute | solution.py:340
  24.8 1.1 %shard_map.176 = (f32[256,128]{1,0:T(8,128)S(1)}, bf16[256,512]{1,0:T(8,128)(2,1)S(1)}, bf16[256,128]{1,0:T(8,128)(2,1)S(1)}, f32[1,128]{1,0:T(1,128)S(1)}, bf16...) custom-call(s32[1]{0:T(128)} %bitcast.2.me_ref, ...), custom_call_target="tpu_custom_call" | custom-call | tf_op jit(solution)/shard_map/pallas_call | solution.py:439
  25.9 0.8 %collective-permute-start.10 = (bf16[256,128]{1,0:T(8,128)(2,1)S(1)}, bf16[256,128]{1,0:T(8,128)(2,1)S(1)}, u32[]{:S(2)}, u32[]{:S(2)}) collective-permute-start(bf16[256,128]{1,0:T(8,128)(2,1)S(1)} %get-tuple-element.70), channel_id=1, source_target_pairs={{0,12},{4,8},{8,4},{12,0},{16,28},{20,24},{24,20},{28,16},{1,13},{... | collective-permute-start | bytes 196616 | tf_op jit(solution)/shard_map/ppermute | solution.py:340
  26.7 1.0 %collective-permute-start.11 = (bf16[256,128]{1,0:T(8,128)(2,1)S(1)}, bf16[256,128]{1,0:T(8,128)(2,1)S(1)}, u32[]{:S(2)}, u32[]{:S(2)}) collective-permute-start(bf16[256,128]{1,0:T(8,128)(2,1)S(1)} %get-tuple-element.71), channel_id=1, source_target_pairs={{0,8},{4,12},{8,0},{12,4},{16,24},{20,28},{24,16},{28,20},{1,9},{5... | collective-permute-start | bytes 196616 | tf_op jit(solution)/shard_map/ppermute | solution.py:340
  27.7 1.8 %collective-permute-start.12 = (bf16[256,128]{1,0:T(8,128)(2,1)S(1)}, bf16[256,128]{1,0:T(8,128)(2,1)S(1)}, u32[]{:S(2)}, u32[]{:S(2)}) collective-permute-start(bf16[256,128]{1,0:T(8,128)(2,1)S(1)} %get-tuple-element.72), channel_id=1, source_target_pairs={{0,4},{4,0},{8,12},{12,8},{16,20},{20,16},{24,28},{28,24},{1,5},{5... | collective-permute-start | bytes 196616 | tf_op jit(solution)/shard_map/ppermute | solution.py:340
  29.5 0.4 collective-permute-start.6
  29.9 0.9 %shard_map.177 = (bf16[256,128]{1,0:T(8,128)(2,1)}, f32[256,128]{1,0:T(8,128)S(1)}, bf16[4,64,128]{2,1,0:T(8,128)(2,1)S(1)}) custom-call(s32[1]{0:T(128)} %bitcast.side_ref, s32[1]{0:T(128)} %bitcast.1.seat_ref, f32[256,128]{1,0:T(8,128)S(1)} %get-tuple-element.56.own_ref, bf16[256,512]{1,0:T(8,128)(2,1)S(1)} %get-tuple-element.57.grad_ref, ...), custom_call_target="tpu_custom_call" | custom-call | flops 100000000 | bytes 1000000 | tf_op jit(solution)/shard_map/pallas_call | solution.py:460
  30.7 1.0 %collective-permute-done.10.refs_0_ = bf16[256,128]{1,0:T(8,128)(2,1)S(1)} collective-permute-done((bf16[256,128]{1,0:T(8,128)(2,1)S(1)}, bf16[256,128]{1,0:T(8,128)(2,1)S(1)}, u32[]{:S(2)}, u32[]{:S(2)}) %collective-permute-start.10) | collective-permute-done | bytes 65568 | tf_op jit(solution)/shard_map/ppermute | solution.py:340
  31.7 0.7 %collective-permute-done.12.refs_2_ = bf16[256,128]{1,0:T(8,128)(2,1)S(1)} collective-permute-done((bf16[256,128]{1,0:T(8,128)(2,1)S(1)}, bf16[256,128]{1,0:T(8,128)(2,1)S(1)}, u32[]{:S(2)}, u32[]{:S(2)}) %collective-permute-start.12) | collective-permute-done | bytes 65568 | tf_op jit(solution)/shard_map/ppermute | solution.py:340
  32.5 0.9 %collective-permute-start.13 = (bf16[256,128]{1,0:T(8,128)(2,1)S(1)}, bf16[256,128]{1,0:T(8,128)(2,1)S(1)}, u32[]{:S(2)}, u32[]{:S(2)}) collective-permute-start(bf16[256,128]{1,0:T(8,128)(2,1)S(1)} %shard_map.180.own_ref), channel_id=1, source_target_pairs={{0,16},{4,20},{8,24},{12,28},{16,0},{20,4},{24,8},{28,12},{1,17},{... | collective-permute-start | bytes 196616 | tf_op jit(solution)/shard_map/ppermute | solution.py:340
  33.4 1.2 %collective-permute-done.6.mirror_ref = bf16[4,56,128]{2,1,0:T(8,128)(2,1)S(1)} collective-permute-done((bf16[4,56,128]{2,1,0:T(8,128)(2,1)S(1)}, bf16[4,56,128]{2,1,0:T(8,128)(2,1)S(1)}, u32[]{:S(2)}, u32[]{:S(2)}) %collective-permute-start.6) | collective-permute-done | bytes 57376 | tf_op jit(solution)/shard_map/ppermute | solution.py:340
  34.6 0.9 %collective-permute-start.7 = (bf16[128,128]{1,0:T(8,128)(2,1)S(1)}, bf16[128,128]{1,0:T(8,128)(2,1)S(1)}, u32[]{:S(2)}, u32[]{:S(2)}) collective-permute-start(bf16[128,128]{1,0:T(8,128)(2,1)S(1)} %get-tuple-element.66), channel_id=1, source_target_pairs={{0,4},{4,0},{8,12},{12,8},{16,20},{20,16},{24,28},{28,24},{1,5},{5... | collective-permute-start | bytes 98312 | tf_op jit(solution)/shard_map/ppermute | solution.py:340
  35.5 0.5 %collective-permute-start.8 = (bf16[128,128]{1,0:T(8,128)(2,1)S(1)}, bf16[128,128]{1,0:T(8,128)(2,1)S(1)}, u32[]{:S(2)}, u32[]{:S(2)}) collective-permute-start(bf16[128,128]{1,0:T(8,128)(2,1)S(1)} %get-tuple-element.67), channel_id=1, source_target_pairs={{0,8},{4,12},{8,0},{12,4},{16,24},{20,28},{24,16},{28,20},{1,9},{5... | collective-permute-start | bytes 98312 | tf_op jit(solution)/shard_map/ppermute | solution.py:340
  36.0 2.1 %collective-permute-start.9 = (bf16[128,128]{1,0:T(8,128)(2,1)S(1)}, bf16[128,128]{1,0:T(8,128)(2,1)S(1)}, u32[]{:S(2)}, u32[]{:S(2)}) collective-permute-start(bf16[128,128]{1,0:T(8,128)(2,1)S(1)} %get-tuple-element.68), channel_id=1, source_target_pairs={{0,12},{4,8},{8,4},{12,0},{16,28},{20,24},{24,20},{28,16},{1,13},{... | collective-permute-start | bytes 98312 | tf_op jit(solution)/shard_map/ppermute | solution.py:340
  38.2 0.2 collective-permute-done.13.other_ref
  38.4 0.3 collective-permute-start.16
  38.7 0.9 %collective-permute-start.15 = (bf16[256,128]{1,0:T(8,128)(2,1)S(1)}, bf16[256,128]{1,0:T(8,128)(2,1)S(1)}, u32[]{:S(2)}, u32[]{:S(2)}) collective-permute-start(bf16[256,128]{1,0:T(8,128)(2,1)S(1)} %shard_map.181.refs_0_), channel_id=1, source_target_pairs={{0,4},{4,0},{8,12},{12,8},{16,20},{20,16},{24,28},{28,24},{1,5},{5... | collective-permute-start | bytes 196616 | tf_op jit(solution)/shard_map/ppermute | solution.py:340
  39.6 2.4 %collective-permute-start.14 = (bf16[256,128]{1,0:T(8,128)(2,1)S(1)}, bf16[256,128]{1,0:T(8,128)(2,1)S(1)}, u32[]{:S(2)}, u32[]{:S(2)}) collective-permute-start(bf16[256,128]{1,0:T(8,128)(2,1)S(1)} %shard_map.181.refs_0_), channel_id=1, source_target_pairs={{0,12},{4,8},{8,4},{12,0},{16,28},{20,24},{24,20},{28,16},{1,13},{... | collective-permute-start | bytes 196616 | tf_op jit(solution)/shard_map/ppermute | solution.py:340
  42.0 0.9 %shard_map.179 = (bf16[256,128]{1,0:T(8,128)(2,1)}, f32[1,128]{1,0:T(1,128)}) custom-call(s32[1]{0:T(128)} %bitcast.side_ref, s32[1]{0:T(128)} %bitcast.1.seat_ref, f32[256,128]{1,0:T(8,128)S(1)} %get-tuple-element.61.back_ref, bf16[256,512]{1,0:T(8,128)(2,1)S(1)} %get-tuple-element.62.mark_ref, bf16[128,128]{1,0:T(8,128)(2,1)S(1)} %get-tuple-element.65.refs_0_, ...), custom_call_target="tpu_custom_call" | custom-call | flops 2000000000 | bytes 1000000 | tf_op jit(solution)/shard_map/pallas_call | solution.py:492
  42.8 0.1 collective-permute-done.15.refs_1_
  43.0 0.8 %shard_map.182 = (f32[128,512]{1,0:T(8,128)}, f32[128,512]{1,0:T(8,128)}) custom-call(s32[1]{0:T(128)} %bitcast.1.seat_ref, bf16[256,128]{1,0:T(8,128)(2,1)S(1)} %shard_map.181.refs_0_, bf16[256,128]{1,0:T(8,128)(2,1)S(1)} %collective-permute-done.15.refs_1_, bf16[256,128]{1,0:T(8,128)(2,1)S(1)} %collective-permute-done.16.refs_2_), custom_call_target="tpu_custom_call" | custom-call | tf_op jit(solution)/shard_map/pallas_call | solution.py:502
  43.8 1.0 %collective-permute-done.14.got_ref = bf16[256,128]{1,0:T(8,128)(2,1)S(1)} collective-permute-done((bf16[256,128]{1,0:T(8,128)(2,1)S(1)}, bf16[256,128]{1,0:T(8,128)(2,1)S(1)}, u32[]{:S(2)}, u32[]{:S(2)}) %collective-permute-start.14) | collective-permute-done | bytes 65568 | tf_op jit(solution)/shard_map/ppermute | solution.py:340
  44.8 0.7 %shard_map.183 = (f32[128,512]{1,0:T(8,128)}, f32[128,512]{1,0:T(8,128)}) custom-call(s32[1]{0:T(128)} %bitcast.1.seat_ref, bf16[256,128]{1,0:T(8,128)(2,1)S(1)} %collective-permute-done.14.got_ref, f32[128,512]{1,0:T(8,128)} %get-tuple-element.74.begun_self_ref, ...), custom_call_target="tpu_custom_call", output_to_operand_aliasing={{0}: (2, {}), {1}: (3, {})} | custom-call | tf_op jit(solution)/shard_map/pallas_call | solution.py:511
  (21 shorter events, 0.2 us)
Async XLA Ops:
  2.6 16.1 %collective-permute-start.1 = (bf16[1552,128]{1,0:T(8,128)(2,1)S(1)}, bf16[1552,128]{1,0:T(8,128)(2,1)S(1)}, u32[]{:S(2)}, u32[]{:S(2)}) collective-permute-start(bf16[1552,128]{1,0:T(8,128)(2,1)S(1)} %get-tuple-element.51.refs_0_), channel_id=1, source_target_pairs={{0,2},{1,3},{2,0},{3,1},{4,6},{5,7},{6,4},{7,5},{8,10},{9,11},{10,... | collective-permute-start | bytes 1191944 | tf_op jit(solution)/shard_map/ppermute | solution.py:340
  5.6 13.1 %all-to-all-start = ((bf16[8,56,128]{2,1,0:T(8,128)(2,1)}), bf16[8,56,128]{2,1,0:T(8,128)(2,1)S(1)}, u32[]{:S(2)}, u32[]{:S(2)}) async-start(bf16[8,56,128]{2,1,0:T(8,128)(2,1)} %get-tuple-element.53), calls=%async_computation | async-start | bytes 229376 | tf_op jit(solution)/shard_map/all_to_all | solution.py:344
  11.4 12.1 %collective-permute-start = (bf16[1552,128]{1,0:T(8,128)(2,1)S(1)}, bf16[1552,128]{1,0:T(8,128)(2,1)S(1)}, u32[]{:S(2)}, u32[]{:S(2)}) collective-permute-start(bf16[1552,128]{1,0:T(8,128)(2,1)S(1)} %get-tuple-element.51.refs_0_), channel_id=1, source_target_pairs={{0,1},{1,0},{2,3},{3,2},{4,5},{5,4},{6,7},{7,6},{8,9},{9,8},{10,11... | collective-permute-start | bytes 1191944 | tf_op jit(solution)/shard_map/ppermute | solution.py:340
  12.1 6.6 %copy-start.1 = (bf16[256,128]{1,0:T(8,128)(2,1)S(1)}, bf16[256,128]{1,0:T(8,128)(2,1)}, u32[]{:S(2)}) copy-start(bf16[256,128]{1,0:T(8,128)(2,1)} %x_ref.5) | copy-start | bytes 196612
  18.7 6.1 %copy-start = (bf16[128,512]{1,0:T(8,128)(2,1)S(1)}, bf16[128,512]{1,0:T(8,128)(2,1)}, u32[]{:S(2)}) copy-start(bf16[128,512]{1,0:T(8,128)(2,1)} %ws_ref.5) | copy-start | bytes 393220
  18.7 6.1 %copy-start.2 = (bf16[128,512]{1,0:T(8,128)(2,1)S(1)}, bf16[128,512]{1,0:T(8,128)(2,1)}, u32[]{:S(2)}) copy-start(bf16[128,512]{1,0:T(8,128)(2,1)} %wn_ref.3) | copy-start | bytes 393220
  19.0 5.8 %collective-permute-start.2 = (bf16[1552,128]{1,0:T(8,128)(2,1)S(1)}, bf16[1552,128]{1,0:T(8,128)(2,1)S(1)}, u32[]{:S(2)}, u32[]{:S(2)}) collective-permute-start(bf16[1552,128]{1,0:T(8,128)(2,1)S(1)} %get-tuple-element.54.refs_2_), channel_id=1, source_target_pairs={{0,1},{1,0},{2,3},{3,2},{4,5},{5,4},{6,7},{7,6},{8,9},{9,8},{10,11... | collective-permute-start | bytes 1191944 | tf_op jit(solution)/shard_map/ppermute | solution.py:340
  19.1 4.5 %collective-permute-start.4 = (bf16[256,128]{1,0:T(8,128)(2,1)S(1)}, bf16[256,128]{1,0:T(8,128)(2,1)S(1)}, u32[]{:S(2)}, u32[]{:S(2)}) collective-permute-start(bf16[256,128]{1,0:T(8,128)(2,1)S(1)} %get-tuple-element.55.refs_4_), channel_id=1, source_target_pairs={{0,2},{1,3},{2,0},{3,1},{4,6},{5,7},{6,4},{7,5},{8,10},{9,11},{10,... | collective-permute-start | bytes 196616 | tf_op jit(solution)/shard_map/ppermute | solution.py:340
  19.7 3.9 %collective-permute-start.3 = (bf16[256,128]{1,0:T(8,128)(2,1)S(1)}, bf16[256,128]{1,0:T(8,128)(2,1)S(1)}, u32[]{:S(2)}, u32[]{:S(2)}) collective-permute-start(bf16[256,128]{1,0:T(8,128)(2,1)S(1)} %get-tuple-element.55.refs_4_), channel_id=1, source_target_pairs={{0,1},{1,0},{2,3},{3,2},{4,5},{5,4},{6,7},{7,6},{8,9},{9,8},{10,11... | collective-permute-start | bytes 196616 | tf_op jit(solution)/shard_map/ppermute | solution.py:340
  23.6 1.3 %collective-permute-start.5 = (bf16[256,128]{1,0:T(8,128)(2,1)S(1)}, bf16[256,128]{1,0:T(8,128)(2,1)S(1)}, u32[]{:S(2)}, u32[]{:S(2)}) collective-permute-start(bf16[256,128]{1,0:T(8,128)(2,1)S(1)} %collective-permute-done.4.refs_6_), channel_id=1, source_target_pairs={{0,1},{1,0},{2,3},{3,2},{4,5},{5,4},{6,7},{7,6},{8,9},{9,8},{10,11... | collective-permute-start | bytes 196616 | tf_op jit(solution)/shard_map/ppermute | solution.py:340
  25.9 5.8 %collective-permute-start.10 = (bf16[256,128]{1,0:T(8,128)(2,1)S(1)}, bf16[256,128]{1,0:T(8,128)(2,1)S(1)}, u32[]{:S(2)}, u32[]{:S(2)}) collective-permute-start(bf16[256,128]{1,0:T(8,128)(2,1)S(1)} %get-tuple-element.70), channel_id=1, source_target_pairs={{0,12},{4,8},{8,4},{12,0},{16,28},{20,24},{24,20},{28,16},{1,13},{... | collective-permute-start | bytes 196616 | tf_op jit(solution)/shard_map/ppermute | solution.py:340
  26.7 5.0 %collective-permute-start.11 = (bf16[256,128]{1,0:T(8,128)(2,1)S(1)}, bf16[256,128]{1,0:T(8,128)(2,1)S(1)}, u32[]{:S(2)}, u32[]{:S(2)}) collective-permute-start(bf16[256,128]{1,0:T(8,128)(2,1)S(1)} %get-tuple-element.71), channel_id=1, source_target_pairs={{0,8},{4,12},{8,0},{12,4},{16,24},{20,28},{24,16},{28,20},{1,9},{5... | collective-permute-start | bytes 196616 | tf_op jit(solution)/shard_map/ppermute | solution.py:340
  27.7 4.7 %collective-permute-start.12 = (bf16[256,128]{1,0:T(8,128)(2,1)S(1)}, bf16[256,128]{1,0:T(8,128)(2,1)S(1)}, u32[]{:S(2)}, u32[]{:S(2)}) collective-permute-start(bf16[256,128]{1,0:T(8,128)(2,1)S(1)} %get-tuple-element.72), channel_id=1, source_target_pairs={{0,4},{4,0},{8,12},{12,8},{16,20},{20,16},{24,28},{28,24},{1,5},{5... | collective-permute-start | bytes 196616 | tf_op jit(solution)/shard_map/ppermute | solution.py:340
  29.5 5.1 %collective-permute-start.6 = (bf16[4,56,128]{2,1,0:T(8,128)(2,1)S(1)}, bf16[4,56,128]{2,1,0:T(8,128)(2,1)S(1)}, u32[]{:S(2)}, u32[]{:S(2)}) collective-permute-start(bf16[4,56,128]{2,1,0:T(8,128)(2,1)S(1)} %get-tuple-element.64), channel_id=1, source_target_pairs={{0,16},{4,20},{8,24},{12,28},{16,0},{20,4},{24,8},{28,12},{1,17},{... | collective-permute-start | bytes 172040 | tf_op jit(solution)/shard_map/ppermute | solution.py:340
  32.5 5.9 %collective-permute-start.13 = (bf16[256,128]{1,0:T(8,128)(2,1)S(1)}, bf16[256,128]{1,0:T(8,128)(2,1)S(1)}, u32[]{:S(2)}, u32[]{:S(2)}) collective-permute-start(bf16[256,128]{1,0:T(8,128)(2,1)S(1)} %shard_map.180.own_ref), channel_id=1, source_target_pairs={{0,16},{4,20},{8,24},{12,28},{16,0},{20,4},{24,8},{28,12},{1,17},{... | collective-permute-start | bytes 196616 | tf_op jit(solution)/shard_map/ppermute | solution.py:340
  34.6 5.0 %collective-permute-start.7 = (bf16[128,128]{1,0:T(8,128)(2,1)S(1)}, bf16[128,128]{1,0:T(8,128)(2,1)S(1)}, u32[]{:S(2)}, u32[]{:S(2)}) collective-permute-start(bf16[128,128]{1,0:T(8,128)(2,1)S(1)} %get-tuple-element.66), channel_id=1, source_target_pairs={{0,4},{4,0},{8,12},{12,8},{16,20},{20,16},{24,28},{28,24},{1,5},{5... | collective-permute-start | bytes 98312 | tf_op jit(solution)/shard_map/ppermute | solution.py:340
  35.5 6.5 %collective-permute-start.8 = (bf16[128,128]{1,0:T(8,128)(2,1)S(1)}, bf16[128,128]{1,0:T(8,128)(2,1)S(1)}, u32[]{:S(2)}, u32[]{:S(2)}) collective-permute-start(bf16[128,128]{1,0:T(8,128)(2,1)S(1)} %get-tuple-element.67), channel_id=1, source_target_pairs={{0,8},{4,12},{8,0},{12,4},{16,24},{20,28},{24,16},{28,20},{1,9},{5... | collective-permute-start | bytes 98312 | tf_op jit(solution)/shard_map/ppermute | solution.py:340
  36.0 6.0 %collective-permute-start.9 = (bf16[128,128]{1,0:T(8,128)(2,1)S(1)}, bf16[128,128]{1,0:T(8,128)(2,1)S(1)}, u32[]{:S(2)}, u32[]{:S(2)}) collective-permute-start(bf16[128,128]{1,0:T(8,128)(2,1)S(1)} %get-tuple-element.68), channel_id=1, source_target_pairs={{0,12},{4,8},{8,4},{12,0},{16,28},{20,24},{24,20},{28,16},{1,13},{... | collective-permute-start | bytes 98312 | tf_op jit(solution)/shard_map/ppermute | solution.py:340
  38.4 4.4 %collective-permute-start.16 = (bf16[256,128]{1,0:T(8,128)(2,1)S(1)}, bf16[256,128]{1,0:T(8,128)(2,1)S(1)}, u32[]{:S(2)}, u32[]{:S(2)}) collective-permute-start(bf16[256,128]{1,0:T(8,128)(2,1)S(1)} %shard_map.181.refs_0_), channel_id=1, source_target_pairs={{0,8},{4,12},{8,0},{12,4},{16,24},{20,28},{24,16},{28,20},{1,9},{5... | collective-permute-start | bytes 196616 | tf_op jit(solution)/shard_map/ppermute | solution.py:340
  38.7 4.3 %collective-permute-start.15 = (bf16[256,128]{1,0:T(8,128)(2,1)S(1)}, bf16[256,128]{1,0:T(8,128)(2,1)S(1)}, u32[]{:S(2)}, u32[]{:S(2)}) collective-permute-start(bf16[256,128]{1,0:T(8,128)(2,1)S(1)} %shard_map.181.refs_0_), channel_id=1, source_target_pairs={{0,4},{4,0},{8,12},{12,8},{16,20},{20,16},{24,28},{28,24},{1,5},{5... | collective-permute-start | bytes 196616 | tf_op jit(solution)/shard_map/ppermute | solution.py:340
  39.6 5.2 %collective-permute-start.14 = (bf16[256,128]{1,0:T(8,128)(2,1)S(1)}, bf16[256,128]{1,0:T(8,128)(2,1)S(1)}, u32[]{:S(2)}, u32[]{:S(2)}) collective-permute-start(bf16[256,128]{1,0:T(8,128)(2,1)S(1)} %shard_map.181.refs_0_), channel_id=1, source_target_pairs={{0,12},{4,8},{8,4},{12,0},{16,28},{20,24},{24,20},{28,16},{1,13},{... | collective-permute-start | bytes 196616 | tf_op jit(solution)/shard_map/ppermute | solution.py:340

commit v21 on v20

--- a/solution.py
+++ b/solution.py
@@ -152,15 +152,14 @@
     return away.astype(BF)
 
 
-def dense_kernel(slots, hub_here, feats, width, count, me_ref, side_ref, seat_ref, x_ref, ws_ref, wn_ref, turned_ref, *refs):
+def dense_kernel(feats, count, me_ref, seat_ref, x_ref, ws_ref, wn_ref, *refs):
     pack_refs, n_refs = refs[:feats], refs[feats : 2 * feats]
-    own_ref, cot_ref, slope_ref, sums_ref, mirror_ref = refs[2 * feats : 2 * feats + 5]
-    send_refs = refs[2 * feats + 5 : 2 * feats + 5 + count]
-    pre_ref, bias_ref = refs[2 * feats + 5 + count :]
+    own_ref, cot_ref, slope_ref, sums_ref = refs[2 * feats : 2 * feats + 4]
+    send_refs = refs[2 * feats + 4 : 2 * feats + 4 + count]
+    pre_ref, bias_ref = refs[2 * feats + 4 + count :]
     rows, cols = x_ref.shape
     depth, full = ws_ref.shape
     blocks = full // cols
-    half = mirror_ref.shape[0]
     share = send_refs[0].shape[-2]
     me = me_ref[0]
     base = 2 * blocks * depth
@@ -192,23 +191,16 @@
         )
     mine = pl.ds(pl.multiple_of(me * cols, cols), cols)
     own_ref[...] = pre_ref[:, mine]
-    neigh_grad = into.astype(BF)
-    slope_ref[...] = neigh_grad
-    sums = jnp.sum(cot_ref[:, mine].astype(F32), axis=0, keepdims=True)
-    sums_ref[...] = sums
-    there = half - side_ref[0] * half
+    slope_ref[...] = into.astype(BF)
+    sums_ref[...] = jnp.sum(cot_ref[:, mine].astype(F32), axis=0, keepdims=True)
     pair = jnp.concatenate([x_ref[...], n_refs[0][...]], axis=1).T
     if count > 1:
         for k, ref in enumerate(send_refs):
             peer = seat_ref[0] ^ k
-            away = ghost_rows(slots, hub_here, width, there + peer, 1, turned_ref, neigh_grad, sums)
-            mirror_ref[k] = away[: mirror_ref.shape[1]]
             block = cot_ref[:, pl.ds(pl.multiple_of(peer * cols, cols), cols)]
             ref[...] = jnp.dot(pair, block, preferred_element_type=F32).astype(BF)
         return
     send_ref = send_refs[0]
-    away = ghost_rows(slots, hub_here, width, there, half, turned_ref, neigh_grad, sums).reshape(half, width, cols)
-    mirror_ref[...] = away[:, : mirror_ref.shape[1]]
     weights = jnp.dot(pair, cot_ref[...], preferred_element_type=F32).astype(BF)
     step = min(share, depth)
     for j in range(blocks):
@@ -224,6 +216,19 @@
     if len(refs) == 1:
         return [(j, refs[0].at[j]) for j in range(refs[0].shape[0])]
     return [(seat ^ k, ref) for k, ref in enumerate(refs)]
+
+
+def mirror_kernel(slots, hub_here, width, count, side_ref, seat_ref, slope_ref, sums_ref, turned_ref, mirror_ref):
+    half, sent, cols = mirror_ref.shape
+    slope, sums = slope_ref[...], sums_ref[...]
+    there = half - side_ref[0] * half
+    if count > 1:
+        for k in range(half):
+            peer = there + (seat_ref[0] ^ k)
+            mirror_ref[k] = ghost_rows(slots, hub_here, width, peer, 1, turned_ref, slope, sums)[:sent]
+        return
+    away = ghost_rows(slots, hub_here, width, there, half, turned_ref, slope, sums).reshape(half, width, cols)
+    mirror_ref[...] = away[:, :sent]
 
 
 def side_kernel(
@@ -436,26 +441,32 @@
     far_neigh = partner(neigh, "feat", 2)
     every = [neigh, partner(neigh, "feat", 1), far_neigh, partner(far_neigh, "feat", 1)]
 
-    own, grad, slope, sums, mirror, *returned = pl.pallas_call(
-        functools.partial(dense_kernel, slots, hub_here, feats, width, count),
+    own, grad, slope, sums, *returned = pl.pallas_call(
+        functools.partial(dense_kernel, feats, count),
         out_shape=(
             shape((rows, cols), F32),
             shape((rows, full), BF),
             shape((rows, cols), BF),
             shape((1, cols), F32),
-            shape((half, sent, cols), BF),
             *([shape((share, cols), BF)] * half if direct else [shape((half, share, cols), BF)]),
         ),
-        in_specs=[SMEM] * 3 + [VMEM] * (4 + 2 * feats),
-        out_specs=(VMEM,) * (5 + count),
+        in_specs=[SMEM] * 2 + [VMEM] * (3 + 2 * feats),
+        out_specs=(VMEM,) * (4 + count),
         scratch_shapes=[
             pltpu.VMEM((rows, full), F32),
             pltpu.VMEM((16, full), BF),
         ],
         compiler_params=PARAMS,
-    )(me, side, seat, features, w_self, w_neigh, turned, pack, near, far, last, *every)
+    )(me, seat, features, w_self, w_neigh, pack, near, far, last, *every)
 
     arrived = swap(returned)[::-1] if direct else [exchange(returned[0], halves)]
+    mirror = pl.pallas_call(
+        functools.partial(mirror_kernel, slots, hub_here, width, count),
+        out_shape=shape((half, sent, cols), BF),
+        in_specs=[SMEM] * 2 + [VMEM] * 3,
+        out_specs=VMEM,
+        compiler_params=PARAMS,
+    )(side, seat, slope, sums, turned)
     mirror = partner(mirror, "dom", half)
     output, back, ghosts = pl.pallas_call(
         functools.partial(side_kernel, slots, hub_here, count),

time: 45.8 us -> 45.9 us (level)
  waiting for transfers between devices: 15.4 us -> 14.4 us
  local copies, waits for them, and re-layouts: 0.02 us -> 0.72 us
    all_to_all x1, waiting for transfers between devices: 6.16 us -> 5.46 us  [exchange(): lax.all_to_all(blocks, 'dom', split_axis=0, concat_axis=0, axis_index_gro...]
    unnamed x6 -> x10, local copies, waits for them, and re-layouts: 0.02 us -> 0.72 us
    pallas_call x1 -> x2, Pallas kernels: 1.07 us -> 1.1 us  [the longest x1 0.93 us: on_device(): pl.pallas_call(functools.partial(dense_kernel, feats, count), out_shape=(...]
  transfers between devices with their start and end apart: 18 -> 18, of which waited for: 9 -> 8; matrix products, arithmetic and copies ran while one was open for 0% -> 0% of each run, Pallas kernels for 7% -> 8%
where the time goes in v21:
time: 45.9 us; the launch traced here: 45.5 us
  starting transfers between devices  22 us (48%)
  waiting for transfers between devices  14.4 us (31%)
  Pallas kernels  7.03 us (15%)
  between operations  1.42 us (3%)
  local copies, waits for them, and re-layouts  0.72 us (2%)
    ppermute x17, starting transfers between devices, partner(): lax.ppermute(block, axis, [(i, i ^ k) for i in range(lax.axis_size(axis))])  16.1 us
    ppermute x17, waiting for transfers between devices, partner(): lax.ppermute(block, axis, [(i, i ^ k) for i in range(lax.axis_size(axis))])  8.95 us
    all_to_all x1, starting transfers between devices, exchange(): lax.all_to_all(blocks, 'dom', split_axis=0, concat_axis=0, axis_index_gro...  5.83 us
    all_to_all x1, waiting for transfers between devices, exchange(): lax.all_to_all(blocks, 'dom', split_axis=0, concat_axis=0, axis_index_gro...  5.46 us
    pallas_call x1, Pallas kernels, on_device(): pl.pallas_call(functools.partial(send_kernel, width), out_shape=(shape((p...  1.96 us
    pallas_call x1, Pallas kernels, on_device(): pl.pallas_call(functools.partial(dense_kernel, feats, count), out_shape=(...  0.93 us
  transfers between devices with their start and end apart: 18, of which 8 were waited for; matrix products, arithmetic and copies ran while one was open for 0% of the time, Pallas kernels for 8%

profile of v21, /device:TPU:0, one launch (start us, length us, event | category | flops | bytes accessed | tf_op | source)
XLA Modules:
  0.0 45.5 jit_solution(8614508304348610256)
XLA Ops:
  0.6 2.0 %shard_map.173 = (bf16[8,56,128]{2,1,0:T(8,128)(2,1)}, bf16[1552,128]{1,0:T(8,128)(2,1)S(1)}, s32[1,8,48]{2,1,0:T(8,128)S(1)}, s32[1,2]{1,0:T(1,128)S(1)}, s32[1...) custom-call(bf16[256,128]{1,0:T(8,128)(2,1)} %x_ref.5, ...), custom_call_target="tpu_custom_call" | custom-call | tf_op jit(solution)/shard_map/pallas_call | solution.py:398
  2.6 3.0 %collective-permute-start.1 = (bf16[1552,128]{1,0:T(8,128)(2,1)S(1)}, bf16[1552,128]{1,0:T(8,128)(2,1)S(1)}, u32[]{:S(2)}, u32[]{:S(2)}) collective-permute-start(bf16[1552,128]{1,0:T(8,128)(2,1)S(1)} %get-tuple-element.41.refs_0_), channel_id=1, source_target_pairs={{0,2},{1,3},{2,0},{3,1},{4,6},{5,7},{6,4},{7,5},{8,10},{9,11},{10,... | collective-permute-start | bytes 1191944 | tf_op jit(solution)/shard_map/ppermute | solution.py:345
  5.6 5.8 %all-to-all-start = ((bf16[8,56,128]{2,1,0:T(8,128)(2,1)}), bf16[8,56,128]{2,1,0:T(8,128)(2,1)S(1)}, u32[]{:S(2)}, u32[]{:S(2)}) async-start(bf16[8,56,128]{2,1,0:T(8,128)(2,1)} %get-tuple-element.51), calls=%async_computation | async-start | bytes 229376 | tf_op jit(solution)/shard_map/all_to_all | solution.py:349
  12.1 0.4 shard_map.174
  12.5 0.7 %copy-done.3 = bf16[256,512]{1,0:T(8,128)(2,1)} copy-done((bf16[256,512]{1,0:T(8,128)(2,1)}, bf16[256,512]{1,0:T(8,128)(2,1)S(1)}, u32[]{:S(2)}) %copy-start.3) | copy-done | bytes 262168
  13.2 5.5 %all-to-all-done.got_ref = bf16[8,56,128]{2,1,0:T(8,128)(2,1)S(1)} async-done(((bf16[8,56,128]{2,1,0:T(8,128)(2,1)}), bf16[8,56,128]{2,1,0:T(8,128)(2,1)S(1)}, u32[]{:S(2)}, u32[]{:S(2)}) %all-to-all-start) | async-done | bytes 114720 | tf_op jit(solution)/shard_map/all_to_all | solution.py:349
  18.7 0.3 shard_map.175
  19.1 0.6 %collective-permute-start.4 = (bf16[256,128]{1,0:T(8,128)(2,1)S(1)}, bf16[256,128]{1,0:T(8,128)(2,1)S(1)}, u32[]{:S(2)}, u32[]{:S(2)}) collective-permute-start(bf16[256,128]{1,0:T(8,128)(2,1)S(1)} %get-tuple-element.53.refs_4_), channel_id=1, source_target_pairs={{0,2},{1,3},{2,0},{3,1},{4,6},{5,7},{6,4},{7,5},{8,10},{9,11},{10,... | collective-permute-start | bytes 196616 | tf_op jit(solution)/shard_map/ppermute | solution.py:345
  19.7 0.2 collective-permute-start.3
  19.8 3.7 %collective-permute-done.4.refs_6_ = bf16[256,128]{1,0:T(8,128)(2,1)S(1)} collective-permute-done((bf16[256,128]{1,0:T(8,128)(2,1)S(1)}, bf16[256,128]{1,0:T(8,128)(2,1)S(1)}, u32[]{:S(2)}, u32[]{:S(2)}) %collective-permute-start.4) | collective-permute-done | bytes 65568 | tf_op jit(solution)/shard_map/ppermute | solution.py:345
  23.6 1.2 %collective-permute-done.5.refs_7_ = bf16[256,128]{1,0:T(8,128)(2,1)S(1)} collective-permute-done((bf16[256,128]{1,0:T(8,128)(2,1)S(1)}, bf16[256,128]{1,0:T(8,128)(2,1)S(1)}, u32[]{:S(2)}, u32[]{:S(2)}) %collective-permute-start.5) | collective-permute-done | bytes 65568 | tf_op jit(solution)/shard_map/ppermute | solution.py:345
  24.8 0.9 %shard_map.176 = (f32[256,128]{1,0:T(8,128)S(1)}, bf16[256,512]{1,0:T(8,128)(2,1)S(1)}, bf16[256,128]{1,0:T(8,128)(2,1)S(1)}, f32[1,128]{1,0:T(1,128)S(1)}, bf16...) custom-call(s32[1]{0:T(128)} %bitcast.2.me_ref, ...), custom_call_target="tpu_custom_call" | custom-call | tf_op jit(solution)/shard_map/pallas_call | solution.py:444
  25.8 0.8 %collective-permute-start.10 = (bf16[256,128]{1,0:T(8,128)(2,1)S(1)}, bf16[256,128]{1,0:T(8,128)(2,1)S(1)}, u32[]{:S(2)}, u32[]{:S(2)}) collective-permute-start(bf16[256,128]{1,0:T(8,128)(2,1)S(1)} %get-tuple-element.68), channel_id=1, source_target_pairs={{0,12},{4,8},{8,4},{12,0},{16,28},{20,24},{24,20},{28,16},{1,13},{... | collective-permute-start | bytes 196616 | tf_op jit(solution)/shard_map/ppermute | solution.py:345
  26.6 1.0 %collective-permute-start.11 = (bf16[256,128]{1,0:T(8,128)(2,1)S(1)}, bf16[256,128]{1,0:T(8,128)(2,1)S(1)}, u32[]{:S(2)}, u32[]{:S(2)}) collective-permute-start(bf16[256,128]{1,0:T(8,128)(2,1)S(1)} %get-tuple-element.69), channel_id=1, source_target_pairs={{0,8},{4,12},{8,0},{12,4},{16,24},{20,28},{24,16},{28,20},{1,9},{5... | collective-permute-start | bytes 196616 | tf_op jit(solution)/shard_map/ppermute | solution.py:345
  27.5 1.8 %collective-permute-start.12 = (bf16[256,128]{1,0:T(8,128)(2,1)S(1)}, bf16[256,128]{1,0:T(8,128)(2,1)S(1)}, u32[]{:S(2)}, u32[]{:S(2)}) collective-permute-start(bf16[256,128]{1,0:T(8,128)(2,1)S(1)} %get-tuple-element.70), channel_id=1, source_target_pairs={{0,4},{4,0},{8,12},{12,8},{16,20},{20,16},{24,28},{28,24},{1,5},{5... | collective-permute-start | bytes 196616 | tf_op jit(solution)/shard_map/ppermute | solution.py:345
  29.3 0.2 shard_map.178
  29.5 0.5 %collective-permute-start.6 = (bf16[4,56,128]{2,1,0:T(8,128)(2,1)S(1)}, bf16[4,56,128]{2,1,0:T(8,128)(2,1)S(1)}, u32[]{:S(2)}, u32[]{:S(2)}) collective-permute-start(bf16[4,56,128]{2,1,0:T(8,128)(2,1)S(1)} %shard_map.178), channel_id=1, source_target_pairs={{0,16},{4,20},{8,24},{12,28},{16,0},{20,4},{24,8},{28,12},{1,17},{... | collective-permute-start | bytes 172040 | tf_op jit(solution)/shard_map/ppermute | solution.py:345
  30.0 0.9 %shard_map.177 = (bf16[256,128]{1,0:T(8,128)(2,1)}, f32[256,128]{1,0:T(8,128)S(1)}, bf16[4,64,128]{2,1,0:T(8,128)(2,1)S(1)}) custom-call(s32[1]{0:T(128)} %bitcast.side_ref, s32[1]{0:T(128)} %bitcast.1.seat_ref, f32[256,128]{1,0:T(8,128)S(1)} %get-tuple-element.54.own_ref, bf16[256,512]{1,0:T(8,128)(2,1)S(1)} %get-tuple-element.55.grad_ref, ...), custom_call_target="tpu_custom_call" | custom-call | flops 100000000 | bytes 1000000 | tf_op jit(solution)/shard_map/pallas_call | solution.py:471
  30.8 0.7 %collective-permute-done.10.refs_0_ = bf16[256,128]{1,0:T(8,128)(2,1)S(1)} collective-permute-done((bf16[256,128]{1,0:T(8,128)(2,1)S(1)}, bf16[256,128]{1,0:T(8,128)(2,1)S(1)}, u32[]{:S(2)}, u32[]{:S(2)}) %collective-permute-start.10) | collective-permute-done | bytes 65568 | tf_op jit(solution)/shard_map/ppermute | solution.py:345
  31.6 0.7 %collective-permute-done.12.refs_2_ = bf16[256,128]{1,0:T(8,128)(2,1)S(1)} collective-permute-done((bf16[256,128]{1,0:T(8,128)(2,1)S(1)}, bf16[256,128]{1,0:T(8,128)(2,1)S(1)}, u32[]{:S(2)}, u32[]{:S(2)}) %collective-permute-start.12) | collective-permute-done | bytes 65568 | tf_op jit(solution)/shard_map/ppermute | solution.py:345
  32.3 1.2 %collective-permute-start.13 = (bf16[256,128]{1,0:T(8,128)(2,1)S(1)}, bf16[256,128]{1,0:T(8,128)(2,1)S(1)}, u32[]{:S(2)}, u32[]{:S(2)}) collective-permute-start(bf16[256,128]{1,0:T(8,128)(2,1)S(1)} %shard_map.181.own_ref), channel_id=1, source_target_pairs={{0,16},{4,20},{8,24},{12,28},{16,0},{20,4},{24,8},{28,12},{1,17},{... | collective-permute-start | bytes 196616 | tf_op jit(solution)/shard_map/ppermute | solution.py:345
  33.5 1.2 %collective-permute-done.6.mirror_ref = bf16[4,56,128]{2,1,0:T(8,128)(2,1)S(1)} collective-permute-done((bf16[4,56,128]{2,1,0:T(8,128)(2,1)S(1)}, bf16[4,56,128]{2,1,0:T(8,128)(2,1)S(1)}, u32[]{:S(2)}, u32[]{:S(2)}) %collective-permute-start.6) | collective-permute-done | bytes 57376 | tf_op jit(solution)/shard_map/ppermute | solution.py:345
  34.7 0.9 %collective-permute-start.7 = (bf16[128,128]{1,0:T(8,128)(2,1)S(1)}, bf16[128,128]{1,0:T(8,128)(2,1)S(1)}, u32[]{:S(2)}, u32[]{:S(2)}) collective-permute-start(bf16[128,128]{1,0:T(8,128)(2,1)S(1)} %get-tuple-element.64), channel_id=1, source_target_pairs={{0,4},{4,0},{8,12},{12,8},{16,20},{20,16},{24,28},{28,24},{1,5},{5... | collective-permute-start | bytes 98312 | tf_op jit(solution)/shard_map/ppermute | solution.py:345
  35.6 0.5 %collective-permute-start.8 = (bf16[128,128]{1,0:T(8,128)(2,1)S(1)}, bf16[128,128]{1,0:T(8,128)(2,1)S(1)}, u32[]{:S(2)}, u32[]{:S(2)}) collective-permute-start(bf16[128,128]{1,0:T(8,128)(2,1)S(1)} %get-tuple-element.65), channel_id=1, source_target_pairs={{0,8},{4,12},{8,0},{12,4},{16,24},{20,28},{24,16},{28,20},{1,9},{5... | collective-permute-start | bytes 98312 | tf_op jit(solution)/shard_map/ppermute | solution.py:345
  36.1 2.2 %collective-permute-start.9 = (bf16[128,128]{1,0:T(8,128)(2,1)S(1)}, bf16[128,128]{1,0:T(8,128)(2,1)S(1)}, u32[]{:S(2)}, u32[]{:S(2)}) collective-permute-start(bf16[128,128]{1,0:T(8,128)(2,1)S(1)} %get-tuple-element.66), channel_id=1, source_target_pairs={{0,12},{4,8},{8,4},{12,0},{16,28},{20,24},{24,20},{28,16},{1,13},{... | collective-permute-start | bytes 98312 | tf_op jit(solution)/shard_map/ppermute | solution.py:345
  38.3 0.3 collective-permute-start.16
  38.6 1.1 %collective-permute-start.15 = (bf16[256,128]{1,0:T(8,128)(2,1)S(1)}, bf16[256,128]{1,0:T(8,128)(2,1)S(1)}, u32[]{:S(2)}, u32[]{:S(2)}) collective-permute-start(bf16[256,128]{1,0:T(8,128)(2,1)S(1)} %shard_map.182.refs_0_), channel_id=1, source_target_pairs={{0,4},{4,0},{8,12},{12,8},{16,20},{20,16},{24,28},{28,24},{1,5},{5... | collective-permute-start | bytes 196616 | tf_op jit(solution)/shard_map/ppermute | solution.py:345
  39.7 2.2 %collective-permute-start.14 = (bf16[256,128]{1,0:T(8,128)(2,1)S(1)}, bf16[256,128]{1,0:T(8,128)(2,1)S(1)}, u32[]{:S(2)}, u32[]{:S(2)}) collective-permute-start(bf16[256,128]{1,0:T(8,128)(2,1)S(1)} %shard_map.182.refs_0_), channel_id=1, source_target_pairs={{0,12},{4,8},{8,4},{12,0},{16,28},{20,24},{24,20},{28,16},{1,13},{... | collective-permute-start | bytes 196616 | tf_op jit(solution)/shard_map/ppermute | solution.py:345
  41.9 0.9 %shard_map.180 = (bf16[256,128]{1,0:T(8,128)(2,1)}, f32[1,128]{1,0:T(1,128)}) custom-call(s32[1]{0:T(128)} %bitcast.side_ref, s32[1]{0:T(128)} %bitcast.1.seat_ref, f32[256,128]{1,0:T(8,128)S(1)} %get-tuple-element.60.back_ref, bf16[256,512]{1,0:T(8,128)(2,1)S(1)} %copy-done.4, bf16[128,128]{1,0:T(8,128)(2,1)S(1)} %get-tuple-element.63.refs_0_, ...), custom_call_target="tpu_custom_call" | custom-call | flops 2000000000 | bytes 1000000 | tf_op jit(solution)/shard_map/pallas_call | solution.py:503
  42.8 0.8 %shard_map.183 = (f32[128,512]{1,0:T(8,128)}, f32[128,512]{1,0:T(8,128)}) custom-call(s32[1]{0:T(128)} %bitcast.1.seat_ref, bf16[256,128]{1,0:T(8,128)(2,1)S(1)} %shard_map.182.refs_0_, bf16[256,128]{1,0:T(8,128)(2,1)S(1)} %collective-permute-done.15.refs_1_, bf16[256,128]{1,0:T(8,128)(2,1)S(1)} %collective-permute-done.16.refs_2_), custom_call_target="tpu_custom_call" | custom-call | tf_op jit(solution)/shard_map/pallas_call | solution.py:513
  43.7 1.2 %collective-permute-done.14.got_ref = bf16[256,128]{1,0:T(8,128)(2,1)S(1)} collective-permute-done((bf16[256,128]{1,0:T(8,128)(2,1)S(1)}, bf16[256,128]{1,0:T(8,128)(2,1)S(1)}, u32[]{:S(2)}, u32[]{:S(2)}) %collective-permute-start.14) | collective-permute-done | bytes 65568 | tf_op jit(solution)/shard_map/ppermute | solution.py:345
  44.9 0.7 %shard_map.184 = (f32[128,512]{1,0:T(8,128)}, f32[128,512]{1,0:T(8,128)}) custom-call(s32[1]{0:T(128)} %bitcast.1.seat_ref, bf16[256,128]{1,0:T(8,128)(2,1)S(1)} %collective-permute-done.14.got_ref, f32[128,512]{1,0:T(8,128)} %get-tuple-element.72.begun_self_ref, ...), custom_call_target="tpu_custom_call", output_to_operand_aliasing={{0}: (2, {}), {1}: (3, {})} | custom-call | tf_op jit(solution)/shard_map/pallas_call | solution.py:522
  (26 shorter events, 0.3 us)
Async XLA Ops:
  2.6 16.1 %collective-permute-start.1 = (bf16[1552,128]{1,0:T(8,128)(2,1)S(1)}, bf16[1552,128]{1,0:T(8,128)(2,1)S(1)}, u32[]{:S(2)}, u32[]{:S(2)}) collective-permute-start(bf16[1552,128]{1,0:T(8,128)(2,1)S(1)} %get-tuple-element.41.refs_0_), channel_id=1, source_target_pairs={{0,2},{1,3},{2,0},{3,1},{4,6},{5,7},{6,4},{7,5},{8,10},{9,11},{10,... | collective-permute-start | bytes 1191944 | tf_op jit(solution)/shard_map/ppermute | solution.py:345
  5.6 13.1 %all-to-all-start = ((bf16[8,56,128]{2,1,0:T(8,128)(2,1)}), bf16[8,56,128]{2,1,0:T(8,128)(2,1)S(1)}, u32[]{:S(2)}, u32[]{:S(2)}) async-start(bf16[8,56,128]{2,1,0:T(8,128)(2,1)} %get-tuple-element.51), calls=%async_computation | async-start | bytes 229376 | tf_op jit(solution)/shard_map/all_to_all | solution.py:349
  11.4 12.1 %collective-permute-start = (bf16[1552,128]{1,0:T(8,128)(2,1)S(1)}, bf16[1552,128]{1,0:T(8,128)(2,1)S(1)}, u32[]{:S(2)}, u32[]{:S(2)}) collective-permute-start(bf16[1552,128]{1,0:T(8,128)(2,1)S(1)} %get-tuple-element.41.refs_0_), channel_id=1, source_target_pairs={{0,1},{1,0},{2,3},{3,2},{4,5},{5,4},{6,7},{7,6},{8,9},{9,8},{10,11... | collective-permute-start | bytes 1191944 | tf_op jit(solution)/shard_map/ppermute | solution.py:345
  12.1 6.6 %copy-start.1 = (bf16[256,128]{1,0:T(8,128)(2,1)S(1)}, bf16[256,128]{1,0:T(8,128)(2,1)}, u32[]{:S(2)}) copy-start(bf16[256,128]{1,0:T(8,128)(2,1)} %x_ref.5) | copy-start | bytes 196612
  12.5 0.7 %copy-start.3 = (bf16[256,512]{1,0:T(8,128)(2,1)}, bf16[256,512]{1,0:T(8,128)(2,1)S(1)}, u32[]{:S(2)}) copy-start(bf16[256,512]{1,0:T(8,128)(2,1)S(1)} %get-tuple-element.61.mark_ref) | copy-start | bytes 786436
  18.7 6.1 %copy-start = (bf16[128,512]{1,0:T(8,128)(2,1)S(1)}, bf16[128,512]{1,0:T(8,128)(2,1)}, u32[]{:S(2)}) copy-start(bf16[128,512]{1,0:T(8,128)(2,1)} %ws_ref.5) | copy-start | bytes 393220
  18.7 6.1 %copy-start.2 = (bf16[128,512]{1,0:T(8,128)(2,1)S(1)}, bf16[128,512]{1,0:T(8,128)(2,1)}, u32[]{:S(2)}) copy-start(bf16[128,512]{1,0:T(8,128)(2,1)} %wn_ref.3) | copy-start | bytes 393220
  19.0 5.8 %collective-permute-start.2 = (bf16[1552,128]{1,0:T(8,128)(2,1)S(1)}, bf16[1552,128]{1,0:T(8,128)(2,1)S(1)}, u32[]{:S(2)}, u32[]{:S(2)}) collective-permute-start(bf16[1552,128]{1,0:T(8,128)(2,1)S(1)} %get-tuple-element.52.refs_2_), channel_id=1, source_target_pairs={{0,1},{1,0},{2,3},{3,2},{4,5},{5,4},{6,7},{7,6},{8,9},{9,8},{10,11... | collective-permute-start | bytes 1191944 | tf_op jit(solution)/shard_map/ppermute | solution.py:345
  19.1 4.5 %collective-permute-start.4 = (bf16[256,128]{1,0:T(8,128)(2,1)S(1)}, bf16[256,128]{1,0:T(8,128)(2,1)S(1)}, u32[]{:S(2)}, u32[]{:S(2)}) collective-permute-start(bf16[256,128]{1,0:T(8,128)(2,1)S(1)} %get-tuple-element.53.refs_4_), channel_id=1, source_target_pairs={{0,2},{1,3},{2,0},{3,1},{4,6},{5,7},{6,4},{7,5},{8,10},{9,11},{10,... | collective-permute-start | bytes 196616 | tf_op jit(solution)/shard_map/ppermute | solution.py:345
  19.7 3.9 %collective-permute-start.3 = (bf16[256,128]{1,0:T(8,128)(2,1)S(1)}, bf16[256,128]{1,0:T(8,128)(2,1)S(1)}, u32[]{:S(2)}, u32[]{:S(2)}) collective-permute-start(bf16[256,128]{1,0:T(8,128)(2,1)S(1)} %get-tuple-element.53.refs_4_), channel_id=1, source_target_pairs={{0,1},{1,0},{2,3},{3,2},{4,5},{5,4},{6,7},{7,6},{8,9},{9,8},{10,11... | collective-permute-start | bytes 196616 | tf_op jit(solution)/shard_map/ppermute | solution.py:345
  23.6 1.3 %collective-permute-start.5 = (bf16[256,128]{1,0:T(8,128)(2,1)S(1)}, bf16[256,128]{1,0:T(8,128)(2,1)S(1)}, u32[]{:S(2)}, u32[]{:S(2)}) collective-permute-start(bf16[256,128]{1,0:T(8,128)(2,1)S(1)} %collective-permute-done.4.refs_6_), channel_id=1, source_target_pairs={{0,1},{1,0},{2,3},{3,2},{4,5},{5,4},{6,7},{7,6},{8,9},{9,8},{10,11... | collective-permute-start | bytes 196616 | tf_op jit(solution)/shard_map/ppermute | solution.py:345
  25.8 5.8 %collective-permute-start.10 = (bf16[256,128]{1,0:T(8,128)(2,1)S(1)}, bf16[256,128]{1,0:T(8,128)(2,1)S(1)}, u32[]{:S(2)}, u32[]{:S(2)}) collective-permute-start(bf16[256,128]{1,0:T(8,128)(2,1)S(1)} %get-tuple-element.68), channel_id=1, source_target_pairs={{0,12},{4,8},{8,4},{12,0},{16,28},{20,24},{24,20},{28,16},{1,13},{... | collective-permute-start | bytes 196616 | tf_op jit(solution)/shard_map/ppermute | solution.py:345
  26.6 5.0 %collective-permute-start.11 = (bf16[256,128]{1,0:T(8,128)(2,1)S(1)}, bf16[256,128]{1,0:T(8,128)(2,1)S(1)}, u32[]{:S(2)}, u32[]{:S(2)}) collective-permute-start(bf16[256,128]{1,0:T(8,128)(2,1)S(1)} %get-tuple-element.69), channel_id=1, source_target_pairs={{0,8},{4,12},{8,0},{12,4},{16,24},{20,28},{24,16},{28,20},{1,9},{5... | collective-permute-start | bytes 196616 | tf_op jit(solution)/shard_map/ppermute | solution.py:345
  27.5 4.7 %collective-permute-start.12 = (bf16[256,128]{1,0:T(8,128)(2,1)S(1)}, bf16[256,128]{1,0:T(8,128)(2,1)S(1)}, u32[]{:S(2)}, u32[]{:S(2)}) collective-permute-start(bf16[256,128]{1,0:T(8,128)(2,1)S(1)} %get-tuple-element.70), channel_id=1, source_target_pairs={{0,4},{4,0},{8,12},{12,8},{16,20},{20,16},{24,28},{28,24},{1,5},{5... | collective-permute-start | bytes 196616 | tf_op jit(solution)/shard_map/ppermute | solution.py:345
  29.5 5.2 %collective-permute-start.6 = (bf16[4,56,128]{2,1,0:T(8,128)(2,1)S(1)}, bf16[4,56,128]{2,1,0:T(8,128)(2,1)S(1)}, u32[]{:S(2)}, u32[]{:S(2)}) collective-permute-start(bf16[4,56,128]{2,1,0:T(8,128)(2,1)S(1)} %shard_map.178), channel_id=1, source_target_pairs={{0,16},{4,20},{8,24},{12,28},{16,0},{20,4},{24,8},{28,12},{1,17},{... | collective-permute-start | bytes 172040 | tf_op jit(solution)/shard_map/ppermute | solution.py:345
  32.3 9.5 %copy-start.4 = (bf16[256,512]{1,0:T(8,128)(2,1)S(1)}, bf16[256,512]{1,0:T(8,128)(2,1)}, u32[]{:S(2)}) copy-start(bf16[256,512]{1,0:T(8,128)(2,1)} %copy-done.3) | copy-start | bytes 786436
  32.3 5.9 %collective-permute-start.13 = (bf16[256,128]{1,0:T(8,128)(2,1)S(1)}, bf16[256,128]{1,0:T(8,128)(2,1)S(1)}, u32[]{:S(2)}, u32[]{:S(2)}) collective-permute-start(bf16[256,128]{1,0:T(8,128)(2,1)S(1)} %shard_map.181.own_ref), channel_id=1, source_target_pairs={{0,16},{4,20},{8,24},{12,28},{16,0},{20,4},{24,8},{28,12},{1,17},{... | collective-permute-start | bytes 196616 | tf_op jit(solution)/shard_map/ppermute | solution.py:345
  34.7 5.0 %collective-permute-start.7 = (bf16[128,128]{1,0:T(8,128)(2,1)S(1)}, bf16[128,128]{1,0:T(8,128)(2,1)S(1)}, u32[]{:S(2)}, u32[]{:S(2)}) collective-permute-start(bf16[128,128]{1,0:T(8,128)(2,1)S(1)} %get-tuple-element.64), channel_id=1, source_target_pairs={{0,4},{4,0},{8,12},{12,8},{16,20},{20,16},{24,28},{28,24},{1,5},{5... | collective-permute-start | bytes 98312 | tf_op jit(solution)/shard_map/ppermute | solution.py:345
  35.6 6.3 %collective-permute-start.8 = (bf16[128,128]{1,0:T(8,128)(2,1)S(1)}, bf16[128,128]{1,0:T(8,128)(2,1)S(1)}, u32[]{:S(2)}, u32[]{:S(2)}) collective-permute-start(bf16[128,128]{1,0:T(8,128)(2,1)S(1)} %get-tuple-element.65), channel_id=1, source_target_pairs={{0,8},{4,12},{8,0},{12,4},{16,24},{20,28},{24,16},{28,20},{1,9},{5... | collective-permute-start | bytes 98312 | tf_op jit(solution)/shard_map/ppermute | solution.py:345
  36.1 5.7 %collective-permute-start.9 = (bf16[128,128]{1,0:T(8,128)(2,1)S(1)}, bf16[128,128]{1,0:T(8,128)(2,1)S(1)}, u32[]{:S(2)}, u32[]{:S(2)}) collective-permute-start(bf16[128,128]{1,0:T(8,128)(2,1)S(1)} %get-tuple-element.66), channel_id=1, source_target_pairs={{0,12},{4,8},{8,4},{12,0},{16,28},{20,24},{24,20},{28,16},{1,13},{... | collective-permute-start | bytes 98312 | tf_op jit(solution)/shard_map/ppermute | solution.py:345
  38.3 4.4 %collective-permute-start.16 = (bf16[256,128]{1,0:T(8,128)(2,1)S(1)}, bf16[256,128]{1,0:T(8,128)(2,1)S(1)}, u32[]{:S(2)}, u32[]{:S(2)}) collective-permute-start(bf16[256,128]{1,0:T(8,128)(2,1)S(1)} %shard_map.182.refs_0_), channel_id=1, source_target_pairs={{0,8},{4,12},{8,0},{12,4},{16,24},{20,28},{24,16},{28,20},{1,9},{5... | collective-permute-start | bytes 196616 | tf_op jit(solution)/shard_map/ppermute | solution.py:345
  38.6 4.3 %collective-permute-start.15 = (bf16[256,128]{1,0:T(8,128)(2,1)S(1)}, bf16[256,128]{1,0:T(8,128)(2,1)S(1)}, u32[]{:S(2)}, u32[]{:S(2)}) collective-permute-start(bf16[256,128]{1,0:T(8,128)(2,1)S(1)} %shard_map.182.refs_0_), channel_id=1, source_target_pairs={{0,4},{4,0},{8,12},{12,8},{16,20},{20,16},{24,28},{28,24},{1,5},{5... | collective-permute-start | bytes 196616 | tf_op jit(solution)/shard_map/ppermute | solution.py:345
  39.7 5.2 %collective-permute-start.14 = (bf16[256,128]{1,0:T(8,128)(2,1)S(1)}, bf16[256,128]{1,0:T(8,128)(2,1)S(1)}, u32[]{:S(2)}, u32[]{:S(2)}) collective-permute-start(bf16[256,128]{1,0:T(8,128)(2,1)S(1)} %shard_map.182.refs_0_), channel_id=1, source_target_pairs={{0,12},{4,8},{8,4},{12,0},{16,28},{20,24},{24,20},{28,16},{1,13},{... | collective-permute-start | bytes 196616 | tf_op jit(solution)/shard_map/ppermute | solution.py:345

commit v22 on v20

--- a/solution.py
+++ b/solution.py
@@ -129,6 +129,10 @@
     mix_ref[:, rows:] = (ghost + hub_mix).astype(BF)
     turned_ref[...] = mix_ref[...].T
     mark_ref[...] = source_matrix(send_v[0], hub_v[...], rows, width)
+
+
+def pass_kernel(held_ref, passed_ref):
+    pass
 
 
 def neigh_kernel(x_ref, mix_ref, far_ref, got_ref, neigh_ref, passed_ref, wide_ref):
@@ -433,7 +437,15 @@
         compiler_params=PARAMS,
     )(features, mix, far, incoming)
     last = partner(far, "feat", 1)
-    far_neigh = partner(neigh, "feat", 2)
+    far_neigh = pl.pallas_call(
+        pass_kernel,
+        out_shape=shape((rows, cols), BF),
+        in_specs=[ANY],
+        out_specs=ANY,
+        input_output_aliases={0: 0},
+        compiler_params=PARAMS,
+        cost_estimate=pl.CostEstimate(flops=10**10, bytes_accessed=10**7, transcendentals=0),
+    )(partner(neigh, "feat", 2))
     every = [neigh, partner(neigh, "feat", 1), far_neigh, partner(far_neigh, "feat", 1)]
 
     own, grad, slope, sums, mirror, *returned = pl.pallas_call(

time: 45.8 us -> 45.5 us (level)
  waiting for transfers between devices: 15.4 us -> 14.8 us
    ppermute x17, waiting for transfers between devices: 9.22 us -> 8.68 us  [partner(): lax.ppermute(block, axis, [(i, i ^ k) for i in range(lax.axis_size(axis))])]
where the time goes in v22:
time: 45.5 us; the launch traced here: 45.2 us
  starting transfers between devices  21.9 us (48%)
  waiting for transfers between devices  14.8 us (33%)
  Pallas kernels  6.99 us (15%)
  between operations  1.37 us (3%)
    ppermute x17, starting transfers between devices, partner(): lax.ppermute(block, axis, [(i, i ^ k) for i in range(lax.axis_size(axis))])  16.1 us
    ppermute x17, waiting for transfers between devices, partner(): lax.ppermute(block, axis, [(i, i ^ k) for i in range(lax.axis_size(axis))])  8.68 us
    all_to_all x1, waiting for transfers between devices, exchange(): lax.all_to_all(blocks, 'dom', split_axis=0, concat_axis=0, axis_index_gro...  6.17 us
    all_to_all x1, starting transfers between devices, exchange(): lax.all_to_all(blocks, 'dom', split_axis=0, concat_axis=0, axis_index_gro...  5.83 us
    pallas_call x1, Pallas kernels, on_device(): pl.pallas_call(functools.partial(send_kernel, width), out_shape=(shape((p...  1.96 us
    pallas_call x1, Pallas kernels, on_device(): pl.pallas_call(functools.partial(dense_kernel, slots, hub_here, feats, wi...  1.07 us
  transfers between devices with their start and end apart: 18, of which 9 were waited for; matrix products, arithmetic and copies ran while one was open for 0% of the time, Pallas kernels for 7%

profile of v22, /device:TPU:0, one launch (start us, length us, event | category | flops | bytes accessed | tf_op | source)
XLA Modules:
  0.0 45.2 jit_solution(17612552028146090440)
XLA Ops:
  0.6 2.0 %shard_map.173 = (bf16[8,56,128]{2,1,0:T(8,128)(2,1)}, bf16[1552,128]{1,0:T(8,128)(2,1)S(1)}, s32[1,8,48]{2,1,0:T(8,128)S(1)}, s32[1,2]{1,0:T(1,128)S(1)}, s32[1...) custom-call(bf16[256,128]{1,0:T(8,128)(2,1)} %x_ref.5, ...), custom_call_target="tpu_custom_call" | custom-call | tf_op jit(solution)/shard_map/pallas_call | solution.py:397
  2.6 3.0 %collective-permute-start.1 = (bf16[1552,128]{1,0:T(8,128)(2,1)S(1)}, bf16[1552,128]{1,0:T(8,128)(2,1)S(1)}, u32[]{:S(2)}, u32[]{:S(2)}) collective-permute-start(bf16[1552,128]{1,0:T(8,128)(2,1)S(1)} %get-tuple-element.51.refs_0_), channel_id=1, source_target_pairs={{0,2},{1,3},{2,0},{3,1},{4,6},{5,7},{6,4},{7,5},{8,10},{9,11},{10,... | collective-permute-start | bytes 1191944 | tf_op jit(solution)/shard_map/ppermute | solution.py:344
  5.6 5.8 %all-to-all-start = ((bf16[8,56,128]{2,1,0:T(8,128)(2,1)}), bf16[8,56,128]{2,1,0:T(8,128)(2,1)S(1)}, u32[]{:S(2)}, u32[]{:S(2)}) async-start(bf16[8,56,128]{2,1,0:T(8,128)(2,1)} %get-tuple-element.53), calls=%async_computation | async-start | bytes 229376 | tf_op jit(solution)/shard_map/all_to_all | solution.py:348
  12.1 0.4 shard_map.174
  12.5 6.2 %all-to-all-done.got_ref = bf16[8,56,128]{2,1,0:T(8,128)(2,1)S(1)} async-done(((bf16[8,56,128]{2,1,0:T(8,128)(2,1)}), bf16[8,56,128]{2,1,0:T(8,128)(2,1)S(1)}, u32[]{:S(2)}, u32[]{:S(2)}) %all-to-all-start) | async-done | bytes 114720 | tf_op jit(solution)/shard_map/all_to_all | solution.py:348
  18.7 0.3 shard_map.175
  19.0 0.6 %collective-permute-start.4 = (bf16[256,128]{1,0:T(8,128)(2,1)S(1)}, bf16[256,128]{1,0:T(8,128)(2,1)S(1)}, u32[]{:S(2)}, u32[]{:S(2)}) collective-permute-start(bf16[256,128]{1,0:T(8,128)(2,1)S(1)} %get-tuple-element.55.refs_4_), channel_id=1, source_target_pairs={{0,2},{1,3},{2,0},{3,1},{4,6},{5,7},{6,4},{7,5},{8,10},{9,11},{10,... | collective-permute-start | bytes 196616 | tf_op jit(solution)/shard_map/ppermute | solution.py:344
  19.6 0.5 %collective-permute-start.3 = (bf16[256,128]{1,0:T(8,128)(2,1)S(1)}, bf16[256,128]{1,0:T(8,128)(2,1)S(1)}, u32[]{:S(2)}, u32[]{:S(2)}) collective-permute-start(bf16[256,128]{1,0:T(8,128)(2,1)S(1)} %get-tuple-element.55.refs_4_), channel_id=1, source_target_pairs={{0,1},{1,0},{2,3},{3,2},{4,5},{5,4},{6,7},{7,6},{8,9},{9,8},{10,11... | collective-permute-start | bytes 196616 | tf_op jit(solution)/shard_map/ppermute | solution.py:344
  20.1 3.2 %collective-permute-done.4.held_ref = bf16[256,128]{1,0:T(8,128)(2,1)S(1)} collective-permute-done((bf16[256,128]{1,0:T(8,128)(2,1)S(1)}, bf16[256,128]{1,0:T(8,128)(2,1)S(1)}, u32[]{:S(2)}, u32[]{:S(2)}) %collective-permute-start.4) | collective-permute-done | bytes 65568 | tf_op jit(solution)/shard_map/ppermute | solution.py:344
  23.3 1.2 %collective-permute-done.5.refs_7_ = bf16[256,128]{1,0:T(8,128)(2,1)S(1)} collective-permute-done((bf16[256,128]{1,0:T(8,128)(2,1)S(1)}, bf16[256,128]{1,0:T(8,128)(2,1)S(1)}, u32[]{:S(2)}, u32[]{:S(2)}) %collective-permute-start.5) | collective-permute-done | bytes 65568 | tf_op jit(solution)/shard_map/ppermute | solution.py:344
  24.6 1.1 %shard_map.177 = (f32[256,128]{1,0:T(8,128)S(1)}, bf16[256,512]{1,0:T(8,128)(2,1)S(1)}, bf16[256,128]{1,0:T(8,128)(2,1)S(1)}, f32[1,128]{1,0:T(1,128)S(1)}, bf16...) custom-call(s32[1]{0:T(128)} %bitcast.2.me_ref, ...), custom_call_target="tpu_custom_call" | custom-call | tf_op jit(solution)/shard_map/pallas_call | solution.py:451
  25.6 0.8 %collective-permute-start.10 = (bf16[256,128]{1,0:T(8,128)(2,1)S(1)}, bf16[256,128]{1,0:T(8,128)(2,1)S(1)}, u32[]{:S(2)}, u32[]{:S(2)}) collective-permute-start(bf16[256,128]{1,0:T(8,128)(2,1)S(1)} %get-tuple-element.70), channel_id=1, source_target_pairs={{0,12},{4,8},{8,4},{12,0},{16,28},{20,24},{24,20},{28,16},{1,13},{... | collective-permute-start | bytes 196616 | tf_op jit(solution)/shard_map/ppermute | solution.py:344
  26.4 1.0 %collective-permute-start.11 = (bf16[256,128]{1,0:T(8,128)(2,1)S(1)}, bf16[256,128]{1,0:T(8,128)(2,1)S(1)}, u32[]{:S(2)}, u32[]{:S(2)}) collective-permute-start(bf16[256,128]{1,0:T(8,128)(2,1)S(1)} %get-tuple-element.71), channel_id=1, source_target_pairs={{0,8},{4,12},{8,0},{12,4},{16,24},{20,28},{24,16},{28,20},{1,9},{5... | collective-permute-start | bytes 196616 | tf_op jit(solution)/shard_map/ppermute | solution.py:344
  27.4 1.8 %collective-permute-start.12 = (bf16[256,128]{1,0:T(8,128)(2,1)S(1)}, bf16[256,128]{1,0:T(8,128)(2,1)S(1)}, u32[]{:S(2)}, u32[]{:S(2)}) collective-permute-start(bf16[256,128]{1,0:T(8,128)(2,1)S(1)} %get-tuple-element.72), channel_id=1, source_target_pairs={{0,4},{4,0},{8,12},{12,8},{16,20},{20,16},{24,28},{28,24},{1,5},{5... | collective-permute-start | bytes 196616 | tf_op jit(solution)/shard_map/ppermute | solution.py:344
  29.2 0.4 collective-permute-start.6
  29.6 0.9 %shard_map.178 = (bf16[256,128]{1,0:T(8,128)(2,1)}, f32[256,128]{1,0:T(8,128)S(1)}, bf16[4,64,128]{2,1,0:T(8,128)(2,1)S(1)}) custom-call(s32[1]{0:T(128)} %bitcast.side_ref, s32[1]{0:T(128)} %bitcast.1.seat_ref, f32[256,128]{1,0:T(8,128)S(1)} %get-tuple-element.56.own_ref, bf16[256,512]{1,0:T(8,128)(2,1)S(1)} %get-tuple-element.57.grad_ref, ...), custom_call_target="tpu_custom_call" | custom-call | flops 100000000 | bytes 1000000 | tf_op jit(solution)/shard_map/pallas_call | solution.py:472
  30.5 1.0 %collective-permute-done.10.refs_0_ = bf16[256,128]{1,0:T(8,128)(2,1)S(1)} collective-permute-done((bf16[256,128]{1,0:T(8,128)(2,1)S(1)}, bf16[256,128]{1,0:T(8,128)(2,1)S(1)}, u32[]{:S(2)}, u32[]{:S(2)}) %collective-permute-start.10) | collective-permute-done | bytes 65568 | tf_op jit(solution)/shard_map/ppermute | solution.py:344
  31.5 0.7 %collective-permute-done.12.refs_2_ = bf16[256,128]{1,0:T(8,128)(2,1)S(1)} collective-permute-done((bf16[256,128]{1,0:T(8,128)(2,1)S(1)}, bf16[256,128]{1,0:T(8,128)(2,1)S(1)}, u32[]{:S(2)}, u32[]{:S(2)}) %collective-permute-start.12) | collective-permute-done | bytes 65568 | tf_op jit(solution)/shard_map/ppermute | solution.py:344
  32.2 0.9 %collective-permute-start.13 = (bf16[256,128]{1,0:T(8,128)(2,1)S(1)}, bf16[256,128]{1,0:T(8,128)(2,1)S(1)}, u32[]{:S(2)}, u32[]{:S(2)}) collective-permute-start(bf16[256,128]{1,0:T(8,128)(2,1)S(1)} %shard_map.181.own_ref), channel_id=1, source_target_pairs={{0,16},{4,20},{8,24},{12,28},{16,0},{20,4},{24,8},{28,12},{1,17},{... | collective-permute-start | bytes 196616 | tf_op jit(solution)/shard_map/ppermute | solution.py:344
  33.1 1.2 %collective-permute-done.6.mirror_ref = bf16[4,56,128]{2,1,0:T(8,128)(2,1)S(1)} collective-permute-done((bf16[4,56,128]{2,1,0:T(8,128)(2,1)S(1)}, bf16[4,56,128]{2,1,0:T(8,128)(2,1)S(1)}, u32[]{:S(2)}, u32[]{:S(2)}) %collective-permute-start.6) | collective-permute-done | bytes 57376 | tf_op jit(solution)/shard_map/ppermute | solution.py:344
  34.3 0.9 %collective-permute-start.7 = (bf16[128,128]{1,0:T(8,128)(2,1)S(1)}, bf16[128,128]{1,0:T(8,128)(2,1)S(1)}, u32[]{:S(2)}, u32[]{:S(2)}) collective-permute-start(bf16[128,128]{1,0:T(8,128)(2,1)S(1)} %get-tuple-element.66), channel_id=1, source_target_pairs={{0,4},{4,0},{8,12},{12,8},{16,20},{20,16},{24,28},{28,24},{1,5},{5... | collective-permute-start | bytes 98312 | tf_op jit(solution)/shard_map/ppermute | solution.py:344
  35.2 0.5 %collective-permute-start.8 = (bf16[128,128]{1,0:T(8,128)(2,1)S(1)}, bf16[128,128]{1,0:T(8,128)(2,1)S(1)}, u32[]{:S(2)}, u32[]{:S(2)}) collective-permute-start(bf16[128,128]{1,0:T(8,128)(2,1)S(1)} %get-tuple-element.67), channel_id=1, source_target_pairs={{0,8},{4,12},{8,0},{12,4},{16,24},{20,28},{24,16},{28,20},{1,9},{5... | collective-permute-start | bytes 98312 | tf_op jit(solution)/shard_map/ppermute | solution.py:344
  35.7 2.1 %collective-permute-start.9 = (bf16[128,128]{1,0:T(8,128)(2,1)S(1)}, bf16[128,128]{1,0:T(8,128)(2,1)S(1)}, u32[]{:S(2)}, u32[]{:S(2)}) collective-permute-start(bf16[128,128]{1,0:T(8,128)(2,1)S(1)} %get-tuple-element.68), channel_id=1, source_target_pairs={{0,12},{4,8},{8,4},{12,0},{16,28},{20,24},{24,20},{28,16},{1,13},{... | collective-permute-start | bytes 98312 | tf_op jit(solution)/shard_map/ppermute | solution.py:344
  37.9 0.2 collective-permute-done.13.other_ref
  38.1 0.3 collective-permute-start.16
  38.4 0.9 %collective-permute-start.15 = (bf16[256,128]{1,0:T(8,128)(2,1)S(1)}, bf16[256,128]{1,0:T(8,128)(2,1)S(1)}, u32[]{:S(2)}, u32[]{:S(2)}) collective-permute-start(bf16[256,128]{1,0:T(8,128)(2,1)S(1)} %shard_map.182.refs_0_), channel_id=1, source_target_pairs={{0,4},{4,0},{8,12},{12,8},{16,20},{20,16},{24,28},{28,24},{1,5},{5... | collective-permute-start | bytes 196616 | tf_op jit(solution)/shard_map/ppermute | solution.py:344
  39.3 2.4 %collective-permute-start.14 = (bf16[256,128]{1,0:T(8,128)(2,1)S(1)}, bf16[256,128]{1,0:T(8,128)(2,1)S(1)}, u32[]{:S(2)}, u32[]{:S(2)}) collective-permute-start(bf16[256,128]{1,0:T(8,128)(2,1)S(1)} %shard_map.182.refs_0_), channel_id=1, source_target_pairs={{0,12},{4,8},{8,4},{12,0},{16,28},{20,24},{24,20},{28,16},{1,13},{... | collective-permute-start | bytes 196616 | tf_op jit(solution)/shard_map/ppermute | solution.py:344
  41.7 0.9 %shard_map.180 = (bf16[256,128]{1,0:T(8,128)(2,1)}, f32[1,128]{1,0:T(1,128)}) custom-call(s32[1]{0:T(128)} %bitcast.side_ref, s32[1]{0:T(128)} %bitcast.1.seat_ref, f32[256,128]{1,0:T(8,128)S(1)} %get-tuple-element.61.back_ref, bf16[256,512]{1,0:T(8,128)(2,1)S(1)} %get-tuple-element.62.mark_ref, bf16[128,128]{1,0:T(8,128)(2,1)S(1)} %get-tuple-element.65.refs_0_, ...), custom_call_target="tpu_custom_call" | custom-call | flops 2000000000 | bytes 1000000 | tf_op jit(solution)/shard_map/pallas_call | solution.py:504
  42.6 0.1 collective-permute-done.15.refs_1_
  42.7 0.8 %shard_map.183 = (f32[128,512]{1,0:T(8,128)}, f32[128,512]{1,0:T(8,128)}) custom-call(s32[1]{0:T(128)} %bitcast.1.seat_ref, bf16[256,128]{1,0:T(8,128)(2,1)S(1)} %shard_map.182.refs_0_, bf16[256,128]{1,0:T(8,128)(2,1)S(1)} %collective-permute-done.15.refs_1_, bf16[256,128]{1,0:T(8,128)(2,1)S(1)} %collective-permute-done.16.refs_2_), custom_call_target="tpu_custom_call" | custom-call | tf_op jit(solution)/shard_map/pallas_call | solution.py:514
  43.5 1.0 %collective-permute-done.14.got_ref = bf16[256,128]{1,0:T(8,128)(2,1)S(1)} collective-permute-done((bf16[256,128]{1,0:T(8,128)(2,1)S(1)}, bf16[256,128]{1,0:T(8,128)(2,1)S(1)}, u32[]{:S(2)}, u32[]{:S(2)}) %collective-permute-start.14) | collective-permute-done | bytes 65568 | tf_op jit(solution)/shard_map/ppermute | solution.py:344
  44.5 0.7 %shard_map.184 = (f32[128,512]{1,0:T(8,128)}, f32[128,512]{1,0:T(8,128)}) custom-call(s32[1]{0:T(128)} %bitcast.1.seat_ref, bf16[256,128]{1,0:T(8,128)(2,1)S(1)} %collective-permute-done.14.got_ref, f32[128,512]{1,0:T(8,128)} %get-tuple-element.74.begun_self_ref, ...), custom_call_target="tpu_custom_call", output_to_operand_aliasing={{0}: (2, {}), {1}: (3, {})} | custom-call | tf_op jit(solution)/shard_map/pallas_call | solution.py:523
  (22 shorter events, 0.1 us)
Async XLA Ops:
  2.6 16.1 %collective-permute-start.1 = (bf16[1552,128]{1,0:T(8,128)(2,1)S(1)}, bf16[1552,128]{1,0:T(8,128)(2,1)S(1)}, u32[]{:S(2)}, u32[]{:S(2)}) collective-permute-start(bf16[1552,128]{1,0:T(8,128)(2,1)S(1)} %get-tuple-element.51.refs_0_), channel_id=1, source_target_pairs={{0,2},{1,3},{2,0},{3,1},{4,6},{5,7},{6,4},{7,5},{8,10},{9,11},{10,... | collective-permute-start | bytes 1191944 | tf_op jit(solution)/shard_map/ppermute | solution.py:344
  5.6 13.1 %all-to-all-start = ((bf16[8,56,128]{2,1,0:T(8,128)(2,1)}), bf16[8,56,128]{2,1,0:T(8,128)(2,1)S(1)}, u32[]{:S(2)}, u32[]{:S(2)}) async-start(bf16[8,56,128]{2,1,0:T(8,128)(2,1)} %get-tuple-element.53), calls=%async_computation | async-start | bytes 229376 | tf_op jit(solution)/shard_map/all_to_all | solution.py:348
  12.1 6.6 %copy-start.1 = (bf16[256,128]{1,0:T(8,128)(2,1)S(1)}, bf16[256,128]{1,0:T(8,128)(2,1)}, u32[]{:S(2)}) copy-start(bf16[256,128]{1,0:T(8,128)(2,1)} %x_ref.5) | copy-start | bytes 196612
  19.0 4.3 %collective-permute-start.4 = (bf16[256,128]{1,0:T(8,128)(2,1)S(1)}, bf16[256,128]{1,0:T(8,128)(2,1)S(1)}, u32[]{:S(2)}, u32[]{:S(2)}) collective-permute-start(bf16[256,128]{1,0:T(8,128)(2,1)S(1)} %get-tuple-element.55.refs_4_), channel_id=1, source_target_pairs={{0,2},{1,3},{2,0},{3,1},{4,6},{5,7},{6,4},{7,5},{8,10},{9,11},{10,... | collective-permute-start | bytes 196616 | tf_op jit(solution)/shard_map/ppermute | solution.py:344
  19.6 3.7 %collective-permute-start = (bf16[1552,128]{1,0:T(8,128)(2,1)S(1)}, bf16[1552,128]{1,0:T(8,128)(2,1)S(1)}, u32[]{:S(2)}, u32[]{:S(2)}) collective-permute-start(bf16[1552,128]{1,0:T(8,128)(2,1)S(1)} %get-tuple-element.51.refs_0_), channel_id=1, source_target_pairs={{0,1},{1,0},{2,3},{3,2},{4,5},{5,4},{6,7},{7,6},{8,9},{9,8},{10,11... | collective-permute-start | bytes 1191944 | tf_op jit(solution)/shard_map/ppermute | solution.py:344
  19.6 3.7 %collective-permute-start.3 = (bf16[256,128]{1,0:T(8,128)(2,1)S(1)}, bf16[256,128]{1,0:T(8,128)(2,1)S(1)}, u32[]{:S(2)}, u32[]{:S(2)}) collective-permute-start(bf16[256,128]{1,0:T(8,128)(2,1)S(1)} %get-tuple-element.55.refs_4_), channel_id=1, source_target_pairs={{0,1},{1,0},{2,3},{3,2},{4,5},{5,4},{6,7},{7,6},{8,9},{9,8},{10,11... | collective-permute-start | bytes 196616 | tf_op jit(solution)/shard_map/ppermute | solution.py:344
  20.1 4.5 %copy-start = (bf16[128,512]{1,0:T(8,128)(2,1)S(1)}, bf16[128,512]{1,0:T(8,128)(2,1)}, u32[]{:S(2)}) copy-start(bf16[128,512]{1,0:T(8,128)(2,1)} %ws_ref.5) | copy-start | bytes 393220
  20.1 4.5 %copy-start.2 = (bf16[128,512]{1,0:T(8,128)(2,1)S(1)}, bf16[128,512]{1,0:T(8,128)(2,1)}, u32[]{:S(2)}) copy-start(bf16[128,512]{1,0:T(8,128)(2,1)} %wn_ref.3) | copy-start | bytes 393220
  20.1 4.5 %collective-permute-start.2 = (bf16[1552,128]{1,0:T(8,128)(2,1)S(1)}, bf16[1552,128]{1,0:T(8,128)(2,1)S(1)}, u32[]{:S(2)}, u32[]{:S(2)}) collective-permute-start(bf16[1552,128]{1,0:T(8,128)(2,1)S(1)} %get-tuple-element.54.refs_2_), channel_id=1, source_target_pairs={{0,1},{1,0},{2,3},{3,2},{4,5},{5,4},{6,7},{7,6},{8,9},{9,8},{10,11... | collective-permute-start | bytes 1191944 | tf_op jit(solution)/shard_map/ppermute | solution.py:344
  23.3 1.3 %collective-permute-start.5 = (bf16[256,128]{1,0:T(8,128)(2,1)S(1)}, bf16[256,128]{1,0:T(8,128)(2,1)S(1)}, u32[]{:S(2)}, u32[]{:S(2)}) collective-permute-start(bf16[256,128]{1,0:T(8,128)(2,1)S(1)} %shard_map.176.refs_6_), channel_id=1, source_target_pairs={{0,1},{1,0},{2,3},{3,2},{4,5},{5,4},{6,7},{7,6},{8,9},{9,8},{10,11... | collective-permute-start | bytes 196616 | tf_op jit(solution)/shard_map/ppermute | solution.py:344
  25.6 5.8 %collective-permute-start.10 = (bf16[256,128]{1,0:T(8,128)(2,1)S(1)}, bf16[256,128]{1,0:T(8,128)(2,1)S(1)}, u32[]{:S(2)}, u32[]{:S(2)}) collective-permute-start(bf16[256,128]{1,0:T(8,128)(2,1)S(1)} %get-tuple-element.70), channel_id=1, source_target_pairs={{0,12},{4,8},{8,4},{12,0},{16,28},{20,24},{24,20},{28,16},{1,13},{... | collective-permute-start | bytes 196616 | tf_op jit(solution)/shard_map/ppermute | solution.py:344
  26.4 5.0 %collective-permute-start.11 = (bf16[256,128]{1,0:T(8,128)(2,1)S(1)}, bf16[256,128]{1,0:T(8,128)(2,1)S(1)}, u32[]{:S(2)}, u32[]{:S(2)}) collective-permute-start(bf16[256,128]{1,0:T(8,128)(2,1)S(1)} %get-tuple-element.71), channel_id=1, source_target_pairs={{0,8},{4,12},{8,0},{12,4},{16,24},{20,28},{24,16},{28,20},{1,9},{5... | collective-permute-start | bytes 196616 | tf_op jit(solution)/shard_map/ppermute | solution.py:344
  27.4 4.7 %collective-permute-start.12 = (bf16[256,128]{1,0:T(8,128)(2,1)S(1)}, bf16[256,128]{1,0:T(8,128)(2,1)S(1)}, u32[]{:S(2)}, u32[]{:S(2)}) collective-permute-start(bf16[256,128]{1,0:T(8,128)(2,1)S(1)} %get-tuple-element.72), channel_id=1, source_target_pairs={{0,4},{4,0},{8,12},{12,8},{16,20},{20,16},{24,28},{28,24},{1,5},{5... | collective-permute-start | bytes 196616 | tf_op jit(solution)/shard_map/ppermute | solution.py:344
  29.2 5.1 %collective-permute-start.6 = (bf16[4,56,128]{2,1,0:T(8,128)(2,1)S(1)}, bf16[4,56,128]{2,1,0:T(8,128)(2,1)S(1)}, u32[]{:S(2)}, u32[]{:S(2)}) collective-permute-start(bf16[4,56,128]{2,1,0:T(8,128)(2,1)S(1)} %get-tuple-element.64), channel_id=1, source_target_pairs={{0,16},{4,20},{8,24},{12,28},{16,0},{20,4},{24,8},{28,12},{1,17},{... | collective-permute-start | bytes 172040 | tf_op jit(solution)/shard_map/ppermute | solution.py:344
  32.2 5.9 %collective-permute-start.13 = (bf16[256,128]{1,0:T(8,128)(2,1)S(1)}, bf16[256,128]{1,0:T(8,128)(2,1)S(1)}, u32[]{:S(2)}, u32[]{:S(2)}) collective-permute-start(bf16[256,128]{1,0:T(8,128)(2,1)S(1)} %shard_map.181.own_ref), channel_id=1, source_target_pairs={{0,16},{4,20},{8,24},{12,28},{16,0},{20,4},{24,8},{28,12},{1,17},{... | collective-permute-start | bytes 196616 | tf_op jit(solution)/shard_map/ppermute | solution.py:344
  34.3 5.0 %collective-permute-start.7 = (bf16[128,128]{1,0:T(8,128)(2,1)S(1)}, bf16[128,128]{1,0:T(8,128)(2,1)S(1)}, u32[]{:S(2)}, u32[]{:S(2)}) collective-permute-start(bf16[128,128]{1,0:T(8,128)(2,1)S(1)} %get-tuple-element.66), channel_id=1, source_target_pairs={{0,4},{4,0},{8,12},{12,8},{16,20},{20,16},{24,28},{28,24},{1,5},{5... | collective-permute-start | bytes 98312 | tf_op jit(solution)/shard_map/ppermute | solution.py:344
  35.2 6.5 %collective-permute-start.8 = (bf16[128,128]{1,0:T(8,128)(2,1)S(1)}, bf16[128,128]{1,0:T(8,128)(2,1)S(1)}, u32[]{:S(2)}, u32[]{:S(2)}) collective-permute-start(bf16[128,128]{1,0:T(8,128)(2,1)S(1)} %get-tuple-element.67), channel_id=1, source_target_pairs={{0,8},{4,12},{8,0},{12,4},{16,24},{20,28},{24,16},{28,20},{1,9},{5... | collective-permute-start | bytes 98312 | tf_op jit(solution)/shard_map/ppermute | solution.py:344
  35.7 6.0 %collective-permute-start.9 = (bf16[128,128]{1,0:T(8,128)(2,1)S(1)}, bf16[128,128]{1,0:T(8,128)(2,1)S(1)}, u32[]{:S(2)}, u32[]{:S(2)}) collective-permute-start(bf16[128,128]{1,0:T(8,128)(2,1)S(1)} %get-tuple-element.68), channel_id=1, source_target_pairs={{0,12},{4,8},{8,4},{12,0},{16,28},{20,24},{24,20},{28,16},{1,13},{... | collective-permute-start | bytes 98312 | tf_op jit(solution)/shard_map/ppermute | solution.py:344
  38.1 4.4 %collective-permute-start.16 = (bf16[256,128]{1,0:T(8,128)(2,1)S(1)}, bf16[256,128]{1,0:T(8,128)(2,1)S(1)}, u32[]{:S(2)}, u32[]{:S(2)}) collective-permute-start(bf16[256,128]{1,0:T(8,128)(2,1)S(1)} %shard_map.182.refs_0_), channel_id=1, source_target_pairs={{0,8},{4,12},{8,0},{12,4},{16,24},{20,28},{24,16},{28,20},{1,9},{5... | collective-permute-start | bytes 196616 | tf_op jit(solution)/shard_map/ppermute | solution.py:344
  38.4 4.3 %collective-permute-start.15 = (bf16[256,128]{1,0:T(8,128)(2,1)S(1)}, bf16[256,128]{1,0:T(8,128)(2,1)S(1)}, u32[]{:S(2)}, u32[]{:S(2)}) collective-permute-start(bf16[256,128]{1,0:T(8,128)(2,1)S(1)} %shard_map.182.refs_0_), channel_id=1, source_target_pairs={{0,4},{4,0},{8,12},{12,8},{16,20},{20,16},{24,28},{28,24},{1,5},{5... | collective-permute-start | bytes 196616 | tf_op jit(solution)/shard_map/ppermute | solution.py:344
  39.3 5.2 %collective-permute-start.14 = (bf16[256,128]{1,0:T(8,128)(2,1)S(1)}, bf16[256,128]{1,0:T(8,128)(2,1)S(1)}, u32[]{:S(2)}, u32[]{:S(2)}) collective-permute-start(bf16[256,128]{1,0:T(8,128)(2,1)S(1)} %shard_map.182.refs_0_), channel_id=1, source_target_pairs={{0,12},{4,8},{8,4},{12,0},{16,28},{20,24},{24,20},{28,16},{1,13},{... | collective-permute-start | bytes 196616 | tf_op jit(solution)/shard_map/ppermute | solution.py:344

commit v23 on v22

--- a/solution.py
+++ b/solution.py
@@ -286,7 +286,7 @@
 def grad_kernel(scale, slots, hub_here, side_ref, seat_ref, back_ref, mark_ref, *refs):
     got_refs, (grad_ref, bias_ref, near_ref, far_ref) = refs[:-4], refs[-4:]
     half, width = near_ref.shape[:2]
-    for j, got_ref in seated(got_refs, seat_ref[0]):
+    for j, got_ref in seated(got_refs[::-1], seat_ref[0]):
         near_ref[j] = got_ref[:width, :]
         far_ref[j] = got_ref[width:, :]
     here = side_ref[0] * half
@@ -509,7 +509,7 @@
         scratch_shapes=[pltpu.VMEM((half, width, cols), BF)] * 2,
         compiler_params=PARAMS,
         cost_estimate=pl.CostEstimate(flops=2 * 10**9, bytes_accessed=10**6, transcendentals=0),
-    )(side, seat, back, mark, *dealt)
+    )(side, seat, back, mark, *dealt[::-1])
     early = half - 1 if direct else 1
     grad_self, grad_neigh = pl.pallas_call(
         functools.partial(spread_kernel, scale),

time: 45.5 us -> 45.6 us (level)
  no operation moved by 1% of the time
where the time goes in v23:
time: 45.6 us; the launch traced here: 45.3 us
  starting transfers between devices  21.9 us (48%)
  waiting for transfers between devices  15 us (33%)
  Pallas kernels  6.99 us (15%)
  between operations  1.37 us (3%)
    ppermute x17, starting transfers between devices, partner(): lax.ppermute(block, axis, [(i, i ^ k) for i in range(lax.axis_size(axis))])  16.1 us
    ppermute x17, waiting for transfers between devices, partner(): lax.ppermute(block, axis, [(i, i ^ k) for i in range(lax.axis_size(axis))])  8.83 us
    all_to_all x1, waiting for transfers between devices, exchange(): lax.all_to_all(blocks, 'dom', split_axis=0, concat_axis=0, axis_index_gro...  6.17 us
    all_to_all x1, starting transfers between devices, exchange(): lax.all_to_all(blocks, 'dom', split_axis=0, concat_axis=0, axis_index_gro...  5.83 us
    pallas_call x1, Pallas kernels, on_device(): pl.pallas_call(functools.partial(send_kernel, width), out_shape=(shape((p...  1.96 us
    pallas_call x1, Pallas kernels, on_device(): pl.pallas_call(functools.partial(dense_kernel, slots, hub_here, feats, wi...  1.07 us
  transfers between devices with their start and end apart: 18, of which 9 were waited for; matrix products, arithmetic and copies ran while one was open for 0% of the time, Pallas kernels for 7%

profile of v23, /device:TPU:0, one launch (start us, length us, event | category | flops | bytes accessed | tf_op | source)
XLA Modules:
  0.0 45.3 jit_solution(17721150852059440119)
XLA Ops:
  0.6 2.0 %shard_map.173 = (bf16[8,56,128]{2,1,0:T(8,128)(2,1)}, bf16[1552,128]{1,0:T(8,128)(2,1)S(1)}, s32[1,8,48]{2,1,0:T(8,128)S(1)}, s32[1,2]{1,0:T(1,128)S(1)}, s32[1...) custom-call(bf16[256,128]{1,0:T(8,128)(2,1)} %x_ref.5, ...), custom_call_target="tpu_custom_call" | custom-call | tf_op jit(solution)/shard_map/pallas_call | solution.py:397
  2.6 3.0 %collective-permute-start.1 = (bf16[1552,128]{1,0:T(8,128)(2,1)S(1)}, bf16[1552,128]{1,0:T(8,128)(2,1)S(1)}, u32[]{:S(2)}, u32[]{:S(2)}) collective-permute-start(bf16[1552,128]{1,0:T(8,128)(2,1)S(1)} %get-tuple-element.51.refs_0_), channel_id=1, source_target_pairs={{0,2},{1,3},{2,0},{3,1},{4,6},{5,7},{6,4},{7,5},{8,10},{9,11},{10,... | collective-permute-start | bytes 1191944 | tf_op jit(solution)/shard_map/ppermute | solution.py:344
  5.6 5.8 %all-to-all-start = ((bf16[8,56,128]{2,1,0:T(8,128)(2,1)}), bf16[8,56,128]{2,1,0:T(8,128)(2,1)S(1)}, u32[]{:S(2)}, u32[]{:S(2)}) async-start(bf16[8,56,128]{2,1,0:T(8,128)(2,1)} %get-tuple-element.53), calls=%async_computation | async-start | bytes 229376 | tf_op jit(solution)/shard_map/all_to_all | solution.py:348
  12.1 0.4 shard_map.174
  12.5 6.2 %all-to-all-done.got_ref = bf16[8,56,128]{2,1,0:T(8,128)(2,1)S(1)} async-done(((bf16[8,56,128]{2,1,0:T(8,128)(2,1)}), bf16[8,56,128]{2,1,0:T(8,128)(2,1)S(1)}, u32[]{:S(2)}, u32[]{:S(2)}) %all-to-all-start) | async-done | bytes 114720 | tf_op jit(solution)/shard_map/all_to_all | solution.py:348
  18.7 0.3 shard_map.175
  19.0 0.6 %collective-permute-start.4 = (bf16[256,128]{1,0:T(8,128)(2,1)S(1)}, bf16[256,128]{1,0:T(8,128)(2,1)S(1)}, u32[]{:S(2)}, u32[]{:S(2)}) collective-permute-start(bf16[256,128]{1,0:T(8,128)(2,1)S(1)} %get-tuple-element.55.refs_4_), channel_id=1, source_target_pairs={{0,2},{1,3},{2,0},{3,1},{4,6},{5,7},{6,4},{7,5},{8,10},{9,11},{10,... | collective-permute-start | bytes 196616 | tf_op jit(solution)/shard_map/ppermute | solution.py:344
  19.6 0.5 %collective-permute-start.3 = (bf16[256,128]{1,0:T(8,128)(2,1)S(1)}, bf16[256,128]{1,0:T(8,128)(2,1)S(1)}, u32[]{:S(2)}, u32[]{:S(2)}) collective-permute-start(bf16[256,128]{1,0:T(8,128)(2,1)S(1)} %get-tuple-element.55.refs_4_), channel_id=1, source_target_pairs={{0,1},{1,0},{2,3},{3,2},{4,5},{5,4},{6,7},{7,6},{8,9},{9,8},{10,11... | collective-permute-start | bytes 196616 | tf_op jit(solution)/shard_map/ppermute | solution.py:344
  20.1 3.2 %collective-permute-done.4.held_ref = bf16[256,128]{1,0:T(8,128)(2,1)S(1)} collective-permute-done((bf16[256,128]{1,0:T(8,128)(2,1)S(1)}, bf16[256,128]{1,0:T(8,128)(2,1)S(1)}, u32[]{:S(2)}, u32[]{:S(2)}) %collective-permute-start.4) | collective-permute-done | bytes 65568 | tf_op jit(solution)/shard_map/ppermute | solution.py:344
  23.3 1.2 %collective-permute-done.5.refs_7_ = bf16[256,128]{1,0:T(8,128)(2,1)S(1)} collective-permute-done((bf16[256,128]{1,0:T(8,128)(2,1)S(1)}, bf16[256,128]{1,0:T(8,128)(2,1)S(1)}, u32[]{:S(2)}, u32[]{:S(2)}) %collective-permute-start.5) | collective-permute-done | bytes 65568 | tf_op jit(solution)/shard_map/ppermute | solution.py:344
  24.6 1.1 %shard_map.177 = (f32[256,128]{1,0:T(8,128)S(1)}, bf16[256,512]{1,0:T(8,128)(2,1)S(1)}, bf16[256,128]{1,0:T(8,128)(2,1)S(1)}, f32[1,128]{1,0:T(1,128)S(1)}, bf16...) custom-call(s32[1]{0:T(128)} %bitcast.2.me_ref, ...), custom_call_target="tpu_custom_call" | custom-call | tf_op jit(solution)/shard_map/pallas_call | solution.py:451
  25.6 0.8 %collective-permute-start.10 = (bf16[256,128]{1,0:T(8,128)(2,1)S(1)}, bf16[256,128]{1,0:T(8,128)(2,1)S(1)}, u32[]{:S(2)}, u32[]{:S(2)}) collective-permute-start(bf16[256,128]{1,0:T(8,128)(2,1)S(1)} %get-tuple-element.70), channel_id=1, source_target_pairs={{0,12},{4,8},{8,4},{12,0},{16,28},{20,24},{24,20},{28,16},{1,13},{... | collective-permute-start | bytes 196616 | tf_op jit(solution)/shard_map/ppermute | solution.py:344
  26.4 1.0 %collective-permute-start.11 = (bf16[256,128]{1,0:T(8,128)(2,1)S(1)}, bf16[256,128]{1,0:T(8,128)(2,1)S(1)}, u32[]{:S(2)}, u32[]{:S(2)}) collective-permute-start(bf16[256,128]{1,0:T(8,128)(2,1)S(1)} %get-tuple-element.71), channel_id=1, source_target_pairs={{0,8},{4,12},{8,0},{12,4},{16,24},{20,28},{24,16},{28,20},{1,9},{5... | collective-permute-start | bytes 196616 | tf_op jit(solution)/shard_map/ppermute | solution.py:344
  27.4 1.8 %collective-permute-start.12 = (bf16[256,128]{1,0:T(8,128)(2,1)S(1)}, bf16[256,128]{1,0:T(8,128)(2,1)S(1)}, u32[]{:S(2)}, u32[]{:S(2)}) collective-permute-start(bf16[256,128]{1,0:T(8,128)(2,1)S(1)} %get-tuple-element.72), channel_id=1, source_target_pairs={{0,4},{4,0},{8,12},{12,8},{16,20},{20,16},{24,28},{28,24},{1,5},{5... | collective-permute-start | bytes 196616 | tf_op jit(solution)/shard_map/ppermute | solution.py:344
  29.2 0.4 collective-permute-start.6
  29.6 0.9 %shard_map.178 = (bf16[256,128]{1,0:T(8,128)(2,1)}, f32[256,128]{1,0:T(8,128)S(1)}, bf16[4,64,128]{2,1,0:T(8,128)(2,1)S(1)}) custom-call(s32[1]{0:T(128)} %bitcast.side_ref, s32[1]{0:T(128)} %bitcast.1.seat_ref, f32[256,128]{1,0:T(8,128)S(1)} %get-tuple-element.56.own_ref, bf16[256,512]{1,0:T(8,128)(2,1)S(1)} %get-tuple-element.57.grad_ref, ...), custom_call_target="tpu_custom_call" | custom-call | flops 100000000 | bytes 1000000 | tf_op jit(solution)/shard_map/pallas_call | solution.py:472
  30.5 1.0 %collective-permute-done.10.refs_0_ = bf16[256,128]{1,0:T(8,128)(2,1)S(1)} collective-permute-done((bf16[256,128]{1,0:T(8,128)(2,1)S(1)}, bf16[256,128]{1,0:T(8,128)(2,1)S(1)}, u32[]{:S(2)}, u32[]{:S(2)}) %collective-permute-start.10) | collective-permute-done | bytes 65568 | tf_op jit(solution)/shard_map/ppermute | solution.py:344
  31.5 0.7 %collective-permute-done.12.refs_2_ = bf16[256,128]{1,0:T(8,128)(2,1)S(1)} collective-permute-done((bf16[256,128]{1,0:T(8,128)(2,1)S(1)}, bf16[256,128]{1,0:T(8,128)(2,1)S(1)}, u32[]{:S(2)}, u32[]{:S(2)}) %collective-permute-start.12) | collective-permute-done | bytes 65568 | tf_op jit(solution)/shard_map/ppermute | solution.py:344
  32.2 0.9 %collective-permute-start.13 = (bf16[256,128]{1,0:T(8,128)(2,1)S(1)}, bf16[256,128]{1,0:T(8,128)(2,1)S(1)}, u32[]{:S(2)}, u32[]{:S(2)}) collective-permute-start(bf16[256,128]{1,0:T(8,128)(2,1)S(1)} %shard_map.181.own_ref), channel_id=1, source_target_pairs={{0,16},{4,20},{8,24},{12,28},{16,0},{20,4},{24,8},{28,12},{1,17},{... | collective-permute-start | bytes 196616 | tf_op jit(solution)/shard_map/ppermute | solution.py:344
  33.1 1.2 %collective-permute-done.6.mirror_ref = bf16[4,56,128]{2,1,0:T(8,128)(2,1)S(1)} collective-permute-done((bf16[4,56,128]{2,1,0:T(8,128)(2,1)S(1)}, bf16[4,56,128]{2,1,0:T(8,128)(2,1)S(1)}, u32[]{:S(2)}, u32[]{:S(2)}) %collective-permute-start.6) | collective-permute-done | bytes 57376 | tf_op jit(solution)/shard_map/ppermute | solution.py:344
  34.3 0.8 %collective-permute-start.7 = (bf16[128,128]{1,0:T(8,128)(2,1)S(1)}, bf16[128,128]{1,0:T(8,128)(2,1)S(1)}, u32[]{:S(2)}, u32[]{:S(2)}) collective-permute-start(bf16[128,128]{1,0:T(8,128)(2,1)S(1)} %get-tuple-element.65), channel_id=1, source_target_pairs={{0,12},{4,8},{8,4},{12,0},{16,28},{20,24},{24,20},{28,16},{1,13},{... | collective-permute-start | bytes 98312 | tf_op jit(solution)/shard_map/ppermute | solution.py:344
  35.2 1.5 %collective-permute-start.8 = (bf16[128,128]{1,0:T(8,128)(2,1)S(1)}, bf16[128,128]{1,0:T(8,128)(2,1)S(1)}, u32[]{:S(2)}, u32[]{:S(2)}) collective-permute-start(bf16[128,128]{1,0:T(8,128)(2,1)S(1)} %get-tuple-element.66), channel_id=1, source_target_pairs={{0,8},{4,12},{8,0},{12,4},{16,24},{20,28},{24,16},{28,20},{1,9},{5... | collective-permute-start | bytes 98312 | tf_op jit(solution)/shard_map/ppermute | solution.py:344
  36.7 1.2 %collective-permute-start.9 = (bf16[128,128]{1,0:T(8,128)(2,1)S(1)}, bf16[128,128]{1,0:T(8,128)(2,1)S(1)}, u32[]{:S(2)}, u32[]{:S(2)}) collective-permute-start(bf16[128,128]{1,0:T(8,128)(2,1)S(1)} %get-tuple-element.67), channel_id=1, source_target_pairs={{0,4},{4,0},{8,12},{12,8},{16,20},{20,16},{24,28},{28,24},{1,5},{5... | collective-permute-start | bytes 98312 | tf_op jit(solution)/shard_map/ppermute | solution.py:344
  37.9 0.2 collective-permute-done.13.other_ref
  38.1 0.6 %collective-permute-start.16 = (bf16[256,128]{1,0:T(8,128)(2,1)S(1)}, bf16[256,128]{1,0:T(8,128)(2,1)S(1)}, u32[]{:S(2)}, u32[]{:S(2)}) collective-permute-start(bf16[256,128]{1,0:T(8,128)(2,1)S(1)} %shard_map.182.refs_0_), channel_id=1, source_target_pairs={{0,8},{4,12},{8,0},{12,4},{16,24},{20,28},{24,16},{28,20},{1,9},{5... | collective-permute-start | bytes 196616 | tf_op jit(solution)/shard_map/ppermute | solution.py:344
  38.8 0.7 %collective-permute-start.15 = (bf16[256,128]{1,0:T(8,128)(2,1)S(1)}, bf16[256,128]{1,0:T(8,128)(2,1)S(1)}, u32[]{:S(2)}, u32[]{:S(2)}) collective-permute-start(bf16[256,128]{1,0:T(8,128)(2,1)S(1)} %shard_map.182.refs_0_), channel_id=1, source_target_pairs={{0,4},{4,0},{8,12},{12,8},{16,20},{20,16},{24,28},{28,24},{1,5},{5... | collective-permute-start | bytes 196616 | tf_op jit(solution)/shard_map/ppermute | solution.py:344
  39.5 2.2 %collective-permute-start.14 = (bf16[256,128]{1,0:T(8,128)(2,1)S(1)}, bf16[256,128]{1,0:T(8,128)(2,1)S(1)}, u32[]{:S(2)}, u32[]{:S(2)}) collective-permute-start(bf16[256,128]{1,0:T(8,128)(2,1)S(1)} %shard_map.182.refs_0_), channel_id=1, source_target_pairs={{0,12},{4,8},{8,4},{12,0},{16,28},{20,24},{24,20},{28,16},{1,13},{... | collective-permute-start | bytes 196616 | tf_op jit(solution)/shard_map/ppermute | solution.py:344
  41.7 0.9 %shard_map.180 = (bf16[256,128]{1,0:T(8,128)(2,1)}, f32[1,128]{1,0:T(1,128)}) custom-call(s32[1]{0:T(128)} %bitcast.side_ref, s32[1]{0:T(128)} %bitcast.1.seat_ref, f32[256,128]{1,0:T(8,128)S(1)} %get-tuple-element.61.back_ref, bf16[256,512]{1,0:T(8,128)(2,1)S(1)} %get-tuple-element.62.mark_ref, bf16[128,128]{1,0:T(8,128)(2,1)S(1)} %collective-permute-done.7.refs_0_, ...), custom_call_target="tpu_custom_call" | custom-call | flops 2000000000 | bytes 1000000 | tf_op jit(solution)/shard_map/pallas_call | solution.py:504
  42.6 0.5 %collective-permute-done.15.refs_1_ = bf16[256,128]{1,0:T(8,128)(2,1)S(1)} collective-permute-done((bf16[256,128]{1,0:T(8,128)(2,1)S(1)}, bf16[256,128]{1,0:T(8,128)(2,1)S(1)}, u32[]{:S(2)}, u32[]{:S(2)}) %collective-permute-start.15) | collective-permute-done | bytes 65568 | tf_op jit(solution)/shard_map/ppermute | solution.py:344
  43.0 0.8 %shard_map.183 = (f32[128,512]{1,0:T(8,128)}, f32[128,512]{1,0:T(8,128)}) custom-call(s32[1]{0:T(128)} %bitcast.1.seat_ref, bf16[256,128]{1,0:T(8,128)(2,1)S(1)} %shard_map.182.refs_0_, bf16[256,128]{1,0:T(8,128)(2,1)S(1)} %collective-permute-done.15.refs_1_, bf16[256,128]{1,0:T(8,128)(2,1)S(1)} %collective-permute-done.16.refs_2_), custom_call_target="tpu_custom_call" | custom-call | tf_op jit(solution)/shard_map/pallas_call | solution.py:514
  43.9 0.8 %collective-permute-done.14.got_ref = bf16[256,128]{1,0:T(8,128)(2,1)S(1)} collective-permute-done((bf16[256,128]{1,0:T(8,128)(2,1)S(1)}, bf16[256,128]{1,0:T(8,128)(2,1)S(1)}, u32[]{:S(2)}, u32[]{:S(2)}) %collective-permute-start.14) | collective-permute-done | bytes 65568 | tf_op jit(solution)/shard_map/ppermute | solution.py:344
  44.6 0.7 %shard_map.184 = (f32[128,512]{1,0:T(8,128)}, f32[128,512]{1,0:T(8,128)}) custom-call(s32[1]{0:T(128)} %bitcast.1.seat_ref, bf16[256,128]{1,0:T(8,128)(2,1)S(1)} %collective-permute-done.14.got_ref, f32[128,512]{1,0:T(8,128)} %get-tuple-element.74.begun_self_ref, ...), custom_call_target="tpu_custom_call", output_to_operand_aliasing={{0}: (2, {}), {1}: (3, {})} | custom-call | tf_op jit(solution)/shard_map/pallas_call | solution.py:523
  (22 shorter events, 0.1 us)
Async XLA Ops:
  2.6 16.1 %collective-permute-start.1 = (bf16[1552,128]{1,0:T(8,128)(2,1)S(1)}, bf16[1552,128]{1,0:T(8,128)(2,1)S(1)}, u32[]{:S(2)}, u32[]{:S(2)}) collective-permute-start(bf16[1552,128]{1,0:T(8,128)(2,1)S(1)} %get-tuple-element.51.refs_0_), channel_id=1, source_target_pairs={{0,2},{1,3},{2,0},{3,1},{4,6},{5,7},{6,4},{7,5},{8,10},{9,11},{10,... | collective-permute-start | bytes 1191944 | tf_op jit(solution)/shard_map/ppermute | solution.py:344
  5.6 13.1 %all-to-all-start = ((bf16[8,56,128]{2,1,0:T(8,128)(2,1)}), bf16[8,56,128]{2,1,0:T(8,128)(2,1)S(1)}, u32[]{:S(2)}, u32[]{:S(2)}) async-start(bf16[8,56,128]{2,1,0:T(8,128)(2,1)} %get-tuple-element.53), calls=%async_computation | async-start | bytes 229376 | tf_op jit(solution)/shard_map/all_to_all | solution.py:348
  12.1 6.6 %copy-start.1 = (bf16[256,128]{1,0:T(8,128)(2,1)S(1)}, bf16[256,128]{1,0:T(8,128)(2,1)}, u32[]{:S(2)}) copy-start(bf16[256,128]{1,0:T(8,128)(2,1)} %x_ref.5) | copy-start | bytes 196612
  19.0 4.3 %collective-permute-start.4 = (bf16[256,128]{1,0:T(8,128)(2,1)S(1)}, bf16[256,128]{1,0:T(8,128)(2,1)S(1)}, u32[]{:S(2)}, u32[]{:S(2)}) collective-permute-start(bf16[256,128]{1,0:T(8,128)(2,1)S(1)} %get-tuple-element.55.refs_4_), channel_id=1, source_target_pairs={{0,2},{1,3},{2,0},{3,1},{4,6},{5,7},{6,4},{7,5},{8,10},{9,11},{10,... | collective-permute-start | bytes 196616 | tf_op jit(solution)/shard_map/ppermute | solution.py:344
  19.6 3.7 %collective-permute-start = (bf16[1552,128]{1,0:T(8,128)(2,1)S(1)}, bf16[1552,128]{1,0:T(8,128)(2,1)S(1)}, u32[]{:S(2)}, u32[]{:S(2)}) collective-permute-start(bf16[1552,128]{1,0:T(8,128)(2,1)S(1)} %get-tuple-element.51.refs_0_), channel_id=1, source_target_pairs={{0,1},{1,0},{2,3},{3,2},{4,5},{5,4},{6,7},{7,6},{8,9},{9,8},{10,11... | collective-permute-start | bytes 1191944 | tf_op jit(solution)/shard_map/ppermute | solution.py:344
  19.6 3.7 %collective-permute-start.3 = (bf16[256,128]{1,0:T(8,128)(2,1)S(1)}, bf16[256,128]{1,0:T(8,128)(2,1)S(1)}, u32[]{:S(2)}, u32[]{:S(2)}) collective-permute-start(bf16[256,128]{1,0:T(8,128)(2,1)S(1)} %get-tuple-element.55.refs_4_), channel_id=1, source_target_pairs={{0,1},{1,0},{2,3},{3,2},{4,5},{5,4},{6,7},{7,6},{8,9},{9,8},{10,11... | collective-permute-start | bytes 196616 | tf_op jit(solution)/shard_map/ppermute | solution.py:344
  20.1 4.5 %copy-start = (bf16[128,512]{1,0:T(8,128)(2,1)S(1)}, bf16[128,512]{1,0:T(8,128)(2,1)}, u32[]{:S(2)}) copy-start(bf16[128,512]{1,0:T(8,128)(2,1)} %ws_ref.5) | copy-start | bytes 393220
  20.1 4.5 %copy-start.2 = (bf16[128,512]{1,0:T(8,128)(2,1)S(1)}, bf16[128,512]{1,0:T(8,128)(2,1)}, u32[]{:S(2)}) copy-start(bf16[128,512]{1,0:T(8,128)(2,1)} %wn_ref.3) | copy-start | bytes 393220
  20.1 4.5 %collective-permute-start.2 = (bf16[1552,128]{1,0:T(8,128)(2,1)S(1)}, bf16[1552,128]{1,0:T(8,128)(2,1)S(1)}, u32[]{:S(2)}, u32[]{:S(2)}) collective-permute-start(bf16[1552,128]{1,0:T(8,128)(2,1)S(1)} %get-tuple-element.54.refs_2_), channel_id=1, source_target_pairs={{0,1},{1,0},{2,3},{3,2},{4,5},{5,4},{6,7},{7,6},{8,9},{9,8},{10,11... | collective-permute-start | bytes 1191944 | tf_op jit(solution)/shard_map/ppermute | solution.py:344
  23.3 1.3 %collective-permute-start.5 = (bf16[256,128]{1,0:T(8,128)(2,1)S(1)}, bf16[256,128]{1,0:T(8,128)(2,1)S(1)}, u32[]{:S(2)}, u32[]{:S(2)}) collective-permute-start(bf16[256,128]{1,0:T(8,128)(2,1)S(1)} %shard_map.176.refs_6_), channel_id=1, source_target_pairs={{0,1},{1,0},{2,3},{3,2},{4,5},{5,4},{6,7},{7,6},{8,9},{9,8},{10,11... | collective-permute-start | bytes 196616 | tf_op jit(solution)/shard_map/ppermute | solution.py:344
  25.6 5.8 %collective-permute-start.10 = (bf16[256,128]{1,0:T(8,128)(2,1)S(1)}, bf16[256,128]{1,0:T(8,128)(2,1)S(1)}, u32[]{:S(2)}, u32[]{:S(2)}) collective-permute-start(bf16[256,128]{1,0:T(8,128)(2,1)S(1)} %get-tuple-element.70), channel_id=1, source_target_pairs={{0,12},{4,8},{8,4},{12,0},{16,28},{20,24},{24,20},{28,16},{1,13},{... | collective-permute-start | bytes 196616 | tf_op jit(solution)/shard_map/ppermute | solution.py:344
  26.4 5.0 %collective-permute-start.11 = (bf16[256,128]{1,0:T(8,128)(2,1)S(1)}, bf16[256,128]{1,0:T(8,128)(2,1)S(1)}, u32[]{:S(2)}, u32[]{:S(2)}) collective-permute-start(bf16[256,128]{1,0:T(8,128)(2,1)S(1)} %get-tuple-element.71), channel_id=1, source_target_pairs={{0,8},{4,12},{8,0},{12,4},{16,24},{20,28},{24,16},{28,20},{1,9},{5... | collective-permute-start | bytes 196616 | tf_op jit(solution)/shard_map/ppermute | solution.py:344
  27.4 4.7 %collective-permute-start.12 = (bf16[256,128]{1,0:T(8,128)(2,1)S(1)}, bf16[256,128]{1,0:T(8,128)(2,1)S(1)}, u32[]{:S(2)}, u32[]{:S(2)}) collective-permute-start(bf16[256,128]{1,0:T(8,128)(2,1)S(1)} %get-tuple-element.72), channel_id=1, source_target_pairs={{0,4},{4,0},{8,12},{12,8},{16,20},{20,16},{24,28},{28,24},{1,5},{5... | collective-permute-start | bytes 196616 | tf_op jit(solution)/shard_map/ppermute | solution.py:344
  29.2 5.1 %collective-permute-start.6 = (bf16[4,56,128]{2,1,0:T(8,128)(2,1)S(1)}, bf16[4,56,128]{2,1,0:T(8,128)(2,1)S(1)}, u32[]{:S(2)}, u32[]{:S(2)}) collective-permute-start(bf16[4,56,128]{2,1,0:T(8,128)(2,1)S(1)} %get-tuple-element.64), channel_id=1, source_target_pairs={{0,16},{4,20},{8,24},{12,28},{16,0},{20,4},{24,8},{28,12},{1,17},{... | collective-permute-start | bytes 172040 | tf_op jit(solution)/shard_map/ppermute | solution.py:344
  32.2 5.9 %collective-permute-start.13 = (bf16[256,128]{1,0:T(8,128)(2,1)S(1)}, bf16[256,128]{1,0:T(8,128)(2,1)S(1)}, u32[]{:S(2)}, u32[]{:S(2)}) collective-permute-start(bf16[256,128]{1,0:T(8,128)(2,1)S(1)} %shard_map.181.own_ref), channel_id=1, source_target_pairs={{0,16},{4,20},{8,24},{12,28},{16,0},{20,4},{24,8},{28,12},{1,17},{... | collective-permute-start | bytes 196616 | tf_op jit(solution)/shard_map/ppermute | solution.py:344
  34.3 5.1 %collective-permute-start.7 = (bf16[128,128]{1,0:T(8,128)(2,1)S(1)}, bf16[128,128]{1,0:T(8,128)(2,1)S(1)}, u32[]{:S(2)}, u32[]{:S(2)}) collective-permute-start(bf16[128,128]{1,0:T(8,128)(2,1)S(1)} %get-tuple-element.65), channel_id=1, source_target_pairs={{0,12},{4,8},{8,4},{12,0},{16,28},{20,24},{24,20},{28,16},{1,13},{... | collective-permute-start | bytes 98312 | tf_op jit(solution)/shard_map/ppermute | solution.py:344
  35.2 6.5 %collective-permute-start.8 = (bf16[128,128]{1,0:T(8,128)(2,1)S(1)}, bf16[128,128]{1,0:T(8,128)(2,1)S(1)}, u32[]{:S(2)}, u32[]{:S(2)}) collective-permute-start(bf16[128,128]{1,0:T(8,128)(2,1)S(1)} %get-tuple-element.66), channel_id=1, source_target_pairs={{0,8},{4,12},{8,0},{12,4},{16,24},{20,28},{24,16},{28,20},{1,9},{5... | collective-permute-start | bytes 98312 | tf_op jit(solution)/shard_map/ppermute | solution.py:344
  36.7 5.0 %collective-permute-start.9 = (bf16[128,128]{1,0:T(8,128)(2,1)S(1)}, bf16[128,128]{1,0:T(8,128)(2,1)S(1)}, u32[]{:S(2)}, u32[]{:S(2)}) collective-permute-start(bf16[128,128]{1,0:T(8,128)(2,1)S(1)} %get-tuple-element.67), channel_id=1, source_target_pairs={{0,4},{4,0},{8,12},{12,8},{16,20},{20,16},{24,28},{28,24},{1,5},{5... | collective-permute-start | bytes 98312 | tf_op jit(solution)/shard_map/ppermute | solution.py:344
  38.1 4.4 %collective-permute-start.16 = (bf16[256,128]{1,0:T(8,128)(2,1)S(1)}, bf16[256,128]{1,0:T(8,128)(2,1)S(1)}, u32[]{:S(2)}, u32[]{:S(2)}) collective-permute-start(bf16[256,128]{1,0:T(8,128)(2,1)S(1)} %shard_map.182.refs_0_), channel_id=1, source_target_pairs={{0,8},{4,12},{8,0},{12,4},{16,24},{20,28},{24,16},{28,20},{1,9},{5... | collective-permute-start | bytes 196616 | tf_op jit(solution)/shard_map/ppermute | solution.py:344
  38.8 4.3 %collective-permute-start.15 = (bf16[256,128]{1,0:T(8,128)(2,1)S(1)}, bf16[256,128]{1,0:T(8,128)(2,1)S(1)}, u32[]{:S(2)}, u32[]{:S(2)}) collective-permute-start(bf16[256,128]{1,0:T(8,128)(2,1)S(1)} %shard_map.182.refs_0_), channel_id=1, source_target_pairs={{0,4},{4,0},{8,12},{12,8},{16,20},{20,16},{24,28},{28,24},{1,5},{5... | collective-permute-start | bytes 196616 | tf_op jit(solution)/shard_map/ppermute | solution.py:344
  39.5 5.2 %collective-permute-start.14 = (bf16[256,128]{1,0:T(8,128)(2,1)S(1)}, bf16[256,128]{1,0:T(8,128)(2,1)S(1)}, u32[]{:S(2)}, u32[]{:S(2)}) collective-permute-start(bf16[256,128]{1,0:T(8,128)(2,1)S(1)} %shard_map.182.refs_0_), channel_id=1, source_target_pairs={{0,12},{4,8},{8,4},{12,0},{16,28},{20,24},{24,20},{28,16},{1,13},{... | collective-permute-start | bytes 196616 | tf_op jit(solution)/shard_map/ppermute | solution.py:344

commit v24 on v22

--- a/solution.py
+++ b/solution.py
@@ -318,7 +318,7 @@
     depth, full = self_ref.shape
     cols = wide_ref.shape[-1]
     if len(got_refs) > 1:
-        parts = [(j, ref[...]) for j, ref in seated(got_refs, seat_ref[0])]
+        parts = [(j, ref[...]) for j, ref in seated(got_refs[::-1], seat_ref[0])]
     else:
         whole = got_refs[0][...].reshape(2 * full // cols * depth, cols)
         parts = [(j, whole[2 * j * depth : 2 * (j + 1) * depth]) for j in range(full // cols)]
@@ -518,7 +518,7 @@
         out_specs=(HBM,) * 2,
         scratch_shapes=[pltpu.VMEM((blocks, 2 * depth, cols), F32), pltpu.SemaphoreType.DMA((2 * blocks,))],
         compiler_params=PARAMS,
-    )(seat, *parts[:early])
+    )(seat, *parts[:early][::-1])
     if direct:
         grad_self, grad_neigh = pl.pallas_call(
             functools.partial(finish_kernel, scale, early),

time: 45.5 us -> 45.6 us (level)
  no operation moved by 1% of the time
where the time goes in v24:
time: 45.6 us; the launch traced here: 45.3 us
  starting transfers between devices  21.9 us (48%)
  waiting for transfers between devices  15 us (33%)
  Pallas kernels  6.99 us (15%)
  between operations  1.37 us (3%)
    ppermute x17, starting transfers between devices, partner(): lax.ppermute(block, axis, [(i, i ^ k) for i in range(lax.axis_size(axis))])  16.1 us
    ppermute x17, waiting for transfers between devices, partner(): lax.ppermute(block, axis, [(i, i ^ k) for i in range(lax.axis_size(axis))])  8.83 us
    all_to_all x1, waiting for transfers between devices, exchange(): lax.all_to_all(blocks, 'dom', split_axis=0, concat_axis=0, axis_index_gro...  6.17 us
    all_to_all x1, starting transfers between devices, exchange(): lax.all_to_all(blocks, 'dom', split_axis=0, concat_axis=0, axis_index_gro...  5.83 us
    pallas_call x1, Pallas kernels, on_device(): pl.pallas_call(functools.partial(send_kernel, width), out_shape=(shape((p...  1.96 us
    pallas_call x1, Pallas kernels, on_device(): pl.pallas_call(functools.partial(dense_kernel, slots, hub_here, feats, wi...  1.07 us
  transfers between devices with their start and end apart: 18, of which 9 were waited for; matrix products, arithmetic and copies ran while one was open for 0% of the time, Pallas kernels for 7%

profile of v24, /device:TPU:0, one launch (start us, length us, event | category | flops | bytes accessed | tf_op | source)
XLA Modules:
  0.0 45.3 jit_solution(8769033048694599359)
XLA Ops:
  0.6 2.0 %shard_map.173 = (bf16[8,56,128]{2,1,0:T(8,128)(2,1)}, bf16[1552,128]{1,0:T(8,128)(2,1)S(1)}, s32[1,8,48]{2,1,0:T(8,128)S(1)}, s32[1,2]{1,0:T(1,128)S(1)}, s32[1...) custom-call(bf16[256,128]{1,0:T(8,128)(2,1)} %x_ref.5, ...), custom_call_target="tpu_custom_call" | custom-call | tf_op jit(solution)/shard_map/pallas_call | solution.py:397
  2.6 3.0 %collective-permute-start.1 = (bf16[1552,128]{1,0:T(8,128)(2,1)S(1)}, bf16[1552,128]{1,0:T(8,128)(2,1)S(1)}, u32[]{:S(2)}, u32[]{:S(2)}) collective-permute-start(bf16[1552,128]{1,0:T(8,128)(2,1)S(1)} %get-tuple-element.51.refs_0_), channel_id=1, source_target_pairs={{0,2},{1,3},{2,0},{3,1},{4,6},{5,7},{6,4},{7,5},{8,10},{9,11},{10,... | collective-permute-start | bytes 1191944 | tf_op jit(solution)/shard_map/ppermute | solution.py:344
  5.6 5.8 %all-to-all-start = ((bf16[8,56,128]{2,1,0:T(8,128)(2,1)}), bf16[8,56,128]{2,1,0:T(8,128)(2,1)S(1)}, u32[]{:S(2)}, u32[]{:S(2)}) async-start(bf16[8,56,128]{2,1,0:T(8,128)(2,1)} %get-tuple-element.53), calls=%async_computation | async-start | bytes 229376 | tf_op jit(solution)/shard_map/all_to_all | solution.py:348
  12.1 0.4 shard_map.174
  12.5 6.2 %all-to-all-done.got_ref = bf16[8,56,128]{2,1,0:T(8,128)(2,1)S(1)} async-done(((bf16[8,56,128]{2,1,0:T(8,128)(2,1)}), bf16[8,56,128]{2,1,0:T(8,128)(2,1)S(1)}, u32[]{:S(2)}, u32[]{:S(2)}) %all-to-all-start) | async-done | bytes 114720 | tf_op jit(solution)/shard_map/all_to_all | solution.py:348
  18.7 0.3 shard_map.175
  19.0 0.6 %collective-permute-start.4 = (bf16[256,128]{1,0:T(8,128)(2,1)S(1)}, bf16[256,128]{1,0:T(8,128)(2,1)S(1)}, u32[]{:S(2)}, u32[]{:S(2)}) collective-permute-start(bf16[256,128]{1,0:T(8,128)(2,1)S(1)} %get-tuple-element.55.refs_4_), channel_id=1, source_target_pairs={{0,2},{1,3},{2,0},{3,1},{4,6},{5,7},{6,4},{7,5},{8,10},{9,11},{10,... | collective-permute-start | bytes 196616 | tf_op jit(solution)/shard_map/ppermute | solution.py:344
  19.6 0.5 %collective-permute-start.3 = (bf16[256,128]{1,0:T(8,128)(2,1)S(1)}, bf16[256,128]{1,0:T(8,128)(2,1)S(1)}, u32[]{:S(2)}, u32[]{:S(2)}) collective-permute-start(bf16[256,128]{1,0:T(8,128)(2,1)S(1)} %get-tuple-element.55.refs_4_), channel_id=1, source_target_pairs={{0,1},{1,0},{2,3},{3,2},{4,5},{5,4},{6,7},{7,6},{8,9},{9,8},{10,11... | collective-permute-start | bytes 196616 | tf_op jit(solution)/shard_map/ppermute | solution.py:344
  20.1 3.2 %collective-permute-done.4.held_ref = bf16[256,128]{1,0:T(8,128)(2,1)S(1)} collective-permute-done((bf16[256,128]{1,0:T(8,128)(2,1)S(1)}, bf16[256,128]{1,0:T(8,128)(2,1)S(1)}, u32[]{:S(2)}, u32[]{:S(2)}) %collective-permute-start.4) | collective-permute-done | bytes 65568 | tf_op jit(solution)/shard_map/ppermute | solution.py:344
  23.3 1.2 %collective-permute-done.5.refs_7_ = bf16[256,128]{1,0:T(8,128)(2,1)S(1)} collective-permute-done((bf16[256,128]{1,0:T(8,128)(2,1)S(1)}, bf16[256,128]{1,0:T(8,128)(2,1)S(1)}, u32[]{:S(2)}, u32[]{:S(2)}) %collective-permute-start.5) | collective-permute-done | bytes 65568 | tf_op jit(solution)/shard_map/ppermute | solution.py:344
  24.6 1.1 %shard_map.177 = (f32[256,128]{1,0:T(8,128)S(1)}, bf16[256,512]{1,0:T(8,128)(2,1)S(1)}, bf16[256,128]{1,0:T(8,128)(2,1)S(1)}, f32[1,128]{1,0:T(1,128)S(1)}, bf16...) custom-call(s32[1]{0:T(128)} %bitcast.2.me_ref, ...), custom_call_target="tpu_custom_call" | custom-call | tf_op jit(solution)/shard_map/pallas_call | solution.py:451
  25.6 0.8 %collective-permute-start.10 = (bf16[256,128]{1,0:T(8,128)(2,1)S(1)}, bf16[256,128]{1,0:T(8,128)(2,1)S(1)}, u32[]{:S(2)}, u32[]{:S(2)}) collective-permute-start(bf16[256,128]{1,0:T(8,128)(2,1)S(1)} %get-tuple-element.70), channel_id=1, source_target_pairs={{0,12},{4,8},{8,4},{12,0},{16,28},{20,24},{24,20},{28,16},{1,13},{... | collective-permute-start | bytes 196616 | tf_op jit(solution)/shard_map/ppermute | solution.py:344
  26.4 1.0 %collective-permute-start.11 = (bf16[256,128]{1,0:T(8,128)(2,1)S(1)}, bf16[256,128]{1,0:T(8,128)(2,1)S(1)}, u32[]{:S(2)}, u32[]{:S(2)}) collective-permute-start(bf16[256,128]{1,0:T(8,128)(2,1)S(1)} %get-tuple-element.71), channel_id=1, source_target_pairs={{0,8},{4,12},{8,0},{12,4},{16,24},{20,28},{24,16},{28,20},{1,9},{5... | collective-permute-start | bytes 196616 | tf_op jit(solution)/shard_map/ppermute | solution.py:344
  27.4 1.8 %collective-permute-start.12 = (bf16[256,128]{1,0:T(8,128)(2,1)S(1)}, bf16[256,128]{1,0:T(8,128)(2,1)S(1)}, u32[]{:S(2)}, u32[]{:S(2)}) collective-permute-start(bf16[256,128]{1,0:T(8,128)(2,1)S(1)} %get-tuple-element.72), channel_id=1, source_target_pairs={{0,4},{4,0},{8,12},{12,8},{16,20},{20,16},{24,28},{28,24},{1,5},{5... | collective-permute-start | bytes 196616 | tf_op jit(solution)/shard_map/ppermute | solution.py:344
  29.2 0.4 collective-permute-start.6
  29.6 0.9 %shard_map.178 = (bf16[256,128]{1,0:T(8,128)(2,1)}, f32[256,128]{1,0:T(8,128)S(1)}, bf16[4,64,128]{2,1,0:T(8,128)(2,1)S(1)}) custom-call(s32[1]{0:T(128)} %bitcast.side_ref, s32[1]{0:T(128)} %bitcast.1.seat_ref, f32[256,128]{1,0:T(8,128)S(1)} %get-tuple-element.56.own_ref, bf16[256,512]{1,0:T(8,128)(2,1)S(1)} %get-tuple-element.57.grad_ref, ...), custom_call_target="tpu_custom_call" | custom-call | flops 100000000 | bytes 1000000 | tf_op jit(solution)/shard_map/pallas_call | solution.py:472
  30.5 1.0 %collective-permute-done.10.refs_0_ = bf16[256,128]{1,0:T(8,128)(2,1)S(1)} collective-permute-done((bf16[256,128]{1,0:T(8,128)(2,1)S(1)}, bf16[256,128]{1,0:T(8,128)(2,1)S(1)}, u32[]{:S(2)}, u32[]{:S(2)}) %collective-permute-start.10) | collective-permute-done | bytes 65568 | tf_op jit(solution)/shard_map/ppermute | solution.py:344
  31.5 0.7 %collective-permute-done.12.refs_2_ = bf16[256,128]{1,0:T(8,128)(2,1)S(1)} collective-permute-done((bf16[256,128]{1,0:T(8,128)(2,1)S(1)}, bf16[256,128]{1,0:T(8,128)(2,1)S(1)}, u32[]{:S(2)}, u32[]{:S(2)}) %collective-permute-start.12) | collective-permute-done | bytes 65568 | tf_op jit(solution)/shard_map/ppermute | solution.py:344
  32.2 0.9 %collective-permute-start.13 = (bf16[256,128]{1,0:T(8,128)(2,1)S(1)}, bf16[256,128]{1,0:T(8,128)(2,1)S(1)}, u32[]{:S(2)}, u32[]{:S(2)}) collective-permute-start(bf16[256,128]{1,0:T(8,128)(2,1)S(1)} %shard_map.181.own_ref), channel_id=1, source_target_pairs={{0,16},{4,20},{8,24},{12,28},{16,0},{20,4},{24,8},{28,12},{1,17},{... | collective-permute-start | bytes 196616 | tf_op jit(solution)/shard_map/ppermute | solution.py:344
  33.1 1.2 %collective-permute-done.6.mirror_ref = bf16[4,56,128]{2,1,0:T(8,128)(2,1)S(1)} collective-permute-done((bf16[4,56,128]{2,1,0:T(8,128)(2,1)S(1)}, bf16[4,56,128]{2,1,0:T(8,128)(2,1)S(1)}, u32[]{:S(2)}, u32[]{:S(2)}) %collective-permute-start.6) | collective-permute-done | bytes 57376 | tf_op jit(solution)/shard_map/ppermute | solution.py:344
  34.3 0.9 %collective-permute-start.7 = (bf16[128,128]{1,0:T(8,128)(2,1)S(1)}, bf16[128,128]{1,0:T(8,128)(2,1)S(1)}, u32[]{:S(2)}, u32[]{:S(2)}) collective-permute-start(bf16[128,128]{1,0:T(8,128)(2,1)S(1)} %get-tuple-element.66), channel_id=1, source_target_pairs={{0,4},{4,0},{8,12},{12,8},{16,20},{20,16},{24,28},{28,24},{1,5},{5... | collective-permute-start | bytes 98312 | tf_op jit(solution)/shard_map/ppermute | solution.py:344
  35.2 0.5 %collective-permute-start.8 = (bf16[128,128]{1,0:T(8,128)(2,1)S(1)}, bf16[128,128]{1,0:T(8,128)(2,1)S(1)}, u32[]{:S(2)}, u32[]{:S(2)}) collective-permute-start(bf16[128,128]{1,0:T(8,128)(2,1)S(1)} %get-tuple-element.67), channel_id=1, source_target_pairs={{0,8},{4,12},{8,0},{12,4},{16,24},{20,28},{24,16},{28,20},{1,9},{5... | collective-permute-start | bytes 98312 | tf_op jit(solution)/shard_map/ppermute | solution.py:344
  35.7 2.1 %collective-permute-start.9 = (bf16[128,128]{1,0:T(8,128)(2,1)S(1)}, bf16[128,128]{1,0:T(8,128)(2,1)S(1)}, u32[]{:S(2)}, u32[]{:S(2)}) collective-permute-start(bf16[128,128]{1,0:T(8,128)(2,1)S(1)} %get-tuple-element.68), channel_id=1, source_target_pairs={{0,12},{4,8},{8,4},{12,0},{16,28},{20,24},{24,20},{28,16},{1,13},{... | collective-permute-start | bytes 98312 | tf_op jit(solution)/shard_map/ppermute | solution.py:344
  37.9 0.2 collective-permute-done.13.other_ref
  38.1 1.0 %collective-permute-start.16 = (bf16[256,128]{1,0:T(8,128)(2,1)S(1)}, bf16[256,128]{1,0:T(8,128)(2,1)S(1)}, u32[]{:S(2)}, u32[]{:S(2)}) collective-permute-start(bf16[256,128]{1,0:T(8,128)(2,1)S(1)} %shard_map.182.refs_2_), channel_id=1, source_target_pairs={{0,4},{4,0},{8,12},{12,8},{16,20},{20,16},{24,28},{28,24},{1,5},{5... | collective-permute-start | bytes 196616 | tf_op jit(solution)/shard_map/ppermute | solution.py:344
  39.2 0.2 collective-permute-start.15
  39.3 2.4 %collective-permute-start.14 = (bf16[256,128]{1,0:T(8,128)(2,1)S(1)}, bf16[256,128]{1,0:T(8,128)(2,1)S(1)}, u32[]{:S(2)}, u32[]{:S(2)}) collective-permute-start(bf16[256,128]{1,0:T(8,128)(2,1)S(1)} %shard_map.182.refs_2_), channel_id=1, source_target_pairs={{0,12},{4,8},{8,4},{12,0},{16,28},{20,24},{24,20},{28,16},{1,13},{... | collective-permute-start | bytes 196616 | tf_op jit(solution)/shard_map/ppermute | solution.py:344
  41.7 0.9 %shard_map.180 = (bf16[256,128]{1,0:T(8,128)(2,1)}, f32[1,128]{1,0:T(1,128)}) custom-call(s32[1]{0:T(128)} %bitcast.side_ref, s32[1]{0:T(128)} %bitcast.1.seat_ref, f32[256,128]{1,0:T(8,128)S(1)} %get-tuple-element.61.back_ref, bf16[256,512]{1,0:T(8,128)(2,1)S(1)} %get-tuple-element.62.mark_ref, bf16[128,128]{1,0:T(8,128)(2,1)S(1)} %get-tuple-element.65.refs_0_, ...), custom_call_target="tpu_custom_call" | custom-call | flops 2000000000 | bytes 1000000 | tf_op jit(solution)/shard_map/pallas_call | solution.py:504
  42.6 0.9 %collective-permute-done.15.refs_0_ = bf16[256,128]{1,0:T(8,128)(2,1)S(1)} collective-permute-done((bf16[256,128]{1,0:T(8,128)(2,1)S(1)}, bf16[256,128]{1,0:T(8,128)(2,1)S(1)}, u32[]{:S(2)}, u32[]{:S(2)}) %collective-permute-start.15) | collective-permute-done | bytes 65568 | tf_op jit(solution)/shard_map/ppermute | solution.py:344
  43.4 0.8 %shard_map.183 = (f32[128,512]{1,0:T(8,128)}, f32[128,512]{1,0:T(8,128)}) custom-call(s32[1]{0:T(128)} %bitcast.1.seat_ref, bf16[256,128]{1,0:T(8,128)(2,1)S(1)} %collective-permute-done.15.refs_0_, bf16[256,128]{1,0:T(8,128)(2,1)S(1)} %collective-permute-done.16.refs_1_, bf16[256,128]{1,0:T(8,128)(2,1)S(1)} %shard_map.182.refs_2_), custom_call_target="tpu_custom_call" | custom-call | tf_op jit(solution)/shard_map/pallas_call | solution.py:514
  44.3 0.4 collective-permute-done.14.got_ref
  44.6 0.7 %shard_map.184 = (f32[128,512]{1,0:T(8,128)}, f32[128,512]{1,0:T(8,128)}) custom-call(s32[1]{0:T(128)} %bitcast.1.seat_ref, bf16[256,128]{1,0:T(8,128)(2,1)S(1)} %collective-permute-done.14.got_ref, f32[128,512]{1,0:T(8,128)} %get-tuple-element.74.begun_self_ref, ...), custom_call_target="tpu_custom_call", output_to_operand_aliasing={{0}: (2, {}), {1}: (3, {})} | custom-call | tf_op jit(solution)/shard_map/pallas_call | solution.py:523
  (22 shorter events, 0.1 us)
Async XLA Ops:
  2.6 16.1 %collective-permute-start.1 = (bf16[1552,128]{1,0:T(8,128)(2,1)S(1)}, bf16[1552,128]{1,0:T(8,128)(2,1)S(1)}, u32[]{:S(2)}, u32[]{:S(2)}) collective-permute-start(bf16[1552,128]{1,0:T(8,128)(2,1)S(1)} %get-tuple-element.51.refs_0_), channel_id=1, source_target_pairs={{0,2},{1,3},{2,0},{3,1},{4,6},{5,7},{6,4},{7,5},{8,10},{9,11},{10,... | collective-permute-start | bytes 1191944 | tf_op jit(solution)/shard_map/ppermute | solution.py:344
  5.6 13.1 %all-to-all-start = ((bf16[8,56,128]{2,1,0:T(8,128)(2,1)}), bf16[8,56,128]{2,1,0:T(8,128)(2,1)S(1)}, u32[]{:S(2)}, u32[]{:S(2)}) async-start(bf16[8,56,128]{2,1,0:T(8,128)(2,1)} %get-tuple-element.53), calls=%async_computation | async-start | bytes 229376 | tf_op jit(solution)/shard_map/all_to_all | solution.py:348
  12.1 6.6 %copy-start.1 = (bf16[256,128]{1,0:T(8,128)(2,1)S(1)}, bf16[256,128]{1,0:T(8,128)(2,1)}, u32[]{:S(2)}) copy-start(bf16[256,128]{1,0:T(8,128)(2,1)} %x_ref.5) | copy-start | bytes 196612
  19.0 4.3 %collective-permute-start.4 = (bf16[256,128]{1,0:T(8,128)(2,1)S(1)}, bf16[256,128]{1,0:T(8,128)(2,1)S(1)}, u32[]{:S(2)}, u32[]{:S(2)}) collective-permute-start(bf16[256,128]{1,0:T(8,128)(2,1)S(1)} %get-tuple-element.55.refs_4_), channel_id=1, source_target_pairs={{0,2},{1,3},{2,0},{3,1},{4,6},{5,7},{6,4},{7,5},{8,10},{9,11},{10,... | collective-permute-start | bytes 196616 | tf_op jit(solution)/shard_map/ppermute | solution.py:344
  19.6 3.7 %collective-permute-start = (bf16[1552,128]{1,0:T(8,128)(2,1)S(1)}, bf16[1552,128]{1,0:T(8,128)(2,1)S(1)}, u32[]{:S(2)}, u32[]{:S(2)}) collective-permute-start(bf16[1552,128]{1,0:T(8,128)(2,1)S(1)} %get-tuple-element.51.refs_0_), channel_id=1, source_target_pairs={{0,1},{1,0},{2,3},{3,2},{4,5},{5,4},{6,7},{7,6},{8,9},{9,8},{10,11... | collective-permute-start | bytes 1191944 | tf_op jit(solution)/shard_map/ppermute | solution.py:344
  19.6 3.7 %collective-permute-start.3 = (bf16[256,128]{1,0:T(8,128)(2,1)S(1)}, bf16[256,128]{1,0:T(8,128)(2,1)S(1)}, u32[]{:S(2)}, u32[]{:S(2)}) collective-permute-start(bf16[256,128]{1,0:T(8,128)(2,1)S(1)} %get-tuple-element.55.refs_4_), channel_id=1, source_target_pairs={{0,1},{1,0},{2,3},{3,2},{4,5},{5,4},{6,7},{7,6},{8,9},{9,8},{10,11... | collective-permute-start | bytes 196616 | tf_op jit(solution)/shard_map/ppermute | solution.py:344
  20.1 4.5 %copy-start = (bf16[128,512]{1,0:T(8,128)(2,1)S(1)}, bf16[128,512]{1,0:T(8,128)(2,1)}, u32[]{:S(2)}) copy-start(bf16[128,512]{1,0:T(8,128)(2,1)} %ws_ref.5) | copy-start | bytes 393220
  20.1 4.5 %copy-start.2 = (bf16[128,512]{1,0:T(8,128)(2,1)S(1)}, bf16[128,512]{1,0:T(8,128)(2,1)}, u32[]{:S(2)}) copy-start(bf16[128,512]{1,0:T(8,128)(2,1)} %wn_ref.3) | copy-start | bytes 393220
  20.1 4.5 %collective-permute-start.2 = (bf16[1552,128]{1,0:T(8,128)(2,1)S(1)}, bf16[1552,128]{1,0:T(8,128)(2,1)S(1)}, u32[]{:S(2)}, u32[]{:S(2)}) collective-permute-start(bf16[1552,128]{1,0:T(8,128)(2,1)S(1)} %get-tuple-element.54.refs_2_), channel_id=1, source_target_pairs={{0,1},{1,0},{2,3},{3,2},{4,5},{5,4},{6,7},{7,6},{8,9},{9,8},{10,11... | collective-permute-start | bytes 1191944 | tf_op jit(solution)/shard_map/ppermute | solution.py:344
  23.3 1.3 %collective-permute-start.5 = (bf16[256,128]{1,0:T(8,128)(2,1)S(1)}, bf16[256,128]{1,0:T(8,128)(2,1)S(1)}, u32[]{:S(2)}, u32[]{:S(2)}) collective-permute-start(bf16[256,128]{1,0:T(8,128)(2,1)S(1)} %shard_map.176.refs_6_), channel_id=1, source_target_pairs={{0,1},{1,0},{2,3},{3,2},{4,5},{5,4},{6,7},{7,6},{8,9},{9,8},{10,11... | collective-permute-start | bytes 196616 | tf_op jit(solution)/shard_map/ppermute | solution.py:344
  25.6 5.8 %collective-permute-start.10 = (bf16[256,128]{1,0:T(8,128)(2,1)S(1)}, bf16[256,128]{1,0:T(8,128)(2,1)S(1)}, u32[]{:S(2)}, u32[]{:S(2)}) collective-permute-start(bf16[256,128]{1,0:T(8,128)(2,1)S(1)} %get-tuple-element.70), channel_id=1, source_target_pairs={{0,12},{4,8},{8,4},{12,0},{16,28},{20,24},{24,20},{28,16},{1,13},{... | collective-permute-start | bytes 196616 | tf_op jit(solution)/shard_map/ppermute | solution.py:344
  26.4 5.0 %collective-permute-start.11 = (bf16[256,128]{1,0:T(8,128)(2,1)S(1)}, bf16[256,128]{1,0:T(8,128)(2,1)S(1)}, u32[]{:S(2)}, u32[]{:S(2)}) collective-permute-start(bf16[256,128]{1,0:T(8,128)(2,1)S(1)} %get-tuple-element.71), channel_id=1, source_target_pairs={{0,8},{4,12},{8,0},{12,4},{16,24},{20,28},{24,16},{28,20},{1,9},{5... | collective-permute-start | bytes 196616 | tf_op jit(solution)/shard_map/ppermute | solution.py:344
  27.4 4.7 %collective-permute-start.12 = (bf16[256,128]{1,0:T(8,128)(2,1)S(1)}, bf16[256,128]{1,0:T(8,128)(2,1)S(1)}, u32[]{:S(2)}, u32[]{:S(2)}) collective-permute-start(bf16[256,128]{1,0:T(8,128)(2,1)S(1)} %get-tuple-element.72), channel_id=1, source_target_pairs={{0,4},{4,0},{8,12},{12,8},{16,20},{20,16},{24,28},{28,24},{1,5},{5... | collective-permute-start | bytes 196616 | tf_op jit(solution)/shard_map/ppermute | solution.py:344
  29.2 5.1 %collective-permute-start.6 = (bf16[4,56,128]{2,1,0:T(8,128)(2,1)S(1)}, bf16[4,56,128]{2,1,0:T(8,128)(2,1)S(1)}, u32[]{:S(2)}, u32[]{:S(2)}) collective-permute-start(bf16[4,56,128]{2,1,0:T(8,128)(2,1)S(1)} %get-tuple-element.64), channel_id=1, source_target_pairs={{0,16},{4,20},{8,24},{12,28},{16,0},{20,4},{24,8},{28,12},{1,17},{... | collective-permute-start | bytes 172040 | tf_op jit(solution)/shard_map/ppermute | solution.py:344
  32.2 5.9 %collective-permute-start.13 = (bf16[256,128]{1,0:T(8,128)(2,1)S(1)}, bf16[256,128]{1,0:T(8,128)(2,1)S(1)}, u32[]{:S(2)}, u32[]{:S(2)}) collective-permute-start(bf16[256,128]{1,0:T(8,128)(2,1)S(1)} %shard_map.181.own_ref), channel_id=1, source_target_pairs={{0,16},{4,20},{8,24},{12,28},{16,0},{20,4},{24,8},{28,12},{1,17},{... | collective-permute-start | bytes 196616 | tf_op jit(solution)/shard_map/ppermute | solution.py:344
  34.3 5.0 %collective-permute-start.7 = (bf16[128,128]{1,0:T(8,128)(2,1)S(1)}, bf16[128,128]{1,0:T(8,128)(2,1)S(1)}, u32[]{:S(2)}, u32[]{:S(2)}) collective-permute-start(bf16[128,128]{1,0:T(8,128)(2,1)S(1)} %get-tuple-element.66), channel_id=1, source_target_pairs={{0,4},{4,0},{8,12},{12,8},{16,20},{20,16},{24,28},{28,24},{1,5},{5... | collective-permute-start | bytes 98312 | tf_op jit(solution)/shard_map/ppermute | solution.py:344
  35.2 6.5 %collective-permute-start.8 = (bf16[128,128]{1,0:T(8,128)(2,1)S(1)}, bf16[128,128]{1,0:T(8,128)(2,1)S(1)}, u32[]{:S(2)}, u32[]{:S(2)}) collective-permute-start(bf16[128,128]{1,0:T(8,128)(2,1)S(1)} %get-tuple-element.67), channel_id=1, source_target_pairs={{0,8},{4,12},{8,0},{12,4},{16,24},{20,28},{24,16},{28,20},{1,9},{5... | collective-permute-start | bytes 98312 | tf_op jit(solution)/shard_map/ppermute | solution.py:344
  35.7 6.0 %collective-permute-start.9 = (bf16[128,128]{1,0:T(8,128)(2,1)S(1)}, bf16[128,128]{1,0:T(8,128)(2,1)S(1)}, u32[]{:S(2)}, u32[]{:S(2)}) collective-permute-start(bf16[128,128]{1,0:T(8,128)(2,1)S(1)} %get-tuple-element.68), channel_id=1, source_target_pairs={{0,12},{4,8},{8,4},{12,0},{16,28},{20,24},{24,20},{28,16},{1,13},{... | collective-permute-start | bytes 98312 | tf_op jit(solution)/shard_map/ppermute | solution.py:344
  38.1 4.4 %collective-permute-start.16 = (bf16[256,128]{1,0:T(8,128)(2,1)S(1)}, bf16[256,128]{1,0:T(8,128)(2,1)S(1)}, u32[]{:S(2)}, u32[]{:S(2)}) collective-permute-start(bf16[256,128]{1,0:T(8,128)(2,1)S(1)} %shard_map.182.refs_2_), channel_id=1, source_target_pairs={{0,4},{4,0},{8,12},{12,8},{16,20},{20,16},{24,28},{28,24},{1,5},{5... | collective-permute-start | bytes 196616 | tf_op jit(solution)/shard_map/ppermute | solution.py:344
  39.2 4.3 %collective-permute-start.15 = (bf16[256,128]{1,0:T(8,128)(2,1)S(1)}, bf16[256,128]{1,0:T(8,128)(2,1)S(1)}, u32[]{:S(2)}, u32[]{:S(2)}) collective-permute-start(bf16[256,128]{1,0:T(8,128)(2,1)S(1)} %shard_map.182.refs_2_), channel_id=1, source_target_pairs={{0,8},{4,12},{8,0},{12,4},{16,24},{20,28},{24,16},{28,20},{1,9},{5... | collective-permute-start | bytes 196616 | tf_op jit(solution)/shard_map/ppermute | solution.py:344
  39.3 5.3 %collective-permute-start.14 = (bf16[256,128]{1,0:T(8,128)(2,1)S(1)}, bf16[256,128]{1,0:T(8,128)(2,1)S(1)}, u32[]{:S(2)}, u32[]{:S(2)}) collective-permute-start(bf16[256,128]{1,0:T(8,128)(2,1)S(1)} %shard_map.182.refs_2_), channel_id=1, source_target_pairs={{0,12},{4,8},{8,4},{12,0},{16,28},{20,24},{24,20},{28,16},{1,13},{... | collective-permute-start | bytes 196616 | tf_op jit(solution)/shard_map/ppermute | solution.py:344
